TPU v7x, 32 devices: a whole 2x2x4 slice. The times are simulated.
32 devices in a mesh: parts: 2 (over y), ep: 4 (over x, core), tp: 4 (over z).
Axes of the slice: x: 2, y: 2, z: 4, core: 2. Of those that a mesh axis runs over, the one named last changes fastest.
Arguments:
- query_latent: bfloat16 [512, 32, 512], P(('parts', 'ep'), 'tp'), parts along dimension 0, may hold values from -63 to 63
- query_rope: bfloat16 [512, 2048], P(('parts', 'ep'), 'tp'), parts along dimension 0, may hold values from -5 to 5
- cache_latent: bfloat16 [512, 256, 512], P(('parts', 'ep')), parts along dimension 0, may hold values from -5 to 5
- cache_rope: bfloat16 [512, 64, 256], P(('parts', 'ep')), parts along dimension 0, may hold values from -4.5 to 4.5
- cache_length: int32 [512], P(('parts', 'ep')), parts along dimension 0, may hold values from 2 to 256, as said below
- value_up: bfloat16 [32, 512, 128], P('tp'), may hold values from -0.25 to 0.25
- output_weight: bfloat16 [4096, 7168], P('tp', 'ep'), may hold values from -0.1875 to 0.1875
- residual: bfloat16 [512, 7168], P('parts', 'ep'), parts along dimension 0, may hold values from -40 to 40
- norm_gain: float32 [7168], P('ep'), may hold values from 0.25 to 1.75
- routed_experts: int32 [512, 2], P('parts'), parts along dimension 0, may hold values from 0 to 3, all different within a row; in each aligned block of 64 rows (0 to 63, 64 to 127, ...) at most 64 rows name the same one
- expert_gates: float32 [512, 2], P('parts'), parts along dimension 0, may hold values from 0.2 to 1
- gate_weight: bfloat16 [4, 7168, 2048], P('ep', None, 'tp'), may hold values from -0.0625 to 0.0625
- up_weight: bfloat16 [4, 7168, 2048], P('ep', None, 'tp'), may hold values from -0.0625 to 0.0625
- down_weight: bfloat16 [4, 2048, 7168], P('ep', 'tp'), may hold values from -0.125 to 0.125
Outputs:
- stream_out: bfloat16 [512, 7168], P(('parts', 'tp'), 'ep'), parts along dimension 0
- expert_mix: bfloat16 [512, 7168], P(('parts', 'tp'), 'ep'), parts along dimension 0
There are 2 independent parts, one for each index of `parts`. A program takes and returns all parts, laid end to end along the dimension named above; an argument that names none is the same for every part. Nothing has to cross between parts.
Inputs may be any that keep to these rules, and one draw needn't show every extreme that they name: Row r attends to cache positions 0 to cache_length[r] - 1; the first row of every group has all 256. `routed_experts`: each row names 2 different experts. Cut the rows into 4 aligned blocks of equal length: within one block no expert is named by more than 64 rows, and some expert reaches 64 in some block.
All inputs are finite; a program needn't handle non-finite values.
Results may differ from a plain program's by a relative error of at most 0.02.
Values may be sent and summed in bfloat16 or wider, within the bound.
No kernel may reach another device: no remote copies, remote signals or barrier semaphores. Data moves between devices by JAX's collectives and lax.ppermute only.
A program may use at most 128 MiB of HBM per device.

v0:
```python
import jax
import jax.numpy as jnp
from jax import lax
from jax.sharding import PartitionSpec as P

score_scale = 1.0 / 192.0**0.5
norm_epsilon = 1e-06


def slot_positions(routed, block_count, expert_count, capacity, local_experts):
    entry_rows, top_count = routed.shape
    entries = routed.reshape(block_count, entry_rows // block_count * top_count)
    one_hot = (
        entries[:, :, None] == jnp.arange(expert_count, dtype=jnp.int32)[None, None, :]
    ).astype(jnp.int32)
    earlier = jnp.cumsum(one_hot, axis=1) - one_hot
    slot_index = jnp.sum(earlier * one_hot, axis=-1)
    owner = entries // local_experts
    within = entries % local_experts
    block_index = jnp.arange(block_count, dtype=jnp.int32)[:, None]
    placed = ((owner * block_count + block_index) * capacity + slot_index) * local_experts + within
    return placed.reshape(entry_rows, top_count)


def shards(
    query_latent,
    query_rope,
    cache_latent,
    cache_rope,
    cache_length,
    value_up,
    output_weight,
    residual,
    norm_gain,
    routed_experts,
    expert_gates,
    gate_weight,
    up_weight,
    down_weight,
):
    ep_count = lax.axis_size("ep")
    tp_count = lax.axis_size("tp")
    local_rows, local_heads, latent_width = query_latent.shape
    cache_positions = cache_latent.shape[1]
    rope_width = cache_rope.shape[1]
    value_width = value_up.shape[2]
    column_count = output_weight.shape[1]
    local_experts = gate_weight.shape[0]
    row_total, top_count = routed_experts.shape
    block_rows = row_total // tp_count
    expert_count = local_experts * ep_count
    capacity = 2 * block_rows * top_count // expert_count
    rope_query = query_rope.reshape(local_rows, local_heads, rope_width)
    latent_part = jnp.einsum(
        "rhc,rlc->rhl", query_latent, cache_latent, preferred_element_type=jnp.float32
    )
    rope_part = jnp.einsum(
        "rhp,rpl->rhl", rope_query, cache_rope, preferred_element_type=jnp.float32
    )
    scores = (latent_part + rope_part) * score_scale
    visible = (
        jnp.arange(cache_positions, dtype=jnp.int32)[None, None, :] < cache_length[:, None, None]
    )
    scores = jnp.where(visible, scores, -jnp.inf)
    peak_score = jnp.max(scores, axis=-1, keepdims=True)
    weights = jnp.where(visible, jnp.exp(scores - peak_score), 0.0)
    probabilities = (weights / jnp.sum(weights, axis=-1, keepdims=True)).astype(jnp.bfloat16)
    latent_out = jnp.einsum(
        "rhl,rlc->rhc", probabilities, cache_latent, preferred_element_type=jnp.float32
    ).astype(jnp.bfloat16)
    head_out = jnp.einsum(
        "rhc,hcv->rhv", latent_out, value_up, preferred_element_type=jnp.float32
    ).astype(jnp.bfloat16)
    head_out = head_out.reshape(local_rows, local_heads * value_width)
    partial_sum = jnp.dot(
        lax.all_gather(head_out, "ep", axis=0, tiled=True),
        output_weight,
        preferred_element_type=jnp.float32,
    )
    first_own = lax.axis_index("tp") * block_rows
    attention = lax.psum(partial_sum.astype(jnp.bfloat16), "tp").astype(jnp.float32)
    hidden = (residual.astype(jnp.float32) + attention).astype(jnp.bfloat16)
    hidden_wide = hidden.astype(jnp.float32)
    square_sum = lax.psum(jnp.sum(hidden_wide * hidden_wide, axis=-1), "ep")
    inverse_rms = lax.rsqrt(square_sum / (column_count * ep_count) + norm_epsilon)
    normed = (hidden_wide * inverse_rms[:, None] * norm_gain).astype(jnp.bfloat16)
    positions = slot_positions(routed_experts, tp_count, expert_count, capacity, local_experts)
    flat_positions = positions.reshape(-1)
    slot_total = expert_count * tp_count * capacity
    placement_matrix = (
        flat_positions[:, None] == jnp.arange(slot_total, dtype=jnp.int32)[None, :]
    ).astype(jnp.bfloat16)
    repeated = jnp.broadcast_to(
        normed[:, None, :], (normed.shape[0], top_count, column_count)
    ).reshape(-1, column_count)
    send_buffer = jnp.einsum(
        "ep,ec->pc", placement_matrix, repeated, preferred_element_type=jnp.float32
    ).astype(jnp.bfloat16)
    send_buffer = send_buffer.reshape(ep_count, tp_count, capacity, local_experts, column_count)
    arrived = lax.all_to_all(send_buffer, "ep", split_axis=0, concat_axis=4, tiled=True)
    arrived = arrived.reshape(tp_count * capacity, local_experts, column_count * ep_count)
    gate_part = jnp.einsum("sjd,jdf->sjf", arrived, gate_weight, preferred_element_type=jnp.float32)
    up_part = jnp.einsum("sjd,jdf->sjf", arrived, up_weight, preferred_element_type=jnp.float32)
    activation = (jax.nn.silu(gate_part) * up_part).astype(jnp.bfloat16)
    expert_out = lax.psum_scatter(
        jnp.einsum(
            "sjf,jfd->sjd", activation, down_weight, preferred_element_type=jnp.float32
        ).astype(jnp.bfloat16),
        "tp",
        scatter_dimension=0,
        tiled=True,
    )
    returned = lax.all_to_all(expert_out, "ep", split_axis=2, concat_axis=0, tiled=True)
    returned = returned.reshape(ep_count * capacity * local_experts, column_count)
    own_hidden = lax.dynamic_slice_in_dim(hidden, first_own, block_rows, 0)
    own_routed = lax.dynamic_slice_in_dim(routed_experts, first_own, block_rows, 0)
    own_positions = slot_positions(own_routed, 1, expert_count, capacity, local_experts)
    own_gates = lax.dynamic_slice_in_dim(expert_gates, first_own, block_rows, 0)
    own_slots = ep_count * capacity * local_experts
    combine = jnp.sum(
        jnp.where(
            own_positions[:, :, None] == jnp.arange(own_slots, dtype=jnp.int32)[None, None, :],
            own_gates[:, :, None],
            0.0,
        ),
        axis=1,
    )
    mixed = jnp.dot(combine, returned.astype(jnp.float32), precision=lax.Precision.HIGHEST).astype(
        jnp.bfloat16
    )
    return (own_hidden, mixed)


def solution(mesh):
    return jax.shard_map(
        shards,
        mesh=mesh,
        in_specs=(
            P(("parts", "ep"), "tp", None),
            P(("parts", "ep"), "tp"),
            P(("parts", "ep"), None, None),
            P(("parts", "ep"), None, None),
            P(("parts", "ep")),
            P("tp", None, None),
            P("tp", "ep"),
            P("parts", "ep"),
            P("ep"),
            P("parts", None),
            P("parts", None),
            P("ep", None, "tp"),
            P("ep", None, "tp"),
            P("ep", "tp", None),
        ),
        out_specs=(P(("parts", "tp"), "ep"), P(("parts", "tp"), "ep")),
        check_vma=False,
    )
```

profile of v0, /device:TPU:0, one launch (start us, length us, event | category | flops | bytes accessed | tf_op | source)
XLA Modules:
  0.0 326.7 jit_solution(8978609634509124880)
XLA Ops:
  7.2 0.9 iota_compare_fusion.5
  8.1 1.0 reshape.241
  9.1 10.4 %fusion.47 = f32[64,8,256]{2,1,0:T(8,128)S(1)} fusion(bf16[64,8,512]{2,1,0:T(8,128)(2,1)} %param.14, bf16[64,256,512]{2,1,0:T(8,128)(2,1)} %param.16), kind=kOutput, calls=%fused_computation.63 | convolution fusion | flops 134217728 | bytes 17825792 | tf_op jit(solution)/shard_map/rhc,rlc->rhl/dot_general | solution.py:54
  19.5 0.6 fusion.46
  20.1 8.2 %convolution_convert_fusion.4 = bf16[64,8,512]{2,1,0:T(8,128)(2,1)S(1)} fusion(bf16[64,256,512]{2,1,0:T(8,128)(2,1)} %param.16, f32[64,8,256]{2,1,0:T(8,128)S(1)} %get-tuple-element.5, f32[64,8]{1,0:T(8,128)S(1)} %get-tuple-element.4), kind=kOutput, calls=%fused_computation.19 | convolution fusion | flops 134742016 | bytes 17827840 | tf_op jit(solution)/shard_map/rhl,rlc->rhc/dot_general | solution.py:68
  28.3 0.4 fusion.30
  28.7 8.6 %all_gather.3 = bf16[256,1024]{1,0:T(8,128)(2,1)S(1)} all-gather(bf16[64,1024]{1,0:T(8,128)(2,1)S(1)} %bitcast.101), channel_id=1, replica_groups=mesh['parts'=2,'ep'=4,'tp'=4] {'ep'}, dimensions={0}, use_global_device_ids=true | all-gather | bytes 655360 | tf_op jit(solution)/shard_map/all_gather | solution.py:76
  37.4 2.1 convolution_convert_fusion.2
  39.6 0.1 copy.47
  39.7 0.1 eq.79
  39.9 0.1 copy.49
  40.0 0.1 mul.82
  40.2 0.1 fusion.41
  40.3 0.3 reduce_window_sum.23
  40.6 0.2 select_reduce_fusion
  40.8 47.5 %all-reduce.2.cloned.1.call-done = bf16[256,1792]{1,0:T(8,128)(2,1)} async-done(((bf16[256,1792]{1,0:T(8,128)(2,1)}), bf16[256,1792]{1,0:T(8,128)(2,1)}) %all-reduce.2.cloned.1.call-update) | async-done | bytes 917520 | tf_op jit(solution)/shard_map/psum | solution.py:81
  88.3 1.6 fusion.7
  89.9 6.8 %psum.15 = f32[256]{0:T(256)S(1)} all-reduce(f32[256]{0:T(256)S(1)} %get-tuple-element.2), channel_id=1, replica_groups=mesh['parts'=2,'ep'=4,'tp'=4] {'ep'}, use_global_device_ids=true, to_apply=%region_9.10 | all-reduce | flops 256 | bytes 2048 | tf_op jit(solution)/shard_map/psum | solution.py:84
  96.7 0.3 fusion.9
  97.0 0.9 broadcast_in_dim.53
  98.0 1.7 reshape.243
  99.7 3.7 %convolution_convert_fusion.1 = bf16[1024,1792]{1,0:T(8,128)(2,1)S(1)} fusion(bf16[512,1792]{1,0:T(8,128)(2,1)} %reshape.243, s32[512]{0:T(512)S(1)} %bitcast_add_fusion), kind=kOutput, calls=%fused_computation.8 | convolution fusion | flops 1881407488 | bytes 5507072 | tf_op jit(solution)/shard_map/ep,ec->pc/dot_general | solution.py:96
  103.4 45.4 %all_to_all.30 = bf16[4,4,64,1,1792]{4,2,1,3,0:T(8,128)(2,1)S(1)} all-to-all(bf16[4,4,64,1,1792]{4,2,1,3,0:T(8,128)(2,1)S(1)} %bitcast.98), channel_id=1, replica_groups=mesh['parts'=2,'ep'=4,'tp'=4] {'ep'}, dimensions={0} | all-to-all | bytes 7340032 | tf_op jit(solution)/shard_map/all_to_all | solution.py:100
  148.7 2.8 copy.52
  151.6 2.5 copy.57
  154.1 4.1 %fusion.13 = f32[256,1,512]{2,0,1:T(8,128)S(1)} fusion(bf16[256,7168]{1,0:T(8,128)(2,1)} %bitcast.35, bf16[1,7168,512]{2,1,0:T(8,128)(2,1)S(1)} %bitcast.103), kind=kOutput, calls=%fused_computation.22 | convolution fusion | flops 1879048192 | bytes 11534336 | tf_op jit(solution)/shard_map/sjd,jdf->sjf/dot_general | solution.py:102
  158.2 12.1 %fusion.1 = bf16[256,1,7168]{2,0,1:T(8,128)(2,1)} fusion(bf16[1,512,7168]{2,1,0:T(8,128)(2,1)} %param.27, bf16[256,7168]{1,0:T(8,128)(2,1)} %bitcast.35, bf16[1,7168,512]{2,1,0:T(8,128)(2,1)} %param.26, f32[256,1,512]{2,0,1:T(8,128)S(1)} %fusion.13), kind=kOutput, calls=%fused_computation.2 | convolution fusion | flops 3760717824 | bytes 22544384 | tf_op jit(solution)/shard_map/sjf,jfd->sjd/dot_general | solution.py:106
  170.3 0.1 eq.72
  170.4 0.1 fusion.43
  170.5 0.2 reduce_window_sum.22
  170.7 66.5 %reduce-scatter.2.cloned.1.call-done = bf16[64,1,7168]{2,0,1:T(8,128)(2,1)} async-done(((bf16[256,1,7168]{2,0,1:T(8,128)(2,1)}), bf16[64,1,7168]{2,0,1:T(8,128)(2,1)}) %reduce-scatter.2.cloned.1.call-update) | async-done | bytes 917520 | tf_op jit(solution)/shard_map/reduce_scatter | solution.py:105
  237.2 8.3 %copy.53 = bf16[64,1,7168]{0,1,2:T(2,128)(2,1)} copy(bf16[64,1,7168]{2,0,1:T(8,128)(2,1)} %reduce-scatter.2.cloned.1.call-done) | data formatting | bytes 1835008 | tf_op jit(solution)/shard_map/reduce_scatter | solution.py:105
  245.5 0.5 broadcast.190
  246.0 40.0 %reduce.1 = bf16[7168,64]{1,0:T(8,128)(2,1)S(1)} reduce(bf16[7168,1,64]{2,1,0:T(2,128)(2,1)} %bitcast.96, bf16[]{:T(256)} %broadcast.190), dimensions={1}, to_apply=%bitcast.78.reduce_sub_computation | reduce | bytes 1835010
  286.0 2.5 reshape.251
  288.6 3.5 %all-to-all-start.1 = ((bf16[4,2,57344]{2,1,0:T(2,128)(2,1)}), bf16[4,2,57344]{2,1,0:T(2,128)(2,1)S(1)}, u32[]{:S(2)}, u32[]{:S(2)}) async-start(bf16[4,2,57344]{2,1,0:T(2,128)(2,1)} %reshape.251), calls=%async_computation.2 | async-start | bytes 1835008 | tf_op jit(solution)/shard_map/all_to_all | solution.py:113
  292.1 0.2 select_reduce_fusion.2
  292.2 0.1 reduce_sum.51
  292.4 0.1 copy.48
  292.5 0.1 constant_dynamic-slice_fusion
  292.6 0.1 select_reduce_fusion.1
  292.7 0.7 constant_dynamic-slice_fusion.2
  293.4 11.7 %all-to-all-done.1 = bf16[4,2,57344]{2,1,0:T(2,128)(2,1)S(1)} async-done(((bf16[4,2,57344]{2,1,0:T(2,128)(2,1)}), bf16[4,2,57344]{2,1,0:T(2,128)(2,1)S(1)}, u32[]{:S(2)}, u32[]{:S(2)}) %all-to-all-start.1) | async-done | bytes 917536 | tf_op jit(solution)/shard_map/all_to_all | solution.py:113
  305.1 2.9 reshape.252
  308.0 8.3 %copy.54 = bf16[64,1,7168]{2,0,1:T(8,128)(2,1)} copy(bf16[64,1,7168]{0,1,2:T(2,128)(2,1)} %bitcast.97) | data formatting | bytes 1835008 | tf_op jit(solution)/shard_map/all_to_all | solution.py:113
  316.3 2.1 all_to_all.26
  318.4 0.1 copy.55
  318.5 1.3 convolution_convert_fusion.3
  (31 shorter events, 0.2 us)
Async XLA Ops:
  7.2 12.3 %copy-start = (bf16[64,64,256]{2,1,0:T(8,128)(2,1)S(1)}, bf16[64,64,256]{2,1,0:T(8,128)(2,1)}, u32[]{:S(2)}) copy-start(bf16[64,64,256]{2,1,0:T(8,128)(2,1)} %param.17) | copy-start | bytes 6291460
  7.2 81.1 %all-reduce.2.cloned.1.call-start = ((), (), s32[]{:S(2)}) async-start(), calls=%async_computation.3 | async-start | bytes 1835008 | tf_op jit(solution)/shard_map/psum | solution.py:81
  20.1 8.2 %copy-start.2 = (bf16[8,512,128]{2,1,0:T(8,128)(2,1)S(1)}, bf16[8,512,128]{2,1,0:T(8,128)(2,1)}, u32[]{:S(2)}) copy-start(bf16[8,512,128]{2,1,0:T(8,128)(2,1)} %param.19) | copy-start | bytes 3145732
  20.1 17.3 %copy-start.7 = (bf16[1024,1792]{1,0:T(8,128)(2,1)S(1)}, bf16[1024,1792]{1,0:T(8,128)(2,1)}, u32[]{:S(2)}) copy-start(bf16[1024,1792]{1,0:T(8,128)(2,1)} %param.20) | copy-start | bytes 11010052
  28.7 10.8 %copy-start.5 = (s32[256,2]{0,1:T(2,128)S(1)}, s32[256,2]{0,1:T(2,128)}, u32[]{:S(2)}) copy-start(s32[256,2]{0,1:T(2,128)} %param.23) | copy-start | bytes 6148
  37.4 50.9 %copy-start.3 = (bf16[256,1792]{1,0:T(8,128)(2,1)S(1)}, bf16[256,1792]{1,0:T(8,128)(2,1)}, u32[]{:S(2)}) copy-start(bf16[256,1792]{1,0:T(8,128)(2,1)} %param.21) | copy-start | bytes 2752516
  39.5 57.3 %copy-start.4 = (f32[1792]{0:T(1024)S(1)}, f32[1792]{0:T(1024)}, u32[]{:S(2)}) copy-start(f32[1792]{0:T(1024)} %param.22) | copy-start | bytes 21508
  39.5 197.6 %reduce-scatter.2.cloned.1.call-start = ((), (), s32[]{:S(2)}) async-start(), calls=%async_computation.4 | async-start | bytes 4587520 | tf_op jit(solution)/shard_map/reduce_scatter | solution.py:105
  103.4 50.7 %slice-start = ((s8[7340032]{0:T(1024)(128)(4,1)}), s8[4194304]{0:T(1024)(128)(4,1)S(1)}, s32[]{:S(2)}) async-start(s8[7340032]{0:T(1024)(128)(4,1)} %bitcast.102), calls=%async_computation.5 | async-start | bytes 8388608
  148.7 5.3 %slice-start.1 = ((s8[7340032]{0:T(1024)(128)(4,1)}), s8[3145728]{0:T(1024)(128)(4,1)S(1)}, s32[]{:S(2)}) async-start(s8[7340032]{0:T(1024)(128)(4,1)} %bitcast.102), calls=%async_computation.6 | async-start | bytes 6291456
  286.0 6.5 %copy-start.6 = (f32[256,2]{0,1:T(2,128)S(1)}, f32[256,2]{0,1:T(2,128)}, u32[]{:S(2)}) copy-start(f32[256,2]{0,1:T(2,128)} %param.24) | copy-start | bytes 6148
  288.6 16.5 %all-to-all-start.1 = ((bf16[4,2,57344]{2,1,0:T(2,128)(2,1)}), bf16[4,2,57344]{2,1,0:T(2,128)(2,1)S(1)}, u32[]{:S(2)}, u32[]{:S(2)}) async-start(bf16[4,2,57344]{2,1,0:T(2,128)(2,1)} %reshape.251), calls=%async_computation.2 | async-start | bytes 1835008 | tf_op jit(solution)/shard_map/all_to_all | solution.py:113
  308.0 11.8 %copy-start.1 = (bf16[64,64,256]{2,1,0:T(8,128)(2,1)S(1)}, bf16[64,64,256]{2,1,0:T(8,128)(2,1)}, u32[]{:S(2)}) copy-start(bf16[64,64,256]{2,1,0:T(8,128)(2,1)} %param.17) | copy-start | bytes 6291460
Sparse Core Ops, SparseCore 0:
  39.6 48.6 all-reduce.1
  170.4 66.7 reduce-scatter.1
where the time goes:
time: 328 us; the launch traced here: 327 us
  waiting for transfers between devices  126 us (38%)
  blocking collectives  60.8 us (19%)
  other arithmetic  44 us (13%)
  matrix products  42.8 us (13%)
  local copies, waits for them, and re-layouts  35.5 us (11%)
  between operations  14.3 us (4%)
  starting transfers between devices  3.58 us (1%)
    reduce_scatter x1, waiting for transfers between devices, shards(): lax.psum_scatter(jnp.einsum('sjf,jfd->sjd', activation, down_weight, pref...  66.5 us
    psum x1, waiting for transfers between devices, shards(): lax.psum(partial_sum.astype(jnp.bfloat16), 'tp').astype(jnp.float32)  47.5 us
    all_to_all x1, blocking collectives, shards(): lax.all_to_all(send_buffer, 'ep', split_axis=0, concat_axis=4, tiled=True)  45.4 us
    unnamed x2, other arithmetic  40 us
    dot_general x1, matrix products, shards(): jnp.einsum('sjf,jfd->sjd', activation, down_weight, preferred_element_typ...  12.1 us
    all_to_all x1, waiting for transfers between devices, shards(): lax.all_to_all(expert_out, 'ep', split_axis=2, concat_axis=0, tiled=True)  11.7 us
    all_to_all x3, local copies, waits for them, and re-layouts, shards(): lax.all_to_all(expert_out, 'ep', split_axis=2, concat_axis=0, tiled=True)  10.5 us
    dot_general x1, matrix products, shards(): jnp.einsum('rhc,rlc->rhl', query_latent, cache_latent, preferred_element_...  10.4 us
  transfers between devices with their start and end apart: 3, of which 3 were waited for; matrix products, arithmetic and copies ran while one was open for 1% of the time, Pallas kernels for 0%

commit v1 on v0

v1 whole, which is shorter than its diff:
```python
import functools

import jax
import jax.numpy as jnp
from jax import lax
from jax.experimental import pallas as pl
from jax.experimental.pallas import tpu as pltpu
from jax.sharding import PartitionSpec as P

score_scale = 1.0 / 192.0**0.5
norm_epsilon = 1e-06
MIB = 1 << 20


def attention_kernel(step_rows, lengths, q_ref, qr_ref, k_ref, kr_ref, up_ref, out_ref, latent):
    step = pl.program_id(0)
    heads, positions = q_ref.shape[1], k_ref.shape[1]
    place = lax.broadcasted_iota(jnp.int32, (heads, positions), 1)
    lanes = latent.shape[2]
    scores = []
    for r in range(step_rows):
        score = lax.dot_general(
            q_ref[r], k_ref[r], (((1,), (1,)), ((), ())), preferred_element_type=jnp.float32
        )
        score += jnp.dot(qr_ref[r], kr_ref[r], preferred_element_type=jnp.float32)
        scores.append(score)
    probabilities = []
    for r in range(step_rows):
        visible = place < lengths[step * step_rows + r]
        score = jnp.where(visible, scores[r] * score_scale, -jnp.inf)
        weight = jnp.exp(score - jnp.max(score, axis=-1, keepdims=True))
        total = jnp.sum(weight, axis=-1, keepdims=True)
        probabilities.append((weight / total).astype(jnp.bfloat16))
    for r in range(step_rows):
        first = pl.multiple_of((step * step_rows + r) * heads, heads)
        mixed = jnp.dot(probabilities[r], k_ref[r], preferred_element_type=jnp.float32)
        for c in range(latent.shape[0]):
            latent[c, pl.ds(first, heads), :] = mixed[:, c * lanes : (c + 1) * lanes]

    @pl.when(step == pl.num_programs(0) - 1)
    def _():
        rows = out_ref.shape[0]
        width = up_ref.shape[2]
        for h in range(heads):
            parts = [latent[c, pl.ds(h, rows, stride=heads), :] for c in range(latent.shape[0])]
            part = jnp.concatenate(parts, axis=1).astype(jnp.bfloat16)
            out_ref[:, h * width : (h + 1) * width] = jnp.dot(
                part, up_ref[h], preferred_element_type=jnp.float32
            ).astype(jnp.bfloat16)


def attend(query_latent, rope_query, cache_latent, cache_rope, cache_length, value_up):
    rows, heads, latent_width = query_latent.shape
    positions = cache_latent.shape[1]
    rope_width = cache_rope.shape[1]
    value_width = value_up.shape[2]
    step_rows = 16
    by_row = lambda i, lengths: (i, 0, 0)
    return pl.pallas_call(
        functools.partial(attention_kernel, step_rows),
        out_shape=jax.ShapeDtypeStruct((rows, heads * value_width), jnp.bfloat16),
        grid_spec=pltpu.PrefetchScalarGridSpec(
            num_scalar_prefetch=1,
            grid=(rows // step_rows,),
            in_specs=[
                pl.BlockSpec((step_rows, heads, latent_width), by_row),
                pl.BlockSpec((step_rows, heads, rope_width), by_row),
                pl.BlockSpec((step_rows, positions, latent_width), by_row),
                pl.BlockSpec((step_rows, rope_width, positions), by_row),
                pl.BlockSpec(value_up.shape, lambda i, lengths: (0, 0, 0)),
            ],
            out_specs=pl.BlockSpec((rows, heads * value_width), lambda i, lengths: (0, 0)),
            scratch_shapes=[pltpu.VMEM((latent_width // 128, rows * heads, 128), jnp.float32)],
        ),
        compiler_params=pltpu.CompilerParams(vmem_limit_bytes=32 * MIB),
        name="attention",
    )(cache_length, query_latent, rope_query, cache_latent, cache_rope, value_up)


def projection_kernel(count, places, *refs):
    blocks, weight, outs = refs[:count], refs[count], refs[count + 1 : -2]
    gathered, result = refs[-2:]
    height = blocks[0].shape[0]
    for k in range(count):
        first = pl.multiple_of(places[k] * height, height)
        gathered[pl.ds(first, height), :] = blocks[k][...]
    columns = weight.shape[1]
    tile = 256 if columns % 256 == 0 else 128
    for j in range(columns // tile):
        result[:, j * tile : (j + 1) * tile] = jnp.dot(
            gathered[...], weight[:, j * tile : (j + 1) * tile], preferred_element_type=jnp.float32
        ).astype(jnp.bfloat16)
    out_height = outs[0].shape[0]
    for s in range(len(outs)):
        first = pl.multiple_of(places[count + s] * out_height, out_height)
        outs[s][...] = result[pl.ds(first, out_height), :]


def project(places, blocks, weight, out_count):
    count = len(blocks)
    height, depth = blocks[0].shape
    rows, columns = height * count, weight.shape[1]
    whole = pl.BlockSpec(memory_space=pltpu.VMEM)
    return pl.pallas_call(
        functools.partial(projection_kernel, count),
        out_shape=[jax.ShapeDtypeStruct((rows // out_count, columns), jnp.bfloat16)] * out_count,
        in_specs=[pl.BlockSpec(memory_space=pltpu.SMEM)] + [whole] * (count + 1),
        out_specs=[whole] * out_count,
        scratch_shapes=[
            pltpu.VMEM((rows, depth), jnp.bfloat16),
            pltpu.VMEM((rows, columns), jnp.bfloat16),
        ],
        compiler_params=pltpu.CompilerParams(vmem_limit_bytes=32 * MIB),
        name="projection",
    )(places, *blocks, weight)


def expert_kernel(row_blocks, column_blocks, model_width, places, *refs):
    count = row_blocks * column_blocks
    blocks, gains = refs[:count], refs[count : count + column_blocks]
    row_weight, gate_hbm, up_hbm, down_hbm = refs[count + column_blocks : count + column_blocks + 4]
    outs = refs[count + column_blocks + 4 : -8]
    x, gate, up, down, gate_sum, up_sum, active, sems = refs[-8:]
    height, width = blocks[0].shape
    hidden = gate.shape[2]
    copies = []
    for k in range(column_blocks):
        first = pl.multiple_of(places[k] * width, width)
        copies.append(
            (
                pltpu.make_async_copy(gate_hbm.at[0, pl.ds(first, width), :], gate.at[k], sems.at[0, k]),
                pltpu.make_async_copy(up_hbm.at[0, pl.ds(first, width), :], up.at[k], sems.at[1, k]),
                pltpu.make_async_copy(down_hbm.at[0, :, pl.ds(first, width)], down.at[k], sems.at[2, k]),
            )
        )
    for which in ((0, 1), (2,)):
        for k in range(column_blocks):
            for w in which:
                copies[k][w].start()
    squares = [jnp.zeros((height, 1), jnp.float32) for _ in range(row_blocks)]
    tile = min(256, hidden)
    for k in range(column_blocks):
        for s in range(row_blocks):
            wide = blocks[s * column_blocks + k][...].astype(jnp.float32)
            squares[s] += jnp.sum(wide * wide, axis=-1, keepdims=True)
            x[k, s * height : (s + 1) * height, :] = (wide * gains[k][...]).astype(jnp.bfloat16)
        copies[k][0].wait()
        copies[k][1].wait()
        for total, weight in ((gate_sum, gate), (up_sum, up)):
            for j in range(hidden // tile):
                cut = slice(j * tile, (j + 1) * tile)
                product = jnp.dot(x[k], weight[k, :, cut], preferred_element_type=jnp.float32)
                if k == 0:
                    total[:, cut] = product
                else:
                    total[:, cut] += product
    for s in range(row_blocks):
        rows = slice(s * height, (s + 1) * height)
        scale = lax.rsqrt(squares[s] / model_width + norm_epsilon)
        gate_part = gate_sum[rows, :] * scale
        up_part = up_sum[rows, :] * scale
        active[rows, :] = (gate_part / (1.0 + jnp.exp(-gate_part)) * up_part).astype(jnp.bfloat16)
    for k in range(column_blocks):
        copies[k][2].wait()
    tile = 256 if width % 256 == 0 else 128
    for k in range(column_blocks):
        for j in range(width // tile):
            cut = slice(j * tile, (j + 1) * tile)
            product = jnp.dot(active[...], down[k, :, cut], preferred_element_type=jnp.float32)
            for s in range(row_blocks):
                first = pl.multiple_of(places[column_blocks + s] * height, height)
                part = product[s * height : (s + 1) * height, :] * row_weight[pl.ds(first, height), :]
                outs[s * column_blocks + k][:, cut] = part.astype(jnp.bfloat16)


def run_expert(places, blocks, gains, row_weight, gate_weight, up_weight, down_weight):
    row_blocks, column_blocks = len(blocks), len(blocks[0])
    height, width = blocks[0][0].shape
    rows = row_blocks * height
    hidden = gate_weight.shape[2]
    whole = pl.BlockSpec(memory_space=pltpu.VMEM)
    count = row_blocks * column_blocks
    outs = pl.pallas_call(
        functools.partial(expert_kernel, row_blocks, column_blocks, gate_weight.shape[1]),
        out_shape=[jax.ShapeDtypeStruct((height, width), jnp.bfloat16)] * count,
        in_specs=[pl.BlockSpec(memory_space=pltpu.SMEM)]
        + [whole] * (count + column_blocks + 1)
        + [pl.BlockSpec(memory_space=pl.ANY)] * 3,
        out_specs=[whole] * count,
        scratch_shapes=[
            pltpu.VMEM((column_blocks, rows, width), jnp.bfloat16),
            pltpu.VMEM((column_blocks, width, hidden), jnp.bfloat16),
            pltpu.VMEM((column_blocks, width, hidden), jnp.bfloat16),
            pltpu.VMEM((column_blocks, hidden, width), jnp.bfloat16),
            pltpu.VMEM((rows, hidden), jnp.float32),
            pltpu.VMEM((rows, hidden), jnp.float32),
            pltpu.VMEM((rows, hidden), jnp.bfloat16),
            pltpu.SemaphoreType.DMA((3, column_blocks)),
        ],
        compiler_params=pltpu.CompilerParams(vmem_limit_bytes=48 * MIB),
        name="expert",
    )(places, *[b for row in blocks for b in row], *gains, row_weight, gate_weight, up_weight, down_weight)
    return [outs[s * column_blocks : (s + 1) * column_blocks] for s in range(row_blocks)]


def shards(
    query_latent,
    query_rope,
    cache_latent,
    cache_rope,
    cache_length,
    value_up,
    output_weight,
    residual,
    norm_gain,
    routed_experts,
    expert_gates,
    gate_weight,
    up_weight,
    down_weight,
):
    ep_count = lax.axis_size("ep")
    tp_count = lax.axis_size("tp")
    ep_index = lax.axis_index("ep")
    tp_index = lax.axis_index("tp")
    local_rows, local_heads, _ = query_latent.shape
    rope_width = cache_rope.shape[1]
    row_total = routed_experts.shape[0]
    block_rows = row_total // tp_count
    cores = 2
    chips = ep_count // cores

    def from_core(value):
        return lax.ppermute(value, "ep", [(i, i ^ 1) for i in range(ep_count)])

    def from_chip(value, back):
        step = cores * back
        return lax.ppermute(value, "ep", [(i, (i + step) % ep_count) for i in range(ep_count)])

    def from_tp(value, back):
        return lax.ppermute(value, "tp", [(i, (i + back) % tp_count) for i in range(tp_count)])

    def gather_ep(value):
        same = [value] + [from_chip(value, b) for b in range(1, chips)]
        other = [from_core(v) for v in same]
        return [v for pair in zip(same, other) for v in pair]

    chip, core = ep_index // cores, ep_index % cores
    ep_places = [
        (chip - b + chips) % chips * cores + (core if c == 0 else 1 - core)
        for b in range(chips)
        for c in range(cores)
    ]
    tp_places = [(tp_index - b + tp_count) % tp_count for b in range(tp_count)]
    places = jnp.stack(ep_places + tp_places).astype(jnp.int32)

    gains = gather_ep(norm_gain.reshape(1, -1))
    row_weight = jnp.sum(jnp.where(routed_experts == ep_index, expert_gates, 0.0), axis=-1, keepdims=True)

    head_out = attend(
        query_latent,
        query_rope.reshape(local_rows, local_heads, rope_width),
        cache_latent,
        cache_rope,
        cache_length,
        value_up,
    )
    partial = project(places, gather_ep(head_out), output_weight, tp_count)
    arrived = [partial[0]] + [from_tp(partial[b], tp_count - b) for b in range(1, tp_count)]
    own_residual = lax.dynamic_slice_in_dim(residual, tp_index * block_rows, block_rows, 0)
    attention = sum(a.astype(jnp.float32) for a in arrived)
    stream = (own_residual.astype(jnp.float32) + attention).astype(jnp.bfloat16)

    rows_of = [stream] + [from_tp(stream, b) for b in range(1, tp_count)]
    blocks = [gather_ep(r) for r in rows_of]
    outs = run_expert(places, blocks, gains, row_weight, gate_weight, up_weight, down_weight)

    def add(values):
        return sum(v.astype(jnp.float32) for v in values).astype(jnp.bfloat16)

    def back_to_ep(out):
        pairs = [add((out[b * cores], from_core(out[b * cores + 1]))) for b in range(chips)]
        return add([pairs[0]] + [from_chip(pairs[b], chips - b) for b in range(1, chips)])

    returned = [back_to_ep(out) for out in outs]
    mixed = add([returned[0]] + [from_tp(returned[b], tp_count - b) for b in range(1, tp_count)])
    return (stream, mixed)


def solution(mesh):
    return jax.shard_map(
        shards,
        mesh=mesh,
        in_specs=(
            P(("parts", "ep"), "tp", None),
            P(("parts", "ep"), "tp"),
            P(("parts", "ep"), None, None),
            P(("parts", "ep"), None, None),
            P(("parts", "ep")),
            P("tp", None, None),
            P("tp", "ep"),
            P("parts", "ep"),
            P("ep"),
            P("parts", None),
            P("parts", None),
            P("ep", None, "tp"),
            P("ep", None, "tp"),
            P("ep", "tp", None),
        ),
        out_specs=(P(("parts", "tp"), "ep"), P(("parts", "tp"), "ep")),
        check_vma=False,
    )
```

time: 328 us -> 150 us (0.46)
  blocking collectives: 60.8 us -> 0 us
  waiting for transfers between devices: 126 us -> 82.9 us
  matrix products: 42.8 us -> 0 us
  other arithmetic: 44 us -> 2.47 us
  starting transfers between devices: 3.58 us -> 28.2 us
  local copies, waits for them, and re-layouts: 35.5 us -> 13.5 us
  Pallas kernels: 0 us -> 21.5 us
  between operations: 14.3 us -> 0.86 us
    ppermute x0 -> x39, waiting for transfers between devices: none -> 82.9 us  [the longest x9 45.8 us: from_tp(): lax.ppermute(value, 'tp', [(i, (i + back) % tp_count) for i in range(tp_c...]
    reduce_scatter x1 -> x0, waiting for transfers between devices: 66.5 us -> none  [shards(): lax.psum_scatter(jnp.einsum('sjf,jfd->sjd', activation, down_weight, pref...]
    psum x1 -> x0, waiting for transfers between devices: 47.5 us -> none  [shards(): lax.psum(partial_sum.astype(jnp.bfloat16), 'tp').astype(jnp.float32)]
    all_to_all x1 -> x0, blocking collectives: 45.4 us -> none  [shards(): lax.all_to_all(send_buffer, 'ep', split_axis=0, concat_axis=4, tiled=True)]
    dot_general x8 -> x0, matrix products: 42.2 us -> none  [the longest x1 12.1 us: shards(): jnp.einsum('sjf,jfd->sjd', activation, down_weight, preferred_element_typ...]
    unnamed x2 -> x0, other arithmetic: 40 us -> none
    ppermute x0 -> x39, starting transfers between devices: none -> 28.2 us  [the longest x10 13.8 us: from_chip(): lax.ppermute(value, 'ep', [(i, (i + step) % ep_count) for i in range(ep_c...]
    pallas_call x0 -> x3, Pallas kernels: none -> 21.5 us  [the longest x1 11.2 us: run_expert(): pl.pallas_call(functools.partial(expert_kernel, row_blocks, column_blocks...]
  transfers between devices with their start and end apart: 3 -> 39, of which waited for: 3 -> 19; matrix products, arithmetic and copies ran while one was open for 1% -> 1% of each run, Pallas kernels for 0% -> 0%
where the time goes in v1:
time: 150 us; the launch traced here: 149 us
  waiting for transfers between devices  82.9 us (55%)
  starting transfers between devices  28.2 us (19%)
  Pallas kernels  21.5 us (14%)
  local copies, waits for them, and re-layouts  13.5 us (9%)
  other arithmetic  2.47 us (2%)
    ppermute x9, waiting for transfers between devices, from_tp(): lax.ppermute(value, 'tp', [(i, (i + back) % tp_count) for i in range(tp_c...  45.8 us
    ppermute x10, waiting for transfers between devices, from_chip(): lax.ppermute(value, 'ep', [(i, (i + step) % ep_count) for i in range(ep_c...  31.7 us
    ppermute x10, starting transfers between devices, from_chip(): lax.ppermute(value, 'ep', [(i, (i + step) % ep_count) for i in range(ep_c...  13.8 us
    unnamed x28, local copies, waits for them, and re-layouts  12.3 us
    ppermute x9, starting transfers between devices, from_tp(): lax.ppermute(value, 'tp', [(i, (i + back) % tp_count) for i in range(tp_c...  11.4 us
    pallas_call x1, Pallas kernels, run_expert(): pl.pallas_call(functools.partial(expert_kernel, row_blocks, column_blocks...  11.2 us
    pallas_call x1, Pallas kernels, attend(): pl.pallas_call(functools.partial(attention_kernel, step_rows), out_shape=...  8.49 us
    ppermute x20, waiting for transfers between devices, from_core(): return lax.ppermute(value, 'ep', [(i, i ^ 1) for i in range(ep_count)])  5.34 us
  transfers between devices with their start and end apart: 39, of which 19 were waited for; matrix products, arithmetic and copies ran while one was open for 1% of the time, Pallas kernels for 0%

profile of v1, /device:TPU:0, one launch (start us, length us, event | category | flops | bytes accessed | tf_op | source)
XLA Modules:
  0.0 149.3 jit_solution(15637584204996457352)
XLA Ops:
  0.6 1.0 reshape.10.qr_ref
  1.6 5.8 %copy-done = bf16[64,256,512]{2,1,0:T(8,128)(2,1)S(1)} copy-done((bf16[64,256,512]{2,1,0:T(8,128)(2,1)S(1)}, bf16[64,256,512]{2,1,0:T(8,128)(2,1)}, u32[]{:S(2)}) %copy-start) | copy-done | bytes 16777240
  7.4 1.6 %copy-done.2 = bf16[64,64,256]{2,1,0:T(8,128)(2,1)S(1)} copy-done((bf16[64,64,256]{2,1,0:T(8,128)(2,1)S(1)}, bf16[64,64,256]{2,1,0:T(8,128)(2,1)}, u32[]{:S(2)}) %copy-start.2) | copy-done | bytes 2097176
  9.0 1.2 copy-done.3
  10.2 1.0 copy-done.5
  11.2 0.7 copy-done.6
  11.9 8.5 %attention.1.refs_0_ = bf16[64,1024]{1,0:T(8,128)(2,1)S(1)} custom-call(s32[64]{0:T(128)S(1)} %copy-done.6, bf16[64,8,512]{2,1,0:T(8,128)(2,1)S(1)} %copy-done.5, bf16[64,8,64]{2,1,0:T(8,128)(2,1)S(1)} %reshape.10.qr_ref, bf16[64,256,512]{2,1,0:T(8,128)(2,1)S(1)} %copy-done, bf16[64,64,256]{2,1,0:T(8,128)(2,1)S(1)} %copy-done.2, ...), custom_call_target="tpu_custom_call" | custom-call | tf_op jit(solution)/shard_map/attention/pallas_call | solution.py:59
  20.4 3.0 %collective-permute-start.1 = (bf16[64,1024]{1,0:T(8,128)(2,1)S(1)}, bf16[64,1024]{1,0:T(8,128)(2,1)S(1)}, u32[]{:S(2)}, u32[]{:S(2)}) collective-permute-start(bf16[64,1024]{1,0:T(8,128)(2,1)S(1)} %attention.1.refs_0_), channel_id=1, source_target_pairs={{0,8},{4,12},{8,0},{12,4},{1,9},{5,13},{9,1},{13,5},{2,10},{6,14},... | collective-permute-start | bytes 393224 | tf_op jit(solution)/shard_map/ppermute | solution.py:238
  23.4 3.5 %collective-permute-done.1.refs_2_ = bf16[64,1024]{1,0:T(8,128)(2,1)S(1)} collective-permute-done((bf16[64,1024]{1,0:T(8,128)(2,1)S(1)}, bf16[64,1024]{1,0:T(8,128)(2,1)S(1)}, u32[]{:S(2)}, u32[]{:S(2)}) %collective-permute-start.1) | collective-permute-done | bytes 131104 | tf_op jit(solution)/shard_map/ppermute | solution.py:238
  27.0 1.3 collective-permute-done.2.refs_3_
  28.3 2.0 %copy-done.1 = bf16[1024,1792]{1,0:T(8,128)(2,1)S(1)} copy-done((bf16[1024,1792]{1,0:T(8,128)(2,1)S(1)}, bf16[1024,1792]{1,0:T(8,128)(2,1)}, u32[]{:S(2)}) %copy-start.1) | copy-done | bytes 3670040
  30.3 1.8 %projection.1 = (bf16[64,1792]{1,0:T(8,128)(2,1)S(1)}, bf16[64,1792]{1,0:T(8,128)(2,1)S(1)}, bf16[64,1792]{1,0:T(8,128)(2,1)S(1)}, bf16[64,1792]{1,0:T(8,128)(2,1)S(1)}) custom-call(s32[8]{0:T(128)S(1)} %stack.35.places, bf16[64,1024]{1,0:T(8,128)(2,1)S(1)} %attention.1.refs_0_, bf16[64,1024]{1,0:T(8,128)(2,1)S(1)} %collective-permute-done.refs_1_, ...), custom_call_target="tpu_custom_call" | custom-call | tf_op jit(solution)/shard_map/projection/pallas_call | solution.py:104
  32.1 3.9 %collective-permute-start.3 = (bf16[64,1792]{1,0:T(8,128)(2,1)S(1)}, bf16[64,1792]{1,0:T(8,128)(2,1)S(1)}, u32[]{:S(2)}, u32[]{:S(2)}) collective-permute-start(bf16[64,1792]{1,0:T(8,128)(2,1)S(1)} %get-tuple-element.23), channel_id=1, source_target_pairs={{0,3},{1,0},{2,1},{3,2},{4,7},{5,4},{6,5},{7,6},{8,11},{9,8},{10,9... | collective-permute-start | bytes 688136 | tf_op jit(solution)/shard_map/ppermute | solution.py:241
  36.0 1.0 collective-permute-start.5
  37.0 1.6 %collective-permute-start.22 = (f32[1,1792]{1,0:T(1,128)S(1)}, f32[1,1792]{1,0:T(1,128)S(1)}, u32[]{:S(2)}, u32[]{:S(2)}) collective-permute-start(f32[1,1792]{1,0:T(1,128)S(1)} %reshape.11.refs_16_), channel_id=1, source_target_pairs={{0,8},{4,12},{8,0},{12,4},{1,9},{5,13},{9,1},{13,5},{2,10},{6,14},... | collective-permute-start | bytes 21512 | tf_op jit(solution)/shard_map/ppermute | solution.py:238
  38.6 2.1 %collective-permute-done.22.refs_18_ = f32[1,1792]{1,0:T(1,128)S(1)} collective-permute-done((f32[1,1792]{1,0:T(1,128)S(1)}, f32[1,1792]{1,0:T(1,128)S(1)}, u32[]{:S(2)}, u32[]{:S(2)}) %collective-permute-start.22) | collective-permute-done | bytes 7200 | tf_op jit(solution)/shard_map/ppermute | solution.py:238
  40.7 1.3 collective-permute-done.3
  42.0 13.8 %collective-permute-done.4 = bf16[64,1792]{1,0:T(8,128)(2,1)S(1)} collective-permute-done((bf16[64,1792]{1,0:T(8,128)(2,1)S(1)}, bf16[64,1792]{1,0:T(8,128)(2,1)S(1)}, u32[]{:S(2)}, u32[]{:S(2)}) %collective-permute-start.4) | collective-permute-done | bytes 229408 | tf_op jit(solution)/shard_map/ppermute | solution.py:241
  55.8 1.1 add_convert_fusion.13.refs_0_
  56.9 2.9 %collective-permute-start.13 = (bf16[64,1792]{1,0:T(8,128)(2,1)S(1)}, bf16[64,1792]{1,0:T(8,128)(2,1)S(1)}, u32[]{:S(2)}, u32[]{:S(2)}) collective-permute-start(bf16[64,1792]{1,0:T(8,128)(2,1)S(1)} %add_convert_fusion.13.refs_0_), channel_id=1, source_target_pairs={{0,2},{1,3},{2,0},{3,1},{4,6},{5,7},{6,4},{7,5},{8,10},{9,11},{10,... | collective-permute-start | bytes 688136 | tf_op jit(solution)/shard_map/ppermute | solution.py:241
  59.8 1.9 %collective-permute-start.9 = (bf16[64,1792]{1,0:T(8,128)(2,1)S(1)}, bf16[64,1792]{1,0:T(8,128)(2,1)S(1)}, u32[]{:S(2)}, u32[]{:S(2)}) collective-permute-start(bf16[64,1792]{1,0:T(8,128)(2,1)S(1)} %add_convert_fusion.13.refs_0_), channel_id=1, source_target_pairs={{0,1},{1,2},{2,3},{3,0},{4,5},{5,6},{6,7},{7,4},{8,9},{9,10},{10,1... | collective-permute-start | bytes 688136 | tf_op jit(solution)/shard_map/ppermute | solution.py:241
  61.8 1.5 %collective-permute-start.7 = (bf16[64,1792]{1,0:T(8,128)(2,1)S(1)}, bf16[64,1792]{1,0:T(8,128)(2,1)S(1)}, u32[]{:S(2)}, u32[]{:S(2)}) collective-permute-start(bf16[64,1792]{1,0:T(8,128)(2,1)S(1)} %add_convert_fusion.13.refs_0_), channel_id=1, source_target_pairs={{0,8},{4,12},{8,0},{12,4},{1,9},{5,13},{9,1},{13,5},{2,10},{6,14},... | collective-permute-start | bytes 688136 | tf_op jit(solution)/shard_map/ppermute | solution.py:238
  63.3 0.9 collective-permute-done.17.refs_12_
  64.2 1.5 collective-permute-start.19
  65.7 13.8 %collective-permute-done.13.refs_8_ = bf16[64,1792]{1,0:T(8,128)(2,1)S(1)} collective-permute-done((bf16[64,1792]{1,0:T(8,128)(2,1)S(1)}, bf16[64,1792]{1,0:T(8,128)(2,1)S(1)}, u32[]{:S(2)}, u32[]{:S(2)}) %collective-permute-start.13) | collective-permute-done | bytes 229408 | tf_op jit(solution)/shard_map/ppermute | solution.py:241
  79.5 1.5 %collective-permute-start.15 = (bf16[64,1792]{1,0:T(8,128)(2,1)S(1)}, bf16[64,1792]{1,0:T(8,128)(2,1)S(1)}, u32[]{:S(2)}, u32[]{:S(2)}) collective-permute-start(bf16[64,1792]{1,0:T(8,128)(2,1)S(1)} %collective-permute-done.13.refs_8_), channel_id=1, source_target_pairs={{0,8},{4,12},{8,0},{12,4},{1,9},{5,13},{9,1},{13,5},{2,10},{6,14},... | collective-permute-start | bytes 688136 | tf_op jit(solution)/shard_map/ppermute | solution.py:238
  81.3 0.5 collective-permute-start.11
  81.8 0.5 collective-permute-start.8
  82.3 5.6 %collective-permute-done.15.refs_10_ = bf16[64,1792]{1,0:T(8,128)(2,1)S(1)} collective-permute-done((bf16[64,1792]{1,0:T(8,128)(2,1)S(1)}, bf16[64,1792]{1,0:T(8,128)(2,1)S(1)}, u32[]{:S(2)}, u32[]{:S(2)}) %collective-permute-start.15) | collective-permute-done | bytes 229408 | tf_op jit(solution)/shard_map/ppermute | solution.py:238
  87.9 0.5 collective-permute-start.16
  88.4 4.0 %collective-permute-done.11.refs_6_ = bf16[64,1792]{1,0:T(8,128)(2,1)S(1)} collective-permute-done((bf16[64,1792]{1,0:T(8,128)(2,1)S(1)}, bf16[64,1792]{1,0:T(8,128)(2,1)S(1)}, u32[]{:S(2)}, u32[]{:S(2)}) %collective-permute-start.11) | collective-permute-done | bytes 229408 | tf_op jit(solution)/shard_map/ppermute | solution.py:238
  92.7 1.3 collective-permute-done.12.refs_7_
  94.0 11.2 %expert.1 = (bf16[64,1792]{1,0:T(8,128)(2,1)S(1)}, bf16[64,1792]{1,0:T(8,128)(2,1)S(1)}, bf16[64,1792]{1,0:T(8,128)(2,1)S(1)}, bf16[64,1792]{1,0:T(8,128)(2,1)S(...) custom-call(s32[8]{0:T(128)S(1)} %stack.35.places, ...), custom_call_target="tpu_custom_call" | custom-call | tf_op jit(solution)/shard_map/expert/pallas_call | solution.py:183
  105.9 0.4 collective-permute-start.28
  106.9 0.8 collective-permute-done.28
  108.0 0.4 collective-permute-done.32
  108.6 1.2 collective-permute-done.36
  109.9 1.5 %collective-permute-start.29 = (bf16[64,1792]{1,0:T(8,128)(2,1)S(1)}, bf16[64,1792]{1,0:T(8,128)(2,1)S(1)}, u32[]{:S(2)}, u32[]{:S(2)}) collective-permute-start(bf16[64,1792]{1,0:T(8,128)(2,1)S(1)} %add_convert_fusion.8), channel_id=1, source_target_pairs={{0,8},{4,12},{8,0},{12,4},{1,9},{5,13},{9,1},{13,5},{2,10},{6,14},... | collective-permute-start | bytes 688136 | tf_op jit(solution)/shard_map/ppermute | solution.py:238
  111.5 0.6 collective-permute-start.26
  112.0 6.3 %collective-permute-done.29 = bf16[64,1792]{1,0:T(8,128)(2,1)S(1)} collective-permute-done((bf16[64,1792]{1,0:T(8,128)(2,1)S(1)}, bf16[64,1792]{1,0:T(8,128)(2,1)S(1)}, u32[]{:S(2)}, u32[]{:S(2)}) %collective-permute-start.29) | collective-permute-done | bytes 229408 | tf_op jit(solution)/shard_map/ppermute | solution.py:238
  118.3 1.5 %collective-permute-start.33 = (bf16[64,1792]{1,0:T(8,128)(2,1)S(1)}, bf16[64,1792]{1,0:T(8,128)(2,1)S(1)}, u32[]{:S(2)}, u32[]{:S(2)}) collective-permute-start(bf16[64,1792]{1,0:T(8,128)(2,1)S(1)} %add_convert_fusion.5), channel_id=1, source_target_pairs={{0,8},{4,12},{8,0},{12,4},{1,9},{5,13},{9,1},{13,5},{2,10},{6,14},... | collective-permute-start | bytes 688136 | tf_op jit(solution)/shard_map/ppermute | solution.py:238
  119.9 0.6 collective-permute-start.37
  120.5 7.6 %collective-permute-done.33 = bf16[64,1792]{1,0:T(8,128)(2,1)S(1)} collective-permute-done((bf16[64,1792]{1,0:T(8,128)(2,1)S(1)}, bf16[64,1792]{1,0:T(8,128)(2,1)S(1)}, u32[]{:S(2)}, u32[]{:S(2)}) %collective-permute-start.33) | collective-permute-done | bytes 229408 | tf_op jit(solution)/shard_map/ppermute | solution.py:238
  128.3 1.6 %collective-permute-start.34 = (bf16[64,1792]{1,0:T(8,128)(2,1)S(1)}, bf16[64,1792]{1,0:T(8,128)(2,1)S(1)}, u32[]{:S(2)}, u32[]{:S(2)}) collective-permute-start(bf16[64,1792]{1,0:T(8,128)(2,1)S(1)} %add_convert_fusion.4), channel_id=1, source_target_pairs={{0,2},{1,3},{2,0},{3,1},{4,6},{5,7},{6,4},{7,5},{8,10},{9,11},{10,... | collective-permute-start | bytes 688136 | tf_op jit(solution)/shard_map/ppermute | solution.py:241
  129.8 2.5 %collective-permute-done.37 = bf16[64,1792]{1,0:T(8,128)(2,1)S(1)} collective-permute-done((bf16[64,1792]{1,0:T(8,128)(2,1)S(1)}, bf16[64,1792]{1,0:T(8,128)(2,1)S(1)}, u32[]{:S(2)}, u32[]{:S(2)}) %collective-permute-start.37) | collective-permute-done | bytes 229408 | tf_op jit(solution)/shard_map/ppermute | solution.py:238
  132.5 2.8 %collective-permute-done.30 = bf16[64,1792]{1,0:T(8,128)(2,1)S(1)} collective-permute-done((bf16[64,1792]{1,0:T(8,128)(2,1)S(1)}, bf16[64,1792]{1,0:T(8,128)(2,1)S(1)}, u32[]{:S(2)}, u32[]{:S(2)}) %collective-permute-start.30) | collective-permute-done | bytes 229408 | tf_op jit(solution)/shard_map/ppermute | solution.py:241
  135.3 13.2 %collective-permute-done.34 = bf16[64,1792]{1,0:T(8,128)(2,1)S(1)} collective-permute-done((bf16[64,1792]{1,0:T(8,128)(2,1)S(1)}, bf16[64,1792]{1,0:T(8,128)(2,1)S(1)}, u32[]{:S(2)}, u32[]{:S(2)}) %collective-permute-start.34) | collective-permute-done | bytes 229408 | tf_op jit(solution)/shard_map/ppermute | solution.py:241
  148.5 0.9 add_convert_fusion
  (75 shorter events, 2.9 us)
Async XLA Ops:
  1.6 5.8 %copy-start = (bf16[64,256,512]{2,1,0:T(8,128)(2,1)S(1)}, bf16[64,256,512]{2,1,0:T(8,128)(2,1)}, u32[]{:S(2)}) copy-start(bf16[64,256,512]{2,1,0:T(8,128)(2,1)} %k_ref.1) | copy-start | bytes 50331652
  11.9 25.1 %copy-start.11 = (f32[1792]{0:T(1024)S(1)}, f32[1792]{0:T(1024)}, u32[]{:S(2)}) copy-start(f32[1792]{0:T(1024)} %param.22) | copy-start | bytes 21508
  11.9 80.6 %copy-start.12 = (f32[256,2]{0,1:T(2,128)S(1)}, f32[256,2]{0,1:T(2,128)}, u32[]{:S(2)}) copy-start(f32[256,2]{0,1:T(2,128)} %param.24) | copy-start | bytes 6148
  11.9 80.6 %copy-start.13 = (s32[256,2]{0,1:T(2,128)S(1)}, s32[256,2]{0,1:T(2,128)}, u32[]{:S(2)}) copy-start(s32[256,2]{0,1:T(2,128)} %param.23) | copy-start | bytes 6148
  20.4 6.5 %collective-permute-start.1 = (bf16[64,1024]{1,0:T(8,128)(2,1)S(1)}, bf16[64,1024]{1,0:T(8,128)(2,1)S(1)}, u32[]{:S(2)}, u32[]{:S(2)}) collective-permute-start(bf16[64,1024]{1,0:T(8,128)(2,1)S(1)} %attention.1.refs_0_), channel_id=1, source_target_pairs={{0,8},{4,12},{8,0},{12,4},{1,9},{5,13},{9,1},{13,5},{2,10},{6,14},... | collective-permute-start | bytes 393224 | tf_op jit(solution)/shard_map/ppermute | solution.py:238
  23.4 3.6 %collective-permute-start = (bf16[64,1024]{1,0:T(8,128)(2,1)S(1)}, bf16[64,1024]{1,0:T(8,128)(2,1)S(1)}, u32[]{:S(2)}, u32[]{:S(2)}) collective-permute-start(bf16[64,1024]{1,0:T(8,128)(2,1)S(1)} %attention.1.refs_0_), channel_id=1, source_target_pairs={{0,4},{4,0},{8,12},{12,8},{1,5},{5,1},{9,13},{13,9},{2,6},{6,2},{1... | collective-permute-start | bytes 393224 | tf_op jit(solution)/shard_map/ppermute | solution.py:234
  26.9 1.3 collective-permute-start.2
  32.1 10.0 %collective-permute-start.3 = (bf16[64,1792]{1,0:T(8,128)(2,1)S(1)}, bf16[64,1792]{1,0:T(8,128)(2,1)S(1)}, u32[]{:S(2)}, u32[]{:S(2)}) collective-permute-start(bf16[64,1792]{1,0:T(8,128)(2,1)S(1)} %get-tuple-element.23), channel_id=1, source_target_pairs={{0,3},{1,0},{2,1},{3,2},{4,7},{5,4},{6,5},{7,6},{8,11},{9,8},{10,9... | collective-permute-start | bytes 688136 | tf_op jit(solution)/shard_map/ppermute | solution.py:241
  36.0 19.8 %collective-permute-start.4 = (bf16[64,1792]{1,0:T(8,128)(2,1)S(1)}, bf16[64,1792]{1,0:T(8,128)(2,1)S(1)}, u32[]{:S(2)}, u32[]{:S(2)}) collective-permute-start(bf16[64,1792]{1,0:T(8,128)(2,1)S(1)} %get-tuple-element.24), channel_id=1, source_target_pairs={{0,2},{1,3},{2,0},{3,1},{4,6},{5,7},{6,4},{7,5},{8,10},{9,11},{10,... | collective-permute-start | bytes 688136 | tf_op jit(solution)/shard_map/ppermute | solution.py:241
  36.0 19.8 %collective-permute-start.5 = (bf16[64,1792]{1,0:T(8,128)(2,1)S(1)}, bf16[64,1792]{1,0:T(8,128)(2,1)S(1)}, u32[]{:S(2)}, u32[]{:S(2)}) collective-permute-start(bf16[64,1792]{1,0:T(8,128)(2,1)S(1)} %get-tuple-element.25), channel_id=1, source_target_pairs={{0,1},{1,2},{2,3},{3,0},{4,5},{5,6},{6,7},{7,4},{8,9},{9,10},{10,1... | collective-permute-start | bytes 688136 | tf_op jit(solution)/shard_map/ppermute | solution.py:241
  37.0 3.7 %collective-permute-start.22 = (f32[1,1792]{1,0:T(1,128)S(1)}, f32[1,1792]{1,0:T(1,128)S(1)}, u32[]{:S(2)}, u32[]{:S(2)}) collective-permute-start(f32[1,1792]{1,0:T(1,128)S(1)} %reshape.11.refs_16_), channel_id=1, source_target_pairs={{0,8},{4,12},{8,0},{12,4},{1,9},{5,13},{9,1},{13,5},{2,10},{6,14},... | collective-permute-start | bytes 21512 | tf_op jit(solution)/shard_map/ppermute | solution.py:238
  38.6 23.2 %collective-permute-start.21 = (f32[1,1792]{1,0:T(1,128)S(1)}, f32[1,1792]{1,0:T(1,128)S(1)}, u32[]{:S(2)}, u32[]{:S(2)}) collective-permute-start(f32[1,1792]{1,0:T(1,128)S(1)} %reshape.11.refs_16_), channel_id=1, source_target_pairs={{0,4},{4,0},{8,12},{12,8},{1,5},{5,1},{9,13},{13,9},{2,6},{6,2},{1... | collective-permute-start | bytes 21512 | tf_op jit(solution)/shard_map/ppermute | solution.py:234
  40.7 22.6 %collective-permute-start.23 = (f32[1,1792]{1,0:T(1,128)S(1)}, f32[1,1792]{1,0:T(1,128)S(1)}, u32[]{:S(2)}, u32[]{:S(2)}) collective-permute-start(f32[1,1792]{1,0:T(1,128)S(1)} %collective-permute-done.22.refs_18_), channel_id=1, source_target_pairs={{0,4},{4,0},{8,12},{12,8},{1,5},{5,1},{9,13},{13,9},{2,6},{6,2},{1... | collective-permute-start | bytes 21512 | tf_op jit(solution)/shard_map/ppermute | solution.py:234
  56.9 48.3 %copy-start.4 = (bf16[64,1792]{1,0:T(8,128)(2,1)}, bf16[64,1792]{1,0:T(8,128)(2,1)S(1)}, u32[]{:S(2)}) copy-start(bf16[64,1792]{1,0:T(8,128)(2,1)S(1)} %add_convert_fusion.13.refs_0_) | copy-start | bytes 688132
  56.9 7.3 %collective-permute-start.17 = (bf16[64,1792]{1,0:T(8,128)(2,1)S(1)}, bf16[64,1792]{1,0:T(8,128)(2,1)S(1)}, u32[]{:S(2)}, u32[]{:S(2)}) collective-permute-start(bf16[64,1792]{1,0:T(8,128)(2,1)S(1)} %add_convert_fusion.13.refs_0_), channel_id=1, source_target_pairs={{0,3},{1,0},{2,1},{3,2},{4,7},{5,4},{6,5},{7,6},{8,11},{9,8},{10,9... | collective-permute-start | bytes 688136 | tf_op jit(solution)/shard_map/ppermute | solution.py:241
  56.9 22.6 %collective-permute-start.13 = (bf16[64,1792]{1,0:T(8,128)(2,1)S(1)}, bf16[64,1792]{1,0:T(8,128)(2,1)S(1)}, u32[]{:S(2)}, u32[]{:S(2)}) collective-permute-start(bf16[64,1792]{1,0:T(8,128)(2,1)S(1)} %add_convert_fusion.13.refs_0_), channel_id=1, source_target_pairs={{0,2},{1,3},{2,0},{3,1},{4,6},{5,7},{6,4},{7,5},{8,10},{9,11},{10,... | collective-permute-start | bytes 688136 | tf_op jit(solution)/shard_map/ppermute | solution.py:241
  59.8 19.7 %collective-permute-start.9 = (bf16[64,1792]{1,0:T(8,128)(2,1)S(1)}, bf16[64,1792]{1,0:T(8,128)(2,1)S(1)}, u32[]{:S(2)}, u32[]{:S(2)}) collective-permute-start(bf16[64,1792]{1,0:T(8,128)(2,1)S(1)} %add_convert_fusion.13.refs_0_), channel_id=1, source_target_pairs={{0,1},{1,2},{2,3},{3,0},{4,5},{5,6},{6,7},{7,4},{8,9},{9,10},{10,1... | collective-permute-start | bytes 688136 | tf_op jit(solution)/shard_map/ppermute | solution.py:241
  61.8 19.3 %collective-permute-start.7 = (bf16[64,1792]{1,0:T(8,128)(2,1)S(1)}, bf16[64,1792]{1,0:T(8,128)(2,1)S(1)}, u32[]{:S(2)}, u32[]{:S(2)}) collective-permute-start(bf16[64,1792]{1,0:T(8,128)(2,1)S(1)} %add_convert_fusion.13.refs_0_), channel_id=1, source_target_pairs={{0,8},{4,12},{8,0},{12,4},{1,9},{5,13},{9,1},{13,5},{2,10},{6,14},... | collective-permute-start | bytes 688136 | tf_op jit(solution)/shard_map/ppermute | solution.py:238
  63.3 18.0 %collective-permute-start.6 = (bf16[64,1792]{1,0:T(8,128)(2,1)S(1)}, bf16[64,1792]{1,0:T(8,128)(2,1)S(1)}, u32[]{:S(2)}, u32[]{:S(2)}) collective-permute-start(bf16[64,1792]{1,0:T(8,128)(2,1)S(1)} %add_convert_fusion.13.refs_0_), channel_id=1, source_target_pairs={{0,4},{4,0},{8,12},{12,8},{1,5},{5,1},{9,13},{13,9},{2,6},{6,2},{1... | collective-permute-start | bytes 688136 | tf_op jit(solution)/shard_map/ppermute | solution.py:234
  64.2 29.7 %copy-start.7 = (bf16[64,1792]{1,0:T(8,128)(2,1)}, bf16[64,1792]{1,0:T(8,128)(2,1)S(1)}, u32[]{:S(2)}) copy-start(bf16[64,1792]{1,0:T(8,128)(2,1)S(1)} %collective-permute-done.17.refs_12_) | copy-start | bytes 688132
  64.2 17.6 %collective-permute-start.19 = (bf16[64,1792]{1,0:T(8,128)(2,1)S(1)}, bf16[64,1792]{1,0:T(8,128)(2,1)S(1)}, u32[]{:S(2)}, u32[]{:S(2)}) collective-permute-start(bf16[64,1792]{1,0:T(8,128)(2,1)S(1)} %collective-permute-done.17.refs_12_), channel_id=1, source_target_pairs={{0,8},{4,12},{8,0},{12,4},{1,9},{5,13},{9,1},{13,5},{2,10},{6,14},... | collective-permute-start | bytes 688136 | tf_op jit(solution)/shard_map/ppermute | solution.py:238
  79.5 2.3 %collective-permute-start.18 = (bf16[64,1792]{1,0:T(8,128)(2,1)S(1)}, bf16[64,1792]{1,0:T(8,128)(2,1)S(1)}, u32[]{:S(2)}, u32[]{:S(2)}) collective-permute-start(bf16[64,1792]{1,0:T(8,128)(2,1)S(1)} %collective-permute-done.17.refs_12_), channel_id=1, source_target_pairs={{0,4},{4,0},{8,12},{12,8},{1,5},{5,1},{9,13},{13,9},{2,6},{6,2},{1... | collective-permute-start | bytes 688136 | tf_op jit(solution)/shard_map/ppermute | solution.py:234
  79.5 8.4 %collective-permute-start.15 = (bf16[64,1792]{1,0:T(8,128)(2,1)S(1)}, bf16[64,1792]{1,0:T(8,128)(2,1)S(1)}, u32[]{:S(2)}, u32[]{:S(2)}) collective-permute-start(bf16[64,1792]{1,0:T(8,128)(2,1)S(1)} %collective-permute-done.13.refs_8_), channel_id=1, source_target_pairs={{0,8},{4,12},{8,0},{12,4},{1,9},{5,13},{9,1},{13,5},{2,10},{6,14},... | collective-permute-start | bytes 688136 | tf_op jit(solution)/shard_map/ppermute | solution.py:238
  81.0 6.9 %collective-permute-start.14 = (bf16[64,1792]{1,0:T(8,128)(2,1)S(1)}, bf16[64,1792]{1,0:T(8,128)(2,1)S(1)}, u32[]{:S(2)}, u32[]{:S(2)}) collective-permute-start(bf16[64,1792]{1,0:T(8,128)(2,1)S(1)} %collective-permute-done.13.refs_8_), channel_id=1, source_target_pairs={{0,4},{4,0},{8,12},{12,8},{1,5},{5,1},{9,13},{13,9},{2,6},{6,2},{1... | collective-permute-start | bytes 688136 | tf_op jit(solution)/shard_map/ppermute | solution.py:234
  81.3 11.2 %collective-permute-start.11 = (bf16[64,1792]{1,0:T(8,128)(2,1)S(1)}, bf16[64,1792]{1,0:T(8,128)(2,1)S(1)}, u32[]{:S(2)}, u32[]{:S(2)}) collective-permute-start(bf16[64,1792]{1,0:T(8,128)(2,1)S(1)} %collective-permute-done.9.refs_4_), channel_id=1, source_target_pairs={{0,8},{4,12},{8,0},{12,4},{1,9},{5,13},{9,1},{13,5},{2,10},{6,14},... | collective-permute-start | bytes 688136 | tf_op jit(solution)/shard_map/ppermute | solution.py:238
  81.8 12.2 %copy-start.8 = (bf16[64,1792]{1,0:T(8,128)(2,1)}, bf16[64,1792]{1,0:T(8,128)(2,1)S(1)}, u32[]{:S(2)}) copy-start(bf16[64,1792]{1,0:T(8,128)(2,1)S(1)} %collective-permute-done.19.refs_14_) | copy-start | bytes 688132
  81.8 10.8 %collective-permute-start.10 = (bf16[64,1792]{1,0:T(8,128)(2,1)S(1)}, bf16[64,1792]{1,0:T(8,128)(2,1)S(1)}, u32[]{:S(2)}, u32[]{:S(2)}) collective-permute-start(bf16[64,1792]{1,0:T(8,128)(2,1)S(1)} %collective-permute-done.9.refs_4_), channel_id=1, source_target_pairs={{0,4},{4,0},{8,12},{12,8},{1,5},{5,1},{9,13},{13,9},{2,6},{6,2},{1... | collective-permute-start | bytes 688136 | tf_op jit(solution)/shard_map/ppermute | solution.py:234
  81.8 12.1 %copy-start.9 = (bf16[64,1792]{1,0:T(8,128)(2,1)}, bf16[64,1792]{1,0:T(8,128)(2,1)S(1)}, u32[]{:S(2)}) copy-start(bf16[64,1792]{1,0:T(8,128)(2,1)S(1)} %collective-permute-done.18.refs_13_) | copy-start | bytes 688132
  81.8 10.8 %collective-permute-start.8 = (bf16[64,1792]{1,0:T(8,128)(2,1)S(1)}, bf16[64,1792]{1,0:T(8,128)(2,1)S(1)}, u32[]{:S(2)}, u32[]{:S(2)}) collective-permute-start(bf16[64,1792]{1,0:T(8,128)(2,1)S(1)} %collective-permute-done.7.refs_2_), channel_id=1, source_target_pairs={{0,4},{4,0},{8,12},{12,8},{1,5},{5,1},{9,13},{13,9},{2,6},{6,2},{1... | collective-permute-start | bytes 688136 | tf_op jit(solution)/shard_map/ppermute | solution.py:234
  87.9 6.0 %copy-start.10 = (bf16[64,1792]{1,0:T(8,128)(2,1)}, bf16[64,1792]{1,0:T(8,128)(2,1)S(1)}, u32[]{:S(2)}) copy-start(bf16[64,1792]{1,0:T(8,128)(2,1)S(1)} %collective-permute-done.15.refs_10_) | copy-start | bytes 688132
  87.9 4.7 %collective-permute-start.20 = (bf16[64,1792]{1,0:T(8,128)(2,1)S(1)}, bf16[64,1792]{1,0:T(8,128)(2,1)}, u32[]{:S(2)}, u32[]{:S(2)}) collective-permute-start(bf16[64,1792]{1,0:T(8,128)(2,1)S(1)} %collective-permute-done.19.refs_14_), channel_id=1, source_target_pairs={{0,4},{4,0},{8,12},{12,8},{1,5},{5,1},{9,13},{13,9},{2,6},{6,2},{1... | collective-permute-start | bytes 688136 | tf_op jit(solution)/shard_map/ppermute | solution.py:234
  87.9 4.7 %collective-permute-start.16 = (bf16[64,1792]{1,0:T(8,128)(2,1)S(1)}, bf16[64,1792]{1,0:T(8,128)(2,1)}, u32[]{:S(2)}, u32[]{:S(2)}) collective-permute-start(bf16[64,1792]{1,0:T(8,128)(2,1)S(1)} %collective-permute-done.15.refs_10_), channel_id=1, source_target_pairs={{0,4},{4,0},{8,12},{12,8},{1,5},{5,1},{9,13},{13,9},{2,6},{6,2},{1... | collective-permute-start | bytes 688136 | tf_op jit(solution)/shard_map/ppermute | solution.py:234
  92.5 1.5 collective-permute-start.12
  105.2 1.6 %collective-permute-start.25 = (bf16[64,1792]{1,0:T(8,128)(2,1)S(1)}, bf16[64,1792]{1,0:T(8,128)(2,1)S(1)}, u32[]{:S(2)}, u32[]{:S(2)}) collective-permute-start(bf16[64,1792]{1,0:T(8,128)(2,1)S(1)} %get-tuple-element.29), channel_id=1, source_target_pairs={{0,4},{4,0},{8,12},{12,8},{1,5},{5,1},{9,13},{13,9},{2,6},{6,2},{1... | collective-permute-start | bytes 688136 | tf_op jit(solution)/shard_map/ppermute | solution.py:234
  105.4 27.1 %collective-permute-start.24 = (bf16[64,1792]{1,0:T(8,128)(2,1)S(1)}, bf16[64,1792]{1,0:T(8,128)(2,1)S(1)}, u32[]{:S(2)}, u32[]{:S(2)}) collective-permute-start(bf16[64,1792]{1,0:T(8,128)(2,1)S(1)} %get-tuple-element.27), channel_id=1, source_target_pairs={{0,4},{4,0},{8,12},{12,8},{1,5},{5,1},{9,13},{13,9},{2,6},{6,2},{1... | collective-permute-start | bytes 688136 | tf_op jit(solution)/shard_map/ppermute | solution.py:234
  105.8 5.7 %collective-permute-start.27 = (bf16[64,1792]{1,0:T(8,128)(2,1)S(1)}, bf16[64,1792]{1,0:T(8,128)(2,1)S(1)}, u32[]{:S(2)}, u32[]{:S(2)}) collective-permute-start(bf16[64,1792]{1,0:T(8,128)(2,1)S(1)} %get-tuple-element.31), channel_id=1, source_target_pairs={{0,4},{4,0},{8,12},{12,8},{1,5},{5,1},{9,13},{13,9},{2,6},{6,2},{1... | collective-permute-start | bytes 688136 | tf_op jit(solution)/shard_map/ppermute | solution.py:234
  105.9 1.8 %collective-permute-start.28 = (bf16[64,1792]{1,0:T(8,128)(2,1)S(1)}, bf16[64,1792]{1,0:T(8,128)(2,1)S(1)}, u32[]{:S(2)}, u32[]{:S(2)}) collective-permute-start(bf16[64,1792]{1,0:T(8,128)(2,1)S(1)} %get-tuple-element.33), channel_id=1, source_target_pairs={{0,4},{4,0},{8,12},{12,8},{1,5},{5,1},{9,13},{13,9},{2,6},{6,2},{1... | collective-permute-start | bytes 688136 | tf_op jit(solution)/shard_map/ppermute | solution.py:234
  106.3 13.7 %collective-permute-start.31 = (bf16[64,1792]{1,0:T(8,128)(2,1)S(1)}, bf16[64,1792]{1,0:T(8,128)(2,1)S(1)}, u32[]{:S(2)}, u32[]{:S(2)}) collective-permute-start(bf16[64,1792]{1,0:T(8,128)(2,1)S(1)} %get-tuple-element.35), channel_id=1, source_target_pairs={{0,4},{4,0},{8,12},{12,8},{1,5},{5,1},{9,13},{13,9},{2,6},{6,2},{1... | collective-permute-start | bytes 688136 | tf_op jit(solution)/shard_map/ppermute | solution.py:234
  106.7 1.6 %collective-permute-start.32 = (bf16[64,1792]{1,0:T(8,128)(2,1)S(1)}, bf16[64,1792]{1,0:T(8,128)(2,1)S(1)}, u32[]{:S(2)}, u32[]{:S(2)}) collective-permute-start(bf16[64,1792]{1,0:T(8,128)(2,1)S(1)} %get-tuple-element.37), channel_id=1, source_target_pairs={{0,4},{4,0},{8,12},{12,8},{1,5},{5,1},{9,13},{13,9},{2,6},{6,2},{1... | collective-permute-start | bytes 688136 | tf_op jit(solution)/shard_map/ppermute | solution.py:234
  107.7 20.5 %collective-permute-start.35 = (bf16[64,1792]{1,0:T(8,128)(2,1)S(1)}, bf16[64,1792]{1,0:T(8,128)(2,1)S(1)}, u32[]{:S(2)}, u32[]{:S(2)}) collective-permute-start(bf16[64,1792]{1,0:T(8,128)(2,1)S(1)} %get-tuple-element.39), channel_id=1, source_target_pairs={{0,4},{4,0},{8,12},{12,8},{1,5},{5,1},{9,13},{13,9},{2,6},{6,2},{1... | collective-permute-start | bytes 688136 | tf_op jit(solution)/shard_map/ppermute | solution.py:234
  108.4 1.5 collective-permute-start.36
  109.9 8.4 %collective-permute-start.29 = (bf16[64,1792]{1,0:T(8,128)(2,1)S(1)}, bf16[64,1792]{1,0:T(8,128)(2,1)S(1)}, u32[]{:S(2)}, u32[]{:S(2)}) collective-permute-start(bf16[64,1792]{1,0:T(8,128)(2,1)S(1)} %add_convert_fusion.8), channel_id=1, source_target_pairs={{0,8},{4,12},{8,0},{12,4},{1,9},{5,13},{9,1},{13,5},{2,10},{6,14},... | collective-permute-start | bytes 688136 | tf_op jit(solution)/shard_map/ppermute | solution.py:238
  111.5 21.0 %collective-permute-start.26 = (bf16[64,1792]{1,0:T(8,128)(2,1)S(1)}, bf16[64,1792]{1,0:T(8,128)(2,1)S(1)}, u32[]{:S(2)}, u32[]{:S(2)}) collective-permute-start(bf16[64,1792]{1,0:T(8,128)(2,1)S(1)} %add_convert_fusion.11), channel_id=1, source_target_pairs={{0,8},{4,12},{8,0},{12,4},{1,9},{5,13},{9,1},{13,5},{2,10},{6,14},... | collective-permute-start | bytes 688136 | tf_op jit(solution)/shard_map/ppermute | solution.py:238
  118.3 9.8 %collective-permute-start.33 = (bf16[64,1792]{1,0:T(8,128)(2,1)S(1)}, bf16[64,1792]{1,0:T(8,128)(2,1)S(1)}, u32[]{:S(2)}, u32[]{:S(2)}) collective-permute-start(bf16[64,1792]{1,0:T(8,128)(2,1)S(1)} %add_convert_fusion.5), channel_id=1, source_target_pairs={{0,8},{4,12},{8,0},{12,4},{1,9},{5,13},{9,1},{13,5},{2,10},{6,14},... | collective-permute-start | bytes 688136 | tf_op jit(solution)/shard_map/ppermute | solution.py:238
  119.9 12.4 %collective-permute-start.37 = (bf16[64,1792]{1,0:T(8,128)(2,1)S(1)}, bf16[64,1792]{1,0:T(8,128)(2,1)S(1)}, u32[]{:S(2)}, u32[]{:S(2)}) collective-permute-start(bf16[64,1792]{1,0:T(8,128)(2,1)S(1)} %add_convert_fusion.2), channel_id=1, source_target_pairs={{0,8},{4,12},{8,0},{12,4},{1,9},{5,13},{9,1},{13,5},{2,10},{6,14},... | collective-permute-start | bytes 688136 | tf_op jit(solution)/shard_map/ppermute | solution.py:238
  128.1 7.2 %collective-permute-start.30 = (bf16[64,1792]{1,0:T(8,128)(2,1)S(1)}, bf16[64,1792]{1,0:T(8,128)(2,1)S(1)}, u32[]{:S(2)}, u32[]{:S(2)}) collective-permute-start(bf16[64,1792]{1,0:T(8,128)(2,1)S(1)} %add_convert_fusion.7), channel_id=1, source_target_pairs={{0,3},{1,0},{2,1},{3,2},{4,7},{5,4},{6,5},{7,6},{8,11},{9,8},{10,9... | collective-permute-start | bytes 688136 | tf_op jit(solution)/shard_map/ppermute | solution.py:241
  128.3 20.2 %collective-permute-start.34 = (bf16[64,1792]{1,0:T(8,128)(2,1)S(1)}, bf16[64,1792]{1,0:T(8,128)(2,1)S(1)}, u32[]{:S(2)}, u32[]{:S(2)}) collective-permute-start(bf16[64,1792]{1,0:T(8,128)(2,1)S(1)} %add_convert_fusion.4), channel_id=1, source_target_pairs={{0,2},{1,3},{2,0},{3,1},{4,6},{5,7},{6,4},{7,5},{8,10},{9,11},{10,... | collective-permute-start | bytes 688136 | tf_op jit(solution)/shard_map/ppermute | solution.py:241
  132.4 16.1 %collective-permute-start.38 = (bf16[64,1792]{1,0:T(8,128)(2,1)S(1)}, bf16[64,1792]{1,0:T(8,128)(2,1)S(1)}, u32[]{:S(2)}, u32[]{:S(2)}) collective-permute-start(bf16[64,1792]{1,0:T(8,128)(2,1)S(1)} %add_convert_fusion.1), channel_id=1, source_target_pairs={{0,1},{1,2},{2,3},{3,0},{4,5},{5,6},{6,7},{7,4},{8,9},{9,10},{10,1... | collective-permute-start | bytes 688136 | tf_op jit(solution)/shard_map/ppermute | solution.py:241
  (5 other events, 6.6 us)

commit v2 on v1

v2 whole, which is shorter than its diff:
```python
import functools

import jax
import jax.numpy as jnp
from jax import lax
from jax.experimental import pallas as pl
from jax.experimental.pallas import tpu as pltpu
from jax.sharding import PartitionSpec as P

score_scale = 1.0 / 192.0**0.5
norm_epsilon = 1e-06
MIB = 1 << 20


def attention_kernel(step_rows, lengths, q_hbm, qr_hbm, k_hbm, kr_hbm, up_hbm, out_ref, *scratch):
    q, qr, k, kr, up, rope, latent, sems, key_sems = scratch
    rows = k.shape[0]
    positions, latent_width = k.shape[1:]
    rope_width = kr.shape[1]
    heads = q.shape[0] // rows
    steps = rows // step_rows
    copies = [
        pltpu.make_async_copy(source, target, sems.at[i])
        for i, (source, target) in enumerate(((qr_hbm, qr), (q_hbm, q), (up_hbm, up)))
    ]

    def key_copies(step):
        cut = pl.ds(step * step_rows, step_rows)
        return (
            pltpu.make_async_copy(k_hbm.at[cut], k.at[cut], key_sems.at[0, step]),
            pltpu.make_async_copy(kr_hbm.at[cut], kr.at[cut], key_sems.at[1, step]),
        )

    copies[0].start()
    copies[1].start()
    for step in range(steps):
        for copy in key_copies(step):
            copy.start()
    copies[2].start()

    copies[0].wait()
    lane = lax.broadcasted_iota(jnp.int32, (heads, heads * rope_width), 1)
    head = lax.broadcasted_iota(jnp.int32, (heads, heads * rope_width), 0)
    own = jnp.where(lane // rope_width == head, 1.0, 0.0)
    spread = (qr[...].astype(jnp.float32)[:, None, :] * own[None, :, :]).reshape(rows * heads, heads * rope_width)
    lane = lax.broadcasted_iota(jnp.int32, (heads * rope_width, rope_width), 0)
    column = lax.broadcasted_iota(jnp.int32, (heads * rope_width, rope_width), 1)
    fold = jnp.where(lane % rope_width == column, 1.0, 0.0).astype(jnp.bfloat16)
    rope[...] = jnp.dot(spread.astype(jnp.bfloat16), fold, preferred_element_type=jnp.float32).astype(jnp.bfloat16)
    copies[1].wait()

    place = lax.broadcasted_iota(jnp.int32, (heads, positions), 1)
    lanes = latent.shape[2]

    def attend_rows(step, carry):
        for copy in key_copies(step):
            copy.wait()
        scores = []
        for pair in range(step_rows // 2):
            first = step * step_rows + 2 * pair
            cut = pl.ds(pl.multiple_of(first * heads, 2 * heads), 2 * heads)
            for r in range(2):
                score = lax.dot_general(
                    q[cut, :], k[first + r], (((1,), (1,)), ((), ())), preferred_element_type=jnp.float32
                )
                score += jnp.dot(rope[cut, :], kr[first + r], preferred_element_type=jnp.float32)
                scores.append(score[r * heads : (r + 1) * heads, :])
        probabilities = []
        for r in range(step_rows):
            visible = place < lengths[step * step_rows + r]
            score = jnp.where(visible, scores[r] * score_scale, -jnp.inf)
            weight = jnp.exp(score - jnp.max(score, axis=-1, keepdims=True))
            total = jnp.sum(weight, axis=-1, keepdims=True)
            probabilities.append((weight / total).astype(jnp.bfloat16))
        for r in range(step_rows):
            row = step * step_rows + r
            mixed = jnp.dot(probabilities[r], k[row], preferred_element_type=jnp.float32)
            for c in range(latent.shape[0]):
                latent[c, pl.ds(pl.multiple_of(row * heads, heads), heads), :] = mixed[:, c * lanes : (c + 1) * lanes]
        return carry

    lax.fori_loop(0, steps, attend_rows, 0)
    copies[2].wait()
    width = up.shape[2]
    for h in range(heads):
        parts = [latent[c, pl.ds(h, rows, stride=heads), :] for c in range(latent.shape[0])]
        part = jnp.concatenate(parts, axis=1).astype(jnp.bfloat16)
        out_ref[:, h * width : (h + 1) * width] = jnp.dot(
            part, up[h], preferred_element_type=jnp.float32
        ).astype(jnp.bfloat16)


def attend(query_latent, query_rope, cache_latent, cache_rope, cache_length, value_up):
    rows, heads, latent_width = query_latent.shape
    step_rows = 16
    steps = rows // step_rows
    hbm = pl.BlockSpec(memory_space=pltpu.HBM)
    return pl.pallas_call(
        functools.partial(attention_kernel, step_rows),
        out_shape=jax.ShapeDtypeStruct((rows, heads * value_up.shape[2]), jnp.bfloat16),
        in_specs=[pl.BlockSpec(memory_space=pltpu.SMEM)] + [hbm] * 5,
        out_specs=pl.BlockSpec(memory_space=pltpu.VMEM),
        scratch_shapes=[
            pltpu.VMEM((rows * heads, latent_width), jnp.bfloat16),
            pltpu.VMEM(query_rope.shape, jnp.bfloat16),
            pltpu.VMEM(cache_latent.shape, jnp.bfloat16),
            pltpu.VMEM(cache_rope.shape, jnp.bfloat16),
            pltpu.VMEM(value_up.shape, jnp.bfloat16),
            pltpu.VMEM((rows * heads, cache_rope.shape[1]), jnp.bfloat16),
            pltpu.VMEM((latent_width // 128, rows * heads, 128), jnp.float32),
            pltpu.SemaphoreType.DMA((3,)),
            pltpu.SemaphoreType.DMA((2, steps)),
        ],
        compiler_params=pltpu.CompilerParams(vmem_limit_bytes=28 * MIB),
        name="attention",
    )(
        cache_length,
        query_latent.reshape(rows * heads, latent_width),
        query_rope,
        cache_latent,
        cache_rope,
        value_up,
    )


def projection_kernel(count, places, *refs):
    blocks, weight, outs = refs[:count], refs[count], refs[count + 1 : -2]
    gathered, result = refs[-2:]
    height = blocks[0].shape[0]
    for k in range(count):
        first = pl.multiple_of(places[k] * height, height)
        gathered[pl.ds(first, height), :] = blocks[k][...]
    columns = weight.shape[1]
    tile = 256 if columns % 256 == 0 else 128
    for j in range(columns // tile):
        result[:, j * tile : (j + 1) * tile] = jnp.dot(
            gathered[...], weight[:, j * tile : (j + 1) * tile], preferred_element_type=jnp.float32
        ).astype(jnp.bfloat16)
    out_height = outs[0].shape[0]
    for s in range(len(outs)):
        first = pl.multiple_of(places[count + s] * out_height, out_height)
        outs[s][...] = result[pl.ds(first, out_height), :]


def project(places, blocks, weight, out_count):
    count = len(blocks)
    height, depth = blocks[0].shape
    rows, columns = height * count, weight.shape[1]
    whole = pl.BlockSpec(memory_space=pltpu.VMEM)
    return pl.pallas_call(
        functools.partial(projection_kernel, count),
        out_shape=[jax.ShapeDtypeStruct((rows // out_count, columns), jnp.bfloat16)] * out_count,
        in_specs=[pl.BlockSpec(memory_space=pltpu.SMEM)] + [whole] * (count + 1),
        out_specs=[whole] * out_count,
        scratch_shapes=[
            pltpu.VMEM((rows, depth), jnp.bfloat16),
            pltpu.VMEM((rows, columns), jnp.bfloat16),
        ],
        compiler_params=pltpu.CompilerParams(vmem_limit_bytes=32 * MIB),
        name="projection",
    )(places, *blocks, weight)


def expert_kernel(row_blocks, column_blocks, cores, model_width, places, *refs):
    count = row_blocks * column_blocks
    blocks, gains = refs[:count], refs[count : count + column_blocks]
    row_weight, gate, up, down = refs[count + column_blocks : count + column_blocks + 4]
    outs = refs[count + column_blocks + 4 : -4]
    x, gate_sum, up_sum, active = refs[-4:]
    height, width = blocks[0].shape
    hidden = gate.shape[2]
    squares = [jnp.zeros((height, 1), jnp.float32) for _ in range(row_blocks)]
    tile = min(256, hidden)
    for k in range(column_blocks):
        for s in range(row_blocks):
            wide = blocks[s * column_blocks + k][...].astype(jnp.float32)
            squares[s] += jnp.sum(wide * wide, axis=-1, keepdims=True)
            x[k, s * height : (s + 1) * height, :] = (wide * gains[k][...]).astype(jnp.bfloat16)
        depth = pl.ds(pl.multiple_of(places[k] * width, 128), width)
        for total, weight in ((gate_sum, gate), (up_sum, up)):
            for j in range(hidden // tile):
                cut = slice(j * tile, (j + 1) * tile)
                product = jnp.dot(x[k], weight[0, depth, cut], preferred_element_type=jnp.float32)
                if k == 0:
                    total[:, cut] = product
                else:
                    total[:, cut] += product
    for s in range(row_blocks):
        rows = slice(s * height, (s + 1) * height)
        scale = lax.rsqrt(squares[s] / model_width + norm_epsilon)
        gate_part = gate_sum[rows, :] * scale
        up_part = up_sum[rows, :] * scale
        active[rows, :] = (gate_part / (1.0 + jnp.exp(-gate_part)) * up_part).astype(jnp.bfloat16)
    tile = 256 if width % 256 == 0 else 128
    weights = []
    for s in range(row_blocks):
        first = pl.multiple_of(places[column_blocks + s] * height, height)
        weights.append(row_weight[pl.ds(first, height), :])
    for c in reversed(range(cores)):
        for b in range(column_blocks // cores):
            start = pl.multiple_of(places[b * cores + c] * width, 128)
            for j in range(width // tile):
                cut = slice(j * tile, (j + 1) * tile)
                product = jnp.dot(
                    active[...], down[0, :, pl.ds(start + j * tile, tile)], preferred_element_type=jnp.float32
                )
                for s in range(row_blocks):
                    part = product[s * height : (s + 1) * height, :] * weights[s]
                    outs[s * cores + c][b * height : (b + 1) * height, cut] = part.astype(jnp.bfloat16)


def run_expert(places, blocks, gains, row_weight, gate_weight, up_weight, down_weight, cores):
    row_blocks, column_blocks = len(blocks), len(blocks[0])
    height, width = blocks[0][0].shape
    rows = row_blocks * height
    hidden = gate_weight.shape[2]
    whole = pl.BlockSpec(memory_space=pltpu.VMEM)
    count = row_blocks * column_blocks
    out = jax.ShapeDtypeStruct((height * (column_blocks // cores), width), jnp.bfloat16)
    outs = pl.pallas_call(
        functools.partial(expert_kernel, row_blocks, column_blocks, cores, gate_weight.shape[1]),
        out_shape=[out] * (row_blocks * cores),
        in_specs=[pl.BlockSpec(memory_space=pltpu.SMEM)] + [whole] * (count + column_blocks + 4),
        out_specs=[whole] * (row_blocks * cores),
        scratch_shapes=[
            pltpu.VMEM((column_blocks, rows, width), jnp.bfloat16),
            pltpu.VMEM((rows, hidden), jnp.float32),
            pltpu.VMEM((rows, hidden), jnp.float32),
            pltpu.VMEM((rows, hidden), jnp.bfloat16),
        ],
        compiler_params=pltpu.CompilerParams(vmem_limit_bytes=14 * MIB),
        name="expert",
    )(places, *[b for row in blocks for b in row], *gains, row_weight, gate_weight, up_weight, down_weight)
    return [outs[s * cores : (s + 1) * cores] for s in range(row_blocks)]


def add_kernel(groups, *refs):
    used = sum(len(g) for g in groups)
    outs = refs[-len(groups) :]
    at = 0
    for group, out in zip(groups, outs):
        total = None
        for first in group:
            value = refs[at][first : first + out.shape[0], :].astype(jnp.float32)
            total = value if total is None else total + value
            at += 1
        out[...] = total.astype(jnp.bfloat16)


def add(groups, height, after=()):
    values = [value for group in groups for value, _ in group]
    width = values[0].shape[1]
    whole = pl.BlockSpec(memory_space=pltpu.VMEM)
    return pl.pallas_call(
        functools.partial(add_kernel, [[first for _, first in group] for group in groups]),
        out_shape=[jax.ShapeDtypeStruct((height, width), jnp.bfloat16)] * len(groups),
        in_specs=[whole] * len(values) + [pl.BlockSpec(memory_space=pl.ANY)] * len(after),
        out_specs=[whole] * len(groups),
        compiler_params=pltpu.CompilerParams(vmem_limit_bytes=8 * MIB),
        name="add",
    )(*values, *after)


def shards(
    query_latent,
    query_rope,
    cache_latent,
    cache_rope,
    cache_length,
    value_up,
    output_weight,
    residual,
    norm_gain,
    routed_experts,
    expert_gates,
    gate_weight,
    up_weight,
    down_weight,
):
    ep_count = lax.axis_size("ep")
    tp_count = lax.axis_size("tp")
    ep_index = lax.axis_index("ep")
    tp_index = lax.axis_index("tp")
    row_total = routed_experts.shape[0]
    block_rows = row_total // tp_count
    cores = 2
    chips = ep_count // cores

    def from_core(value):
        return lax.ppermute(value, "ep", [(i, i ^ 1) for i in range(ep_count)])

    def from_chip(value, back):
        step = cores * back
        return lax.ppermute(value, "ep", [(i, (i + step) % ep_count) for i in range(ep_count)])

    def from_tp(value, back):
        return lax.ppermute(value, "tp", [(i, (i + back) % tp_count) for i in range(tp_count)])

    def gather_ep(value):
        same = [value] + [from_chip(value, b) for b in range(1, chips)]
        other = [from_core(v) for v in same]
        return [v for pair in zip(same, other) for v in pair]

    chip, core = ep_index // cores, ep_index % cores
    ep_places = [
        (chip - b + chips) % chips * cores + (core if c == 0 else 1 - core)
        for b in range(chips)
        for c in range(cores)
    ]
    tp_places = [(tp_index - b + tp_count) % tp_count for b in range(tp_count)]
    places = jnp.stack(ep_places + tp_places).astype(jnp.int32)

    gains = gather_ep(norm_gain.reshape(1, -1))
    row_weight = jnp.sum(jnp.where(routed_experts == ep_index, expert_gates, 0.0), axis=-1, keepdims=True)

    head_out = attend(query_latent, query_rope, cache_latent, cache_rope, cache_length, value_up)
    partial = project(places, gather_ep(head_out), output_weight, tp_count)
    arrived = [partial[0]] + [from_tp(partial[b], tp_count - b) for b in range(1, tp_count)]
    own_residual = lax.dynamic_slice_in_dim(residual, tp_index * block_rows, block_rows, 0)
    attention = sum(a.astype(jnp.float32) for a in arrived)
    stream = (own_residual.astype(jnp.float32) + attention).astype(jnp.bfloat16)

    near = [b for b in range(1, tp_count) if b != tp_count // 2]
    far = [b for b in range(1, tp_count) if b == tp_count // 2]
    rows_of = {0: stream}
    for b in near:
        rows_of[b] = from_tp(stream, b)
    if far:
        (again,) = add([[(stream, 0)]], block_rows, [rows_of[b] for b in near])
        for b in far:
            rows_of[b] = from_tp(again, b)
    blocks = [gather_ep(rows_of[b]) for b in range(tp_count)]
    outs = run_expert(places, blocks, gains, row_weight, gate_weight, up_weight, down_weight, cores)

    swapped = [from_core(out[1]) for out in outs]
    order = far + near + [0]
    kept, across = {}, {}
    for at, b in enumerate(order):
        before = across[order[at - 2]] if at >= 2 else []
        pair = [[(outs[b][0], c * block_rows), (swapped[b], c * block_rows)] for c in range(chips)]
        sums = add(pair, block_rows, before)
        kept[b] = sums[0]
        across[b] = [from_chip(sums[c], chips - c) for c in range(1, chips)]
    finals = []
    for b in far + near:
        (total,) = add([[(v, 0) for v in [kept[b]] + across[b]]], block_rows)
        finals.append(from_tp(total, tp_count - b))
    (mixed,) = add([[(v, 0) for v in [kept[0]] + across[0] + finals]], block_rows)
    return (stream, mixed)


def solution(mesh):
    return jax.shard_map(
        shards,
        mesh=mesh,
        in_specs=(
            P(("parts", "ep"), "tp", None),
            P(("parts", "ep"), "tp"),
            P(("parts", "ep"), None, None),
            P(("parts", "ep"), None, None),
            P(("parts", "ep")),
            P("tp", None, None),
            P("tp", "ep"),
            P("parts", "ep"),
            P("ep"),
            P("parts", None),
            P("parts", None),
            P("ep", None, "tp"),
            P("ep", None, "tp"),
            P("ep", "tp", None),
        ),
        out_specs=(P(("parts", "tp"), "ep"), P(("parts", "tp"), "ep")),
        check_vma=False,
    )
```

time: 150 us -> 153 us (1.020)
  local copies, waits for them, and re-layouts: 13.5 us -> 22.6 us
  waiting for transfers between devices: 82.9 us -> 76.8 us
  starting transfers between devices: 28.2 us -> 29.9 us
    unnamed x28, local copies, waits for them, and re-layouts: 12.3 us -> 22.4 us
    ppermute x10, waiting for transfers between devices: 31.7 us -> 25.8 us  [from_chip(): lax.ppermute(value, 'ep', [(i, (i + step) % ep_count) for i in range(ep_c...]
    pallas_call x1, Pallas kernels: 11.2 us -> 7.37 us  [run_expert(): pl.pallas_call(functools.partial(expert_kernel, row_blocks, column_blocks...]
    pallas_call x1, Pallas kernels: 8.49 us -> 10.3 us  [attend(): pl.pallas_call(functools.partial(attention_kernel, step_rows), out_shape=...]
    ppermute x20 -> x16, waiting for transfers between devices: 5.34 us -> 3.49 us  [from_core(): return lax.ppermute(value, 'ep', [(i, i ^ 1) for i in range(ep_count)])]
    ppermute x10, starting transfers between devices: 13.8 us -> 15.4 us  [from_chip(): lax.ppermute(value, 'ep', [(i, (i + step) % ep_count) for i in range(ep_c...]
    ppermute x9, waiting for transfers between devices: 45.8 us -> 47.5 us  [from_tp(): lax.ppermute(value, 'tp', [(i, (i + back) % tp_count) for i in range(tp_c...]
  transfers between devices with their start and end apart: 39 -> 35, of which waited for: 19 -> 18; matrix products, arithmetic and copies ran while one was open for 1% -> 0% of each run, Pallas kernels for 0% -> 0%
where the time goes in v2:
time: 153 us; the launch traced here: 152 us
  waiting for transfers between devices  76.8 us (50%)
  starting transfers between devices  29.9 us (20%)
  local copies, waits for them, and re-layouts  22.6 us (15%)
  Pallas kernels  20.9 us (14%)
    ppermute x9, waiting for transfers between devices, from_tp(): lax.ppermute(value, 'tp', [(i, (i + back) % tp_count) for i in range(tp_c...  47.5 us
    ppermute x10, waiting for transfers between devices, from_chip(): lax.ppermute(value, 'ep', [(i, (i + step) % ep_count) for i in range(ep_c...  25.8 us
    unnamed x28, local copies, waits for them, and re-layouts  22.4 us
    ppermute x10, starting transfers between devices, from_chip(): lax.ppermute(value, 'ep', [(i, (i + step) % ep_count) for i in range(ep_c...  15.4 us
    ppermute x9, starting transfers between devices, from_tp(): lax.ppermute(value, 'tp', [(i, (i + back) % tp_count) for i in range(tp_c...  12.1 us
    pallas_call x1, Pallas kernels, attend(): pl.pallas_call(functools.partial(attention_kernel, step_rows), out_shape=...  10.3 us
    pallas_call x1, Pallas kernels, run_expert(): pl.pallas_call(functools.partial(expert_kernel, row_blocks, column_blocks...  7.37 us
    ppermute x16, waiting for transfers between devices, from_core(): return lax.ppermute(value, 'ep', [(i, i ^ 1) for i in range(ep_count)])  3.49 us
  transfers between devices with their start and end apart: 35, of which 18 were waited for; matrix products, arithmetic and copies ran while one was open for 0% of the time, Pallas kernels for 0%

profile of v2, /device:TPU:0, one launch (start us, length us, event | category | flops | bytes accessed | tf_op | source)
XLA Modules:
  0.0 152.2 jit_solution(16082336496729727920)
XLA Ops:
  0.6 5.8 %copy-done = bf16[64,256,512]{2,1,0:T(8,128)(2,1)S(1)} copy-done((bf16[64,256,512]{2,1,0:T(8,128)(2,1)S(1)}, bf16[64,256,512]{2,1,0:T(8,128)(2,1)}, u32[]{:S(2)}) %copy-start) | copy-done | bytes 16777240
  6.4 1.6 %copy-done.5 = bf16[64,64,256]{2,1,0:T(8,128)(2,1)S(1)} copy-done((bf16[64,64,256]{2,1,0:T(8,128)(2,1)S(1)}, bf16[64,64,256]{2,1,0:T(8,128)(2,1)}, u32[]{:S(2)}) %copy-start.5) | copy-done | bytes 2097176
  8.0 1.2 copy-done.7
  9.2 1.0 copy-done.8
  10.3 0.8 copy-done.9
  11.1 0.7 copy-done.10
  11.8 10.3 %attention.1.refs_0_ = bf16[64,1024]{1,0:T(8,128)(2,1)S(1)} custom-call(s32[64]{0:T(128)S(1)} %copy-done.10, bf16[512,512]{1,0:T(8,128)(2,1)S(1)} %bitcast.10, bf16[64,512]{1,0:T(8,128)(2,1)S(1)} %copy-done.9, bf16[64,256,512]{2,1,0:T(8,128)(2,1)S(1)} %copy-done, bf16[64,64,256]{2,1,0:T(8,128)(2,1)S(1)} %copy-done.5, bf16[8,512,128]{2,1,0:T(8,128)(2,1)S(1)} %copy-done.7), custom_call_target="tpu_custom_call" | custom-call | tf_op jit(solution)/shard_map/attention/pallas_call | solution.py:98
  22.1 3.0 %collective-permute-start.1 = (bf16[64,1024]{1,0:T(8,128)(2,1)S(1)}, bf16[64,1024]{1,0:T(8,128)(2,1)S(1)}, u32[]{:S(2)}, u32[]{:S(2)}) collective-permute-start(bf16[64,1024]{1,0:T(8,128)(2,1)S(1)} %attention.1.refs_0_), channel_id=1, source_target_pairs={{0,8},{4,12},{8,0},{12,4},{1,9},{5,13},{9,1},{13,5},{2,10},{6,14},... | collective-permute-start | bytes 393224 | tf_op jit(solution)/shard_map/ppermute | solution.py:294
  25.1 3.5 %collective-permute-done.1.refs_2_ = bf16[64,1024]{1,0:T(8,128)(2,1)S(1)} collective-permute-done((bf16[64,1024]{1,0:T(8,128)(2,1)S(1)}, bf16[64,1024]{1,0:T(8,128)(2,1)S(1)}, u32[]{:S(2)}, u32[]{:S(2)}) %collective-permute-start.1) | collective-permute-done | bytes 131104 | tf_op jit(solution)/shard_map/ppermute | solution.py:294
  28.7 1.3 collective-permute-done.2.refs_3_
  30.0 2.0 %copy-done.4 = bf16[1024,1792]{1,0:T(8,128)(2,1)S(1)} copy-done((bf16[1024,1792]{1,0:T(8,128)(2,1)S(1)}, bf16[1024,1792]{1,0:T(8,128)(2,1)}, u32[]{:S(2)}) %copy-start.4) | copy-done | bytes 3670040
  32.0 1.8 %projection.1 = (bf16[64,1792]{1,0:T(8,128)(2,1)S(1)}, bf16[64,1792]{1,0:T(8,128)(2,1)S(1)}, bf16[64,1792]{1,0:T(8,128)(2,1)S(1)}, bf16[64,1792]{1,0:T(8,128)(2,1)S(1)}) custom-call(s32[8]{0:T(128)S(1)} %stack.35.places, bf16[64,1024]{1,0:T(8,128)(2,1)S(1)} %attention.1.refs_0_, bf16[64,1024]{1,0:T(8,128)(2,1)S(1)} %collective-permute-done.refs_1_, ...), custom_call_target="tpu_custom_call" | custom-call | tf_op jit(solution)/shard_map/projection/pallas_call | solution.py:150
  33.8 3.9 %collective-permute-start.3 = (bf16[64,1792]{1,0:T(8,128)(2,1)S(1)}, bf16[64,1792]{1,0:T(8,128)(2,1)S(1)}, u32[]{:S(2)}, u32[]{:S(2)}) collective-permute-start(bf16[64,1792]{1,0:T(8,128)(2,1)S(1)} %get-tuple-element.23), channel_id=1, source_target_pairs={{0,3},{1,0},{2,1},{3,2},{4,7},{5,4},{6,5},{7,6},{8,11},{9,8},{10,9... | collective-permute-start | bytes 688136 | tf_op jit(solution)/shard_map/ppermute | solution.py:297
  37.7 1.0 collective-permute-start.5
  38.7 5.0 %collective-permute-done.3 = bf16[64,1792]{1,0:T(8,128)(2,1)S(1)} collective-permute-done((bf16[64,1792]{1,0:T(8,128)(2,1)S(1)}, bf16[64,1792]{1,0:T(8,128)(2,1)S(1)}, u32[]{:S(2)}, u32[]{:S(2)}) %collective-permute-start.3) | collective-permute-done | bytes 229408 | tf_op jit(solution)/shard_map/ppermute | solution.py:297
  43.7 13.8 %collective-permute-done.4 = bf16[64,1792]{1,0:T(8,128)(2,1)S(1)} collective-permute-done((bf16[64,1792]{1,0:T(8,128)(2,1)S(1)}, bf16[64,1792]{1,0:T(8,128)(2,1)S(1)}, u32[]{:S(2)}, u32[]{:S(2)}) %collective-permute-start.4) | collective-permute-done | bytes 229408 | tf_op jit(solution)/shard_map/ppermute | solution.py:297
  57.5 1.1 add_convert_fusion.refs_0_
  58.7 2.0 %collective-permute-start.9 = (bf16[64,1792]{1,0:T(8,128)(2,1)S(1)}, bf16[64,1792]{1,0:T(8,128)(2,1)S(1)}, u32[]{:S(2)}, u32[]{:S(2)}) collective-permute-start(bf16[64,1792]{1,0:T(8,128)(2,1)S(1)} %add_convert_fusion.refs_0_), channel_id=1, source_target_pairs={{0,1},{1,2},{2,3},{3,0},{4,5},{5,6},{6,7},{7,4},{8,9},{9,10},{10,1... | collective-permute-start | bytes 688136 | tf_op jit(solution)/shard_map/ppermute | solution.py:297
  60.7 1.5 collective-permute-start.7
  62.2 3.3 %collective-permute-done.13.refs_2_.refs_12_ = bf16[64,1792]{1,0:T(8,128)(2,1)S(1)} collective-permute-done((bf16[64,1792]{1,0:T(8,128)(2,1)S(1)}, bf16[64,1792]{1,0:T(8,128)(2,1)S(1)}, u32[]{:S(2)}, u32[]{:S(2)}) %collective-permute-start.13) | collective-permute-done | bytes 229408 | tf_op jit(solution)/shard_map/ppermute | solution.py:297
  65.5 7.1 %collective-permute-done.9.refs_1_.refs_4_ = bf16[64,1792]{1,0:T(8,128)(2,1)S(1)} collective-permute-done((bf16[64,1792]{1,0:T(8,128)(2,1)S(1)}, bf16[64,1792]{1,0:T(8,128)(2,1)S(1)}, u32[]{:S(2)}, u32[]{:S(2)}) %collective-permute-start.9) | collective-permute-done | bytes 229408 | tf_op jit(solution)/shard_map/ppermute | solution.py:297
  72.7 1.6 %collective-permute-start.22 = (f32[1,1792]{1,0:T(1,128)S(1)}, f32[1,1792]{1,0:T(1,128)S(1)}, u32[]{:S(2)}, u32[]{:S(2)}) collective-permute-start(f32[1,1792]{1,0:T(1,128)S(1)} %reshape.11.refs_16_), channel_id=1, source_target_pairs={{0,8},{4,12},{8,0},{12,4},{1,9},{5,13},{9,1},{13,5},{2,10},{6,14},... | collective-permute-start | bytes 21512 | tf_op jit(solution)/shard_map/ppermute | solution.py:294
  74.3 2.1 %collective-permute-done.22.refs_18_ = f32[1,1792]{1,0:T(1,128)S(1)} collective-permute-done((f32[1,1792]{1,0:T(1,128)S(1)}, f32[1,1792]{1,0:T(1,128)S(1)}, u32[]{:S(2)}, u32[]{:S(2)}) %collective-permute-start.22) | collective-permute-done | bytes 7200 | tf_op jit(solution)/shard_map/ppermute | solution.py:294
  76.4 1.5 collective-permute-start.19
  78.1 1.1 collective-permute-start.11
  79.3 3.9 %collective-permute-done.14.refs_8_ = bf16[64,1792]{1,0:T(8,128)(2,1)S(1)} collective-permute-done((bf16[64,1792]{1,0:T(8,128)(2,1)S(1)}, bf16[64,1792]{1,0:T(8,128)(2,1)S(1)}, u32[]{:S(2)}, u32[]{:S(2)}) %collective-permute-start.14) | collective-permute-done | bytes 229408 | tf_op jit(solution)/shard_map/ppermute | solution.py:297
  83.2 1.5 collective-permute-start.16
  84.8 0.5 collective-permute-start.15
  85.3 4.4 %collective-permute-done.11.refs_6_ = bf16[64,1792]{1,0:T(8,128)(2,1)S(1)} collective-permute-done((bf16[64,1792]{1,0:T(8,128)(2,1)S(1)}, bf16[64,1792]{1,0:T(8,128)(2,1)S(1)}, u32[]{:S(2)}, u32[]{:S(2)}) %collective-permute-start.11) | collective-permute-done | bytes 229408 | tf_op jit(solution)/shard_map/ppermute | solution.py:294
  90.2 4.0 %collective-permute-done.16.refs_10_ = bf16[64,1792]{1,0:T(8,128)(2,1)S(1)} collective-permute-done((bf16[64,1792]{1,0:T(8,128)(2,1)S(1)}, bf16[64,1792]{1,0:T(8,128)(2,1)S(1)}, u32[]{:S(2)}, u32[]{:S(2)}) %collective-permute-start.16) | collective-permute-done | bytes 229408 | tf_op jit(solution)/shard_map/ppermute | solution.py:294
  94.5 1.4 collective-permute-done.17.refs_11_
  95.9 3.1 %copy-done.1 = bf16[1,7168,512]{2,1,0:T(8,128)(2,1)S(1)} copy-done((bf16[1,7168,512]{2,1,0:T(8,128)(2,1)S(1)}, bf16[1,7168,512]{2,1,0:T(8,128)(2,1)}, u32[]{:S(2)}) %copy-start.1) | copy-done | bytes 7340056
  99.0 3.1 %copy-done.2 = bf16[1,7168,512]{2,1,0:T(8,128)(2,1)S(1)} copy-done((bf16[1,7168,512]{2,1,0:T(8,128)(2,1)S(1)}, bf16[1,7168,512]{2,1,0:T(8,128)(2,1)}, u32[]{:S(2)}) %copy-start.2) | copy-done | bytes 7340056
  102.0 3.1 %copy-done.3 = bf16[1,512,7168]{2,1,0:T(8,128)(2,1)S(1)} copy-done((bf16[1,512,7168]{2,1,0:T(8,128)(2,1)S(1)}, bf16[1,512,7168]{2,1,0:T(8,128)(2,1)}, u32[]{:S(2)}) %copy-start.3) | copy-done | bytes 7340056
  105.1 7.4 %expert.1 = (bf16[128,1792]{1,0:T(8,128)(2,1)S(1)}, bf16[128,1792]{1,0:T(8,128)(2,1)S(1)}, bf16[128,1792]{1,0:T(8,128)(2,1)S(1)}, bf16[128,1792]{1,0:T(8,128)(2,...) custom-call(s32[8]{0:T(128)S(1)} %stack.35.places, ...), custom_call_target="tpu_custom_call" | custom-call | tf_op jit(solution)/shard_map/expert/pallas_call | solution.py:220
  113.6 0.8 collective-permute-done.28.refs_1_.refs_3_
  114.5 1.6 %collective-permute-start.29 = (bf16[64,1792]{1,0:T(8,128)(2,1)S(1)}, bf16[64,1792]{1,0:T(8,128)(2,1)S(1)}, u32[]{:S(2)}, u32[]{:S(2)}) collective-permute-start(bf16[64,1792]{1,0:T(8,128)(2,1)S(1)} %get-tuple-element.36), channel_id=1, source_target_pairs={{0,8},{4,12},{8,0},{12,4},{1,9},{5,13},{9,1},{13,5},{2,10},{6,14},... | collective-permute-start | bytes 688136 | tf_op jit(solution)/shard_map/ppermute | solution.py:294
  116.2 0.6 collective-permute-start.26
  116.8 6.2 %collective-permute-done.29.refs_1_.refs_4_ = bf16[64,1792]{1,0:T(8,128)(2,1)S(1)} collective-permute-done((bf16[64,1792]{1,0:T(8,128)(2,1)S(1)}, bf16[64,1792]{1,0:T(8,128)(2,1)S(1)}, u32[]{:S(2)}, u32[]{:S(2)}) %collective-permute-start.29) | collective-permute-done | bytes 229408 | tf_op jit(solution)/shard_map/ppermute | solution.py:294
  123.1 1.6 %collective-permute-start.33 = (bf16[64,1792]{1,0:T(8,128)(2,1)S(1)}, bf16[64,1792]{1,0:T(8,128)(2,1)S(1)}, u32[]{:S(2)}, u32[]{:S(2)}) collective-permute-start(bf16[64,1792]{1,0:T(8,128)(2,1)S(1)} %get-tuple-element.41), channel_id=1, source_target_pairs={{0,8},{4,12},{8,0},{12,4},{1,9},{5,13},{9,1},{13,5},{2,10},{6,14},... | collective-permute-start | bytes 688136 | tf_op jit(solution)/shard_map/ppermute | solution.py:294
  124.7 3.2 %collective-permute-done.26.refs_4_.refs_1_ = bf16[64,1792]{1,0:T(8,128)(2,1)S(1)} collective-permute-done((bf16[64,1792]{1,0:T(8,128)(2,1)S(1)}, bf16[64,1792]{1,0:T(8,128)(2,1)S(1)}, u32[]{:S(2)}, u32[]{:S(2)}) %collective-permute-start.26) | collective-permute-done | bytes 229408 | tf_op jit(solution)/shard_map/ppermute | solution.py:294
  128.0 1.6 %collective-permute-start.27 = (bf16[64,1792]{1,0:T(8,128)(2,1)S(1)}, bf16[64,1792]{1,0:T(8,128)(2,1)S(1)}, u32[]{:S(2)}, u32[]{:S(2)}) collective-permute-start(bf16[64,1792]{1,0:T(8,128)(2,1)S(1)} %get-tuple-element.32), channel_id=1, source_target_pairs={{0,8},{4,12},{8,0},{12,4},{1,9},{5,13},{9,1},{13,5},{2,10},{6,14},... | collective-permute-start | bytes 688136 | tf_op jit(solution)/shard_map/ppermute | solution.py:294
  129.7 0.5 collective-permute-start.31
  130.3 2.5 %collective-permute-start.30 = (bf16[64,1792]{1,0:T(8,128)(2,1)S(1)}, bf16[64,1792]{1,0:T(8,128)(2,1)S(1)}, u32[]{:S(2)}, u32[]{:S(2)}) collective-permute-start(bf16[64,1792]{1,0:T(8,128)(2,1)S(1)} %add.123), channel_id=1, source_target_pairs={{0,2},{1,3},{2,0},{3,1},{4,6},{5,7},{6,4},{7,5},{8,10},{9,11},{10,... | collective-permute-start | bytes 688136 | tf_op jit(solution)/shard_map/ppermute | solution.py:297
  132.9 2.0 %collective-permute-start.34 = (bf16[64,1792]{1,0:T(8,128)(2,1)S(1)}, bf16[64,1792]{1,0:T(8,128)(2,1)S(1)}, u32[]{:S(2)}, u32[]{:S(2)}) collective-permute-start(bf16[64,1792]{1,0:T(8,128)(2,1)S(1)} %add.126), channel_id=1, source_target_pairs={{0,1},{1,2},{2,3},{3,0},{4,5},{5,6},{6,7},{7,4},{8,9},{9,10},{10,1... | collective-permute-start | bytes 688136 | tf_op jit(solution)/shard_map/ppermute | solution.py:297
  134.9 2.1 %collective-permute-done.27.refs_1_ = bf16[64,1792]{1,0:T(8,128)(2,1)S(1)} collective-permute-done((bf16[64,1792]{1,0:T(8,128)(2,1)S(1)}, bf16[64,1792]{1,0:T(8,128)(2,1)S(1)}, u32[]{:S(2)}, u32[]{:S(2)}) %collective-permute-start.27) | collective-permute-done | bytes 229408 | tf_op jit(solution)/shard_map/ppermute | solution.py:294
  137.0 14.4 %collective-permute-done.30.refs_2_ = bf16[64,1792]{1,0:T(8,128)(2,1)S(1)} collective-permute-done((bf16[64,1792]{1,0:T(8,128)(2,1)S(1)}, bf16[64,1792]{1,0:T(8,128)(2,1)S(1)}, u32[]{:S(2)}, u32[]{:S(2)}) %collective-permute-start.30) | collective-permute-done | bytes 229408 | tf_op jit(solution)/shard_map/ppermute | solution.py:297
  151.4 0.8 add.127
  (67 shorter events, 3.2 us)
Async XLA Ops:
  0.6 5.8 %copy-start = (bf16[64,256,512]{2,1,0:T(8,128)(2,1)S(1)}, bf16[64,256,512]{2,1,0:T(8,128)(2,1)}, u32[]{:S(2)}) copy-start(bf16[64,256,512]{2,1,0:T(8,128)(2,1)} %k_hbm.1) | copy-start | bytes 50331652
  6.4 1.6 %copy-start.5 = (bf16[64,64,256]{2,1,0:T(8,128)(2,1)S(1)}, bf16[64,64,256]{2,1,0:T(8,128)(2,1)}, u32[]{:S(2)}) copy-start(bf16[64,64,256]{2,1,0:T(8,128)(2,1)} %kr_hbm.1) | copy-start | bytes 6291460
  8.0 1.2 copy-start.7
  9.2 1.0 copy-start.8
  10.3 0.8 copy-start.9
  11.8 60.9 %copy-start.11 = (f32[1792]{0:T(1024)S(1)}, f32[1792]{0:T(1024)}, u32[]{:S(2)}) copy-start(f32[1792]{0:T(1024)} %param.22) | copy-start | bytes 21508
  11.8 82.5 %copy-start.12 = (f32[256,2]{0,1:T(2,128)S(1)}, f32[256,2]{0,1:T(2,128)}, u32[]{:S(2)}) copy-start(f32[256,2]{0,1:T(2,128)} %param.24) | copy-start | bytes 6148
  11.8 82.5 %copy-start.13 = (s32[256,2]{0,1:T(2,128)S(1)}, s32[256,2]{0,1:T(2,128)}, u32[]{:S(2)}) copy-start(s32[256,2]{0,1:T(2,128)} %param.23) | copy-start | bytes 6148
  22.1 6.5 %collective-permute-start.1 = (bf16[64,1024]{1,0:T(8,128)(2,1)S(1)}, bf16[64,1024]{1,0:T(8,128)(2,1)S(1)}, u32[]{:S(2)}, u32[]{:S(2)}) collective-permute-start(bf16[64,1024]{1,0:T(8,128)(2,1)S(1)} %attention.1.refs_0_), channel_id=1, source_target_pairs={{0,8},{4,12},{8,0},{12,4},{1,9},{5,13},{9,1},{13,5},{2,10},{6,14},... | collective-permute-start | bytes 393224 | tf_op jit(solution)/shard_map/ppermute | solution.py:294
  25.1 3.6 %collective-permute-start = (bf16[64,1024]{1,0:T(8,128)(2,1)S(1)}, bf16[64,1024]{1,0:T(8,128)(2,1)S(1)}, u32[]{:S(2)}, u32[]{:S(2)}) collective-permute-start(bf16[64,1024]{1,0:T(8,128)(2,1)S(1)} %attention.1.refs_0_), channel_id=1, source_target_pairs={{0,4},{4,0},{8,12},{12,8},{1,5},{5,1},{9,13},{13,9},{2,6},{6,2},{1... | collective-permute-start | bytes 393224 | tf_op jit(solution)/shard_map/ppermute | solution.py:290
  28.6 1.3 collective-permute-start.2
  30.0 2.0 %copy-start.4 = (bf16[1024,1792]{1,0:T(8,128)(2,1)S(1)}, bf16[1024,1792]{1,0:T(8,128)(2,1)}, u32[]{:S(2)}) copy-start(bf16[1024,1792]{1,0:T(8,128)(2,1)} %refs_4_.1) | copy-start | bytes 11010052
  33.8 10.0 %collective-permute-start.3 = (bf16[64,1792]{1,0:T(8,128)(2,1)S(1)}, bf16[64,1792]{1,0:T(8,128)(2,1)S(1)}, u32[]{:S(2)}, u32[]{:S(2)}) collective-permute-start(bf16[64,1792]{1,0:T(8,128)(2,1)S(1)} %get-tuple-element.23), channel_id=1, source_target_pairs={{0,3},{1,0},{2,1},{3,2},{4,7},{5,4},{6,5},{7,6},{8,11},{9,8},{10,9... | collective-permute-start | bytes 688136 | tf_op jit(solution)/shard_map/ppermute | solution.py:297
  37.7 19.8 %collective-permute-start.4 = (bf16[64,1792]{1,0:T(8,128)(2,1)S(1)}, bf16[64,1792]{1,0:T(8,128)(2,1)S(1)}, u32[]{:S(2)}, u32[]{:S(2)}) collective-permute-start(bf16[64,1792]{1,0:T(8,128)(2,1)S(1)} %get-tuple-element.24), channel_id=1, source_target_pairs={{0,2},{1,3},{2,0},{3,1},{4,6},{5,7},{6,4},{7,5},{8,10},{9,11},{10,... | collective-permute-start | bytes 688136 | tf_op jit(solution)/shard_map/ppermute | solution.py:297
  37.7 19.8 %collective-permute-start.5 = (bf16[64,1792]{1,0:T(8,128)(2,1)S(1)}, bf16[64,1792]{1,0:T(8,128)(2,1)S(1)}, u32[]{:S(2)}, u32[]{:S(2)}) collective-permute-start(bf16[64,1792]{1,0:T(8,128)(2,1)S(1)} %get-tuple-element.25), channel_id=1, source_target_pairs={{0,1},{1,2},{2,3},{3,0},{4,5},{5,6},{6,7},{7,4},{8,9},{9,10},{10,1... | collective-permute-start | bytes 688136 | tf_op jit(solution)/shard_map/ppermute | solution.py:297
  58.6 53.9 %copy-start.6 = (bf16[64,1792]{1,0:T(8,128)(2,1)}, bf16[64,1792]{1,0:T(8,128)(2,1)S(1)}, u32[]{:S(2)}) copy-start(bf16[64,1792]{1,0:T(8,128)(2,1)S(1)} %add_convert_fusion.refs_0_) | copy-start | bytes 688132
  58.6 6.9 %collective-permute-start.13 = (bf16[64,1792]{1,0:T(8,128)(2,1)S(1)}, bf16[64,1792]{1,0:T(8,128)(2,1)S(1)}, u32[]{:S(2)}, u32[]{:S(2)}) collective-permute-start(bf16[64,1792]{1,0:T(8,128)(2,1)S(1)} %add_convert_fusion.refs_0_), channel_id=1, source_target_pairs={{0,3},{1,0},{2,1},{3,2},{4,7},{5,4},{6,5},{7,6},{8,11},{9,8},{10,9... | collective-permute-start | bytes 688136 | tf_op jit(solution)/shard_map/ppermute | solution.py:297
  58.7 13.9 %collective-permute-start.9 = (bf16[64,1792]{1,0:T(8,128)(2,1)S(1)}, bf16[64,1792]{1,0:T(8,128)(2,1)S(1)}, u32[]{:S(2)}, u32[]{:S(2)}) collective-permute-start(bf16[64,1792]{1,0:T(8,128)(2,1)S(1)} %add_convert_fusion.refs_0_), channel_id=1, source_target_pairs={{0,1},{1,2},{2,3},{3,0},{4,5},{5,6},{6,7},{7,4},{8,9},{9,10},{10,1... | collective-permute-start | bytes 688136 | tf_op jit(solution)/shard_map/ppermute | solution.py:297
  60.7 17.5 %collective-permute-start.7 = (bf16[64,1792]{1,0:T(8,128)(2,1)S(1)}, bf16[64,1792]{1,0:T(8,128)(2,1)S(1)}, u32[]{:S(2)}, u32[]{:S(2)}) collective-permute-start(bf16[64,1792]{1,0:T(8,128)(2,1)S(1)} %add_convert_fusion.refs_0_), channel_id=1, source_target_pairs={{0,8},{4,12},{8,0},{12,4},{1,9},{5,13},{9,1},{13,5},{2,10},{6,14},... | collective-permute-start | bytes 688136 | tf_op jit(solution)/shard_map/ppermute | solution.py:294
  62.2 17.1 %collective-permute-start.6 = (bf16[64,1792]{1,0:T(8,128)(2,1)S(1)}, bf16[64,1792]{1,0:T(8,128)(2,1)S(1)}, u32[]{:S(2)}, u32[]{:S(2)}) collective-permute-start(bf16[64,1792]{1,0:T(8,128)(2,1)S(1)} %add_convert_fusion.refs_0_), channel_id=1, source_target_pairs={{0,4},{4,0},{8,12},{12,8},{1,5},{5,1},{9,13},{13,9},{2,6},{6,2},{1... | collective-permute-start | bytes 688136 | tf_op jit(solution)/shard_map/ppermute | solution.py:290
  72.6 10.6 %collective-permute-start.14 = (bf16[64,1792]{1,0:T(8,128)(2,1)S(1)}, bf16[64,1792]{1,0:T(8,128)(2,1)S(1)}, u32[]{:S(2)}, u32[]{:S(2)}) collective-permute-start(bf16[64,1792]{1,0:T(8,128)(2,1)S(1)} %add.119), channel_id=1, source_target_pairs={{0,2},{1,3},{2,0},{3,1},{4,6},{5,7},{6,4},{7,5},{8,10},{9,11},{10,... | collective-permute-start | bytes 688136 | tf_op jit(solution)/shard_map/ppermute | solution.py:297
  72.7 3.7 %collective-permute-start.22 = (f32[1,1792]{1,0:T(1,128)S(1)}, f32[1,1792]{1,0:T(1,128)S(1)}, u32[]{:S(2)}, u32[]{:S(2)}) collective-permute-start(f32[1,1792]{1,0:T(1,128)S(1)} %reshape.11.refs_16_), channel_id=1, source_target_pairs={{0,8},{4,12},{8,0},{12,4},{1,9},{5,13},{9,1},{13,5},{2,10},{6,14},... | collective-permute-start | bytes 21512 | tf_op jit(solution)/shard_map/ppermute | solution.py:294
  74.3 2.1 %collective-permute-start.21 = (f32[1,1792]{1,0:T(1,128)S(1)}, f32[1,1792]{1,0:T(1,128)S(1)}, u32[]{:S(2)}, u32[]{:S(2)}) collective-permute-start(f32[1,1792]{1,0:T(1,128)S(1)} %reshape.11.refs_16_), channel_id=1, source_target_pairs={{0,4},{4,0},{8,12},{12,8},{1,5},{5,1},{9,13},{13,9},{2,6},{6,2},{1... | collective-permute-start | bytes 21512 | tf_op jit(solution)/shard_map/ppermute | solution.py:290
  76.4 1.5 collective-permute-start.23
  76.4 8.4 %collective-permute-start.19 = (bf16[64,1792]{1,0:T(8,128)(2,1)S(1)}, bf16[64,1792]{1,0:T(8,128)(2,1)S(1)}, u32[]{:S(2)}, u32[]{:S(2)}) collective-permute-start(bf16[64,1792]{1,0:T(8,128)(2,1)S(1)} %collective-permute-done.13.refs_2_.refs_12_), channel_id=1, source_target_pairs={{0,8},{4,12},{8,0},{12,4},{1,9},{5,13},{9,1},{13,5},{2,10},{6,14},... | collective-permute-start | bytes 688136 | tf_op jit(solution)/shard_map/ppermute | solution.py:294
  77.9 6.9 %collective-permute-start.18 = (bf16[64,1792]{1,0:T(8,128)(2,1)S(1)}, bf16[64,1792]{1,0:T(8,128)(2,1)S(1)}, u32[]{:S(2)}, u32[]{:S(2)}) collective-permute-start(bf16[64,1792]{1,0:T(8,128)(2,1)S(1)} %collective-permute-done.13.refs_2_.refs_12_), channel_id=1, source_target_pairs={{0,4},{4,0},{8,12},{12,8},{1,5},{5,1},{9,13},{13,9},{2,6},{6,2},{1... | collective-permute-start | bytes 688136 | tf_op jit(solution)/shard_map/ppermute | solution.py:290
  78.1 11.6 %collective-permute-start.11 = (bf16[64,1792]{1,0:T(8,128)(2,1)S(1)}, bf16[64,1792]{1,0:T(8,128)(2,1)S(1)}, u32[]{:S(2)}, u32[]{:S(2)}) collective-permute-start(bf16[64,1792]{1,0:T(8,128)(2,1)S(1)} %collective-permute-done.9.refs_1_.refs_4_), channel_id=1, source_target_pairs={{0,8},{4,12},{8,0},{12,4},{1,9},{5,13},{9,1},{13,5},{2,10},{6,14},... | collective-permute-start | bytes 688136 | tf_op jit(solution)/shard_map/ppermute | solution.py:294
  79.2 10.5 %collective-permute-start.10 = (bf16[64,1792]{1,0:T(8,128)(2,1)S(1)}, bf16[64,1792]{1,0:T(8,128)(2,1)S(1)}, u32[]{:S(2)}, u32[]{:S(2)}) collective-permute-start(bf16[64,1792]{1,0:T(8,128)(2,1)S(1)} %collective-permute-done.9.refs_1_.refs_4_), channel_id=1, source_target_pairs={{0,4},{4,0},{8,12},{12,8},{1,5},{5,1},{9,13},{13,9},{2,6},{6,2},{1... | collective-permute-start | bytes 688136 | tf_op jit(solution)/shard_map/ppermute | solution.py:290
  83.2 11.0 %collective-permute-start.16 = (bf16[64,1792]{1,0:T(8,128)(2,1)S(1)}, bf16[64,1792]{1,0:T(8,128)(2,1)S(1)}, u32[]{:S(2)}, u32[]{:S(2)}) collective-permute-start(bf16[64,1792]{1,0:T(8,128)(2,1)S(1)} %collective-permute-done.14.refs_8_), channel_id=1, source_target_pairs={{0,8},{4,12},{8,0},{12,4},{1,9},{5,13},{9,1},{13,5},{2,10},{6,14},... | collective-permute-start | bytes 688136 | tf_op jit(solution)/shard_map/ppermute | solution.py:294
  84.8 9.6 %collective-permute-start.8 = (bf16[64,1792]{1,0:T(8,128)(2,1)S(1)}, bf16[64,1792]{1,0:T(8,128)(2,1)S(1)}, u32[]{:S(2)}, u32[]{:S(2)}) collective-permute-start(bf16[64,1792]{1,0:T(8,128)(2,1)S(1)} %collective-permute-done.7.refs_2_), channel_id=1, source_target_pairs={{0,4},{4,0},{8,12},{12,8},{1,5},{5,1},{9,13},{13,9},{2,6},{6,2},{1... | collective-permute-start | bytes 688136 | tf_op jit(solution)/shard_map/ppermute | solution.py:290
  84.8 9.6 %collective-permute-start.15 = (bf16[64,1792]{1,0:T(8,128)(2,1)S(1)}, bf16[64,1792]{1,0:T(8,128)(2,1)S(1)}, u32[]{:S(2)}, u32[]{:S(2)}) collective-permute-start(bf16[64,1792]{1,0:T(8,128)(2,1)S(1)} %collective-permute-done.14.refs_8_), channel_id=1, source_target_pairs={{0,4},{4,0},{8,12},{12,8},{1,5},{5,1},{9,13},{13,9},{2,6},{6,2},{1... | collective-permute-start | bytes 688136 | tf_op jit(solution)/shard_map/ppermute | solution.py:290
  89.7 4.7 %collective-permute-start.20 = (bf16[64,1792]{1,0:T(8,128)(2,1)S(1)}, bf16[64,1792]{1,0:T(8,128)(2,1)S(1)}, u32[]{:S(2)}, u32[]{:S(2)}) collective-permute-start(bf16[64,1792]{1,0:T(8,128)(2,1)S(1)} %collective-permute-done.19.refs_14_), channel_id=1, source_target_pairs={{0,4},{4,0},{8,12},{12,8},{1,5},{5,1},{9,13},{13,9},{2,6},{6,2},{1... | collective-permute-start | bytes 688136 | tf_op jit(solution)/shard_map/ppermute | solution.py:290
  89.7 4.7 %collective-permute-start.12 = (bf16[64,1792]{1,0:T(8,128)(2,1)S(1)}, bf16[64,1792]{1,0:T(8,128)(2,1)}, u32[]{:S(2)}, u32[]{:S(2)}) collective-permute-start(bf16[64,1792]{1,0:T(8,128)(2,1)S(1)} %collective-permute-done.11.refs_6_), channel_id=1, source_target_pairs={{0,4},{4,0},{8,12},{12,8},{1,5},{5,1},{9,13},{13,9},{2,6},{6,2},{1... | collective-permute-start | bytes 688136 | tf_op jit(solution)/shard_map/ppermute | solution.py:290
  94.3 1.6 %collective-permute-start.17 = (bf16[64,1792]{1,0:T(8,128)(2,1)S(1)}, bf16[64,1792]{1,0:T(8,128)(2,1)}, u32[]{:S(2)}, u32[]{:S(2)}) collective-permute-start(bf16[64,1792]{1,0:T(8,128)(2,1)S(1)} %collective-permute-done.16.refs_10_), channel_id=1, source_target_pairs={{0,4},{4,0},{8,12},{12,8},{1,5},{5,1},{9,13},{13,9},{2,6},{6,2},{1... | collective-permute-start | bytes 688136 | tf_op jit(solution)/shard_map/ppermute | solution.py:290
  95.9 3.1 %copy-start.1 = (bf16[1,7168,512]{2,1,0:T(8,128)(2,1)S(1)}, bf16[1,7168,512]{2,1,0:T(8,128)(2,1)}, u32[]{:S(2)}) copy-start(bf16[1,7168,512]{2,1,0:T(8,128)(2,1)} %refs_21_.1) | copy-start | bytes 22020100
  99.0 3.1 %copy-start.2 = (bf16[1,7168,512]{2,1,0:T(8,128)(2,1)S(1)}, bf16[1,7168,512]{2,1,0:T(8,128)(2,1)}, u32[]{:S(2)}) copy-start(bf16[1,7168,512]{2,1,0:T(8,128)(2,1)} %refs_22_.1) | copy-start | bytes 22020100
  102.0 3.1 %copy-start.3 = (bf16[1,512,7168]{2,1,0:T(8,128)(2,1)S(1)}, bf16[1,512,7168]{2,1,0:T(8,128)(2,1)}, u32[]{:S(2)}) copy-start(bf16[1,512,7168]{2,1,0:T(8,128)(2,1)} %refs_23_.1) | copy-start | bytes 22020100
  112.5 1.9 %collective-permute-start.28 = (bf16[128,1792]{1,0:T(8,128)(2,1)S(1)}, bf16[128,1792]{1,0:T(8,128)(2,1)S(1)}, u32[]{:S(2)}, u32[]{:S(2)}) collective-permute-start(bf16[128,1792]{1,0:T(8,128)(2,1)S(1)} %get-tuple-element.34), channel_id=1, source_target_pairs={{0,4},{4,0},{8,12},{12,8},{1,5},{5,1},{9,13},{13,9},{2,6},{6,2},{1... | collective-permute-start | bytes 1376264 | tf_op jit(solution)/shard_map/ppermute | solution.py:290
  112.7 3.3 %collective-permute-start.25 = (bf16[128,1792]{1,0:T(8,128)(2,1)S(1)}, bf16[128,1792]{1,0:T(8,128)(2,1)S(1)}, u32[]{:S(2)}, u32[]{:S(2)}) collective-permute-start(bf16[128,1792]{1,0:T(8,128)(2,1)S(1)} %get-tuple-element.29), channel_id=1, source_target_pairs={{0,4},{4,0},{8,12},{12,8},{1,5},{5,1},{9,13},{13,9},{2,6},{6,2},{1... | collective-permute-start | bytes 1376264 | tf_op jit(solution)/shard_map/ppermute | solution.py:290
  113.1 3.7 %collective-permute-start.32 = (bf16[128,1792]{1,0:T(8,128)(2,1)S(1)}, bf16[128,1792]{1,0:T(8,128)(2,1)S(1)}, u32[]{:S(2)}, u32[]{:S(2)}) collective-permute-start(bf16[128,1792]{1,0:T(8,128)(2,1)S(1)} %get-tuple-element.39), channel_id=1, source_target_pairs={{0,4},{4,0},{8,12},{12,8},{1,5},{5,1},{9,13},{13,9},{2,6},{6,2},{1... | collective-permute-start | bytes 1376264 | tf_op jit(solution)/shard_map/ppermute | solution.py:290
  113.3 11.5 %collective-permute-start.24 = (bf16[128,1792]{1,0:T(8,128)(2,1)S(1)}, bf16[128,1792]{1,0:T(8,128)(2,1)S(1)}, u32[]{:S(2)}, u32[]{:S(2)}) collective-permute-start(bf16[128,1792]{1,0:T(8,128)(2,1)S(1)} %get-tuple-element.27), channel_id=1, source_target_pairs={{0,4},{4,0},{8,12},{12,8},{1,5},{5,1},{9,13},{13,9},{2,6},{6,2},{1... | collective-permute-start | bytes 1376264 | tf_op jit(solution)/shard_map/ppermute | solution.py:290
  114.5 8.5 %collective-permute-start.29 = (bf16[64,1792]{1,0:T(8,128)(2,1)S(1)}, bf16[64,1792]{1,0:T(8,128)(2,1)S(1)}, u32[]{:S(2)}, u32[]{:S(2)}) collective-permute-start(bf16[64,1792]{1,0:T(8,128)(2,1)S(1)} %get-tuple-element.36), channel_id=1, source_target_pairs={{0,8},{4,12},{8,0},{12,4},{1,9},{5,13},{9,1},{13,5},{2,10},{6,14},... | collective-permute-start | bytes 688136 | tf_op jit(solution)/shard_map/ppermute | solution.py:294
  116.2 11.7 %collective-permute-start.26 = (bf16[64,1792]{1,0:T(8,128)(2,1)S(1)}, bf16[64,1792]{1,0:T(8,128)(2,1)S(1)}, u32[]{:S(2)}, u32[]{:S(2)}) collective-permute-start(bf16[64,1792]{1,0:T(8,128)(2,1)S(1)} %get-tuple-element.30), channel_id=1, source_target_pairs={{0,8},{4,12},{8,0},{12,4},{1,9},{5,13},{9,1},{13,5},{2,10},{6,14},... | collective-permute-start | bytes 688136 | tf_op jit(solution)/shard_map/ppermute | solution.py:294
  123.1 9.7 %collective-permute-start.33 = (bf16[64,1792]{1,0:T(8,128)(2,1)S(1)}, bf16[64,1792]{1,0:T(8,128)(2,1)S(1)}, u32[]{:S(2)}, u32[]{:S(2)}) collective-permute-start(bf16[64,1792]{1,0:T(8,128)(2,1)S(1)} %get-tuple-element.41), channel_id=1, source_target_pairs={{0,8},{4,12},{8,0},{12,4},{1,9},{5,13},{9,1},{13,5},{2,10},{6,14},... | collective-permute-start | bytes 688136 | tf_op jit(solution)/shard_map/ppermute | solution.py:294
  128.0 8.9 %collective-permute-start.27 = (bf16[64,1792]{1,0:T(8,128)(2,1)S(1)}, bf16[64,1792]{1,0:T(8,128)(2,1)S(1)}, u32[]{:S(2)}, u32[]{:S(2)}) collective-permute-start(bf16[64,1792]{1,0:T(8,128)(2,1)S(1)} %get-tuple-element.32), channel_id=1, source_target_pairs={{0,8},{4,12},{8,0},{12,4},{1,9},{5,13},{9,1},{13,5},{2,10},{6,14},... | collective-permute-start | bytes 688136 | tf_op jit(solution)/shard_map/ppermute | solution.py:294
  129.7 7.3 %collective-permute-start.31 = (bf16[64,1792]{1,0:T(8,128)(2,1)S(1)}, bf16[64,1792]{1,0:T(8,128)(2,1)S(1)}, u32[]{:S(2)}, u32[]{:S(2)}) collective-permute-start(bf16[64,1792]{1,0:T(8,128)(2,1)S(1)} %add.124), channel_id=1, source_target_pairs={{0,3},{1,0},{2,1},{3,2},{4,7},{5,4},{6,5},{7,6},{8,11},{9,8},{10,9... | collective-permute-start | bytes 688136 | tf_op jit(solution)/shard_map/ppermute | solution.py:297
  130.3 21.1 %collective-permute-start.30 = (bf16[64,1792]{1,0:T(8,128)(2,1)S(1)}, bf16[64,1792]{1,0:T(8,128)(2,1)S(1)}, u32[]{:S(2)}, u32[]{:S(2)}) collective-permute-start(bf16[64,1792]{1,0:T(8,128)(2,1)S(1)} %add.123), channel_id=1, source_target_pairs={{0,2},{1,3},{2,0},{3,1},{4,6},{5,7},{6,4},{7,5},{8,10},{9,11},{10,... | collective-permute-start | bytes 688136 | tf_op jit(solution)/shard_map/ppermute | solution.py:297
  132.9 18.5 %collective-permute-start.34 = (bf16[64,1792]{1,0:T(8,128)(2,1)S(1)}, bf16[64,1792]{1,0:T(8,128)(2,1)S(1)}, u32[]{:S(2)}, u32[]{:S(2)}) collective-permute-start(bf16[64,1792]{1,0:T(8,128)(2,1)S(1)} %add.126), channel_id=1, source_target_pairs={{0,1},{1,2},{2,3},{3,0},{4,5},{5,6},{6,7},{7,4},{8,9},{9,10},{10,1... | collective-permute-start | bytes 688136 | tf_op jit(solution)/shard_map/ppermute | solution.py:297
  (1 other events, 0.7 us)

commit v3 on v2

--- a/solution.py
+++ b/solution.py
@@ -111,7 +111,10 @@
             pltpu.SemaphoreType.DMA((3,)),
             pltpu.SemaphoreType.DMA((2, steps)),
         ],
-        compiler_params=pltpu.CompilerParams(vmem_limit_bytes=28 * MIB),
+        cost_estimate=pl.CostEstimate(
+            flops=64 * heads * cache_latent.size, bytes_accessed=2 * cache_latent.size, transcendentals=0
+        ),
+        compiler_params=pltpu.CompilerParams(vmem_limit_bytes=58 * MIB),
         name="attention",
     )(
         cache_length,
@@ -123,8 +126,8 @@
     )
 
 
-def projection_kernel(count, places, *refs):
-    blocks, weight, outs = refs[:count], refs[count], refs[count + 1 : -2]
+def projection_kernel(count, out_count, places, *refs):
+    blocks, weight, outs = refs[:count], refs[count], refs[-2 - out_count : -2]
     gathered, result = refs[-2:]
     height = blocks[0].shape[0]
     for k in range(count):
@@ -142,23 +145,42 @@
         outs[s][...] = result[pl.ds(first, out_height), :]
 
 
-def project(places, blocks, weight, out_count):
+def project(places, blocks, weight, out_count, after):
     count = len(blocks)
     height, depth = blocks[0].shape
     rows, columns = height * count, weight.shape[1]
     whole = pl.BlockSpec(memory_space=pltpu.VMEM)
     return pl.pallas_call(
-        functools.partial(projection_kernel, count),
+        functools.partial(projection_kernel, count, out_count),
         out_shape=[jax.ShapeDtypeStruct((rows // out_count, columns), jnp.bfloat16)] * out_count,
-        in_specs=[pl.BlockSpec(memory_space=pltpu.SMEM)] + [whole] * (count + 1),
+        in_specs=[pl.BlockSpec(memory_space=pltpu.SMEM)]
+        + [whole] * (count + 1)
+        + [pl.BlockSpec(memory_space=pl.ANY)] * len(after),
         out_specs=[whole] * out_count,
         scratch_shapes=[
             pltpu.VMEM((rows, depth), jnp.bfloat16),
             pltpu.VMEM((rows, columns), jnp.bfloat16),
         ],
-        compiler_params=pltpu.CompilerParams(vmem_limit_bytes=32 * MIB),
+        cost_estimate=pl.CostEstimate(flops=2 * rows * depth * columns, bytes_accessed=4 * MIB, transcendentals=0),
+        compiler_params=pltpu.CompilerParams(vmem_limit_bytes=8 * MIB),
         name="projection",
-    )(places, *blocks, weight)
+    )(places, *blocks, weight, *after)
+
+
+def touch_kernel(*refs):
+    refs[-1][...] = jnp.zeros(refs[-1].shape, jnp.float32)
+
+
+def touch(values, after):
+    return pl.pallas_call(
+        touch_kernel,
+        out_shape=jax.ShapeDtypeStruct((8, 128), jnp.float32),
+        in_specs=[pl.BlockSpec(memory_space=pltpu.VMEM)] * len(values)
+        + [pl.BlockSpec(memory_space=pl.ANY)] * len(after),
+        out_specs=pl.BlockSpec(memory_space=pltpu.VMEM),
+        compiler_params=pltpu.CompilerParams(vmem_limit_bytes=24 * MIB),
+        name="touch",
+    )(*values, *after)
 
 
 def expert_kernel(row_blocks, column_blocks, cores, model_width, places, *refs):
@@ -228,7 +250,10 @@
             pltpu.VMEM((rows, hidden), jnp.float32),
             pltpu.VMEM((rows, hidden), jnp.bfloat16),
         ],
-        compiler_params=pltpu.CompilerParams(vmem_limit_bytes=14 * MIB),
+        cost_estimate=pl.CostEstimate(
+            flops=6 * rows * hidden * gate_weight.shape[1], bytes_accessed=8 * MIB, transcendentals=rows * hidden
+        ),
+        compiler_params=pltpu.CompilerParams(vmem_limit_bytes=2 * rows * (gate_weight.shape[1] + 5 * hidden) + 5 * MIB),
         name="expert",
     )(places, *[b for row in blocks for b in row], *gains, row_weight, gate_weight, up_weight, down_weight)
     return [outs[s * cores : (s + 1) * cores] for s in range(row_blocks)]
@@ -293,8 +318,8 @@
         step = cores * back
         return lax.ppermute(value, "ep", [(i, (i + step) % ep_count) for i in range(ep_count)])
 
-    def from_tp(value, back):
-        return lax.ppermute(value, "tp", [(i, (i + back) % tp_count) for i in range(tp_count)])
+    def from_tp(value, bits):
+        return lax.ppermute(value, "tp", [(i, i ^ bits) for i in range(tp_count)])
 
     def gather_ep(value):
         same = [value] + [from_chip(value, b) for b in range(1, chips)]
@@ -307,45 +332,51 @@
         for b in range(chips)
         for c in range(cores)
     ]
-    tp_places = [(tp_index - b + tp_count) % tp_count for b in range(tp_count)]
+    tp_places = [tp_index ^ k for k in range(tp_count)]
     places = jnp.stack(ep_places + tp_places).astype(jnp.int32)
 
     gains = gather_ep(norm_gain.reshape(1, -1))
     row_weight = jnp.sum(jnp.where(routed_experts == ep_index, expert_gates, 0.0), axis=-1, keepdims=True)
 
     head_out = attend(query_latent, query_rope, cache_latent, cache_rope, cache_length, value_up)
-    partial = project(places, gather_ep(head_out), output_weight, tp_count)
-    arrived = [partial[0]] + [from_tp(partial[b], tp_count - b) for b in range(1, tp_count)]
+    partial = project(places, gather_ep(head_out), output_weight, tp_count, gains)
+    expert_weights = [gate_weight, up_weight, down_weight]
+    touched = touch(expert_weights, [partial[0]])
+
     own_residual = lax.dynamic_slice_in_dim(residual, tp_index * block_rows, block_rows, 0)
-    attention = sum(a.astype(jnp.float32) for a in arrived)
-    stream = (own_residual.astype(jnp.float32) + attention).astype(jnp.bfloat16)
-
-    near = [b for b in range(1, tp_count) if b != tp_count // 2]
-    far = [b for b in range(1, tp_count) if b == tp_count // 2]
+    terms = [[(value, 0)] for value in partial]
+    for k in reversed(range(1, tp_count)):
+        total = add([terms[k]], block_rows)[0] if len(terms[k]) > 1 else terms[k][0][0]
+        low = k & -k
+        terms[k ^ low].append((from_tp(total, low), 0))
+    (stream,) = add([terms[0] + [(own_residual, 0)]], block_rows, [touched])
+
     rows_of = {0: stream}
-    for b in near:
-        rows_of[b] = from_tp(stream, b)
-    if far:
-        (again,) = add([[(stream, 0)]], block_rows, [rows_of[b] for b in near])
-        for b in far:
-            rows_of[b] = from_tp(again, b)
-    blocks = [gather_ep(rows_of[b]) for b in range(tp_count)]
-    outs = run_expert(places, blocks, gains, row_weight, gate_weight, up_weight, down_weight, cores)
+    for k in range(1, tp_count):
+        low = k & -k
+        rows_of[k] = from_tp(rows_of[k ^ low], low)
+    blocks = [gather_ep(rows_of[k]) for k in range(tp_count)]
+    outs = run_expert(places, blocks, gains, row_weight, *expert_weights, cores)
 
     swapped = [from_core(out[1]) for out in outs]
-    order = far + near + [0]
-    kept, across = {}, {}
-    for at, b in enumerate(order):
-        before = across[order[at - 2]] if at >= 2 else []
-        pair = [[(outs[b][0], c * block_rows), (swapped[b], c * block_rows)] for c in range(chips)]
+    terms = [[] for _ in range(tp_count)]
+    arrivals = []
+    for k in reversed(range(tp_count)):
+        before = []
+        if len(arrivals) == 1:
+            before = arrivals[0]
+        elif len(arrivals) > 1:
+            before = arrivals[-2]
+        pair = [[(outs[k][0], c * block_rows), (swapped[k], c * block_rows)] for c in range(chips)]
         sums = add(pair, block_rows, before)
-        kept[b] = sums[0]
-        across[b] = [from_chip(sums[c], chips - c) for c in range(1, chips)]
-    finals = []
-    for b in far + near:
-        (total,) = add([[(v, 0) for v in [kept[b]] + across[b]]], block_rows)
-        finals.append(from_tp(total, tp_count - b))
-    (mixed,) = add([[(v, 0) for v in [kept[0]] + across[0] + finals]], block_rows)
+        across = [from_chip(sums[c], chips - c) for c in range(1, chips)]
+        arrivals.append(across)
+        terms[k] += [(value, 0) for value in [sums[0]] + across]
+        if k:
+            (total,) = add([terms[k]], block_rows)
+            low = k & -k
+            terms[k ^ low].append((from_tp(total, low), 0))
+    (mixed,) = add([terms[0]], block_rows)
     return (stream, mixed)
 
 

time: 153 us -> 134 us (0.88)
  waiting for transfers between devices: 76.8 us -> 54.4 us
  Pallas kernels: 20.9 us -> 26.1 us
    ppermute x9, waiting for transfers between devices: 47.5 us -> 26.3 us  [from_tp(): return lax.ppermute(value, 'tp', [(i, i ^ bits) for i in range(tp_count)])]
    pallas_call x1, Pallas kernels: 10.3 us -> 14.7 us  [attend(): pl.pallas_call(functools.partial(attention_kernel, step_rows), out_shape=...]
    unnamed x28 -> x26, local copies, waits for them, and re-layouts: 22.4 us -> 22.4 us
  transfers between devices with their start and end apart: 35 -> 35, of which waited for: 18 -> 17; matrix products, arithmetic and copies ran while one was open for 0% -> 0% of each run, Pallas kernels for 0% -> 1%
where the time goes in v3:
time: 134 us
  waiting for transfers between devices  54.4 us (41%)
  starting transfers between devices  29.6 us (22%)
  Pallas kernels  26.1 us (19%)
  local copies, waits for them, and re-layouts  22.6 us (17%)
    ppermute x9, waiting for transfers between devices, from_tp(): return lax.ppermute(value, 'tp', [(i, i ^ bits) for i in range(tp_count)])  26.3 us
    ppermute x10, waiting for transfers between devices, from_chip(): lax.ppermute(value, 'ep', [(i, (i + step) % ep_count) for i in range(ep_c...  24.4 us
    unnamed x26, local copies, waits for them, and re-layouts  22.4 us
    ppermute x10, starting transfers between devices, from_chip(): lax.ppermute(value, 'ep', [(i, (i + step) % ep_count) for i in range(ep_c...  15.1 us
    pallas_call x1, Pallas kernels, attend(): pl.pallas_call(functools.partial(attention_kernel, step_rows), out_shape=...  14.7 us
    ppermute x9, starting transfers between devices, from_tp(): return lax.ppermute(value, 'tp', [(i, i ^ bits) for i in range(tp_count)])  12.2 us
    pallas_call x1, Pallas kernels, run_expert(): pl.pallas_call(functools.partial(expert_kernel, row_blocks, column_blocks...  7.47 us
    ppermute x16, waiting for transfers between devices, from_core(): return lax.ppermute(value, 'ep', [(i, i ^ 1) for i in range(ep_count)])  3.66 us
  transfers between devices with their start and end apart: 35, of which 17 were waited for; matrix products, arithmetic and copies ran while one was open for 0% of the time, Pallas kernels for 1%

profile of v3, /device:TPU:0, one launch (start us, length us, event | category | flops | bytes accessed | tf_op | source)
XLA Modules:
  0.0 133.5 jit_solution(3204314432455533764)
XLA Ops:
  0.7 14.7 %attention.1.refs_0_ = bf16[64,1024]{1,0:T(8,128)(2,1)} custom-call(s32[64]{0:T(128)} %lengths.1, bf16[512,512]{1,0:T(8,128)(2,1)} %bitcast.10, bf16[64,512]{1,0:T(8,128)(2,1)} %qr_hbm.1, bf16[64,256,512]{2,1,0:T(8,128)(2,1)} %k_hbm.1, bf16[64,64,256]{2,1,0:T(8,128)(2,1)} %kr_hbm.1, bf16[8,512,128]{2,1,0:T(8,128)(2,1)} %up_hbm.1), custom_call_target="tpu_custom_call" | custom-call | flops 4294967296 | bytes 16777216 | tf_op jit(solution)/shard_map/attention/pallas_call | solution.py:98
  15.3 3.0 %collective-permute-start.1 = (bf16[64,1024]{1,0:T(8,128)(2,1)}, bf16[64,1024]{1,0:T(8,128)(2,1)S(1)}, u32[]{:S(2)}, u32[]{:S(2)}) collective-permute-start(bf16[64,1024]{1,0:T(8,128)(2,1)} %attention.1.refs_0_), channel_id=1, source_target_pairs={{0,8},{4,12},{8,0},{12,4},{1,9},{5,13},{9,1},{13,5},{2,10},{6,14},... | collective-permute-start | bytes 393224 | tf_op jit(solution)/shard_map/ppermute | solution.py:319
  18.3 3.7 %collective-permute-done.1.refs_2_ = bf16[64,1024]{1,0:T(8,128)(2,1)S(1)} collective-permute-done((bf16[64,1024]{1,0:T(8,128)(2,1)}, bf16[64,1024]{1,0:T(8,128)(2,1)S(1)}, u32[]{:S(2)}, u32[]{:S(2)}) %collective-permute-start.1) | collective-permute-done | bytes 131104 | tf_op jit(solution)/shard_map/ppermute | solution.py:319
  22.0 1.8 %collective-permute-start.4 = (f32[1,1792]{1,0:T(1,128)S(1)}, f32[1,1792]{1,0:T(1,128)S(1)}, u32[]{:S(2)}, u32[]{:S(2)}) collective-permute-start(f32[1,1792]{1,0:T(1,128)S(1)} %reshape.11.refs_5_.refs_16_), channel_id=1, source_target_pairs={{0,8},{4,12},{8,0},{12,4},{1,9},{5,13},{9,1},{13,5},{2,10},{6,14},... | collective-permute-start | bytes 21512 | tf_op jit(solution)/shard_map/ppermute | solution.py:319
  24.1 1.7 %collective-permute-done.4.refs_7_.refs_18_ = f32[1,1792]{1,0:T(1,128)S(1)} collective-permute-done((f32[1,1792]{1,0:T(1,128)S(1)}, f32[1,1792]{1,0:T(1,128)S(1)}, u32[]{:S(2)}, u32[]{:S(2)}) %collective-permute-start.4) | collective-permute-done | bytes 7200 | tf_op jit(solution)/shard_map/ppermute | solution.py:319
  25.8 1.1 collective-permute-done.5.refs_8_.refs_19_
  26.9 2.0 %copy-done.7 = bf16[1024,1792]{1,0:T(8,128)(2,1)S(1)} copy-done((bf16[1024,1792]{1,0:T(8,128)(2,1)S(1)}, bf16[1024,1792]{1,0:T(8,128)(2,1)}, u32[]{:S(2)}) %copy-start.7) | copy-done | bytes 3670040
  29.0 0.9 copy-done.9
  29.9 1.7 %projection.1 = (bf16[64,1792]{1,0:T(8,128)(2,1)S(1)}, bf16[64,1792]{1,0:T(8,128)(2,1)S(1)}, bf16[64,1792]{1,0:T(8,128)(2,1)S(1)}, bf16[64,1792]{1,0:T(8,128)(2,1)S(1)}) custom-call(s32[8]{0:T(128)S(1)} %stack.35.places, bf16[64,1024]{1,0:T(8,128)(2,1)S(1)} %copy-done.9, bf16[64,1024]{1,0:T(8,128)(2,1)S(1)} %collective-permute-done.refs_1_, ...), custom_call_target="tpu_custom_call" | custom-call | flops 939524096 | bytes 4194304 | tf_op jit(solution)/shard_map/projection/pallas_call | solution.py:153
  31.6 1.9 %collective-permute-start.6 = (bf16[64,1792]{1,0:T(8,128)(2,1)S(1)}, bf16[64,1792]{1,0:T(8,128)(2,1)S(1)}, u32[]{:S(2)}, u32[]{:S(2)}) collective-permute-start(bf16[64,1792]{1,0:T(8,128)(2,1)S(1)} %get-tuple-element.24), channel_id=1, source_target_pairs={{0,1},{1,0},{2,3},{3,2},{4,5},{5,4},{6,7},{7,6},{8,9},{9,8},{10,11... | collective-permute-start | bytes 688136 | tf_op jit(solution)/shard_map/ppermute | solution.py:322
  33.7 6.4 %collective-permute-done.6.refs_1_ = bf16[64,1792]{1,0:T(8,128)(2,1)S(1)} collective-permute-done((bf16[64,1792]{1,0:T(8,128)(2,1)S(1)}, bf16[64,1792]{1,0:T(8,128)(2,1)S(1)}, u32[]{:S(2)}, u32[]{:S(2)}) %collective-permute-start.6) | collective-permute-done | bytes 229408 | tf_op jit(solution)/shard_map/ppermute | solution.py:322
  40.2 2.9 %collective-permute-start.7 = (bf16[64,1792]{1,0:T(8,128)(2,1)S(1)}, bf16[64,1792]{1,0:T(8,128)(2,1)S(1)}, u32[]{:S(2)}, u32[]{:S(2)}) collective-permute-start(bf16[64,1792]{1,0:T(8,128)(2,1)S(1)} %add.59), channel_id=1, source_target_pairs={{0,2},{1,3},{2,0},{3,1},{4,6},{5,7},{6,4},{7,5},{8,10},{9,11},{10,... | collective-permute-start | bytes 688136 | tf_op jit(solution)/shard_map/ppermute | solution.py:322
  43.1 3.1 %copy-done.1 = bf16[1,7168,512]{2,1,0:T(8,128)(2,1)S(1)} copy-done((bf16[1,7168,512]{2,1,0:T(8,128)(2,1)S(1)}, bf16[1,7168,512]{2,1,0:T(8,128)(2,1)}, u32[]{:S(2)}) %copy-start.1) | copy-done | bytes 7340056
  46.2 3.1 %copy-done.3 = bf16[1,7168,512]{2,1,0:T(8,128)(2,1)S(1)} copy-done((bf16[1,7168,512]{2,1,0:T(8,128)(2,1)S(1)}, bf16[1,7168,512]{2,1,0:T(8,128)(2,1)}, u32[]{:S(2)}) %copy-start.3) | copy-done | bytes 7340056
  49.3 3.1 %copy-done.5 = bf16[1,512,7168]{2,1,0:T(8,128)(2,1)S(1)} copy-done((bf16[1,512,7168]{2,1,0:T(8,128)(2,1)S(1)}, bf16[1,512,7168]{2,1,0:T(8,128)(2,1)}, u32[]{:S(2)}) %copy-start.5) | copy-done | bytes 7340056
  52.4 0.8 add.60.refs_0_
  53.3 4.1 %collective-permute-start.12 = (bf16[64,1792]{1,0:T(8,128)(2,1)}, bf16[64,1792]{1,0:T(8,128)(2,1)S(1)}, u32[]{:S(2)}, u32[]{:S(2)}) collective-permute-start(bf16[64,1792]{1,0:T(8,128)(2,1)} %add.60.refs_0_), channel_id=1, source_target_pairs={{0,1},{1,0},{2,3},{3,2},{4,5},{5,4},{6,7},{7,6},{8,9},{9,8},{10,11... | collective-permute-start | bytes 688136 | tf_op jit(solution)/shard_map/ppermute | solution.py:322
  57.4 1.5 %collective-permute-start.10 = (bf16[64,1792]{1,0:T(8,128)(2,1)}, bf16[64,1792]{1,0:T(8,128)(2,1)S(1)}, u32[]{:S(2)}, u32[]{:S(2)}) collective-permute-start(bf16[64,1792]{1,0:T(8,128)(2,1)} %add.60.refs_0_), channel_id=1, source_target_pairs={{0,8},{4,12},{8,0},{12,4},{1,9},{5,13},{9,1},{13,5},{2,10},{6,14},... | collective-permute-start | bytes 688136 | tf_op jit(solution)/shard_map/ppermute | solution.py:319
  58.9 6.2 %collective-permute-done.16.refs_8_ = bf16[64,1792]{1,0:T(8,128)(2,1)S(1)} collective-permute-done((bf16[64,1792]{1,0:T(8,128)(2,1)}, bf16[64,1792]{1,0:T(8,128)(2,1)S(1)}, u32[]{:S(2)}, u32[]{:S(2)}) %collective-permute-start.16) | collective-permute-done | bytes 229408 | tf_op jit(solution)/shard_map/ppermute | solution.py:322
  65.1 1.5 %collective-permute-start.18 = (bf16[64,1792]{1,0:T(8,128)(2,1)S(1)}, bf16[64,1792]{1,0:T(8,128)(2,1)S(1)}, u32[]{:S(2)}, u32[]{:S(2)}) collective-permute-start(bf16[64,1792]{1,0:T(8,128)(2,1)S(1)} %collective-permute-done.16.refs_8_), channel_id=1, source_target_pairs={{0,8},{4,12},{8,0},{12,4},{1,9},{5,13},{9,1},{13,5},{2,10},{6,14},... | collective-permute-start | bytes 688136 | tf_op jit(solution)/shard_map/ppermute | solution.py:319
  66.6 0.6 collective-permute-start.14
  67.3 4.0 %collective-permute-done.20.refs_12_ = bf16[64,1792]{1,0:T(8,128)(2,1)S(1)} collective-permute-done((bf16[64,1792]{1,0:T(8,128)(2,1)S(1)}, bf16[64,1792]{1,0:T(8,128)(2,1)S(1)}, u32[]{:S(2)}, u32[]{:S(2)}) %collective-permute-start.20) | collective-permute-done | bytes 229408 | tf_op jit(solution)/shard_map/ppermute | solution.py:322
  71.4 1.5 %collective-permute-start.22 = (bf16[64,1792]{1,0:T(8,128)(2,1)S(1)}, bf16[64,1792]{1,0:T(8,128)(2,1)S(1)}, u32[]{:S(2)}, u32[]{:S(2)}) collective-permute-start(bf16[64,1792]{1,0:T(8,128)(2,1)S(1)} %collective-permute-done.20.refs_12_), channel_id=1, source_target_pairs={{0,8},{4,12},{8,0},{12,4},{1,9},{5,13},{9,1},{13,5},{2,10},{6,14},... | collective-permute-start | bytes 688136 | tf_op jit(solution)/shard_map/ppermute | solution.py:319
  73.1 0.5 collective-permute-start.21
  73.6 4.4 %collective-permute-done.14.refs_6_ = bf16[64,1792]{1,0:T(8,128)(2,1)S(1)} collective-permute-done((bf16[64,1792]{1,0:T(8,128)(2,1)S(1)}, bf16[64,1792]{1,0:T(8,128)(2,1)S(1)}, u32[]{:S(2)}, u32[]{:S(2)}) %collective-permute-start.14) | collective-permute-done | bytes 229408 | tf_op jit(solution)/shard_map/ppermute | solution.py:319
  78.0 0.5 collective-permute-start.15
  78.5 2.7 %collective-permute-done.22.refs_14_ = bf16[64,1792]{1,0:T(8,128)(2,1)S(1)} collective-permute-done((bf16[64,1792]{1,0:T(8,128)(2,1)S(1)}, bf16[64,1792]{1,0:T(8,128)(2,1)S(1)}, u32[]{:S(2)}, u32[]{:S(2)}) %collective-permute-start.22) | collective-permute-done | bytes 229408 | tf_op jit(solution)/shard_map/ppermute | solution.py:319
  81.4 1.4 %collective-permute-done.23.refs_15_ = bf16[64,1792]{1,0:T(8,128)(2,1)} collective-permute-done((bf16[64,1792]{1,0:T(8,128)(2,1)S(1)}, bf16[64,1792]{1,0:T(8,128)(2,1)}, u32[]{:S(2)}, u32[]{:S(2)}) %collective-permute-start.23) | collective-permute-done | bytes 229408 | tf_op jit(solution)/shard_map/ppermute | solution.py:315
  82.8 3.1 %copy-done.2 = bf16[1,7168,512]{2,1,0:T(8,128)(2,1)S(1)} copy-done((bf16[1,7168,512]{2,1,0:T(8,128)(2,1)S(1)}, bf16[1,7168,512]{2,1,0:T(8,128)(2,1)}, u32[]{:S(2)}) %copy-start.2) | copy-done | bytes 7340056
  85.9 3.1 %copy-done.4 = bf16[1,7168,512]{2,1,0:T(8,128)(2,1)S(1)} copy-done((bf16[1,7168,512]{2,1,0:T(8,128)(2,1)S(1)}, bf16[1,7168,512]{2,1,0:T(8,128)(2,1)}, u32[]{:S(2)}) %copy-start.4) | copy-done | bytes 7340056
  89.0 3.1 %copy-done.6 = bf16[1,512,7168]{2,1,0:T(8,128)(2,1)S(1)} copy-done((bf16[1,512,7168]{2,1,0:T(8,128)(2,1)S(1)}, bf16[1,512,7168]{2,1,0:T(8,128)(2,1)}, u32[]{:S(2)}) %copy-start.6) | copy-done | bytes 7340056
  92.1 0.9 copy-done.8
  93.0 7.5 %expert.1 = (bf16[128,1792]{1,0:T(8,128)(2,1)S(1)}, bf16[128,1792]{1,0:T(8,128)(2,1)S(1)}, bf16[128,1792]{1,0:T(8,128)(2,1)S(1)}, bf16[128,1792]{1,0:T(8,128)(2,...) custom-call(s32[8]{0:T(128)S(1)} %stack.35.places, ...), custom_call_target="tpu_custom_call" | custom-call | flops 5637144576 | bytes 8388608 | tf_op jit(solution)/shard_map/expert/pallas_call | solution.py:242
  101.2 1.1 collective-permute-done.24.refs_1_.refs_3_
  102.5 1.6 %collective-permute-start.25 = (bf16[64,1792]{1,0:T(8,128)(2,1)S(1)}, bf16[64,1792]{1,0:T(8,128)(2,1)S(1)}, u32[]{:S(2)}, u32[]{:S(2)}) collective-permute-start(bf16[64,1792]{1,0:T(8,128)(2,1)S(1)} %get-tuple-element.29), channel_id=1, source_target_pairs={{0,8},{4,12},{8,0},{12,4},{1,9},{5,13},{9,1},{13,5},{2,10},{6,14},... | collective-permute-start | bytes 688136 | tf_op jit(solution)/shard_map/ppermute | solution.py:319
  104.1 6.2 %collective-permute-done.25.refs_1_.refs_4_ = bf16[64,1792]{1,0:T(8,128)(2,1)S(1)} collective-permute-done((bf16[64,1792]{1,0:T(8,128)(2,1)S(1)}, bf16[64,1792]{1,0:T(8,128)(2,1)S(1)}, u32[]{:S(2)}, u32[]{:S(2)}) %collective-permute-start.25) | collective-permute-done | bytes 229408 | tf_op jit(solution)/shard_map/ppermute | solution.py:319
  110.3 1.8 %collective-permute-start.26 = (bf16[64,1792]{1,0:T(8,128)(2,1)S(1)}, bf16[64,1792]{1,0:T(8,128)(2,1)S(1)}, u32[]{:S(2)}, u32[]{:S(2)}) collective-permute-start(bf16[64,1792]{1,0:T(8,128)(2,1)S(1)} %add.62), channel_id=1, source_target_pairs={{0,1},{1,0},{2,3},{3,2},{4,5},{5,4},{6,7},{7,6},{8,9},{9,8},{10,11... | collective-permute-start | bytes 688136 | tf_op jit(solution)/shard_map/ppermute | solution.py:322
  112.2 1.6 %collective-permute-start.28 = (bf16[64,1792]{1,0:T(8,128)(2,1)S(1)}, bf16[64,1792]{1,0:T(8,128)(2,1)S(1)}, u32[]{:S(2)}, u32[]{:S(2)}) collective-permute-start(bf16[64,1792]{1,0:T(8,128)(2,1)S(1)} %get-tuple-element.33), channel_id=1, source_target_pairs={{0,8},{4,12},{8,0},{12,4},{1,9},{5,13},{9,1},{13,5},{2,10},{6,14},... | collective-permute-start | bytes 688136 | tf_op jit(solution)/shard_map/ppermute | solution.py:319
  113.9 0.6 collective-permute-start.31
  114.5 2.7 %collective-permute-done.26.refs_0_ = bf16[64,1792]{1,0:T(8,128)(2,1)S(1)} collective-permute-done((bf16[64,1792]{1,0:T(8,128)(2,1)S(1)}, bf16[64,1792]{1,0:T(8,128)(2,1)S(1)}, u32[]{:S(2)}, u32[]{:S(2)}) %collective-permute-start.26) | collective-permute-done | bytes 229408 | tf_op jit(solution)/shard_map/ppermute | solution.py:322
  117.2 3.6 %collective-permute-done.28.refs_2_.refs_4_ = bf16[64,1792]{1,0:T(8,128)(2,1)S(1)} collective-permute-done((bf16[64,1792]{1,0:T(8,128)(2,1)S(1)}, bf16[64,1792]{1,0:T(8,128)(2,1)S(1)}, u32[]{:S(2)}, u32[]{:S(2)}) %collective-permute-start.28) | collective-permute-done | bytes 229408 | tf_op jit(solution)/shard_map/ppermute | solution.py:319
  120.9 0.9 collective-permute-start.29
  121.8 2.0 %collective-permute-done.31.refs_1_ = bf16[64,1792]{1,0:T(8,128)(2,1)S(1)} collective-permute-done((bf16[64,1792]{1,0:T(8,128)(2,1)S(1)}, bf16[64,1792]{1,0:T(8,128)(2,1)S(1)}, u32[]{:S(2)}, u32[]{:S(2)}) %collective-permute-start.31) | collective-permute-done | bytes 229408 | tf_op jit(solution)/shard_map/ppermute | solution.py:319
  123.8 0.4 collective-permute-start.32
  124.3 1.5 %collective-permute-start.34 = (bf16[64,1792]{1,0:T(8,128)(2,1)S(1)}, bf16[64,1792]{1,0:T(8,128)(2,1)S(1)}, u32[]{:S(2)}, u32[]{:S(2)}) collective-permute-start(bf16[64,1792]{1,0:T(8,128)(2,1)S(1)} %get-tuple-element.41), channel_id=1, source_target_pairs={{0,8},{4,12},{8,0},{12,4},{1,9},{5,13},{9,1},{13,5},{2,10},{6,14},... | collective-permute-start | bytes 688136 | tf_op jit(solution)/shard_map/ppermute | solution.py:319
  125.8 4.5 %collective-permute-done.29.refs_0_ = bf16[64,1792]{1,0:T(8,128)(2,1)S(1)} collective-permute-done((bf16[64,1792]{1,0:T(8,128)(2,1)S(1)}, bf16[64,1792]{1,0:T(8,128)(2,1)S(1)}, u32[]{:S(2)}, u32[]{:S(2)}) %collective-permute-start.29) | collective-permute-done | bytes 229408 | tf_op jit(solution)/shard_map/ppermute | solution.py:322
  130.3 2.4 %collective-permute-done.32.refs_1_ = bf16[64,1792]{1,0:T(8,128)(2,1)S(1)} collective-permute-done((bf16[64,1792]{1,0:T(8,128)(2,1)S(1)}, bf16[64,1792]{1,0:T(8,128)(2,1)S(1)}, u32[]{:S(2)}, u32[]{:S(2)}) %collective-permute-start.32) | collective-permute-done | bytes 229408 | tf_op jit(solution)/shard_map/ppermute | solution.py:322
  132.7 0.8 add.68
  (67 shorter events, 2.7 us)
Async XLA Ops:
  0.6 42.5 %copy-start = (bf16[256,1792]{1,0:T(8,128)(2,1)S(1)}, bf16[256,1792]{1,0:T(8,128)(2,1)}, u32[]{:S(2)}) copy-start(bf16[256,1792]{1,0:T(8,128)(2,1)} %param.21) | copy-start | bytes 2752516
  0.6 21.4 %copy-start.10 = (f32[1792]{0:T(1024)S(1)}, f32[1792]{0:T(1024)}, u32[]{:S(2)}) copy-start(f32[1792]{0:T(1024)} %param.22) | copy-start | bytes 21508
  15.3 6.7 %collective-permute-start.1 = (bf16[64,1024]{1,0:T(8,128)(2,1)}, bf16[64,1024]{1,0:T(8,128)(2,1)S(1)}, u32[]{:S(2)}, u32[]{:S(2)}) collective-permute-start(bf16[64,1024]{1,0:T(8,128)(2,1)} %attention.1.refs_0_), channel_id=1, source_target_pairs={{0,8},{4,12},{8,0},{12,4},{1,9},{5,13},{9,1},{13,5},{2,10},{6,14},... | collective-permute-start | bytes 393224 | tf_op jit(solution)/shard_map/ppermute | solution.py:319
  18.3 8.6 %collective-permute-start = (bf16[64,1024]{1,0:T(8,128)(2,1)}, bf16[64,1024]{1,0:T(8,128)(2,1)S(1)}, u32[]{:S(2)}, u32[]{:S(2)}) collective-permute-start(bf16[64,1024]{1,0:T(8,128)(2,1)} %attention.1.refs_0_), channel_id=1, source_target_pairs={{0,4},{4,0},{8,12},{12,8},{1,5},{5,1},{9,13},{13,9},{2,6},{6,2},{1... | collective-permute-start | bytes 393224 | tf_op jit(solution)/shard_map/ppermute | solution.py:315
  22.0 4.9 %collective-permute-start.2 = (bf16[64,1024]{1,0:T(8,128)(2,1)S(1)}, bf16[64,1024]{1,0:T(8,128)(2,1)S(1)}, u32[]{:S(2)}, u32[]{:S(2)}) collective-permute-start(bf16[64,1024]{1,0:T(8,128)(2,1)S(1)} %collective-permute-done.1.refs_2_), channel_id=1, source_target_pairs={{0,4},{4,0},{8,12},{12,8},{1,5},{5,1},{9,13},{13,9},{2,6},{6,2},{1... | collective-permute-start | bytes 393224 | tf_op jit(solution)/shard_map/ppermute | solution.py:315
  22.0 3.7 %collective-permute-start.4 = (f32[1,1792]{1,0:T(1,128)S(1)}, f32[1,1792]{1,0:T(1,128)S(1)}, u32[]{:S(2)}, u32[]{:S(2)}) collective-permute-start(f32[1,1792]{1,0:T(1,128)S(1)} %reshape.11.refs_5_.refs_16_), channel_id=1, source_target_pairs={{0,8},{4,12},{8,0},{12,4},{1,9},{5,13},{9,1},{13,5},{2,10},{6,14},... | collective-permute-start | bytes 21512 | tf_op jit(solution)/shard_map/ppermute | solution.py:319
  23.9 2.0 %collective-permute-start.3 = (f32[1,1792]{1,0:T(1,128)S(1)}, f32[1,1792]{1,0:T(1,128)S(1)}, u32[]{:S(2)}, u32[]{:S(2)}) collective-permute-start(f32[1,1792]{1,0:T(1,128)S(1)} %reshape.11.refs_5_.refs_16_), channel_id=1, source_target_pairs={{0,4},{4,0},{8,12},{12,8},{1,5},{5,1},{9,13},{13,9},{2,6},{6,2},{1... | collective-permute-start | bytes 21512 | tf_op jit(solution)/shard_map/ppermute | solution.py:315
  25.8 1.2 collective-permute-start.5
  26.9 2.0 %copy-start.7 = (bf16[1024,1792]{1,0:T(8,128)(2,1)S(1)}, bf16[1024,1792]{1,0:T(8,128)(2,1)}, u32[]{:S(2)}) copy-start(bf16[1024,1792]{1,0:T(8,128)(2,1)} %refs_4_.1) | copy-start | bytes 11010052
  29.0 0.9 copy-start.9
  31.6 8.5 %collective-permute-start.6 = (bf16[64,1792]{1,0:T(8,128)(2,1)S(1)}, bf16[64,1792]{1,0:T(8,128)(2,1)S(1)}, u32[]{:S(2)}, u32[]{:S(2)}) collective-permute-start(bf16[64,1792]{1,0:T(8,128)(2,1)S(1)} %get-tuple-element.24), channel_id=1, source_target_pairs={{0,1},{1,0},{2,3},{3,2},{4,5},{5,4},{6,7},{7,6},{8,9},{9,8},{10,11... | collective-permute-start | bytes 688136 | tf_op jit(solution)/shard_map/ppermute | solution.py:322
  33.5 18.9 %collective-permute-start.8 = (bf16[64,1792]{1,0:T(8,128)(2,1)S(1)}, bf16[64,1792]{1,0:T(8,128)(2,1)S(1)}, u32[]{:S(2)}, u32[]{:S(2)}) collective-permute-start(bf16[64,1792]{1,0:T(8,128)(2,1)S(1)} %get-tuple-element.25), channel_id=1, source_target_pairs={{0,1},{1,0},{2,3},{3,2},{4,5},{5,4},{6,7},{7,6},{8,9},{9,8},{10,11... | collective-permute-start | bytes 688136 | tf_op jit(solution)/shard_map/ppermute | solution.py:322
  40.2 12.2 %collective-permute-start.7 = (bf16[64,1792]{1,0:T(8,128)(2,1)S(1)}, bf16[64,1792]{1,0:T(8,128)(2,1)S(1)}, u32[]{:S(2)}, u32[]{:S(2)}) collective-permute-start(bf16[64,1792]{1,0:T(8,128)(2,1)S(1)} %add.59), channel_id=1, source_target_pairs={{0,2},{1,3},{2,0},{3,1},{4,6},{5,7},{6,4},{7,5},{8,10},{9,11},{10,... | collective-permute-start | bytes 688136 | tf_op jit(solution)/shard_map/ppermute | solution.py:322
  43.1 3.1 %copy-start.1 = (bf16[1,7168,512]{2,1,0:T(8,128)(2,1)S(1)}, bf16[1,7168,512]{2,1,0:T(8,128)(2,1)}, u32[]{:S(2)}) copy-start(bf16[1,7168,512]{2,1,0:T(8,128)(2,1)} %refs_21_.1) | copy-start | bytes 22020100
  46.2 3.1 %copy-start.3 = (bf16[1,7168,512]{2,1,0:T(8,128)(2,1)S(1)}, bf16[1,7168,512]{2,1,0:T(8,128)(2,1)}, u32[]{:S(2)}) copy-start(bf16[1,7168,512]{2,1,0:T(8,128)(2,1)} %refs_22_.1) | copy-start | bytes 22020100
  49.3 3.1 %copy-start.5 = (bf16[1,512,7168]{2,1,0:T(8,128)(2,1)S(1)}, bf16[1,512,7168]{2,1,0:T(8,128)(2,1)}, u32[]{:S(2)}) copy-start(bf16[1,512,7168]{2,1,0:T(8,128)(2,1)} %refs_23_.1) | copy-start | bytes 22020100
  52.4 28.9 %copy-start.11 = (f32[256,2]{0,1:T(2,128)S(1)}, f32[256,2]{0,1:T(2,128)}, u32[]{:S(2)}) copy-start(f32[256,2]{0,1:T(2,128)} %param.24) | copy-start | bytes 6148
  52.4 28.9 %copy-start.12 = (s32[256,2]{0,1:T(2,128)S(1)}, s32[256,2]{0,1:T(2,128)}, u32[]{:S(2)}) copy-start(s32[256,2]{0,1:T(2,128)} %param.23) | copy-start | bytes 6148
  53.2 11.9 %collective-permute-start.16 = (bf16[64,1792]{1,0:T(8,128)(2,1)}, bf16[64,1792]{1,0:T(8,128)(2,1)S(1)}, u32[]{:S(2)}, u32[]{:S(2)}) collective-permute-start(bf16[64,1792]{1,0:T(8,128)(2,1)} %add.60.refs_0_), channel_id=1, source_target_pairs={{0,2},{1,3},{2,0},{3,1},{4,6},{5,7},{6,4},{7,5},{8,10},{9,11},{10,... | collective-permute-start | bytes 688136 | tf_op jit(solution)/shard_map/ppermute | solution.py:322
  53.3 13.3 %collective-permute-start.12 = (bf16[64,1792]{1,0:T(8,128)(2,1)}, bf16[64,1792]{1,0:T(8,128)(2,1)S(1)}, u32[]{:S(2)}, u32[]{:S(2)}) collective-permute-start(bf16[64,1792]{1,0:T(8,128)(2,1)} %add.60.refs_0_), channel_id=1, source_target_pairs={{0,1},{1,0},{2,3},{3,2},{4,5},{5,4},{6,7},{7,6},{8,9},{9,8},{10,11... | collective-permute-start | bytes 688136 | tf_op jit(solution)/shard_map/ppermute | solution.py:322
  57.4 9.2 %collective-permute-start.10 = (bf16[64,1792]{1,0:T(8,128)(2,1)}, bf16[64,1792]{1,0:T(8,128)(2,1)S(1)}, u32[]{:S(2)}, u32[]{:S(2)}) collective-permute-start(bf16[64,1792]{1,0:T(8,128)(2,1)} %add.60.refs_0_), channel_id=1, source_target_pairs={{0,8},{4,12},{8,0},{12,4},{1,9},{5,13},{9,1},{13,5},{2,10},{6,14},... | collective-permute-start | bytes 688136 | tf_op jit(solution)/shard_map/ppermute | solution.py:319
  58.9 8.3 %collective-permute-start.9 = (bf16[64,1792]{1,0:T(8,128)(2,1)}, bf16[64,1792]{1,0:T(8,128)(2,1)S(1)}, u32[]{:S(2)}, u32[]{:S(2)}) collective-permute-start(bf16[64,1792]{1,0:T(8,128)(2,1)} %add.60.refs_0_), channel_id=1, source_target_pairs={{0,4},{4,0},{8,12},{12,8},{1,5},{5,1},{9,13},{13,9},{2,6},{6,2},{1... | collective-permute-start | bytes 688136 | tf_op jit(solution)/shard_map/ppermute | solution.py:315
  65.1 6.3 %collective-permute-start.20 = (bf16[64,1792]{1,0:T(8,128)(2,1)S(1)}, bf16[64,1792]{1,0:T(8,128)(2,1)S(1)}, u32[]{:S(2)}, u32[]{:S(2)}) collective-permute-start(bf16[64,1792]{1,0:T(8,128)(2,1)S(1)} %collective-permute-done.16.refs_8_), channel_id=1, source_target_pairs={{0,1},{1,0},{2,3},{3,2},{4,5},{5,4},{6,7},{7,6},{8,9},{9,8},{10,11... | collective-permute-start | bytes 688136 | tf_op jit(solution)/shard_map/ppermute | solution.py:322
  65.1 8.0 %collective-permute-start.18 = (bf16[64,1792]{1,0:T(8,128)(2,1)S(1)}, bf16[64,1792]{1,0:T(8,128)(2,1)S(1)}, u32[]{:S(2)}, u32[]{:S(2)}) collective-permute-start(bf16[64,1792]{1,0:T(8,128)(2,1)S(1)} %collective-permute-done.16.refs_8_), channel_id=1, source_target_pairs={{0,8},{4,12},{8,0},{12,4},{1,9},{5,13},{9,1},{13,5},{2,10},{6,14},... | collective-permute-start | bytes 688136 | tf_op jit(solution)/shard_map/ppermute | solution.py:319
  66.6 6.5 %collective-permute-start.17 = (bf16[64,1792]{1,0:T(8,128)(2,1)S(1)}, bf16[64,1792]{1,0:T(8,128)(2,1)S(1)}, u32[]{:S(2)}, u32[]{:S(2)}) collective-permute-start(bf16[64,1792]{1,0:T(8,128)(2,1)S(1)} %collective-permute-done.16.refs_8_), channel_id=1, source_target_pairs={{0,4},{4,0},{8,12},{12,8},{1,5},{5,1},{9,13},{13,9},{2,6},{6,2},{1... | collective-permute-start | bytes 688136 | tf_op jit(solution)/shard_map/ppermute | solution.py:315
  66.6 11.4 %collective-permute-start.14 = (bf16[64,1792]{1,0:T(8,128)(2,1)S(1)}, bf16[64,1792]{1,0:T(8,128)(2,1)S(1)}, u32[]{:S(2)}, u32[]{:S(2)}) collective-permute-start(bf16[64,1792]{1,0:T(8,128)(2,1)S(1)} %collective-permute-done.12.refs_4_), channel_id=1, source_target_pairs={{0,8},{4,12},{8,0},{12,4},{1,9},{5,13},{9,1},{13,5},{2,10},{6,14},... | collective-permute-start | bytes 688136 | tf_op jit(solution)/shard_map/ppermute | solution.py:319
  67.2 10.8 %collective-permute-start.13 = (bf16[64,1792]{1,0:T(8,128)(2,1)S(1)}, bf16[64,1792]{1,0:T(8,128)(2,1)S(1)}, u32[]{:S(2)}, u32[]{:S(2)}) collective-permute-start(bf16[64,1792]{1,0:T(8,128)(2,1)S(1)} %collective-permute-done.12.refs_4_), channel_id=1, source_target_pairs={{0,4},{4,0},{8,12},{12,8},{1,5},{5,1},{9,13},{13,9},{2,6},{6,2},{1... | collective-permute-start | bytes 688136 | tf_op jit(solution)/shard_map/ppermute | solution.py:315
  71.4 9.8 %collective-permute-start.22 = (bf16[64,1792]{1,0:T(8,128)(2,1)S(1)}, bf16[64,1792]{1,0:T(8,128)(2,1)S(1)}, u32[]{:S(2)}, u32[]{:S(2)}) collective-permute-start(bf16[64,1792]{1,0:T(8,128)(2,1)S(1)} %collective-permute-done.20.refs_12_), channel_id=1, source_target_pairs={{0,8},{4,12},{8,0},{12,4},{1,9},{5,13},{9,1},{13,5},{2,10},{6,14},... | collective-permute-start | bytes 688136 | tf_op jit(solution)/shard_map/ppermute | solution.py:319
  73.1 8.3 %collective-permute-start.11 = (bf16[64,1792]{1,0:T(8,128)(2,1)S(1)}, bf16[64,1792]{1,0:T(8,128)(2,1)}, u32[]{:S(2)}, u32[]{:S(2)}) collective-permute-start(bf16[64,1792]{1,0:T(8,128)(2,1)S(1)} %collective-permute-done.10.refs_2_), channel_id=1, source_target_pairs={{0,4},{4,0},{8,12},{12,8},{1,5},{5,1},{9,13},{13,9},{2,6},{6,2},{1... | collective-permute-start | bytes 688136 | tf_op jit(solution)/shard_map/ppermute | solution.py:315
  73.1 8.3 %collective-permute-start.21 = (bf16[64,1792]{1,0:T(8,128)(2,1)S(1)}, bf16[64,1792]{1,0:T(8,128)(2,1)}, u32[]{:S(2)}, u32[]{:S(2)}) collective-permute-start(bf16[64,1792]{1,0:T(8,128)(2,1)S(1)} %collective-permute-done.20.refs_12_), channel_id=1, source_target_pairs={{0,4},{4,0},{8,12},{12,8},{1,5},{5,1},{9,13},{13,9},{2,6},{6,2},{1... | collective-permute-start | bytes 688136 | tf_op jit(solution)/shard_map/ppermute | solution.py:315
  78.0 3.4 %collective-permute-start.19 = (bf16[64,1792]{1,0:T(8,128)(2,1)S(1)}, bf16[64,1792]{1,0:T(8,128)(2,1)}, u32[]{:S(2)}, u32[]{:S(2)}) collective-permute-start(bf16[64,1792]{1,0:T(8,128)(2,1)S(1)} %collective-permute-done.18.refs_10_), channel_id=1, source_target_pairs={{0,4},{4,0},{8,12},{12,8},{1,5},{5,1},{9,13},{13,9},{2,6},{6,2},{1... | collective-permute-start | bytes 688136 | tf_op jit(solution)/shard_map/ppermute | solution.py:315
  78.0 3.4 %collective-permute-start.15 = (bf16[64,1792]{1,0:T(8,128)(2,1)S(1)}, bf16[64,1792]{1,0:T(8,128)(2,1)}, u32[]{:S(2)}, u32[]{:S(2)}) collective-permute-start(bf16[64,1792]{1,0:T(8,128)(2,1)S(1)} %collective-permute-done.14.refs_6_), channel_id=1, source_target_pairs={{0,4},{4,0},{8,12},{12,8},{1,5},{5,1},{9,13},{13,9},{2,6},{6,2},{1... | collective-permute-start | bytes 688136 | tf_op jit(solution)/shard_map/ppermute | solution.py:315
  81.2 1.6 %collective-permute-start.23 = (bf16[64,1792]{1,0:T(8,128)(2,1)S(1)}, bf16[64,1792]{1,0:T(8,128)(2,1)}, u32[]{:S(2)}, u32[]{:S(2)}) collective-permute-start(bf16[64,1792]{1,0:T(8,128)(2,1)S(1)} %collective-permute-done.22.refs_14_), channel_id=1, source_target_pairs={{0,4},{4,0},{8,12},{12,8},{1,5},{5,1},{9,13},{13,9},{2,6},{6,2},{1... | collective-permute-start | bytes 688136 | tf_op jit(solution)/shard_map/ppermute | solution.py:315
  82.8 3.1 %copy-start.2 = (bf16[1,7168,512]{2,1,0:T(8,128)(2,1)S(1)}, bf16[1,7168,512]{2,1,0:T(8,128)(2,1)}, u32[]{:S(2)}) copy-start(bf16[1,7168,512]{2,1,0:T(8,128)(2,1)} %refs_21_.1) | copy-start | bytes 22020100
  85.9 3.1 %copy-start.4 = (bf16[1,7168,512]{2,1,0:T(8,128)(2,1)S(1)}, bf16[1,7168,512]{2,1,0:T(8,128)(2,1)}, u32[]{:S(2)}) copy-start(bf16[1,7168,512]{2,1,0:T(8,128)(2,1)} %refs_22_.1) | copy-start | bytes 22020100
  89.0 3.1 %copy-start.6 = (bf16[1,512,7168]{2,1,0:T(8,128)(2,1)S(1)}, bf16[1,512,7168]{2,1,0:T(8,128)(2,1)}, u32[]{:S(2)}) copy-start(bf16[1,512,7168]{2,1,0:T(8,128)(2,1)} %refs_23_.1) | copy-start | bytes 22020100
  92.1 0.9 copy-start.8
  100.5 1.9 %collective-permute-start.24 = (bf16[128,1792]{1,0:T(8,128)(2,1)S(1)}, bf16[128,1792]{1,0:T(8,128)(2,1)S(1)}, u32[]{:S(2)}, u32[]{:S(2)}) collective-permute-start(bf16[128,1792]{1,0:T(8,128)(2,1)S(1)} %get-tuple-element.27), channel_id=1, source_target_pairs={{0,4},{4,0},{8,12},{12,8},{1,5},{5,1},{9,13},{13,9},{2,6},{6,2},{1... | collective-permute-start | bytes 1376264 | tf_op jit(solution)/shard_map/ppermute | solution.py:315
  100.7 11.4 %collective-permute-start.27 = (bf16[128,1792]{1,0:T(8,128)(2,1)S(1)}, bf16[128,1792]{1,0:T(8,128)(2,1)S(1)}, u32[]{:S(2)}, u32[]{:S(2)}) collective-permute-start(bf16[128,1792]{1,0:T(8,128)(2,1)S(1)} %get-tuple-element.31), channel_id=1, source_target_pairs={{0,4},{4,0},{8,12},{12,8},{1,5},{5,1},{9,13},{13,9},{2,6},{6,2},{1... | collective-permute-start | bytes 1376264 | tf_op jit(solution)/shard_map/ppermute | solution.py:315
  101.1 12.7 %collective-permute-start.30 = (bf16[128,1792]{1,0:T(8,128)(2,1)S(1)}, bf16[128,1792]{1,0:T(8,128)(2,1)S(1)}, u32[]{:S(2)}, u32[]{:S(2)}) collective-permute-start(bf16[128,1792]{1,0:T(8,128)(2,1)S(1)} %get-tuple-element.35), channel_id=1, source_target_pairs={{0,4},{4,0},{8,12},{12,8},{1,5},{5,1},{9,13},{13,9},{2,6},{6,2},{1... | collective-permute-start | bytes 1376264 | tf_op jit(solution)/shard_map/ppermute | solution.py:315
  102.5 7.7 %collective-permute-start.25 = (bf16[64,1792]{1,0:T(8,128)(2,1)S(1)}, bf16[64,1792]{1,0:T(8,128)(2,1)S(1)}, u32[]{:S(2)}, u32[]{:S(2)}) collective-permute-start(bf16[64,1792]{1,0:T(8,128)(2,1)S(1)} %get-tuple-element.29), channel_id=1, source_target_pairs={{0,8},{4,12},{8,0},{12,4},{1,9},{5,13},{9,1},{13,5},{2,10},{6,14},... | collective-permute-start | bytes 688136 | tf_op jit(solution)/shard_map/ppermute | solution.py:319
  104.1 20.1 %collective-permute-start.33 = (bf16[128,1792]{1,0:T(8,128)(2,1)S(1)}, bf16[128,1792]{1,0:T(8,128)(2,1)S(1)}, u32[]{:S(2)}, u32[]{:S(2)}) collective-permute-start(bf16[128,1792]{1,0:T(8,128)(2,1)S(1)} %get-tuple-element.39), channel_id=1, source_target_pairs={{0,4},{4,0},{8,12},{12,8},{1,5},{5,1},{9,13},{13,9},{2,6},{6,2},{1... | collective-permute-start | bytes 1376264 | tf_op jit(solution)/shard_map/ppermute | solution.py:315
  110.3 6.9 %collective-permute-start.26 = (bf16[64,1792]{1,0:T(8,128)(2,1)S(1)}, bf16[64,1792]{1,0:T(8,128)(2,1)S(1)}, u32[]{:S(2)}, u32[]{:S(2)}) collective-permute-start(bf16[64,1792]{1,0:T(8,128)(2,1)S(1)} %add.62), channel_id=1, source_target_pairs={{0,1},{1,0},{2,3},{3,2},{4,5},{5,4},{6,7},{7,6},{8,9},{9,8},{10,11... | collective-permute-start | bytes 688136 | tf_op jit(solution)/shard_map/ppermute | solution.py:322
  112.2 8.6 %collective-permute-start.28 = (bf16[64,1792]{1,0:T(8,128)(2,1)S(1)}, bf16[64,1792]{1,0:T(8,128)(2,1)S(1)}, u32[]{:S(2)}, u32[]{:S(2)}) collective-permute-start(bf16[64,1792]{1,0:T(8,128)(2,1)S(1)} %get-tuple-element.33), channel_id=1, source_target_pairs={{0,8},{4,12},{8,0},{12,4},{1,9},{5,13},{9,1},{13,5},{2,10},{6,14},... | collective-permute-start | bytes 688136 | tf_op jit(solution)/shard_map/ppermute | solution.py:319
  113.9 9.9 %collective-permute-start.31 = (bf16[64,1792]{1,0:T(8,128)(2,1)S(1)}, bf16[64,1792]{1,0:T(8,128)(2,1)S(1)}, u32[]{:S(2)}, u32[]{:S(2)}) collective-permute-start(bf16[64,1792]{1,0:T(8,128)(2,1)S(1)} %get-tuple-element.37), channel_id=1, source_target_pairs={{0,8},{4,12},{8,0},{12,4},{1,9},{5,13},{9,1},{13,5},{2,10},{6,14},... | collective-permute-start | bytes 688136 | tf_op jit(solution)/shard_map/ppermute | solution.py:319
  120.9 9.4 %collective-permute-start.29 = (bf16[64,1792]{1,0:T(8,128)(2,1)S(1)}, bf16[64,1792]{1,0:T(8,128)(2,1)S(1)}, u32[]{:S(2)}, u32[]{:S(2)}) collective-permute-start(bf16[64,1792]{1,0:T(8,128)(2,1)S(1)} %add.64), channel_id=1, source_target_pairs={{0,2},{1,3},{2,0},{3,1},{4,6},{5,7},{6,4},{7,5},{8,10},{9,11},{10,... | collective-permute-start | bytes 688136 | tf_op jit(solution)/shard_map/ppermute | solution.py:322
  123.8 8.9 %collective-permute-start.32 = (bf16[64,1792]{1,0:T(8,128)(2,1)S(1)}, bf16[64,1792]{1,0:T(8,128)(2,1)S(1)}, u32[]{:S(2)}, u32[]{:S(2)}) collective-permute-start(bf16[64,1792]{1,0:T(8,128)(2,1)S(1)} %add.66), channel_id=1, source_target_pairs={{0,1},{1,0},{2,3},{3,2},{4,5},{5,4},{6,7},{7,6},{8,9},{9,8},{10,11... | collective-permute-start | bytes 688136 | tf_op jit(solution)/shard_map/ppermute | solution.py:322
  124.3 8.4 %collective-permute-start.34 = (bf16[64,1792]{1,0:T(8,128)(2,1)S(1)}, bf16[64,1792]{1,0:T(8,128)(2,1)S(1)}, u32[]{:S(2)}, u32[]{:S(2)}) collective-permute-start(bf16[64,1792]{1,0:T(8,128)(2,1)S(1)} %get-tuple-element.41), channel_id=1, source_target_pairs={{0,8},{4,12},{8,0},{12,4},{1,9},{5,13},{9,1},{13,5},{2,10},{6,14},... | collective-permute-start | bytes 688136 | tf_op jit(solution)/shard_map/ppermute | solution.py:319

commit v4 on v3

--- a/solution.py
+++ b/solution.py
@@ -52,19 +52,33 @@
     place = lax.broadcasted_iota(jnp.int32, (heads, positions), 1)
     lanes = latent.shape[2]
 
-    def attend_rows(step, carry):
-        for copy in key_copies(step):
-            copy.wait()
+    def score_rows(step):
         scores = []
         for pair in range(step_rows // 2):
             first = step * step_rows + 2 * pair
-            cut = pl.ds(pl.multiple_of(first * heads, 2 * heads), 2 * heads)
+            cut = slice(first * heads, (first + 2) * heads)
             for r in range(2):
                 score = lax.dot_general(
                     q[cut, :], k[first + r], (((1,), (1,)), ((), ())), preferred_element_type=jnp.float32
                 )
                 score += jnp.dot(rope[cut, :], kr[first + r], preferred_element_type=jnp.float32)
                 scores.append(score[r * heads : (r + 1) * heads, :])
+        return scores
+
+    def mix_rows(step, probabilities):
+        for r in range(step_rows):
+            row = step * step_rows + r
+            mixed = jnp.dot(probabilities[r], k[row], preferred_element_type=jnp.float32)
+            for c in range(latent.shape[0]):
+                latent[c, row * heads : (row + 1) * heads, :] = mixed[:, c * lanes : (c + 1) * lanes]
+
+    probabilities = None
+    for step in range(steps):
+        for copy in key_copies(step):
+            copy.wait()
+        scores = score_rows(step)
+        if step:
+            mix_rows(step - 1, probabilities)
         probabilities = []
         for r in range(step_rows):
             visible = place < lengths[step * step_rows + r]
@@ -72,14 +86,7 @@
             weight = jnp.exp(score - jnp.max(score, axis=-1, keepdims=True))
             total = jnp.sum(weight, axis=-1, keepdims=True)
             probabilities.append((weight / total).astype(jnp.bfloat16))
-        for r in range(step_rows):
-            row = step * step_rows + r
-            mixed = jnp.dot(probabilities[r], k[row], preferred_element_type=jnp.float32)
-            for c in range(latent.shape[0]):
-                latent[c, pl.ds(pl.multiple_of(row * heads, heads), heads), :] = mixed[:, c * lanes : (c + 1) * lanes]
-        return carry
-
-    lax.fori_loop(0, steps, attend_rows, 0)
+    mix_rows(steps - 1, probabilities)
     copies[2].wait()
     width = up.shape[2]
     for h in range(heads):
@@ -92,7 +99,7 @@
 
 def attend(query_latent, query_rope, cache_latent, cache_rope, cache_length, value_up):
     rows, heads, latent_width = query_latent.shape
-    step_rows = 16
+    step_rows = 8
     steps = rows // step_rows
     hbm = pl.BlockSpec(memory_space=pltpu.HBM)
     return pl.pallas_call(
@@ -114,7 +121,7 @@
         cost_estimate=pl.CostEstimate(
             flops=64 * heads * cache_latent.size, bytes_accessed=2 * cache_latent.size, transcendentals=0
         ),
-        compiler_params=pltpu.CompilerParams(vmem_limit_bytes=58 * MIB),
+        compiler_params=pltpu.CompilerParams(vmem_limit_bytes=60 * MIB),
         name="attention",
     )(
         cache_length,
@@ -126,71 +133,86 @@
     )
 
 
-def projection_kernel(count, out_count, places, *refs):
-    blocks, weight, outs = refs[:count], refs[count], refs[-2 - out_count : -2]
-    gathered, result = refs[-2:]
+def projection_kernel(count, parts, out_count, places, *refs):
+    blocks, weight_hbm = refs[:count], refs[count]
+    outs, (gathered, weight, sums, result, sems, weight_sems) = refs[-6 - out_count : -6], refs[-6:]
     height = blocks[0].shape[0]
+    depth, columns = weight.shape
+    step = depth // parts
+    weight_copies = [
+        pltpu.make_async_copy(
+            weight_hbm.at[pl.ds(i * step, step)], weight.at[pl.ds(i * step, step)], weight_sems.at[i]
+        )
+        for i in range(parts)
+    ]
+    copies = []
     for k in range(count):
         first = pl.multiple_of(places[k] * height, height)
-        gathered[pl.ds(first, height), :] = blocks[k][...]
-    columns = weight.shape[1]
+        copies.append(pltpu.make_async_copy(blocks[k], gathered.at[pl.ds(first, height), :], sems.at[k]))
+    for copy in copies + weight_copies:
+        copy.start()
+    for copy in copies:
+        copy.wait()
     tile = 256 if columns % 256 == 0 else 128
-    for j in range(columns // tile):
-        result[:, j * tile : (j + 1) * tile] = jnp.dot(
-            gathered[...], weight[:, j * tile : (j + 1) * tile], preferred_element_type=jnp.float32
-        ).astype(jnp.bfloat16)
+    for i in range(parts):
+        weight_copies[i].wait()
+        rows = slice(i * step, (i + 1) * step)
+        for j in range(columns // tile):
+            cut = slice(j * tile, (j + 1) * tile)
+            product = jnp.dot(gathered[:, rows], weight[rows, cut], preferred_element_type=jnp.float32)
+            if i:
+                product += sums[:, cut]
+            if i < parts - 1:
+                sums[:, cut] = product
+            else:
+                result[:, cut] = product.astype(jnp.bfloat16)
     out_height = outs[0].shape[0]
-    for s in range(len(outs)):
+    for s in range(out_count):
         first = pl.multiple_of(places[count + s] * out_height, out_height)
         outs[s][...] = result[pl.ds(first, out_height), :]
 
 
-def project(places, blocks, weight, out_count, after):
-    count = len(blocks)
+def project(places, blocks, weight, out_count):
+    count, parts = len(blocks), 2
     height, depth = blocks[0].shape
     rows, columns = height * count, weight.shape[1]
-    whole = pl.BlockSpec(memory_space=pltpu.VMEM)
     return pl.pallas_call(
-        functools.partial(projection_kernel, count, out_count),
+        functools.partial(projection_kernel, count, parts, out_count),
         out_shape=[jax.ShapeDtypeStruct((rows // out_count, columns), jnp.bfloat16)] * out_count,
-        in_specs=[pl.BlockSpec(memory_space=pltpu.SMEM)]
-        + [whole] * (count + 1)
-        + [pl.BlockSpec(memory_space=pl.ANY)] * len(after),
-        out_specs=[whole] * out_count,
+        in_specs=[pl.BlockSpec(memory_space=pltpu.SMEM)] + [pl.BlockSpec(memory_space=pl.ANY)] * (count + 1),
+        out_specs=[pl.BlockSpec(memory_space=pltpu.VMEM)] * out_count,
         scratch_shapes=[
             pltpu.VMEM((rows, depth), jnp.bfloat16),
+            pltpu.VMEM(weight.shape, jnp.bfloat16),
+            pltpu.VMEM((rows, columns), jnp.float32),
             pltpu.VMEM((rows, columns), jnp.bfloat16),
+            pltpu.SemaphoreType.DMA((count,)),
+            pltpu.SemaphoreType.DMA((parts,)),
         ],
-        cost_estimate=pl.CostEstimate(flops=2 * rows * depth * columns, bytes_accessed=4 * MIB, transcendentals=0),
-        compiler_params=pltpu.CompilerParams(vmem_limit_bytes=8 * MIB),
+        cost_estimate=pl.CostEstimate(flops=2 * rows * depth * columns, bytes_accessed=2 * weight.size, transcendentals=0),
+        compiler_params=pltpu.CompilerParams(vmem_limit_bytes=53 * MIB),
         name="projection",
-    )(places, *blocks, weight, *after)
-
-
-def touch_kernel(*refs):
-    refs[-1][...] = jnp.zeros(refs[-1].shape, jnp.float32)
-
-
-def touch(values, after):
-    return pl.pallas_call(
-        touch_kernel,
-        out_shape=jax.ShapeDtypeStruct((8, 128), jnp.float32),
-        in_specs=[pl.BlockSpec(memory_space=pltpu.VMEM)] * len(values)
-        + [pl.BlockSpec(memory_space=pl.ANY)] * len(after),
-        out_specs=pl.BlockSpec(memory_space=pltpu.VMEM),
-        compiler_params=pltpu.CompilerParams(vmem_limit_bytes=24 * MIB),
-        name="touch",
-    )(*values, *after)
-
-
-def expert_kernel(row_blocks, column_blocks, cores, model_width, places, *refs):
+    )(places, *blocks, weight)
+
+
+def gate_kernel(row_blocks, column_blocks, model_width, places, *refs):
     count = row_blocks * column_blocks
     blocks, gains = refs[:count], refs[count : count + column_blocks]
-    row_weight, gate, up, down = refs[count + column_blocks : count + column_blocks + 4]
-    outs = refs[count + column_blocks + 4 : -4]
-    x, gate_sum, up_sum, active = refs[-4:]
+    gate_hbm, up_hbm = refs[count + column_blocks : count + column_blocks + 2]
+    active, x, gate, up, gate_sum, up_sum, sems = refs[-7:]
     height, width = blocks[0].shape
     hidden = gate.shape[2]
+    copies = []
+    for k in range(column_blocks):
+        first = pl.multiple_of(places[k] * width, width)
+        copies.append(
+            (
+                pltpu.make_async_copy(gate_hbm.at[0, pl.ds(first, width), :], gate.at[k], sems.at[0, k]),
+                pltpu.make_async_copy(up_hbm.at[0, pl.ds(first, width), :], up.at[k], sems.at[1, k]),
+            )
+        )
+        copies[k][0].start()
+        copies[k][1].start()
     squares = [jnp.zeros((height, 1), jnp.float32) for _ in range(row_blocks)]
     tile = min(256, hidden)
     for k in range(column_blocks):
@@ -198,11 +220,11 @@
             wide = blocks[s * column_blocks + k][...].astype(jnp.float32)
             squares[s] += jnp.sum(wide * wide, axis=-1, keepdims=True)
             x[k, s * height : (s + 1) * height, :] = (wide * gains[k][...]).astype(jnp.bfloat16)
-        depth = pl.ds(pl.multiple_of(places[k] * width, 128), width)
-        for total, weight in ((gate_sum, gate), (up_sum, up)):
+        for w, total, weight in ((0, gate_sum, gate), (1, up_sum, up)):
+            copies[k][w].wait()
             for j in range(hidden // tile):
                 cut = slice(j * tile, (j + 1) * tile)
-                product = jnp.dot(x[k], weight[0, depth, cut], preferred_element_type=jnp.float32)
+                product = jnp.dot(x[k], weight[k, :, cut], preferred_element_type=jnp.float32)
                 if k == 0:
                     total[:, cut] = product
                 else:
@@ -213,49 +235,87 @@
         gate_part = gate_sum[rows, :] * scale
         up_part = up_sum[rows, :] * scale
         active[rows, :] = (gate_part / (1.0 + jnp.exp(-gate_part)) * up_part).astype(jnp.bfloat16)
+
+
+def activate(places, blocks, gains, gate_weight, up_weight, after):
+    row_blocks, column_blocks = len(blocks), len(blocks[0])
+    height, width = blocks[0][0].shape
+    rows = row_blocks * height
+    model_width, hidden = gate_weight.shape[1:]
+    whole = pl.BlockSpec(memory_space=pltpu.VMEM)
+    count = row_blocks * column_blocks
+    return pl.pallas_call(
+        functools.partial(gate_kernel, row_blocks, column_blocks, model_width),
+        out_shape=jax.ShapeDtypeStruct((rows, hidden), jnp.bfloat16),
+        in_specs=[pl.BlockSpec(memory_space=pltpu.SMEM)]
+        + [whole] * (count + column_blocks)
+        + [pl.BlockSpec(memory_space=pl.ANY)] * (2 + len(after)),
+        out_specs=whole,
+        scratch_shapes=[
+            pltpu.VMEM((column_blocks, rows, width), jnp.bfloat16),
+            pltpu.VMEM((column_blocks, width, hidden), jnp.bfloat16),
+            pltpu.VMEM((column_blocks, width, hidden), jnp.bfloat16),
+            pltpu.VMEM((rows, hidden), jnp.float32),
+            pltpu.VMEM((rows, hidden), jnp.float32),
+            pltpu.SemaphoreType.DMA((2, column_blocks)),
+        ],
+        cost_estimate=pl.CostEstimate(
+            flops=4 * rows * gate_weight.size, bytes_accessed=4 * gate_weight.size, transcendentals=rows * hidden
+        ),
+        compiler_params=pltpu.CompilerParams(vmem_limit_bytes=49 * MIB),
+        name="activate",
+    )(places, *[b for row in blocks for b in row], *gains, gate_weight, up_weight, *after)
+
+
+def down_kernel(row_blocks, column_blocks, cores, places, active, row_weight, down_hbm, *refs):
+    outs = refs[-2 - row_blocks * cores : -2]
+    down, sems = refs[-2:]
+    width = down.shape[2]
+    height = active.shape[0] // row_blocks
+    order = [b * cores + c for c in reversed(range(cores)) for b in range(column_blocks // cores)]
+    copies = {}
+    for k in order:
+        first = pl.multiple_of(places[k] * width, width)
+        copies[k] = pltpu.make_async_copy(down_hbm.at[0, :, pl.ds(first, width)], down.at[k], sems.at[k])
+        copies[k].start()
     tile = 256 if width % 256 == 0 else 128
     weights = []
     for s in range(row_blocks):
         first = pl.multiple_of(places[column_blocks + s] * height, height)
         weights.append(row_weight[pl.ds(first, height), :])
-    for c in reversed(range(cores)):
-        for b in range(column_blocks // cores):
-            start = pl.multiple_of(places[b * cores + c] * width, 128)
-            for j in range(width // tile):
-                cut = slice(j * tile, (j + 1) * tile)
-                product = jnp.dot(
-                    active[...], down[0, :, pl.ds(start + j * tile, tile)], preferred_element_type=jnp.float32
-                )
-                for s in range(row_blocks):
-                    part = product[s * height : (s + 1) * height, :] * weights[s]
-                    outs[s * cores + c][b * height : (b + 1) * height, cut] = part.astype(jnp.bfloat16)
-
-
-def run_expert(places, blocks, gains, row_weight, gate_weight, up_weight, down_weight, cores):
-    row_blocks, column_blocks = len(blocks), len(blocks[0])
-    height, width = blocks[0][0].shape
-    rows = row_blocks * height
-    hidden = gate_weight.shape[2]
+    for k in order:
+        b, c = k // cores, k % cores
+        copies[k].wait()
+        for j in range(width // tile):
+            cut = slice(j * tile, (j + 1) * tile)
+            product = jnp.dot(active[...], down[k, :, cut], preferred_element_type=jnp.float32)
+            for s in range(row_blocks):
+                part = product[s * height : (s + 1) * height, :] * weights[s]
+                outs[s * cores + c][b * height : (b + 1) * height, cut] = part.astype(jnp.bfloat16)
+
+
+def project_down(places, active, row_weight, down_weight, row_blocks, column_blocks, cores, after):
+    rows, hidden = active.shape
+    width = down_weight.shape[2] // column_blocks
     whole = pl.BlockSpec(memory_space=pltpu.VMEM)
-    count = row_blocks * column_blocks
-    out = jax.ShapeDtypeStruct((height * (column_blocks // cores), width), jnp.bfloat16)
+    out = jax.ShapeDtypeStruct((rows // row_blocks * (column_blocks // cores), width), jnp.bfloat16)
     outs = pl.pallas_call(
-        functools.partial(expert_kernel, row_blocks, column_blocks, cores, gate_weight.shape[1]),
+        functools.partial(down_kernel, row_blocks, column_blocks, cores),
         out_shape=[out] * (row_blocks * cores),
-        in_specs=[pl.BlockSpec(memory_space=pltpu.SMEM)] + [whole] * (count + column_blocks + 4),
+        in_specs=[pl.BlockSpec(memory_space=pltpu.SMEM)]
+        + [whole] * 2
+        + [pl.BlockSpec(memory_space=pl.ANY)] * (1 + len(after)),
         out_specs=[whole] * (row_blocks * cores),
         scratch_shapes=[
-            pltpu.VMEM((column_blocks, rows, width), jnp.bfloat16),
-            pltpu.VMEM((rows, hidden), jnp.float32),
-            pltpu.VMEM((rows, hidden), jnp.float32),
-            pltpu.VMEM((rows, hidden), jnp.bfloat16),
+            pltpu.VMEM((column_blocks, hidden, width), jnp.bfloat16),
+            pltpu.SemaphoreType.DMA((column_blocks,)),
         ],
         cost_estimate=pl.CostEstimate(
-            flops=6 * rows * hidden * gate_weight.shape[1], bytes_accessed=8 * MIB, transcendentals=rows * hidden
+            flops=2 * rows * down_weight.size, bytes_accessed=2 * down_weight.size, transcendentals=0
         ),
-        compiler_params=pltpu.CompilerParams(vmem_limit_bytes=2 * rows * (gate_weight.shape[1] + 5 * hidden) + 5 * MIB),
-        name="expert",
-    )(places, *[b for row in blocks for b in row], *gains, row_weight, gate_weight, up_weight, down_weight)
+        compiler_params=pltpu.CompilerParams(vmem_limit_bytes=49 * MIB),
+        name="down",
+    )(places, active, row_weight, down_weight, *after)
     return [outs[s * cores : (s + 1) * cores] for s in range(row_blocks)]
 
 
@@ -339,45 +399,56 @@
     row_weight = jnp.sum(jnp.where(routed_experts == ep_index, expert_gates, 0.0), axis=-1, keepdims=True)
 
     head_out = attend(query_latent, query_rope, cache_latent, cache_rope, cache_length, value_up)
-    partial = project(places, gather_ep(head_out), output_weight, tp_count, gains)
-    expert_weights = [gate_weight, up_weight, down_weight]
-    touched = touch(expert_weights, [partial[0]])
+    partial = project(places, gather_ep(head_out), output_weight, tp_count)
 
     own_residual = lax.dynamic_slice_in_dim(residual, tp_index * block_rows, block_rows, 0)
     terms = [[(value, 0)] for value in partial]
+    first = []
     for k in reversed(range(1, tp_count)):
-        total = add([terms[k]], block_rows)[0] if len(terms[k]) > 1 else terms[k][0][0]
+        total = terms[k][0][0]
+        if len(terms[k]) > 1 or (k == 1 and first):
+            (total,) = add([terms[k]], block_rows, first)
         low = k & -k
-        terms[k ^ low].append((from_tp(total, low), 0))
-    (stream,) = add([terms[0] + [(own_residual, 0)]], block_rows, [touched])
+        arrived = from_tp(total, low)
+        terms[k ^ low].append((arrived, 0))
+        first = first or [arrived]
+    stream_terms = terms[0] + [(own_residual, 0)]
+    stream, stream_out = add([stream_terms, stream_terms], block_rows, gains)
 
     rows_of = {0: stream}
     for k in range(1, tp_count):
         low = k & -k
         rows_of[k] = from_tp(rows_of[k ^ low], low)
     blocks = [gather_ep(rows_of[k]) for k in range(tp_count)]
-    outs = run_expert(places, blocks, gains, row_weight, *expert_weights, cores)
-
-    swapped = [from_core(out[1]) for out in outs]
+
+    half = tp_count // 2
+    groups = [list(reversed(range(1, half + 1))), list(reversed(range(half + 1, tp_count))) + [0]]
     terms = [[] for _ in range(tp_count)]
     arrivals = []
-    for k in reversed(range(tp_count)):
-        before = []
-        if len(arrivals) == 1:
-            before = arrivals[0]
-        elif len(arrivals) > 1:
-            before = arrivals[-2]
-        pair = [[(outs[k][0], c * block_rows), (swapped[k], c * block_rows)] for c in range(chips)]
-        sums = add(pair, block_rows, before)
-        across = [from_chip(sums[c], chips - c) for c in range(1, chips)]
-        arrivals.append(across)
-        terms[k] += [(value, 0) for value in [sums[0]] + across]
-        if k:
-            (total,) = add([terms[k]], block_rows)
-            low = k & -k
-            terms[k ^ low].append((from_tp(total, low), 0))
+    hold_gate, hold_down = blocks[0], [blocks[tp_count - 1][-2]]
+    for group in groups:
+        chosen = jnp.stack(ep_places + [tp_places[k] for k in group]).astype(jnp.int32)
+        active = activate(chosen, [blocks[k] for k in group], gains, gate_weight, up_weight, hold_gate)
+        outs = project_down(
+            chosen, active, row_weight, down_weight, len(group), ep_count, cores, hold_down
+        )
+        swapped = [from_core(out[1]) for out in outs]
+        for at, k in enumerate(group):
+            pair = [[(outs[at][0], c * block_rows), (swapped[at], c * block_rows)] for c in range(chips)]
+            wait = arrivals[0] if len(arrivals) == 1 else arrivals[-2] if arrivals else []
+            sums = add(pair, block_rows, wait)
+            across = [from_chip(sums[c], chips - c) for c in range(1, chips)]
+            if not arrivals:
+                hold_gate, hold_down = [sums[-1]], across
+            arrivals.append(across)
+            terms[k] += [(value, 0) for value in [sums[0]] + across]
+    for group in groups:
+        for k in group:
+            if k:
+                (total,) = add([terms[k]], block_rows)
+                terms[0].append((from_tp(total, k), 0))
     (mixed,) = add([terms[0]], block_rows)
-    return (stream, mixed)
+    return (stream_out, mixed)
 
 
 def solution(mesh):

time: 134 us -> 133 us (level)
  Pallas kernels: 26.1 us -> 46.6 us
  local copies, waits for them, and re-layouts: 22.6 us -> 7.96 us
  waiting for transfers between devices: 54.4 us -> 45.3 us
  starting transfers between devices: 29.6 us -> 31.8 us
    pallas_call x3 -> x5, Pallas kernels: 9.2 us -> 27.3 us  [the longest x2 13.8 us: activate(): pl.pallas_call(functools.partial(gate_kernel, row_blocks, column_blocks,...]
    unnamed x26 -> x28, local copies, waits for them, and re-layouts: 22.4 us -> 7.55 us
    ppermute x10, waiting for transfers between devices: 24.4 us -> 19.6 us  [from_chip(): lax.ppermute(value, 'ep', [(i, (i + step) % ep_count) for i in range(ep_c...]
    ppermute x9, starting transfers between devices: 12.2 us -> 16.3 us  [from_tp(): return lax.ppermute(value, 'tp', [(i, i ^ bits) for i in range(tp_count)])]
    ppermute x9, waiting for transfers between devices: 26.3 us -> 23.1 us  [from_tp(): return lax.ppermute(value, 'tp', [(i, i ^ bits) for i in range(tp_count)])]
    pallas_call x1, Pallas kernels: 14.7 us -> 16.3 us  [attend(): pl.pallas_call(functools.partial(attention_kernel, step_rows), out_shape=...]
    ppermute x10, starting transfers between devices: 15.1 us -> 13.7 us  [from_chip(): lax.ppermute(value, 'ep', [(i, (i + step) % ep_count) for i in range(ep_c...]
    pallas_call x10 -> x11, Pallas kernels: 2.29 us -> 2.99 us  [add(): pl.pallas_call(functools.partial(add_kernel, [[first for _, first in grou...]
  transfers between devices with their start and end apart: 35 -> 35, of which waited for: 17 -> 14; matrix products, arithmetic and copies ran while one was open for 0% -> 0% of each run, Pallas kernels for 1% -> 15%
where the time goes in v4:
time: 133 us
  Pallas kernels  46.6 us (35%)
  waiting for transfers between devices  45.3 us (34%)
  starting transfers between devices  31.8 us (24%)
  local copies, waits for them, and re-layouts  7.96 us (6%)
    ppermute x9, waiting for transfers between devices, from_tp(): return lax.ppermute(value, 'tp', [(i, i ^ bits) for i in range(tp_count)])  23.1 us
    ppermute x10, waiting for transfers between devices, from_chip(): lax.ppermute(value, 'ep', [(i, (i + step) % ep_count) for i in range(ep_c...  19.6 us
    ppermute x9, starting transfers between devices, from_tp(): return lax.ppermute(value, 'tp', [(i, i ^ bits) for i in range(tp_count)])  16.3 us
    pallas_call x1, Pallas kernels, attend(): pl.pallas_call(functools.partial(attention_kernel, step_rows), out_shape=...  16.3 us
    pallas_call x2, Pallas kernels, activate(): pl.pallas_call(functools.partial(gate_kernel, row_blocks, column_blocks,...  13.8 us
    ppermute x10, starting transfers between devices, from_chip(): lax.ppermute(value, 'ep', [(i, (i + step) % ep_count) for i in range(ep_c...  13.7 us
    pallas_call x2, Pallas kernels, project_down(): pl.pallas_call(functools.partial(down_kernel, row_blocks, column_blocks,...  8.39 us
    unnamed x28, local copies, waits for them, and re-layouts  7.55 us
  transfers between devices with their start and end apart: 35, of which 14 were waited for; matrix products, arithmetic and copies ran while one was open for 0% of the time, Pallas kernels for 15%

profile of v4, /device:TPU:0, one launch (start us, length us, event | category | flops | bytes accessed | tf_op | source)
XLA Modules:
  0.0 132.6 jit_solution(6051012993874100167)
XLA Ops:
  0.7 16.3 %attention.1.refs_0_ = bf16[64,1024]{1,0:T(8,128)(2,1)} custom-call(s32[64]{0:T(128)} %lengths.1, bf16[512,512]{1,0:T(8,128)(2,1)} %bitcast.10, bf16[64,512]{1,0:T(8,128)(2,1)} %qr_hbm.1, bf16[64,256,512]{2,1,0:T(8,128)(2,1)} %k_hbm.1, bf16[64,64,256]{2,1,0:T(8,128)(2,1)} %kr_hbm.1, bf16[8,512,128]{2,1,0:T(8,128)(2,1)} %up_hbm.1), custom_call_target="tpu_custom_call" | custom-call | flops 4294967296 | bytes 16777216 | tf_op jit(solution)/shard_map/attention/pallas_call | solution.py:105
  17.0 3.0 %collective-permute-start.1 = (bf16[64,1024]{1,0:T(8,128)(2,1)}, bf16[64,1024]{1,0:T(8,128)(2,1)S(1)}, u32[]{:S(2)}, u32[]{:S(2)}) collective-permute-start(bf16[64,1024]{1,0:T(8,128)(2,1)} %attention.1.refs_0_), channel_id=1, source_target_pairs={{0,8},{4,12},{8,0},{12,4},{1,9},{5,13},{9,1},{13,5},{2,10},{6,14},... | collective-permute-start | bytes 393224 | tf_op jit(solution)/shard_map/ppermute | solution.py:379
  20.0 3.7 %collective-permute-done.1.refs_2_ = bf16[64,1024]{1,0:T(8,128)(2,1)S(1)} collective-permute-done((bf16[64,1024]{1,0:T(8,128)(2,1)}, bf16[64,1024]{1,0:T(8,128)(2,1)S(1)}, u32[]{:S(2)}, u32[]{:S(2)}) %collective-permute-start.1) | collective-permute-done | bytes 131104 | tf_op jit(solution)/shard_map/ppermute | solution.py:379
  23.8 1.3 collective-permute-done.2.refs_3_
  25.0 0.9 copy-done.1
  25.9 5.1 %projection.1 = (bf16[64,1792]{1,0:T(8,128)(2,1)S(1)}, bf16[64,1792]{1,0:T(8,128)(2,1)}, bf16[64,1792]{1,0:T(8,128)(2,1)}, bf16[64,1792]{1,0:T(8,128)(2,1)}) custom-call(s32[8]{0:T(128)S(1)} %stack.53.places, bf16[64,1024]{1,0:T(8,128)(2,1)S(1)} %copy-done.1, bf16[64,1024]{1,0:T(8,128)(2,1)S(1)} %collective-permute-done.refs_1_, ...), custom_call_target="tpu_custom_call" | custom-call | flops 939524096 | bytes 3670016 | tf_op jit(solution)/shard_map/projection/pallas_call | solution.py:179
  31.1 1.9 %collective-permute-start.3 = (bf16[64,1792]{1,0:T(8,128)(2,1)}, bf16[64,1792]{1,0:T(8,128)(2,1)S(1)}, u32[]{:S(2)}, u32[]{:S(2)}) collective-permute-start(bf16[64,1792]{1,0:T(8,128)(2,1)} %get-tuple-element.26), channel_id=1, source_target_pairs={{0,1},{1,0},{2,3},{3,2},{4,5},{5,4},{6,7},{7,6},{8,9},{9,8},{10,11... | collective-permute-start | bytes 688136 | tf_op jit(solution)/shard_map/ppermute | solution.py:382
  32.9 1.6 %collective-permute-start.7 = (f32[1,1792]{1,0:T(1,128)S(1)}, f32[1,1792]{1,0:T(1,128)S(1)}, u32[]{:S(2)}, u32[]{:S(2)}) collective-permute-start(f32[1,1792]{1,0:T(1,128)S(1)} %reshape.11.refs_8_), channel_id=1, source_target_pairs={{0,8},{4,12},{8,0},{12,4},{1,9},{5,13},{9,1},{13,5},{2,10},{6,14},... | collective-permute-start | bytes 21512 | tf_op jit(solution)/shard_map/ppermute | solution.py:379
  34.5 2.1 %collective-permute-done.7.refs_10_ = f32[1,1792]{1,0:T(1,128)S(1)} collective-permute-done((f32[1,1792]{1,0:T(1,128)S(1)}, f32[1,1792]{1,0:T(1,128)S(1)}, u32[]{:S(2)}, u32[]{:S(2)}) %collective-permute-start.7) | collective-permute-done | bytes 7200 | tf_op jit(solution)/shard_map/ppermute | solution.py:379
  36.7 2.4 %collective-permute-done.3.refs_1_.refs_2_ = bf16[64,1792]{1,0:T(8,128)(2,1)S(1)} collective-permute-done((bf16[64,1792]{1,0:T(8,128)(2,1)}, bf16[64,1792]{1,0:T(8,128)(2,1)S(1)}, u32[]{:S(2)}, u32[]{:S(2)}) %collective-permute-start.3) | collective-permute-done | bytes 229408 | tf_op jit(solution)/shard_map/ppermute | solution.py:382
  39.1 0.9 copy-done.9
  40.0 1.8 %collective-permute-start.5 = (bf16[64,1792]{1,0:T(8,128)(2,1)S(1)}, bf16[64,1792]{1,0:T(8,128)(2,1)S(1)}, u32[]{:S(2)}, u32[]{:S(2)}) collective-permute-start(bf16[64,1792]{1,0:T(8,128)(2,1)S(1)} %add.61), channel_id=1, source_target_pairs={{0,1},{1,0},{2,3},{3,2},{4,5},{5,4},{6,7},{7,6},{8,9},{9,8},{10,11... | collective-permute-start | bytes 688136 | tf_op jit(solution)/shard_map/ppermute | solution.py:382
  41.8 0.9 copy-done.6
  42.8 2.7 %collective-permute-start.4 = (bf16[64,1792]{1,0:T(8,128)(2,1)S(1)}, bf16[64,1792]{1,0:T(8,128)(2,1)S(1)}, u32[]{:S(2)}, u32[]{:S(2)}) collective-permute-start(bf16[64,1792]{1,0:T(8,128)(2,1)S(1)} %add.60), channel_id=1, source_target_pairs={{0,2},{1,3},{2,0},{3,1},{4,6},{5,7},{6,4},{7,5},{8,10},{9,11},{10,... | collective-permute-start | bytes 688136 | tf_op jit(solution)/shard_map/ppermute | solution.py:382
  45.5 4.9 %collective-permute-done.5.refs_2_.refs_6_ = bf16[64,1792]{1,0:T(8,128)(2,1)S(1)} collective-permute-done((bf16[64,1792]{1,0:T(8,128)(2,1)S(1)}, bf16[64,1792]{1,0:T(8,128)(2,1)S(1)}, u32[]{:S(2)}, u32[]{:S(2)}) %collective-permute-start.5) | collective-permute-done | bytes 229408 | tf_op jit(solution)/shard_map/ppermute | solution.py:382
  50.5 5.2 %collective-permute-done.4.refs_1_.refs_5_ = bf16[64,1792]{1,0:T(8,128)(2,1)S(1)} collective-permute-done((bf16[64,1792]{1,0:T(8,128)(2,1)S(1)}, bf16[64,1792]{1,0:T(8,128)(2,1)S(1)}, u32[]{:S(2)}, u32[]{:S(2)}) %collective-permute-start.4) | collective-permute-done | bytes 229408 | tf_op jit(solution)/shard_map/ppermute | solution.py:382
  55.7 0.9 add.62
  56.5 2.7 %collective-permute-start.20 = (bf16[64,1792]{1,0:T(8,128)(2,1)S(1)}, bf16[64,1792]{1,0:T(8,128)(2,1)S(1)}, u32[]{:S(2)}, u32[]{:S(2)}) collective-permute-start(bf16[64,1792]{1,0:T(8,128)(2,1)S(1)} %get-tuple-element.29.refs_14_.refs_4_), channel_id=1, source_target_pairs={{0,1},{1,0},{2,3},{3,2},{4,5},{5,4},{6,7},{7,6},{8,9},{9,8},{10,11... | collective-permute-start | bytes 688136 | tf_op jit(solution)/shard_map/ppermute | solution.py:382
  59.2 1.5 %collective-permute-start.15 = (bf16[64,1792]{1,0:T(8,128)(2,1)S(1)}, bf16[64,1792]{1,0:T(8,128)(2,1)S(1)}, u32[]{:S(2)}, u32[]{:S(2)}) collective-permute-start(bf16[64,1792]{1,0:T(8,128)(2,1)S(1)} %get-tuple-element.29.refs_14_.refs_4_), channel_id=1, source_target_pairs={{0,8},{4,12},{8,0},{12,4},{1,9},{5,13},{9,1},{13,5},{2,10},{6,14},... | collective-permute-start | bytes 688136 | tf_op jit(solution)/shard_map/ppermute | solution.py:379
  60.7 4.9 %collective-permute-done.9.refs_0_ = bf16[64,1792]{1,0:T(8,128)(2,1)S(1)} collective-permute-done((bf16[64,1792]{1,0:T(8,128)(2,1)S(1)}, bf16[64,1792]{1,0:T(8,128)(2,1)S(1)}, u32[]{:S(2)}, u32[]{:S(2)}) %collective-permute-start.9) | collective-permute-done | bytes 229408 | tf_op jit(solution)/shard_map/ppermute | solution.py:382
  65.6 1.5 %collective-permute-start.18 = (bf16[64,1792]{1,0:T(8,128)(2,1)S(1)}, bf16[64,1792]{1,0:T(8,128)(2,1)S(1)}, u32[]{:S(2)}, u32[]{:S(2)}) collective-permute-start(bf16[64,1792]{1,0:T(8,128)(2,1)S(1)} %collective-permute-done.9.refs_0_), channel_id=1, source_target_pairs={{0,8},{4,12},{8,0},{12,4},{1,9},{5,13},{9,1},{13,5},{2,10},{6,14},... | collective-permute-start | bytes 688136 | tf_op jit(solution)/shard_map/ppermute | solution.py:379
  67.1 0.5 collective-permute-start.22
  67.7 1.3 collective-permute-start.10
  69.2 3.4 %collective-permute-done.18.refs_2_ = bf16[64,1792]{1,0:T(8,128)(2,1)S(1)} collective-permute-done((bf16[64,1792]{1,0:T(8,128)(2,1)S(1)}, bf16[64,1792]{1,0:T(8,128)(2,1)S(1)}, u32[]{:S(2)}, u32[]{:S(2)}) %collective-permute-start.18) | collective-permute-done | bytes 229408 | tf_op jit(solution)/shard_map/ppermute | solution.py:379
  72.6 2.5 %collective-permute-done.22.refs_6_ = bf16[64,1792]{1,0:T(8,128)(2,1)S(1)} collective-permute-done((bf16[64,1792]{1,0:T(8,128)(2,1)S(1)}, bf16[64,1792]{1,0:T(8,128)(2,1)S(1)}, u32[]{:S(2)}, u32[]{:S(2)}) %collective-permute-start.22) | collective-permute-done | bytes 229408 | tf_op jit(solution)/shard_map/ppermute | solution.py:379
  75.1 0.7 copy-done.2
  76.3 0.7 copy-done.4
  77.0 1.5 %collective-permute-start.12 = (bf16[64,1792]{1,0:T(8,128)(2,1)S(1)}, bf16[64,1792]{1,0:T(8,128)(2,1)S(1)}, u32[]{:S(2)}, u32[]{:S(2)}) collective-permute-start(bf16[64,1792]{1,0:T(8,128)(2,1)S(1)} %collective-permute-done.10.refs_0_), channel_id=1, source_target_pairs={{0,8},{4,12},{8,0},{12,4},{1,9},{5,13},{9,1},{13,5},{2,10},{6,14},... | collective-permute-start | bytes 688136 | tf_op jit(solution)/shard_map/ppermute | solution.py:379
  78.8 0.9 copy-done.3
  79.7 0.9 copy-done.5
  80.6 7.1 %activate.2.active = bf16[128,512]{1,0:T(8,128)(2,1)S(1)} custom-call(s32[6]{0:T(128)S(1)} %stack.55.places, bf16[64,1792]{1,0:T(8,128)(2,1)S(1)} %collective-permute-done.9.refs_0_, bf16[64,1792]{1,0:T(8,128)(2,1)} %collective-permute-done.17.refs_1_, bf16[64,1792]{1,0:T(8,128)(2,1)S(1)} %copy-done.3, bf16[64,1792]{1,0:T(8,128)(2,1)} %collective-permute-done.19.refs_3_, ...), custom_call_target="tpu_custom_call" | custom-call | flops 1879048192 | bytes 14680064 | tf_op jit(solution)/shard_map/activate/pallas_call | solution.py:247
  87.7 4.2 %down.2 = (bf16[128,1792]{1,0:T(8,128)(2,1)S(1)}, bf16[128,1792]{1,0:T(8,128)(2,1)S(1)}, bf16[128,1792]{1,0:T(8,128)(2,1)S(1)}, bf16[128,1792]{1,0:T(8,128)(2,1)S(1)}) custom-call(s32[6]{0:T(128)S(1)} %stack.55.places, bf16[128,512]{1,0:T(8,128)(2,1)S(1)} %activate.2.active, f32[256,1]{1,0:T(8,128)S(1)} %copy.16.row_weight, bf16[1,512,7168]{2,1,0:T(8,128)(2,1)} %down_hbm.3, ...), custom_call_target="tpu_custom_call" | custom-call | flops 939524096 | bytes 7340032 | tf_op jit(solution)/shard_map/down/pallas_call | solution.py:302
  92.0 0.8 copy-done.10
  93.2 1.3 collective-permute-done.24.refs_1_.refs_3_
  94.5 0.7 add.63
  95.3 0.7 copy-done.7
  96.6 6.8 %activate.3.active = bf16[128,512]{1,0:T(8,128)(2,1)S(1)} custom-call(s32[6]{0:T(128)S(1)} %stack.54.places, bf16[64,1792]{1,0:T(8,128)(2,1)S(1)} %collective-permute-done.10.refs_0_, bf16[64,1792]{1,0:T(8,128)(2,1)S(1)} %collective-permute-done.11.refs_1_, bf16[64,1792]{1,0:T(8,128)(2,1)S(1)} %collective-permute-done.12.refs_0_.refs_2_, ...), custom_call_target="tpu_custom_call" | custom-call | flops 1879048192 | bytes 14680064 | tf_op jit(solution)/shard_map/activate/pallas_call | solution.py:247
  103.9 4.2 %down.3 = (bf16[128,1792]{1,0:T(8,128)(2,1)S(1)}, bf16[128,1792]{1,0:T(8,128)(2,1)S(1)}, bf16[128,1792]{1,0:T(8,128)(2,1)S(1)}, bf16[128,1792]{1,0:T(8,128)(2,1)S(1)}) custom-call(s32[6]{0:T(128)S(1)} %stack.54.places, bf16[128,512]{1,0:T(8,128)(2,1)S(1)} %activate.3.active, f32[256,1]{1,0:T(8,128)S(1)} %copy.16.row_weight, bf16[1,512,7168]{2,1,0:T(8,128)(2,1)} %down_hbm.3, ...), custom_call_target="tpu_custom_call" | custom-call | flops 939524096 | bytes 7340032 | tf_op jit(solution)/shard_map/down/pallas_call | solution.py:302
  108.7 1.2 collective-permute-start.28
  110.0 1.3 collective-permute-start.33
  111.4 1.4 %collective-permute-start.30 = (bf16[64,1792]{1,0:T(8,128)(2,1)S(1)}, bf16[64,1792]{1,0:T(8,128)(2,1)S(1)}, u32[]{:S(2)}, u32[]{:S(2)}) collective-permute-start(bf16[64,1792]{1,0:T(8,128)(2,1)S(1)} %add.66), channel_id=1, source_target_pairs={{0,2},{1,3},{2,0},{3,1},{4,6},{5,7},{6,4},{7,5},{8,10},{9,11},{10,... | collective-permute-start | bytes 688136 | tf_op jit(solution)/shard_map/ppermute | solution.py:382
  112.7 4.5 %collective-permute-done.28.refs_4_.refs_1_ = bf16[64,1792]{1,0:T(8,128)(2,1)S(1)} collective-permute-done((bf16[64,1792]{1,0:T(8,128)(2,1)S(1)}, bf16[64,1792]{1,0:T(8,128)(2,1)S(1)}, u32[]{:S(2)}, u32[]{:S(2)}) %collective-permute-start.28) | collective-permute-done | bytes 229408 | tf_op jit(solution)/shard_map/ppermute | solution.py:379
  117.3 0.6 collective-permute-start.31
  118.1 1.1 collective-permute-start.29
  119.2 3.0 %collective-permute-done.33.refs_1_ = bf16[64,1792]{1,0:T(8,128)(2,1)S(1)} collective-permute-done((bf16[64,1792]{1,0:T(8,128)(2,1)S(1)}, bf16[64,1792]{1,0:T(8,128)(2,1)S(1)}, u32[]{:S(2)}, u32[]{:S(2)}) %collective-permute-start.33) | collective-permute-done | bytes 229408 | tf_op jit(solution)/shard_map/ppermute | solution.py:379
  122.2 3.9 %collective-permute-start.34 = (bf16[64,1792]{1,0:T(8,128)(2,1)S(1)}, bf16[64,1792]{1,0:T(8,128)(2,1)S(1)}, u32[]{:S(2)}, u32[]{:S(2)}) collective-permute-start(bf16[64,1792]{1,0:T(8,128)(2,1)S(1)} %add.69), channel_id=1, source_target_pairs={{0,3},{1,2},{2,1},{3,0},{4,7},{5,6},{6,5},{7,4},{8,11},{9,10},{10,... | collective-permute-start | bytes 688136 | tf_op jit(solution)/shard_map/ppermute | solution.py:382
  126.2 5.6 %collective-permute-done.31.refs_3_ = bf16[64,1792]{1,0:T(8,128)(2,1)S(1)} collective-permute-done((bf16[64,1792]{1,0:T(8,128)(2,1)S(1)}, bf16[64,1792]{1,0:T(8,128)(2,1)S(1)}, u32[]{:S(2)}, u32[]{:S(2)}) %collective-permute-start.31) | collective-permute-done | bytes 229408 | tf_op jit(solution)/shard_map/ppermute | solution.py:382
  131.8 0.8 add.70
  (74 shorter events, 3.9 us)
Async XLA Ops:
  0.6 44.9 %copy-start = (bf16[256,1792]{1,0:T(8,128)(2,1)S(1)}, bf16[256,1792]{1,0:T(8,128)(2,1)}, u32[]{:S(2)}) copy-start(bf16[256,1792]{1,0:T(8,128)(2,1)} %param.21) | copy-start | bytes 2752516
  0.6 32.3 %copy-start.11 = (f32[1792]{0:T(1024)S(1)}, f32[1792]{0:T(1024)}, u32[]{:S(2)}) copy-start(f32[1792]{0:T(1024)} %param.22) | copy-start | bytes 21508
  16.9 61.5 %copy-start.12 = (f32[256,2]{0,1:T(2,128)S(1)}, f32[256,2]{0,1:T(2,128)}, u32[]{:S(2)}) copy-start(f32[256,2]{0,1:T(2,128)} %param.24) | copy-start | bytes 6148
  17.0 61.5 %copy-start.13 = (s32[256,2]{0,1:T(2,128)S(1)}, s32[256,2]{0,1:T(2,128)}, u32[]{:S(2)}) copy-start(s32[256,2]{0,1:T(2,128)} %param.23) | copy-start | bytes 6148
  17.0 6.7 %collective-permute-start.1 = (bf16[64,1024]{1,0:T(8,128)(2,1)}, bf16[64,1024]{1,0:T(8,128)(2,1)S(1)}, u32[]{:S(2)}, u32[]{:S(2)}) collective-permute-start(bf16[64,1024]{1,0:T(8,128)(2,1)} %attention.1.refs_0_), channel_id=1, source_target_pairs={{0,8},{4,12},{8,0},{12,4},{1,9},{5,13},{9,1},{13,5},{2,10},{6,14},... | collective-permute-start | bytes 393224 | tf_op jit(solution)/shard_map/ppermute | solution.py:379
  20.0 3.8 %collective-permute-start = (bf16[64,1024]{1,0:T(8,128)(2,1)}, bf16[64,1024]{1,0:T(8,128)(2,1)S(1)}, u32[]{:S(2)}, u32[]{:S(2)}) collective-permute-start(bf16[64,1024]{1,0:T(8,128)(2,1)} %attention.1.refs_0_), channel_id=1, source_target_pairs={{0,4},{4,0},{8,12},{12,8},{1,5},{5,1},{9,13},{13,9},{2,6},{6,2},{1... | collective-permute-start | bytes 393224 | tf_op jit(solution)/shard_map/ppermute | solution.py:375
  23.7 1.3 %collective-permute-start.2 = (bf16[64,1024]{1,0:T(8,128)(2,1)S(1)}, bf16[64,1024]{1,0:T(8,128)(2,1)S(1)}, u32[]{:S(2)}, u32[]{:S(2)}) collective-permute-start(bf16[64,1024]{1,0:T(8,128)(2,1)S(1)} %collective-permute-done.1.refs_2_), channel_id=1, source_target_pairs={{0,4},{4,0},{8,12},{12,8},{1,5},{5,1},{9,13},{13,9},{2,6},{6,2},{1... | collective-permute-start | bytes 393224 | tf_op jit(solution)/shard_map/ppermute | solution.py:375
  25.0 0.9 copy-start.1
  31.1 8.0 %collective-permute-start.3 = (bf16[64,1792]{1,0:T(8,128)(2,1)}, bf16[64,1792]{1,0:T(8,128)(2,1)S(1)}, u32[]{:S(2)}, u32[]{:S(2)}) collective-permute-start(bf16[64,1792]{1,0:T(8,128)(2,1)} %get-tuple-element.26), channel_id=1, source_target_pairs={{0,1},{1,0},{2,3},{3,2},{4,5},{5,4},{6,7},{7,6},{8,9},{9,8},{10,11... | collective-permute-start | bytes 688136 | tf_op jit(solution)/shard_map/ppermute | solution.py:382
  32.9 3.7 %collective-permute-start.7 = (f32[1,1792]{1,0:T(1,128)S(1)}, f32[1,1792]{1,0:T(1,128)S(1)}, u32[]{:S(2)}, u32[]{:S(2)}) collective-permute-start(f32[1,1792]{1,0:T(1,128)S(1)} %reshape.11.refs_8_), channel_id=1, source_target_pairs={{0,8},{4,12},{8,0},{12,4},{1,9},{5,13},{9,1},{13,5},{2,10},{6,14},... | collective-permute-start | bytes 21512 | tf_op jit(solution)/shard_map/ppermute | solution.py:379
  34.5 11.0 %collective-permute-start.6 = (f32[1,1792]{1,0:T(1,128)S(1)}, f32[1,1792]{1,0:T(1,128)S(1)}, u32[]{:S(2)}, u32[]{:S(2)}) collective-permute-start(f32[1,1792]{1,0:T(1,128)S(1)} %reshape.11.refs_8_), channel_id=1, source_target_pairs={{0,4},{4,0},{8,12},{12,8},{1,5},{5,1},{9,13},{13,9},{2,6},{6,2},{1... | collective-permute-start | bytes 21512 | tf_op jit(solution)/shard_map/ppermute | solution.py:375
  36.7 8.9 %collective-permute-start.8 = (f32[1,1792]{1,0:T(1,128)S(1)}, f32[1,1792]{1,0:T(1,128)S(1)}, u32[]{:S(2)}, u32[]{:S(2)}) collective-permute-start(f32[1,1792]{1,0:T(1,128)S(1)} %collective-permute-done.7.refs_10_), channel_id=1, source_target_pairs={{0,4},{4,0},{8,12},{12,8},{1,5},{5,1},{9,13},{13,9},{2,6},{6,2},{1... | collective-permute-start | bytes 21512 | tf_op jit(solution)/shard_map/ppermute | solution.py:375
  39.1 0.9 copy-start.9
  40.0 10.4 %collective-permute-start.5 = (bf16[64,1792]{1,0:T(8,128)(2,1)S(1)}, bf16[64,1792]{1,0:T(8,128)(2,1)S(1)}, u32[]{:S(2)}, u32[]{:S(2)}) collective-permute-start(bf16[64,1792]{1,0:T(8,128)(2,1)S(1)} %add.61), channel_id=1, source_target_pairs={{0,1},{1,0},{2,3},{3,2},{4,5},{5,4},{6,7},{7,6},{8,9},{9,8},{10,11... | collective-permute-start | bytes 688136 | tf_op jit(solution)/shard_map/ppermute | solution.py:382
  41.8 0.9 copy-start.6
  42.8 12.8 %collective-permute-start.4 = (bf16[64,1792]{1,0:T(8,128)(2,1)S(1)}, bf16[64,1792]{1,0:T(8,128)(2,1)S(1)}, u32[]{:S(2)}, u32[]{:S(2)}) collective-permute-start(bf16[64,1792]{1,0:T(8,128)(2,1)S(1)} %add.60), channel_id=1, source_target_pairs={{0,2},{1,3},{2,0},{3,1},{4,6},{5,7},{6,4},{7,5},{8,10},{9,11},{10,... | collective-permute-start | bytes 688136 | tf_op jit(solution)/shard_map/ppermute | solution.py:382
  56.5 9.1 %collective-permute-start.9 = (bf16[64,1792]{1,0:T(8,128)(2,1)S(1)}, bf16[64,1792]{1,0:T(8,128)(2,1)S(1)}, u32[]{:S(2)}, u32[]{:S(2)}) collective-permute-start(bf16[64,1792]{1,0:T(8,128)(2,1)S(1)} %get-tuple-element.29.refs_14_.refs_4_), channel_id=1, source_target_pairs={{0,2},{1,3},{2,0},{3,1},{4,6},{5,7},{6,4},{7,5},{8,10},{9,11},{10,... | collective-permute-start | bytes 688136 | tf_op jit(solution)/shard_map/ppermute | solution.py:382
  56.5 10.6 %collective-permute-start.20 = (bf16[64,1792]{1,0:T(8,128)(2,1)S(1)}, bf16[64,1792]{1,0:T(8,128)(2,1)S(1)}, u32[]{:S(2)}, u32[]{:S(2)}) collective-permute-start(bf16[64,1792]{1,0:T(8,128)(2,1)S(1)} %get-tuple-element.29.refs_14_.refs_4_), channel_id=1, source_target_pairs={{0,1},{1,0},{2,3},{3,2},{4,5},{5,4},{6,7},{7,6},{8,9},{9,8},{10,11... | collective-permute-start | bytes 688136 | tf_op jit(solution)/shard_map/ppermute | solution.py:382
  59.2 8.5 %collective-permute-start.15 = (bf16[64,1792]{1,0:T(8,128)(2,1)S(1)}, bf16[64,1792]{1,0:T(8,128)(2,1)S(1)}, u32[]{:S(2)}, u32[]{:S(2)}) collective-permute-start(bf16[64,1792]{1,0:T(8,128)(2,1)S(1)} %get-tuple-element.29.refs_14_.refs_4_), channel_id=1, source_target_pairs={{0,8},{4,12},{8,0},{12,4},{1,9},{5,13},{9,1},{13,5},{2,10},{6,14},... | collective-permute-start | bytes 688136 | tf_op jit(solution)/shard_map/ppermute | solution.py:379
  60.7 8.3 %collective-permute-start.14 = (bf16[64,1792]{1,0:T(8,128)(2,1)S(1)}, bf16[64,1792]{1,0:T(8,128)(2,1)S(1)}, u32[]{:S(2)}, u32[]{:S(2)}) collective-permute-start(bf16[64,1792]{1,0:T(8,128)(2,1)S(1)} %get-tuple-element.29.refs_14_.refs_4_), channel_id=1, source_target_pairs={{0,4},{4,0},{8,12},{12,8},{1,5},{5,1},{9,13},{13,9},{2,6},{6,2},{1... | collective-permute-start | bytes 688136 | tf_op jit(solution)/shard_map/ppermute | solution.py:375
  65.6 7.0 %collective-permute-start.18 = (bf16[64,1792]{1,0:T(8,128)(2,1)S(1)}, bf16[64,1792]{1,0:T(8,128)(2,1)S(1)}, u32[]{:S(2)}, u32[]{:S(2)}) collective-permute-start(bf16[64,1792]{1,0:T(8,128)(2,1)S(1)} %collective-permute-done.9.refs_0_), channel_id=1, source_target_pairs={{0,8},{4,12},{8,0},{12,4},{1,9},{5,13},{9,1},{13,5},{2,10},{6,14},... | collective-permute-start | bytes 688136 | tf_op jit(solution)/shard_map/ppermute | solution.py:379
  67.1 7.9 %collective-permute-start.22 = (bf16[64,1792]{1,0:T(8,128)(2,1)S(1)}, bf16[64,1792]{1,0:T(8,128)(2,1)S(1)}, u32[]{:S(2)}, u32[]{:S(2)}) collective-permute-start(bf16[64,1792]{1,0:T(8,128)(2,1)S(1)} %collective-permute-done.20.refs_4_), channel_id=1, source_target_pairs={{0,8},{4,12},{8,0},{12,4},{1,9},{5,13},{9,1},{13,5},{2,10},{6,14},... | collective-permute-start | bytes 688136 | tf_op jit(solution)/shard_map/ppermute | solution.py:379
  67.7 8.1 %collective-permute-start.16 = (bf16[64,1792]{1,0:T(8,128)(2,1)S(1)}, bf16[64,1792]{1,0:T(8,128)(2,1)S(1)}, u32[]{:S(2)}, u32[]{:S(2)}) collective-permute-start(bf16[64,1792]{1,0:T(8,128)(2,1)S(1)} %collective-permute-done.15.refs_16_.refs_6_), channel_id=1, source_target_pairs={{0,4},{4,0},{8,12},{12,8},{1,5},{5,1},{9,13},{13,9},{2,6},{6,2},{1... | collective-permute-start | bytes 688136 | tf_op jit(solution)/shard_map/ppermute | solution.py:375
  67.7 9.3 %collective-permute-start.10 = (bf16[64,1792]{1,0:T(8,128)(2,1)S(1)}, bf16[64,1792]{1,0:T(8,128)(2,1)S(1)}, u32[]{:S(2)}, u32[]{:S(2)}) collective-permute-start(bf16[64,1792]{1,0:T(8,128)(2,1)S(1)} %collective-permute-done.9.refs_0_), channel_id=1, source_target_pairs={{0,1},{1,0},{2,3},{3,2},{4,5},{5,4},{6,7},{7,6},{8,9},{9,8},{10,11... | collective-permute-start | bytes 688136 | tf_op jit(solution)/shard_map/ppermute | solution.py:382
  69.0 9.7 %collective-permute-start.17 = (bf16[64,1792]{1,0:T(8,128)(2,1)S(1)}, bf16[64,1792]{1,0:T(8,128)(2,1)}, u32[]{:S(2)}, u32[]{:S(2)}) collective-permute-start(bf16[64,1792]{1,0:T(8,128)(2,1)S(1)} %collective-permute-done.9.refs_0_), channel_id=1, source_target_pairs={{0,4},{4,0},{8,12},{12,8},{1,5},{5,1},{9,13},{13,9},{2,6},{6,2},{1... | collective-permute-start | bytes 688136 | tf_op jit(solution)/shard_map/ppermute | solution.py:375
  72.6 6.1 %collective-permute-start.21 = (bf16[64,1792]{1,0:T(8,128)(2,1)S(1)}, bf16[64,1792]{1,0:T(8,128)(2,1)}, u32[]{:S(2)}, u32[]{:S(2)}) collective-permute-start(bf16[64,1792]{1,0:T(8,128)(2,1)S(1)} %collective-permute-done.20.refs_4_), channel_id=1, source_target_pairs={{0,4},{4,0},{8,12},{12,8},{1,5},{5,1},{9,13},{13,9},{2,6},{6,2},{1... | collective-permute-start | bytes 688136 | tf_op jit(solution)/shard_map/ppermute | solution.py:375
  75.0 3.7 %collective-permute-start.19 = (bf16[64,1792]{1,0:T(8,128)(2,1)S(1)}, bf16[64,1792]{1,0:T(8,128)(2,1)}, u32[]{:S(2)}, u32[]{:S(2)}) collective-permute-start(bf16[64,1792]{1,0:T(8,128)(2,1)S(1)} %collective-permute-done.18.refs_2_), channel_id=1, source_target_pairs={{0,4},{4,0},{8,12},{12,8},{1,5},{5,1},{9,13},{13,9},{2,6},{6,2},{1... | collective-permute-start | bytes 688136 | tf_op jit(solution)/shard_map/ppermute | solution.py:375
  75.7 3.0 %collective-permute-start.23 = (bf16[64,1792]{1,0:T(8,128)(2,1)S(1)}, bf16[64,1792]{1,0:T(8,128)(2,1)}, u32[]{:S(2)}, u32[]{:S(2)}) collective-permute-start(bf16[64,1792]{1,0:T(8,128)(2,1)S(1)} %collective-permute-done.22.refs_6_), channel_id=1, source_target_pairs={{0,4},{4,0},{8,12},{12,8},{1,5},{5,1},{9,13},{13,9},{2,6},{6,2},{1... | collective-permute-start | bytes 688136 | tf_op jit(solution)/shard_map/ppermute | solution.py:375
  76.3 0.7 copy-start.4
  77.0 10.8 %collective-permute-start.12 = (bf16[64,1792]{1,0:T(8,128)(2,1)S(1)}, bf16[64,1792]{1,0:T(8,128)(2,1)S(1)}, u32[]{:S(2)}, u32[]{:S(2)}) collective-permute-start(bf16[64,1792]{1,0:T(8,128)(2,1)S(1)} %collective-permute-done.10.refs_0_), channel_id=1, source_target_pairs={{0,8},{4,12},{8,0},{12,4},{1,9},{5,13},{9,1},{13,5},{2,10},{6,14},... | collective-permute-start | bytes 688136 | tf_op jit(solution)/shard_map/ppermute | solution.py:379
  78.7 0.9 copy-start.3
  79.7 0.9 copy-start.5
  91.9 0.8 copy-start.10
  92.7 1.8 %collective-permute-start.24 = (bf16[128,1792]{1,0:T(8,128)(2,1)S(1)}, bf16[128,1792]{1,0:T(8,128)(2,1)S(1)}, u32[]{:S(2)}, u32[]{:S(2)}) collective-permute-start(bf16[128,1792]{1,0:T(8,128)(2,1)S(1)} %get-tuple-element.31), channel_id=1, source_target_pairs={{0,4},{4,0},{8,12},{12,8},{1,5},{5,1},{9,13},{13,9},{2,6},{6,2},{1... | collective-permute-start | bytes 1376264 | tf_op jit(solution)/shard_map/ppermute | solution.py:375
  92.7 3.9 %collective-permute-start.11 = (bf16[64,1792]{1,0:T(8,128)(2,1)S(1)}, bf16[64,1792]{1,0:T(8,128)(2,1)S(1)}, u32[]{:S(2)}, u32[]{:S(2)}) collective-permute-start(bf16[64,1792]{1,0:T(8,128)(2,1)S(1)} %collective-permute-done.10.refs_0_), channel_id=1, source_target_pairs={{0,4},{4,0},{8,12},{12,8},{1,5},{5,1},{9,13},{13,9},{2,6},{6,2},{1... | collective-permute-start | bytes 688136 | tf_op jit(solution)/shard_map/ppermute | solution.py:375
  93.2 3.4 %collective-permute-start.13 = (bf16[64,1792]{1,0:T(8,128)(2,1)S(1)}, bf16[64,1792]{1,0:T(8,128)(2,1)}, u32[]{:S(2)}, u32[]{:S(2)}) collective-permute-start(bf16[64,1792]{1,0:T(8,128)(2,1)S(1)} %collective-permute-done.12.refs_0_.refs_2_), channel_id=1, source_target_pairs={{0,4},{4,0},{8,12},{12,8},{1,5},{5,1},{9,13},{13,9},{2,6},{6,2},{1... | collective-permute-start | bytes 688136 | tf_op jit(solution)/shard_map/ppermute | solution.py:375
  95.3 0.7 copy-start.7
  96.0 7.9 %collective-permute-start.25 = (bf16[64,1792]{1,0:T(8,128)(2,1)}, bf16[64,1792]{1,0:T(8,128)(2,1)S(1)}, u32[]{:S(2)}, u32[]{:S(2)}) collective-permute-start(bf16[64,1792]{1,0:T(8,128)(2,1)} %get-tuple-element.32.refs_14_), channel_id=1, source_target_pairs={{0,8},{4,12},{8,0},{12,4},{1,9},{5,13},{9,1},{13,5},{2,10},{6,14},... | collective-permute-start | bytes 688136 | tf_op jit(solution)/shard_map/ppermute | solution.py:379
  96.6 12.0 %collective-permute-start.27 = (bf16[128,1792]{1,0:T(8,128)(2,1)}, bf16[128,1792]{1,0:T(8,128)(2,1)S(1)}, u32[]{:S(2)}, u32[]{:S(2)}) collective-permute-start(bf16[128,1792]{1,0:T(8,128)(2,1)} %copy-done.10), channel_id=1, source_target_pairs={{0,4},{4,0},{8,12},{12,8},{1,5},{5,1},{9,13},{13,9},{2,6},{6,2},{1... | collective-permute-start | bytes 1376264 | tf_op jit(solution)/shard_map/ppermute | solution.py:375
  103.4 7.9 %copy-start.8 = (bf16[64,1792]{1,0:T(8,128)(2,1)S(1)}, bf16[64,1792]{1,0:T(8,128)(2,1)}, u32[]{:S(2)}) copy-start(bf16[64,1792]{1,0:T(8,128)(2,1)} %copy-done.7) | copy-start | bytes 688132
  108.1 1.9 %collective-permute-start.32 = (bf16[128,1792]{1,0:T(8,128)(2,1)S(1)}, bf16[128,1792]{1,0:T(8,128)(2,1)S(1)}, u32[]{:S(2)}, u32[]{:S(2)}) collective-permute-start(bf16[128,1792]{1,0:T(8,128)(2,1)S(1)} %get-tuple-element.43), channel_id=1, source_target_pairs={{0,4},{4,0},{8,12},{12,8},{1,5},{5,1},{9,13},{13,9},{2,6},{6,2},{1... | collective-permute-start | bytes 1376264 | tf_op jit(solution)/shard_map/ppermute | solution.py:375
  108.2 9.8 %collective-permute-start.26 = (bf16[128,1792]{1,0:T(8,128)(2,1)S(1)}, bf16[128,1792]{1,0:T(8,128)(2,1)S(1)}, u32[]{:S(2)}, u32[]{:S(2)}) collective-permute-start(bf16[128,1792]{1,0:T(8,128)(2,1)S(1)} %get-tuple-element.34), channel_id=1, source_target_pairs={{0,4},{4,0},{8,12},{12,8},{1,5},{5,1},{9,13},{13,9},{2,6},{6,2},{1... | collective-permute-start | bytes 1376264 | tf_op jit(solution)/shard_map/ppermute | solution.py:375
  108.7 8.5 %collective-permute-start.28 = (bf16[64,1792]{1,0:T(8,128)(2,1)S(1)}, bf16[64,1792]{1,0:T(8,128)(2,1)S(1)}, u32[]{:S(2)}, u32[]{:S(2)}) collective-permute-start(bf16[64,1792]{1,0:T(8,128)(2,1)S(1)} %get-tuple-element.37), channel_id=1, source_target_pairs={{0,8},{4,12},{8,0},{12,4},{1,9},{5,13},{9,1},{13,5},{2,10},{6,14},... | collective-permute-start | bytes 688136 | tf_op jit(solution)/shard_map/ppermute | solution.py:379
  110.0 12.1 %collective-permute-start.33 = (bf16[64,1792]{1,0:T(8,128)(2,1)S(1)}, bf16[64,1792]{1,0:T(8,128)(2,1)S(1)}, u32[]{:S(2)}, u32[]{:S(2)}) collective-permute-start(bf16[64,1792]{1,0:T(8,128)(2,1)S(1)} %get-tuple-element.45), channel_id=1, source_target_pairs={{0,8},{4,12},{8,0},{12,4},{1,9},{5,13},{9,1},{13,5},{2,10},{6,14},... | collective-permute-start | bytes 688136 | tf_op jit(solution)/shard_map/ppermute | solution.py:379
  111.4 14.8 %collective-permute-start.30 = (bf16[64,1792]{1,0:T(8,128)(2,1)S(1)}, bf16[64,1792]{1,0:T(8,128)(2,1)S(1)}, u32[]{:S(2)}, u32[]{:S(2)}) collective-permute-start(bf16[64,1792]{1,0:T(8,128)(2,1)S(1)} %add.66), channel_id=1, source_target_pairs={{0,2},{1,3},{2,0},{3,1},{4,6},{5,7},{6,4},{7,5},{8,10},{9,11},{10,... | collective-permute-start | bytes 688136 | tf_op jit(solution)/shard_map/ppermute | solution.py:382
  117.3 14.5 %collective-permute-start.31 = (bf16[64,1792]{1,0:T(8,128)(2,1)S(1)}, bf16[64,1792]{1,0:T(8,128)(2,1)S(1)}, u32[]{:S(2)}, u32[]{:S(2)}) collective-permute-start(bf16[64,1792]{1,0:T(8,128)(2,1)S(1)} %add.67), channel_id=1, source_target_pairs={{0,1},{1,0},{2,3},{3,2},{4,5},{5,4},{6,7},{7,6},{8,9},{9,8},{10,11... | collective-permute-start | bytes 688136 | tf_op jit(solution)/shard_map/ppermute | solution.py:382
  118.1 13.7 %collective-permute-start.29 = (bf16[64,1792]{1,0:T(8,128)(2,1)S(1)}, bf16[64,1792]{1,0:T(8,128)(2,1)S(1)}, u32[]{:S(2)}, u32[]{:S(2)}) collective-permute-start(bf16[64,1792]{1,0:T(8,128)(2,1)S(1)} %get-tuple-element.39), channel_id=1, source_target_pairs={{0,8},{4,12},{8,0},{12,4},{1,9},{5,13},{9,1},{13,5},{2,10},{6,14},... | collective-permute-start | bytes 688136 | tf_op jit(solution)/shard_map/ppermute | solution.py:379
  122.2 9.6 %collective-permute-start.34 = (bf16[64,1792]{1,0:T(8,128)(2,1)S(1)}, bf16[64,1792]{1,0:T(8,128)(2,1)S(1)}, u32[]{:S(2)}, u32[]{:S(2)}) collective-permute-start(bf16[64,1792]{1,0:T(8,128)(2,1)S(1)} %add.69), channel_id=1, source_target_pairs={{0,3},{1,2},{2,1},{3,0},{4,7},{5,6},{6,5},{7,4},{8,11},{9,10},{10,... | collective-permute-start | bytes 688136 | tf_op jit(solution)/shard_map/ppermute | solution.py:382
  (1 other events, 0.7 us)

commit v5 on v1

v5 whole, which is shorter than its diff:
```python
import functools

import jax
import jax.numpy as jnp
from jax import lax
from jax.experimental import pallas as pl
from jax.experimental.pallas import tpu as pltpu
from jax.sharding import PartitionSpec as P

score_scale = 1.0 / 192.0**0.5
norm_epsilon = 1e-06
MIB = 1 << 20


def in_hbm(value):
    return pltpu.with_memory_space_constraint(value, pltpu.HBM)


def in_vmem(value):
    return pltpu.with_memory_space_constraint(value, pltpu.VMEM)


def fetch_kernel(parts, *refs):
    source, target, sems = refs[0], refs[-2], refs[-1]
    step = source.shape[-2] // parts
    copies = []
    for i in range(parts):
        cut = (slice(None),) * (len(source.shape) - 2) + (pl.ds(i * step, step),)
        copies.append(pltpu.make_async_copy(source.at[cut], target.at[cut], sems.at[i]))
    for copy in copies:
        copy.start()
    for copy in copies:
        copy.wait()


def fetch(value, after):
    parts = 4
    return pl.pallas_call(
        functools.partial(fetch_kernel, parts),
        out_shape=pltpu.VMEM(value.shape, value.dtype),
        in_specs=[pl.BlockSpec(memory_space=pl.ANY)] * (1 + len(after)),
        out_specs=pl.BlockSpec(memory_space=pltpu.VMEM),
        scratch_shapes=[pltpu.SemaphoreType.DMA((parts,))],
        cost_estimate=pl.CostEstimate(flops=0, bytes_accessed=4 * value.size, transcendentals=0),
        compiler_params=pltpu.CompilerParams(vmem_limit_bytes=1 * MIB),
        name="fetch",
    )(in_hbm(value), *after)


def attention_kernel(step_rows, lengths, q_ref, qr_ref, k_ref, kr_ref, up_ref, out_ref, latent, rope):
    step = pl.program_id(0)
    heads, positions = q_ref.shape[1], k_ref.shape[1]
    rope_width = kr_ref.shape[1]

    @pl.when(step == 0)
    def _():
        all_rows = qr_ref.shape[0]
        width = heads * rope_width
        lane = lax.broadcasted_iota(jnp.int32, (heads, width), 1)
        head = lax.broadcasted_iota(jnp.int32, (heads, width), 0)
        own = jnp.where(lane // rope_width == head, 1.0, 0.0)
        spread = qr_ref[...].astype(jnp.float32)[:, None, :] * own[None, :, :]
        spread = spread.reshape(all_rows * heads, width).astype(jnp.bfloat16)
        lane = lax.broadcasted_iota(jnp.int32, (width, rope_width), 0)
        column = lax.broadcasted_iota(jnp.int32, (width, rope_width), 1)
        fold = jnp.where(lane % rope_width == column, 1.0, 0.0).astype(jnp.bfloat16)
        rope[...] = jnp.dot(spread, fold, preferred_element_type=jnp.float32)

    place = lax.broadcasted_iota(jnp.int32, (heads, positions), 1)
    lanes = latent.shape[2]
    lanes = latent.shape[2]
    scores = []
    for r in range(step_rows):
        first = pl.multiple_of((step * step_rows + r) * heads, heads)
        score = lax.dot_general(
            q_ref[r], k_ref[r], (((1,), (1,)), ((), ())), preferred_element_type=jnp.float32
        )
        score += jnp.dot(
            rope[pl.ds(first, heads), :].astype(jnp.bfloat16), kr_ref[r], preferred_element_type=jnp.float32
        )
        scores.append(score)
    probabilities = []
    for r in range(step_rows):
        visible = place < lengths[step * step_rows + r]
        score = jnp.where(visible, scores[r] * score_scale, -jnp.inf)
        weight = jnp.exp(score - jnp.max(score, axis=-1, keepdims=True))
        total = jnp.sum(weight, axis=-1, keepdims=True)
        probabilities.append((weight / total).astype(jnp.bfloat16))
    for r in range(step_rows):
        first = pl.multiple_of((step * step_rows + r) * heads, heads)
        mixed = jnp.dot(probabilities[r], k_ref[r], preferred_element_type=jnp.float32)
        for c in range(latent.shape[0]):
            latent[c, pl.ds(first, heads), :] = mixed[:, c * lanes : (c + 1) * lanes]

    @pl.when(step == pl.num_programs(0) - 1)
    def _():
        rows = out_ref.shape[0]
        width = up_ref.shape[2]
        for h in range(heads):
            parts = [latent[c, pl.ds(h, rows, stride=heads), :] for c in range(latent.shape[0])]
            part = jnp.concatenate(parts, axis=1).astype(jnp.bfloat16)
            out_ref[:, h * width : (h + 1) * width] = jnp.dot(
                part, up_ref[h], preferred_element_type=jnp.float32
            ).astype(jnp.bfloat16)


def attend(query_latent, query_rope, cache_latent, cache_rope, cache_length, value_up):
    rows, heads, latent_width = query_latent.shape
    positions = cache_latent.shape[1]
    rope_width = cache_rope.shape[1]
    value_width = value_up.shape[2]
    step_rows = 16
    by_row = lambda i, lengths: (i, 0, 0)
    return pl.pallas_call(
        functools.partial(attention_kernel, step_rows),
        out_shape=jax.ShapeDtypeStruct((rows, heads * value_width), jnp.bfloat16),
        grid_spec=pltpu.PrefetchScalarGridSpec(
            num_scalar_prefetch=1,
            grid=(rows // step_rows,),
            in_specs=[
                pl.BlockSpec((step_rows, heads, latent_width), by_row),
                pl.BlockSpec(query_rope.shape, lambda i, lengths: (0, 0)),
                pl.BlockSpec((step_rows, positions, latent_width), by_row),
                pl.BlockSpec((step_rows, rope_width, positions), by_row),
                pl.BlockSpec(value_up.shape, lambda i, lengths: (0, 0, 0)),
            ],
            out_specs=pl.BlockSpec((rows, heads * value_width), lambda i, lengths: (0, 0)),
            scratch_shapes=[
                pltpu.VMEM((latent_width // 128, rows * heads, 128), jnp.float32),
                pltpu.VMEM((rows * heads, rope_width), jnp.float32),
            ],
        ),
        cost_estimate=pl.CostEstimate(
            flops=64 * heads * cache_latent.size, bytes_accessed=2 * cache_latent.size, transcendentals=0
        ),
        compiler_params=pltpu.CompilerParams(vmem_limit_bytes=20 * MIB),
        name="attention",
    )(
        cache_length,
        in_hbm(query_latent),
        in_hbm(query_rope),
        in_hbm(cache_latent),
        in_hbm(cache_rope),
        in_hbm(value_up),
    )


def projection_kernel(count, out_count, places, *refs):
    blocks, weight, outs = refs[:count], refs[count], refs[-2 - out_count : -2]
    gathered, result = refs[-2:]
    height = blocks[0].shape[0]
    for k in range(count):
        first = pl.multiple_of(places[k] * height, height)
        gathered[pl.ds(first, height), :] = blocks[k][...]
    columns = weight.shape[1]
    tile = 256 if columns % 256 == 0 else 128
    for j in range(columns // tile):
        result[:, j * tile : (j + 1) * tile] = jnp.dot(
            gathered[...], weight[:, j * tile : (j + 1) * tile], preferred_element_type=jnp.float32
        ).astype(jnp.bfloat16)
    out_height = outs[0].shape[0]
    for s in range(len(outs)):
        first = pl.multiple_of(places[count + s] * out_height, out_height)
        outs[s][...] = result[pl.ds(first, out_height), :]


def project(places, blocks, weight, out_count):
    count = len(blocks)
    height, depth = blocks[0].shape
    rows, columns = height * count, weight.shape[1]
    whole = pl.BlockSpec(memory_space=pltpu.VMEM)
    return pl.pallas_call(
        functools.partial(projection_kernel, count, out_count),
        out_shape=[jax.ShapeDtypeStruct((rows // out_count, columns), jnp.bfloat16)] * out_count,
        in_specs=[pl.BlockSpec(memory_space=pltpu.SMEM)] + [whole] * (count + 1),
        out_specs=[whole] * out_count,
        scratch_shapes=[
            pltpu.VMEM((rows, depth), jnp.bfloat16),
            pltpu.VMEM((rows, columns), jnp.bfloat16),
        ],
        cost_estimate=pl.CostEstimate(flops=2 * rows * depth * columns, bytes_accessed=4 * MIB, transcendentals=0),
        compiler_params=pltpu.CompilerParams(vmem_limit_bytes=8 * MIB),
        name="projection",
    )(places, *blocks, in_vmem(weight))


def gate_kernel(row_blocks, column_blocks, model_width, places, *refs):
    count = row_blocks * column_blocks
    blocks, gains = refs[:count], refs[count : count + column_blocks]
    gate, up = refs[count + column_blocks : count + column_blocks + 2]
    active, x, gate_sum, up_sum = refs[-4:]
    height, width = blocks[0].shape
    hidden = gate.shape[2]
    squares = [jnp.zeros((height, 1), jnp.float32) for _ in range(row_blocks)]
    tile = min(256, hidden)
    for k in range(column_blocks):
        for s in range(row_blocks):
            wide = blocks[s * column_blocks + k][...].astype(jnp.float32)
            squares[s] += jnp.sum(wide * wide, axis=-1, keepdims=True)
            x[k, s * height : (s + 1) * height, :] = (wide * gains[k][...]).astype(jnp.bfloat16)
        depth = pl.ds(pl.multiple_of(places[k] * width, 128), width)
        for total, weight in ((gate_sum, gate), (up_sum, up)):
            for j in range(hidden // tile):
                cut = slice(j * tile, (j + 1) * tile)
                product = jnp.dot(x[k], weight[0, depth, cut], preferred_element_type=jnp.float32)
                if k == 0:
                    total[:, cut] = product
                else:
                    total[:, cut] += product
    for s in range(row_blocks):
        rows = slice(s * height, (s + 1) * height)
        scale = lax.rsqrt(squares[s] / model_width + norm_epsilon)
        gate_part = gate_sum[rows, :] * scale
        up_part = up_sum[rows, :] * scale
        active[rows, :] = (gate_part / (1.0 + jnp.exp(-gate_part)) * up_part).astype(jnp.bfloat16)


def activate(places, blocks, gains, gate_weight, up_weight, after):
    row_blocks, column_blocks = len(blocks), len(blocks[0])
    height, width = blocks[0][0].shape
    rows = row_blocks * height
    model_width, hidden = gate_weight.shape[1:]
    whole = pl.BlockSpec(memory_space=pltpu.VMEM)
    count = row_blocks * column_blocks
    return pl.pallas_call(
        functools.partial(gate_kernel, row_blocks, column_blocks, model_width),
        out_shape=jax.ShapeDtypeStruct((rows, hidden), jnp.bfloat16),
        in_specs=[pl.BlockSpec(memory_space=pltpu.SMEM)]
        + [whole] * (count + column_blocks + 2)
        + [pl.BlockSpec(memory_space=pl.ANY)] * len(after),
        out_specs=whole,
        scratch_shapes=[
            pltpu.VMEM((column_blocks, rows, width), jnp.bfloat16),
            pltpu.VMEM((rows, hidden), jnp.float32),
            pltpu.VMEM((rows, hidden), jnp.float32),
        ],
        cost_estimate=pl.CostEstimate(
            flops=4 * rows * gate_weight.size, bytes_accessed=4 * gate_weight.size, transcendentals=rows * hidden
        ),
        compiler_params=pltpu.CompilerParams(vmem_limit_bytes=2 * rows * (model_width + 4 * hidden) + 4 * MIB),
        name="activate",
    )(places, *[b for row in blocks for b in row], *gains, in_vmem(gate_weight), in_vmem(up_weight), *after)


def down_kernel(row_blocks, column_blocks, cores, places, active, row_weight, down, *refs):
    outs = refs[-row_blocks * cores :]
    width = down.shape[2] // column_blocks
    height = active.shape[0] // row_blocks
    order = [b * cores + c for c in reversed(range(cores)) for b in range(column_blocks // cores)]
    tile = 256 if width % 256 == 0 else 128
    weights = []
    for s in range(row_blocks):
        first = pl.multiple_of(places[column_blocks + s] * height, height)
        weights.append(row_weight[pl.ds(first, height), :])
    for k in order:
        b, c = k // cores, k % cores
        start = pl.multiple_of(places[k] * width, 128)
        for j in range(width // tile):
            cut = slice(j * tile, (j + 1) * tile)
            product = jnp.dot(
                active[...], down[0, :, pl.ds(start + j * tile, tile)], preferred_element_type=jnp.float32
            )
            for s in range(row_blocks):
                part = product[s * height : (s + 1) * height, :] * weights[s]
                outs[s * cores + c][b * height : (b + 1) * height, cut] = part.astype(jnp.bfloat16)


def project_down(places, active, row_weight, down_weight, row_blocks, column_blocks, cores, after):
    rows, hidden = active.shape
    width = down_weight.shape[2] // column_blocks
    whole = pl.BlockSpec(memory_space=pltpu.VMEM)
    out = jax.ShapeDtypeStruct((rows // row_blocks * (column_blocks // cores), width), jnp.bfloat16)
    outs = pl.pallas_call(
        functools.partial(down_kernel, row_blocks, column_blocks, cores),
        out_shape=[out] * (row_blocks * cores),
        in_specs=[pl.BlockSpec(memory_space=pltpu.SMEM)]
        + [whole] * 3
        + [pl.BlockSpec(memory_space=pl.ANY)] * len(after),
        out_specs=[whole] * (row_blocks * cores),
        cost_estimate=pl.CostEstimate(
            flops=2 * rows * down_weight.size, bytes_accessed=2 * down_weight.size, transcendentals=0
        ),
        compiler_params=pltpu.CompilerParams(vmem_limit_bytes=4 * MIB),
        name="down",
    )(places, active, row_weight, in_vmem(down_weight), *after)
    return [outs[s * cores : (s + 1) * cores] for s in range(row_blocks)]


def add_kernel(groups, *refs):
    used = sum(len(g) for g in groups)
    outs = refs[-len(groups) :]
    at = 0
    for group, out in zip(groups, outs):
        total = None
        for first in group:
            value = refs[at][first : first + out.shape[0], :].astype(jnp.float32)
            total = value if total is None else total + value
            at += 1
        out[...] = total.astype(jnp.bfloat16)


def add(groups, height, after=()):
    values = [value for group in groups for value, _ in group]
    width = values[0].shape[1]
    whole = pl.BlockSpec(memory_space=pltpu.VMEM)
    return pl.pallas_call(
        functools.partial(add_kernel, [[first for _, first in group] for group in groups]),
        out_shape=[jax.ShapeDtypeStruct((height, width), jnp.bfloat16)] * len(groups),
        in_specs=[whole] * len(values) + [pl.BlockSpec(memory_space=pl.ANY)] * len(after),
        out_specs=[whole] * len(groups),
        compiler_params=pltpu.CompilerParams(vmem_limit_bytes=8 * MIB),
        name="add",
    )(*values, *after)


def shards(
    query_latent,
    query_rope,
    cache_latent,
    cache_rope,
    cache_length,
    value_up,
    output_weight,
    residual,
    norm_gain,
    routed_experts,
    expert_gates,
    gate_weight,
    up_weight,
    down_weight,
):
    ep_count = lax.axis_size("ep")
    tp_count = lax.axis_size("tp")
    ep_index = lax.axis_index("ep")
    tp_index = lax.axis_index("tp")
    row_total = routed_experts.shape[0]
    block_rows = row_total // tp_count
    cores = 2
    chips = ep_count // cores

    def from_core(value):
        return lax.ppermute(value, "ep", [(i, i ^ 1) for i in range(ep_count)])

    def from_chip(value, back):
        step = cores * back
        return lax.ppermute(value, "ep", [(i, (i + step) % ep_count) for i in range(ep_count)])

    def from_tp(value, bits):
        return lax.ppermute(value, "tp", [(i, i ^ bits) for i in range(tp_count)])

    def gather_ep(value):
        same = [value] + [from_chip(value, b) for b in range(1, chips)]
        other = [from_core(v) for v in same]
        return [v for pair in zip(same, other) for v in pair]

    chip, core = ep_index // cores, ep_index % cores
    ep_places = [
        (chip - b + chips) % chips * cores + (core if c == 0 else 1 - core)
        for b in range(chips)
        for c in range(cores)
    ]
    tp_places = [tp_index ^ k for k in range(tp_count)]
    places = jnp.stack(ep_places + tp_places).astype(jnp.int32)

    gains = gather_ep(norm_gain.reshape(1, -1))
    row_weight = jnp.sum(jnp.where(routed_experts == ep_index, expert_gates, 0.0), axis=-1, keepdims=True)

    head_out = attend(query_latent, query_rope, cache_latent, cache_rope, cache_length, value_up)
    output_weight = fetch(output_weight, [head_out])
    partial = project(places, gather_ep(head_out), output_weight, tp_count)

    own_residual = lax.dynamic_slice_in_dim(residual, tp_index * block_rows, block_rows, 0)
    gate_weight = fetch(gate_weight, [partial[0]])
    terms = [[(value, 0)] for value in partial]
    first = []
    for k in reversed(range(1, tp_count)):
        total = terms[k][0][0]
        if len(terms[k]) > 1 or (k == 1 and first):
            (total,) = add([terms[k]], block_rows, first)
        low = k & -k
        arrived = from_tp(total, low)
        terms[k ^ low].append((arrived, 0))
        first = [total] if first else [arrived]
    up_weight = fetch(up_weight, [total])
    down_weight = fetch(down_weight, [total])
    stream_terms = terms[0] + [(own_residual, 0)]
    stream, stream_out = add([stream_terms, stream_terms], block_rows, gains + [gate_weight, up_weight, down_weight])

    rows_of = {0: stream}
    for k in range(1, tp_count):
        low = k & -k
        rows_of[k] = from_tp(rows_of[k ^ low], low)
    blocks = [gather_ep(rows_of[k]) for k in range(tp_count)]

    half = tp_count // 2
    groups = [list(reversed(range(1, half + 1))), list(reversed(range(half + 1, tp_count))) + [0]]
    terms = [[] for _ in range(tp_count)]
    arrivals = []
    hold_gate, hold_down = blocks[0], [blocks[tp_count - 1][-2]]
    for group in groups:
        chosen = jnp.stack(ep_places + [tp_places[k] for k in group]).astype(jnp.int32)
        active = activate(chosen, [blocks[k] for k in group], gains, gate_weight, up_weight, hold_gate)
        outs = project_down(
            chosen, active, row_weight, down_weight, len(group), ep_count, cores, hold_down
        )
        swapped = [from_core(out[1]) for out in outs]
        for at, k in enumerate(group):
            pair = [[(outs[at][0], c * block_rows), (swapped[at], c * block_rows)] for c in range(chips)]
            wait = arrivals[0] if len(arrivals) == 1 else arrivals[-2] if arrivals else []
            sums = add(pair, block_rows, wait)
            across = [from_chip(sums[c], chips - c) for c in range(1, chips)]
            if not arrivals:
                hold_gate, hold_down = [sums[-1]], across
            arrivals.append(across)
            terms[k] += [(value, 0) for value in [sums[0]] + across]
    for group in groups:
        for k in group:
            if k:
                (total,) = add([terms[k]], block_rows)
                terms[0].append((from_tp(total, k), 0))
    (mixed,) = add([terms[0]], block_rows)
    return (stream_out, mixed)


def solution(mesh):
    return jax.shard_map(
        shards,
        mesh=mesh,
        in_specs=(
            P(("parts", "ep"), "tp", None),
            P(("parts", "ep"), "tp"),
            P(("parts", "ep"), None, None),
            P(("parts", "ep"), None, None),
            P(("parts", "ep")),
            P("tp", None, None),
            P("tp", "ep"),
            P("parts", "ep"),
            P("ep"),
            P("parts", None),
            P("parts", None),
            P("ep", None, "tp"),
            P("ep", None, "tp"),
            P("ep", "tp", None),
        ),
        out_specs=(P(("parts", "tp"), "ep"), P(("parts", "tp"), "ep")),
        check_vma=False,
    )
```

time: 150 us -> 140 us (0.933)
  waiting for transfers between devices: 82.9 us -> 48.2 us
  Pallas kernels: 21.5 us -> 44.6 us
  local copies, waits for them, and re-layouts: 13.5 us -> 22.2 us
  starting transfers between devices: 28.2 us -> 23.4 us
  other arithmetic: 2.47 us -> 0.02 us
    ppermute x9, waiting for transfers between devices: 45.8 us -> 21.8 us  [from_tp(): return lax.ppermute(value, 'tp', [(i, i ^ bits) for i in range(tp_count)])]
    pallas_call x2 -> x20, Pallas kernels: 13 us -> 31.5 us  [the longest x4 16.9 us: fetch(): pl.pallas_call(functools.partial(fetch_kernel, parts), out_shape=pltpu.VM...]
    unnamed x28 -> x42, local copies, waits for them, and re-layouts: 12.3 us -> 21.7 us
    ppermute x10, waiting for transfers between devices: 31.7 us -> 25 us  [from_chip(): lax.ppermute(value, 'ep', [(i, (i + step) % ep_count) for i in range(ep_c...]
    pallas_call x1, Pallas kernels: 8.49 us -> 13.2 us  [attend(): pl.pallas_call(functools.partial(attention_kernel, step_rows), out_shape=...]
    ppermute x9, starting transfers between devices: 11.4 us -> 7.18 us  [from_tp(): return lax.ppermute(value, 'tp', [(i, i ^ bits) for i in range(tp_count)])]
    ppermute x20 -> x16, waiting for transfers between devices: 5.34 us -> 1.48 us  [from_core(): return lax.ppermute(value, 'ep', [(i, i ^ 1) for i in range(ep_count)])]
    convert_element_type x9 -> x0, other arithmetic: 2.45 us -> none  [the longest x8 1.37 us: add(): return sum((v.astype(jnp.float32) for v in values)).astype(jnp.bfloat16)]
  transfers between devices with their start and end apart: 39 -> 35, of which waited for: 19 -> 11; matrix products, arithmetic and copies ran while one was open for 1% -> 0% of each run, Pallas kernels for 0% -> 18%
where the time goes in v5:
time: 140 us; the launch traced here: 139 us
  waiting for transfers between devices  48.2 us (34%)
  Pallas kernels  44.6 us (32%)
  starting transfers between devices  23.4 us (17%)
  local copies, waits for them, and re-layouts  22.2 us (16%)
    ppermute x10, waiting for transfers between devices, from_chip(): lax.ppermute(value, 'ep', [(i, (i + step) % ep_count) for i in range(ep_c...  25 us
    ppermute x9, waiting for transfers between devices, from_tp(): return lax.ppermute(value, 'tp', [(i, i ^ bits) for i in range(tp_count)])  21.8 us
    unnamed x42, local copies, waits for them, and re-layouts  21.7 us
    pallas_call x4, Pallas kernels, fetch(): pl.pallas_call(functools.partial(fetch_kernel, parts), out_shape=pltpu.VM...  16.9 us
    ppermute x10, starting transfers between devices, from_chip(): lax.ppermute(value, 'ep', [(i, (i + step) % ep_count) for i in range(ep_c...  14 us
    pallas_call x1, Pallas kernels, attend(): pl.pallas_call(functools.partial(attention_kernel, step_rows), out_shape=...  13.2 us
    ppermute x9, starting transfers between devices, from_tp(): return lax.ppermute(value, 'tp', [(i, i ^ bits) for i in range(tp_count)])  7.18 us
    pallas_call x2, Pallas kernels, activate(): pl.pallas_call(functools.partial(gate_kernel, row_blocks, column_blocks,...  5.37 us
  transfers between devices with their start and end apart: 35, of which 11 were waited for; matrix products, arithmetic and copies ran while one was open for 0% of the time, Pallas kernels for 18%

profile of v5, /device:TPU:0, one launch (start us, length us, event | category | flops | bytes accessed | tf_op | source)
XLA Modules:
  0.0 139.5 jit_solution(15859024536735827648)
XLA Ops:
  0.7 0.7 copy-done.17
  1.4 13.2 %attention.1.refs_1_.refs_0_ = bf16[64,1024]{1,0:T(8,128)(2,1)S(1)} custom-call(s32[64]{0:T(128)S(1)} %copy-done.17, bf16[64,8,512]{2,1,0:T(8,128)(2,1)} %q_ref.1, bf16[64,512]{1,0:T(8,128)(2,1)} %qr_ref.1, bf16[64,256,512]{2,1,0:T(8,128)(2,1)} %k_ref.1, bf16[64,64,256]{2,1,0:T(8,128)(2,1)} %kr_ref.1, bf16[8,512,128]{2,1,0:T(8,128)(2,1)} %up_ref.1), custom_call_target="tpu_custom_call" | custom-call | flops 4294967296 | bytes 16777216 | tf_op jit(solution)/shard_map/attention/pallas_call | solution.py:114
  14.6 3.0 %collective-permute-start.1 = (bf16[64,1024]{1,0:T(8,128)(2,1)S(1)}, bf16[64,1024]{1,0:T(8,128)(2,1)S(1)}, u32[]{:S(2)}, u32[]{:S(2)}) collective-permute-start(bf16[64,1024]{1,0:T(8,128)(2,1)S(1)} %attention.1.refs_1_.refs_0_), channel_id=1, source_target_pairs={{0,8},{4,12},{8,0},{12,4},{1,9},{5,13},{9,1},{13,5},{2,10},{6,14},... | collective-permute-start | bytes 393224 | tf_op jit(solution)/shard_map/ppermute | solution.py:346
  17.6 3.5 %collective-permute-done.1.refs_2_ = bf16[64,1024]{1,0:T(8,128)(2,1)S(1)} collective-permute-done((bf16[64,1024]{1,0:T(8,128)(2,1)S(1)}, bf16[64,1024]{1,0:T(8,128)(2,1)S(1)}, u32[]{:S(2)}, u32[]{:S(2)}) %collective-permute-start.1) | collective-permute-done | bytes 131104 | tf_op jit(solution)/shard_map/ppermute | solution.py:346
  21.1 2.0 %fetch.4.refs_4_ = bf16[1024,1792]{1,0:T(8,128)(2,1)S(1)} custom-call(bf16[1024,1792]{1,0:T(8,128)(2,1)} %refs_0_.4, bf16[64,1024]{1,0:T(8,128)(2,1)S(1)} %attention.1.refs_1_.refs_0_), custom_call_target="tpu_custom_call" | custom-call | bytes 7340032 | tf_op jit(solution)/shard_map/fetch/pallas_call | solution.py:38
  23.2 1.8 %copy-done.11 = bf16[1024,1792]{1,0:T(8,128)(2,1)} copy-done((bf16[1024,1792]{1,0:T(8,128)(2,1)}, bf16[1024,1792]{1,0:T(8,128)(2,1)S(1)}, u32[]{:S(2)}) %copy-start.11) | copy-done | bytes 3670040
  25.0 2.0 %copy-done.12 = bf16[1024,1792]{1,0:T(8,128)(2,1)S(1)} copy-done((bf16[1024,1792]{1,0:T(8,128)(2,1)S(1)}, bf16[1024,1792]{1,0:T(8,128)(2,1)}, u32[]{:S(2)}) %copy-start.12) | copy-done | bytes 3670040
  27.1 1.7 %projection.1 = (bf16[64,1792]{1,0:T(8,128)(2,1)S(1)}, bf16[64,1792]{1,0:T(8,128)(2,1)S(1)}, bf16[64,1792]{1,0:T(8,128)(2,1)S(1)}, bf16[64,1792]{1,0:T(8,128)(2,1)S(1)}) custom-call(s32[8]{0:T(128)S(1)} %stack.53.places, bf16[64,1024]{1,0:T(8,128)(2,1)S(1)} %attention.1.refs_1_.refs_0_, bf16[64,1024]{1,0:T(8,128)(2,1)S(1)} %collective-permute-done.refs_1_, ...), custom_call_target="tpu_custom_call" | custom-call | flops 939524096 | bytes 4194304 | tf_op jit(solution)/shard_map/projection/pallas_call | solution.py:172
  28.8 1.9 %collective-permute-start.3 = (bf16[64,1792]{1,0:T(8,128)(2,1)S(1)}, bf16[64,1792]{1,0:T(8,128)(2,1)S(1)}, u32[]{:S(2)}, u32[]{:S(2)}) collective-permute-start(bf16[64,1792]{1,0:T(8,128)(2,1)S(1)} %get-tuple-element.26), channel_id=1, source_target_pairs={{0,1},{1,0},{2,3},{3,2},{4,5},{5,4},{6,7},{7,6},{8,9},{9,8},{10,11... | collective-permute-start | bytes 688136 | tf_op jit(solution)/shard_map/ppermute | solution.py:349
  30.7 1.6 %collective-permute-start.7 = (f32[1,1792]{1,0:T(1,128)S(1)}, f32[1,1792]{1,0:T(1,128)S(1)}, u32[]{:S(2)}, u32[]{:S(2)}) collective-permute-start(f32[1,1792]{1,0:T(1,128)S(1)} %reshape.7.refs_8_), channel_id=1, source_target_pairs={{0,8},{4,12},{8,0},{12,4},{1,9},{5,13},{9,1},{13,5},{2,10},{6,14},... | collective-permute-start | bytes 21512 | tf_op jit(solution)/shard_map/ppermute | solution.py:346
  32.3 2.1 %collective-permute-done.7.refs_10_ = f32[1,1792]{1,0:T(1,128)S(1)} collective-permute-done((f32[1,1792]{1,0:T(1,128)S(1)}, f32[1,1792]{1,0:T(1,128)S(1)}, u32[]{:S(2)}, u32[]{:S(2)}) %collective-permute-start.7) | collective-permute-done | bytes 7200 | tf_op jit(solution)/shard_map/ppermute | solution.py:346
  34.4 2.6 %collective-permute-done.3.refs_1_.refs_2_ = bf16[64,1792]{1,0:T(8,128)(2,1)S(1)} collective-permute-done((bf16[64,1792]{1,0:T(8,128)(2,1)S(1)}, bf16[64,1792]{1,0:T(8,128)(2,1)S(1)}, u32[]{:S(2)}, u32[]{:S(2)}) %collective-permute-start.3) | collective-permute-done | bytes 229408 | tf_op jit(solution)/shard_map/ppermute | solution.py:349
  37.0 2.8 %collective-permute-start.4 = (bf16[64,1792]{1,0:T(8,128)(2,1)S(1)}, bf16[64,1792]{1,0:T(8,128)(2,1)S(1)}, u32[]{:S(2)}, u32[]{:S(2)}) collective-permute-start(bf16[64,1792]{1,0:T(8,128)(2,1)S(1)} %add.60.refs_1_), channel_id=1, source_target_pairs={{0,2},{1,3},{2,0},{3,1},{4,6},{5,7},{6,4},{7,5},{8,10},{9,11},{10,... | collective-permute-start | bytes 688136 | tf_op jit(solution)/shard_map/ppermute | solution.py:349
  39.9 1.6 %collective-permute-start.5 = (bf16[64,1792]{1,0:T(8,128)(2,1)S(1)}, bf16[64,1792]{1,0:T(8,128)(2,1)S(1)}, u32[]{:S(2)}, u32[]{:S(2)}) collective-permute-start(bf16[64,1792]{1,0:T(8,128)(2,1)S(1)} %add.61.refs_1_), channel_id=1, source_target_pairs={{0,1},{1,0},{2,3},{3,2},{4,5},{5,4},{6,7},{7,6},{8,9},{9,8},{10,11... | collective-permute-start | bytes 688136 | tf_op jit(solution)/shard_map/ppermute | solution.py:349
  41.5 3.2 %fetch.5.refs_12_ = bf16[1,7168,512]{2,1,0:T(8,128)(2,1)S(1)} custom-call(bf16[1,7168,512]{2,1,0:T(8,128)(2,1)} %refs_0_.5, bf16[64,1792]{1,0:T(8,128)(2,1)S(1)} %get-tuple-element.24.refs_1_.refs_0_.refs_4_), custom_call_target="tpu_custom_call" | custom-call | bytes 14680064 | tf_op jit(solution)/shard_map/fetch/pallas_call | solution.py:38
  44.7 5.8 %fetch.6.refs_13_ = bf16[1,7168,512]{2,1,0:T(8,128)(2,1)S(1)} custom-call(bf16[1,7168,512]{2,1,0:T(8,128)(2,1)} %refs_0_.6, bf16[64,1792]{1,0:T(8,128)(2,1)S(1)} %add.61.refs_1_), custom_call_target="tpu_custom_call" | custom-call | bytes 14680064 | tf_op jit(solution)/shard_map/fetch/pallas_call | solution.py:38
  50.6 5.8 %fetch.7.refs_14_.down = bf16[1,512,7168]{2,1,0:T(8,128)(2,1)S(1)} custom-call(bf16[1,512,7168]{2,1,0:T(8,128)(2,1)} %refs_0_.7, bf16[64,1792]{1,0:T(8,128)(2,1)S(1)} %add.61.refs_1_), custom_call_target="tpu_custom_call" | custom-call | bytes 14680064 | tf_op jit(solution)/shard_map/fetch/pallas_call | solution.py:38
  56.5 1.1 add.62
  57.6 1.8 %copy-done.8 = bf16[1,512,7168]{2,1,0:T(8,128)(2,1)} copy-done((bf16[1,512,7168]{2,1,0:T(8,128)(2,1)}, bf16[1,512,7168]{2,1,0:T(8,128)(2,1)S(1)}, u32[]{:S(2)}) %copy-start.8) | copy-done | bytes 7340056
  60.0 1.7 %collective-permute-start.15 = (bf16[64,1792]{1,0:T(8,128)(2,1)S(1)}, bf16[64,1792]{1,0:T(8,128)(2,1)S(1)}, u32[]{:S(2)}, u32[]{:S(2)}) collective-permute-start(bf16[64,1792]{1,0:T(8,128)(2,1)S(1)} %get-tuple-element.29.refs_14_.refs_4_), channel_id=1, source_target_pairs={{0,8},{4,12},{8,0},{12,4},{1,9},{5,13},{9,1},{13,5},{2,10},{6,14},... | collective-permute-start | bytes 688136 | tf_op jit(solution)/shard_map/ppermute | solution.py:346
  61.7 10.1 %collective-permute-done.9.refs_0_ = bf16[64,1792]{1,0:T(8,128)(2,1)S(1)} collective-permute-done((bf16[64,1792]{1,0:T(8,128)(2,1)S(1)}, bf16[64,1792]{1,0:T(8,128)(2,1)S(1)}, u32[]{:S(2)}, u32[]{:S(2)}) %collective-permute-start.9) | collective-permute-done | bytes 229408 | tf_op jit(solution)/shard_map/ppermute | solution.py:349
  71.8 1.5 %collective-permute-start.18 = (bf16[64,1792]{1,0:T(8,128)(2,1)S(1)}, bf16[64,1792]{1,0:T(8,128)(2,1)S(1)}, u32[]{:S(2)}, u32[]{:S(2)}) collective-permute-start(bf16[64,1792]{1,0:T(8,128)(2,1)S(1)} %collective-permute-done.9.refs_0_), channel_id=1, source_target_pairs={{0,8},{4,12},{8,0},{12,4},{1,9},{5,13},{9,1},{13,5},{2,10},{6,14},... | collective-permute-start | bytes 688136 | tf_op jit(solution)/shard_map/ppermute | solution.py:346
  73.3 0.5 collective-permute-start.22
  74.3 5.9 %collective-permute-done.18.refs_2_ = bf16[64,1792]{1,0:T(8,128)(2,1)S(1)} collective-permute-done((bf16[64,1792]{1,0:T(8,128)(2,1)S(1)}, bf16[64,1792]{1,0:T(8,128)(2,1)S(1)}, u32[]{:S(2)}, u32[]{:S(2)}) %collective-permute-start.18) | collective-permute-done | bytes 229408 | tf_op jit(solution)/shard_map/ppermute | solution.py:346
  80.2 4.0 %collective-permute-done.22.refs_6_ = bf16[64,1792]{1,0:T(8,128)(2,1)S(1)} collective-permute-done((bf16[64,1792]{1,0:T(8,128)(2,1)S(1)}, bf16[64,1792]{1,0:T(8,128)(2,1)S(1)}, u32[]{:S(2)}, u32[]{:S(2)}) %collective-permute-start.22) | collective-permute-done | bytes 229408 | tf_op jit(solution)/shard_map/ppermute | solution.py:346
  84.7 1.5 %collective-permute-start.12 = (bf16[64,1792]{1,0:T(8,128)(2,1)S(1)}, bf16[64,1792]{1,0:T(8,128)(2,1)S(1)}, u32[]{:S(2)}, u32[]{:S(2)}) collective-permute-start(bf16[64,1792]{1,0:T(8,128)(2,1)S(1)} %collective-permute-done.10.refs_0_), channel_id=1, source_target_pairs={{0,8},{4,12},{8,0},{12,4},{1,9},{5,13},{9,1},{13,5},{2,10},{6,14},... | collective-permute-start | bytes 688136 | tf_op jit(solution)/shard_map/ppermute | solution.py:346
  86.5 3.1 %copy-done.3 = bf16[1,7168,512]{2,1,0:T(8,128)(2,1)S(1)} copy-done((bf16[1,7168,512]{2,1,0:T(8,128)(2,1)S(1)}, bf16[1,7168,512]{2,1,0:T(8,128)(2,1)}, u32[]{:S(2)}) %copy-start.3) | copy-done | bytes 7340056
  89.6 3.1 %copy-done.6 = bf16[1,7168,512]{2,1,0:T(8,128)(2,1)S(1)} copy-done((bf16[1,7168,512]{2,1,0:T(8,128)(2,1)S(1)}, bf16[1,7168,512]{2,1,0:T(8,128)(2,1)}, u32[]{:S(2)}) %copy-start.6) | copy-done | bytes 7340056
  92.7 2.7 %activate.2.active = bf16[128,512]{1,0:T(8,128)(2,1)S(1)} custom-call(s32[6]{0:T(128)S(1)} %stack.55.places, bf16[64,1792]{1,0:T(8,128)(2,1)S(1)} %collective-permute-done.9.refs_0_, bf16[64,1792]{1,0:T(8,128)(2,1)S(1)} %collective-permute-done.17.refs_1_, bf16[64,1792]{1,0:T(8,128)(2,1)S(1)} %collective-permute-done.18.refs_2_, ...), custom_call_target="tpu_custom_call" | custom-call | flops 1879048192 | bytes 14680064 | tf_op jit(solution)/shard_map/activate/pallas_call | solution.py:225
  95.8 2.4 %down.2 = (bf16[128,1792]{1,0:T(8,128)(2,1)S(1)}, bf16[128,1792]{1,0:T(8,128)(2,1)S(1)}, bf16[128,1792]{1,0:T(8,128)(2,1)S(1)}, bf16[128,1792]{1,0:T(8,128)(2,1)}) custom-call(s32[6]{0:T(128)S(1)} %stack.55.places, bf16[128,512]{1,0:T(8,128)(2,1)S(1)} %activate.2.active, f32[256,1]{1,0:T(8,128)S(1)} %copy.16.row_weight, bf16[1,512,7168]{2,1,0:T(8,128)(2,1)S(1)} %copy-done.9, ...), custom_call_target="tpu_custom_call" | custom-call | flops 939524096 | bytes 7340032 | tf_op jit(solution)/shard_map/down/pallas_call | solution.py:273
  98.7 1.3 collective-permute-done.24.refs_1_.refs_3_
  100.0 0.7 add.63
  100.8 0.7 copy-done.15
  101.5 1.0 collective-permute-start.25
  102.6 0.7 copy-done.13
  103.3 3.1 %copy-done.4 = bf16[1,7168,512]{2,1,0:T(8,128)(2,1)S(1)} copy-done((bf16[1,7168,512]{2,1,0:T(8,128)(2,1)S(1)}, bf16[1,7168,512]{2,1,0:T(8,128)(2,1)}, u32[]{:S(2)}) %copy-start.4) | copy-done | bytes 7340056
  106.3 3.1 %copy-done.7 = bf16[1,7168,512]{2,1,0:T(8,128)(2,1)S(1)} copy-done((bf16[1,7168,512]{2,1,0:T(8,128)(2,1)S(1)}, bf16[1,7168,512]{2,1,0:T(8,128)(2,1)}, u32[]{:S(2)}) %copy-start.7) | copy-done | bytes 7340056
  109.4 0.9 copy-done.14
  110.4 2.7 %activate.3.active = bf16[128,512]{1,0:T(8,128)(2,1)S(1)} custom-call(s32[6]{0:T(128)S(1)} %stack.54.places, bf16[64,1792]{1,0:T(8,128)(2,1)S(1)} %collective-permute-done.10.refs_0_, bf16[64,1792]{1,0:T(8,128)(2,1)S(1)} %collective-permute-done.11.refs_1_, bf16[64,1792]{1,0:T(8,128)(2,1)S(1)} %collective-permute-done.12.refs_0_.refs_2_, ...), custom_call_target="tpu_custom_call" | custom-call | flops 1879048192 | bytes 14680064 | tf_op jit(solution)/shard_map/activate/pallas_call | solution.py:225
  113.4 1.8 %down.3 = (bf16[128,1792]{1,0:T(8,128)(2,1)S(1)}, bf16[128,1792]{1,0:T(8,128)(2,1)S(1)}, bf16[128,1792]{1,0:T(8,128)(2,1)S(1)}, bf16[128,1792]{1,0:T(8,128)(2,1)S(1)}) custom-call(s32[6]{0:T(128)S(1)} %stack.54.places, bf16[128,512]{1,0:T(8,128)(2,1)S(1)} %activate.3.active, f32[256,1]{1,0:T(8,128)S(1)} %copy.16.row_weight, ...), custom_call_target="tpu_custom_call" | custom-call | flops 939524096 | bytes 7340032 | tf_op jit(solution)/shard_map/down/pallas_call | solution.py:273
  115.2 0.6 collective-permute-start.32
  116.0 1.1 collective-permute-start.28
  117.3 1.1 collective-permute-start.33
  118.6 5.9 %collective-permute-done.28.refs_4_.refs_1_ = bf16[64,1792]{1,0:T(8,128)(2,1)S(1)} collective-permute-done((bf16[64,1792]{1,0:T(8,128)(2,1)S(1)}, bf16[64,1792]{1,0:T(8,128)(2,1)S(1)}, u32[]{:S(2)}, u32[]{:S(2)}) %collective-permute-start.28) | collective-permute-done | bytes 229408 | tf_op jit(solution)/shard_map/ppermute | solution.py:346
  124.7 1.1 collective-permute-start.29
  125.8 3.6 %collective-permute-done.33.refs_1_ = bf16[64,1792]{1,0:T(8,128)(2,1)S(1)} collective-permute-done((bf16[64,1792]{1,0:T(8,128)(2,1)S(1)}, bf16[64,1792]{1,0:T(8,128)(2,1)S(1)}, u32[]{:S(2)}, u32[]{:S(2)}) %collective-permute-start.33) | collective-permute-done | bytes 229408 | tf_op jit(solution)/shard_map/ppermute | solution.py:346
  129.5 9.1 %collective-permute-done.31.refs_3_ = bf16[64,1792]{1,0:T(8,128)(2,1)S(1)} collective-permute-done((bf16[64,1792]{1,0:T(8,128)(2,1)S(1)}, bf16[64,1792]{1,0:T(8,128)(2,1)S(1)}, u32[]{:S(2)}, u32[]{:S(2)}) %collective-permute-start.31) | collective-permute-done | bytes 229408 | tf_op jit(solution)/shard_map/ppermute | solution.py:349
  138.6 0.8 add.70
  (92 shorter events, 4.5 us)
Async XLA Ops:
  0.6 40.9 %copy-start = (bf16[256,1792]{1,0:T(8,128)(2,1)S(1)}, bf16[256,1792]{1,0:T(8,128)(2,1)}, u32[]{:S(2)}) copy-start(bf16[256,1792]{1,0:T(8,128)(2,1)} %param.21) | copy-start | bytes 2752516
  14.6 16.1 %copy-start.18 = (f32[1792]{0:T(1024)S(1)}, f32[1792]{0:T(1024)}, u32[]{:S(2)}) copy-start(f32[1792]{0:T(1024)} %param.22) | copy-start | bytes 21508
  14.6 6.5 %collective-permute-start.1 = (bf16[64,1024]{1,0:T(8,128)(2,1)S(1)}, bf16[64,1024]{1,0:T(8,128)(2,1)S(1)}, u32[]{:S(2)}, u32[]{:S(2)}) collective-permute-start(bf16[64,1024]{1,0:T(8,128)(2,1)S(1)} %attention.1.refs_1_.refs_0_), channel_id=1, source_target_pairs={{0,8},{4,12},{8,0},{12,4},{1,9},{5,13},{9,1},{13,5},{2,10},{6,14},... | collective-permute-start | bytes 393224 | tf_op jit(solution)/shard_map/ppermute | solution.py:346
  17.6 7.4 %collective-permute-start = (bf16[64,1024]{1,0:T(8,128)(2,1)S(1)}, bf16[64,1024]{1,0:T(8,128)(2,1)S(1)}, u32[]{:S(2)}, u32[]{:S(2)}) collective-permute-start(bf16[64,1024]{1,0:T(8,128)(2,1)S(1)} %attention.1.refs_1_.refs_0_), channel_id=1, source_target_pairs={{0,4},{4,0},{8,12},{12,8},{1,5},{5,1},{9,13},{13,9},{2,6},{6,2},{1... | collective-permute-start | bytes 393224 | tf_op jit(solution)/shard_map/ppermute | solution.py:342
  21.1 3.9 %collective-permute-start.2 = (bf16[64,1024]{1,0:T(8,128)(2,1)S(1)}, bf16[64,1024]{1,0:T(8,128)(2,1)S(1)}, u32[]{:S(2)}, u32[]{:S(2)}) collective-permute-start(bf16[64,1024]{1,0:T(8,128)(2,1)S(1)} %collective-permute-done.1.refs_2_), channel_id=1, source_target_pairs={{0,4},{4,0},{8,12},{12,8},{1,5},{5,1},{9,13},{13,9},{2,6},{6,2},{1... | collective-permute-start | bytes 393224 | tf_op jit(solution)/shard_map/ppermute | solution.py:342
  28.8 8.2 %collective-permute-start.3 = (bf16[64,1792]{1,0:T(8,128)(2,1)S(1)}, bf16[64,1792]{1,0:T(8,128)(2,1)S(1)}, u32[]{:S(2)}, u32[]{:S(2)}) collective-permute-start(bf16[64,1792]{1,0:T(8,128)(2,1)S(1)} %get-tuple-element.26), channel_id=1, source_target_pairs={{0,1},{1,0},{2,3},{3,2},{4,5},{5,4},{6,7},{7,6},{8,9},{9,8},{10,11... | collective-permute-start | bytes 688136 | tf_op jit(solution)/shard_map/ppermute | solution.py:349
  30.7 3.7 %collective-permute-start.7 = (f32[1,1792]{1,0:T(1,128)S(1)}, f32[1,1792]{1,0:T(1,128)S(1)}, u32[]{:S(2)}, u32[]{:S(2)}) collective-permute-start(f32[1,1792]{1,0:T(1,128)S(1)} %reshape.7.refs_8_), channel_id=1, source_target_pairs={{0,8},{4,12},{8,0},{12,4},{1,9},{5,13},{9,1},{13,5},{2,10},{6,14},... | collective-permute-start | bytes 21512 | tf_op jit(solution)/shard_map/ppermute | solution.py:346
  32.3 24.2 %collective-permute-start.6 = (f32[1,1792]{1,0:T(1,128)S(1)}, f32[1,1792]{1,0:T(1,128)S(1)}, u32[]{:S(2)}, u32[]{:S(2)}) collective-permute-start(f32[1,1792]{1,0:T(1,128)S(1)} %reshape.7.refs_8_), channel_id=1, source_target_pairs={{0,4},{4,0},{8,12},{12,8},{1,5},{5,1},{9,13},{13,9},{2,6},{6,2},{1... | collective-permute-start | bytes 21512 | tf_op jit(solution)/shard_map/ppermute | solution.py:342
  34.4 22.1 %collective-permute-start.8 = (f32[1,1792]{1,0:T(1,128)S(1)}, f32[1,1792]{1,0:T(1,128)S(1)}, u32[]{:S(2)}, u32[]{:S(2)}) collective-permute-start(f32[1,1792]{1,0:T(1,128)S(1)} %collective-permute-done.7.refs_10_), channel_id=1, source_target_pairs={{0,4},{4,0},{8,12},{12,8},{1,5},{5,1},{9,13},{13,9},{2,6},{6,2},{1... | collective-permute-start | bytes 21512 | tf_op jit(solution)/shard_map/ppermute | solution.py:342
  37.0 19.5 %collective-permute-start.4 = (bf16[64,1792]{1,0:T(8,128)(2,1)S(1)}, bf16[64,1792]{1,0:T(8,128)(2,1)S(1)}, u32[]{:S(2)}, u32[]{:S(2)}) collective-permute-start(bf16[64,1792]{1,0:T(8,128)(2,1)S(1)} %add.60.refs_1_), channel_id=1, source_target_pairs={{0,2},{1,3},{2,0},{3,1},{4,6},{5,7},{6,4},{7,5},{8,10},{9,11},{10,... | collective-permute-start | bytes 688136 | tf_op jit(solution)/shard_map/ppermute | solution.py:349
  39.9 16.6 %collective-permute-start.5 = (bf16[64,1792]{1,0:T(8,128)(2,1)S(1)}, bf16[64,1792]{1,0:T(8,128)(2,1)S(1)}, u32[]{:S(2)}, u32[]{:S(2)}) collective-permute-start(bf16[64,1792]{1,0:T(8,128)(2,1)S(1)} %add.61.refs_1_), channel_id=1, source_target_pairs={{0,1},{1,0},{2,3},{3,2},{4,5},{5,4},{6,7},{7,6},{8,9},{9,8},{10,11... | collective-permute-start | bytes 688136 | tf_op jit(solution)/shard_map/ppermute | solution.py:349
  44.7 11.8 %copy-start.2 = (bf16[1,7168,512]{2,1,0:T(8,128)(2,1)}, bf16[1,7168,512]{2,1,0:T(8,128)(2,1)S(1)}, u32[]{:S(2)}) copy-start(bf16[1,7168,512]{2,1,0:T(8,128)(2,1)S(1)} %fetch.5.refs_12_) | copy-start | bytes 22020100
  50.6 5.9 %copy-start.5 = (bf16[1,7168,512]{2,1,0:T(8,128)(2,1)}, bf16[1,7168,512]{2,1,0:T(8,128)(2,1)S(1)}, u32[]{:S(2)}) copy-start(bf16[1,7168,512]{2,1,0:T(8,128)(2,1)S(1)} %fetch.6.refs_13_) | copy-start | bytes 22020100
  56.4 29.8 %copy-start.19 = (f32[256,2]{0,1:T(2,128)S(1)}, f32[256,2]{0,1:T(2,128)}, u32[]{:S(2)}) copy-start(f32[256,2]{0,1:T(2,128)} %param.24) | copy-start | bytes 6148
  56.5 29.8 %copy-start.20 = (s32[256,2]{0,1:T(2,128)S(1)}, s32[256,2]{0,1:T(2,128)}, u32[]{:S(2)}) copy-start(s32[256,2]{0,1:T(2,128)} %param.23) | copy-start | bytes 6148
  59.4 12.4 %collective-permute-start.9 = (bf16[64,1792]{1,0:T(8,128)(2,1)S(1)}, bf16[64,1792]{1,0:T(8,128)(2,1)S(1)}, u32[]{:S(2)}, u32[]{:S(2)}) collective-permute-start(bf16[64,1792]{1,0:T(8,128)(2,1)S(1)} %get-tuple-element.29.refs_14_.refs_4_), channel_id=1, source_target_pairs={{0,2},{1,3},{2,0},{3,1},{4,6},{5,7},{6,4},{7,5},{8,10},{9,11},{10,... | collective-permute-start | bytes 688136 | tf_op jit(solution)/shard_map/ppermute | solution.py:349
  59.7 13.5 %collective-permute-start.20 = (bf16[64,1792]{1,0:T(8,128)(2,1)S(1)}, bf16[64,1792]{1,0:T(8,128)(2,1)S(1)}, u32[]{:S(2)}, u32[]{:S(2)}) collective-permute-start(bf16[64,1792]{1,0:T(8,128)(2,1)S(1)} %get-tuple-element.29.refs_14_.refs_4_), channel_id=1, source_target_pairs={{0,1},{1,0},{2,3},{3,2},{4,5},{5,4},{6,7},{7,6},{8,9},{9,8},{10,11... | collective-permute-start | bytes 688136 | tf_op jit(solution)/shard_map/ppermute | solution.py:349
  60.0 13.8 %collective-permute-start.15 = (bf16[64,1792]{1,0:T(8,128)(2,1)S(1)}, bf16[64,1792]{1,0:T(8,128)(2,1)S(1)}, u32[]{:S(2)}, u32[]{:S(2)}) collective-permute-start(bf16[64,1792]{1,0:T(8,128)(2,1)S(1)} %get-tuple-element.29.refs_14_.refs_4_), channel_id=1, source_target_pairs={{0,8},{4,12},{8,0},{12,4},{1,9},{5,13},{9,1},{13,5},{2,10},{6,14},... | collective-permute-start | bytes 688136 | tf_op jit(solution)/shard_map/ppermute | solution.py:346
  61.7 12.1 %collective-permute-start.14 = (bf16[64,1792]{1,0:T(8,128)(2,1)S(1)}, bf16[64,1792]{1,0:T(8,128)(2,1)S(1)}, u32[]{:S(2)}, u32[]{:S(2)}) collective-permute-start(bf16[64,1792]{1,0:T(8,128)(2,1)S(1)} %get-tuple-element.29.refs_14_.refs_4_), channel_id=1, source_target_pairs={{0,4},{4,0},{8,12},{12,8},{1,5},{5,1},{9,13},{13,9},{2,6},{6,2},{1... | collective-permute-start | bytes 688136 | tf_op jit(solution)/shard_map/ppermute | solution.py:342
  71.8 8.5 %collective-permute-start.18 = (bf16[64,1792]{1,0:T(8,128)(2,1)S(1)}, bf16[64,1792]{1,0:T(8,128)(2,1)S(1)}, u32[]{:S(2)}, u32[]{:S(2)}) collective-permute-start(bf16[64,1792]{1,0:T(8,128)(2,1)S(1)} %collective-permute-done.9.refs_0_), channel_id=1, source_target_pairs={{0,8},{4,12},{8,0},{12,4},{1,9},{5,13},{9,1},{13,5},{2,10},{6,14},... | collective-permute-start | bytes 688136 | tf_op jit(solution)/shard_map/ppermute | solution.py:346
  73.3 10.9 %collective-permute-start.22 = (bf16[64,1792]{1,0:T(8,128)(2,1)S(1)}, bf16[64,1792]{1,0:T(8,128)(2,1)S(1)}, u32[]{:S(2)}, u32[]{:S(2)}) collective-permute-start(bf16[64,1792]{1,0:T(8,128)(2,1)S(1)} %collective-permute-done.20.refs_4_), channel_id=1, source_target_pairs={{0,8},{4,12},{8,0},{12,4},{1,9},{5,13},{9,1},{13,5},{2,10},{6,14},... | collective-permute-start | bytes 688136 | tf_op jit(solution)/shard_map/ppermute | solution.py:346
  73.8 10.4 %collective-permute-start.16 = (bf16[64,1792]{1,0:T(8,128)(2,1)S(1)}, bf16[64,1792]{1,0:T(8,128)(2,1)S(1)}, u32[]{:S(2)}, u32[]{:S(2)}) collective-permute-start(bf16[64,1792]{1,0:T(8,128)(2,1)S(1)} %collective-permute-done.15.refs_16_.refs_6_), channel_id=1, source_target_pairs={{0,4},{4,0},{8,12},{12,8},{1,5},{5,1},{9,13},{13,9},{2,6},{6,2},{1... | collective-permute-start | bytes 688136 | tf_op jit(solution)/shard_map/ppermute | solution.py:342
  73.8 10.9 %collective-permute-start.10 = (bf16[64,1792]{1,0:T(8,128)(2,1)S(1)}, bf16[64,1792]{1,0:T(8,128)(2,1)S(1)}, u32[]{:S(2)}, u32[]{:S(2)}) collective-permute-start(bf16[64,1792]{1,0:T(8,128)(2,1)S(1)} %collective-permute-done.9.refs_0_), channel_id=1, source_target_pairs={{0,1},{1,0},{2,3},{3,2},{4,5},{5,4},{6,7},{7,6},{8,9},{9,8},{10,11... | collective-permute-start | bytes 688136 | tf_op jit(solution)/shard_map/ppermute | solution.py:349
  73.8 12.6 %collective-permute-start.17 = (bf16[64,1792]{1,0:T(8,128)(2,1)S(1)}, bf16[64,1792]{1,0:T(8,128)(2,1)S(1)}, u32[]{:S(2)}, u32[]{:S(2)}) collective-permute-start(bf16[64,1792]{1,0:T(8,128)(2,1)S(1)} %collective-permute-done.9.refs_0_), channel_id=1, source_target_pairs={{0,4},{4,0},{8,12},{12,8},{1,5},{5,1},{9,13},{13,9},{2,6},{6,2},{1... | collective-permute-start | bytes 688136 | tf_op jit(solution)/shard_map/ppermute | solution.py:342
  80.2 6.2 %collective-permute-start.21 = (bf16[64,1792]{1,0:T(8,128)(2,1)S(1)}, bf16[64,1792]{1,0:T(8,128)(2,1)S(1)}, u32[]{:S(2)}, u32[]{:S(2)}) collective-permute-start(bf16[64,1792]{1,0:T(8,128)(2,1)S(1)} %collective-permute-done.20.refs_4_), channel_id=1, source_target_pairs={{0,4},{4,0},{8,12},{12,8},{1,5},{5,1},{9,13},{13,9},{2,6},{6,2},{1... | collective-permute-start | bytes 688136 | tf_op jit(solution)/shard_map/ppermute | solution.py:342
  84.2 2.3 %collective-permute-start.19 = (bf16[64,1792]{1,0:T(8,128)(2,1)S(1)}, bf16[64,1792]{1,0:T(8,128)(2,1)S(1)}, u32[]{:S(2)}, u32[]{:S(2)}) collective-permute-start(bf16[64,1792]{1,0:T(8,128)(2,1)S(1)} %collective-permute-done.18.refs_2_), channel_id=1, source_target_pairs={{0,4},{4,0},{8,12},{12,8},{1,5},{5,1},{9,13},{13,9},{2,6},{6,2},{1... | collective-permute-start | bytes 688136 | tf_op jit(solution)/shard_map/ppermute | solution.py:342
  84.2 2.3 %collective-permute-start.23 = (bf16[64,1792]{1,0:T(8,128)(2,1)S(1)}, bf16[64,1792]{1,0:T(8,128)(2,1)S(1)}, u32[]{:S(2)}, u32[]{:S(2)}) collective-permute-start(bf16[64,1792]{1,0:T(8,128)(2,1)S(1)} %collective-permute-done.22.refs_6_), channel_id=1, source_target_pairs={{0,4},{4,0},{8,12},{12,8},{1,5},{5,1},{9,13},{13,9},{2,6},{6,2},{1... | collective-permute-start | bytes 688136 | tf_op jit(solution)/shard_map/ppermute | solution.py:342
  84.7 10.6 %collective-permute-start.12 = (bf16[64,1792]{1,0:T(8,128)(2,1)S(1)}, bf16[64,1792]{1,0:T(8,128)(2,1)S(1)}, u32[]{:S(2)}, u32[]{:S(2)}) collective-permute-start(bf16[64,1792]{1,0:T(8,128)(2,1)S(1)} %collective-permute-done.10.refs_0_), channel_id=1, source_target_pairs={{0,8},{4,12},{8,0},{12,4},{1,9},{5,13},{9,1},{13,5},{2,10},{6,14},... | collective-permute-start | bytes 688136 | tf_op jit(solution)/shard_map/ppermute | solution.py:346
  86.5 3.1 %copy-start.3 = (bf16[1,7168,512]{2,1,0:T(8,128)(2,1)S(1)}, bf16[1,7168,512]{2,1,0:T(8,128)(2,1)}, u32[]{:S(2)}) copy-start(bf16[1,7168,512]{2,1,0:T(8,128)(2,1)} %copy-done.2) | copy-start | bytes 22020100
  89.6 3.1 %copy-start.6 = (bf16[1,7168,512]{2,1,0:T(8,128)(2,1)S(1)}, bf16[1,7168,512]{2,1,0:T(8,128)(2,1)}, u32[]{:S(2)}) copy-start(bf16[1,7168,512]{2,1,0:T(8,128)(2,1)} %copy-done.5) | copy-start | bytes 22020100
  92.7 3.1 %copy-start.9 = (bf16[1,512,7168]{2,1,0:T(8,128)(2,1)S(1)}, bf16[1,512,7168]{2,1,0:T(8,128)(2,1)}, u32[]{:S(2)}) copy-start(bf16[1,512,7168]{2,1,0:T(8,128)(2,1)} %copy-done.8) | copy-start | bytes 22020100
  98.2 1.8 %collective-permute-start.24 = (bf16[128,1792]{1,0:T(8,128)(2,1)S(1)}, bf16[128,1792]{1,0:T(8,128)(2,1)S(1)}, u32[]{:S(2)}, u32[]{:S(2)}) collective-permute-start(bf16[128,1792]{1,0:T(8,128)(2,1)S(1)} %get-tuple-element.31), channel_id=1, source_target_pairs={{0,4},{4,0},{8,12},{12,8},{1,5},{5,1},{9,13},{13,9},{2,6},{6,2},{1... | collective-permute-start | bytes 1376264 | tf_op jit(solution)/shard_map/ppermute | solution.py:342
  98.2 4.3 %collective-permute-start.11 = (bf16[64,1792]{1,0:T(8,128)(2,1)S(1)}, bf16[64,1792]{1,0:T(8,128)(2,1)S(1)}, u32[]{:S(2)}, u32[]{:S(2)}) collective-permute-start(bf16[64,1792]{1,0:T(8,128)(2,1)S(1)} %collective-permute-done.10.refs_0_), channel_id=1, source_target_pairs={{0,4},{4,0},{8,12},{12,8},{1,5},{5,1},{9,13},{13,9},{2,6},{6,2},{1... | collective-permute-start | bytes 688136 | tf_op jit(solution)/shard_map/ppermute | solution.py:342
  98.7 3.8 %collective-permute-start.13 = (bf16[64,1792]{1,0:T(8,128)(2,1)S(1)}, bf16[64,1792]{1,0:T(8,128)(2,1)S(1)}, u32[]{:S(2)}, u32[]{:S(2)}) collective-permute-start(bf16[64,1792]{1,0:T(8,128)(2,1)S(1)} %collective-permute-done.12.refs_0_.refs_2_), channel_id=1, source_target_pairs={{0,4},{4,0},{8,12},{12,8},{1,5},{5,1},{9,13},{13,9},{2,6},{6,2},{1... | collective-permute-start | bytes 688136 | tf_op jit(solution)/shard_map/ppermute | solution.py:342
  101.5 11.6 %collective-permute-start.25 = (bf16[64,1792]{1,0:T(8,128)(2,1)}, bf16[64,1792]{1,0:T(8,128)(2,1)S(1)}, u32[]{:S(2)}, u32[]{:S(2)}) collective-permute-start(bf16[64,1792]{1,0:T(8,128)(2,1)} %get-tuple-element.32.refs_14_), channel_id=1, source_target_pairs={{0,8},{4,12},{8,0},{12,4},{1,9},{5,13},{9,1},{13,5},{2,10},{6,14},... | collective-permute-start | bytes 688136 | tf_op jit(solution)/shard_map/ppermute | solution.py:346
  102.5 13.3 %collective-permute-start.27 = (bf16[128,1792]{1,0:T(8,128)(2,1)}, bf16[128,1792]{1,0:T(8,128)(2,1)S(1)}, u32[]{:S(2)}, u32[]{:S(2)}) collective-permute-start(bf16[128,1792]{1,0:T(8,128)(2,1)} %get-tuple-element.36), channel_id=1, source_target_pairs={{0,4},{4,0},{8,12},{12,8},{1,5},{5,1},{9,13},{13,9},{2,6},{6,2},{1... | collective-permute-start | bytes 1376264 | tf_op jit(solution)/shard_map/ppermute | solution.py:342
  103.3 3.1 %copy-start.4 = (bf16[1,7168,512]{2,1,0:T(8,128)(2,1)S(1)}, bf16[1,7168,512]{2,1,0:T(8,128)(2,1)}, u32[]{:S(2)}) copy-start(bf16[1,7168,512]{2,1,0:T(8,128)(2,1)} %copy-done.2) | copy-start | bytes 22020100
  110.4 3.1 %copy-start.10 = (bf16[1,512,7168]{2,1,0:T(8,128)(2,1)S(1)}, bf16[1,512,7168]{2,1,0:T(8,128)(2,1)}, u32[]{:S(2)}) copy-start(bf16[1,512,7168]{2,1,0:T(8,128)(2,1)} %copy-done.8) | copy-start | bytes 22020100
  110.4 29.1 %copy-start.1 = (bf16[256,1792]{1,0:T(8,128)(2,1)S(1)}, bf16[256,1792]{1,0:T(8,128)(2,1)}, u32[]{:S(2)}) copy-start(bf16[256,1792]{1,0:T(8,128)(2,1)} %param.21) | copy-start | bytes 2752516
  113.1 5.4 %copy-start.16 = (bf16[64,1792]{1,0:T(8,128)(2,1)S(1)}, bf16[64,1792]{1,0:T(8,128)(2,1)}, u32[]{:S(2)}) copy-start(bf16[64,1792]{1,0:T(8,128)(2,1)} %copy-done.15) | copy-start | bytes 688132
  115.2 2.0 %collective-permute-start.32 = (bf16[128,1792]{1,0:T(8,128)(2,1)S(1)}, bf16[128,1792]{1,0:T(8,128)(2,1)S(1)}, u32[]{:S(2)}, u32[]{:S(2)}) collective-permute-start(bf16[128,1792]{1,0:T(8,128)(2,1)S(1)} %get-tuple-element.43), channel_id=1, source_target_pairs={{0,4},{4,0},{8,12},{12,8},{1,5},{5,1},{9,13},{13,9},{2,6},{6,2},{1... | collective-permute-start | bytes 1376264 | tf_op jit(solution)/shard_map/ppermute | solution.py:342
  115.8 8.8 %collective-permute-start.26 = (bf16[128,1792]{1,0:T(8,128)(2,1)S(1)}, bf16[128,1792]{1,0:T(8,128)(2,1)S(1)}, u32[]{:S(2)}, u32[]{:S(2)}) collective-permute-start(bf16[128,1792]{1,0:T(8,128)(2,1)S(1)} %get-tuple-element.34), channel_id=1, source_target_pairs={{0,4},{4,0},{8,12},{12,8},{1,5},{5,1},{9,13},{13,9},{2,6},{6,2},{1... | collective-permute-start | bytes 1376264 | tf_op jit(solution)/shard_map/ppermute | solution.py:342
  116.0 8.5 %collective-permute-start.28 = (bf16[64,1792]{1,0:T(8,128)(2,1)S(1)}, bf16[64,1792]{1,0:T(8,128)(2,1)S(1)}, u32[]{:S(2)}, u32[]{:S(2)}) collective-permute-start(bf16[64,1792]{1,0:T(8,128)(2,1)S(1)} %get-tuple-element.37), channel_id=1, source_target_pairs={{0,8},{4,12},{8,0},{12,4},{1,9},{5,13},{9,1},{13,5},{2,10},{6,14},... | collective-permute-start | bytes 688136 | tf_op jit(solution)/shard_map/ppermute | solution.py:346
  117.3 12.0 %collective-permute-start.33 = (bf16[64,1792]{1,0:T(8,128)(2,1)S(1)}, bf16[64,1792]{1,0:T(8,128)(2,1)S(1)}, u32[]{:S(2)}, u32[]{:S(2)}) collective-permute-start(bf16[64,1792]{1,0:T(8,128)(2,1)S(1)} %get-tuple-element.45), channel_id=1, source_target_pairs={{0,8},{4,12},{8,0},{12,4},{1,9},{5,13},{9,1},{13,5},{2,10},{6,14},... | collective-permute-start | bytes 688136 | tf_op jit(solution)/shard_map/ppermute | solution.py:346
  118.5 11.0 %collective-permute-start.30 = (bf16[64,1792]{1,0:T(8,128)(2,1)S(1)}, bf16[64,1792]{1,0:T(8,128)(2,1)S(1)}, u32[]{:S(2)}, u32[]{:S(2)}) collective-permute-start(bf16[64,1792]{1,0:T(8,128)(2,1)S(1)} %add.66), channel_id=1, source_target_pairs={{0,2},{1,3},{2,0},{3,1},{4,6},{5,7},{6,4},{7,5},{8,10},{9,11},{10,... | collective-permute-start | bytes 688136 | tf_op jit(solution)/shard_map/ppermute | solution.py:349
  124.5 14.1 %collective-permute-start.31 = (bf16[64,1792]{1,0:T(8,128)(2,1)S(1)}, bf16[64,1792]{1,0:T(8,128)(2,1)S(1)}, u32[]{:S(2)}, u32[]{:S(2)}) collective-permute-start(bf16[64,1792]{1,0:T(8,128)(2,1)S(1)} %add.67), channel_id=1, source_target_pairs={{0,1},{1,0},{2,3},{3,2},{4,5},{5,4},{6,7},{7,6},{8,9},{9,8},{10,11... | collective-permute-start | bytes 688136 | tf_op jit(solution)/shard_map/ppermute | solution.py:349
  124.7 13.9 %collective-permute-start.29 = (bf16[64,1792]{1,0:T(8,128)(2,1)S(1)}, bf16[64,1792]{1,0:T(8,128)(2,1)S(1)}, u32[]{:S(2)}, u32[]{:S(2)}) collective-permute-start(bf16[64,1792]{1,0:T(8,128)(2,1)S(1)} %get-tuple-element.39), channel_id=1, source_target_pairs={{0,8},{4,12},{8,0},{12,4},{1,9},{5,13},{9,1},{13,5},{2,10},{6,14},... | collective-permute-start | bytes 688136 | tf_op jit(solution)/shard_map/ppermute | solution.py:346
  129.4 9.2 %collective-permute-start.34 = (bf16[64,1792]{1,0:T(8,128)(2,1)S(1)}, bf16[64,1792]{1,0:T(8,128)(2,1)S(1)}, u32[]{:S(2)}, u32[]{:S(2)}) collective-permute-start(bf16[64,1792]{1,0:T(8,128)(2,1)S(1)} %add.69), channel_id=1, source_target_pairs={{0,3},{1,2},{2,1},{3,0},{4,7},{5,6},{6,5},{7,4},{8,11},{9,10},{10,... | collective-permute-start | bytes 688136 | tf_op jit(solution)/shard_map/ppermute | solution.py:349
  (8 other events, 12.9 us)

commit v6 on v5

--- a/solution.py
+++ b/solution.py
@@ -47,7 +47,8 @@
     )(in_hbm(value), *after)
 
 
-def attention_kernel(step_rows, lengths, q_ref, qr_ref, k_ref, kr_ref, up_ref, out_ref, latent, rope):
+def attention_kernel(step_rows, lengths, q_ref, qr_ref, k_ref, kr_ref, up_ref, *refs):
+    out_ref, latent, rope = refs[-3:]
     step = pl.program_id(0)
     heads, positions = q_ref.shape[1], k_ref.shape[1]
     rope_width = kr_ref.shape[1]
@@ -104,7 +105,7 @@
             ).astype(jnp.bfloat16)
 
 
-def attend(query_latent, query_rope, cache_latent, cache_rope, cache_length, value_up):
+def attend(query_latent, query_rope, cache_latent, cache_rope, cache_length, value_up, after):
     rows, heads, latent_width = query_latent.shape
     positions = cache_latent.shape[1]
     rope_width = cache_rope.shape[1]
@@ -123,7 +124,8 @@
                 pl.BlockSpec((step_rows, positions, latent_width), by_row),
                 pl.BlockSpec((step_rows, rope_width, positions), by_row),
                 pl.BlockSpec(value_up.shape, lambda i, lengths: (0, 0, 0)),
-            ],
+            ]
+            + [pl.BlockSpec(memory_space=pl.ANY)] * len(after),
             out_specs=pl.BlockSpec((rows, heads * value_width), lambda i, lengths: (0, 0)),
             scratch_shapes=[
                 pltpu.VMEM((latent_width // 128, rows * heads, 128), jnp.float32),
@@ -142,6 +144,7 @@
         in_hbm(cache_latent),
         in_hbm(cache_rope),
         in_hbm(value_up),
+        *after,
     )
 
 
@@ -242,7 +245,8 @@
     )(places, *[b for row in blocks for b in row], *gains, in_vmem(gate_weight), in_vmem(up_weight), *after)
 
 
-def down_kernel(row_blocks, column_blocks, cores, places, active, row_weight, down, *refs):
+def down_kernel(slots, column_blocks, cores, places, active, row_weight, down, *refs):
+    row_blocks = len(slots)
     outs = refs[-row_blocks * cores :]
     width = down.shape[2] // column_blocks
     height = active.shape[0] // row_blocks
@@ -250,7 +254,7 @@
     tile = 256 if width % 256 == 0 else 128
     weights = []
     for s in range(row_blocks):
-        first = pl.multiple_of(places[column_blocks + s] * height, height)
+        first = pl.multiple_of(places[column_blocks + slots[s]] * height, height)
         weights.append(row_weight[pl.ds(first, height), :])
     for k in order:
         b, c = k // cores, k % cores
@@ -265,13 +269,14 @@
                 outs[s * cores + c][b * height : (b + 1) * height, cut] = part.astype(jnp.bfloat16)
 
 
-def project_down(places, active, row_weight, down_weight, row_blocks, column_blocks, cores, after):
+def project_down(places, active, row_weight, down_weight, slots, column_blocks, cores, after):
+    row_blocks = len(slots)
     rows, hidden = active.shape
     width = down_weight.shape[2] // column_blocks
     whole = pl.BlockSpec(memory_space=pltpu.VMEM)
     out = jax.ShapeDtypeStruct((rows // row_blocks * (column_blocks // cores), width), jnp.bfloat16)
     outs = pl.pallas_call(
-        functools.partial(down_kernel, row_blocks, column_blocks, cores),
+        functools.partial(down_kernel, slots, column_blocks, cores),
         out_shape=[out] * (row_blocks * cores),
         in_specs=[pl.BlockSpec(memory_space=pltpu.SMEM)]
         + [whole] * 3
@@ -362,25 +367,24 @@
     tp_places = [tp_index ^ k for k in range(tp_count)]
     places = jnp.stack(ep_places + tp_places).astype(jnp.int32)
 
-    gains = gather_ep(norm_gain.reshape(1, -1))
+    gain = norm_gain.reshape(1, -1)
+    gains = gather_ep(gain)
+    own_residual = lax.dynamic_slice_in_dim(residual, tp_index * block_rows, block_rows, 0)
     row_weight = jnp.sum(jnp.where(routed_experts == ep_index, expert_gates, 0.0), axis=-1, keepdims=True)
 
-    head_out = attend(query_latent, query_rope, cache_latent, cache_rope, cache_length, value_up)
-    output_weight = fetch(output_weight, [head_out])
+    head_out = attend(query_latent, query_rope, cache_latent, cache_rope, cache_length, value_up, [places])
+    output_weight = fetch(output_weight, [head_out, row_weight, own_residual, gain])
     partial = project(places, gather_ep(head_out), output_weight, tp_count)
 
-    own_residual = lax.dynamic_slice_in_dim(residual, tp_index * block_rows, block_rows, 0)
     gate_weight = fetch(gate_weight, [partial[0]])
     terms = [[(value, 0)] for value in partial]
-    first = []
     for k in reversed(range(1, tp_count)):
         total = terms[k][0][0]
-        if len(terms[k]) > 1 or (k == 1 and first):
-            (total,) = add([terms[k]], block_rows, first)
+        if len(terms[k]) > 1 or k == 1:
+            (total,) = add([terms[k]], block_rows, [gate_weight] if k == 1 else [])
         low = k & -k
         arrived = from_tp(total, low)
         terms[k ^ low].append((arrived, 0))
-        first = [total] if first else [arrived]
     up_weight = fetch(up_weight, [total])
     down_weight = fetch(down_weight, [total])
     stream_terms = terms[0] + [(own_residual, 0)]
@@ -398,11 +402,8 @@
     arrivals = []
     hold_gate, hold_down = blocks[0], [blocks[tp_count - 1][-2]]
     for group in groups:
-        chosen = jnp.stack(ep_places + [tp_places[k] for k in group]).astype(jnp.int32)
-        active = activate(chosen, [blocks[k] for k in group], gains, gate_weight, up_weight, hold_gate)
-        outs = project_down(
-            chosen, active, row_weight, down_weight, len(group), ep_count, cores, hold_down
-        )
+        active = activate(places, [blocks[k] for k in group], gains, gate_weight, up_weight, hold_gate)
+        outs = project_down(places, active, row_weight, down_weight, group, ep_count, cores, hold_down)
         swapped = [from_core(out[1]) for out in outs]
         for at, k in enumerate(group):
             pair = [[(outs[at][0], c * block_rows), (swapped[at], c * block_rows)] for c in range(chips)]

time: 140 us -> 121 us (0.86)
  local copies, waits for them, and re-layouts: 22.2 us -> 1.01 us
  Pallas kernels: 44.6 us -> 37.9 us
  starting transfers between devices: 23.4 us -> 28.7 us
  waiting for transfers between devices: 48.2 us -> 51.7 us
    unnamed x42 -> x12, local copies, waits for them, and re-layouts: 21.7 us -> 0.77 us
    ppermute x10, waiting for transfers between devices: 25 us -> 30.3 us  [from_chip(): lax.ppermute(value, 'ep', [(i, (i + step) % ep_count) for i in range(ep_c...]
    pallas_call x4, Pallas kernels: 16.9 us -> 11.6 us  [fetch(): pl.pallas_call(functools.partial(fetch_kernel, parts), out_shape=pltpu.VM...]
    ppermute x9, starting transfers between devices: 7.18 us -> 11.2 us  [from_tp(): return lax.ppermute(value, 'tp', [(i, i ^ bits) for i in range(tp_count)])]
    ppermute x9, waiting for transfers between devices: 21.8 us -> 20.2 us  [from_tp(): return lax.ppermute(value, 'tp', [(i, i ^ bits) for i in range(tp_count)])]
  transfers between devices with their start and end apart: 35 -> 35, of which waited for: 11 -> 14; matrix products, arithmetic and copies ran while one was open for 0% -> 0% of each run, Pallas kernels for 18% -> 16%
where the time goes in v6:
time: 121 us; the launch traced here: 120 us
  waiting for transfers between devices  51.7 us (43%)
  Pallas kernels  37.9 us (31%)
  starting transfers between devices  28.7 us (24%)
    ppermute x10, waiting for transfers between devices, from_chip(): lax.ppermute(value, 'ep', [(i, (i + step) % ep_count) for i in range(ep_c...  30.3 us
    ppermute x9, waiting for transfers between devices, from_tp(): return lax.ppermute(value, 'tp', [(i, i ^ bits) for i in range(tp_count)])  20.2 us
    ppermute x10, starting transfers between devices, from_chip(): lax.ppermute(value, 'ep', [(i, (i + step) % ep_count) for i in range(ep_c...  15.3 us
    pallas_call x1, Pallas kernels, attend(): pl.pallas_call(functools.partial(attention_kernel, step_rows), out_shape=...  13.2 us
    pallas_call x4, Pallas kernels, fetch(): pl.pallas_call(functools.partial(fetch_kernel, parts), out_shape=pltpu.VM...  11.6 us
    ppermute x9, starting transfers between devices, from_tp(): return lax.ppermute(value, 'tp', [(i, i ^ bits) for i in range(tp_count)])  11.2 us
    pallas_call x2, Pallas kernels, activate(): pl.pallas_call(functools.partial(gate_kernel, row_blocks, column_blocks,...  5.48 us
    pallas_call x2, Pallas kernels, project_down(): pl.pallas_call(functools.partial(down_kernel, slots, column_blocks, cores...  3.55 us
  transfers between devices with their start and end apart: 35, of which 14 were waited for; matrix products, arithmetic and copies ran while one was open for 0% of the time, Pallas kernels for 16%

profile of v6, /device:TPU:0, one launch (start us, length us, event | category | flops | bytes accessed | tf_op | source)
XLA Modules:
  0.0 120.4 jit_solution(1609325240757226121)
XLA Ops:
  0.8 0.7 copy-done.2
  1.5 13.2 %attention.1.refs_1_.refs_0_ = bf16[64,1024]{1,0:T(8,128)(2,1)S(1)} custom-call(s32[64]{0:T(128)S(1)} %copy-done.2, bf16[64,8,512]{2,1,0:T(8,128)(2,1)} %q_ref.1, bf16[64,512]{1,0:T(8,128)(2,1)} %qr_ref.1, bf16[64,256,512]{2,1,0:T(8,128)(2,1)} %k_ref.1, bf16[64,64,256]{2,1,0:T(8,128)(2,1)} %kr_ref.1, bf16[8,512,128]{2,1,0:T(8,128)(2,1)} %up_ref.1, ...), custom_call_target="tpu_custom_call" | custom-call | flops 4294967296 | bytes 16777216 | tf_op jit(solution)/shard_map/attention/pallas_call | solution.py:115
  14.7 3.0 %collective-permute-start.1 = (bf16[64,1024]{1,0:T(8,128)(2,1)S(1)}, bf16[64,1024]{1,0:T(8,128)(2,1)S(1)}, u32[]{:S(2)}, u32[]{:S(2)}) collective-permute-start(bf16[64,1024]{1,0:T(8,128)(2,1)S(1)} %attention.1.refs_1_.refs_0_), channel_id=1, source_target_pairs={{0,8},{4,12},{8,0},{12,4},{1,9},{5,13},{9,1},{13,5},{2,10},{6,14},... | collective-permute-start | bytes 393224 | tf_op jit(solution)/shard_map/ppermute | solution.py:351
  17.8 0.1 copy.16.refs_2_.row_weight
  17.9 3.3 %collective-permute-done.1.refs_2_ = bf16[64,1024]{1,0:T(8,128)(2,1)S(1)} collective-permute-done((bf16[64,1024]{1,0:T(8,128)(2,1)S(1)}, bf16[64,1024]{1,0:T(8,128)(2,1)S(1)}, u32[]{:S(2)}, u32[]{:S(2)}) %collective-permute-start.1) | collective-permute-done | bytes 131104 | tf_op jit(solution)/shard_map/ppermute | solution.py:351
  21.3 2.0 %fetch.4.refs_4_ = bf16[1024,1792]{1,0:T(8,128)(2,1)S(1)} custom-call(bf16[1024,1792]{1,0:T(8,128)(2,1)} %refs_0_.4, bf16[64,1024]{1,0:T(8,128)(2,1)S(1)} %attention.1.refs_1_.refs_0_, f32[256,1]{1,0:T(8,128)S(1)} %copy.16.refs_2_.row_weight, bf16[64,1792]{1,0:T(8,128)(2,1)S(1)} %constant_dynamic-slice_fusion.refs_3_.refs_7_, ...), custom_call_target="tpu_custom_call" | custom-call | bytes 7340032 | tf_op jit(solution)/shard_map/fetch/pallas_call | solution.py:38
  23.3 1.8 %projection.1 = (bf16[64,1792]{1,0:T(8,128)(2,1)S(1)}, bf16[64,1792]{1,0:T(8,128)(2,1)S(1)}, bf16[64,1792]{1,0:T(8,128)(2,1)S(1)}, bf16[64,1792]{1,0:T(8,128)(2,1)S(1)}) custom-call(s32[8]{0:T(128)S(1)} %stack.35.refs_0_.places, bf16[64,1024]{1,0:T(8,128)(2,1)S(1)} %attention.1.refs_1_.refs_0_, bf16[64,1024]{1,0:T(8,128)(2,1)S(1)} %collective-permute-done.refs_1_, ...), custom_call_target="tpu_custom_call" | custom-call | flops 939524096 | bytes 4194304 | tf_op jit(solution)/shard_map/projection/pallas_call | solution.py:175
  25.1 1.9 %collective-permute-start.3 = (bf16[64,1792]{1,0:T(8,128)(2,1)S(1)}, bf16[64,1792]{1,0:T(8,128)(2,1)S(1)}, u32[]{:S(2)}, u32[]{:S(2)}) collective-permute-start(bf16[64,1792]{1,0:T(8,128)(2,1)S(1)} %get-tuple-element.26), channel_id=1, source_target_pairs={{0,1},{1,0},{2,3},{3,2},{4,5},{5,4},{6,7},{7,6},{8,9},{9,8},{10,11... | collective-permute-start | bytes 688136 | tf_op jit(solution)/shard_map/ppermute | solution.py:354
  27.0 3.2 %fetch.5.refs_1_.refs_12_ = bf16[1,7168,512]{2,1,0:T(8,128)(2,1)S(1)} custom-call(bf16[1,7168,512]{2,1,0:T(8,128)(2,1)} %refs_0_.5, bf16[64,1792]{1,0:T(8,128)(2,1)S(1)} %get-tuple-element.24.refs_1_.refs_0_.refs_4_), custom_call_target="tpu_custom_call" | custom-call | bytes 14680064 | tf_op jit(solution)/shard_map/fetch/pallas_call | solution.py:38
  30.2 0.3 collective-permute-start.5
  30.5 2.9 %collective-permute-done.3.refs_1_ = bf16[64,1792]{1,0:T(8,128)(2,1)S(1)} collective-permute-done((bf16[64,1792]{1,0:T(8,128)(2,1)S(1)}, bf16[64,1792]{1,0:T(8,128)(2,1)S(1)}, u32[]{:S(2)}, u32[]{:S(2)}) %collective-permute-start.3) | collective-permute-done | bytes 229408 | tf_op jit(solution)/shard_map/ppermute | solution.py:354
  33.4 3.0 %collective-permute-start.4 = (bf16[64,1792]{1,0:T(8,128)(2,1)S(1)}, bf16[64,1792]{1,0:T(8,128)(2,1)S(1)}, u32[]{:S(2)}, u32[]{:S(2)}) collective-permute-start(bf16[64,1792]{1,0:T(8,128)(2,1)S(1)} %add.60), channel_id=1, source_target_pairs={{0,2},{1,3},{2,0},{3,1},{4,6},{5,7},{6,4},{7,5},{8,10},{9,11},{10,... | collective-permute-start | bytes 688136 | tf_op jit(solution)/shard_map/ppermute | solution.py:354
  36.4 1.5 %collective-permute-start.7 = (f32[1,1792]{1,0:T(1,128)S(1)}, f32[1,1792]{1,0:T(1,128)S(1)}, u32[]{:S(2)}, u32[]{:S(2)}) collective-permute-start(f32[1,1792]{1,0:T(1,128)S(1)} %reshape.7.refs_4_.refs_8_), channel_id=1, source_target_pairs={{0,8},{4,12},{8,0},{12,4},{1,9},{5,13},{9,1},{13,5},{2,10},{6,14},... | collective-permute-start | bytes 21512 | tf_op jit(solution)/shard_map/ppermute | solution.py:351
  37.9 2.1 %collective-permute-done.7.refs_10_ = f32[1,1792]{1,0:T(1,128)S(1)} collective-permute-done((f32[1,1792]{1,0:T(1,128)S(1)}, f32[1,1792]{1,0:T(1,128)S(1)}, u32[]{:S(2)}, u32[]{:S(2)}) %collective-permute-start.7) | collective-permute-done | bytes 7200 | tf_op jit(solution)/shard_map/ppermute | solution.py:351
  40.1 3.2 %fetch.6.refs_13_ = bf16[1,7168,512]{2,1,0:T(8,128)(2,1)S(1)} custom-call(bf16[1,7168,512]{2,1,0:T(8,128)(2,1)} %refs_0_.6, bf16[64,1792]{1,0:T(8,128)(2,1)S(1)} %add.61.refs_1_), custom_call_target="tpu_custom_call" | custom-call | bytes 14680064 | tf_op jit(solution)/shard_map/fetch/pallas_call | solution.py:38
  43.2 3.2 %fetch.7.refs_14_.down = bf16[1,512,7168]{2,1,0:T(8,128)(2,1)S(1)} custom-call(bf16[1,512,7168]{2,1,0:T(8,128)(2,1)} %refs_0_.7, bf16[64,1792]{1,0:T(8,128)(2,1)S(1)} %add.61.refs_1_), custom_call_target="tpu_custom_call" | custom-call | bytes 14680064 | tf_op jit(solution)/shard_map/fetch/pallas_call | solution.py:38
  46.5 0.1 collective-permute-done.4.refs_1_.refs_5_
  46.6 0.8 add.62
  47.5 4.2 %collective-permute-start.20 = (bf16[64,1792]{1,0:T(8,128)(2,1)S(1)}, bf16[64,1792]{1,0:T(8,128)(2,1)S(1)}, u32[]{:S(2)}, u32[]{:S(2)}) collective-permute-start(bf16[64,1792]{1,0:T(8,128)(2,1)S(1)} %get-tuple-element.29.refs_14_.refs_4_), channel_id=1, source_target_pairs={{0,1},{1,0},{2,3},{3,2},{4,5},{5,4},{6,7},{7,6},{8,9},{9,8},{10,11... | collective-permute-start | bytes 688136 | tf_op jit(solution)/shard_map/ppermute | solution.py:354
  51.6 1.5 %collective-permute-start.15 = (bf16[64,1792]{1,0:T(8,128)(2,1)S(1)}, bf16[64,1792]{1,0:T(8,128)(2,1)S(1)}, u32[]{:S(2)}, u32[]{:S(2)}) collective-permute-start(bf16[64,1792]{1,0:T(8,128)(2,1)S(1)} %get-tuple-element.29.refs_14_.refs_4_), channel_id=1, source_target_pairs={{0,8},{4,12},{8,0},{12,4},{1,9},{5,13},{9,1},{13,5},{2,10},{6,14},... | collective-permute-start | bytes 688136 | tf_op jit(solution)/shard_map/ppermute | solution.py:351
  53.1 8.1 %collective-permute-done.9.refs_0_ = bf16[64,1792]{1,0:T(8,128)(2,1)S(1)} collective-permute-done((bf16[64,1792]{1,0:T(8,128)(2,1)S(1)}, bf16[64,1792]{1,0:T(8,128)(2,1)S(1)}, u32[]{:S(2)}, u32[]{:S(2)}) %collective-permute-start.9) | collective-permute-done | bytes 229408 | tf_op jit(solution)/shard_map/ppermute | solution.py:354
  61.2 1.5 %collective-permute-start.18 = (bf16[64,1792]{1,0:T(8,128)(2,1)S(1)}, bf16[64,1792]{1,0:T(8,128)(2,1)S(1)}, u32[]{:S(2)}, u32[]{:S(2)}) collective-permute-start(bf16[64,1792]{1,0:T(8,128)(2,1)S(1)} %collective-permute-done.9.refs_0_), channel_id=1, source_target_pairs={{0,8},{4,12},{8,0},{12,4},{1,9},{5,13},{9,1},{13,5},{2,10},{6,14},... | collective-permute-start | bytes 688136 | tf_op jit(solution)/shard_map/ppermute | solution.py:351
  62.7 0.5 collective-permute-start.22
  63.3 0.5 collective-permute-start.17
  63.8 6.0 %collective-permute-done.18.refs_2_ = bf16[64,1792]{1,0:T(8,128)(2,1)S(1)} collective-permute-done((bf16[64,1792]{1,0:T(8,128)(2,1)S(1)}, bf16[64,1792]{1,0:T(8,128)(2,1)S(1)}, u32[]{:S(2)}, u32[]{:S(2)}) %collective-permute-start.18) | collective-permute-done | bytes 229408 | tf_op jit(solution)/shard_map/ppermute | solution.py:351
  69.7 3.5 %collective-permute-done.22.refs_6_ = bf16[64,1792]{1,0:T(8,128)(2,1)S(1)} collective-permute-done((bf16[64,1792]{1,0:T(8,128)(2,1)S(1)}, bf16[64,1792]{1,0:T(8,128)(2,1)S(1)}, u32[]{:S(2)}, u32[]{:S(2)}) %collective-permute-start.22) | collective-permute-done | bytes 229408 | tf_op jit(solution)/shard_map/ppermute | solution.py:351
  73.2 0.5 collective-permute-start.23
  73.7 1.5 %collective-permute-start.12 = (bf16[64,1792]{1,0:T(8,128)(2,1)S(1)}, bf16[64,1792]{1,0:T(8,128)(2,1)S(1)}, u32[]{:S(2)}, u32[]{:S(2)}) collective-permute-start(bf16[64,1792]{1,0:T(8,128)(2,1)S(1)} %collective-permute-done.10.refs_0_), channel_id=1, source_target_pairs={{0,8},{4,12},{8,0},{12,4},{1,9},{5,13},{9,1},{13,5},{2,10},{6,14},... | collective-permute-start | bytes 688136 | tf_op jit(solution)/shard_map/ppermute | solution.py:351
  75.2 2.8 %activate.2.active = bf16[128,512]{1,0:T(8,128)(2,1)S(1)} custom-call(s32[8]{0:T(128)S(1)} %stack.35.refs_0_.places, bf16[64,1792]{1,0:T(8,128)(2,1)S(1)} %collective-permute-done.9.refs_0_, bf16[64,1792]{1,0:T(8,128)(2,1)S(1)} %collective-permute-done.17.refs_1_, bf16[64,1792]{1,0:T(8,128)(2,1)S(1)} %collective-permute-done.18.refs_2_, ...), custom_call_target="tpu_custom_call" | custom-call | flops 1879048192 | bytes 14680064 | tf_op jit(solution)/shard_map/activate/pallas_call | solution.py:228
  78.0 3.3 %collective-permute-done.12.refs_0_.refs_2_ = bf16[64,1792]{1,0:T(8,128)(2,1)S(1)} collective-permute-done((bf16[64,1792]{1,0:T(8,128)(2,1)S(1)}, bf16[64,1792]{1,0:T(8,128)(2,1)S(1)}, u32[]{:S(2)}, u32[]{:S(2)}) %collective-permute-start.12) | collective-permute-done | bytes 229408 | tf_op jit(solution)/shard_map/ppermute | solution.py:351
  81.3 1.8 %down.2 = (bf16[128,1792]{1,0:T(8,128)(2,1)S(1)}, bf16[128,1792]{1,0:T(8,128)(2,1)S(1)}, bf16[128,1792]{1,0:T(8,128)(2,1)S(1)}, bf16[128,1792]{1,0:T(8,128)(2,1)S(1)}) custom-call(s32[8]{0:T(128)S(1)} %stack.35.refs_0_.places, bf16[128,512]{1,0:T(8,128)(2,1)S(1)} %activate.2.active, f32[256,1]{1,0:T(8,128)S(1)} %copy.16.refs_2_.row_weight, ...), custom_call_target="tpu_custom_call" | custom-call | flops 939524096 | bytes 7340032 | tf_op jit(solution)/shard_map/down/pallas_call | solution.py:278
  83.2 0.5 collective-permute-start.11
  83.7 1.2 %collective-permute-done.24.refs_1_.refs_3_ = bf16[128,1792]{1,0:T(8,128)(2,1)S(1)} collective-permute-done((bf16[128,1792]{1,0:T(8,128)(2,1)S(1)}, bf16[128,1792]{1,0:T(8,128)(2,1)S(1)}, u32[]{:S(2)}, u32[]{:S(2)}) %collective-permute-start.24) | collective-permute-done | bytes 458784 | tf_op jit(solution)/shard_map/ppermute | solution.py:347
  85.1 1.5 %collective-permute-start.25 = (bf16[64,1792]{1,0:T(8,128)(2,1)S(1)}, bf16[64,1792]{1,0:T(8,128)(2,1)S(1)}, u32[]{:S(2)}, u32[]{:S(2)}) collective-permute-start(bf16[64,1792]{1,0:T(8,128)(2,1)S(1)} %get-tuple-element.32.refs_14_), channel_id=1, source_target_pairs={{0,8},{4,12},{8,0},{12,4},{1,9},{5,13},{9,1},{13,5},{2,10},{6,14},... | collective-permute-start | bytes 688136 | tf_op jit(solution)/shard_map/ppermute | solution.py:351
  86.6 2.7 %activate.3.active = bf16[128,512]{1,0:T(8,128)(2,1)S(1)} custom-call(s32[8]{0:T(128)S(1)} %stack.35.refs_0_.places, bf16[64,1792]{1,0:T(8,128)(2,1)S(1)} %collective-permute-done.10.refs_0_, bf16[64,1792]{1,0:T(8,128)(2,1)S(1)} %collective-permute-done.11.refs_1_, bf16[64,1792]{1,0:T(8,128)(2,1)S(1)} %collective-permute-done.12.refs_0_.refs_2_, ...), custom_call_target="tpu_custom_call" | custom-call | flops 1879048192 | bytes 14680064 | tf_op jit(solution)/shard_map/activate/pallas_call | solution.py:228
  89.3 3.4 %collective-permute-done.25.refs_0_.refs_4_.refs_1_ = bf16[64,1792]{1,0:T(8,128)(2,1)S(1)} collective-permute-done((bf16[64,1792]{1,0:T(8,128)(2,1)S(1)}, bf16[64,1792]{1,0:T(8,128)(2,1)S(1)}, u32[]{:S(2)}, u32[]{:S(2)}) %collective-permute-start.25) | collective-permute-done | bytes 229408 | tf_op jit(solution)/shard_map/ppermute | solution.py:351
  92.8 1.8 %down.3 = (bf16[128,1792]{1,0:T(8,128)(2,1)S(1)}, bf16[128,1792]{1,0:T(8,128)(2,1)S(1)}, bf16[128,1792]{1,0:T(8,128)(2,1)S(1)}, bf16[128,1792]{1,0:T(8,128)(2,1)S(1)}) custom-call(s32[8]{0:T(128)S(1)} %stack.35.refs_0_.places, bf16[128,512]{1,0:T(8,128)(2,1)S(1)} %activate.3.active, f32[256,1]{1,0:T(8,128)S(1)} %copy.16.refs_2_.row_weight, ...), custom_call_target="tpu_custom_call" | custom-call | flops 939524096 | bytes 7340032 | tf_op jit(solution)/shard_map/down/pallas_call | solution.py:278
  94.6 0.5 collective-permute-start.26
  95.3 1.5 %collective-permute-start.28 = (bf16[64,1792]{1,0:T(8,128)(2,1)S(1)}, bf16[64,1792]{1,0:T(8,128)(2,1)S(1)}, u32[]{:S(2)}, u32[]{:S(2)}) collective-permute-start(bf16[64,1792]{1,0:T(8,128)(2,1)S(1)} %get-tuple-element.37), channel_id=1, source_target_pairs={{0,8},{4,12},{8,0},{12,4},{1,9},{5,13},{9,1},{13,5},{2,10},{6,14},... | collective-permute-start | bytes 688136 | tf_op jit(solution)/shard_map/ppermute | solution.py:351
  96.9 1.2 collective-permute-start.33
  98.2 5.5 %collective-permute-done.28.refs_4_.refs_1_ = bf16[64,1792]{1,0:T(8,128)(2,1)S(1)} collective-permute-done((bf16[64,1792]{1,0:T(8,128)(2,1)S(1)}, bf16[64,1792]{1,0:T(8,128)(2,1)S(1)}, u32[]{:S(2)}, u32[]{:S(2)}) %collective-permute-start.28) | collective-permute-done | bytes 229408 | tf_op jit(solution)/shard_map/ppermute | solution.py:351
  103.9 0.1 add.65
  104.0 1.5 %collective-permute-start.29 = (bf16[64,1792]{1,0:T(8,128)(2,1)S(1)}, bf16[64,1792]{1,0:T(8,128)(2,1)S(1)}, u32[]{:S(2)}, u32[]{:S(2)}) collective-permute-start(bf16[64,1792]{1,0:T(8,128)(2,1)S(1)} %get-tuple-element.39), channel_id=1, source_target_pairs={{0,8},{4,12},{8,0},{12,4},{1,9},{5,13},{9,1},{13,5},{2,10},{6,14},... | collective-permute-start | bytes 688136 | tf_op jit(solution)/shard_map/ppermute | solution.py:351
  105.6 3.1 %collective-permute-done.33.refs_1_ = bf16[64,1792]{1,0:T(8,128)(2,1)S(1)} collective-permute-done((bf16[64,1792]{1,0:T(8,128)(2,1)S(1)}, bf16[64,1792]{1,0:T(8,128)(2,1)S(1)}, u32[]{:S(2)}, u32[]{:S(2)}) %collective-permute-start.33) | collective-permute-done | bytes 229408 | tf_op jit(solution)/shard_map/ppermute | solution.py:351
  108.8 1.7 %collective-permute-start.34 = (bf16[64,1792]{1,0:T(8,128)(2,1)S(1)}, bf16[64,1792]{1,0:T(8,128)(2,1)S(1)}, u32[]{:S(2)}, u32[]{:S(2)}) collective-permute-start(bf16[64,1792]{1,0:T(8,128)(2,1)S(1)} %add.69), channel_id=1, source_target_pairs={{0,3},{1,2},{2,1},{3,0},{4,7},{5,6},{6,5},{7,4},{8,11},{9,10},{10,... | collective-permute-start | bytes 688136 | tf_op jit(solution)/shard_map/ppermute | solution.py:354
  110.5 0.2 collective-permute-done.30.refs_2_
  110.6 8.9 %collective-permute-done.31.refs_3_ = bf16[64,1792]{1,0:T(8,128)(2,1)S(1)} collective-permute-done((bf16[64,1792]{1,0:T(8,128)(2,1)S(1)}, bf16[64,1792]{1,0:T(8,128)(2,1)S(1)}, u32[]{:S(2)}, u32[]{:S(2)}) %collective-permute-start.31) | collective-permute-done | bytes 229408 | tf_op jit(solution)/shard_map/ppermute | solution.py:354
  119.5 0.8 add.70
  (60 shorter events, 1.2 us)
Async XLA Ops:
  0.6 20.6 %copy-start = (bf16[256,1792]{1,0:T(8,128)(2,1)S(1)}, bf16[256,1792]{1,0:T(8,128)(2,1)}, u32[]{:S(2)}) copy-start(bf16[256,1792]{1,0:T(8,128)(2,1)} %param.21) | copy-start | bytes 2752516
  0.8 0.7 copy-start.2
  1.5 16.2 %copy-start.4 = (f32[256,2]{0,1:T(2,128)S(1)}, f32[256,2]{0,1:T(2,128)}, u32[]{:S(2)}) copy-start(f32[256,2]{0,1:T(2,128)} %param.24) | copy-start | bytes 6148
  1.5 16.2 %copy-start.5 = (s32[256,2]{0,1:T(2,128)S(1)}, s32[256,2]{0,1:T(2,128)}, u32[]{:S(2)}) copy-start(s32[256,2]{0,1:T(2,128)} %param.23) | copy-start | bytes 6148
  1.5 16.4 %copy-start.3 = (f32[1792]{0:T(1024)S(1)}, f32[1792]{0:T(1024)}, u32[]{:S(2)}) copy-start(f32[1792]{0:T(1024)} %param.22) | copy-start | bytes 21508
  14.7 6.5 %collective-permute-start.1 = (bf16[64,1024]{1,0:T(8,128)(2,1)S(1)}, bf16[64,1024]{1,0:T(8,128)(2,1)S(1)}, u32[]{:S(2)}, u32[]{:S(2)}) collective-permute-start(bf16[64,1024]{1,0:T(8,128)(2,1)S(1)} %attention.1.refs_1_.refs_0_), channel_id=1, source_target_pairs={{0,8},{4,12},{8,0},{12,4},{1,9},{5,13},{9,1},{13,5},{2,10},{6,14},... | collective-permute-start | bytes 393224 | tf_op jit(solution)/shard_map/ppermute | solution.py:351
  17.7 5.6 %collective-permute-start = (bf16[64,1024]{1,0:T(8,128)(2,1)S(1)}, bf16[64,1024]{1,0:T(8,128)(2,1)S(1)}, u32[]{:S(2)}, u32[]{:S(2)}) collective-permute-start(bf16[64,1024]{1,0:T(8,128)(2,1)S(1)} %attention.1.refs_1_.refs_0_), channel_id=1, source_target_pairs={{0,4},{4,0},{8,12},{12,8},{1,5},{5,1},{9,13},{13,9},{2,6},{6,2},{1... | collective-permute-start | bytes 393224 | tf_op jit(solution)/shard_map/ppermute | solution.py:347
  21.2 2.1 %collective-permute-start.2 = (bf16[64,1024]{1,0:T(8,128)(2,1)S(1)}, bf16[64,1024]{1,0:T(8,128)(2,1)S(1)}, u32[]{:S(2)}, u32[]{:S(2)}) collective-permute-start(bf16[64,1024]{1,0:T(8,128)(2,1)S(1)} %collective-permute-done.1.refs_2_), channel_id=1, source_target_pairs={{0,4},{4,0},{8,12},{12,8},{1,5},{5,1},{9,13},{13,9},{2,6},{6,2},{1... | collective-permute-start | bytes 393224 | tf_op jit(solution)/shard_map/ppermute | solution.py:347
  25.1 8.3 %collective-permute-start.3 = (bf16[64,1792]{1,0:T(8,128)(2,1)S(1)}, bf16[64,1792]{1,0:T(8,128)(2,1)S(1)}, u32[]{:S(2)}, u32[]{:S(2)}) collective-permute-start(bf16[64,1792]{1,0:T(8,128)(2,1)S(1)} %get-tuple-element.26), channel_id=1, source_target_pairs={{0,1},{1,0},{2,3},{3,2},{4,5},{5,4},{6,7},{7,6},{8,9},{9,8},{10,11... | collective-permute-start | bytes 688136 | tf_op jit(solution)/shard_map/ppermute | solution.py:354
  30.2 16.3 %collective-permute-start.5 = (bf16[64,1792]{1,0:T(8,128)(2,1)S(1)}, bf16[64,1792]{1,0:T(8,128)(2,1)S(1)}, u32[]{:S(2)}, u32[]{:S(2)}) collective-permute-start(bf16[64,1792]{1,0:T(8,128)(2,1)S(1)} %add.61.refs_1_), channel_id=1, source_target_pairs={{0,1},{1,0},{2,3},{3,2},{4,5},{5,4},{6,7},{7,6},{8,9},{9,8},{10,11... | collective-permute-start | bytes 688136 | tf_op jit(solution)/shard_map/ppermute | solution.py:354
  33.4 13.2 %collective-permute-start.4 = (bf16[64,1792]{1,0:T(8,128)(2,1)S(1)}, bf16[64,1792]{1,0:T(8,128)(2,1)S(1)}, u32[]{:S(2)}, u32[]{:S(2)}) collective-permute-start(bf16[64,1792]{1,0:T(8,128)(2,1)S(1)} %add.60), channel_id=1, source_target_pairs={{0,2},{1,3},{2,0},{3,1},{4,6},{5,7},{6,4},{7,5},{8,10},{9,11},{10,... | collective-permute-start | bytes 688136 | tf_op jit(solution)/shard_map/ppermute | solution.py:354
  36.4 3.6 %collective-permute-start.7 = (f32[1,1792]{1,0:T(1,128)S(1)}, f32[1,1792]{1,0:T(1,128)S(1)}, u32[]{:S(2)}, u32[]{:S(2)}) collective-permute-start(f32[1,1792]{1,0:T(1,128)S(1)} %reshape.7.refs_4_.refs_8_), channel_id=1, source_target_pairs={{0,8},{4,12},{8,0},{12,4},{1,9},{5,13},{9,1},{13,5},{2,10},{6,14},... | collective-permute-start | bytes 21512 | tf_op jit(solution)/shard_map/ppermute | solution.py:351
  37.9 8.5 %collective-permute-start.6 = (f32[1,1792]{1,0:T(1,128)S(1)}, f32[1,1792]{1,0:T(1,128)S(1)}, u32[]{:S(2)}, u32[]{:S(2)}) collective-permute-start(f32[1,1792]{1,0:T(1,128)S(1)} %reshape.7.refs_4_.refs_8_), channel_id=1, source_target_pairs={{0,4},{4,0},{8,12},{12,8},{1,5},{5,1},{9,13},{13,9},{2,6},{6,2},{1... | collective-permute-start | bytes 21512 | tf_op jit(solution)/shard_map/ppermute | solution.py:347
  40.1 6.4 %collective-permute-start.8 = (f32[1,1792]{1,0:T(1,128)S(1)}, f32[1,1792]{1,0:T(1,128)S(1)}, u32[]{:S(2)}, u32[]{:S(2)}) collective-permute-start(f32[1,1792]{1,0:T(1,128)S(1)} %collective-permute-done.7.refs_10_), channel_id=1, source_target_pairs={{0,4},{4,0},{8,12},{12,8},{1,5},{5,1},{9,13},{13,9},{2,6},{6,2},{1... | collective-permute-start | bytes 21512 | tf_op jit(solution)/shard_map/ppermute | solution.py:347
  47.4 13.8 %collective-permute-start.9 = (bf16[64,1792]{1,0:T(8,128)(2,1)S(1)}, bf16[64,1792]{1,0:T(8,128)(2,1)S(1)}, u32[]{:S(2)}, u32[]{:S(2)}) collective-permute-start(bf16[64,1792]{1,0:T(8,128)(2,1)S(1)} %get-tuple-element.29.refs_14_.refs_4_), channel_id=1, source_target_pairs={{0,2},{1,3},{2,0},{3,1},{4,6},{5,7},{6,4},{7,5},{8,10},{9,11},{10,... | collective-permute-start | bytes 688136 | tf_op jit(solution)/shard_map/ppermute | solution.py:354
  47.5 15.3 %collective-permute-start.20 = (bf16[64,1792]{1,0:T(8,128)(2,1)S(1)}, bf16[64,1792]{1,0:T(8,128)(2,1)S(1)}, u32[]{:S(2)}, u32[]{:S(2)}) collective-permute-start(bf16[64,1792]{1,0:T(8,128)(2,1)S(1)} %get-tuple-element.29.refs_14_.refs_4_), channel_id=1, source_target_pairs={{0,1},{1,0},{2,3},{3,2},{4,5},{5,4},{6,7},{7,6},{8,9},{9,8},{10,11... | collective-permute-start | bytes 688136 | tf_op jit(solution)/shard_map/ppermute | solution.py:354
  51.6 11.6 %collective-permute-start.15 = (bf16[64,1792]{1,0:T(8,128)(2,1)S(1)}, bf16[64,1792]{1,0:T(8,128)(2,1)S(1)}, u32[]{:S(2)}, u32[]{:S(2)}) collective-permute-start(bf16[64,1792]{1,0:T(8,128)(2,1)S(1)} %get-tuple-element.29.refs_14_.refs_4_), channel_id=1, source_target_pairs={{0,8},{4,12},{8,0},{12,4},{1,9},{5,13},{9,1},{13,5},{2,10},{6,14},... | collective-permute-start | bytes 688136 | tf_op jit(solution)/shard_map/ppermute | solution.py:351
  53.1 10.1 %collective-permute-start.14 = (bf16[64,1792]{1,0:T(8,128)(2,1)S(1)}, bf16[64,1792]{1,0:T(8,128)(2,1)S(1)}, u32[]{:S(2)}, u32[]{:S(2)}) collective-permute-start(bf16[64,1792]{1,0:T(8,128)(2,1)S(1)} %get-tuple-element.29.refs_14_.refs_4_), channel_id=1, source_target_pairs={{0,4},{4,0},{8,12},{12,8},{1,5},{5,1},{9,13},{13,9},{2,6},{6,2},{1... | collective-permute-start | bytes 688136 | tf_op jit(solution)/shard_map/ppermute | solution.py:347
  61.2 8.5 %collective-permute-start.18 = (bf16[64,1792]{1,0:T(8,128)(2,1)S(1)}, bf16[64,1792]{1,0:T(8,128)(2,1)S(1)}, u32[]{:S(2)}, u32[]{:S(2)}) collective-permute-start(bf16[64,1792]{1,0:T(8,128)(2,1)S(1)} %collective-permute-done.9.refs_0_), channel_id=1, source_target_pairs={{0,8},{4,12},{8,0},{12,4},{1,9},{5,13},{9,1},{13,5},{2,10},{6,14},... | collective-permute-start | bytes 688136 | tf_op jit(solution)/shard_map/ppermute | solution.py:351
  62.7 10.5 %collective-permute-start.22 = (bf16[64,1792]{1,0:T(8,128)(2,1)S(1)}, bf16[64,1792]{1,0:T(8,128)(2,1)S(1)}, u32[]{:S(2)}, u32[]{:S(2)}) collective-permute-start(bf16[64,1792]{1,0:T(8,128)(2,1)S(1)} %collective-permute-done.20.refs_4_), channel_id=1, source_target_pairs={{0,8},{4,12},{8,0},{12,4},{1,9},{5,13},{9,1},{13,5},{2,10},{6,14},... | collective-permute-start | bytes 688136 | tf_op jit(solution)/shard_map/ppermute | solution.py:351
  63.2 10.0 %collective-permute-start.16 = (bf16[64,1792]{1,0:T(8,128)(2,1)S(1)}, bf16[64,1792]{1,0:T(8,128)(2,1)S(1)}, u32[]{:S(2)}, u32[]{:S(2)}) collective-permute-start(bf16[64,1792]{1,0:T(8,128)(2,1)S(1)} %collective-permute-done.15.refs_16_.refs_6_), channel_id=1, source_target_pairs={{0,4},{4,0},{8,12},{12,8},{1,5},{5,1},{9,13},{13,9},{2,6},{6,2},{1... | collective-permute-start | bytes 688136 | tf_op jit(solution)/shard_map/ppermute | solution.py:347
  63.2 10.5 %collective-permute-start.10 = (bf16[64,1792]{1,0:T(8,128)(2,1)S(1)}, bf16[64,1792]{1,0:T(8,128)(2,1)S(1)}, u32[]{:S(2)}, u32[]{:S(2)}) collective-permute-start(bf16[64,1792]{1,0:T(8,128)(2,1)S(1)} %collective-permute-done.9.refs_0_), channel_id=1, source_target_pairs={{0,1},{1,0},{2,3},{3,2},{4,5},{5,4},{6,7},{7,6},{8,9},{9,8},{10,11... | collective-permute-start | bytes 688136 | tf_op jit(solution)/shard_map/ppermute | solution.py:354
  63.3 11.9 %collective-permute-start.17 = (bf16[64,1792]{1,0:T(8,128)(2,1)S(1)}, bf16[64,1792]{1,0:T(8,128)(2,1)S(1)}, u32[]{:S(2)}, u32[]{:S(2)}) collective-permute-start(bf16[64,1792]{1,0:T(8,128)(2,1)S(1)} %collective-permute-done.9.refs_0_), channel_id=1, source_target_pairs={{0,4},{4,0},{8,12},{12,8},{1,5},{5,1},{9,13},{13,9},{2,6},{6,2},{1... | collective-permute-start | bytes 688136 | tf_op jit(solution)/shard_map/ppermute | solution.py:347
  69.7 5.4 %collective-permute-start.21 = (bf16[64,1792]{1,0:T(8,128)(2,1)S(1)}, bf16[64,1792]{1,0:T(8,128)(2,1)S(1)}, u32[]{:S(2)}, u32[]{:S(2)}) collective-permute-start(bf16[64,1792]{1,0:T(8,128)(2,1)S(1)} %collective-permute-done.20.refs_4_), channel_id=1, source_target_pairs={{0,4},{4,0},{8,12},{12,8},{1,5},{5,1},{9,13},{13,9},{2,6},{6,2},{1... | collective-permute-start | bytes 688136 | tf_op jit(solution)/shard_map/ppermute | solution.py:347
  73.2 2.0 %collective-permute-start.19 = (bf16[64,1792]{1,0:T(8,128)(2,1)S(1)}, bf16[64,1792]{1,0:T(8,128)(2,1)S(1)}, u32[]{:S(2)}, u32[]{:S(2)}) collective-permute-start(bf16[64,1792]{1,0:T(8,128)(2,1)S(1)} %collective-permute-done.18.refs_2_), channel_id=1, source_target_pairs={{0,4},{4,0},{8,12},{12,8},{1,5},{5,1},{9,13},{13,9},{2,6},{6,2},{1... | collective-permute-start | bytes 688136 | tf_op jit(solution)/shard_map/ppermute | solution.py:347
  73.2 2.0 %collective-permute-start.23 = (bf16[64,1792]{1,0:T(8,128)(2,1)S(1)}, bf16[64,1792]{1,0:T(8,128)(2,1)S(1)}, u32[]{:S(2)}, u32[]{:S(2)}) collective-permute-start(bf16[64,1792]{1,0:T(8,128)(2,1)S(1)} %collective-permute-done.22.refs_6_), channel_id=1, source_target_pairs={{0,4},{4,0},{8,12},{12,8},{1,5},{5,1},{9,13},{13,9},{2,6},{6,2},{1... | collective-permute-start | bytes 688136 | tf_op jit(solution)/shard_map/ppermute | solution.py:347
  73.7 7.6 %collective-permute-start.12 = (bf16[64,1792]{1,0:T(8,128)(2,1)S(1)}, bf16[64,1792]{1,0:T(8,128)(2,1)S(1)}, u32[]{:S(2)}, u32[]{:S(2)}) collective-permute-start(bf16[64,1792]{1,0:T(8,128)(2,1)S(1)} %collective-permute-done.10.refs_0_), channel_id=1, source_target_pairs={{0,8},{4,12},{8,0},{12,4},{1,9},{5,13},{9,1},{13,5},{2,10},{6,14},... | collective-permute-start | bytes 688136 | tf_op jit(solution)/shard_map/ppermute | solution.py:351
  83.1 1.9 %collective-permute-start.24 = (bf16[128,1792]{1,0:T(8,128)(2,1)S(1)}, bf16[128,1792]{1,0:T(8,128)(2,1)S(1)}, u32[]{:S(2)}, u32[]{:S(2)}) collective-permute-start(bf16[128,1792]{1,0:T(8,128)(2,1)S(1)} %get-tuple-element.31), channel_id=1, source_target_pairs={{0,4},{4,0},{8,12},{12,8},{1,5},{5,1},{9,13},{13,9},{2,6},{6,2},{1... | collective-permute-start | bytes 1376264 | tf_op jit(solution)/shard_map/ppermute | solution.py:347
  83.2 3.4 %collective-permute-start.11 = (bf16[64,1792]{1,0:T(8,128)(2,1)S(1)}, bf16[64,1792]{1,0:T(8,128)(2,1)S(1)}, u32[]{:S(2)}, u32[]{:S(2)}) collective-permute-start(bf16[64,1792]{1,0:T(8,128)(2,1)S(1)} %collective-permute-done.10.refs_0_), channel_id=1, source_target_pairs={{0,4},{4,0},{8,12},{12,8},{1,5},{5,1},{9,13},{13,9},{2,6},{6,2},{1... | collective-permute-start | bytes 688136 | tf_op jit(solution)/shard_map/ppermute | solution.py:347
  83.7 2.9 %collective-permute-start.13 = (bf16[64,1792]{1,0:T(8,128)(2,1)S(1)}, bf16[64,1792]{1,0:T(8,128)(2,1)S(1)}, u32[]{:S(2)}, u32[]{:S(2)}) collective-permute-start(bf16[64,1792]{1,0:T(8,128)(2,1)S(1)} %collective-permute-done.12.refs_0_.refs_2_), channel_id=1, source_target_pairs={{0,4},{4,0},{8,12},{12,8},{1,5},{5,1},{9,13},{13,9},{2,6},{6,2},{1... | collective-permute-start | bytes 688136 | tf_op jit(solution)/shard_map/ppermute | solution.py:347
  85.1 7.7 %collective-permute-start.25 = (bf16[64,1792]{1,0:T(8,128)(2,1)S(1)}, bf16[64,1792]{1,0:T(8,128)(2,1)S(1)}, u32[]{:S(2)}, u32[]{:S(2)}) collective-permute-start(bf16[64,1792]{1,0:T(8,128)(2,1)S(1)} %get-tuple-element.32.refs_14_), channel_id=1, source_target_pairs={{0,8},{4,12},{8,0},{12,4},{1,9},{5,13},{9,1},{13,5},{2,10},{6,14},... | collective-permute-start | bytes 688136 | tf_op jit(solution)/shard_map/ppermute | solution.py:351
  86.6 8.6 %collective-permute-start.27 = (bf16[128,1792]{1,0:T(8,128)(2,1)S(1)}, bf16[128,1792]{1,0:T(8,128)(2,1)S(1)}, u32[]{:S(2)}, u32[]{:S(2)}) collective-permute-start(bf16[128,1792]{1,0:T(8,128)(2,1)S(1)} %get-tuple-element.36), channel_id=1, source_target_pairs={{0,4},{4,0},{8,12},{12,8},{1,5},{5,1},{9,13},{13,9},{2,6},{6,2},{1... | collective-permute-start | bytes 1376264 | tf_op jit(solution)/shard_map/ppermute | solution.py:347
  86.6 33.7 %copy-start.1 = (bf16[256,1792]{1,0:T(8,128)(2,1)S(1)}, bf16[256,1792]{1,0:T(8,128)(2,1)}, u32[]{:S(2)}) copy-start(bf16[256,1792]{1,0:T(8,128)(2,1)} %param.21) | copy-start | bytes 2752516
  94.6 2.2 %collective-permute-start.32 = (bf16[128,1792]{1,0:T(8,128)(2,1)S(1)}, bf16[128,1792]{1,0:T(8,128)(2,1)S(1)}, u32[]{:S(2)}, u32[]{:S(2)}) collective-permute-start(bf16[128,1792]{1,0:T(8,128)(2,1)S(1)} %get-tuple-element.43), channel_id=1, source_target_pairs={{0,4},{4,0},{8,12},{12,8},{1,5},{5,1},{9,13},{13,9},{2,6},{6,2},{1... | collective-permute-start | bytes 1376264 | tf_op jit(solution)/shard_map/ppermute | solution.py:347
  94.6 9.3 %collective-permute-start.26 = (bf16[128,1792]{1,0:T(8,128)(2,1)S(1)}, bf16[128,1792]{1,0:T(8,128)(2,1)S(1)}, u32[]{:S(2)}, u32[]{:S(2)}) collective-permute-start(bf16[128,1792]{1,0:T(8,128)(2,1)S(1)} %get-tuple-element.34), channel_id=1, source_target_pairs={{0,4},{4,0},{8,12},{12,8},{1,5},{5,1},{9,13},{13,9},{2,6},{6,2},{1... | collective-permute-start | bytes 1376264 | tf_op jit(solution)/shard_map/ppermute | solution.py:347
  95.3 8.5 %collective-permute-start.28 = (bf16[64,1792]{1,0:T(8,128)(2,1)S(1)}, bf16[64,1792]{1,0:T(8,128)(2,1)S(1)}, u32[]{:S(2)}, u32[]{:S(2)}) collective-permute-start(bf16[64,1792]{1,0:T(8,128)(2,1)S(1)} %get-tuple-element.37), channel_id=1, source_target_pairs={{0,8},{4,12},{8,0},{12,4},{1,9},{5,13},{9,1},{13,5},{2,10},{6,14},... | collective-permute-start | bytes 688136 | tf_op jit(solution)/shard_map/ppermute | solution.py:351
  96.9 11.8 %collective-permute-start.33 = (bf16[64,1792]{1,0:T(8,128)(2,1)S(1)}, bf16[64,1792]{1,0:T(8,128)(2,1)S(1)}, u32[]{:S(2)}, u32[]{:S(2)}) collective-permute-start(bf16[64,1792]{1,0:T(8,128)(2,1)S(1)} %get-tuple-element.45), channel_id=1, source_target_pairs={{0,8},{4,12},{8,0},{12,4},{1,9},{5,13},{9,1},{13,5},{2,10},{6,14},... | collective-permute-start | bytes 688136 | tf_op jit(solution)/shard_map/ppermute | solution.py:351
  98.2 12.5 %collective-permute-start.30 = (bf16[64,1792]{1,0:T(8,128)(2,1)S(1)}, bf16[64,1792]{1,0:T(8,128)(2,1)S(1)}, u32[]{:S(2)}, u32[]{:S(2)}) collective-permute-start(bf16[64,1792]{1,0:T(8,128)(2,1)S(1)} %add.66), channel_id=1, source_target_pairs={{0,2},{1,3},{2,0},{3,1},{4,6},{5,7},{6,4},{7,5},{8,10},{9,11},{10,... | collective-permute-start | bytes 688136 | tf_op jit(solution)/shard_map/ppermute | solution.py:354
  103.8 15.7 %collective-permute-start.31 = (bf16[64,1792]{1,0:T(8,128)(2,1)S(1)}, bf16[64,1792]{1,0:T(8,128)(2,1)S(1)}, u32[]{:S(2)}, u32[]{:S(2)}) collective-permute-start(bf16[64,1792]{1,0:T(8,128)(2,1)S(1)} %add.67), channel_id=1, source_target_pairs={{0,1},{1,0},{2,3},{3,2},{4,5},{5,4},{6,7},{7,6},{8,9},{9,8},{10,11... | collective-permute-start | bytes 688136 | tf_op jit(solution)/shard_map/ppermute | solution.py:354
  104.0 15.5 %collective-permute-start.29 = (bf16[64,1792]{1,0:T(8,128)(2,1)S(1)}, bf16[64,1792]{1,0:T(8,128)(2,1)S(1)}, u32[]{:S(2)}, u32[]{:S(2)}) collective-permute-start(bf16[64,1792]{1,0:T(8,128)(2,1)S(1)} %get-tuple-element.39), channel_id=1, source_target_pairs={{0,8},{4,12},{8,0},{12,4},{1,9},{5,13},{9,1},{13,5},{2,10},{6,14},... | collective-permute-start | bytes 688136 | tf_op jit(solution)/shard_map/ppermute | solution.py:351
  108.8 10.8 %collective-permute-start.34 = (bf16[64,1792]{1,0:T(8,128)(2,1)S(1)}, bf16[64,1792]{1,0:T(8,128)(2,1)S(1)}, u32[]{:S(2)}, u32[]{:S(2)}) collective-permute-start(bf16[64,1792]{1,0:T(8,128)(2,1)S(1)} %add.69), channel_id=1, source_target_pairs={{0,3},{1,2},{2,1},{3,0},{4,7},{5,6},{6,5},{7,4},{8,11},{9,10},{10,... | collective-permute-start | bytes 688136 | tf_op jit(solution)/shard_map/ppermute | solution.py:354

commit v7 on v6

--- a/solution.py
+++ b/solution.py
@@ -10,6 +10,7 @@
 score_scale = 1.0 / 192.0**0.5
 norm_epsilon = 1e-06
 MIB = 1 << 20
+light = pl.CostEstimate(flops=1, bytes_accessed=1, transcendentals=0)
 
 
 def in_hbm(value):
@@ -237,9 +238,7 @@
             pltpu.VMEM((rows, hidden), jnp.float32),
             pltpu.VMEM((rows, hidden), jnp.float32),
         ],
-        cost_estimate=pl.CostEstimate(
-            flops=4 * rows * gate_weight.size, bytes_accessed=4 * gate_weight.size, transcendentals=rows * hidden
-        ),
+        cost_estimate=light,
         compiler_params=pltpu.CompilerParams(vmem_limit_bytes=2 * rows * (model_width + 4 * hidden) + 4 * MIB),
         name="activate",
     )(places, *[b for row in blocks for b in row], *gains, in_vmem(gate_weight), in_vmem(up_weight), *after)
@@ -282,9 +281,7 @@
         + [whole] * 3
         + [pl.BlockSpec(memory_space=pl.ANY)] * len(after),
         out_specs=[whole] * (row_blocks * cores),
-        cost_estimate=pl.CostEstimate(
-            flops=2 * rows * down_weight.size, bytes_accessed=2 * down_weight.size, transcendentals=0
-        ),
+        cost_estimate=light,
         compiler_params=pltpu.CompilerParams(vmem_limit_bytes=4 * MIB),
         name="down",
     )(places, active, row_weight, in_vmem(down_weight), *after)
@@ -313,6 +310,7 @@
         out_shape=[jax.ShapeDtypeStruct((height, width), jnp.bfloat16)] * len(groups),
         in_specs=[whole] * len(values) + [pl.BlockSpec(memory_space=pl.ANY)] * len(after),
         out_specs=[whole] * len(groups),
+        cost_estimate=light,
         compiler_params=pltpu.CompilerParams(vmem_limit_bytes=8 * MIB),
         name="add",
     )(*values, *after)
@@ -397,28 +395,35 @@
     blocks = [gather_ep(rows_of[k]) for k in range(tp_count)]
 
     half = tp_count // 2
-    groups = [list(reversed(range(1, half + 1))), list(reversed(range(half + 1, tp_count))) + [0]]
+    groups = [list(range(half, 0, -1)), list(range(tp_count - 1, half, -1))]
+    if tp_count == 4:
+        groups = [[2, 0], [3, 1]]
+    else:
+        groups[1].append(0)
+    late = groups[1]
+    hold_gate, hold_down, across = [rows_of[late[0]]], blocks[late[1]][-2:-1], blocks[late[0]][-2:-1]
     terms = [[] for _ in range(tp_count)]
-    arrivals = []
-    hold_gate, hold_down = blocks[0], [blocks[tp_count - 1][-2]]
     for group in groups:
         active = activate(places, [blocks[k] for k in group], gains, gate_weight, up_weight, hold_gate)
         outs = project_down(places, active, row_weight, down_weight, group, ep_count, cores, hold_down)
         swapped = [from_core(out[1]) for out in outs]
         for at, k in enumerate(group):
             pair = [[(outs[at][0], c * block_rows), (swapped[at], c * block_rows)] for c in range(chips)]
-            wait = arrivals[0] if len(arrivals) == 1 else arrivals[-2] if arrivals else []
-            sums = add(pair, block_rows, wait)
+            sums = add(pair, block_rows, across)
             across = [from_chip(sums[c], chips - c) for c in range(1, chips)]
-            if not arrivals:
-                hold_gate, hold_down = [sums[-1]], across
-            arrivals.append(across)
             terms[k] += [(value, 0) for value in [sums[0]] + across]
+            if at == 0:
+                hold_gate, hold_down = sums[1:], across
+        across = []
+    before = []
     for group in groups:
         for k in group:
             if k:
-                (total,) = add([terms[k]], block_rows)
-                terms[0].append((from_tp(total, k), 0))
+                (total,) = add([terms[k]], block_rows, before)
+                before = [from_tp(total, k)]
+                terms[0].append((before[0], 0))
+                if k < half:
+                    before = []
     (mixed,) = add([terms[0]], block_rows)
     return (stream_out, mixed)
 

time: 121 us -> 128 us (1.058)
  waiting for transfers between devices: 51.7 us -> 63.9 us
  starting transfers between devices: 28.7 us -> 24.6 us
    ppermute x9, waiting for transfers between devices: 20.2 us -> 39.2 us  [from_tp(): return lax.ppermute(value, 'tp', [(i, i ^ bits) for i in range(tp_count)])]
    ppermute x10, waiting for transfers between devices: 30.3 us -> 23.1 us  [from_chip(): lax.ppermute(value, 'ep', [(i, (i + step) % ep_count) for i in range(ep_c...]
    ppermute x10, starting transfers between devices: 15.3 us -> 12.1 us  [from_chip(): lax.ppermute(value, 'ep', [(i, (i + step) % ep_count) for i in range(ep_c...]
  transfers between devices with their start and end apart: 35 -> 35, of which waited for: 14 -> 18; matrix products, arithmetic and copies ran while one was open for 0% -> 0% of each run, Pallas kernels for 16% -> 14%
where the time goes in v7:
time: 128 us
  waiting for transfers between devices  63.9 us (50%)
  Pallas kernels  37.9 us (30%)
  starting transfers between devices  24.6 us (19%)
    ppermute x9, waiting for transfers between devices, from_tp(): return lax.ppermute(value, 'tp', [(i, i ^ bits) for i in range(tp_count)])  39.2 us
    ppermute x10, waiting for transfers between devices, from_chip(): lax.ppermute(value, 'ep', [(i, (i + step) % ep_count) for i in range(ep_c...  23.1 us
    pallas_call x1, Pallas kernels, attend(): pl.pallas_call(functools.partial(attention_kernel, step_rows), out_shape=...  13.2 us
    ppermute x10, starting transfers between devices, from_chip(): lax.ppermute(value, 'ep', [(i, (i + step) % ep_count) for i in range(ep_c...  12.1 us
    pallas_call x4, Pallas kernels, fetch(): pl.pallas_call(functools.partial(fetch_kernel, parts), out_shape=pltpu.VM...  11.6 us
    ppermute x9, starting transfers between devices, from_tp(): return lax.ppermute(value, 'tp', [(i, i ^ bits) for i in range(tp_count)])  10.5 us
    pallas_call x2, Pallas kernels, activate(): pl.pallas_call(functools.partial(gate_kernel, row_blocks, column_blocks,...  5.48 us
    pallas_call x2, Pallas kernels, project_down(): pl.pallas_call(functools.partial(down_kernel, slots, column_blocks, cores...  3.56 us
  transfers between devices with their start and end apart: 35, of which 18 were waited for; matrix products, arithmetic and copies ran while one was open for 0% of the time, Pallas kernels for 14%

profile of v7, /device:TPU:0, one launch (start us, length us, event | category | flops | bytes accessed | tf_op | source)
XLA Modules:
  0.0 128.3 jit_solution(11964112469438803093)
XLA Ops:
  0.8 0.7 copy-done.2
  1.5 13.2 %attention.1.refs_1_.refs_0_ = bf16[64,1024]{1,0:T(8,128)(2,1)S(1)} custom-call(s32[64]{0:T(128)S(1)} %copy-done.2, bf16[64,8,512]{2,1,0:T(8,128)(2,1)} %q_ref.1, bf16[64,512]{1,0:T(8,128)(2,1)} %qr_ref.1, bf16[64,256,512]{2,1,0:T(8,128)(2,1)} %k_ref.1, bf16[64,64,256]{2,1,0:T(8,128)(2,1)} %kr_ref.1, bf16[8,512,128]{2,1,0:T(8,128)(2,1)} %up_ref.1, ...), custom_call_target="tpu_custom_call" | custom-call | flops 4294967296 | bytes 16777216 | tf_op jit(solution)/shard_map/attention/pallas_call | solution.py:116
  14.7 3.0 %collective-permute-start.1 = (bf16[64,1024]{1,0:T(8,128)(2,1)S(1)}, bf16[64,1024]{1,0:T(8,128)(2,1)S(1)}, u32[]{:S(2)}, u32[]{:S(2)}) collective-permute-start(bf16[64,1024]{1,0:T(8,128)(2,1)S(1)} %attention.1.refs_1_.refs_0_), channel_id=1, source_target_pairs={{0,8},{4,12},{8,0},{12,4},{1,9},{5,13},{9,1},{13,5},{2,10},{6,14},... | collective-permute-start | bytes 393224 | tf_op jit(solution)/shard_map/ppermute | solution.py:349
  17.9 3.3 %collective-permute-done.1.refs_2_ = bf16[64,1024]{1,0:T(8,128)(2,1)S(1)} collective-permute-done((bf16[64,1024]{1,0:T(8,128)(2,1)S(1)}, bf16[64,1024]{1,0:T(8,128)(2,1)S(1)}, u32[]{:S(2)}, u32[]{:S(2)}) %collective-permute-start.1) | collective-permute-done | bytes 131104 | tf_op jit(solution)/shard_map/ppermute | solution.py:349
  21.3 2.0 %fetch.4.refs_4_ = bf16[1024,1792]{1,0:T(8,128)(2,1)S(1)} custom-call(bf16[1024,1792]{1,0:T(8,128)(2,1)} %refs_0_.4, bf16[64,1024]{1,0:T(8,128)(2,1)S(1)} %attention.1.refs_1_.refs_0_, f32[256,1]{1,0:T(8,128)S(1)} %copy.16.refs_2_.row_weight, bf16[64,1792]{1,0:T(8,128)(2,1)S(1)} %constant_dynamic-slice_fusion.refs_3_.refs_7_, ...), custom_call_target="tpu_custom_call" | custom-call | bytes 7340032 | tf_op jit(solution)/shard_map/fetch/pallas_call | solution.py:39
  23.3 1.8 %projection.1 = (bf16[64,1792]{1,0:T(8,128)(2,1)S(1)}, bf16[64,1792]{1,0:T(8,128)(2,1)S(1)}, bf16[64,1792]{1,0:T(8,128)(2,1)S(1)}, bf16[64,1792]{1,0:T(8,128)(2,1)S(1)}) custom-call(s32[8]{0:T(128)S(1)} %stack.35.refs_0_.places, bf16[64,1024]{1,0:T(8,128)(2,1)S(1)} %attention.1.refs_1_.refs_0_, bf16[64,1024]{1,0:T(8,128)(2,1)S(1)} %collective-permute-done.refs_1_, ...), custom_call_target="tpu_custom_call" | custom-call | flops 939524096 | bytes 4194304 | tf_op jit(solution)/shard_map/projection/pallas_call | solution.py:176
  25.1 1.9 %collective-permute-start.3 = (bf16[64,1792]{1,0:T(8,128)(2,1)S(1)}, bf16[64,1792]{1,0:T(8,128)(2,1)S(1)}, u32[]{:S(2)}, u32[]{:S(2)}) collective-permute-start(bf16[64,1792]{1,0:T(8,128)(2,1)S(1)} %get-tuple-element.26), channel_id=1, source_target_pairs={{0,1},{1,0},{2,3},{3,2},{4,5},{5,4},{6,7},{7,6},{8,9},{9,8},{10,11... | collective-permute-start | bytes 688136 | tf_op jit(solution)/shard_map/ppermute | solution.py:352
  27.0 3.2 %fetch.5.refs_1_.refs_12_ = bf16[1,7168,512]{2,1,0:T(8,128)(2,1)S(1)} custom-call(bf16[1,7168,512]{2,1,0:T(8,128)(2,1)} %refs_0_.5, bf16[64,1792]{1,0:T(8,128)(2,1)S(1)} %get-tuple-element.24.refs_1_.refs_0_.refs_4_), custom_call_target="tpu_custom_call" | custom-call | bytes 14680064 | tf_op jit(solution)/shard_map/fetch/pallas_call | solution.py:39
  30.5 2.9 %collective-permute-done.3.refs_1_ = bf16[64,1792]{1,0:T(8,128)(2,1)S(1)} collective-permute-done((bf16[64,1792]{1,0:T(8,128)(2,1)S(1)}, bf16[64,1792]{1,0:T(8,128)(2,1)S(1)}, u32[]{:S(2)}, u32[]{:S(2)}) %collective-permute-start.3) | collective-permute-done | bytes 229408 | tf_op jit(solution)/shard_map/ppermute | solution.py:352
  33.4 3.0 %collective-permute-start.4 = (bf16[64,1792]{1,0:T(8,128)(2,1)S(1)}, bf16[64,1792]{1,0:T(8,128)(2,1)S(1)}, u32[]{:S(2)}, u32[]{:S(2)}) collective-permute-start(bf16[64,1792]{1,0:T(8,128)(2,1)S(1)} %add.60), channel_id=1, source_target_pairs={{0,2},{1,3},{2,0},{3,1},{4,6},{5,7},{6,4},{7,5},{8,10},{9,11},{10,... | collective-permute-start | bytes 688136 | tf_op jit(solution)/shard_map/ppermute | solution.py:352
  36.4 1.5 %collective-permute-start.7 = (f32[1,1792]{1,0:T(1,128)S(1)}, f32[1,1792]{1,0:T(1,128)S(1)}, u32[]{:S(2)}, u32[]{:S(2)}) collective-permute-start(f32[1,1792]{1,0:T(1,128)S(1)} %reshape.7.refs_4_.refs_8_), channel_id=1, source_target_pairs={{0,8},{4,12},{8,0},{12,4},{1,9},{5,13},{9,1},{13,5},{2,10},{6,14},... | collective-permute-start | bytes 21512 | tf_op jit(solution)/shard_map/ppermute | solution.py:349
  37.9 2.1 %collective-permute-done.7.refs_10_ = f32[1,1792]{1,0:T(1,128)S(1)} collective-permute-done((f32[1,1792]{1,0:T(1,128)S(1)}, f32[1,1792]{1,0:T(1,128)S(1)}, u32[]{:S(2)}, u32[]{:S(2)}) %collective-permute-start.7) | collective-permute-done | bytes 7200 | tf_op jit(solution)/shard_map/ppermute | solution.py:349
  40.1 3.2 %fetch.6.refs_13_ = bf16[1,7168,512]{2,1,0:T(8,128)(2,1)S(1)} custom-call(bf16[1,7168,512]{2,1,0:T(8,128)(2,1)} %refs_0_.6, bf16[64,1792]{1,0:T(8,128)(2,1)S(1)} %add.61.refs_1_), custom_call_target="tpu_custom_call" | custom-call | bytes 14680064 | tf_op jit(solution)/shard_map/fetch/pallas_call | solution.py:39
  43.2 3.2 %fetch.7.refs_14_.down = bf16[1,512,7168]{2,1,0:T(8,128)(2,1)S(1)} custom-call(bf16[1,512,7168]{2,1,0:T(8,128)(2,1)} %refs_0_.7, bf16[64,1792]{1,0:T(8,128)(2,1)S(1)} %add.61.refs_1_), custom_call_target="tpu_custom_call" | custom-call | bytes 14680064 | tf_op jit(solution)/shard_map/fetch/pallas_call | solution.py:39
  46.6 0.8 add.62
  47.5 0.4 collective-permute-start.13
  47.8 1.6 %collective-permute-start.14 = (bf16[64,1792]{1,0:T(8,128)(2,1)S(1)}, bf16[64,1792]{1,0:T(8,128)(2,1)S(1)}, u32[]{:S(2)}, u32[]{:S(2)}) collective-permute-start(bf16[64,1792]{1,0:T(8,128)(2,1)S(1)} %get-tuple-element.29.refs_4_), channel_id=1, source_target_pairs={{0,8},{4,12},{8,0},{12,4},{1,9},{5,13},{9,1},{13,5},{2,10},{6,14},... | collective-permute-start | bytes 688136 | tf_op jit(solution)/shard_map/ppermute | solution.py:349
  49.4 11.8 %collective-permute-done.9.refs_0_ = bf16[64,1792]{1,0:T(8,128)(2,1)S(1)} collective-permute-done((bf16[64,1792]{1,0:T(8,128)(2,1)S(1)}, bf16[64,1792]{1,0:T(8,128)(2,1)S(1)}, u32[]{:S(2)}, u32[]{:S(2)}) %collective-permute-start.9) | collective-permute-done | bytes 229408 | tf_op jit(solution)/shard_map/ppermute | solution.py:352
  61.2 1.5 %collective-permute-start.11 = (bf16[64,1792]{1,0:T(8,128)(2,1)S(1)}, bf16[64,1792]{1,0:T(8,128)(2,1)S(1)}, u32[]{:S(2)}, u32[]{:S(2)}) collective-permute-start(bf16[64,1792]{1,0:T(8,128)(2,1)S(1)} %collective-permute-done.9.refs_0_), channel_id=1, source_target_pairs={{0,8},{4,12},{8,0},{12,4},{1,9},{5,13},{9,1},{13,5},{2,10},{6,14},... | collective-permute-start | bytes 688136 | tf_op jit(solution)/shard_map/ppermute | solution.py:349
  62.7 2.0 %collective-permute-start.16 = (bf16[64,1792]{1,0:T(8,128)(2,1)S(1)}, bf16[64,1792]{1,0:T(8,128)(2,1)S(1)}, u32[]{:S(2)}, u32[]{:S(2)}) collective-permute-start(bf16[64,1792]{1,0:T(8,128)(2,1)S(1)} %collective-permute-done.9.refs_0_), channel_id=1, source_target_pairs={{0,1},{1,0},{2,3},{3,2},{4,5},{5,4},{6,7},{7,6},{8,9},{9,8},{10,11... | collective-permute-start | bytes 688136 | tf_op jit(solution)/shard_map/ppermute | solution.py:352
  64.9 3.3 %collective-permute-done.11.refs_2_ = bf16[64,1792]{1,0:T(8,128)(2,1)S(1)} collective-permute-done((bf16[64,1792]{1,0:T(8,128)(2,1)S(1)}, bf16[64,1792]{1,0:T(8,128)(2,1)S(1)}, u32[]{:S(2)}, u32[]{:S(2)}) %collective-permute-start.11) | collective-permute-done | bytes 229408 | tf_op jit(solution)/shard_map/ppermute | solution.py:349
  68.2 3.0 %collective-permute-done.17.refs_4_ = bf16[64,1792]{1,0:T(8,128)(2,1)S(1)} collective-permute-done((bf16[64,1792]{1,0:T(8,128)(2,1)S(1)}, bf16[64,1792]{1,0:T(8,128)(2,1)S(1)}, u32[]{:S(2)}, u32[]{:S(2)}) %collective-permute-start.17) | collective-permute-done | bytes 229408 | tf_op jit(solution)/shard_map/ppermute | solution.py:352
  71.2 0.5 collective-permute-start.18
  71.7 2.6 %collective-permute-done.16.refs_14_.refs_0_ = bf16[64,1792]{1,0:T(8,128)(2,1)S(1)} collective-permute-done((bf16[64,1792]{1,0:T(8,128)(2,1)S(1)}, bf16[64,1792]{1,0:T(8,128)(2,1)S(1)}, u32[]{:S(2)}, u32[]{:S(2)}) %collective-permute-start.16) | collective-permute-done | bytes 229408 | tf_op jit(solution)/shard_map/ppermute | solution.py:352
  74.3 2.8 %activate.2.active = bf16[128,512]{1,0:T(8,128)(2,1)S(1)} custom-call(s32[8]{0:T(128)S(1)} %stack.35.refs_0_.places, bf16[64,1792]{1,0:T(8,128)(2,1)S(1)} %collective-permute-done.9.refs_0_, bf16[64,1792]{1,0:T(8,128)(2,1)S(1)} %collective-permute-done.10.refs_1_, bf16[64,1792]{1,0:T(8,128)(2,1)S(1)} %collective-permute-done.11.refs_2_, ...), custom_call_target="tpu_custom_call" | custom-call | flops 1 | bytes 1 | tf_op jit(solution)/shard_map/activate/pallas_call | solution.py:229
  77.2 1.8 %down.2 = (bf16[128,1792]{1,0:T(8,128)(2,1)S(1)}, bf16[128,1792]{1,0:T(8,128)(2,1)S(1)}, bf16[128,1792]{1,0:T(8,128)(2,1)S(1)}, bf16[128,1792]{1,0:T(8,128)(2,1)S(1)}) custom-call(s32[8]{0:T(128)S(1)} %stack.35.refs_0_.places, bf16[128,512]{1,0:T(8,128)(2,1)S(1)} %activate.2.active, f32[256,1]{1,0:T(8,128)S(1)} %copy.16.refs_2_.row_weight, ...), custom_call_target="tpu_custom_call" | custom-call | flops 1 | bytes 1 | tf_op jit(solution)/shard_map/down/pallas_call | solution.py:277
  79.1 0.6 collective-permute-start.21
  79.9 0.3 collective-permute-start.25
  80.4 6.7 %collective-permute-done.21.refs_4_.refs_2_ = bf16[64,1792]{1,0:T(8,128)(2,1)S(1)} collective-permute-done((bf16[64,1792]{1,0:T(8,128)(2,1)S(1)}, bf16[64,1792]{1,0:T(8,128)(2,1)S(1)}, u32[]{:S(2)}, u32[]{:S(2)}) %collective-permute-start.21) | collective-permute-done | bytes 229408 | tf_op jit(solution)/shard_map/ppermute | solution.py:349
  87.2 0.6 collective-permute-start.22
  87.9 0.7 collective-permute-done.26.refs_3_
  88.6 2.7 %activate.3.active = bf16[128,512]{1,0:T(8,128)(2,1)S(1)} custom-call(s32[8]{0:T(128)S(1)} %stack.35.refs_0_.places, bf16[64,1792]{1,0:T(8,128)(2,1)S(1)} %collective-permute-done.16.refs_14_.refs_0_, bf16[64,1792]{1,0:T(8,128)(2,1)S(1)} %collective-permute-done.25.refs_1_, bf16[64,1792]{1,0:T(8,128)(2,1)S(1)} %collective-permute-done.21.refs_4_.refs_2_, ...), custom_call_target="tpu_custom_call" | custom-call | flops 1 | bytes 1 | tf_op jit(solution)/shard_map/activate/pallas_call | solution.py:229
  91.3 4.0 %collective-permute-done.22.refs_4_.refs_1_.refs_0_ = bf16[64,1792]{1,0:T(8,128)(2,1)S(1)} collective-permute-done((bf16[64,1792]{1,0:T(8,128)(2,1)S(1)}, bf16[64,1792]{1,0:T(8,128)(2,1)S(1)}, u32[]{:S(2)}, u32[]{:S(2)}) %collective-permute-start.22) | collective-permute-done | bytes 229408 | tf_op jit(solution)/shard_map/ppermute | solution.py:349
  95.3 1.8 %down.3 = (bf16[128,1792]{1,0:T(8,128)(2,1)S(1)}, bf16[128,1792]{1,0:T(8,128)(2,1)S(1)}, bf16[128,1792]{1,0:T(8,128)(2,1)S(1)}, bf16[128,1792]{1,0:T(8,128)(2,1)S(1)}) custom-call(s32[8]{0:T(128)S(1)} %stack.35.refs_0_.places, bf16[128,512]{1,0:T(8,128)(2,1)S(1)} %activate.3.active, f32[256,1]{1,0:T(8,128)S(1)} %copy.16.refs_2_.row_weight, ...), custom_call_target="tpu_custom_call" | custom-call | flops 1 | bytes 1 | tf_op jit(solution)/shard_map/down/pallas_call | solution.py:277
  97.2 0.5 collective-permute-start.32
  97.7 0.5 collective-permute-start.24
  98.2 0.7 collective-permute-done.29.refs_1_.refs_3_
  99.1 0.6 collective-permute-start.30
  99.7 11.1 %collective-permute-done.24.refs_2_ = bf16[64,1792]{1,0:T(8,128)(2,1)S(1)} collective-permute-done((bf16[64,1792]{1,0:T(8,128)(2,1)S(1)}, bf16[64,1792]{1,0:T(8,128)(2,1)S(1)}, u32[]{:S(2)}, u32[]{:S(2)}) %collective-permute-start.24) | collective-permute-done | bytes 229408 | tf_op jit(solution)/shard_map/ppermute | solution.py:352
  110.9 1.8 %collective-permute-start.31 = (bf16[64,1792]{1,0:T(8,128)(2,1)S(1)}, bf16[64,1792]{1,0:T(8,128)(2,1)S(1)}, u32[]{:S(2)}, u32[]{:S(2)}) collective-permute-start(bf16[64,1792]{1,0:T(8,128)(2,1)S(1)} %add.67), channel_id=1, source_target_pairs={{0,3},{1,2},{2,1},{3,0},{4,7},{5,6},{6,5},{7,4},{8,11},{9,10},{10,... | collective-permute-start | bytes 688136 | tf_op jit(solution)/shard_map/ppermute | solution.py:352
  112.8 0.6 collective-permute-start.33
  113.4 1.6 %collective-permute-start.23 = (bf16[64,1792]{1,0:T(8,128)(2,1)S(1)}, bf16[64,1792]{1,0:T(8,128)(2,1)S(1)}, u32[]{:S(2)}, u32[]{:S(2)}) collective-permute-start(bf16[64,1792]{1,0:T(8,128)(2,1)S(1)} %get-tuple-element.36), channel_id=1, source_target_pairs={{0,8},{4,12},{8,0},{12,4},{1,9},{5,13},{9,1},{13,5},{2,10},{6,14},... | collective-permute-start | bytes 688136 | tf_op jit(solution)/shard_map/ppermute | solution.py:349
  115.0 5.3 %collective-permute-done.31.refs_2_.refs_3_ = bf16[64,1792]{1,0:T(8,128)(2,1)S(1)} collective-permute-done((bf16[64,1792]{1,0:T(8,128)(2,1)S(1)}, bf16[64,1792]{1,0:T(8,128)(2,1)S(1)}, u32[]{:S(2)}, u32[]{:S(2)}) %collective-permute-start.31) | collective-permute-done | bytes 229408 | tf_op jit(solution)/shard_map/ppermute | solution.py:352
  120.4 1.0 collective-permute-done.33.refs_1_
  121.4 1.0 collective-permute-start.34
  122.4 2.6 %collective-permute-done.23.refs_1_ = bf16[64,1792]{1,0:T(8,128)(2,1)S(1)} collective-permute-done((bf16[64,1792]{1,0:T(8,128)(2,1)S(1)}, bf16[64,1792]{1,0:T(8,128)(2,1)S(1)}, u32[]{:S(2)}, u32[]{:S(2)}) %collective-permute-start.23) | collective-permute-done | bytes 229408 | tf_op jit(solution)/shard_map/ppermute | solution.py:349
  125.0 2.5 %collective-permute-done.34.refs_4_ = bf16[64,1792]{1,0:T(8,128)(2,1)S(1)} collective-permute-done((bf16[64,1792]{1,0:T(8,128)(2,1)S(1)}, bf16[64,1792]{1,0:T(8,128)(2,1)S(1)}, u32[]{:S(2)}, u32[]{:S(2)}) %collective-permute-start.34) | collective-permute-done | bytes 229408 | tf_op jit(solution)/shard_map/ppermute | solution.py:352
  127.5 0.8 add.70
  (60 shorter events, 2.3 us)
Async XLA Ops:
  0.6 20.6 %copy-start = (bf16[256,1792]{1,0:T(8,128)(2,1)S(1)}, bf16[256,1792]{1,0:T(8,128)(2,1)}, u32[]{:S(2)}) copy-start(bf16[256,1792]{1,0:T(8,128)(2,1)} %param.21) | copy-start | bytes 2752516
  0.8 0.7 copy-start.2
  1.5 16.2 %copy-start.4 = (f32[256,2]{0,1:T(2,128)S(1)}, f32[256,2]{0,1:T(2,128)}, u32[]{:S(2)}) copy-start(f32[256,2]{0,1:T(2,128)} %param.24) | copy-start | bytes 6148
  1.5 16.2 %copy-start.5 = (s32[256,2]{0,1:T(2,128)S(1)}, s32[256,2]{0,1:T(2,128)}, u32[]{:S(2)}) copy-start(s32[256,2]{0,1:T(2,128)} %param.23) | copy-start | bytes 6148
  1.5 16.4 %copy-start.3 = (f32[1792]{0:T(1024)S(1)}, f32[1792]{0:T(1024)}, u32[]{:S(2)}) copy-start(f32[1792]{0:T(1024)} %param.22) | copy-start | bytes 21508
  14.7 6.5 %collective-permute-start.1 = (bf16[64,1024]{1,0:T(8,128)(2,1)S(1)}, bf16[64,1024]{1,0:T(8,128)(2,1)S(1)}, u32[]{:S(2)}, u32[]{:S(2)}) collective-permute-start(bf16[64,1024]{1,0:T(8,128)(2,1)S(1)} %attention.1.refs_1_.refs_0_), channel_id=1, source_target_pairs={{0,8},{4,12},{8,0},{12,4},{1,9},{5,13},{9,1},{13,5},{2,10},{6,14},... | collective-permute-start | bytes 393224 | tf_op jit(solution)/shard_map/ppermute | solution.py:349
  17.7 5.6 %collective-permute-start = (bf16[64,1024]{1,0:T(8,128)(2,1)S(1)}, bf16[64,1024]{1,0:T(8,128)(2,1)S(1)}, u32[]{:S(2)}, u32[]{:S(2)}) collective-permute-start(bf16[64,1024]{1,0:T(8,128)(2,1)S(1)} %attention.1.refs_1_.refs_0_), channel_id=1, source_target_pairs={{0,4},{4,0},{8,12},{12,8},{1,5},{5,1},{9,13},{13,9},{2,6},{6,2},{1... | collective-permute-start | bytes 393224 | tf_op jit(solution)/shard_map/ppermute | solution.py:345
  21.2 2.1 %collective-permute-start.2 = (bf16[64,1024]{1,0:T(8,128)(2,1)S(1)}, bf16[64,1024]{1,0:T(8,128)(2,1)S(1)}, u32[]{:S(2)}, u32[]{:S(2)}) collective-permute-start(bf16[64,1024]{1,0:T(8,128)(2,1)S(1)} %collective-permute-done.1.refs_2_), channel_id=1, source_target_pairs={{0,4},{4,0},{8,12},{12,8},{1,5},{5,1},{9,13},{13,9},{2,6},{6,2},{1... | collective-permute-start | bytes 393224 | tf_op jit(solution)/shard_map/ppermute | solution.py:345
  25.1 8.3 %collective-permute-start.3 = (bf16[64,1792]{1,0:T(8,128)(2,1)S(1)}, bf16[64,1792]{1,0:T(8,128)(2,1)S(1)}, u32[]{:S(2)}, u32[]{:S(2)}) collective-permute-start(bf16[64,1792]{1,0:T(8,128)(2,1)S(1)} %get-tuple-element.26), channel_id=1, source_target_pairs={{0,1},{1,0},{2,3},{3,2},{4,5},{5,4},{6,7},{7,6},{8,9},{9,8},{10,11... | collective-permute-start | bytes 688136 | tf_op jit(solution)/shard_map/ppermute | solution.py:352
  30.2 16.3 %collective-permute-start.5 = (bf16[64,1792]{1,0:T(8,128)(2,1)S(1)}, bf16[64,1792]{1,0:T(8,128)(2,1)S(1)}, u32[]{:S(2)}, u32[]{:S(2)}) collective-permute-start(bf16[64,1792]{1,0:T(8,128)(2,1)S(1)} %add.61.refs_1_), channel_id=1, source_target_pairs={{0,1},{1,0},{2,3},{3,2},{4,5},{5,4},{6,7},{7,6},{8,9},{9,8},{10,11... | collective-permute-start | bytes 688136 | tf_op jit(solution)/shard_map/ppermute | solution.py:352
  33.4 13.2 %collective-permute-start.4 = (bf16[64,1792]{1,0:T(8,128)(2,1)S(1)}, bf16[64,1792]{1,0:T(8,128)(2,1)S(1)}, u32[]{:S(2)}, u32[]{:S(2)}) collective-permute-start(bf16[64,1792]{1,0:T(8,128)(2,1)S(1)} %add.60), channel_id=1, source_target_pairs={{0,2},{1,3},{2,0},{3,1},{4,6},{5,7},{6,4},{7,5},{8,10},{9,11},{10,... | collective-permute-start | bytes 688136 | tf_op jit(solution)/shard_map/ppermute | solution.py:352
  36.4 3.6 %collective-permute-start.7 = (f32[1,1792]{1,0:T(1,128)S(1)}, f32[1,1792]{1,0:T(1,128)S(1)}, u32[]{:S(2)}, u32[]{:S(2)}) collective-permute-start(f32[1,1792]{1,0:T(1,128)S(1)} %reshape.7.refs_4_.refs_8_), channel_id=1, source_target_pairs={{0,8},{4,12},{8,0},{12,4},{1,9},{5,13},{9,1},{13,5},{2,10},{6,14},... | collective-permute-start | bytes 21512 | tf_op jit(solution)/shard_map/ppermute | solution.py:349
  37.9 8.5 %collective-permute-start.6 = (f32[1,1792]{1,0:T(1,128)S(1)}, f32[1,1792]{1,0:T(1,128)S(1)}, u32[]{:S(2)}, u32[]{:S(2)}) collective-permute-start(f32[1,1792]{1,0:T(1,128)S(1)} %reshape.7.refs_4_.refs_8_), channel_id=1, source_target_pairs={{0,4},{4,0},{8,12},{12,8},{1,5},{5,1},{9,13},{13,9},{2,6},{6,2},{1... | collective-permute-start | bytes 21512 | tf_op jit(solution)/shard_map/ppermute | solution.py:345
  40.1 6.4 %collective-permute-start.8 = (f32[1,1792]{1,0:T(1,128)S(1)}, f32[1,1792]{1,0:T(1,128)S(1)}, u32[]{:S(2)}, u32[]{:S(2)}) collective-permute-start(f32[1,1792]{1,0:T(1,128)S(1)} %collective-permute-done.7.refs_10_), channel_id=1, source_target_pairs={{0,4},{4,0},{8,12},{12,8},{1,5},{5,1},{9,13},{13,9},{2,6},{6,2},{1... | collective-permute-start | bytes 21512 | tf_op jit(solution)/shard_map/ppermute | solution.py:345
  47.4 13.7 %collective-permute-start.9 = (bf16[64,1792]{1,0:T(8,128)(2,1)S(1)}, bf16[64,1792]{1,0:T(8,128)(2,1)S(1)}, u32[]{:S(2)}, u32[]{:S(2)}) collective-permute-start(bf16[64,1792]{1,0:T(8,128)(2,1)S(1)} %get-tuple-element.29.refs_4_), channel_id=1, source_target_pairs={{0,2},{1,3},{2,0},{3,1},{4,6},{5,7},{6,4},{7,5},{8,10},{9,11},{10,... | collective-permute-start | bytes 688136 | tf_op jit(solution)/shard_map/ppermute | solution.py:352
  47.5 15.2 %collective-permute-start.13 = (bf16[64,1792]{1,0:T(8,128)(2,1)S(1)}, bf16[64,1792]{1,0:T(8,128)(2,1)S(1)}, u32[]{:S(2)}, u32[]{:S(2)}) collective-permute-start(bf16[64,1792]{1,0:T(8,128)(2,1)S(1)} %get-tuple-element.29.refs_4_), channel_id=1, source_target_pairs={{0,4},{4,0},{8,12},{12,8},{1,5},{5,1},{9,13},{13,9},{2,6},{6,2},{1... | collective-permute-start | bytes 688136 | tf_op jit(solution)/shard_map/ppermute | solution.py:345
  47.8 16.8 %collective-permute-start.14 = (bf16[64,1792]{1,0:T(8,128)(2,1)S(1)}, bf16[64,1792]{1,0:T(8,128)(2,1)S(1)}, u32[]{:S(2)}, u32[]{:S(2)}) collective-permute-start(bf16[64,1792]{1,0:T(8,128)(2,1)S(1)} %get-tuple-element.29.refs_4_), channel_id=1, source_target_pairs={{0,8},{4,12},{8,0},{12,4},{1,9},{5,13},{9,1},{13,5},{2,10},{6,14},... | collective-permute-start | bytes 688136 | tf_op jit(solution)/shard_map/ppermute | solution.py:349
  61.2 7.1 %collective-permute-start.11 = (bf16[64,1792]{1,0:T(8,128)(2,1)S(1)}, bf16[64,1792]{1,0:T(8,128)(2,1)S(1)}, u32[]{:S(2)}, u32[]{:S(2)}) collective-permute-start(bf16[64,1792]{1,0:T(8,128)(2,1)S(1)} %collective-permute-done.9.refs_0_), channel_id=1, source_target_pairs={{0,8},{4,12},{8,0},{12,4},{1,9},{5,13},{9,1},{13,5},{2,10},{6,14},... | collective-permute-start | bytes 688136 | tf_op jit(solution)/shard_map/ppermute | solution.py:349
  62.7 8.5 %collective-permute-start.17 = (bf16[64,1792]{1,0:T(8,128)(2,1)S(1)}, bf16[64,1792]{1,0:T(8,128)(2,1)S(1)}, u32[]{:S(2)}, u32[]{:S(2)}) collective-permute-start(bf16[64,1792]{1,0:T(8,128)(2,1)S(1)} %get-tuple-element.29.refs_4_), channel_id=1, source_target_pairs={{0,1},{1,0},{2,3},{3,2},{4,5},{5,4},{6,7},{7,6},{8,9},{9,8},{10,11... | collective-permute-start | bytes 688136 | tf_op jit(solution)/shard_map/ppermute | solution.py:352
  62.7 9.1 %collective-permute-start.10 = (bf16[64,1792]{1,0:T(8,128)(2,1)S(1)}, bf16[64,1792]{1,0:T(8,128)(2,1)S(1)}, u32[]{:S(2)}, u32[]{:S(2)}) collective-permute-start(bf16[64,1792]{1,0:T(8,128)(2,1)S(1)} %collective-permute-done.9.refs_0_), channel_id=1, source_target_pairs={{0,4},{4,0},{8,12},{12,8},{1,5},{5,1},{9,13},{13,9},{2,6},{6,2},{1... | collective-permute-start | bytes 688136 | tf_op jit(solution)/shard_map/ppermute | solution.py:345
  62.7 11.7 %collective-permute-start.16 = (bf16[64,1792]{1,0:T(8,128)(2,1)S(1)}, bf16[64,1792]{1,0:T(8,128)(2,1)S(1)}, u32[]{:S(2)}, u32[]{:S(2)}) collective-permute-start(bf16[64,1792]{1,0:T(8,128)(2,1)S(1)} %collective-permute-done.9.refs_0_), channel_id=1, source_target_pairs={{0,1},{1,0},{2,3},{3,2},{4,5},{5,4},{6,7},{7,6},{8,9},{9,8},{10,11... | collective-permute-start | bytes 688136 | tf_op jit(solution)/shard_map/ppermute | solution.py:352
  64.7 7.0 %collective-permute-start.15 = (bf16[64,1792]{1,0:T(8,128)(2,1)S(1)}, bf16[64,1792]{1,0:T(8,128)(2,1)S(1)}, u32[]{:S(2)}, u32[]{:S(2)}) collective-permute-start(bf16[64,1792]{1,0:T(8,128)(2,1)S(1)} %collective-permute-done.14.refs_6_), channel_id=1, source_target_pairs={{0,4},{4,0},{8,12},{12,8},{1,5},{5,1},{9,13},{13,9},{2,6},{6,2},{1... | collective-permute-start | bytes 688136 | tf_op jit(solution)/shard_map/ppermute | solution.py:345
  68.2 6.1 %collective-permute-start.12 = (bf16[64,1792]{1,0:T(8,128)(2,1)S(1)}, bf16[64,1792]{1,0:T(8,128)(2,1)S(1)}, u32[]{:S(2)}, u32[]{:S(2)}) collective-permute-start(bf16[64,1792]{1,0:T(8,128)(2,1)S(1)} %collective-permute-done.11.refs_2_), channel_id=1, source_target_pairs={{0,4},{4,0},{8,12},{12,8},{1,5},{5,1},{9,13},{13,9},{2,6},{6,2},{1... | collective-permute-start | bytes 688136 | tf_op jit(solution)/shard_map/ppermute | solution.py:345
  71.2 6.0 %collective-permute-start.18 = (bf16[64,1792]{1,0:T(8,128)(2,1)S(1)}, bf16[64,1792]{1,0:T(8,128)(2,1)S(1)}, u32[]{:S(2)}, u32[]{:S(2)}) collective-permute-start(bf16[64,1792]{1,0:T(8,128)(2,1)S(1)} %collective-permute-done.17.refs_4_), channel_id=1, source_target_pairs={{0,8},{4,12},{8,0},{12,4},{1,9},{5,13},{9,1},{13,5},{2,10},{6,14},... | collective-permute-start | bytes 688136 | tf_op jit(solution)/shard_map/ppermute | solution.py:349
  79.0 8.1 %collective-permute-start.20 = (bf16[128,1792]{1,0:T(8,128)(2,1)S(1)}, bf16[128,1792]{1,0:T(8,128)(2,1)S(1)}, u32[]{:S(2)}, u32[]{:S(2)}) collective-permute-start(bf16[128,1792]{1,0:T(8,128)(2,1)S(1)} %get-tuple-element.33), channel_id=1, source_target_pairs={{0,4},{4,0},{8,12},{12,8},{1,5},{5,1},{9,13},{13,9},{2,6},{6,2},{1... | collective-permute-start | bytes 1376264 | tf_op jit(solution)/shard_map/ppermute | solution.py:345
  79.1 8.0 %collective-permute-start.21 = (bf16[64,1792]{1,0:T(8,128)(2,1)S(1)}, bf16[64,1792]{1,0:T(8,128)(2,1)S(1)}, u32[]{:S(2)}, u32[]{:S(2)}) collective-permute-start(bf16[64,1792]{1,0:T(8,128)(2,1)S(1)} %collective-permute-done.16.refs_14_.refs_0_), channel_id=1, source_target_pairs={{0,8},{4,12},{8,0},{12,4},{1,9},{5,13},{9,1},{13,5},{2,10},{6,14},... | collective-permute-start | bytes 688136 | tf_op jit(solution)/shard_map/ppermute | solution.py:349
  79.7 8.1 %collective-permute-start.27 = (bf16[64,1792]{1,0:T(8,128)(2,1)S(1)}, bf16[64,1792]{1,0:T(8,128)(2,1)S(1)}, u32[]{:S(2)}, u32[]{:S(2)}) collective-permute-start(bf16[64,1792]{1,0:T(8,128)(2,1)S(1)} %collective-permute-done.17.refs_4_), channel_id=1, source_target_pairs={{0,4},{4,0},{8,12},{12,8},{1,5},{5,1},{9,13},{13,9},{2,6},{6,2},{1... | collective-permute-start | bytes 688136 | tf_op jit(solution)/shard_map/ppermute | solution.py:345
  79.9 8.0 %collective-permute-start.25 = (bf16[64,1792]{1,0:T(8,128)(2,1)S(1)}, bf16[64,1792]{1,0:T(8,128)(2,1)S(1)}, u32[]{:S(2)}, u32[]{:S(2)}) collective-permute-start(bf16[64,1792]{1,0:T(8,128)(2,1)S(1)} %collective-permute-done.16.refs_14_.refs_0_), channel_id=1, source_target_pairs={{0,4},{4,0},{8,12},{12,8},{1,5},{5,1},{9,13},{13,9},{2,6},{6,2},{1... | collective-permute-start | bytes 688136 | tf_op jit(solution)/shard_map/ppermute | solution.py:345
  80.2 7.6 %collective-permute-start.28 = (bf16[64,1792]{1,0:T(8,128)(2,1)S(1)}, bf16[64,1792]{1,0:T(8,128)(2,1)S(1)}, u32[]{:S(2)}, u32[]{:S(2)}) collective-permute-start(bf16[64,1792]{1,0:T(8,128)(2,1)S(1)} %collective-permute-done.18.refs_0_.refs_6_), channel_id=1, source_target_pairs={{0,4},{4,0},{8,12},{12,8},{1,5},{5,1},{9,13},{13,9},{2,6},{6,2},{1... | collective-permute-start | bytes 688136 | tf_op jit(solution)/shard_map/ppermute | solution.py:345
  87.1 1.5 %collective-permute-start.26 = (bf16[64,1792]{1,0:T(8,128)(2,1)S(1)}, bf16[64,1792]{1,0:T(8,128)(2,1)S(1)}, u32[]{:S(2)}, u32[]{:S(2)}) collective-permute-start(bf16[64,1792]{1,0:T(8,128)(2,1)S(1)} %collective-permute-done.21.refs_4_.refs_2_), channel_id=1, source_target_pairs={{0,4},{4,0},{8,12},{12,8},{1,5},{5,1},{9,13},{13,9},{2,6},{6,2},{1... | collective-permute-start | bytes 688136 | tf_op jit(solution)/shard_map/ppermute | solution.py:345
  87.2 8.1 %collective-permute-start.22 = (bf16[64,1792]{1,0:T(8,128)(2,1)S(1)}, bf16[64,1792]{1,0:T(8,128)(2,1)S(1)}, u32[]{:S(2)}, u32[]{:S(2)}) collective-permute-start(bf16[64,1792]{1,0:T(8,128)(2,1)S(1)} %get-tuple-element.34.refs_14_), channel_id=1, source_target_pairs={{0,8},{4,12},{8,0},{12,4},{1,9},{5,13},{9,1},{13,5},{2,10},{6,14},... | collective-permute-start | bytes 688136 | tf_op jit(solution)/shard_map/ppermute | solution.py:349
  88.6 39.7 %copy-start.1 = (bf16[256,1792]{1,0:T(8,128)(2,1)S(1)}, bf16[256,1792]{1,0:T(8,128)(2,1)}, u32[]{:S(2)}) copy-start(bf16[256,1792]{1,0:T(8,128)(2,1)} %param.21) | copy-start | bytes 2752516
  97.1 1.9 %collective-permute-start.29 = (bf16[128,1792]{1,0:T(8,128)(2,1)S(1)}, bf16[128,1792]{1,0:T(8,128)(2,1)S(1)}, u32[]{:S(2)}, u32[]{:S(2)}) collective-permute-start(bf16[128,1792]{1,0:T(8,128)(2,1)S(1)} %get-tuple-element.39), channel_id=1, source_target_pairs={{0,4},{4,0},{8,12},{12,8},{1,5},{5,1},{9,13},{13,9},{2,6},{6,2},{1... | collective-permute-start | bytes 1376264 | tf_op jit(solution)/shard_map/ppermute | solution.py:345
  97.2 15.5 %collective-permute-start.32 = (bf16[128,1792]{1,0:T(8,128)(2,1)S(1)}, bf16[128,1792]{1,0:T(8,128)(2,1)S(1)}, u32[]{:S(2)}, u32[]{:S(2)}) collective-permute-start(bf16[128,1792]{1,0:T(8,128)(2,1)S(1)} %get-tuple-element.43), channel_id=1, source_target_pairs={{0,4},{4,0},{8,12},{12,8},{1,5},{5,1},{9,13},{13,9},{2,6},{6,2},{1... | collective-permute-start | bytes 1376264 | tf_op jit(solution)/shard_map/ppermute | solution.py:345
  97.7 13.1 %collective-permute-start.24 = (bf16[64,1792]{1,0:T(8,128)(2,1)S(1)}, bf16[64,1792]{1,0:T(8,128)(2,1)S(1)}, u32[]{:S(2)}, u32[]{:S(2)}) collective-permute-start(bf16[64,1792]{1,0:T(8,128)(2,1)S(1)} %add.65), channel_id=1, source_target_pairs={{0,2},{1,3},{2,0},{3,1},{4,6},{5,7},{6,4},{7,5},{8,10},{9,11},{10,... | collective-permute-start | bytes 688136 | tf_op jit(solution)/shard_map/ppermute | solution.py:352
  99.1 11.7 %collective-permute-start.30 = (bf16[64,1792]{1,0:T(8,128)(2,1)S(1)}, bf16[64,1792]{1,0:T(8,128)(2,1)S(1)}, u32[]{:S(2)}, u32[]{:S(2)}) collective-permute-start(bf16[64,1792]{1,0:T(8,128)(2,1)S(1)} %get-tuple-element.41), channel_id=1, source_target_pairs={{0,8},{4,12},{8,0},{12,4},{1,9},{5,13},{9,1},{13,5},{2,10},{6,14},... | collective-permute-start | bytes 688136 | tf_op jit(solution)/shard_map/ppermute | solution.py:349
  99.7 13.6 %collective-permute-start.19 = (bf16[128,1792]{1,0:T(8,128)(2,1)S(1)}, bf16[128,1792]{1,0:T(8,128)(2,1)S(1)}, u32[]{:S(2)}, u32[]{:S(2)}) collective-permute-start(bf16[128,1792]{1,0:T(8,128)(2,1)S(1)} %get-tuple-element.31), channel_id=1, source_target_pairs={{0,4},{4,0},{8,12},{12,8},{1,5},{5,1},{9,13},{13,9},{2,6},{6,2},{1... | collective-permute-start | bytes 1376264 | tf_op jit(solution)/shard_map/ppermute | solution.py:345
  110.9 9.5 %collective-permute-start.31 = (bf16[64,1792]{1,0:T(8,128)(2,1)S(1)}, bf16[64,1792]{1,0:T(8,128)(2,1)S(1)}, u32[]{:S(2)}, u32[]{:S(2)}) collective-permute-start(bf16[64,1792]{1,0:T(8,128)(2,1)S(1)} %add.67), channel_id=1, source_target_pairs={{0,3},{1,2},{2,1},{3,0},{4,7},{5,6},{6,5},{7,4},{8,11},{9,10},{10,... | collective-permute-start | bytes 688136 | tf_op jit(solution)/shard_map/ppermute | solution.py:352
  112.8 8.6 %collective-permute-start.33 = (bf16[64,1792]{1,0:T(8,128)(2,1)S(1)}, bf16[64,1792]{1,0:T(8,128)(2,1)S(1)}, u32[]{:S(2)}, u32[]{:S(2)}) collective-permute-start(bf16[64,1792]{1,0:T(8,128)(2,1)S(1)} %get-tuple-element.45), channel_id=1, source_target_pairs={{0,8},{4,12},{8,0},{12,4},{1,9},{5,13},{9,1},{13,5},{2,10},{6,14},... | collective-permute-start | bytes 688136 | tf_op jit(solution)/shard_map/ppermute | solution.py:349
  113.4 11.6 %collective-permute-start.23 = (bf16[64,1792]{1,0:T(8,128)(2,1)S(1)}, bf16[64,1792]{1,0:T(8,128)(2,1)S(1)}, u32[]{:S(2)}, u32[]{:S(2)}) collective-permute-start(bf16[64,1792]{1,0:T(8,128)(2,1)S(1)} %get-tuple-element.36), channel_id=1, source_target_pairs={{0,8},{4,12},{8,0},{12,4},{1,9},{5,13},{9,1},{13,5},{2,10},{6,14},... | collective-permute-start | bytes 688136 | tf_op jit(solution)/shard_map/ppermute | solution.py:349
  121.4 6.1 %collective-permute-start.34 = (bf16[64,1792]{1,0:T(8,128)(2,1)S(1)}, bf16[64,1792]{1,0:T(8,128)(2,1)S(1)}, u32[]{:S(2)}, u32[]{:S(2)}) collective-permute-start(bf16[64,1792]{1,0:T(8,128)(2,1)S(1)} %add.69), channel_id=1, source_target_pairs={{0,1},{1,0},{2,3},{3,2},{4,5},{5,4},{6,7},{7,6},{8,9},{9,8},{10,11... | collective-permute-start | bytes 688136 | tf_op jit(solution)/shard_map/ppermute | solution.py:352

commit v8 on v6

--- a/solution.py
+++ b/solution.py
@@ -396,29 +396,23 @@
         rows_of[k] = from_tp(rows_of[k ^ low], low)
     blocks = [gather_ep(rows_of[k]) for k in range(tp_count)]
 
-    half = tp_count // 2
-    groups = [list(reversed(range(1, half + 1))), list(reversed(range(half + 1, tp_count))) + [0]]
+    slots = list(reversed(range(tp_count)))
+    active = activate(places, [blocks[k] for k in slots], gains, gate_weight, up_weight, [])
+    outs = project_down(places, active, row_weight, down_weight, slots, ep_count, cores, [])
+    swapped = [from_core(out[1]) for out in outs]
     terms = [[] for _ in range(tp_count)]
     arrivals = []
-    hold_gate, hold_down = blocks[0], [blocks[tp_count - 1][-2]]
-    for group in groups:
-        active = activate(places, [blocks[k] for k in group], gains, gate_weight, up_weight, hold_gate)
-        outs = project_down(places, active, row_weight, down_weight, group, ep_count, cores, hold_down)
-        swapped = [from_core(out[1]) for out in outs]
-        for at, k in enumerate(group):
-            pair = [[(outs[at][0], c * block_rows), (swapped[at], c * block_rows)] for c in range(chips)]
-            wait = arrivals[0] if len(arrivals) == 1 else arrivals[-2] if arrivals else []
-            sums = add(pair, block_rows, wait)
-            across = [from_chip(sums[c], chips - c) for c in range(1, chips)]
-            if not arrivals:
-                hold_gate, hold_down = [sums[-1]], across
-            arrivals.append(across)
-            terms[k] += [(value, 0) for value in [sums[0]] + across]
-    for group in groups:
-        for k in group:
-            if k:
-                (total,) = add([terms[k]], block_rows)
-                terms[0].append((from_tp(total, k), 0))
+    for at, k in enumerate(slots):
+        before = arrivals[0] if len(arrivals) == 1 else arrivals[-2] if arrivals else []
+        pair = [[(outs[at][0], c * block_rows), (swapped[at], c * block_rows)] for c in range(chips)]
+        sums = add(pair, block_rows, before)
+        across = [from_chip(sums[c], chips - c) for c in range(1, chips)]
+        arrivals.append(across)
+        terms[k] += [(value, 0) for value in [sums[0]] + across]
+        if k:
+            (total,) = add([terms[k]], block_rows)
+            low = k & -k
+            terms[k ^ low].append((from_tp(total, low), 0))
     (mixed,) = add([terms[0]], block_rows)
     return (stream_out, mixed)
 

time: 121 us -> 122 us (level)
  waiting for transfers between devices: 51.7 us -> 53.8 us
  Pallas kernels: 37.9 us -> 36.4 us
    ppermute x9, waiting for transfers between devices: 20.2 us -> 25.5 us  [from_tp(): return lax.ppermute(value, 'tp', [(i, i ^ bits) for i in range(tp_count)])]
    ppermute x10, waiting for transfers between devices: 30.3 us -> 25.6 us  [from_chip(): lax.ppermute(value, 'ep', [(i, (i + step) % ep_count) for i in range(ep_c...]
    ppermute x9, starting transfers between devices: 11.2 us -> 12.7 us  [from_tp(): return lax.ppermute(value, 'tp', [(i, i ^ bits) for i in range(tp_count)])]
    ppermute x16, waiting for transfers between devices: 1.27 us -> 2.66 us  [from_core(): return lax.ppermute(value, 'ep', [(i, i ^ 1) for i in range(ep_count)])]
    pallas_call x2 -> x1, Pallas kernels: 3.55 us -> 2.7 us  [project_down(): pl.pallas_call(functools.partial(down_kernel, slots, column_blocks, cores...]
    pallas_call x2 -> x1, Pallas kernels: 5.48 us -> 4.85 us  [activate(): pl.pallas_call(functools.partial(gate_kernel, row_blocks, column_blocks,...]
  transfers between devices with their start and end apart: 35 -> 35, of which waited for: 14 -> 16; matrix products, arithmetic and copies ran while one was open for 0% -> 0% of each run, Pallas kernels for 16% -> 10%
where the time goes in v8:
time: 122 us
  waiting for transfers between devices  53.8 us (44%)
  Pallas kernels  36.4 us (30%)
  starting transfers between devices  29.3 us (24%)
    ppermute x10, waiting for transfers between devices, from_chip(): lax.ppermute(value, 'ep', [(i, (i + step) % ep_count) for i in range(ep_c...  25.6 us
    ppermute x9, waiting for transfers between devices, from_tp(): return lax.ppermute(value, 'tp', [(i, i ^ bits) for i in range(tp_count)])  25.5 us
    ppermute x10, starting transfers between devices, from_chip(): lax.ppermute(value, 'ep', [(i, (i + step) % ep_count) for i in range(ep_c...  15.1 us
    pallas_call x1, Pallas kernels, attend(): pl.pallas_call(functools.partial(attention_kernel, step_rows), out_shape=...  13.2 us
    ppermute x9, starting transfers between devices, from_tp(): return lax.ppermute(value, 'tp', [(i, i ^ bits) for i in range(tp_count)])  12.7 us
    pallas_call x4, Pallas kernels, fetch(): pl.pallas_call(functools.partial(fetch_kernel, parts), out_shape=pltpu.VM...  11.6 us
    pallas_call x1, Pallas kernels, activate(): pl.pallas_call(functools.partial(gate_kernel, row_blocks, column_blocks,...  4.85 us
    pallas_call x1, Pallas kernels, project_down(): pl.pallas_call(functools.partial(down_kernel, slots, column_blocks, cores...  2.7 us
  transfers between devices with their start and end apart: 35, of which 16 were waited for; matrix products, arithmetic and copies ran while one was open for 0% of the time, Pallas kernels for 10%

profile of v8, /device:TPU:0, one launch (start us, length us, event | category | flops | bytes accessed | tf_op | source)
XLA Modules:
  0.0 121.5 jit_solution(17799508971171171259)
XLA Ops:
  0.8 0.7 copy-done.2
  1.5 13.2 %attention.1.refs_1_.refs_0_ = bf16[64,1024]{1,0:T(8,128)(2,1)S(1)} custom-call(s32[64]{0:T(128)S(1)} %copy-done.2, bf16[64,8,512]{2,1,0:T(8,128)(2,1)} %q_ref.1, bf16[64,512]{1,0:T(8,128)(2,1)} %qr_ref.1, bf16[64,256,512]{2,1,0:T(8,128)(2,1)} %k_ref.1, bf16[64,64,256]{2,1,0:T(8,128)(2,1)} %kr_ref.1, bf16[8,512,128]{2,1,0:T(8,128)(2,1)} %up_ref.1, ...), custom_call_target="tpu_custom_call" | custom-call | flops 4294967296 | bytes 16777216 | tf_op jit(solution)/shard_map/attention/pallas_call | solution.py:115
  14.7 3.0 %collective-permute-start.1 = (bf16[64,1024]{1,0:T(8,128)(2,1)S(1)}, bf16[64,1024]{1,0:T(8,128)(2,1)S(1)}, u32[]{:S(2)}, u32[]{:S(2)}) collective-permute-start(bf16[64,1024]{1,0:T(8,128)(2,1)S(1)} %attention.1.refs_1_.refs_0_), channel_id=1, source_target_pairs={{0,8},{4,12},{8,0},{12,4},{1,9},{5,13},{9,1},{13,5},{2,10},{6,14},... | collective-permute-start | bytes 393224 | tf_op jit(solution)/shard_map/ppermute | solution.py:351
  17.8 0.1 copy.16.refs_2_.row_weight
  17.9 3.3 %collective-permute-done.1.refs_2_ = bf16[64,1024]{1,0:T(8,128)(2,1)S(1)} collective-permute-done((bf16[64,1024]{1,0:T(8,128)(2,1)S(1)}, bf16[64,1024]{1,0:T(8,128)(2,1)S(1)}, u32[]{:S(2)}, u32[]{:S(2)}) %collective-permute-start.1) | collective-permute-done | bytes 131104 | tf_op jit(solution)/shard_map/ppermute | solution.py:351
  21.3 2.0 %fetch.4.refs_4_ = bf16[1024,1792]{1,0:T(8,128)(2,1)S(1)} custom-call(bf16[1024,1792]{1,0:T(8,128)(2,1)} %refs_0_.4, bf16[64,1024]{1,0:T(8,128)(2,1)S(1)} %attention.1.refs_1_.refs_0_, f32[256,1]{1,0:T(8,128)S(1)} %copy.16.refs_2_.row_weight, bf16[64,1792]{1,0:T(8,128)(2,1)S(1)} %constant_dynamic-slice_fusion.refs_3_.refs_7_, ...), custom_call_target="tpu_custom_call" | custom-call | bytes 7340032 | tf_op jit(solution)/shard_map/fetch/pallas_call | solution.py:38
  23.3 1.8 %projection.1 = (bf16[64,1792]{1,0:T(8,128)(2,1)S(1)}, bf16[64,1792]{1,0:T(8,128)(2,1)S(1)}, bf16[64,1792]{1,0:T(8,128)(2,1)S(1)}, bf16[64,1792]{1,0:T(8,128)(2,1)S(1)}) custom-call(s32[8]{0:T(128)S(1)} %stack.35.refs_0_.places, bf16[64,1024]{1,0:T(8,128)(2,1)S(1)} %attention.1.refs_1_.refs_0_, bf16[64,1024]{1,0:T(8,128)(2,1)S(1)} %collective-permute-done.refs_1_, ...), custom_call_target="tpu_custom_call" | custom-call | flops 939524096 | bytes 4194304 | tf_op jit(solution)/shard_map/projection/pallas_call | solution.py:175
  25.1 1.9 %collective-permute-start.3 = (bf16[64,1792]{1,0:T(8,128)(2,1)S(1)}, bf16[64,1792]{1,0:T(8,128)(2,1)S(1)}, u32[]{:S(2)}, u32[]{:S(2)}) collective-permute-start(bf16[64,1792]{1,0:T(8,128)(2,1)S(1)} %get-tuple-element.26), channel_id=1, source_target_pairs={{0,1},{1,0},{2,3},{3,2},{4,5},{5,4},{6,7},{7,6},{8,9},{9,8},{10,11... | collective-permute-start | bytes 688136 | tf_op jit(solution)/shard_map/ppermute | solution.py:354
  27.0 3.2 %fetch.5.refs_1_.refs_12_.refs_20_ = bf16[1,7168,512]{2,1,0:T(8,128)(2,1)S(1)} custom-call(bf16[1,7168,512]{2,1,0:T(8,128)(2,1)} %refs_0_.5, bf16[64,1792]{1,0:T(8,128)(2,1)S(1)} %get-tuple-element.24.refs_1_.refs_0_.refs_4_), custom_call_target="tpu_custom_call" | custom-call | bytes 14680064 | tf_op jit(solution)/shard_map/fetch/pallas_call | solution.py:38
  30.2 0.3 collective-permute-start.5
  30.5 2.9 %collective-permute-done.3.refs_1_ = bf16[64,1792]{1,0:T(8,128)(2,1)S(1)} collective-permute-done((bf16[64,1792]{1,0:T(8,128)(2,1)S(1)}, bf16[64,1792]{1,0:T(8,128)(2,1)S(1)}, u32[]{:S(2)}, u32[]{:S(2)}) %collective-permute-start.3) | collective-permute-done | bytes 229408 | tf_op jit(solution)/shard_map/ppermute | solution.py:354
  33.4 3.0 %collective-permute-start.4 = (bf16[64,1792]{1,0:T(8,128)(2,1)S(1)}, bf16[64,1792]{1,0:T(8,128)(2,1)S(1)}, u32[]{:S(2)}, u32[]{:S(2)}) collective-permute-start(bf16[64,1792]{1,0:T(8,128)(2,1)S(1)} %add.60), channel_id=1, source_target_pairs={{0,2},{1,3},{2,0},{3,1},{4,6},{5,7},{6,4},{7,5},{8,10},{9,11},{10,... | collective-permute-start | bytes 688136 | tf_op jit(solution)/shard_map/ppermute | solution.py:354
  36.4 1.5 %collective-permute-start.7 = (f32[1,1792]{1,0:T(1,128)S(1)}, f32[1,1792]{1,0:T(1,128)S(1)}, u32[]{:S(2)}, u32[]{:S(2)}) collective-permute-start(f32[1,1792]{1,0:T(1,128)S(1)} %reshape.7.refs_4_.refs_8_.refs_16_), channel_id=1, source_target_pairs={{0,8},{4,12},{8,0},{12,4},{1,9},{5,13},{9,1},{13,5},{2,10},{6,14},... | collective-permute-start | bytes 21512 | tf_op jit(solution)/shard_map/ppermute | solution.py:351
  37.9 2.1 %collective-permute-done.7.refs_10_.refs_18_ = f32[1,1792]{1,0:T(1,128)S(1)} collective-permute-done((f32[1,1792]{1,0:T(1,128)S(1)}, f32[1,1792]{1,0:T(1,128)S(1)}, u32[]{:S(2)}, u32[]{:S(2)}) %collective-permute-start.7) | collective-permute-done | bytes 7200 | tf_op jit(solution)/shard_map/ppermute | solution.py:351
  40.1 3.2 %fetch.7.refs_14_.down = bf16[1,512,7168]{2,1,0:T(8,128)(2,1)S(1)} custom-call(bf16[1,512,7168]{2,1,0:T(8,128)(2,1)} %refs_0_.7, bf16[64,1792]{1,0:T(8,128)(2,1)S(1)} %add.61.refs_1_), custom_call_target="tpu_custom_call" | custom-call | bytes 14680064 | tf_op jit(solution)/shard_map/fetch/pallas_call | solution.py:38
  43.3 3.2 %fetch.6.refs_13_.refs_21_ = bf16[1,7168,512]{2,1,0:T(8,128)(2,1)S(1)} custom-call(bf16[1,7168,512]{2,1,0:T(8,128)(2,1)} %refs_0_.6, bf16[64,1792]{1,0:T(8,128)(2,1)S(1)} %add.61.refs_1_), custom_call_target="tpu_custom_call" | custom-call | bytes 14680064 | tf_op jit(solution)/shard_map/fetch/pallas_call | solution.py:38
  46.6 0.8 add.62
  47.5 1.7 %collective-permute-start.22 = (bf16[64,1792]{1,0:T(8,128)(2,1)S(1)}, bf16[64,1792]{1,0:T(8,128)(2,1)S(1)}, u32[]{:S(2)}, u32[]{:S(2)}) collective-permute-start(bf16[64,1792]{1,0:T(8,128)(2,1)S(1)} %get-tuple-element.29.refs_12_), channel_id=1, source_target_pairs={{0,8},{4,12},{8,0},{12,4},{1,9},{5,13},{9,1},{13,5},{2,10},{6,14},... | collective-permute-start | bytes 688136 | tf_op jit(solution)/shard_map/ppermute | solution.py:351
  49.2 4.0 %collective-permute-start.17 = (bf16[64,1792]{1,0:T(8,128)(2,1)S(1)}, bf16[64,1792]{1,0:T(8,128)(2,1)S(1)}, u32[]{:S(2)}, u32[]{:S(2)}) collective-permute-start(bf16[64,1792]{1,0:T(8,128)(2,1)S(1)} %get-tuple-element.29.refs_12_), channel_id=1, source_target_pairs={{0,1},{1,0},{2,3},{3,2},{4,5},{5,4},{6,7},{7,6},{8,9},{9,8},{10,11... | collective-permute-start | bytes 688136 | tf_op jit(solution)/shard_map/ppermute | solution.py:354
  53.1 8.0 %collective-permute-done.9.refs_4_ = bf16[64,1792]{1,0:T(8,128)(2,1)S(1)} collective-permute-done((bf16[64,1792]{1,0:T(8,128)(2,1)S(1)}, bf16[64,1792]{1,0:T(8,128)(2,1)S(1)}, u32[]{:S(2)}, u32[]{:S(2)}) %collective-permute-start.9) | collective-permute-done | bytes 229408 | tf_op jit(solution)/shard_map/ppermute | solution.py:354
  61.2 1.6 %collective-permute-start.19 = (bf16[64,1792]{1,0:T(8,128)(2,1)S(1)}, bf16[64,1792]{1,0:T(8,128)(2,1)S(1)}, u32[]{:S(2)}, u32[]{:S(2)}) collective-permute-start(bf16[64,1792]{1,0:T(8,128)(2,1)S(1)} %collective-permute-done.17.refs_8_), channel_id=1, source_target_pairs={{0,8},{4,12},{8,0},{12,4},{1,9},{5,13},{9,1},{13,5},{2,10},{6,14},... | collective-permute-start | bytes 688136 | tf_op jit(solution)/shard_map/ppermute | solution.py:351
  62.8 0.2 collective-permute-start.18
  63.0 0.5 collective-permute-start.15
  63.5 4.8 %collective-permute-done.10.refs_0_ = bf16[64,1792]{1,0:T(8,128)(2,1)S(1)} collective-permute-done((bf16[64,1792]{1,0:T(8,128)(2,1)S(1)}, bf16[64,1792]{1,0:T(8,128)(2,1)S(1)}, u32[]{:S(2)}, u32[]{:S(2)}) %collective-permute-start.10) | collective-permute-done | bytes 229408 | tf_op jit(solution)/shard_map/ppermute | solution.py:354
  68.2 1.5 %collective-permute-start.12 = (bf16[64,1792]{1,0:T(8,128)(2,1)S(1)}, bf16[64,1792]{1,0:T(8,128)(2,1)S(1)}, u32[]{:S(2)}, u32[]{:S(2)}) collective-permute-start(bf16[64,1792]{1,0:T(8,128)(2,1)S(1)} %collective-permute-done.10.refs_0_), channel_id=1, source_target_pairs={{0,8},{4,12},{8,0},{12,4},{1,9},{5,13},{9,1},{13,5},{2,10},{6,14},... | collective-permute-start | bytes 688136 | tf_op jit(solution)/shard_map/ppermute | solution.py:351
  69.8 0.5 collective-permute-start.11
  70.3 4.2 %collective-permute-done.15.refs_6_ = bf16[64,1792]{1,0:T(8,128)(2,1)S(1)} collective-permute-done((bf16[64,1792]{1,0:T(8,128)(2,1)S(1)}, bf16[64,1792]{1,0:T(8,128)(2,1)S(1)}, u32[]{:S(2)}, u32[]{:S(2)}) %collective-permute-start.15) | collective-permute-done | bytes 229408 | tf_op jit(solution)/shard_map/ppermute | solution.py:351
  74.6 4.5 %collective-permute-done.12.refs_2_ = bf16[64,1792]{1,0:T(8,128)(2,1)S(1)} collective-permute-done((bf16[64,1792]{1,0:T(8,128)(2,1)S(1)}, bf16[64,1792]{1,0:T(8,128)(2,1)S(1)}, u32[]{:S(2)}, u32[]{:S(2)}) %collective-permute-start.12) | collective-permute-done | bytes 229408 | tf_op jit(solution)/shard_map/ppermute | solution.py:351
  79.1 1.5 %collective-permute-done.13.refs_3_ = bf16[64,1792]{1,0:T(8,128)(2,1)S(1)} collective-permute-done((bf16[64,1792]{1,0:T(8,128)(2,1)S(1)}, bf16[64,1792]{1,0:T(8,128)(2,1)S(1)}, u32[]{:S(2)}, u32[]{:S(2)}) %collective-permute-start.13) | collective-permute-done | bytes 229408 | tf_op jit(solution)/shard_map/ppermute | solution.py:347
  80.5 4.8 %activate.1.active = bf16[256,512]{1,0:T(8,128)(2,1)S(1)} custom-call(s32[8]{0:T(128)S(1)} %stack.35.refs_0_.places, bf16[64,1792]{1,0:T(8,128)(2,1)S(1)} %collective-permute-done.10.refs_0_, bf16[64,1792]{1,0:T(8,128)(2,1)S(1)} %collective-permute-done.11.refs_1_, bf16[64,1792]{1,0:T(8,128)(2,1)S(1)} %collective-permute-done.12.refs_2_, ...), custom_call_target="tpu_custom_call" | custom-call | flops 3758096384 | bytes 14680064 | tf_op jit(solution)/shard_map/activate/pallas_call | solution.py:228
  85.4 2.7 %down.1 = (bf16[128,1792]{1,0:T(8,128)(2,1)S(1)}, bf16[128,1792]{1,0:T(8,128)(2,1)S(1)}, bf16[128,1792]{1,0:T(8,128)(2,1)S(1)}, bf16[128,1792]{1,0:T(8,128)(2,1)...) custom-call(s32[8]{0:T(128)S(1)} %stack.35.refs_0_.places, ...), custom_call_target="tpu_custom_call" | custom-call | flops 1879048192 | bytes 7340032 | tf_op jit(solution)/shard_map/down/pallas_call | solution.py:278
  88.1 0.2 collective-permute-start.24
  88.3 0.4 collective-permute-start.27
  88.8 1.2 collective-permute-done.24.refs_1_.refs_3_
  90.1 1.6 %collective-permute-start.25 = (bf16[64,1792]{1,0:T(8,128)(2,1)S(1)}, bf16[64,1792]{1,0:T(8,128)(2,1)S(1)}, u32[]{:S(2)}, u32[]{:S(2)}) collective-permute-start(bf16[64,1792]{1,0:T(8,128)(2,1)S(1)} %get-tuple-element.33), channel_id=1, source_target_pairs={{0,8},{4,12},{8,0},{12,4},{1,9},{5,13},{9,1},{13,5},{2,10},{6,14},... | collective-permute-start | bytes 688136 | tf_op jit(solution)/shard_map/ppermute | solution.py:351
  91.7 6.1 %collective-permute-done.25.refs_1_.refs_4_ = bf16[64,1792]{1,0:T(8,128)(2,1)S(1)} collective-permute-done((bf16[64,1792]{1,0:T(8,128)(2,1)S(1)}, bf16[64,1792]{1,0:T(8,128)(2,1)S(1)}, u32[]{:S(2)}, u32[]{:S(2)}) %collective-permute-start.25) | collective-permute-done | bytes 229408 | tf_op jit(solution)/shard_map/ppermute | solution.py:351
  97.9 2.1 %collective-permute-start.26 = (bf16[64,1792]{1,0:T(8,128)(2,1)S(1)}, bf16[64,1792]{1,0:T(8,128)(2,1)S(1)}, u32[]{:S(2)}, u32[]{:S(2)}) collective-permute-start(bf16[64,1792]{1,0:T(8,128)(2,1)S(1)} %add.64), channel_id=1, source_target_pairs={{0,1},{1,0},{2,3},{3,2},{4,5},{5,4},{6,7},{7,6},{8,9},{9,8},{10,11... | collective-permute-start | bytes 688136 | tf_op jit(solution)/shard_map/ppermute | solution.py:354
  100.1 1.6 %collective-permute-start.28 = (bf16[64,1792]{1,0:T(8,128)(2,1)S(1)}, bf16[64,1792]{1,0:T(8,128)(2,1)S(1)}, u32[]{:S(2)}, u32[]{:S(2)}) collective-permute-start(bf16[64,1792]{1,0:T(8,128)(2,1)S(1)} %get-tuple-element.37), channel_id=1, source_target_pairs={{0,8},{4,12},{8,0},{12,4},{1,9},{5,13},{9,1},{13,5},{2,10},{6,14},... | collective-permute-start | bytes 688136 | tf_op jit(solution)/shard_map/ppermute | solution.py:351
  101.8 0.6 collective-permute-start.31
  102.3 2.7 %collective-permute-done.26.refs_0_ = bf16[64,1792]{1,0:T(8,128)(2,1)S(1)} collective-permute-done((bf16[64,1792]{1,0:T(8,128)(2,1)S(1)}, bf16[64,1792]{1,0:T(8,128)(2,1)S(1)}, u32[]{:S(2)}, u32[]{:S(2)}) %collective-permute-start.26) | collective-permute-done | bytes 229408 | tf_op jit(solution)/shard_map/ppermute | solution.py:354
  105.0 3.6 %collective-permute-done.28.refs_2_.refs_4_ = bf16[64,1792]{1,0:T(8,128)(2,1)S(1)} collective-permute-done((bf16[64,1792]{1,0:T(8,128)(2,1)S(1)}, bf16[64,1792]{1,0:T(8,128)(2,1)S(1)}, u32[]{:S(2)}, u32[]{:S(2)}) %collective-permute-start.28) | collective-permute-done | bytes 229408 | tf_op jit(solution)/shard_map/ppermute | solution.py:351
  108.8 1.2 collective-permute-start.29
  109.9 1.7 %collective-permute-done.31.refs_1_ = bf16[64,1792]{1,0:T(8,128)(2,1)S(1)} collective-permute-done((bf16[64,1792]{1,0:T(8,128)(2,1)S(1)}, bf16[64,1792]{1,0:T(8,128)(2,1)S(1)}, u32[]{:S(2)}, u32[]{:S(2)}) %collective-permute-start.31) | collective-permute-done | bytes 229408 | tf_op jit(solution)/shard_map/ppermute | solution.py:351
  111.6 0.4 collective-permute-start.32
  112.1 1.6 %collective-permute-start.34 = (bf16[64,1792]{1,0:T(8,128)(2,1)S(1)}, bf16[64,1792]{1,0:T(8,128)(2,1)S(1)}, u32[]{:S(2)}, u32[]{:S(2)}) collective-permute-start(bf16[64,1792]{1,0:T(8,128)(2,1)S(1)} %get-tuple-element.45), channel_id=1, source_target_pairs={{0,8},{4,12},{8,0},{12,4},{1,9},{5,13},{9,1},{13,5},{2,10},{6,14},... | collective-permute-start | bytes 688136 | tf_op jit(solution)/shard_map/ppermute | solution.py:351
  113.7 4.6 %collective-permute-done.29.refs_0_ = bf16[64,1792]{1,0:T(8,128)(2,1)S(1)} collective-permute-done((bf16[64,1792]{1,0:T(8,128)(2,1)S(1)}, bf16[64,1792]{1,0:T(8,128)(2,1)S(1)}, u32[]{:S(2)}, u32[]{:S(2)}) %collective-permute-start.29) | collective-permute-done | bytes 229408 | tf_op jit(solution)/shard_map/ppermute | solution.py:354
  118.3 2.4 %collective-permute-done.32.refs_1_ = bf16[64,1792]{1,0:T(8,128)(2,1)S(1)} collective-permute-done((bf16[64,1792]{1,0:T(8,128)(2,1)S(1)}, bf16[64,1792]{1,0:T(8,128)(2,1)S(1)}, u32[]{:S(2)}, u32[]{:S(2)}) %collective-permute-start.32) | collective-permute-done | bytes 229408 | tf_op jit(solution)/shard_map/ppermute | solution.py:354
  120.7 0.8 add.70
  (58 shorter events, 1.3 us)
Async XLA Ops:
  0.6 20.6 %copy-start = (bf16[256,1792]{1,0:T(8,128)(2,1)S(1)}, bf16[256,1792]{1,0:T(8,128)(2,1)}, u32[]{:S(2)}) copy-start(bf16[256,1792]{1,0:T(8,128)(2,1)} %param.21) | copy-start | bytes 2752516
  0.8 0.7 copy-start.2
  1.5 16.2 %copy-start.3 = (f32[1792]{0:T(1024)S(1)}, f32[1792]{0:T(1024)}, u32[]{:S(2)}) copy-start(f32[1792]{0:T(1024)} %param.22) | copy-start | bytes 21508
  1.5 16.2 %copy-start.4 = (f32[256,2]{0,1:T(2,128)S(1)}, f32[256,2]{0,1:T(2,128)}, u32[]{:S(2)}) copy-start(f32[256,2]{0,1:T(2,128)} %param.24) | copy-start | bytes 6148
  1.5 16.2 %copy-start.5 = (s32[256,2]{0,1:T(2,128)S(1)}, s32[256,2]{0,1:T(2,128)}, u32[]{:S(2)}) copy-start(s32[256,2]{0,1:T(2,128)} %param.23) | copy-start | bytes 6148
  14.7 6.5 %collective-permute-start.1 = (bf16[64,1024]{1,0:T(8,128)(2,1)S(1)}, bf16[64,1024]{1,0:T(8,128)(2,1)S(1)}, u32[]{:S(2)}, u32[]{:S(2)}) collective-permute-start(bf16[64,1024]{1,0:T(8,128)(2,1)S(1)} %attention.1.refs_1_.refs_0_), channel_id=1, source_target_pairs={{0,8},{4,12},{8,0},{12,4},{1,9},{5,13},{9,1},{13,5},{2,10},{6,14},... | collective-permute-start | bytes 393224 | tf_op jit(solution)/shard_map/ppermute | solution.py:351
  17.7 5.6 %collective-permute-start = (bf16[64,1024]{1,0:T(8,128)(2,1)S(1)}, bf16[64,1024]{1,0:T(8,128)(2,1)S(1)}, u32[]{:S(2)}, u32[]{:S(2)}) collective-permute-start(bf16[64,1024]{1,0:T(8,128)(2,1)S(1)} %attention.1.refs_1_.refs_0_), channel_id=1, source_target_pairs={{0,4},{4,0},{8,12},{12,8},{1,5},{5,1},{9,13},{13,9},{2,6},{6,2},{1... | collective-permute-start | bytes 393224 | tf_op jit(solution)/shard_map/ppermute | solution.py:347
  21.2 2.1 %collective-permute-start.2 = (bf16[64,1024]{1,0:T(8,128)(2,1)S(1)}, bf16[64,1024]{1,0:T(8,128)(2,1)S(1)}, u32[]{:S(2)}, u32[]{:S(2)}) collective-permute-start(bf16[64,1024]{1,0:T(8,128)(2,1)S(1)} %collective-permute-done.1.refs_2_), channel_id=1, source_target_pairs={{0,4},{4,0},{8,12},{12,8},{1,5},{5,1},{9,13},{13,9},{2,6},{6,2},{1... | collective-permute-start | bytes 393224 | tf_op jit(solution)/shard_map/ppermute | solution.py:347
  25.1 8.3 %collective-permute-start.3 = (bf16[64,1792]{1,0:T(8,128)(2,1)S(1)}, bf16[64,1792]{1,0:T(8,128)(2,1)S(1)}, u32[]{:S(2)}, u32[]{:S(2)}) collective-permute-start(bf16[64,1792]{1,0:T(8,128)(2,1)S(1)} %get-tuple-element.26), channel_id=1, source_target_pairs={{0,1},{1,0},{2,3},{3,2},{4,5},{5,4},{6,7},{7,6},{8,9},{9,8},{10,11... | collective-permute-start | bytes 688136 | tf_op jit(solution)/shard_map/ppermute | solution.py:354
  30.2 16.3 %collective-permute-start.5 = (bf16[64,1792]{1,0:T(8,128)(2,1)S(1)}, bf16[64,1792]{1,0:T(8,128)(2,1)S(1)}, u32[]{:S(2)}, u32[]{:S(2)}) collective-permute-start(bf16[64,1792]{1,0:T(8,128)(2,1)S(1)} %add.61.refs_1_), channel_id=1, source_target_pairs={{0,1},{1,0},{2,3},{3,2},{4,5},{5,4},{6,7},{7,6},{8,9},{9,8},{10,11... | collective-permute-start | bytes 688136 | tf_op jit(solution)/shard_map/ppermute | solution.py:354
  33.4 13.2 %collective-permute-start.4 = (bf16[64,1792]{1,0:T(8,128)(2,1)S(1)}, bf16[64,1792]{1,0:T(8,128)(2,1)S(1)}, u32[]{:S(2)}, u32[]{:S(2)}) collective-permute-start(bf16[64,1792]{1,0:T(8,128)(2,1)S(1)} %add.60), channel_id=1, source_target_pairs={{0,2},{1,3},{2,0},{3,1},{4,6},{5,7},{6,4},{7,5},{8,10},{9,11},{10,... | collective-permute-start | bytes 688136 | tf_op jit(solution)/shard_map/ppermute | solution.py:354
  36.4 3.6 %collective-permute-start.7 = (f32[1,1792]{1,0:T(1,128)S(1)}, f32[1,1792]{1,0:T(1,128)S(1)}, u32[]{:S(2)}, u32[]{:S(2)}) collective-permute-start(f32[1,1792]{1,0:T(1,128)S(1)} %reshape.7.refs_4_.refs_8_.refs_16_), channel_id=1, source_target_pairs={{0,8},{4,12},{8,0},{12,4},{1,9},{5,13},{9,1},{13,5},{2,10},{6,14},... | collective-permute-start | bytes 21512 | tf_op jit(solution)/shard_map/ppermute | solution.py:351
  37.9 8.5 %collective-permute-start.6 = (f32[1,1792]{1,0:T(1,128)S(1)}, f32[1,1792]{1,0:T(1,128)S(1)}, u32[]{:S(2)}, u32[]{:S(2)}) collective-permute-start(f32[1,1792]{1,0:T(1,128)S(1)} %reshape.7.refs_4_.refs_8_.refs_16_), channel_id=1, source_target_pairs={{0,4},{4,0},{8,12},{12,8},{1,5},{5,1},{9,13},{13,9},{2,6},{6,2},{1... | collective-permute-start | bytes 21512 | tf_op jit(solution)/shard_map/ppermute | solution.py:347
  40.1 6.4 %collective-permute-start.8 = (f32[1,1792]{1,0:T(1,128)S(1)}, f32[1,1792]{1,0:T(1,128)S(1)}, u32[]{:S(2)}, u32[]{:S(2)}) collective-permute-start(f32[1,1792]{1,0:T(1,128)S(1)} %collective-permute-done.7.refs_10_.refs_18_), channel_id=1, source_target_pairs={{0,4},{4,0},{8,12},{12,8},{1,5},{5,1},{9,13},{13,9},{2,6},{6,2},{1... | collective-permute-start | bytes 21512 | tf_op jit(solution)/shard_map/ppermute | solution.py:347
  47.5 13.7 %collective-permute-start.9 = (bf16[64,1792]{1,0:T(8,128)(2,1)S(1)}, bf16[64,1792]{1,0:T(8,128)(2,1)S(1)}, u32[]{:S(2)}, u32[]{:S(2)}) collective-permute-start(bf16[64,1792]{1,0:T(8,128)(2,1)S(1)} %get-tuple-element.29.refs_12_), channel_id=1, source_target_pairs={{0,2},{1,3},{2,0},{3,1},{4,6},{5,7},{6,4},{7,5},{8,10},{9,11},{10,... | collective-permute-start | bytes 688136 | tf_op jit(solution)/shard_map/ppermute | solution.py:354
  47.5 13.7 %collective-permute-start.22 = (bf16[64,1792]{1,0:T(8,128)(2,1)S(1)}, bf16[64,1792]{1,0:T(8,128)(2,1)S(1)}, u32[]{:S(2)}, u32[]{:S(2)}) collective-permute-start(bf16[64,1792]{1,0:T(8,128)(2,1)S(1)} %get-tuple-element.29.refs_12_), channel_id=1, source_target_pairs={{0,8},{4,12},{8,0},{12,4},{1,9},{5,13},{9,1},{13,5},{2,10},{6,14},... | collective-permute-start | bytes 688136 | tf_op jit(solution)/shard_map/ppermute | solution.py:351
  49.2 12.0 %collective-permute-start.17 = (bf16[64,1792]{1,0:T(8,128)(2,1)S(1)}, bf16[64,1792]{1,0:T(8,128)(2,1)S(1)}, u32[]{:S(2)}, u32[]{:S(2)}) collective-permute-start(bf16[64,1792]{1,0:T(8,128)(2,1)S(1)} %get-tuple-element.29.refs_12_), channel_id=1, source_target_pairs={{0,1},{1,0},{2,3},{3,2},{4,5},{5,4},{6,7},{7,6},{8,9},{9,8},{10,11... | collective-permute-start | bytes 688136 | tf_op jit(solution)/shard_map/ppermute | solution.py:354
  53.1 9.8 %collective-permute-start.21 = (bf16[64,1792]{1,0:T(8,128)(2,1)S(1)}, bf16[64,1792]{1,0:T(8,128)(2,1)S(1)}, u32[]{:S(2)}, u32[]{:S(2)}) collective-permute-start(bf16[64,1792]{1,0:T(8,128)(2,1)S(1)} %get-tuple-element.29.refs_12_), channel_id=1, source_target_pairs={{0,4},{4,0},{8,12},{12,8},{1,5},{5,1},{9,13},{13,9},{2,6},{6,2},{1... | collective-permute-start | bytes 688136 | tf_op jit(solution)/shard_map/ppermute | solution.py:347
  61.2 7.1 %collective-permute-start.10 = (bf16[64,1792]{1,0:T(8,128)(2,1)S(1)}, bf16[64,1792]{1,0:T(8,128)(2,1)S(1)}, u32[]{:S(2)}, u32[]{:S(2)}) collective-permute-start(bf16[64,1792]{1,0:T(8,128)(2,1)S(1)} %collective-permute-done.9.refs_4_), channel_id=1, source_target_pairs={{0,1},{1,0},{2,3},{3,2},{4,5},{5,4},{6,7},{7,6},{8,9},{9,8},{10,11... | collective-permute-start | bytes 688136 | tf_op jit(solution)/shard_map/ppermute | solution.py:354
  61.2 8.6 %collective-permute-start.23 = (bf16[64,1792]{1,0:T(8,128)(2,1)S(1)}, bf16[64,1792]{1,0:T(8,128)(2,1)S(1)}, u32[]{:S(2)}, u32[]{:S(2)}) collective-permute-start(bf16[64,1792]{1,0:T(8,128)(2,1)S(1)} %collective-permute-done.22.refs_14_), channel_id=1, source_target_pairs={{0,4},{4,0},{8,12},{12,8},{1,5},{5,1},{9,13},{13,9},{2,6},{6,2},{1... | collective-permute-start | bytes 688136 | tf_op jit(solution)/shard_map/ppermute | solution.py:347
  61.2 8.6 %collective-permute-start.19 = (bf16[64,1792]{1,0:T(8,128)(2,1)S(1)}, bf16[64,1792]{1,0:T(8,128)(2,1)S(1)}, u32[]{:S(2)}, u32[]{:S(2)}) collective-permute-start(bf16[64,1792]{1,0:T(8,128)(2,1)S(1)} %collective-permute-done.17.refs_8_), channel_id=1, source_target_pairs={{0,8},{4,12},{8,0},{12,4},{1,9},{5,13},{9,1},{13,5},{2,10},{6,14},... | collective-permute-start | bytes 688136 | tf_op jit(solution)/shard_map/ppermute | solution.py:351
  62.8 7.5 %collective-permute-start.18 = (bf16[64,1792]{1,0:T(8,128)(2,1)S(1)}, bf16[64,1792]{1,0:T(8,128)(2,1)S(1)}, u32[]{:S(2)}, u32[]{:S(2)}) collective-permute-start(bf16[64,1792]{1,0:T(8,128)(2,1)S(1)} %collective-permute-done.17.refs_8_), channel_id=1, source_target_pairs={{0,4},{4,0},{8,12},{12,8},{1,5},{5,1},{9,13},{13,9},{2,6},{6,2},{1... | collective-permute-start | bytes 688136 | tf_op jit(solution)/shard_map/ppermute | solution.py:347
  63.0 11.6 %collective-permute-start.15 = (bf16[64,1792]{1,0:T(8,128)(2,1)S(1)}, bf16[64,1792]{1,0:T(8,128)(2,1)S(1)}, u32[]{:S(2)}, u32[]{:S(2)}) collective-permute-start(bf16[64,1792]{1,0:T(8,128)(2,1)S(1)} %collective-permute-done.9.refs_4_), channel_id=1, source_target_pairs={{0,8},{4,12},{8,0},{12,4},{1,9},{5,13},{9,1},{13,5},{2,10},{6,14},... | collective-permute-start | bytes 688136 | tf_op jit(solution)/shard_map/ppermute | solution.py:351
  68.2 10.8 %collective-permute-start.12 = (bf16[64,1792]{1,0:T(8,128)(2,1)S(1)}, bf16[64,1792]{1,0:T(8,128)(2,1)S(1)}, u32[]{:S(2)}, u32[]{:S(2)}) collective-permute-start(bf16[64,1792]{1,0:T(8,128)(2,1)S(1)} %collective-permute-done.10.refs_0_), channel_id=1, source_target_pairs={{0,8},{4,12},{8,0},{12,4},{1,9},{5,13},{9,1},{13,5},{2,10},{6,14},... | collective-permute-start | bytes 688136 | tf_op jit(solution)/shard_map/ppermute | solution.py:351
  69.8 9.3 %collective-permute-start.14 = (bf16[64,1792]{1,0:T(8,128)(2,1)S(1)}, bf16[64,1792]{1,0:T(8,128)(2,1)S(1)}, u32[]{:S(2)}, u32[]{:S(2)}) collective-permute-start(bf16[64,1792]{1,0:T(8,128)(2,1)S(1)} %collective-permute-done.9.refs_4_), channel_id=1, source_target_pairs={{0,4},{4,0},{8,12},{12,8},{1,5},{5,1},{9,13},{13,9},{2,6},{6,2},{1... | collective-permute-start | bytes 688136 | tf_op jit(solution)/shard_map/ppermute | solution.py:347
  69.8 9.3 %collective-permute-start.11 = (bf16[64,1792]{1,0:T(8,128)(2,1)S(1)}, bf16[64,1792]{1,0:T(8,128)(2,1)S(1)}, u32[]{:S(2)}, u32[]{:S(2)}) collective-permute-start(bf16[64,1792]{1,0:T(8,128)(2,1)S(1)} %collective-permute-done.10.refs_0_), channel_id=1, source_target_pairs={{0,4},{4,0},{8,12},{12,8},{1,5},{5,1},{9,13},{13,9},{2,6},{6,2},{1... | collective-permute-start | bytes 688136 | tf_op jit(solution)/shard_map/ppermute | solution.py:347
  70.3 8.8 %collective-permute-start.20 = (bf16[64,1792]{1,0:T(8,128)(2,1)S(1)}, bf16[64,1792]{1,0:T(8,128)(2,1)S(1)}, u32[]{:S(2)}, u32[]{:S(2)}) collective-permute-start(bf16[64,1792]{1,0:T(8,128)(2,1)S(1)} %collective-permute-done.19.refs_10_), channel_id=1, source_target_pairs={{0,4},{4,0},{8,12},{12,8},{1,5},{5,1},{9,13},{13,9},{2,6},{6,2},{1... | collective-permute-start | bytes 688136 | tf_op jit(solution)/shard_map/ppermute | solution.py:347
  74.6 4.5 %collective-permute-start.16 = (bf16[64,1792]{1,0:T(8,128)(2,1)S(1)}, bf16[64,1792]{1,0:T(8,128)(2,1)S(1)}, u32[]{:S(2)}, u32[]{:S(2)}) collective-permute-start(bf16[64,1792]{1,0:T(8,128)(2,1)S(1)} %collective-permute-done.15.refs_6_), channel_id=1, source_target_pairs={{0,4},{4,0},{8,12},{12,8},{1,5},{5,1},{9,13},{13,9},{2,6},{6,2},{1... | collective-permute-start | bytes 688136 | tf_op jit(solution)/shard_map/ppermute | solution.py:347
  79.1 1.5 %collective-permute-start.13 = (bf16[64,1792]{1,0:T(8,128)(2,1)S(1)}, bf16[64,1792]{1,0:T(8,128)(2,1)S(1)}, u32[]{:S(2)}, u32[]{:S(2)}) collective-permute-start(bf16[64,1792]{1,0:T(8,128)(2,1)S(1)} %collective-permute-done.12.refs_2_), channel_id=1, source_target_pairs={{0,4},{4,0},{8,12},{12,8},{1,5},{5,1},{9,13},{13,9},{2,6},{6,2},{1... | collective-permute-start | bytes 688136 | tf_op jit(solution)/shard_map/ppermute | solution.py:347
  85.4 36.1 %copy-start.1 = (bf16[256,1792]{1,0:T(8,128)(2,1)S(1)}, bf16[256,1792]{1,0:T(8,128)(2,1)}, u32[]{:S(2)}) copy-start(bf16[256,1792]{1,0:T(8,128)(2,1)} %param.21) | copy-start | bytes 2752516
  88.1 1.9 %collective-permute-start.24 = (bf16[128,1792]{1,0:T(8,128)(2,1)S(1)}, bf16[128,1792]{1,0:T(8,128)(2,1)S(1)}, u32[]{:S(2)}, u32[]{:S(2)}) collective-permute-start(bf16[128,1792]{1,0:T(8,128)(2,1)S(1)} %get-tuple-element.31), channel_id=1, source_target_pairs={{0,4},{4,0},{8,12},{12,8},{1,5},{5,1},{9,13},{13,9},{2,6},{6,2},{1... | collective-permute-start | bytes 1376264 | tf_op jit(solution)/shard_map/ppermute | solution.py:347
  88.3 11.6 %collective-permute-start.27 = (bf16[128,1792]{1,0:T(8,128)(2,1)S(1)}, bf16[128,1792]{1,0:T(8,128)(2,1)S(1)}, u32[]{:S(2)}, u32[]{:S(2)}) collective-permute-start(bf16[128,1792]{1,0:T(8,128)(2,1)S(1)} %get-tuple-element.35), channel_id=1, source_target_pairs={{0,4},{4,0},{8,12},{12,8},{1,5},{5,1},{9,13},{13,9},{2,6},{6,2},{1... | collective-permute-start | bytes 1376264 | tf_op jit(solution)/shard_map/ppermute | solution.py:347
  88.7 13.0 %collective-permute-start.30 = (bf16[128,1792]{1,0:T(8,128)(2,1)S(1)}, bf16[128,1792]{1,0:T(8,128)(2,1)S(1)}, u32[]{:S(2)}, u32[]{:S(2)}) collective-permute-start(bf16[128,1792]{1,0:T(8,128)(2,1)S(1)} %get-tuple-element.39), channel_id=1, source_target_pairs={{0,4},{4,0},{8,12},{12,8},{1,5},{5,1},{9,13},{13,9},{2,6},{6,2},{1... | collective-permute-start | bytes 1376264 | tf_op jit(solution)/shard_map/ppermute | solution.py:347
  90.1 7.7 %collective-permute-start.25 = (bf16[64,1792]{1,0:T(8,128)(2,1)S(1)}, bf16[64,1792]{1,0:T(8,128)(2,1)S(1)}, u32[]{:S(2)}, u32[]{:S(2)}) collective-permute-start(bf16[64,1792]{1,0:T(8,128)(2,1)S(1)} %get-tuple-element.33), channel_id=1, source_target_pairs={{0,8},{4,12},{8,0},{12,4},{1,9},{5,13},{9,1},{13,5},{2,10},{6,14},... | collective-permute-start | bytes 688136 | tf_op jit(solution)/shard_map/ppermute | solution.py:351
  91.7 20.3 %collective-permute-start.33 = (bf16[128,1792]{1,0:T(8,128)(2,1)S(1)}, bf16[128,1792]{1,0:T(8,128)(2,1)S(1)}, u32[]{:S(2)}, u32[]{:S(2)}) collective-permute-start(bf16[128,1792]{1,0:T(8,128)(2,1)S(1)} %get-tuple-element.43), channel_id=1, source_target_pairs={{0,4},{4,0},{8,12},{12,8},{1,5},{5,1},{9,13},{13,9},{2,6},{6,2},{1... | collective-permute-start | bytes 1376264 | tf_op jit(solution)/shard_map/ppermute | solution.py:347
  97.9 7.2 %collective-permute-start.26 = (bf16[64,1792]{1,0:T(8,128)(2,1)S(1)}, bf16[64,1792]{1,0:T(8,128)(2,1)S(1)}, u32[]{:S(2)}, u32[]{:S(2)}) collective-permute-start(bf16[64,1792]{1,0:T(8,128)(2,1)S(1)} %add.64), channel_id=1, source_target_pairs={{0,1},{1,0},{2,3},{3,2},{4,5},{5,4},{6,7},{7,6},{8,9},{9,8},{10,11... | collective-permute-start | bytes 688136 | tf_op jit(solution)/shard_map/ppermute | solution.py:354
  100.1 8.6 %collective-permute-start.28 = (bf16[64,1792]{1,0:T(8,128)(2,1)S(1)}, bf16[64,1792]{1,0:T(8,128)(2,1)S(1)}, u32[]{:S(2)}, u32[]{:S(2)}) collective-permute-start(bf16[64,1792]{1,0:T(8,128)(2,1)S(1)} %get-tuple-element.37), channel_id=1, source_target_pairs={{0,8},{4,12},{8,0},{12,4},{1,9},{5,13},{9,1},{13,5},{2,10},{6,14},... | collective-permute-start | bytes 688136 | tf_op jit(solution)/shard_map/ppermute | solution.py:351
  101.8 9.8 %collective-permute-start.31 = (bf16[64,1792]{1,0:T(8,128)(2,1)S(1)}, bf16[64,1792]{1,0:T(8,128)(2,1)S(1)}, u32[]{:S(2)}, u32[]{:S(2)}) collective-permute-start(bf16[64,1792]{1,0:T(8,128)(2,1)S(1)} %get-tuple-element.41), channel_id=1, source_target_pairs={{0,8},{4,12},{8,0},{12,4},{1,9},{5,13},{9,1},{13,5},{2,10},{6,14},... | collective-permute-start | bytes 688136 | tf_op jit(solution)/shard_map/ppermute | solution.py:351
  108.8 9.6 %collective-permute-start.29 = (bf16[64,1792]{1,0:T(8,128)(2,1)S(1)}, bf16[64,1792]{1,0:T(8,128)(2,1)S(1)}, u32[]{:S(2)}, u32[]{:S(2)}) collective-permute-start(bf16[64,1792]{1,0:T(8,128)(2,1)S(1)} %add.66), channel_id=1, source_target_pairs={{0,2},{1,3},{2,0},{3,1},{4,6},{5,7},{6,4},{7,5},{8,10},{9,11},{10,... | collective-permute-start | bytes 688136 | tf_op jit(solution)/shard_map/ppermute | solution.py:354
  111.6 9.1 %collective-permute-start.32 = (bf16[64,1792]{1,0:T(8,128)(2,1)S(1)}, bf16[64,1792]{1,0:T(8,128)(2,1)S(1)}, u32[]{:S(2)}, u32[]{:S(2)}) collective-permute-start(bf16[64,1792]{1,0:T(8,128)(2,1)S(1)} %add.68), channel_id=1, source_target_pairs={{0,1},{1,0},{2,3},{3,2},{4,5},{5,4},{6,7},{7,6},{8,9},{9,8},{10,11... | collective-permute-start | bytes 688136 | tf_op jit(solution)/shard_map/ppermute | solution.py:354
  112.1 8.6 %collective-permute-start.34 = (bf16[64,1792]{1,0:T(8,128)(2,1)S(1)}, bf16[64,1792]{1,0:T(8,128)(2,1)S(1)}, u32[]{:S(2)}, u32[]{:S(2)}) collective-permute-start(bf16[64,1792]{1,0:T(8,128)(2,1)S(1)} %get-tuple-element.45), channel_id=1, source_target_pairs={{0,8},{4,12},{8,0},{12,4},{1,9},{5,13},{9,1},{13,5},{2,10},{6,14},... | collective-permute-start | bytes 688136 | tf_op jit(solution)/shard_map/ppermute | solution.py:351

commit v9 on v8

--- a/solution.py
+++ b/solution.py
@@ -10,6 +10,7 @@
 score_scale = 1.0 / 192.0**0.5
 norm_epsilon = 1e-06
 MIB = 1 << 20
+light = pl.CostEstimate(flops=1, bytes_accessed=1, transcendentals=0)
 
 
 def in_hbm(value):
@@ -47,14 +48,21 @@
     )(in_hbm(value), *after)
 
 
-def attention_kernel(step_rows, lengths, q_ref, qr_ref, k_ref, kr_ref, up_ref, *refs):
-    out_ref, latent, rope = refs[-3:]
+def attention_kernel(step_rows, parts, lengths, q_ref, qr_ref, k_ref, kr_ref, up_ref, weight_hbm, *refs):
+    out_ref, weight, latent, rope, sems = refs[-5:]
     step = pl.program_id(0)
+    height = weight_hbm.shape[0] // parts
+    copies = []
+    for i in range(parts):
+        cut = pl.ds(i * height, height)
+        copies.append(pltpu.make_async_copy(weight_hbm.at[cut], weight.at[cut], sems.at[i]))
     heads, positions = q_ref.shape[1], k_ref.shape[1]
     rope_width = kr_ref.shape[1]
 
     @pl.when(step == 0)
     def _():
+        for copy in copies:
+            copy.start()
         all_rows = qr_ref.shape[0]
         width = heads * rope_width
         lane = lax.broadcasted_iota(jnp.int32, (heads, width), 1)
@@ -95,6 +103,8 @@
 
     @pl.when(step == pl.num_programs(0) - 1)
     def _():
+        for copy in copies:
+            copy.wait()
         rows = out_ref.shape[0]
         width = up_ref.shape[2]
         for h in range(heads):
@@ -105,16 +115,19 @@
             ).astype(jnp.bfloat16)
 
 
-def attend(query_latent, query_rope, cache_latent, cache_rope, cache_length, value_up, after):
+def attend(query_latent, query_rope, cache_latent, cache_rope, cache_length, value_up, output_weight, after):
     rows, heads, latent_width = query_latent.shape
     positions = cache_latent.shape[1]
     rope_width = cache_rope.shape[1]
     value_width = value_up.shape[2]
-    step_rows = 16
+    step_rows, parts = 16, 4
     by_row = lambda i, lengths: (i, 0, 0)
     return pl.pallas_call(
-        functools.partial(attention_kernel, step_rows),
-        out_shape=jax.ShapeDtypeStruct((rows, heads * value_width), jnp.bfloat16),
+        functools.partial(attention_kernel, step_rows, parts),
+        out_shape=[
+            jax.ShapeDtypeStruct((rows, heads * value_width), jnp.bfloat16),
+            pltpu.VMEM(output_weight.shape, output_weight.dtype),
+        ],
         grid_spec=pltpu.PrefetchScalarGridSpec(
             num_scalar_prefetch=1,
             grid=(rows // step_rows,),
@@ -125,11 +138,15 @@
                 pl.BlockSpec((step_rows, rope_width, positions), by_row),
                 pl.BlockSpec(value_up.shape, lambda i, lengths: (0, 0, 0)),
             ]
-            + [pl.BlockSpec(memory_space=pl.ANY)] * len(after),
-            out_specs=pl.BlockSpec((rows, heads * value_width), lambda i, lengths: (0, 0)),
+            + [pl.BlockSpec(memory_space=pl.ANY)] * (1 + len(after)),
+            out_specs=[
+                pl.BlockSpec((rows, heads * value_width), lambda i, lengths: (0, 0)),
+                pl.BlockSpec(memory_space=pl.ANY),
+            ],
             scratch_shapes=[
                 pltpu.VMEM((latent_width // 128, rows * heads, 128), jnp.float32),
                 pltpu.VMEM((rows * heads, rope_width), jnp.float32),
+                pltpu.SemaphoreType.DMA((parts,)),
             ],
         ),
         cost_estimate=pl.CostEstimate(
@@ -144,47 +161,64 @@
         in_hbm(cache_latent),
         in_hbm(cache_rope),
         in_hbm(value_up),
+        in_hbm(output_weight),
         *after,
     )
 
 
-def projection_kernel(count, out_count, places, *refs):
-    blocks, weight, outs = refs[:count], refs[count], refs[-2 - out_count : -2]
-    gathered, result = refs[-2:]
+def projection_kernel(count, out_count, halves, places, *refs):
+    blocks, weight, residual_hbm = refs[:count], refs[count], refs[count + 1]
+    outs, (gathered, result, residual, sem) = refs[-4 - out_count * halves : -4], refs[-4:]
     height = blocks[0].shape[0]
+    columns = weight.shape[1]
+    out_height = result.shape[0] // out_count
+    half = out_height // halves
+    own = pl.multiple_of(places[count] * out_height, out_height)
+    copy = pltpu.make_async_copy(residual_hbm.at[pl.ds(own, out_height), :], residual, sem)
+    copy.start()
     for k in range(count):
         first = pl.multiple_of(places[k] * height, height)
         gathered[pl.ds(first, height), :] = blocks[k][...]
-    columns = weight.shape[1]
     tile = 256 if columns % 256 == 0 else 128
     for j in range(columns // tile):
         result[:, j * tile : (j + 1) * tile] = jnp.dot(
             gathered[...], weight[:, j * tile : (j + 1) * tile], preferred_element_type=jnp.float32
-        ).astype(jnp.bfloat16)
-    out_height = outs[0].shape[0]
-    for s in range(len(outs)):
-        first = pl.multiple_of(places[count + s] * out_height, out_height)
-        outs[s][...] = result[pl.ds(first, out_height), :]
-
-
-def project(places, blocks, weight, out_count):
+        )
+    copy.wait()
+    for h in range(halves):
+        for s in range(out_count):
+            first = pl.multiple_of(places[count + s] * out_height + h * half, half)
+            part = result[pl.ds(first, half), :]
+            if s == 0:
+                part += residual[h * half : (h + 1) * half, :].astype(jnp.float32)
+            outs[h * out_count + s][...] = part.astype(outs[h * out_count + s].dtype)
+
+
+def project(places, blocks, weight, residual, out_count, halves):
     count = len(blocks)
     height, depth = blocks[0].shape
     rows, columns = height * count, weight.shape[1]
+    half = rows // out_count // halves
     whole = pl.BlockSpec(memory_space=pltpu.VMEM)
-    return pl.pallas_call(
-        functools.partial(projection_kernel, count, out_count),
-        out_shape=[jax.ShapeDtypeStruct((rows // out_count, columns), jnp.bfloat16)] * out_count,
-        in_specs=[pl.BlockSpec(memory_space=pltpu.SMEM)] + [whole] * (count + 1),
-        out_specs=[whole] * out_count,
+    kinds = ([jnp.float32] + [jnp.bfloat16] * (out_count - 1)) * halves
+    outs = pl.pallas_call(
+        functools.partial(projection_kernel, count, out_count, halves),
+        out_shape=[jax.ShapeDtypeStruct((half, columns), kind) for kind in kinds],
+        in_specs=[pl.BlockSpec(memory_space=pltpu.SMEM)]
+        + [whole] * (count + 1)
+        + [pl.BlockSpec(memory_space=pl.ANY)],
+        out_specs=[whole] * len(kinds),
         scratch_shapes=[
             pltpu.VMEM((rows, depth), jnp.bfloat16),
-            pltpu.VMEM((rows, columns), jnp.bfloat16),
+            pltpu.VMEM((rows, columns), jnp.float32),
+            pltpu.VMEM((half * halves, columns), jnp.bfloat16),
+            pltpu.SemaphoreType.DMA,
         ],
-        cost_estimate=pl.CostEstimate(flops=2 * rows * depth * columns, bytes_accessed=4 * MIB, transcendentals=0),
+        cost_estimate=light,
         compiler_params=pltpu.CompilerParams(vmem_limit_bytes=8 * MIB),
         name="projection",
-    )(places, *blocks, in_vmem(weight))
+    )(places, *blocks, in_vmem(weight), in_hbm(residual))
+    return [outs[h * out_count : (h + 1) * out_count] for h in range(halves)]
 
 
 def gate_kernel(row_blocks, column_blocks, model_width, places, *refs):
@@ -237,25 +271,29 @@
             pltpu.VMEM((rows, hidden), jnp.float32),
             pltpu.VMEM((rows, hidden), jnp.float32),
         ],
-        cost_estimate=pl.CostEstimate(
-            flops=4 * rows * gate_weight.size, bytes_accessed=4 * gate_weight.size, transcendentals=rows * hidden
-        ),
+        cost_estimate=light,
         compiler_params=pltpu.CompilerParams(vmem_limit_bytes=2 * rows * (model_width + 4 * hidden) + 4 * MIB),
         name="activate",
     )(places, *[b for row in blocks for b in row], *gains, in_vmem(gate_weight), in_vmem(up_weight), *after)
 
 
-def down_kernel(slots, column_blocks, cores, places, active, row_weight, down, *refs):
-    row_blocks = len(slots)
-    outs = refs[-row_blocks * cores :]
+def down_kernel(groups, half, height, column_blocks, cores, places, active, routed, gates, down, *refs):
+    outs = refs[-len(groups) * cores :]
     width = down.shape[2] // column_blocks
-    height = active.shape[0] // row_blocks
-    order = [b * cores + c for c in reversed(range(cores)) for b in range(column_blocks // cores)]
+    rows = routed.shape[1]
+    chips = column_blocks // cores
+    order = [b * cores + c for c in reversed(range(cores)) for b in range(chips)]
     tile = 256 if width % 256 == 0 else 128
-    weights = []
-    for s in range(row_blocks):
-        first = pl.multiple_of(places[column_blocks + slots[s]] * height, height)
-        weights.append(row_weight[pl.ds(first, height), :])
+    block_rows = rows // sum(len(g) for g in groups)
+    gate = jnp.sum(jnp.where(routed[...] == places[0], gates[...], 0.0), axis=0, keepdims=True)
+    line = lax.broadcasted_iota(jnp.int32, (height, rows), 0)
+    column = lax.broadcasted_iota(jnp.int32, (height, rows), 1)
+    weights, spots = [], []
+    for g, group in enumerate(groups):
+        for at, k in enumerate(group):
+            first = places[column_blocks + k] * block_rows + half * height
+            weights.append(jnp.sum(jnp.where(column == line + first, gate, 0.0), axis=1, keepdims=True))
+            spots.append((g, at * chips))
     for k in order:
         b, c = k // cores, k % cores
         start = pl.multiple_of(places[k] * width, 128)
@@ -264,55 +302,56 @@
             product = jnp.dot(
                 active[...], down[0, :, pl.ds(start + j * tile, tile)], preferred_element_type=jnp.float32
             )
-            for s in range(row_blocks):
+            for s, (g, base) in enumerate(spots):
                 part = product[s * height : (s + 1) * height, :] * weights[s]
-                outs[s * cores + c][b * height : (b + 1) * height, cut] = part.astype(jnp.bfloat16)
-
-
-def project_down(places, active, row_weight, down_weight, slots, column_blocks, cores, after):
-    row_blocks = len(slots)
-    rows, hidden = active.shape
+                outs[g * cores + c][(base + b) * height : (base + b + 1) * height, cut] = part.astype(jnp.bfloat16)
+
+
+def project_down(places, active, routed, gates, down_weight, groups, half, height, column_blocks, cores, after):
     width = down_weight.shape[2] // column_blocks
+    chips = column_blocks // cores
     whole = pl.BlockSpec(memory_space=pltpu.VMEM)
-    out = jax.ShapeDtypeStruct((rows // row_blocks * (column_blocks // cores), width), jnp.bfloat16)
+    kinds = [
+        jax.ShapeDtypeStruct((len(g) * chips * height, width), jnp.bfloat16) for g in groups for _ in range(cores)
+    ]
     outs = pl.pallas_call(
-        functools.partial(down_kernel, slots, column_blocks, cores),
-        out_shape=[out] * (row_blocks * cores),
+        functools.partial(down_kernel, groups, half, height, column_blocks, cores),
+        out_shape=kinds,
         in_specs=[pl.BlockSpec(memory_space=pltpu.SMEM)]
-        + [whole] * 3
+        + [whole] * 4
         + [pl.BlockSpec(memory_space=pl.ANY)] * len(after),
-        out_specs=[whole] * (row_blocks * cores),
-        cost_estimate=pl.CostEstimate(
-            flops=2 * rows * down_weight.size, bytes_accessed=2 * down_weight.size, transcendentals=0
-        ),
+        out_specs=[whole] * len(kinds),
+        cost_estimate=light,
         compiler_params=pltpu.CompilerParams(vmem_limit_bytes=4 * MIB),
         name="down",
-    )(places, active, row_weight, in_vmem(down_weight), *after)
-    return [outs[s * cores : (s + 1) * cores] for s in range(row_blocks)]
-
-
-def add_kernel(groups, *refs):
-    used = sum(len(g) for g in groups)
-    outs = refs[-len(groups) :]
+    )(places, active, routed, gates, in_vmem(down_weight), *after)
+    return [outs[g * cores : (g + 1) * cores] for g in range(len(groups))]
+
+
+def add_kernel(plan, height, *refs):
+    outs = refs[-len(plan) :]
     at = 0
-    for group, out in zip(groups, outs):
-        total = None
-        for first in group:
-            value = refs[at][first : first + out.shape[0], :].astype(jnp.float32)
-            total = value if total is None else total + value
-            at += 1
-        out[...] = total.astype(jnp.bfloat16)
-
-
-def add(groups, height, after=()):
-    values = [value for group in groups for value, _ in group]
+    for pieces, out in zip(plan, outs):
+        for p, piece in enumerate(pieces):
+            total = None
+            for first in piece:
+                value = refs[at][first : first + height, :].astype(jnp.float32)
+                total = value if total is None else total + value
+                at += 1
+            out[p * height : (p + 1) * height, :] = total.astype(jnp.bfloat16)
+
+
+def add(outputs, height, after=()):
+    values = [value for pieces in outputs for piece in pieces for value, _ in piece]
     width = values[0].shape[1]
     whole = pl.BlockSpec(memory_space=pltpu.VMEM)
+    plan = [[[first for _, first in piece] for piece in pieces] for pieces in outputs]
     return pl.pallas_call(
-        functools.partial(add_kernel, [[first for _, first in group] for group in groups]),
-        out_shape=[jax.ShapeDtypeStruct((height, width), jnp.bfloat16)] * len(groups),
+        functools.partial(add_kernel, plan, height),
+        out_shape=[jax.ShapeDtypeStruct((height * len(pieces), width), jnp.bfloat16) for pieces in outputs],
         in_specs=[whole] * len(values) + [pl.BlockSpec(memory_space=pl.ANY)] * len(after),
-        out_specs=[whole] * len(groups),
+        out_specs=[whole] * len(outputs),
+        cost_estimate=light,
         compiler_params=pltpu.CompilerParams(vmem_limit_bytes=8 * MIB),
         name="add",
     )(*values, *after)
@@ -353,6 +392,13 @@
     def from_tp(value, bits):
         return lax.ppermute(value, "tp", [(i, i ^ bits) for i in range(tp_count)])
 
+    def spread_tp(value):
+        rows = [value]
+        for k in range(1, tp_count):
+            low = k & -k
+            rows.append(from_tp(rows[k ^ low], low))
+        return rows
+
     def gather_ep(value):
         same = [value] + [from_chip(value, b) for b in range(1, chips)]
         other = [from_core(v) for v in same]
@@ -367,53 +413,97 @@
     tp_places = [tp_index ^ k for k in range(tp_count)]
     places = jnp.stack(ep_places + tp_places).astype(jnp.int32)
 
+    halves = 2
+    half_rows = block_rows // halves
     gain = norm_gain.reshape(1, -1)
     gains = gather_ep(gain)
-    own_residual = lax.dynamic_slice_in_dim(residual, tp_index * block_rows, block_rows, 0)
-    row_weight = jnp.sum(jnp.where(routed_experts == ep_index, expert_gates, 0.0), axis=-1, keepdims=True)
-
-    head_out = attend(query_latent, query_rope, cache_latent, cache_rope, cache_length, value_up, [places])
-    output_weight = fetch(output_weight, [head_out, row_weight, own_residual, gain])
-    partial = project(places, gather_ep(head_out), output_weight, tp_count)
-
-    gate_weight = fetch(gate_weight, [partial[0]])
-    terms = [[(value, 0)] for value in partial]
-    for k in reversed(range(1, tp_count)):
-        total = terms[k][0][0]
-        if len(terms[k]) > 1 or k == 1:
-            (total,) = add([terms[k]], block_rows, [gate_weight] if k == 1 else [])
+    routed, gates = routed_experts.T, expert_gates.T
+
+    head_out, output_weight = attend(
+        query_latent,
+        query_rope,
+        cache_latent,
+        cache_rope,
+        cache_length,
+        value_up,
+        output_weight,
+        [places, gain],
+    )
+    partial = project(places, gather_ep(head_out), output_weight, residual, tp_count, halves)
+
+    gate_weight = fetch(gate_weight, [partial[0][0]])
+    terms = [[[(value, 0)] for value in partial[h]] for h in range(halves)]
+    first_arrival, second_sum = None, None
+    streams, rows_of, blocks = [], [], []
+
+    def send_back(h, k, after):
+        total = terms[h][k][0][0]
+        if len(terms[h][k]) > 1 or after:
+            (total,) = add([[terms[h][k]]], half_rows, after)
         low = k & -k
         arrived = from_tp(total, low)
-        terms[k ^ low].append((arrived, 0))
-    up_weight = fetch(up_weight, [total])
-    down_weight = fetch(down_weight, [total])
-    stream_terms = terms[0] + [(own_residual, 0)]
-    stream, stream_out = add([stream_terms, stream_terms], block_rows, gains + [gate_weight, up_weight, down_weight])
-
-    rows_of = {0: stream}
-    for k in range(1, tp_count):
-        low = k & -k
-        rows_of[k] = from_tp(rows_of[k ^ low], low)
-    blocks = [gather_ep(rows_of[k]) for k in range(tp_count)]
+        terms[h][k ^ low].append((arrived, 0))
+        return total, arrived
+
+    last = tp_count - 1
+    _, first_arrival = send_back(0, last, [])
+    totals = [send_back(0, k, [gate_weight] if k == 1 else []) for k in reversed(range(1, last))]
+    up_weight = fetch(up_weight, [totals[0][0]])
+    _, late_arrival = send_back(1, last, [totals[0][0]])
+    (stream,) = add([[terms[0][0]]], half_rows, [up_weight, *gains])
+    streams.append(stream)
+    rows_of.append(spread_tp(stream))
+    late = [send_back(1, k, [stream]) for k in reversed(range(1, last))]
+    down_weight = fetch(down_weight, [stream])
+    (stream,) = add([[terms[1][0]]], half_rows, [rows_of[0][tp_count // 2], down_weight])
+    streams.append(stream)
+    rows_of.append(spread_tp(stream))
+    blocks = [[gather_ep(rows) for rows in rows_of[h]] for h in range(halves)]
 
     slots = list(reversed(range(tp_count)))
-    active = activate(places, [blocks[k] for k in slots], gains, gate_weight, up_weight, [])
-    outs = project_down(places, active, row_weight, down_weight, slots, ep_count, cores, [])
-    swapped = [from_core(out[1]) for out in outs]
-    terms = [[] for _ in range(tp_count)]
-    arrivals = []
-    for at, k in enumerate(slots):
-        before = arrivals[0] if len(arrivals) == 1 else arrivals[-2] if arrivals else []
-        pair = [[(outs[at][0], c * block_rows), (swapped[at], c * block_rows)] for c in range(chips)]
-        sums = add(pair, block_rows, before)
-        across = [from_chip(sums[c], chips - c) for c in range(1, chips)]
-        arrivals.append(across)
-        terms[k] += [(value, 0) for value in [sums[0]] + across]
-        if k:
-            (total,) = add([terms[k]], block_rows)
-            low = k & -k
-            terms[k ^ low].append((from_tp(total, low), 0))
-    (mixed,) = add([terms[0]], block_rows)
+    groups = [slots[i : i + 2] for i in range(0, tp_count, 2)]
+    terms = [[[] for _ in range(tp_count)] for _ in range(halves)]
+
+    def run_expert(h, hold_gate, hold_down):
+        active = activate(places, [blocks[h][k] for k in slots], gains, gate_weight, up_weight, hold_gate)
+        outs = project_down(
+            places, active, routed, gates, down_weight, groups, h, half_rows, ep_count, cores, hold_down
+        )
+        return outs, [from_core(out[1]) for out in outs]
+
+    def add_cores(h, g, outs, swapped, after):
+        def rows(at, b):
+            first = (at * chips + b) * half_rows
+            return [(outs[g][0], first), (swapped[g], first)]
+
+        count = len(groups[g])
+        return add([[rows(at, b) for at in range(count)] for b in range(chips)], half_rows, after)
+
+    def cross(h, g, sums):
+        across = [from_chip(sums[b], chips - b) for b in range(1, chips)]
+        for at, k in enumerate(groups[g]):
+            terms[h][k] += [(value, at * half_rows) for value in [sums[0]] + across]
+        return across
+
+    late_rows = [rows_of[1][last]] + [blocks[1][k][-2] for k in range(last)]
+    outs, swapped = run_expert(0, late_rows, blocks[1][last][-2:-1])
+    sums = add_cores(0, 0, outs, swapped, [])
+    across = cross(0, 0, sums)
+    sent = {last: send_back(0, last, [])}
+    rest = [add_cores(0, g, outs, swapped, across) for g in range(1, len(groups))]
+    late_outs, late_swapped = run_expert(1, sums[-1:], sent[last][:1] + rest[0][-1:])
+    for g in range(1, len(groups)):
+        across = cross(0, g, rest[g - 1])
+    across = cross(1, 0, add_cores(1, 0, late_outs, late_swapped, across + [sent[last][1]]))
+    for k in reversed(range(1, last)):
+        sent[k] = send_back(0, k, [])
+    early = [sent[k][0] for k in range(1, last)]
+    for g in range(1, len(groups)):
+        across = cross(1, g, add_cores(1, g, late_outs, late_swapped, across + early))
+    for k in reversed(range(1, tp_count)):
+        send_back(1, k, [sent[k][1]])
+    (mixed,) = add([[terms[h][0] for h in range(halves)]], half_rows)
+    (stream_out,) = add([[[(stream, 0)] for stream in streams]], half_rows)
     return (stream_out, mixed)
 
 

time: 122 us -> 132 us (1.082)
  starting transfers between devices: 29.3 us -> 46.4 us
  waiting for transfers between devices: 53.8 us -> 46.3 us
    ppermute x9 -> x18, starting transfers between devices: 12.7 us -> 22.1 us  [from_tp(): return lax.ppermute(value, 'tp', [(i, i ^ bits) for i in range(tp_count)])]
    ppermute x10 -> x14, waiting for transfers between devices: 25.6 us -> 19.5 us  [from_chip(): lax.ppermute(value, 'ep', [(i, (i + step) % ep_count) for i in range(ep_c...]
    ppermute x10 -> x14, starting transfers between devices: 15.1 us -> 20.7 us  [from_chip(): lax.ppermute(value, 'ep', [(i, (i + step) % ep_count) for i in range(ep_c...]
    ppermute x9 -> x18, waiting for transfers between devices: 25.5 us -> 22.6 us  [from_tp(): return lax.ppermute(value, 'tp', [(i, i ^ bits) for i in range(tp_count)])]
    ppermute x16 -> x24, starting transfers between devices: 1.47 us -> 3.59 us  [from_core(): return lax.ppermute(value, 'ep', [(i, i ^ 1) for i in range(ep_count)])]
    pallas_call x4 -> x3, Pallas kernels: 11.6 us -> 9.56 us  [fetch(): pl.pallas_call(functools.partial(fetch_kernel, parts), out_shape=pltpu.VM...]
    pallas_call x14 -> x23, Pallas kernels: 20 us -> 21.7 us  [the longest x1 13.2 us: attend(): pl.pallas_call(functools.partial(attention_kernel, step_rows, parts), out...]
    ppermute x16 -> x24, waiting for transfers between devices: 2.66 us -> 4.18 us  [from_core(): return lax.ppermute(value, 'ep', [(i, i ^ 1) for i in range(ep_count)])]
  transfers between devices with their start and end apart: 35 -> 56, of which waited for: 16 -> 25; matrix products, arithmetic and copies ran while one was open for 0% -> 0% of each run, Pallas kernels for 10% -> 13%
where the time goes in v9:
time: 132 us
  starting transfers between devices  46.4 us (35%)
  waiting for transfers between devices  46.3 us (35%)
  Pallas kernels  37 us (28%)
  local copies, waits for them, and re-layouts  1.46 us (1%)
    ppermute x18, waiting for transfers between devices, from_tp(): return lax.ppermute(value, 'tp', [(i, i ^ bits) for i in range(tp_count)])  22.6 us
    ppermute x18, starting transfers between devices, from_tp(): return lax.ppermute(value, 'tp', [(i, i ^ bits) for i in range(tp_count)])  22.1 us
    ppermute x14, starting transfers between devices, from_chip(): lax.ppermute(value, 'ep', [(i, (i + step) % ep_count) for i in range(ep_c...  20.7 us
    ppermute x14, waiting for transfers between devices, from_chip(): lax.ppermute(value, 'ep', [(i, (i + step) % ep_count) for i in range(ep_c...  19.5 us
    pallas_call x1, Pallas kernels, attend(): pl.pallas_call(functools.partial(attention_kernel, step_rows, parts), out...  13.2 us
    pallas_call x3, Pallas kernels, fetch(): pl.pallas_call(functools.partial(fetch_kernel, parts), out_shape=pltpu.VM...  9.56 us
    pallas_call x2, Pallas kernels, activate(): pl.pallas_call(functools.partial(gate_kernel, row_blocks, column_blocks,...  5.73 us
    ppermute x24, waiting for transfers between devices, from_core(): return lax.ppermute(value, 'ep', [(i, i ^ 1) for i in range(ep_count)])  4.18 us
  transfers between devices with their start and end apart: 56, of which 25 were waited for; matrix products, arithmetic and copies ran while one was open for 0% of the time, Pallas kernels for 13%

profile of v9, /device:TPU:0, one launch (start us, length us, event | category | flops | bytes accessed | tf_op | source)
XLA Modules:
  0.0 132.1 jit_solution(14917167492696710409)
XLA Ops:
  2.1 13.2 %attention.1 = (bf16[64,1024]{1,0:T(8,128)(2,1)S(1)}, bf16[1024,1792]{1,0:T(8,128)(2,1)S(1)}) custom-call(s32[64]{0:T(128)S(1)} %copy-done.2, bf16[64,8,512]{2,1,0:T(8,128)(2,1)} %q_ref.1, bf16[64,512]{1,0:T(8,128)(2,1)} %qr_ref.1, bf16[64,256,512]{2,1,0:T(8,128)(2,1)} %k_ref.1, bf16[64,64,256]{2,1,0:T(8,128)(2,1)} %kr_ref.1, bf16[8,512,128]{2,1,0:T(8,128)(2,1)} %up_ref.1, ...), custom_call_target="tpu_custom_call" | custom-call | flops 4294967296 | bytes 16777216 | tf_op jit(solution)/shard_map/attention/pallas_call | solution.py:125
  15.4 3.0 %collective-permute-start.1 = (bf16[64,1024]{1,0:T(8,128)(2,1)S(1)}, bf16[64,1024]{1,0:T(8,128)(2,1)S(1)}, u32[]{:S(2)}, u32[]{:S(2)}) collective-permute-start(bf16[64,1024]{1,0:T(8,128)(2,1)S(1)} %get-tuple-element.28.refs_0_), channel_id=1, source_target_pairs={{0,8},{4,12},{8,0},{12,4},{1,9},{5,13},{9,1},{13,5},{2,10},{6,14},... | collective-permute-start | bytes 393224 | tf_op jit(solution)/shard_map/ppermute | solution.py:390
  18.4 3.5 %collective-permute-done.1.refs_2_ = bf16[64,1024]{1,0:T(8,128)(2,1)S(1)} collective-permute-done((bf16[64,1024]{1,0:T(8,128)(2,1)S(1)}, bf16[64,1024]{1,0:T(8,128)(2,1)S(1)}, u32[]{:S(2)}, u32[]{:S(2)}) %collective-permute-start.1) | collective-permute-done | bytes 131104 | tf_op jit(solution)/shard_map/ppermute | solution.py:390
  21.9 1.3 %collective-permute-done.2.refs_3_ = bf16[64,1024]{1,0:T(8,128)(2,1)S(1)} collective-permute-done((bf16[64,1024]{1,0:T(8,128)(2,1)S(1)}, bf16[64,1024]{1,0:T(8,128)(2,1)S(1)}, u32[]{:S(2)}, u32[]{:S(2)}) %collective-permute-start.2) | collective-permute-done | bytes 131104 | tf_op jit(solution)/shard_map/ppermute | solution.py:386
  23.2 2.5 %projection.1 = (f32[32,1792]{1,0:T(8,128)S(1)}, bf16[32,1792]{1,0:T(8,128)(2,1)S(1)}, bf16[32,1792]{1,0:T(8,128)(2,1)S(1)}, bf16[32,1792]{1,0:T(8,128)(2,1)S(1)...) custom-call(s32[8]{0:T(128)S(1)} %stack.35.refs_0_.places, ...), custom_call_target="tpu_custom_call" | custom-call | flops 1 | bytes 1 | tf_op jit(solution)/shard_map/projection/pallas_call | solution.py:204
  25.7 1.9 %collective-permute-start.3 = (bf16[32,1792]{1,0:T(8,128)(2,1)S(1)}, bf16[32,1792]{1,0:T(8,128)(2,1)S(1)}, u32[]{:S(2)}, u32[]{:S(2)}) collective-permute-start(bf16[32,1792]{1,0:T(8,128)(2,1)S(1)} %get-tuple-element.32), channel_id=1, source_target_pairs={{0,1},{1,0},{2,3},{3,2},{4,5},{5,4},{6,7},{7,6},{8,9},{9,8},{10,11... | collective-permute-start | bytes 344072 | tf_op jit(solution)/shard_map/ppermute | solution.py:393
  27.6 3.2 %fetch.3.refs_1_.refs_20_ = bf16[1,7168,512]{2,1,0:T(8,128)(2,1)S(1)} custom-call(bf16[1,7168,512]{2,1,0:T(8,128)(2,1)} %refs_0_.3, f32[32,1792]{1,0:T(8,128)S(1)} %get-tuple-element.30.refs_1_.refs_0_), custom_call_target="tpu_custom_call" | custom-call | bytes 14680064 | tf_op jit(solution)/shard_map/fetch/pallas_call | solution.py:39
  31.1 2.9 %collective-permute-start.4 = (bf16[32,1792]{1,0:T(8,128)(2,1)S(1)}, bf16[32,1792]{1,0:T(8,128)(2,1)S(1)}, u32[]{:S(2)}, u32[]{:S(2)}) collective-permute-start(bf16[32,1792]{1,0:T(8,128)(2,1)S(1)} %add.64.refs_1_), channel_id=1, source_target_pairs={{0,2},{1,3},{2,0},{3,1},{4,6},{5,7},{6,4},{7,5},{8,10},{9,11},{10,... | collective-permute-start | bytes 344072 | tf_op jit(solution)/shard_map/ppermute | solution.py:393
  34.1 1.6 %collective-permute-start.9 = (bf16[32,1792]{1,0:T(8,128)(2,1)S(1)}, bf16[32,1792]{1,0:T(8,128)(2,1)S(1)}, u32[]{:S(2)}, u32[]{:S(2)}) collective-permute-start(bf16[32,1792]{1,0:T(8,128)(2,1)S(1)} %add.67), channel_id=1, source_target_pairs={{0,1},{1,0},{2,3},{3,2},{4,5},{5,4},{6,7},{7,6},{8,9},{9,8},{10,11... | collective-permute-start | bytes 344072 | tf_op jit(solution)/shard_map/ppermute | solution.py:393
  35.7 1.5 %collective-permute-start.7 = (f32[1,1792]{1,0:T(1,128)S(1)}, f32[1,1792]{1,0:T(1,128)S(1)}, u32[]{:S(2)}, u32[]{:S(2)}) collective-permute-start(f32[1,1792]{1,0:T(1,128)S(1)} %reshape.7.refs_1_.refs_4_.refs_16_), channel_id=1, source_target_pairs={{0,8},{4,12},{8,0},{12,4},{1,9},{5,13},{9,1},{13,5},{2,10},{6,14},... | collective-permute-start | bytes 21512 | tf_op jit(solution)/shard_map/ppermute | solution.py:390
  37.2 2.1 %collective-permute-done.7.refs_6_.refs_18_ = f32[1,1792]{1,0:T(1,128)S(1)} collective-permute-done((f32[1,1792]{1,0:T(1,128)S(1)}, f32[1,1792]{1,0:T(1,128)S(1)}, u32[]{:S(2)}, u32[]{:S(2)}) %collective-permute-start.7) | collective-permute-done | bytes 7200 | tf_op jit(solution)/shard_map/ppermute | solution.py:390
  39.3 3.2 %fetch.4.refs_3_.refs_21_ = bf16[1,7168,512]{2,1,0:T(8,128)(2,1)S(1)} custom-call(bf16[1,7168,512]{2,1,0:T(8,128)(2,1)} %refs_0_.4, bf16[32,1792]{1,0:T(8,128)(2,1)S(1)} %add.64.refs_1_), custom_call_target="tpu_custom_call" | custom-call | bytes 14680064 | tf_op jit(solution)/shard_map/fetch/pallas_call | solution.py:39
  43.8 2.4 %collective-permute-start.12 = (bf16[32,1792]{1,0:T(8,128)(2,1)S(1)}, bf16[32,1792]{1,0:T(8,128)(2,1)S(1)}, u32[]{:S(2)}, u32[]{:S(2)}) collective-permute-start(bf16[32,1792]{1,0:T(8,128)(2,1)S(1)} %add.66.refs_2_.refs_1_.refs_0_.refs_12_), channel_id=1, source_target_pairs={{0,2},{1,3},{2,0},{3,1},{4,6},{5,7},{6,4},{7,5},{8,10},{9,11},{10,... | collective-permute-start | bytes 344072 | tf_op jit(solution)/shard_map/ppermute | solution.py:393
  46.2 1.6 %collective-permute-start.20 = (bf16[32,1792]{1,0:T(8,128)(2,1)S(1)}, bf16[32,1792]{1,0:T(8,128)(2,1)S(1)}, u32[]{:S(2)}, u32[]{:S(2)}) collective-permute-start(bf16[32,1792]{1,0:T(8,128)(2,1)S(1)} %add.66.refs_2_.refs_1_.refs_0_.refs_12_), channel_id=1, source_target_pairs={{0,1},{1,0},{2,3},{3,2},{4,5},{5,4},{6,7},{7,6},{8,9},{9,8},{10,11... | collective-permute-start | bytes 344072 | tf_op jit(solution)/shard_map/ppermute | solution.py:393
  47.8 1.5 %collective-permute-start.25 = (bf16[32,1792]{1,0:T(8,128)(2,1)S(1)}, bf16[32,1792]{1,0:T(8,128)(2,1)S(1)}, u32[]{:S(2)}, u32[]{:S(2)}) collective-permute-start(bf16[32,1792]{1,0:T(8,128)(2,1)S(1)} %add.66.refs_2_.refs_1_.refs_0_.refs_12_), channel_id=1, source_target_pairs={{0,8},{4,12},{8,0},{12,4},{1,9},{5,13},{9,1},{13,5},{2,10},{6,14},... | collective-permute-start | bytes 344072 | tf_op jit(solution)/shard_map/ppermute | solution.py:390
  49.3 3.2 %fetch.5.refs_4_.down = bf16[1,512,7168]{2,1,0:T(8,128)(2,1)S(1)} custom-call(bf16[1,512,7168]{2,1,0:T(8,128)(2,1)} %refs_0_.5, bf16[32,1792]{1,0:T(8,128)(2,1)S(1)} %add.66.refs_2_.refs_1_.refs_0_.refs_12_), custom_call_target="tpu_custom_call" | custom-call | bytes 14680064 | tf_op jit(solution)/shard_map/fetch/pallas_call | solution.py:39
  52.5 2.6 %collective-permute-done.10.refs_1_ = bf16[32,1792]{1,0:T(8,128)(2,1)S(1)} collective-permute-done((bf16[32,1792]{1,0:T(8,128)(2,1)S(1)}, bf16[32,1792]{1,0:T(8,128)(2,1)S(1)}, u32[]{:S(2)}, u32[]{:S(2)}) %collective-permute-start.10) | collective-permute-done | bytes 114720 | tf_op jit(solution)/shard_map/ppermute | solution.py:393
  55.1 1.8 %collective-permute-done.12.refs_3_.refs_4_ = bf16[32,1792]{1,0:T(8,128)(2,1)S(1)} collective-permute-done((bf16[32,1792]{1,0:T(8,128)(2,1)S(1)}, bf16[32,1792]{1,0:T(8,128)(2,1)S(1)}, u32[]{:S(2)}, u32[]{:S(2)}) %collective-permute-start.12) | collective-permute-done | bytes 114720 | tf_op jit(solution)/shard_map/ppermute | solution.py:393
  57.0 1.8 %collective-permute-start.30 = (bf16[32,1792]{1,0:T(8,128)(2,1)S(1)}, bf16[32,1792]{1,0:T(8,128)(2,1)S(1)}, u32[]{:S(2)}, u32[]{:S(2)}) collective-permute-start(bf16[32,1792]{1,0:T(8,128)(2,1)S(1)} %add.70.refs_1_.refs_12_), channel_id=1, source_target_pairs={{0,1},{1,0},{2,3},{3,2},{4,5},{5,4},{6,7},{7,6},{8,9},{9,8},{10,11... | collective-permute-start | bytes 344072 | tf_op jit(solution)/shard_map/ppermute | solution.py:393
  58.9 1.5 %collective-permute-start.29 = (bf16[32,1792]{1,0:T(8,128)(2,1)S(1)}, bf16[32,1792]{1,0:T(8,128)(2,1)S(1)}, u32[]{:S(2)}, u32[]{:S(2)}) collective-permute-start(bf16[32,1792]{1,0:T(8,128)(2,1)S(1)} %add.70.refs_1_.refs_12_), channel_id=1, source_target_pairs={{0,8},{4,12},{8,0},{12,4},{1,9},{5,13},{9,1},{13,5},{2,10},{6,14},... | collective-permute-start | bytes 344072 | tf_op jit(solution)/shard_map/ppermute | solution.py:390
  61.1 2.8 %collective-permute-done.27.refs_4_ = bf16[32,1792]{1,0:T(8,128)(2,1)S(1)} collective-permute-done((bf16[32,1792]{1,0:T(8,128)(2,1)S(1)}, bf16[32,1792]{1,0:T(8,128)(2,1)S(1)}, u32[]{:S(2)}, u32[]{:S(2)}) %collective-permute-start.27) | collective-permute-done | bytes 114720 | tf_op jit(solution)/shard_map/ppermute | solution.py:393
  64.0 1.5 %collective-permute-start.22 = (bf16[32,1792]{1,0:T(8,128)(2,1)S(1)}, bf16[32,1792]{1,0:T(8,128)(2,1)S(1)}, u32[]{:S(2)}, u32[]{:S(2)}) collective-permute-start(bf16[32,1792]{1,0:T(8,128)(2,1)S(1)} %collective-permute-done.20.refs_8_), channel_id=1, source_target_pairs={{0,8},{4,12},{8,0},{12,4},{1,9},{5,13},{9,1},{13,5},{2,10},{6,14},... | collective-permute-start | bytes 344072 | tf_op jit(solution)/shard_map/ppermute | solution.py:390
  66.7 1.6 %collective-permute-start.28 = (bf16[32,1792]{1,0:T(8,128)(2,1)S(1)}, bf16[32,1792]{1,0:T(8,128)(2,1)S(1)}, u32[]{:S(2)}, u32[]{:S(2)}) collective-permute-start(bf16[32,1792]{1,0:T(8,128)(2,1)S(1)} %collective-permute-done.27.refs_4_), channel_id=1, source_target_pairs={{0,1},{1,0},{2,3},{3,2},{4,5},{5,4},{6,7},{7,6},{8,9},{9,8},{10,11... | collective-permute-start | bytes 344072 | tf_op jit(solution)/shard_map/ppermute | solution.py:393
  68.9 1.5 %collective-permute-start.31 = (bf16[32,1792]{1,0:T(8,128)(2,1)S(1)}, bf16[32,1792]{1,0:T(8,128)(2,1)S(1)}, u32[]{:S(2)}, u32[]{:S(2)}) collective-permute-start(bf16[32,1792]{1,0:T(8,128)(2,1)S(1)} %collective-permute-done.30.refs_8_), channel_id=1, source_target_pairs={{0,8},{4,12},{8,0},{12,4},{1,9},{5,13},{9,1},{13,5},{2,10},{6,14},... | collective-permute-start | bytes 344072 | tf_op jit(solution)/shard_map/ppermute | solution.py:390
  70.9 1.5 %collective-permute-start.32 = (bf16[32,1792]{1,0:T(8,128)(2,1)S(1)}, bf16[32,1792]{1,0:T(8,128)(2,1)S(1)}, u32[]{:S(2)}, u32[]{:S(2)}) collective-permute-start(bf16[32,1792]{1,0:T(8,128)(2,1)S(1)} %collective-permute-done.27.refs_4_), channel_id=1, source_target_pairs={{0,8},{4,12},{8,0},{12,4},{1,9},{5,13},{9,1},{13,5},{2,10},{6,14},... | collective-permute-start | bytes 344072 | tf_op jit(solution)/shard_map/ppermute | solution.py:390
  72.9 2.0 %collective-permute-done.31.refs_24_.refs_10_ = bf16[32,1792]{1,0:T(8,128)(2,1)S(1)} collective-permute-done((bf16[32,1792]{1,0:T(8,128)(2,1)S(1)}, bf16[32,1792]{1,0:T(8,128)(2,1)S(1)}, u32[]{:S(2)}, u32[]{:S(2)}) %collective-permute-start.31) | collective-permute-done | bytes 114720 | tf_op jit(solution)/shard_map/ppermute | solution.py:390
  75.0 1.7 %collective-permute-done.15.refs_2_ = bf16[32,1792]{1,0:T(8,128)(2,1)S(1)} collective-permute-done((bf16[32,1792]{1,0:T(8,128)(2,1)S(1)}, bf16[32,1792]{1,0:T(8,128)(2,1)S(1)}, u32[]{:S(2)}, u32[]{:S(2)}) %collective-permute-start.15) | collective-permute-done | bytes 114720 | tf_op jit(solution)/shard_map/ppermute | solution.py:390
  76.6 1.2 collective-permute-done.32.refs_25_.refs_6_
  77.9 1.5 %collective-permute-start.33 = (bf16[32,1792]{1,0:T(8,128)(2,1)S(1)}, bf16[32,1792]{1,0:T(8,128)(2,1)S(1)}, u32[]{:S(2)}, u32[]{:S(2)}) collective-permute-start(bf16[32,1792]{1,0:T(8,128)(2,1)S(1)} %collective-permute-done.28.refs_22_.refs_0_), channel_id=1, source_target_pairs={{0,8},{4,12},{8,0},{12,4},{1,9},{5,13},{9,1},{13,5},{2,10},{6,14},... | collective-permute-start | bytes 344072 | tf_op jit(solution)/shard_map/ppermute | solution.py:390
  79.4 2.9 %activate.2.active = bf16[128,512]{1,0:T(8,128)(2,1)S(1)} custom-call(s32[8]{0:T(128)S(1)} %stack.35.refs_0_.places, bf16[32,1792]{1,0:T(8,128)(2,1)S(1)} %collective-permute-done.13.refs_0_, bf16[32,1792]{1,0:T(8,128)(2,1)S(1)} %collective-permute-done.14.refs_1_, bf16[32,1792]{1,0:T(8,128)(2,1)S(1)} %collective-permute-done.15.refs_2_, ...), custom_call_target="tpu_custom_call" | custom-call | flops 1 | bytes 1 | tf_op jit(solution)/shard_map/activate/pallas_call | solution.py:262
  82.7 1.8 %down.2 = (bf16[128,1792]{1,0:T(8,128)(2,1)S(1)}, bf16[128,1792]{1,0:T(8,128)(2,1)S(1)}, bf16[128,1792]{1,0:T(8,128)(2,1)S(1)}, bf16[128,1792]{1,0:T(8,128)(2,1)S(1)}) custom-call(s32[8]{0:T(128)S(1)} %stack.35.refs_0_.places, bf16[128,512]{1,0:T(8,128)(2,1)S(1)} %activate.2.active, s32[2,256]{1,0:T(2,128)S(1)} %bitcast.10, f32[2,256]{1,0:T(2,128)S(1)} %bitcast.12, ...), custom_call_target="tpu_custom_call" | custom-call | flops 1 | bytes 1 | tf_op jit(solution)/shard_map/down/pallas_call | solution.py:317
  85.6 1.5 %collective-permute-done.47.refs_13_ = bf16[32,1792]{1,0:T(8,128)(2,1)S(1)} collective-permute-done((bf16[32,1792]{1,0:T(8,128)(2,1)S(1)}, bf16[32,1792]{1,0:T(8,128)(2,1)S(1)}, u32[]{:S(2)}, u32[]{:S(2)}) %collective-permute-start.47) | collective-permute-done | bytes 114720 | tf_op jit(solution)/shard_map/ppermute | solution.py:386
  87.8 1.5 %collective-permute-start.36 = (bf16[64,1792]{1,0:T(8,128)(2,1)S(1)}, bf16[64,1792]{1,0:T(8,128)(2,1)S(1)}, u32[]{:S(2)}, u32[]{:S(2)}) collective-permute-start(bf16[64,1792]{1,0:T(8,128)(2,1)S(1)} %get-tuple-element.42.refs_22_), channel_id=1, source_target_pairs={{0,8},{4,12},{8,0},{12,4},{1,9},{5,13},{9,1},{13,5},{2,10},{6,14},... | collective-permute-start | bytes 688136 | tf_op jit(solution)/shard_map/ppermute | solution.py:390
  91.2 2.9 %activate.3.active = bf16[128,512]{1,0:T(8,128)(2,1)S(1)} custom-call(s32[8]{0:T(128)S(1)} %stack.35.refs_0_.places, bf16[32,1792]{1,0:T(8,128)(2,1)S(1)} %collective-permute-done.28.refs_22_.refs_0_, bf16[32,1792]{1,0:T(8,128)(2,1)S(1)} %collective-permute-done.41.refs_1_, bf16[32,1792]{1,0:T(8,128)(2,1)S(1)} %collective-permute-done.33.refs_0_.refs_2_, ...), custom_call_target="tpu_custom_call" | custom-call | flops 1 | bytes 1 | tf_op jit(solution)/shard_map/activate/pallas_call | solution.py:262
  94.0 1.4 %collective-permute-done.36.refs_8_.refs_1_ = bf16[64,1792]{1,0:T(8,128)(2,1)S(1)} collective-permute-done((bf16[64,1792]{1,0:T(8,128)(2,1)S(1)}, bf16[64,1792]{1,0:T(8,128)(2,1)S(1)}, u32[]{:S(2)}, u32[]{:S(2)}) %collective-permute-start.36) | collective-permute-done | bytes 229408 | tf_op jit(solution)/shard_map/ppermute | solution.py:390
  95.7 1.8 %down.3 = (bf16[128,1792]{1,0:T(8,128)(2,1)S(1)}, bf16[128,1792]{1,0:T(8,128)(2,1)S(1)}, bf16[128,1792]{1,0:T(8,128)(2,1)S(1)}, bf16[128,1792]{1,0:T(8,128)(2,1)S(1)}) custom-call(s32[8]{0:T(128)S(1)} %stack.35.refs_0_.places, bf16[128,512]{1,0:T(8,128)(2,1)S(1)} %activate.3.active, s32[2,256]{1,0:T(2,128)S(1)} %bitcast.11, f32[2,256]{1,0:T(2,128)S(1)} %bitcast.13, ...), custom_call_target="tpu_custom_call" | custom-call | flops 1 | bytes 1 | tf_op jit(solution)/shard_map/down/pallas_call | solution.py:317
  97.5 1.5 %collective-permute-start.37 = (bf16[64,1792]{1,0:T(8,128)(2,1)S(1)}, bf16[64,1792]{1,0:T(8,128)(2,1)S(1)}, u32[]{:S(2)}, u32[]{:S(2)}) collective-permute-start(bf16[64,1792]{1,0:T(8,128)(2,1)S(1)} %get-tuple-element.44.refs_1_), channel_id=1, source_target_pairs={{0,8},{4,12},{8,0},{12,4},{1,9},{5,13},{9,1},{13,5},{2,10},{6,14},... | collective-permute-start | bytes 688136 | tf_op jit(solution)/shard_map/ppermute | solution.py:390
  100.3 4.3 %collective-permute-done.38.refs_2_.refs_9_ = bf16[32,1792]{1,0:T(8,128)(2,1)S(1)} collective-permute-done((bf16[32,1792]{1,0:T(8,128)(2,1)S(1)}, bf16[32,1792]{1,0:T(8,128)(2,1)S(1)}, u32[]{:S(2)}, u32[]{:S(2)}) %collective-permute-start.38) | collective-permute-done | bytes 114720 | tf_op jit(solution)/shard_map/ppermute | solution.py:393
  105.7 1.5 %collective-permute-start.51 = (bf16[64,1792]{1,0:T(8,128)(2,1)S(1)}, bf16[64,1792]{1,0:T(8,128)(2,1)S(1)}, u32[]{:S(2)}, u32[]{:S(2)}) collective-permute-start(bf16[64,1792]{1,0:T(8,128)(2,1)S(1)} %get-tuple-element.50), channel_id=1, source_target_pairs={{0,8},{4,12},{8,0},{12,4},{1,9},{5,13},{9,1},{13,5},{2,10},{6,14},... | collective-permute-start | bytes 688136 | tf_op jit(solution)/shard_map/ppermute | solution.py:390
  107.3 5.6 %collective-permute-done.51.refs_8_.refs_1_ = bf16[64,1792]{1,0:T(8,128)(2,1)S(1)} collective-permute-done((bf16[64,1792]{1,0:T(8,128)(2,1)S(1)}, bf16[64,1792]{1,0:T(8,128)(2,1)S(1)}, u32[]{:S(2)}, u32[]{:S(2)}) %collective-permute-start.51) | collective-permute-done | bytes 229408 | tf_op jit(solution)/shard_map/ppermute | solution.py:390
  113.0 1.5 %collective-permute-start.52 = (bf16[64,1792]{1,0:T(8,128)(2,1)S(1)}, bf16[64,1792]{1,0:T(8,128)(2,1)S(1)}, u32[]{:S(2)}, u32[]{:S(2)}) collective-permute-start(bf16[64,1792]{1,0:T(8,128)(2,1)S(1)} %get-tuple-element.52), channel_id=1, source_target_pairs={{0,8},{4,12},{8,0},{12,4},{1,9},{5,13},{9,1},{13,5},{2,10},{6,14},... | collective-permute-start | bytes 688136 | tf_op jit(solution)/shard_map/ppermute | solution.py:390
  114.6 1.8 %collective-permute-start.39 = (bf16[32,1792]{1,0:T(8,128)(2,1)S(1)}, bf16[32,1792]{1,0:T(8,128)(2,1)S(1)}, u32[]{:S(2)}, u32[]{:S(2)}) collective-permute-start(bf16[32,1792]{1,0:T(8,128)(2,1)S(1)} %add.75.refs_10_), channel_id=1, source_target_pairs={{0,2},{1,3},{2,0},{3,1},{4,6},{5,7},{6,4},{7,5},{8,10},{9,11},{10,... | collective-permute-start | bytes 344072 | tf_op jit(solution)/shard_map/ppermute | solution.py:393
  116.4 1.1 collective-permute-start.53
  118.5 2.4 %collective-permute-done.39.refs_3_.refs_2_ = bf16[32,1792]{1,0:T(8,128)(2,1)S(1)} collective-permute-done((bf16[32,1792]{1,0:T(8,128)(2,1)S(1)}, bf16[32,1792]{1,0:T(8,128)(2,1)S(1)}, u32[]{:S(2)}, u32[]{:S(2)}) %collective-permute-start.39) | collective-permute-done | bytes 114720 | tf_op jit(solution)/shard_map/ppermute | solution.py:393
  120.9 2.7 %collective-permute-done.53.refs_2_ = bf16[32,1792]{1,0:T(8,128)(2,1)S(1)} collective-permute-done((bf16[32,1792]{1,0:T(8,128)(2,1)S(1)}, bf16[32,1792]{1,0:T(8,128)(2,1)S(1)}, u32[]{:S(2)}, u32[]{:S(2)}) %collective-permute-start.53) | collective-permute-done | bytes 114720 | tf_op jit(solution)/shard_map/ppermute | solution.py:393
  124.0 1.2 collective-permute-done.40.refs_2_.refs_3_
  125.3 1.3 collective-permute-start.55
  127.3 3.5 %collective-permute-done.54.refs_6_ = bf16[32,1792]{1,0:T(8,128)(2,1)S(1)} collective-permute-done((bf16[32,1792]{1,0:T(8,128)(2,1)S(1)}, bf16[32,1792]{1,0:T(8,128)(2,1)S(1)}, u32[]{:S(2)}, u32[]{:S(2)}) %collective-permute-start.54) | collective-permute-done | bytes 114720 | tf_op jit(solution)/shard_map/ppermute | solution.py:393
  (100 shorter events, 16.9 us)
Async XLA Ops:
  15.4 6.5 %collective-permute-start.1 = (bf16[64,1024]{1,0:T(8,128)(2,1)S(1)}, bf16[64,1024]{1,0:T(8,128)(2,1)S(1)}, u32[]{:S(2)}, u32[]{:S(2)}) collective-permute-start(bf16[64,1024]{1,0:T(8,128)(2,1)S(1)} %get-tuple-element.28.refs_0_), channel_id=1, source_target_pairs={{0,8},{4,12},{8,0},{12,4},{1,9},{5,13},{9,1},{13,5},{2,10},{6,14},... | collective-permute-start | bytes 393224 | tf_op jit(solution)/shard_map/ppermute | solution.py:390
  18.4 3.5 %collective-permute-start = (bf16[64,1024]{1,0:T(8,128)(2,1)S(1)}, bf16[64,1024]{1,0:T(8,128)(2,1)S(1)}, u32[]{:S(2)}, u32[]{:S(2)}) collective-permute-start(bf16[64,1024]{1,0:T(8,128)(2,1)S(1)} %get-tuple-element.28.refs_0_), channel_id=1, source_target_pairs={{0,4},{4,0},{8,12},{12,8},{1,5},{5,1},{9,13},{13,9},{2,6},{6,2},{1... | collective-permute-start | bytes 393224 | tf_op jit(solution)/shard_map/ppermute | solution.py:386
  25.7 5.4 %collective-permute-start.3 = (bf16[32,1792]{1,0:T(8,128)(2,1)S(1)}, bf16[32,1792]{1,0:T(8,128)(2,1)S(1)}, u32[]{:S(2)}, u32[]{:S(2)}) collective-permute-start(bf16[32,1792]{1,0:T(8,128)(2,1)S(1)} %get-tuple-element.32), channel_id=1, source_target_pairs={{0,1},{1,0},{2,3},{3,2},{4,5},{5,4},{6,7},{7,6},{8,9},{9,8},{10,11... | collective-permute-start | bytes 344072 | tf_op jit(solution)/shard_map/ppermute | solution.py:393
  30.8 11.7 %collective-permute-start.5 = (bf16[32,1792]{1,0:T(8,128)(2,1)S(1)}, bf16[32,1792]{1,0:T(8,128)(2,1)S(1)}, u32[]{:S(2)}, u32[]{:S(2)}) collective-permute-start(bf16[32,1792]{1,0:T(8,128)(2,1)S(1)} %add.65), channel_id=1, source_target_pairs={{0,1},{1,0},{2,3},{3,2},{4,5},{5,4},{6,7},{7,6},{8,9},{9,8},{10,11... | collective-permute-start | bytes 344072 | tf_op jit(solution)/shard_map/ppermute | solution.py:393
  31.1 11.4 %collective-permute-start.4 = (bf16[32,1792]{1,0:T(8,128)(2,1)S(1)}, bf16[32,1792]{1,0:T(8,128)(2,1)S(1)}, u32[]{:S(2)}, u32[]{:S(2)}) collective-permute-start(bf16[32,1792]{1,0:T(8,128)(2,1)S(1)} %add.64.refs_1_), channel_id=1, source_target_pairs={{0,2},{1,3},{2,0},{3,1},{4,6},{5,7},{6,4},{7,5},{8,10},{9,11},{10,... | collective-permute-start | bytes 344072 | tf_op jit(solution)/shard_map/ppermute | solution.py:393
  34.1 9.1 %collective-permute-start.9 = (bf16[32,1792]{1,0:T(8,128)(2,1)S(1)}, bf16[32,1792]{1,0:T(8,128)(2,1)S(1)}, u32[]{:S(2)}, u32[]{:S(2)}) collective-permute-start(bf16[32,1792]{1,0:T(8,128)(2,1)S(1)} %add.67), channel_id=1, source_target_pairs={{0,1},{1,0},{2,3},{3,2},{4,5},{5,4},{6,7},{7,6},{8,9},{9,8},{10,11... | collective-permute-start | bytes 344072 | tf_op jit(solution)/shard_map/ppermute | solution.py:393
  35.7 3.6 %collective-permute-start.7 = (f32[1,1792]{1,0:T(1,128)S(1)}, f32[1,1792]{1,0:T(1,128)S(1)}, u32[]{:S(2)}, u32[]{:S(2)}) collective-permute-start(f32[1,1792]{1,0:T(1,128)S(1)} %reshape.7.refs_1_.refs_4_.refs_16_), channel_id=1, source_target_pairs={{0,8},{4,12},{8,0},{12,4},{1,9},{5,13},{9,1},{13,5},{2,10},{6,14},... | collective-permute-start | bytes 21512 | tf_op jit(solution)/shard_map/ppermute | solution.py:390
  37.2 5.4 %collective-permute-start.6 = (f32[1,1792]{1,0:T(1,128)S(1)}, f32[1,1792]{1,0:T(1,128)S(1)}, u32[]{:S(2)}, u32[]{:S(2)}) collective-permute-start(f32[1,1792]{1,0:T(1,128)S(1)} %reshape.7.refs_1_.refs_4_.refs_16_), channel_id=1, source_target_pairs={{0,4},{4,0},{8,12},{12,8},{1,5},{5,1},{9,13},{13,9},{2,6},{6,2},{1... | collective-permute-start | bytes 21512 | tf_op jit(solution)/shard_map/ppermute | solution.py:386
  39.3 3.2 %collective-permute-start.8 = (f32[1,1792]{1,0:T(1,128)S(1)}, f32[1,1792]{1,0:T(1,128)S(1)}, u32[]{:S(2)}, u32[]{:S(2)}) collective-permute-start(f32[1,1792]{1,0:T(1,128)S(1)} %collective-permute-done.7.refs_6_.refs_18_), channel_id=1, source_target_pairs={{0,4},{4,0},{8,12},{12,8},{1,5},{5,1},{9,13},{13,9},{2,6},{6,2},{1... | collective-permute-start | bytes 21512 | tf_op jit(solution)/shard_map/ppermute | solution.py:386
  42.6 9.8 %collective-permute-start.11 = (bf16[32,1792]{1,0:T(8,128)(2,1)S(1)}, bf16[32,1792]{1,0:T(8,128)(2,1)S(1)}, u32[]{:S(2)}, u32[]{:S(2)}) collective-permute-start(bf16[32,1792]{1,0:T(8,128)(2,1)S(1)} %add.69), channel_id=1, source_target_pairs={{0,1},{1,0},{2,3},{3,2},{4,5},{5,4},{6,7},{7,6},{8,9},{9,8},{10,11... | collective-permute-start | bytes 344072 | tf_op jit(solution)/shard_map/ppermute | solution.py:393
  43.2 11.9 %collective-permute-start.10 = (bf16[32,1792]{1,0:T(8,128)(2,1)S(1)}, bf16[32,1792]{1,0:T(8,128)(2,1)S(1)}, u32[]{:S(2)}, u32[]{:S(2)}) collective-permute-start(bf16[32,1792]{1,0:T(8,128)(2,1)S(1)} %add.68), channel_id=1, source_target_pairs={{0,2},{1,3},{2,0},{3,1},{4,6},{5,7},{6,4},{7,5},{8,10},{9,11},{10,... | collective-permute-start | bytes 344072 | tf_op jit(solution)/shard_map/ppermute | solution.py:393
  43.8 13.1 %collective-permute-start.12 = (bf16[32,1792]{1,0:T(8,128)(2,1)S(1)}, bf16[32,1792]{1,0:T(8,128)(2,1)S(1)}, u32[]{:S(2)}, u32[]{:S(2)}) collective-permute-start(bf16[32,1792]{1,0:T(8,128)(2,1)S(1)} %add.66.refs_2_.refs_1_.refs_0_.refs_12_), channel_id=1, source_target_pairs={{0,2},{1,3},{2,0},{3,1},{4,6},{5,7},{6,4},{7,5},{8,10},{9,11},{10,... | collective-permute-start | bytes 344072 | tf_op jit(solution)/shard_map/ppermute | solution.py:393
  46.2 12.7 %collective-permute-start.20 = (bf16[32,1792]{1,0:T(8,128)(2,1)S(1)}, bf16[32,1792]{1,0:T(8,128)(2,1)S(1)}, u32[]{:S(2)}, u32[]{:S(2)}) collective-permute-start(bf16[32,1792]{1,0:T(8,128)(2,1)S(1)} %add.66.refs_2_.refs_1_.refs_0_.refs_12_), channel_id=1, source_target_pairs={{0,1},{1,0},{2,3},{3,2},{4,5},{5,4},{6,7},{7,6},{8,9},{9,8},{10,11... | collective-permute-start | bytes 344072 | tf_op jit(solution)/shard_map/ppermute | solution.py:393
  47.8 12.6 %collective-permute-start.25 = (bf16[32,1792]{1,0:T(8,128)(2,1)S(1)}, bf16[32,1792]{1,0:T(8,128)(2,1)S(1)}, u32[]{:S(2)}, u32[]{:S(2)}) collective-permute-start(bf16[32,1792]{1,0:T(8,128)(2,1)S(1)} %add.66.refs_2_.refs_1_.refs_0_.refs_12_), channel_id=1, source_target_pairs={{0,8},{4,12},{8,0},{12,4},{1,9},{5,13},{9,1},{13,5},{2,10},{6,14},... | collective-permute-start | bytes 344072 | tf_op jit(solution)/shard_map/ppermute | solution.py:390
  52.5 8.1 %collective-permute-start.24 = (bf16[32,1792]{1,0:T(8,128)(2,1)S(1)}, bf16[32,1792]{1,0:T(8,128)(2,1)S(1)}, u32[]{:S(2)}, u32[]{:S(2)}) collective-permute-start(bf16[32,1792]{1,0:T(8,128)(2,1)S(1)} %add.66.refs_2_.refs_1_.refs_0_.refs_12_), channel_id=1, source_target_pairs={{0,4},{4,0},{8,12},{12,8},{1,5},{5,1},{9,13},{13,9},{2,6},{6,2},{1... | collective-permute-start | bytes 344072 | tf_op jit(solution)/shard_map/ppermute | solution.py:386
  56.9 7.0 %collective-permute-start.27 = (bf16[32,1792]{1,0:T(8,128)(2,1)S(1)}, bf16[32,1792]{1,0:T(8,128)(2,1)S(1)}, u32[]{:S(2)}, u32[]{:S(2)}) collective-permute-start(bf16[32,1792]{1,0:T(8,128)(2,1)S(1)} %add.70.refs_1_.refs_12_), channel_id=1, source_target_pairs={{0,2},{1,3},{2,0},{3,1},{4,6},{5,7},{6,4},{7,5},{8,10},{9,11},{10,... | collective-permute-start | bytes 344072 | tf_op jit(solution)/shard_map/ppermute | solution.py:393
  57.0 8.4 %collective-permute-start.30 = (bf16[32,1792]{1,0:T(8,128)(2,1)S(1)}, bf16[32,1792]{1,0:T(8,128)(2,1)S(1)}, u32[]{:S(2)}, u32[]{:S(2)}) collective-permute-start(bf16[32,1792]{1,0:T(8,128)(2,1)S(1)} %add.70.refs_1_.refs_12_), channel_id=1, source_target_pairs={{0,1},{1,0},{2,3},{3,2},{4,5},{5,4},{6,7},{7,6},{8,9},{9,8},{10,11... | collective-permute-start | bytes 344072 | tf_op jit(solution)/shard_map/ppermute | solution.py:393
  58.9 6.6 %collective-permute-start.29 = (bf16[32,1792]{1,0:T(8,128)(2,1)S(1)}, bf16[32,1792]{1,0:T(8,128)(2,1)S(1)}, u32[]{:S(2)}, u32[]{:S(2)}) collective-permute-start(bf16[32,1792]{1,0:T(8,128)(2,1)S(1)} %add.70.refs_1_.refs_12_), channel_id=1, source_target_pairs={{0,8},{4,12},{8,0},{12,4},{1,9},{5,13},{9,1},{13,5},{2,10},{6,14},... | collective-permute-start | bytes 344072 | tf_op jit(solution)/shard_map/ppermute | solution.py:390
  60.4 6.3 %collective-permute-start.13 = (bf16[32,1792]{1,0:T(8,128)(2,1)S(1)}, bf16[32,1792]{1,0:T(8,128)(2,1)S(1)}, u32[]{:S(2)}, u32[]{:S(2)}) collective-permute-start(bf16[32,1792]{1,0:T(8,128)(2,1)S(1)} %collective-permute-done.12.refs_3_.refs_4_), channel_id=1, source_target_pairs={{0,1},{1,0},{2,3},{3,2},{4,5},{5,4},{6,7},{7,6},{8,9},{9,8},{10,11... | collective-permute-start | bytes 344072 | tf_op jit(solution)/shard_map/ppermute | solution.py:393
  60.6 6.1 %collective-permute-start.18 = (bf16[32,1792]{1,0:T(8,128)(2,1)S(1)}, bf16[32,1792]{1,0:T(8,128)(2,1)S(1)}, u32[]{:S(2)}, u32[]{:S(2)}) collective-permute-start(bf16[32,1792]{1,0:T(8,128)(2,1)S(1)} %collective-permute-done.12.refs_3_.refs_4_), channel_id=1, source_target_pairs={{0,8},{4,12},{8,0},{12,4},{1,9},{5,13},{9,1},{13,5},{2,10},{6,14},... | collective-permute-start | bytes 344072 | tf_op jit(solution)/shard_map/ppermute | solution.py:390
  64.0 4.9 %collective-permute-start.22 = (bf16[32,1792]{1,0:T(8,128)(2,1)S(1)}, bf16[32,1792]{1,0:T(8,128)(2,1)S(1)}, u32[]{:S(2)}, u32[]{:S(2)}) collective-permute-start(bf16[32,1792]{1,0:T(8,128)(2,1)S(1)} %collective-permute-done.20.refs_8_), channel_id=1, source_target_pairs={{0,8},{4,12},{8,0},{12,4},{1,9},{5,13},{9,1},{13,5},{2,10},{6,14},... | collective-permute-start | bytes 344072 | tf_op jit(solution)/shard_map/ppermute | solution.py:390
  65.4 4.9 %collective-permute-start.17 = (bf16[32,1792]{1,0:T(8,128)(2,1)S(1)}, bf16[32,1792]{1,0:T(8,128)(2,1)S(1)}, u32[]{:S(2)}, u32[]{:S(2)}) collective-permute-start(bf16[32,1792]{1,0:T(8,128)(2,1)S(1)} %collective-permute-done.12.refs_3_.refs_4_), channel_id=1, source_target_pairs={{0,4},{4,0},{8,12},{12,8},{1,5},{5,1},{9,13},{13,9},{2,6},{6,2},{1... | collective-permute-start | bytes 344072 | tf_op jit(solution)/shard_map/ppermute | solution.py:386
  65.5 5.5 %collective-permute-start.21 = (bf16[32,1792]{1,0:T(8,128)(2,1)S(1)}, bf16[32,1792]{1,0:T(8,128)(2,1)S(1)}, u32[]{:S(2)}, u32[]{:S(2)}) collective-permute-start(bf16[32,1792]{1,0:T(8,128)(2,1)S(1)} %collective-permute-done.20.refs_8_), channel_id=1, source_target_pairs={{0,4},{4,0},{8,12},{12,8},{1,5},{5,1},{9,13},{13,9},{2,6},{6,2},{1... | collective-permute-start | bytes 344072 | tf_op jit(solution)/shard_map/ppermute | solution.py:386
  66.7 5.7 %collective-permute-start.26 = (bf16[32,1792]{1,0:T(8,128)(2,1)S(1)}, bf16[32,1792]{1,0:T(8,128)(2,1)S(1)}, u32[]{:S(2)}, u32[]{:S(2)}) collective-permute-start(bf16[32,1792]{1,0:T(8,128)(2,1)S(1)} %collective-permute-done.25.refs_14_), channel_id=1, source_target_pairs={{0,4},{4,0},{8,12},{12,8},{1,5},{5,1},{9,13},{13,9},{2,6},{6,2},{1... | collective-permute-start | bytes 344072 | tf_op jit(solution)/shard_map/ppermute | solution.py:386
  66.7 5.7 %collective-permute-start.28 = (bf16[32,1792]{1,0:T(8,128)(2,1)S(1)}, bf16[32,1792]{1,0:T(8,128)(2,1)S(1)}, u32[]{:S(2)}, u32[]{:S(2)}) collective-permute-start(bf16[32,1792]{1,0:T(8,128)(2,1)S(1)} %collective-permute-done.27.refs_4_), channel_id=1, source_target_pairs={{0,1},{1,0},{2,3},{3,2},{4,5},{5,4},{6,7},{7,6},{8,9},{9,8},{10,11... | collective-permute-start | bytes 344072 | tf_op jit(solution)/shard_map/ppermute | solution.py:393
  68.9 6.1 %collective-permute-start.31 = (bf16[32,1792]{1,0:T(8,128)(2,1)S(1)}, bf16[32,1792]{1,0:T(8,128)(2,1)S(1)}, u32[]{:S(2)}, u32[]{:S(2)}) collective-permute-start(bf16[32,1792]{1,0:T(8,128)(2,1)S(1)} %collective-permute-done.30.refs_8_), channel_id=1, source_target_pairs={{0,8},{4,12},{8,0},{12,4},{1,9},{5,13},{9,1},{13,5},{2,10},{6,14},... | collective-permute-start | bytes 344072 | tf_op jit(solution)/shard_map/ppermute | solution.py:390
  70.4 6.3 %collective-permute-start.15 = (bf16[32,1792]{1,0:T(8,128)(2,1)S(1)}, bf16[32,1792]{1,0:T(8,128)(2,1)S(1)}, u32[]{:S(2)}, u32[]{:S(2)}) collective-permute-start(bf16[32,1792]{1,0:T(8,128)(2,1)S(1)} %collective-permute-done.13.refs_0_), channel_id=1, source_target_pairs={{0,8},{4,12},{8,0},{12,4},{1,9},{5,13},{9,1},{13,5},{2,10},{6,14},... | collective-permute-start | bytes 344072 | tf_op jit(solution)/shard_map/ppermute | solution.py:390
  70.9 6.9 %collective-permute-start.32 = (bf16[32,1792]{1,0:T(8,128)(2,1)S(1)}, bf16[32,1792]{1,0:T(8,128)(2,1)S(1)}, u32[]{:S(2)}, u32[]{:S(2)}) collective-permute-start(bf16[32,1792]{1,0:T(8,128)(2,1)S(1)} %collective-permute-done.27.refs_4_), channel_id=1, source_target_pairs={{0,8},{4,12},{8,0},{12,4},{1,9},{5,13},{9,1},{13,5},{2,10},{6,14},... | collective-permute-start | bytes 344072 | tf_op jit(solution)/shard_map/ppermute | solution.py:390
  72.4 6.9 %collective-permute-start.14 = (bf16[32,1792]{1,0:T(8,128)(2,1)S(1)}, bf16[32,1792]{1,0:T(8,128)(2,1)S(1)}, u32[]{:S(2)}, u32[]{:S(2)}) collective-permute-start(bf16[32,1792]{1,0:T(8,128)(2,1)S(1)} %collective-permute-done.13.refs_0_), channel_id=1, source_target_pairs={{0,4},{4,0},{8,12},{12,8},{1,5},{5,1},{9,13},{13,9},{2,6},{6,2},{1... | collective-permute-start | bytes 344072 | tf_op jit(solution)/shard_map/ppermute | solution.py:386
  72.4 6.9 %collective-permute-start.19 = (bf16[32,1792]{1,0:T(8,128)(2,1)S(1)}, bf16[32,1792]{1,0:T(8,128)(2,1)S(1)}, u32[]{:S(2)}, u32[]{:S(2)}) collective-permute-start(bf16[32,1792]{1,0:T(8,128)(2,1)S(1)} %collective-permute-done.18.refs_6_), channel_id=1, source_target_pairs={{0,4},{4,0},{8,12},{12,8},{1,5},{5,1},{9,13},{13,9},{2,6},{6,2},{1... | collective-permute-start | bytes 344072 | tf_op jit(solution)/shard_map/ppermute | solution.py:386
  75.0 4.4 %collective-permute-start.23 = (bf16[32,1792]{1,0:T(8,128)(2,1)S(1)}, bf16[32,1792]{1,0:T(8,128)(2,1)S(1)}, u32[]{:S(2)}, u32[]{:S(2)}) collective-permute-start(bf16[32,1792]{1,0:T(8,128)(2,1)S(1)} %collective-permute-done.22.refs_10_), channel_id=1, source_target_pairs={{0,4},{4,0},{8,12},{12,8},{1,5},{5,1},{9,13},{13,9},{2,6},{6,2},{1... | collective-permute-start | bytes 344072 | tf_op jit(solution)/shard_map/ppermute | solution.py:386
  76.6 2.7 %collective-permute-start.16 = (bf16[32,1792]{1,0:T(8,128)(2,1)S(1)}, bf16[32,1792]{1,0:T(8,128)(2,1)S(1)}, u32[]{:S(2)}, u32[]{:S(2)}) collective-permute-start(bf16[32,1792]{1,0:T(8,128)(2,1)S(1)} %collective-permute-done.15.refs_2_), channel_id=1, source_target_pairs={{0,4},{4,0},{8,12},{12,8},{1,5},{5,1},{9,13},{13,9},{2,6},{6,2},{1... | collective-permute-start | bytes 344072 | tf_op jit(solution)/shard_map/ppermute | solution.py:386
  77.9 4.8 %collective-permute-start.33 = (bf16[32,1792]{1,0:T(8,128)(2,1)S(1)}, bf16[32,1792]{1,0:T(8,128)(2,1)S(1)}, u32[]{:S(2)}, u32[]{:S(2)}) collective-permute-start(bf16[32,1792]{1,0:T(8,128)(2,1)S(1)} %collective-permute-done.28.refs_22_.refs_0_), channel_id=1, source_target_pairs={{0,8},{4,12},{8,0},{12,4},{1,9},{5,13},{9,1},{13,5},{2,10},{6,14},... | collective-permute-start | bytes 344072 | tf_op jit(solution)/shard_map/ppermute | solution.py:390
  84.4 2.8 %collective-permute-start.35 = (bf16[128,1792]{1,0:T(8,128)(2,1)S(1)}, bf16[128,1792]{1,0:T(8,128)(2,1)S(1)}, u32[]{:S(2)}, u32[]{:S(2)}) collective-permute-start(bf16[128,1792]{1,0:T(8,128)(2,1)S(1)} %get-tuple-element.41), channel_id=1, source_target_pairs={{0,4},{4,0},{8,12},{12,8},{1,5},{5,1},{9,13},{13,9},{2,6},{6,2},{1... | collective-permute-start | bytes 1376264 | tf_op jit(solution)/shard_map/ppermute | solution.py:386
  84.5 11.0 %collective-permute-start.34 = (bf16[128,1792]{1,0:T(8,128)(2,1)S(1)}, bf16[128,1792]{1,0:T(8,128)(2,1)S(1)}, u32[]{:S(2)}, u32[]{:S(2)}) collective-permute-start(bf16[128,1792]{1,0:T(8,128)(2,1)S(1)} %get-tuple-element.39), channel_id=1, source_target_pairs={{0,4},{4,0},{8,12},{12,8},{1,5},{5,1},{9,13},{13,9},{2,6},{6,2},{1... | collective-permute-start | bytes 1376264 | tf_op jit(solution)/shard_map/ppermute | solution.py:386
  85.5 3.8 %collective-permute-start.45 = (bf16[32,1792]{1,0:T(8,128)(2,1)S(1)}, bf16[32,1792]{1,0:T(8,128)(2,1)S(1)}, u32[]{:S(2)}, u32[]{:S(2)}) collective-permute-start(bf16[32,1792]{1,0:T(8,128)(2,1)S(1)} %collective-permute-done.30.refs_8_), channel_id=1, source_target_pairs={{0,4},{4,0},{8,12},{12,8},{1,5},{5,1},{9,13},{13,9},{2,6},{6,2},{1... | collective-permute-start | bytes 344072 | tf_op jit(solution)/shard_map/ppermute | solution.py:386
  87.8 7.7 %collective-permute-start.36 = (bf16[64,1792]{1,0:T(8,128)(2,1)S(1)}, bf16[64,1792]{1,0:T(8,128)(2,1)S(1)}, u32[]{:S(2)}, u32[]{:S(2)}) collective-permute-start(bf16[64,1792]{1,0:T(8,128)(2,1)S(1)} %get-tuple-element.42.refs_22_), channel_id=1, source_target_pairs={{0,8},{4,12},{8,0},{12,4},{1,9},{5,13},{9,1},{13,5},{2,10},{6,14},... | collective-permute-start | bytes 688136 | tf_op jit(solution)/shard_map/ppermute | solution.py:390
  97.4 8.1 %collective-permute-start.50 = (bf16[128,1792]{1,0:T(8,128)(2,1)S(1)}, bf16[128,1792]{1,0:T(8,128)(2,1)S(1)}, u32[]{:S(2)}, u32[]{:S(2)}) collective-permute-start(bf16[128,1792]{1,0:T(8,128)(2,1)S(1)} %get-tuple-element.49), channel_id=1, source_target_pairs={{0,4},{4,0},{8,12},{12,8},{1,5},{5,1},{9,13},{13,9},{2,6},{6,2},{1... | collective-permute-start | bytes 1376264 | tf_op jit(solution)/shard_map/ppermute | solution.py:386
  97.5 8.0 %collective-permute-start.37 = (bf16[64,1792]{1,0:T(8,128)(2,1)S(1)}, bf16[64,1792]{1,0:T(8,128)(2,1)S(1)}, u32[]{:S(2)}, u32[]{:S(2)}) collective-permute-start(bf16[64,1792]{1,0:T(8,128)(2,1)S(1)} %get-tuple-element.44.refs_1_), channel_id=1, source_target_pairs={{0,8},{4,12},{8,0},{12,4},{1,9},{5,13},{9,1},{13,5},{2,10},{6,14},... | collective-permute-start | bytes 688136 | tf_op jit(solution)/shard_map/ppermute | solution.py:390
  99.1 8.2 %collective-permute-start.49 = (bf16[128,1792]{1,0:T(8,128)(2,1)S(1)}, bf16[128,1792]{1,0:T(8,128)(2,1)S(1)}, u32[]{:S(2)}, u32[]{:S(2)}) collective-permute-start(bf16[128,1792]{1,0:T(8,128)(2,1)S(1)} %get-tuple-element.47), channel_id=1, source_target_pairs={{0,4},{4,0},{8,12},{12,8},{1,5},{5,1},{9,13},{13,9},{2,6},{6,2},{1... | collective-permute-start | bytes 1376264 | tf_op jit(solution)/shard_map/ppermute | solution.py:386
  99.2 5.4 %collective-permute-start.38 = (bf16[32,1792]{1,0:T(8,128)(2,1)S(1)}, bf16[32,1792]{1,0:T(8,128)(2,1)S(1)}, u32[]{:S(2)}, u32[]{:S(2)}) collective-permute-start(bf16[32,1792]{1,0:T(8,128)(2,1)S(1)} %add.74.refs_0_), channel_id=1, source_target_pairs={{0,1},{1,0},{2,3},{3,2},{4,5},{5,4},{6,7},{7,6},{8,9},{9,8},{10,11... | collective-permute-start | bytes 344072 | tf_op jit(solution)/shard_map/ppermute | solution.py:393
  105.7 7.2 %collective-permute-start.51 = (bf16[64,1792]{1,0:T(8,128)(2,1)S(1)}, bf16[64,1792]{1,0:T(8,128)(2,1)S(1)}, u32[]{:S(2)}, u32[]{:S(2)}) collective-permute-start(bf16[64,1792]{1,0:T(8,128)(2,1)S(1)} %get-tuple-element.50), channel_id=1, source_target_pairs={{0,8},{4,12},{8,0},{12,4},{1,9},{5,13},{9,1},{13,5},{2,10},{6,14},... | collective-permute-start | bytes 688136 | tf_op jit(solution)/shard_map/ppermute | solution.py:390
  113.0 12.2 %collective-permute-start.52 = (bf16[64,1792]{1,0:T(8,128)(2,1)S(1)}, bf16[64,1792]{1,0:T(8,128)(2,1)S(1)}, u32[]{:S(2)}, u32[]{:S(2)}) collective-permute-start(bf16[64,1792]{1,0:T(8,128)(2,1)S(1)} %get-tuple-element.52), channel_id=1, source_target_pairs={{0,8},{4,12},{8,0},{12,4},{1,9},{5,13},{9,1},{13,5},{2,10},{6,14},... | collective-permute-start | bytes 688136 | tf_op jit(solution)/shard_map/ppermute | solution.py:390
  114.6 6.4 %collective-permute-start.39 = (bf16[32,1792]{1,0:T(8,128)(2,1)S(1)}, bf16[32,1792]{1,0:T(8,128)(2,1)S(1)}, u32[]{:S(2)}, u32[]{:S(2)}) collective-permute-start(bf16[32,1792]{1,0:T(8,128)(2,1)S(1)} %add.75.refs_10_), channel_id=1, source_target_pairs={{0,2},{1,3},{2,0},{3,1},{4,6},{5,7},{6,4},{7,5},{8,10},{9,11},{10,... | collective-permute-start | bytes 344072 | tf_op jit(solution)/shard_map/ppermute | solution.py:393
  116.4 7.3 %collective-permute-start.53 = (bf16[32,1792]{1,0:T(8,128)(2,1)S(1)}, bf16[32,1792]{1,0:T(8,128)(2,1)S(1)}, u32[]{:S(2)}, u32[]{:S(2)}) collective-permute-start(bf16[32,1792]{1,0:T(8,128)(2,1)S(1)} %add.79), channel_id=1, source_target_pairs={{0,1},{1,0},{2,3},{3,2},{4,5},{5,4},{6,7},{7,6},{8,9},{9,8},{10,11... | collective-permute-start | bytes 344072 | tf_op jit(solution)/shard_map/ppermute | solution.py:393
  117.5 7.7 %collective-permute-start.40 = (bf16[32,1792]{1,0:T(8,128)(2,1)S(1)}, bf16[32,1792]{1,0:T(8,128)(2,1)S(1)}, u32[]{:S(2)}, u32[]{:S(2)}) collective-permute-start(bf16[32,1792]{1,0:T(8,128)(2,1)S(1)} %add.76.refs_9_), channel_id=1, source_target_pairs={{0,1},{1,0},{2,3},{3,2},{4,5},{5,4},{6,7},{7,6},{8,9},{9,8},{10,11... | collective-permute-start | bytes 344072 | tf_op jit(solution)/shard_map/ppermute | solution.py:393
  123.7 7.1 %collective-permute-start.54 = (bf16[32,1792]{1,0:T(8,128)(2,1)S(1)}, bf16[32,1792]{1,0:T(8,128)(2,1)S(1)}, u32[]{:S(2)}, u32[]{:S(2)}) collective-permute-start(bf16[32,1792]{1,0:T(8,128)(2,1)S(1)} %add.80), channel_id=1, source_target_pairs={{0,2},{1,3},{2,0},{3,1},{4,6},{5,7},{6,4},{7,5},{8,10},{9,11},{10,... | collective-permute-start | bytes 344072 | tf_op jit(solution)/shard_map/ppermute | solution.py:393
  125.3 6.0 %collective-permute-start.55 = (bf16[32,1792]{1,0:T(8,128)(2,1)S(1)}, bf16[32,1792]{1,0:T(8,128)(2,1)S(1)}, u32[]{:S(2)}, u32[]{:S(2)}) collective-permute-start(bf16[32,1792]{1,0:T(8,128)(2,1)S(1)} %add.81), channel_id=1, source_target_pairs={{0,1},{1,0},{2,3},{3,2},{4,5},{5,4},{6,7},{7,6},{8,9},{9,8},{10,11... | collective-permute-start | bytes 344072 | tf_op jit(solution)/shard_map/ppermute | solution.py:393
  (11 other events, 67.2 us)

commit v10 on v8

--- a/solution.py
+++ b/solution.py
@@ -47,14 +47,25 @@
     )(in_hbm(value), *after)
 
 
-def attention_kernel(step_rows, lengths, q_ref, qr_ref, k_ref, kr_ref, up_ref, *refs):
-    out_ref, latent, rope = refs[-3:]
+def attention_kernel(step_rows, pieces, lengths, q_ref, qr_ref, k_hbm, kr_hbm, up_ref, *refs):
+    out_ref, latent, rope, k_ref, kr_ref, sems = refs[-6:]
     step = pl.program_id(0)
     heads, positions = q_ref.shape[1], k_ref.shape[1]
     rope_width = kr_ref.shape[1]
 
+    def copies(at):
+        whole = pl.ds(at * step_rows, step_rows)
+        made = [pltpu.make_async_copy(kr_hbm.at[whole], kr_ref.at[whole], sems.at[at, pieces])]
+        for i in range(pieces):
+            part = pl.ds(at * step_rows + i * (step_rows // pieces), step_rows // pieces)
+            made.append(pltpu.make_async_copy(k_hbm.at[part], k_ref.at[part], sems.at[at, i]))
+        return made
+
     @pl.when(step == 0)
     def _():
+        for at in range(k_ref.shape[0] // step_rows):
+            for copy in copies(at):
+                copy.start()
         all_rows = qr_ref.shape[0]
         width = heads * rope_width
         lane = lax.broadcasted_iota(jnp.int32, (heads, width), 1)
@@ -67,6 +78,8 @@
         fold = jnp.where(lane % rope_width == column, 1.0, 0.0).astype(jnp.bfloat16)
         rope[...] = jnp.dot(spread, fold, preferred_element_type=jnp.float32)
 
+    for copy in copies(step):
+        copy.wait()
     place = lax.broadcasted_iota(jnp.int32, (heads, positions), 1)
     lanes = latent.shape[2]
     lanes = latent.shape[2]
@@ -74,10 +87,10 @@
     for r in range(step_rows):
         first = pl.multiple_of((step * step_rows + r) * heads, heads)
         score = lax.dot_general(
-            q_ref[r], k_ref[r], (((1,), (1,)), ((), ())), preferred_element_type=jnp.float32
+            q_ref[r], k_ref[step * step_rows + r], (((1,), (1,)), ((), ())), preferred_element_type=jnp.float32
         )
         score += jnp.dot(
-            rope[pl.ds(first, heads), :].astype(jnp.bfloat16), kr_ref[r], preferred_element_type=jnp.float32
+            rope[pl.ds(first, heads), :].astype(jnp.bfloat16), kr_ref[step * step_rows + r], preferred_element_type=jnp.float32
         )
         scores.append(score)
     probabilities = []
@@ -89,7 +102,7 @@
         probabilities.append((weight / total).astype(jnp.bfloat16))
     for r in range(step_rows):
         first = pl.multiple_of((step * step_rows + r) * heads, heads)
-        mixed = jnp.dot(probabilities[r], k_ref[r], preferred_element_type=jnp.float32)
+        mixed = jnp.dot(probabilities[r], k_ref[step * step_rows + r], preferred_element_type=jnp.float32)
         for c in range(latent.shape[0]):
             latent[c, pl.ds(first, heads), :] = mixed[:, c * lanes : (c + 1) * lanes]
 
@@ -107,13 +120,12 @@
 
 def attend(query_latent, query_rope, cache_latent, cache_rope, cache_length, value_up, after):
     rows, heads, latent_width = query_latent.shape
-    positions = cache_latent.shape[1]
     rope_width = cache_rope.shape[1]
     value_width = value_up.shape[2]
-    step_rows = 16
+    step_rows, pieces = 16, 2
     by_row = lambda i, lengths: (i, 0, 0)
     return pl.pallas_call(
-        functools.partial(attention_kernel, step_rows),
+        functools.partial(attention_kernel, step_rows, pieces),
         out_shape=jax.ShapeDtypeStruct((rows, heads * value_width), jnp.bfloat16),
         grid_spec=pltpu.PrefetchScalarGridSpec(
             num_scalar_prefetch=1,
@@ -121,8 +133,8 @@
             in_specs=[
                 pl.BlockSpec((step_rows, heads, latent_width), by_row),
                 pl.BlockSpec(query_rope.shape, lambda i, lengths: (0, 0)),
-                pl.BlockSpec((step_rows, positions, latent_width), by_row),
-                pl.BlockSpec((step_rows, rope_width, positions), by_row),
+                pl.BlockSpec(memory_space=pl.ANY),
+                pl.BlockSpec(memory_space=pl.ANY),
                 pl.BlockSpec(value_up.shape, lambda i, lengths: (0, 0, 0)),
             ]
             + [pl.BlockSpec(memory_space=pl.ANY)] * len(after),
@@ -130,12 +142,15 @@
             scratch_shapes=[
                 pltpu.VMEM((latent_width // 128, rows * heads, 128), jnp.float32),
                 pltpu.VMEM((rows * heads, rope_width), jnp.float32),
+                pltpu.VMEM(cache_latent.shape, jnp.bfloat16),
+                pltpu.VMEM(cache_rope.shape, jnp.bfloat16),
+                pltpu.SemaphoreType.DMA((rows // step_rows, pieces + 1)),
             ],
         ),
         cost_estimate=pl.CostEstimate(
             flops=64 * heads * cache_latent.size, bytes_accessed=2 * cache_latent.size, transcendentals=0
         ),
-        compiler_params=pltpu.CompilerParams(vmem_limit_bytes=20 * MIB),
+        compiler_params=pltpu.CompilerParams(vmem_limit_bytes=28 * MIB),
         name="attention",
     )(
         cache_length,
@@ -245,19 +260,18 @@
     )(places, *[b for row in blocks for b in row], *gains, in_vmem(gate_weight), in_vmem(up_weight), *after)
 
 
-def down_kernel(slots, column_blocks, cores, places, active, row_weight, down, *refs):
+def down_kernel(slots, column_blocks, cores, core, places, active, row_weight, down, *refs):
     row_blocks = len(slots)
-    outs = refs[-row_blocks * cores :]
+    outs = refs[-row_blocks:]
     width = down.shape[2] // column_blocks
     height = active.shape[0] // row_blocks
-    order = [b * cores + c for c in reversed(range(cores)) for b in range(column_blocks // cores)]
     tile = 256 if width % 256 == 0 else 128
     weights = []
     for s in range(row_blocks):
         first = pl.multiple_of(places[column_blocks + slots[s]] * height, height)
         weights.append(row_weight[pl.ds(first, height), :])
-    for k in order:
-        b, c = k // cores, k % cores
+    for b in range(column_blocks // cores):
+        k = b * cores + core
         start = pl.multiple_of(places[k] * width, 128)
         for j in range(width // tile):
             cut = slice(j * tile, (j + 1) * tile)
@@ -266,29 +280,29 @@
             )
             for s in range(row_blocks):
                 part = product[s * height : (s + 1) * height, :] * weights[s]
-                outs[s * cores + c][b * height : (b + 1) * height, cut] = part.astype(jnp.bfloat16)
-
-
-def project_down(places, active, row_weight, down_weight, slots, column_blocks, cores, after):
+                outs[s][b * height : (b + 1) * height, cut] = part.astype(jnp.bfloat16)
+
+
+def project_down(places, active, row_weight, down_weight, slots, column_blocks, cores, core, after):
     row_blocks = len(slots)
-    rows, hidden = active.shape
+    rows = active.shape[0]
     width = down_weight.shape[2] // column_blocks
     whole = pl.BlockSpec(memory_space=pltpu.VMEM)
     out = jax.ShapeDtypeStruct((rows // row_blocks * (column_blocks // cores), width), jnp.bfloat16)
     outs = pl.pallas_call(
-        functools.partial(down_kernel, slots, column_blocks, cores),
-        out_shape=[out] * (row_blocks * cores),
+        functools.partial(down_kernel, slots, column_blocks, cores, core),
+        out_shape=[out] * row_blocks,
         in_specs=[pl.BlockSpec(memory_space=pltpu.SMEM)]
         + [whole] * 3
         + [pl.BlockSpec(memory_space=pl.ANY)] * len(after),
-        out_specs=[whole] * (row_blocks * cores),
+        out_specs=[whole] * row_blocks,
         cost_estimate=pl.CostEstimate(
-            flops=2 * rows * down_weight.size, bytes_accessed=2 * down_weight.size, transcendentals=0
+            flops=2 * rows * down_weight.size // cores, bytes_accessed=2 * down_weight.size // cores, transcendentals=0
         ),
         compiler_params=pltpu.CompilerParams(vmem_limit_bytes=4 * MIB),
         name="down",
     )(places, active, row_weight, in_vmem(down_weight), *after)
-    return [outs[s * cores : (s + 1) * cores] for s in range(row_blocks)]
+    return outs
 
 
 def add_kernel(groups, *refs):
@@ -376,16 +390,17 @@
     output_weight = fetch(output_weight, [head_out, row_weight, own_residual, gain])
     partial = project(places, gather_ep(head_out), output_weight, tp_count)
 
-    gate_weight = fetch(gate_weight, [partial[0]])
+    up_weight = fetch(up_weight, [partial[0]])
     terms = [[(value, 0)] for value in partial]
     for k in reversed(range(1, tp_count)):
         total = terms[k][0][0]
         if len(terms[k]) > 1 or k == 1:
-            (total,) = add([terms[k]], block_rows, [gate_weight] if k == 1 else [])
+            (total,) = add([terms[k]], block_rows, [gate_weight if k == 1 else up_weight])
+        if k == tp_count // 2:
+            gate_weight = fetch(gate_weight, [total])
         low = k & -k
         arrived = from_tp(total, low)
         terms[k ^ low].append((arrived, 0))
-    up_weight = fetch(up_weight, [total])
     down_weight = fetch(down_weight, [total])
     stream_terms = terms[0] + [(own_residual, 0)]
     stream, stream_out = add([stream_terms, stream_terms], block_rows, gains + [gate_weight, up_weight, down_weight])
@@ -398,16 +413,15 @@
 
     slots = list(reversed(range(tp_count)))
     active = activate(places, [blocks[k] for k in slots], gains, gate_weight, up_weight, [])
-    outs = project_down(places, active, row_weight, down_weight, slots, ep_count, cores, [])
-    swapped = [from_core(out[1]) for out in outs]
+    others = project_down(places, active, row_weight, down_weight, slots, ep_count, cores, 1, [])
+    swapped = [from_core(out) for out in others]
+    outs = project_down(places, active, row_weight, down_weight, slots, ep_count, cores, 0, others[:1])
     terms = [[] for _ in range(tp_count)]
-    arrivals = []
+    across = []
     for at, k in enumerate(slots):
-        before = arrivals[0] if len(arrivals) == 1 else arrivals[-2] if arrivals else []
-        pair = [[(outs[at][0], c * block_rows), (swapped[at], c * block_rows)] for c in range(chips)]
-        sums = add(pair, block_rows, before)
+        pair = [[(outs[at], c * block_rows), (swapped[at], c * block_rows)] for c in range(chips)]
+        sums = add(pair, block_rows, across)
         across = [from_chip(sums[c], chips - c) for c in range(1, chips)]
-        arrivals.append(across)
         terms[k] += [(value, 0) for value in [sums[0]] + across]
         if k:
             (total,) = add([terms[k]], block_rows)

time: 122 us -> 124 us (1.016)
  starting transfers between devices: 29.3 us -> 32.8 us
  waiting for transfers between devices: 53.8 us -> 52.4 us
    ppermute x9, starting transfers between devices: 12.7 us -> 16 us  [from_tp(): return lax.ppermute(value, 'tp', [(i, i ^ bits) for i in range(tp_count)])]
    ppermute x10, waiting for transfers between devices: 25.6 us -> 23.7 us  [from_chip(): lax.ppermute(value, 'ep', [(i, (i + step) % ep_count) for i in range(ep_c...]
    ppermute x9, waiting for transfers between devices: 25.5 us -> 27.2 us  [from_tp(): return lax.ppermute(value, 'tp', [(i, i ^ bits) for i in range(tp_count)])]
    pallas_call x1 -> x2, Pallas kernels: 2.7 us -> 3.41 us  [project_down(): pl.pallas_call(functools.partial(down_kernel, slots, column_blocks, cores...]
  transfers between devices with their start and end apart: 35 -> 35, of which waited for: 16 -> 17; matrix products, arithmetic and copies ran while one was open for 0% -> 0% of each run, Pallas kernels for 10% -> 11%
where the time goes in v10:
time: 124 us
  waiting for transfers between devices  52.4 us (42%)
  Pallas kernels  36.7 us (30%)
  starting transfers between devices  32.8 us (26%)
    ppermute x9, waiting for transfers between devices, from_tp(): return lax.ppermute(value, 'tp', [(i, i ^ bits) for i in range(tp_count)])  27.2 us
    ppermute x10, waiting for transfers between devices, from_chip(): lax.ppermute(value, 'ep', [(i, (i + step) % ep_count) for i in range(ep_c...  23.7 us
    ppermute x9, starting transfers between devices, from_tp(): return lax.ppermute(value, 'tp', [(i, i ^ bits) for i in range(tp_count)])  16 us
    ppermute x10, starting transfers between devices, from_chip(): lax.ppermute(value, 'ep', [(i, (i + step) % ep_count) for i in range(ep_c...  15.7 us
    pallas_call x1, Pallas kernels, attend(): pl.pallas_call(functools.partial(attention_kernel, step_rows, pieces), ou...  12.8 us
    pallas_call x4, Pallas kernels, fetch(): pl.pallas_call(functools.partial(fetch_kernel, parts), out_shape=pltpu.VM...  11.6 us
    pallas_call x1, Pallas kernels, activate(): pl.pallas_call(functools.partial(gate_kernel, row_blocks, column_blocks,...  4.78 us
    pallas_call x2, Pallas kernels, project_down(): pl.pallas_call(functools.partial(down_kernel, slots, column_blocks, cores...  3.41 us
  transfers between devices with their start and end apart: 35, of which 17 were waited for; matrix products, arithmetic and copies ran while one was open for 0% of the time, Pallas kernels for 11%

profile of v10, /device:TPU:0, one launch (start us, length us, event | category | flops | bytes accessed | tf_op | source)
XLA Modules:
  0.0 123.9 jit_solution(15897016946966538481)
XLA Ops:
  0.8 0.7 copy-done.2
  1.5 12.8 %attention.1.refs_1_.refs_0_ = bf16[64,1024]{1,0:T(8,128)(2,1)S(1)} custom-call(s32[64]{0:T(128)S(1)} %copy-done.2, bf16[64,8,512]{2,1,0:T(8,128)(2,1)} %q_ref.1, bf16[64,512]{1,0:T(8,128)(2,1)} %qr_ref.1, bf16[64,256,512]{2,1,0:T(8,128)(2,1)} %k_hbm.1, bf16[64,64,256]{2,1,0:T(8,128)(2,1)} %kr_hbm.1, bf16[8,512,128]{2,1,0:T(8,128)(2,1)} %up_ref.1, ...), custom_call_target="tpu_custom_call" | custom-call | flops 4294967296 | bytes 16777216 | tf_op jit(solution)/shard_map/attention/pallas_call | solution.py:127
  14.3 3.0 %collective-permute-start.1 = (bf16[64,1024]{1,0:T(8,128)(2,1)S(1)}, bf16[64,1024]{1,0:T(8,128)(2,1)S(1)}, u32[]{:S(2)}, u32[]{:S(2)}) collective-permute-start(bf16[64,1024]{1,0:T(8,128)(2,1)S(1)} %attention.1.refs_1_.refs_0_), channel_id=1, source_target_pairs={{0,8},{4,12},{8,0},{12,4},{1,9},{5,13},{9,1},{13,5},{2,10},{6,14},... | collective-permute-start | bytes 393224 | tf_op jit(solution)/shard_map/ppermute | solution.py:365
  17.5 3.3 %collective-permute-done.1.refs_2_ = bf16[64,1024]{1,0:T(8,128)(2,1)S(1)} collective-permute-done((bf16[64,1024]{1,0:T(8,128)(2,1)S(1)}, bf16[64,1024]{1,0:T(8,128)(2,1)S(1)}, u32[]{:S(2)}, u32[]{:S(2)}) %collective-permute-start.1) | collective-permute-done | bytes 131104 | tf_op jit(solution)/shard_map/ppermute | solution.py:365
  20.9 2.0 %fetch.4.refs_4_ = bf16[1024,1792]{1,0:T(8,128)(2,1)S(1)} custom-call(bf16[1024,1792]{1,0:T(8,128)(2,1)} %refs_0_.4, bf16[64,1024]{1,0:T(8,128)(2,1)S(1)} %attention.1.refs_1_.refs_0_, f32[256,1]{1,0:T(8,128)S(1)} %copy.16.refs_2_.row_weight, bf16[64,1792]{1,0:T(8,128)(2,1)S(1)} %constant_dynamic-slice_fusion.refs_3_.refs_7_, ...), custom_call_target="tpu_custom_call" | custom-call | bytes 7340032 | tf_op jit(solution)/shard_map/fetch/pallas_call | solution.py:38
  22.9 1.8 %projection.1 = (bf16[64,1792]{1,0:T(8,128)(2,1)S(1)}, bf16[64,1792]{1,0:T(8,128)(2,1)S(1)}, bf16[64,1792]{1,0:T(8,128)(2,1)S(1)}, bf16[64,1792]{1,0:T(8,128)(2,1)S(1)}) custom-call(s32[8]{0:T(128)S(1)} %stack.35.refs_0_.places, bf16[64,1024]{1,0:T(8,128)(2,1)S(1)} %attention.1.refs_1_.refs_0_, bf16[64,1024]{1,0:T(8,128)(2,1)S(1)} %collective-permute-done.refs_1_, ...), custom_call_target="tpu_custom_call" | custom-call | flops 939524096 | bytes 4194304 | tf_op jit(solution)/shard_map/projection/pallas_call | solution.py:190
  24.7 1.9 %collective-permute-start.3 = (bf16[64,1792]{1,0:T(8,128)(2,1)S(1)}, bf16[64,1792]{1,0:T(8,128)(2,1)S(1)}, u32[]{:S(2)}, u32[]{:S(2)}) collective-permute-start(bf16[64,1792]{1,0:T(8,128)(2,1)S(1)} %get-tuple-element.26), channel_id=1, source_target_pairs={{0,1},{1,0},{2,3},{3,2},{4,5},{5,4},{6,7},{7,6},{8,9},{9,8},{10,11... | collective-permute-start | bytes 688136 | tf_op jit(solution)/shard_map/ppermute | solution.py:368
  26.6 3.2 %fetch.5.refs_2_.refs_13_.refs_21_ = bf16[1,7168,512]{2,1,0:T(8,128)(2,1)S(1)} custom-call(bf16[1,7168,512]{2,1,0:T(8,128)(2,1)} %refs_0_.5, bf16[64,1792]{1,0:T(8,128)(2,1)S(1)} %get-tuple-element.24.refs_1_.refs_0_.refs_4_), custom_call_target="tpu_custom_call" | custom-call | bytes 14680064 | tf_op jit(solution)/shard_map/fetch/pallas_call | solution.py:38
  29.8 3.1 %collective-permute-done.3.refs_1_ = bf16[64,1792]{1,0:T(8,128)(2,1)S(1)} collective-permute-done((bf16[64,1792]{1,0:T(8,128)(2,1)S(1)}, bf16[64,1792]{1,0:T(8,128)(2,1)S(1)}, u32[]{:S(2)}, u32[]{:S(2)}) %collective-permute-start.3) | collective-permute-done | bytes 229408 | tf_op jit(solution)/shard_map/ppermute | solution.py:368
  32.9 2.8 %collective-permute-start.4 = (bf16[64,1792]{1,0:T(8,128)(2,1)S(1)}, bf16[64,1792]{1,0:T(8,128)(2,1)S(1)}, u32[]{:S(2)}, u32[]{:S(2)}) collective-permute-start(bf16[64,1792]{1,0:T(8,128)(2,1)S(1)} %add.60.refs_1_), channel_id=1, source_target_pairs={{0,2},{1,3},{2,0},{3,1},{4,6},{5,7},{6,4},{7,5},{8,10},{9,11},{10,... | collective-permute-start | bytes 688136 | tf_op jit(solution)/shard_map/ppermute | solution.py:368
  35.8 3.2 %fetch.6.refs_1_.refs_12_.refs_20_ = bf16[1,7168,512]{2,1,0:T(8,128)(2,1)S(1)} custom-call(bf16[1,7168,512]{2,1,0:T(8,128)(2,1)} %refs_0_.6, bf16[64,1792]{1,0:T(8,128)(2,1)S(1)} %add.60.refs_1_), custom_call_target="tpu_custom_call" | custom-call | bytes 14680064 | tf_op jit(solution)/shard_map/fetch/pallas_call | solution.py:38
  39.0 1.6 %collective-permute-start.5 = (bf16[64,1792]{1,0:T(8,128)(2,1)S(1)}, bf16[64,1792]{1,0:T(8,128)(2,1)S(1)}, u32[]{:S(2)}, u32[]{:S(2)}) collective-permute-start(bf16[64,1792]{1,0:T(8,128)(2,1)S(1)} %add.61.refs_1_), channel_id=1, source_target_pairs={{0,1},{1,0},{2,3},{3,2},{4,5},{5,4},{6,7},{7,6},{8,9},{9,8},{10,11... | collective-permute-start | bytes 688136 | tf_op jit(solution)/shard_map/ppermute | solution.py:368
  40.6 1.5 %collective-permute-start.7 = (f32[1,1792]{1,0:T(1,128)S(1)}, f32[1,1792]{1,0:T(1,128)S(1)}, u32[]{:S(2)}, u32[]{:S(2)}) collective-permute-start(f32[1,1792]{1,0:T(1,128)S(1)} %reshape.7.refs_4_.refs_8_.refs_16_), channel_id=1, source_target_pairs={{0,8},{4,12},{8,0},{12,4},{1,9},{5,13},{9,1},{13,5},{2,10},{6,14},... | collective-permute-start | bytes 21512 | tf_op jit(solution)/shard_map/ppermute | solution.py:365
  42.1 2.1 %collective-permute-done.7.refs_10_.refs_18_ = f32[1,1792]{1,0:T(1,128)S(1)} collective-permute-done((f32[1,1792]{1,0:T(1,128)S(1)}, f32[1,1792]{1,0:T(1,128)S(1)}, u32[]{:S(2)}, u32[]{:S(2)}) %collective-permute-start.7) | collective-permute-done | bytes 7200 | tf_op jit(solution)/shard_map/ppermute | solution.py:365
  44.3 3.2 %fetch.7.refs_14_.down = bf16[1,512,7168]{2,1,0:T(8,128)(2,1)S(1)} custom-call(bf16[1,512,7168]{2,1,0:T(8,128)(2,1)} %refs_0_.7, bf16[64,1792]{1,0:T(8,128)(2,1)S(1)} %add.61.refs_1_), custom_call_target="tpu_custom_call" | custom-call | bytes 14680064 | tf_op jit(solution)/shard_map/fetch/pallas_call | solution.py:38
  47.5 2.3 %collective-permute-done.5.refs_2_.refs_6_ = bf16[64,1792]{1,0:T(8,128)(2,1)S(1)} collective-permute-done((bf16[64,1792]{1,0:T(8,128)(2,1)S(1)}, bf16[64,1792]{1,0:T(8,128)(2,1)S(1)}, u32[]{:S(2)}, u32[]{:S(2)}) %collective-permute-start.5) | collective-permute-done | bytes 229408 | tf_op jit(solution)/shard_map/ppermute | solution.py:368
  49.7 0.8 add.62
  50.6 0.5 collective-permute-start.9
  51.1 1.5 %collective-permute-start.22 = (bf16[64,1792]{1,0:T(8,128)(2,1)S(1)}, bf16[64,1792]{1,0:T(8,128)(2,1)S(1)}, u32[]{:S(2)}, u32[]{:S(2)}) collective-permute-start(bf16[64,1792]{1,0:T(8,128)(2,1)S(1)} %get-tuple-element.29.refs_12_), channel_id=1, source_target_pairs={{0,8},{4,12},{8,0},{12,4},{1,9},{5,13},{9,1},{13,5},{2,10},{6,14},... | collective-permute-start | bytes 688136 | tf_op jit(solution)/shard_map/ppermute | solution.py:365
  52.6 2.5 %collective-permute-start.17 = (bf16[64,1792]{1,0:T(8,128)(2,1)S(1)}, bf16[64,1792]{1,0:T(8,128)(2,1)S(1)}, u32[]{:S(2)}, u32[]{:S(2)}) collective-permute-start(bf16[64,1792]{1,0:T(8,128)(2,1)S(1)} %get-tuple-element.29.refs_12_), channel_id=1, source_target_pairs={{0,1},{1,0},{2,3},{3,2},{4,5},{5,4},{6,7},{7,6},{8,9},{9,8},{10,11... | collective-permute-start | bytes 688136 | tf_op jit(solution)/shard_map/ppermute | solution.py:368
  55.1 7.3 %collective-permute-done.9.refs_4_ = bf16[64,1792]{1,0:T(8,128)(2,1)S(1)} collective-permute-done((bf16[64,1792]{1,0:T(8,128)(2,1)S(1)}, bf16[64,1792]{1,0:T(8,128)(2,1)S(1)}, u32[]{:S(2)}, u32[]{:S(2)}) %collective-permute-start.9) | collective-permute-done | bytes 229408 | tf_op jit(solution)/shard_map/ppermute | solution.py:368
  62.3 1.3 %collective-permute-done.17.refs_8_ = bf16[64,1792]{1,0:T(8,128)(2,1)S(1)} collective-permute-done((bf16[64,1792]{1,0:T(8,128)(2,1)S(1)}, bf16[64,1792]{1,0:T(8,128)(2,1)S(1)}, u32[]{:S(2)}, u32[]{:S(2)}) %collective-permute-start.17) | collective-permute-done | bytes 229408 | tf_op jit(solution)/shard_map/ppermute | solution.py:368
  63.6 0.6 collective-permute-start.19
  64.2 1.4 %collective-permute-start.15 = (bf16[64,1792]{1,0:T(8,128)(2,1)S(1)}, bf16[64,1792]{1,0:T(8,128)(2,1)S(1)}, u32[]{:S(2)}, u32[]{:S(2)}) collective-permute-start(bf16[64,1792]{1,0:T(8,128)(2,1)S(1)} %collective-permute-done.9.refs_4_), channel_id=1, source_target_pairs={{0,8},{4,12},{8,0},{12,4},{1,9},{5,13},{9,1},{13,5},{2,10},{6,14},... | collective-permute-start | bytes 688136 | tf_op jit(solution)/shard_map/ppermute | solution.py:365
  65.7 4.1 %collective-permute-done.10.refs_0_ = bf16[64,1792]{1,0:T(8,128)(2,1)S(1)} collective-permute-done((bf16[64,1792]{1,0:T(8,128)(2,1)S(1)}, bf16[64,1792]{1,0:T(8,128)(2,1)S(1)}, u32[]{:S(2)}, u32[]{:S(2)}) %collective-permute-start.10) | collective-permute-done | bytes 229408 | tf_op jit(solution)/shard_map/ppermute | solution.py:368
  69.8 1.5 %collective-permute-start.12 = (bf16[64,1792]{1,0:T(8,128)(2,1)S(1)}, bf16[64,1792]{1,0:T(8,128)(2,1)S(1)}, u32[]{:S(2)}, u32[]{:S(2)}) collective-permute-start(bf16[64,1792]{1,0:T(8,128)(2,1)S(1)} %collective-permute-done.10.refs_0_), channel_id=1, source_target_pairs={{0,8},{4,12},{8,0},{12,4},{1,9},{5,13},{9,1},{13,5},{2,10},{6,14},... | collective-permute-start | bytes 688136 | tf_op jit(solution)/shard_map/ppermute | solution.py:365
  71.3 0.9 collective-permute-done.19.refs_10_
  72.2 0.5 collective-permute-start.20
  72.7 4.4 %collective-permute-done.15.refs_6_ = bf16[64,1792]{1,0:T(8,128)(2,1)S(1)} collective-permute-done((bf16[64,1792]{1,0:T(8,128)(2,1)S(1)}, bf16[64,1792]{1,0:T(8,128)(2,1)S(1)}, u32[]{:S(2)}, u32[]{:S(2)}) %collective-permute-start.15) | collective-permute-done | bytes 229408 | tf_op jit(solution)/shard_map/ppermute | solution.py:365
  77.1 3.1 %collective-permute-done.12.refs_2_ = bf16[64,1792]{1,0:T(8,128)(2,1)S(1)} collective-permute-done((bf16[64,1792]{1,0:T(8,128)(2,1)S(1)}, bf16[64,1792]{1,0:T(8,128)(2,1)S(1)}, u32[]{:S(2)}, u32[]{:S(2)}) %collective-permute-start.12) | collective-permute-done | bytes 229408 | tf_op jit(solution)/shard_map/ppermute | solution.py:365
  80.2 1.5 %collective-permute-done.13.refs_3_ = bf16[64,1792]{1,0:T(8,128)(2,1)S(1)} collective-permute-done((bf16[64,1792]{1,0:T(8,128)(2,1)S(1)}, bf16[64,1792]{1,0:T(8,128)(2,1)S(1)}, u32[]{:S(2)}, u32[]{:S(2)}) %collective-permute-start.13) | collective-permute-done | bytes 229408 | tf_op jit(solution)/shard_map/ppermute | solution.py:361
  81.7 4.8 %activate.1.active = bf16[256,512]{1,0:T(8,128)(2,1)S(1)} custom-call(s32[8]{0:T(128)S(1)} %stack.35.refs_0_.places, bf16[64,1792]{1,0:T(8,128)(2,1)S(1)} %collective-permute-done.10.refs_0_, bf16[64,1792]{1,0:T(8,128)(2,1)S(1)} %collective-permute-done.11.refs_1_, bf16[64,1792]{1,0:T(8,128)(2,1)S(1)} %collective-permute-done.12.refs_2_, ...), custom_call_target="tpu_custom_call" | custom-call | flops 3758096384 | bytes 14680064 | tf_op jit(solution)/shard_map/activate/pallas_call | solution.py:243
  86.4 1.7 %down.2 = (bf16[128,1792]{1,0:T(8,128)(2,1)S(1)}, bf16[128,1792]{1,0:T(8,128)(2,1)S(1)}, bf16[128,1792]{1,0:T(8,128)(2,1)S(1)}, bf16[128,1792]{1,0:T(8,128)(2,1)S(1)}) custom-call(s32[8]{0:T(128)S(1)} %stack.35.refs_0_.places, bf16[256,512]{1,0:T(8,128)(2,1)S(1)} %activate.1.active, f32[256,1]{1,0:T(8,128)S(1)} %copy.16.refs_2_.row_weight, ...), custom_call_target="tpu_custom_call" | custom-call | flops 939524096 | bytes 3670016 | tf_op jit(solution)/shard_map/down/pallas_call | solution.py:292
  88.7 1.7 %down.3 = (bf16[128,1792]{1,0:T(8,128)(2,1)S(1)}, bf16[128,1792]{1,0:T(8,128)(2,1)S(1)}, bf16[128,1792]{1,0:T(8,128)(2,1)S(1)}, bf16[128,1792]{1,0:T(8,128)(2,1)S(1)}) custom-call(s32[8]{0:T(128)S(1)} %stack.35.refs_0_.places, bf16[256,512]{1,0:T(8,128)(2,1)S(1)} %activate.1.active, f32[256,1]{1,0:T(8,128)S(1)} %copy.16.refs_2_.row_weight, ...), custom_call_target="tpu_custom_call" | custom-call | flops 939524096 | bytes 3670016 | tf_op jit(solution)/shard_map/down/pallas_call | solution.py:292
  90.6 1.5 %collective-permute-start.25 = (bf16[64,1792]{1,0:T(8,128)(2,1)S(1)}, bf16[64,1792]{1,0:T(8,128)(2,1)S(1)}, u32[]{:S(2)}, u32[]{:S(2)}) collective-permute-start(bf16[64,1792]{1,0:T(8,128)(2,1)S(1)} %get-tuple-element.33), channel_id=1, source_target_pairs={{0,8},{4,12},{8,0},{12,4},{1,9},{5,13},{9,1},{13,5},{2,10},{6,14},... | collective-permute-start | bytes 688136 | tf_op jit(solution)/shard_map/ppermute | solution.py:365
  92.1 6.2 %collective-permute-done.25.refs_1_.refs_4_ = bf16[64,1792]{1,0:T(8,128)(2,1)S(1)} collective-permute-done((bf16[64,1792]{1,0:T(8,128)(2,1)S(1)}, bf16[64,1792]{1,0:T(8,128)(2,1)S(1)}, u32[]{:S(2)}, u32[]{:S(2)}) %collective-permute-start.25) | collective-permute-done | bytes 229408 | tf_op jit(solution)/shard_map/ppermute | solution.py:365
  98.4 1.6 %collective-permute-start.28 = (bf16[64,1792]{1,0:T(8,128)(2,1)S(1)}, bf16[64,1792]{1,0:T(8,128)(2,1)S(1)}, u32[]{:S(2)}, u32[]{:S(2)}) collective-permute-start(bf16[64,1792]{1,0:T(8,128)(2,1)S(1)} %get-tuple-element.37), channel_id=1, source_target_pairs={{0,8},{4,12},{8,0},{12,4},{1,9},{5,13},{9,1},{13,5},{2,10},{6,14},... | collective-permute-start | bytes 688136 | tf_op jit(solution)/shard_map/ppermute | solution.py:365
  100.0 2.1 %collective-permute-start.26 = (bf16[64,1792]{1,0:T(8,128)(2,1)S(1)}, bf16[64,1792]{1,0:T(8,128)(2,1)S(1)}, u32[]{:S(2)}, u32[]{:S(2)}) collective-permute-start(bf16[64,1792]{1,0:T(8,128)(2,1)S(1)} %add.64), channel_id=1, source_target_pairs={{0,1},{1,0},{2,3},{3,2},{4,5},{5,4},{6,7},{7,6},{8,9},{9,8},{10,11... | collective-permute-start | bytes 688136 | tf_op jit(solution)/shard_map/ppermute | solution.py:368
  102.1 3.2 %collective-permute-done.28.refs_2_.refs_4_ = bf16[64,1792]{1,0:T(8,128)(2,1)S(1)} collective-permute-done((bf16[64,1792]{1,0:T(8,128)(2,1)S(1)}, bf16[64,1792]{1,0:T(8,128)(2,1)S(1)}, u32[]{:S(2)}, u32[]{:S(2)}) %collective-permute-start.28) | collective-permute-done | bytes 229408 | tf_op jit(solution)/shard_map/ppermute | solution.py:365
  105.4 1.6 %collective-permute-start.31 = (bf16[64,1792]{1,0:T(8,128)(2,1)S(1)}, bf16[64,1792]{1,0:T(8,128)(2,1)S(1)}, u32[]{:S(2)}, u32[]{:S(2)}) collective-permute-start(bf16[64,1792]{1,0:T(8,128)(2,1)S(1)} %get-tuple-element.41), channel_id=1, source_target_pairs={{0,8},{4,12},{8,0},{12,4},{1,9},{5,13},{9,1},{13,5},{2,10},{6,14},... | collective-permute-start | bytes 688136 | tf_op jit(solution)/shard_map/ppermute | solution.py:365
  107.0 1.4 %collective-permute-done.26.refs_0_ = bf16[64,1792]{1,0:T(8,128)(2,1)S(1)} collective-permute-done((bf16[64,1792]{1,0:T(8,128)(2,1)S(1)}, bf16[64,1792]{1,0:T(8,128)(2,1)S(1)}, u32[]{:S(2)}, u32[]{:S(2)}) %collective-permute-start.26) | collective-permute-done | bytes 229408 | tf_op jit(solution)/shard_map/ppermute | solution.py:368
  108.5 2.5 %collective-permute-start.29 = (bf16[64,1792]{1,0:T(8,128)(2,1)S(1)}, bf16[64,1792]{1,0:T(8,128)(2,1)S(1)}, u32[]{:S(2)}, u32[]{:S(2)}) collective-permute-start(bf16[64,1792]{1,0:T(8,128)(2,1)S(1)} %add.66), channel_id=1, source_target_pairs={{0,2},{1,3},{2,0},{3,1},{4,6},{5,7},{6,4},{7,5},{8,10},{9,11},{10,... | collective-permute-start | bytes 688136 | tf_op jit(solution)/shard_map/ppermute | solution.py:368
  111.0 0.5 collective-permute-done.31.refs_1_.refs_4_
  111.6 1.6 %collective-permute-start.34 = (bf16[64,1792]{1,0:T(8,128)(2,1)S(1)}, bf16[64,1792]{1,0:T(8,128)(2,1)S(1)}, u32[]{:S(2)}, u32[]{:S(2)}) collective-permute-start(bf16[64,1792]{1,0:T(8,128)(2,1)S(1)} %get-tuple-element.45), channel_id=1, source_target_pairs={{0,8},{4,12},{8,0},{12,4},{1,9},{5,13},{9,1},{13,5},{2,10},{6,14},... | collective-permute-start | bytes 688136 | tf_op jit(solution)/shard_map/ppermute | solution.py:365
  113.2 2.1 %collective-permute-start.32 = (bf16[64,1792]{1,0:T(8,128)(2,1)S(1)}, bf16[64,1792]{1,0:T(8,128)(2,1)S(1)}, u32[]{:S(2)}, u32[]{:S(2)}) collective-permute-start(bf16[64,1792]{1,0:T(8,128)(2,1)S(1)} %add.68), channel_id=1, source_target_pairs={{0,1},{1,0},{2,3},{3,2},{4,5},{5,4},{6,7},{7,6},{8,9},{9,8},{10,11... | collective-permute-start | bytes 688136 | tf_op jit(solution)/shard_map/ppermute | solution.py:368
  115.3 6.6 %collective-permute-done.29.refs_0_ = bf16[64,1792]{1,0:T(8,128)(2,1)S(1)} collective-permute-done((bf16[64,1792]{1,0:T(8,128)(2,1)S(1)}, bf16[64,1792]{1,0:T(8,128)(2,1)S(1)}, u32[]{:S(2)}, u32[]{:S(2)}) %collective-permute-start.29) | collective-permute-done | bytes 229408 | tf_op jit(solution)/shard_map/ppermute | solution.py:368
  121.9 1.2 collective-permute-done.32.refs_1_
  123.1 0.8 add.70
  (59 shorter events, 1.7 us)
Async XLA Ops:
  0.6 20.2 %copy-start = (bf16[256,1792]{1,0:T(8,128)(2,1)S(1)}, bf16[256,1792]{1,0:T(8,128)(2,1)}, u32[]{:S(2)}) copy-start(bf16[256,1792]{1,0:T(8,128)(2,1)} %param.21) | copy-start | bytes 2752516
  0.8 0.7 copy-start.2
  1.5 15.8 %copy-start.3 = (f32[1792]{0:T(1024)S(1)}, f32[1792]{0:T(1024)}, u32[]{:S(2)}) copy-start(f32[1792]{0:T(1024)} %param.22) | copy-start | bytes 21508
  1.5 15.8 %copy-start.4 = (f32[256,2]{0,1:T(2,128)S(1)}, f32[256,2]{0,1:T(2,128)}, u32[]{:S(2)}) copy-start(f32[256,2]{0,1:T(2,128)} %param.24) | copy-start | bytes 6148
  1.5 15.8 %copy-start.5 = (s32[256,2]{0,1:T(2,128)S(1)}, s32[256,2]{0,1:T(2,128)}, u32[]{:S(2)}) copy-start(s32[256,2]{0,1:T(2,128)} %param.23) | copy-start | bytes 6148
  14.3 6.5 %collective-permute-start.1 = (bf16[64,1024]{1,0:T(8,128)(2,1)S(1)}, bf16[64,1024]{1,0:T(8,128)(2,1)S(1)}, u32[]{:S(2)}, u32[]{:S(2)}) collective-permute-start(bf16[64,1024]{1,0:T(8,128)(2,1)S(1)} %attention.1.refs_1_.refs_0_), channel_id=1, source_target_pairs={{0,8},{4,12},{8,0},{12,4},{1,9},{5,13},{9,1},{13,5},{2,10},{6,14},... | collective-permute-start | bytes 393224 | tf_op jit(solution)/shard_map/ppermute | solution.py:365
  17.3 5.6 %collective-permute-start = (bf16[64,1024]{1,0:T(8,128)(2,1)S(1)}, bf16[64,1024]{1,0:T(8,128)(2,1)S(1)}, u32[]{:S(2)}, u32[]{:S(2)}) collective-permute-start(bf16[64,1024]{1,0:T(8,128)(2,1)S(1)} %attention.1.refs_1_.refs_0_), channel_id=1, source_target_pairs={{0,4},{4,0},{8,12},{12,8},{1,5},{5,1},{9,13},{13,9},{2,6},{6,2},{1... | collective-permute-start | bytes 393224 | tf_op jit(solution)/shard_map/ppermute | solution.py:361
  20.8 2.1 %collective-permute-start.2 = (bf16[64,1024]{1,0:T(8,128)(2,1)S(1)}, bf16[64,1024]{1,0:T(8,128)(2,1)S(1)}, u32[]{:S(2)}, u32[]{:S(2)}) collective-permute-start(bf16[64,1024]{1,0:T(8,128)(2,1)S(1)} %collective-permute-done.1.refs_2_), channel_id=1, source_target_pairs={{0,4},{4,0},{8,12},{12,8},{1,5},{5,1},{9,13},{13,9},{2,6},{6,2},{1... | collective-permute-start | bytes 393224 | tf_op jit(solution)/shard_map/ppermute | solution.py:361
  24.7 8.2 %collective-permute-start.3 = (bf16[64,1792]{1,0:T(8,128)(2,1)S(1)}, bf16[64,1792]{1,0:T(8,128)(2,1)S(1)}, u32[]{:S(2)}, u32[]{:S(2)}) collective-permute-start(bf16[64,1792]{1,0:T(8,128)(2,1)S(1)} %get-tuple-element.26), channel_id=1, source_target_pairs={{0,1},{1,0},{2,3},{3,2},{4,5},{5,4},{6,7},{7,6},{8,9},{9,8},{10,11... | collective-permute-start | bytes 688136 | tf_op jit(solution)/shard_map/ppermute | solution.py:368
  32.9 14.5 %collective-permute-start.4 = (bf16[64,1792]{1,0:T(8,128)(2,1)S(1)}, bf16[64,1792]{1,0:T(8,128)(2,1)S(1)}, u32[]{:S(2)}, u32[]{:S(2)}) collective-permute-start(bf16[64,1792]{1,0:T(8,128)(2,1)S(1)} %add.60.refs_1_), channel_id=1, source_target_pairs={{0,2},{1,3},{2,0},{3,1},{4,6},{5,7},{6,4},{7,5},{8,10},{9,11},{10,... | collective-permute-start | bytes 688136 | tf_op jit(solution)/shard_map/ppermute | solution.py:368
  39.0 10.8 %collective-permute-start.5 = (bf16[64,1792]{1,0:T(8,128)(2,1)S(1)}, bf16[64,1792]{1,0:T(8,128)(2,1)S(1)}, u32[]{:S(2)}, u32[]{:S(2)}) collective-permute-start(bf16[64,1792]{1,0:T(8,128)(2,1)S(1)} %add.61.refs_1_), channel_id=1, source_target_pairs={{0,1},{1,0},{2,3},{3,2},{4,5},{5,4},{6,7},{7,6},{8,9},{9,8},{10,11... | collective-permute-start | bytes 688136 | tf_op jit(solution)/shard_map/ppermute | solution.py:368
  40.6 3.6 %collective-permute-start.7 = (f32[1,1792]{1,0:T(1,128)S(1)}, f32[1,1792]{1,0:T(1,128)S(1)}, u32[]{:S(2)}, u32[]{:S(2)}) collective-permute-start(f32[1,1792]{1,0:T(1,128)S(1)} %reshape.7.refs_4_.refs_8_.refs_16_), channel_id=1, source_target_pairs={{0,8},{4,12},{8,0},{12,4},{1,9},{5,13},{9,1},{13,5},{2,10},{6,14},... | collective-permute-start | bytes 21512 | tf_op jit(solution)/shard_map/ppermute | solution.py:365
  42.1 5.3 %collective-permute-start.6 = (f32[1,1792]{1,0:T(1,128)S(1)}, f32[1,1792]{1,0:T(1,128)S(1)}, u32[]{:S(2)}, u32[]{:S(2)}) collective-permute-start(f32[1,1792]{1,0:T(1,128)S(1)} %reshape.7.refs_4_.refs_8_.refs_16_), channel_id=1, source_target_pairs={{0,4},{4,0},{8,12},{12,8},{1,5},{5,1},{9,13},{13,9},{2,6},{6,2},{1... | collective-permute-start | bytes 21512 | tf_op jit(solution)/shard_map/ppermute | solution.py:361
  44.3 3.2 %collective-permute-start.8 = (f32[1,1792]{1,0:T(1,128)S(1)}, f32[1,1792]{1,0:T(1,128)S(1)}, u32[]{:S(2)}, u32[]{:S(2)}) collective-permute-start(f32[1,1792]{1,0:T(1,128)S(1)} %collective-permute-done.7.refs_10_.refs_18_), channel_id=1, source_target_pairs={{0,4},{4,0},{8,12},{12,8},{1,5},{5,1},{9,13},{13,9},{2,6},{6,2},{1... | collective-permute-start | bytes 21512 | tf_op jit(solution)/shard_map/ppermute | solution.py:361
  50.6 11.7 %collective-permute-start.9 = (bf16[64,1792]{1,0:T(8,128)(2,1)S(1)}, bf16[64,1792]{1,0:T(8,128)(2,1)S(1)}, u32[]{:S(2)}, u32[]{:S(2)}) collective-permute-start(bf16[64,1792]{1,0:T(8,128)(2,1)S(1)} %get-tuple-element.29.refs_12_), channel_id=1, source_target_pairs={{0,2},{1,3},{2,0},{3,1},{4,6},{5,7},{6,4},{7,5},{8,10},{9,11},{10,... | collective-permute-start | bytes 688136 | tf_op jit(solution)/shard_map/ppermute | solution.py:368
  51.1 11.2 %collective-permute-start.22 = (bf16[64,1792]{1,0:T(8,128)(2,1)S(1)}, bf16[64,1792]{1,0:T(8,128)(2,1)S(1)}, u32[]{:S(2)}, u32[]{:S(2)}) collective-permute-start(bf16[64,1792]{1,0:T(8,128)(2,1)S(1)} %get-tuple-element.29.refs_12_), channel_id=1, source_target_pairs={{0,8},{4,12},{8,0},{12,4},{1,9},{5,13},{9,1},{13,5},{2,10},{6,14},... | collective-permute-start | bytes 688136 | tf_op jit(solution)/shard_map/ppermute | solution.py:365
  52.6 11.1 %collective-permute-start.17 = (bf16[64,1792]{1,0:T(8,128)(2,1)S(1)}, bf16[64,1792]{1,0:T(8,128)(2,1)S(1)}, u32[]{:S(2)}, u32[]{:S(2)}) collective-permute-start(bf16[64,1792]{1,0:T(8,128)(2,1)S(1)} %get-tuple-element.29.refs_12_), channel_id=1, source_target_pairs={{0,1},{1,0},{2,3},{3,2},{4,5},{5,4},{6,7},{7,6},{8,9},{9,8},{10,11... | collective-permute-start | bytes 688136 | tf_op jit(solution)/shard_map/ppermute | solution.py:368
  55.1 9.2 %collective-permute-start.21 = (bf16[64,1792]{1,0:T(8,128)(2,1)S(1)}, bf16[64,1792]{1,0:T(8,128)(2,1)S(1)}, u32[]{:S(2)}, u32[]{:S(2)}) collective-permute-start(bf16[64,1792]{1,0:T(8,128)(2,1)S(1)} %get-tuple-element.29.refs_12_), channel_id=1, source_target_pairs={{0,4},{4,0},{8,12},{12,8},{1,5},{5,1},{9,13},{13,9},{2,6},{6,2},{1... | collective-permute-start | bytes 688136 | tf_op jit(solution)/shard_map/ppermute | solution.py:361
  62.3 7.5 %collective-permute-start.10 = (bf16[64,1792]{1,0:T(8,128)(2,1)S(1)}, bf16[64,1792]{1,0:T(8,128)(2,1)S(1)}, u32[]{:S(2)}, u32[]{:S(2)}) collective-permute-start(bf16[64,1792]{1,0:T(8,128)(2,1)S(1)} %collective-permute-done.9.refs_4_), channel_id=1, source_target_pairs={{0,1},{1,0},{2,3},{3,2},{4,5},{5,4},{6,7},{7,6},{8,9},{9,8},{10,11... | collective-permute-start | bytes 688136 | tf_op jit(solution)/shard_map/ppermute | solution.py:368
  62.3 9.0 %collective-permute-start.23 = (bf16[64,1792]{1,0:T(8,128)(2,1)S(1)}, bf16[64,1792]{1,0:T(8,128)(2,1)S(1)}, u32[]{:S(2)}, u32[]{:S(2)}) collective-permute-start(bf16[64,1792]{1,0:T(8,128)(2,1)S(1)} %collective-permute-done.22.refs_14_), channel_id=1, source_target_pairs={{0,4},{4,0},{8,12},{12,8},{1,5},{5,1},{9,13},{13,9},{2,6},{6,2},{1... | collective-permute-start | bytes 688136 | tf_op jit(solution)/shard_map/ppermute | solution.py:361
  63.6 8.5 %collective-permute-start.19 = (bf16[64,1792]{1,0:T(8,128)(2,1)S(1)}, bf16[64,1792]{1,0:T(8,128)(2,1)S(1)}, u32[]{:S(2)}, u32[]{:S(2)}) collective-permute-start(bf16[64,1792]{1,0:T(8,128)(2,1)S(1)} %collective-permute-done.17.refs_8_), channel_id=1, source_target_pairs={{0,8},{4,12},{8,0},{12,4},{1,9},{5,13},{9,1},{13,5},{2,10},{6,14},... | collective-permute-start | bytes 688136 | tf_op jit(solution)/shard_map/ppermute | solution.py:365
  64.2 8.0 %collective-permute-start.18 = (bf16[64,1792]{1,0:T(8,128)(2,1)S(1)}, bf16[64,1792]{1,0:T(8,128)(2,1)S(1)}, u32[]{:S(2)}, u32[]{:S(2)}) collective-permute-start(bf16[64,1792]{1,0:T(8,128)(2,1)S(1)} %collective-permute-done.17.refs_8_), channel_id=1, source_target_pairs={{0,4},{4,0},{8,12},{12,8},{1,5},{5,1},{9,13},{13,9},{2,6},{6,2},{1... | collective-permute-start | bytes 688136 | tf_op jit(solution)/shard_map/ppermute | solution.py:361
  64.2 12.9 %collective-permute-start.15 = (bf16[64,1792]{1,0:T(8,128)(2,1)S(1)}, bf16[64,1792]{1,0:T(8,128)(2,1)S(1)}, u32[]{:S(2)}, u32[]{:S(2)}) collective-permute-start(bf16[64,1792]{1,0:T(8,128)(2,1)S(1)} %collective-permute-done.9.refs_4_), channel_id=1, source_target_pairs={{0,8},{4,12},{8,0},{12,4},{1,9},{5,13},{9,1},{13,5},{2,10},{6,14},... | collective-permute-start | bytes 688136 | tf_op jit(solution)/shard_map/ppermute | solution.py:365
  69.8 10.4 %collective-permute-start.12 = (bf16[64,1792]{1,0:T(8,128)(2,1)S(1)}, bf16[64,1792]{1,0:T(8,128)(2,1)S(1)}, u32[]{:S(2)}, u32[]{:S(2)}) collective-permute-start(bf16[64,1792]{1,0:T(8,128)(2,1)S(1)} %collective-permute-done.10.refs_0_), channel_id=1, source_target_pairs={{0,8},{4,12},{8,0},{12,4},{1,9},{5,13},{9,1},{13,5},{2,10},{6,14},... | collective-permute-start | bytes 688136 | tf_op jit(solution)/shard_map/ppermute | solution.py:365
  71.3 8.9 %collective-permute-start.14 = (bf16[64,1792]{1,0:T(8,128)(2,1)S(1)}, bf16[64,1792]{1,0:T(8,128)(2,1)S(1)}, u32[]{:S(2)}, u32[]{:S(2)}) collective-permute-start(bf16[64,1792]{1,0:T(8,128)(2,1)S(1)} %collective-permute-done.9.refs_4_), channel_id=1, source_target_pairs={{0,4},{4,0},{8,12},{12,8},{1,5},{5,1},{9,13},{13,9},{2,6},{6,2},{1... | collective-permute-start | bytes 688136 | tf_op jit(solution)/shard_map/ppermute | solution.py:361
  72.2 8.0 %collective-permute-start.11 = (bf16[64,1792]{1,0:T(8,128)(2,1)S(1)}, bf16[64,1792]{1,0:T(8,128)(2,1)S(1)}, u32[]{:S(2)}, u32[]{:S(2)}) collective-permute-start(bf16[64,1792]{1,0:T(8,128)(2,1)S(1)} %collective-permute-done.10.refs_0_), channel_id=1, source_target_pairs={{0,4},{4,0},{8,12},{12,8},{1,5},{5,1},{9,13},{13,9},{2,6},{6,2},{1... | collective-permute-start | bytes 688136 | tf_op jit(solution)/shard_map/ppermute | solution.py:361
  72.2 8.0 %collective-permute-start.20 = (bf16[64,1792]{1,0:T(8,128)(2,1)S(1)}, bf16[64,1792]{1,0:T(8,128)(2,1)S(1)}, u32[]{:S(2)}, u32[]{:S(2)}) collective-permute-start(bf16[64,1792]{1,0:T(8,128)(2,1)S(1)} %collective-permute-done.19.refs_10_), channel_id=1, source_target_pairs={{0,4},{4,0},{8,12},{12,8},{1,5},{5,1},{9,13},{13,9},{2,6},{6,2},{1... | collective-permute-start | bytes 688136 | tf_op jit(solution)/shard_map/ppermute | solution.py:361
  77.1 3.1 %collective-permute-start.16 = (bf16[64,1792]{1,0:T(8,128)(2,1)S(1)}, bf16[64,1792]{1,0:T(8,128)(2,1)S(1)}, u32[]{:S(2)}, u32[]{:S(2)}) collective-permute-start(bf16[64,1792]{1,0:T(8,128)(2,1)S(1)} %collective-permute-done.15.refs_6_), channel_id=1, source_target_pairs={{0,4},{4,0},{8,12},{12,8},{1,5},{5,1},{9,13},{13,9},{2,6},{6,2},{1... | collective-permute-start | bytes 688136 | tf_op jit(solution)/shard_map/ppermute | solution.py:361
  80.2 1.5 %collective-permute-start.13 = (bf16[64,1792]{1,0:T(8,128)(2,1)S(1)}, bf16[64,1792]{1,0:T(8,128)(2,1)S(1)}, u32[]{:S(2)}, u32[]{:S(2)}) collective-permute-start(bf16[64,1792]{1,0:T(8,128)(2,1)S(1)} %collective-permute-done.12.refs_2_), channel_id=1, source_target_pairs={{0,4},{4,0},{8,12},{12,8},{1,5},{5,1},{9,13},{13,9},{2,6},{6,2},{1... | collective-permute-start | bytes 688136 | tf_op jit(solution)/shard_map/ppermute | solution.py:361
  88.2 2.3 %collective-permute-start.24 = (bf16[128,1792]{1,0:T(8,128)(2,1)S(1)}, bf16[128,1792]{1,0:T(8,128)(2,1)S(1)}, u32[]{:S(2)}, u32[]{:S(2)}) collective-permute-start(bf16[128,1792]{1,0:T(8,128)(2,1)S(1)} %get-tuple-element.30.refs_0_), channel_id=1, source_target_pairs={{0,4},{4,0},{8,12},{12,8},{1,5},{5,1},{9,13},{13,9},{2,6},{6,2},{1... | collective-permute-start | bytes 1376264 | tf_op jit(solution)/shard_map/ppermute | solution.py:361
  88.4 3.8 %collective-permute-start.27 = (bf16[128,1792]{1,0:T(8,128)(2,1)S(1)}, bf16[128,1792]{1,0:T(8,128)(2,1)S(1)}, u32[]{:S(2)}, u32[]{:S(2)}) collective-permute-start(bf16[128,1792]{1,0:T(8,128)(2,1)S(1)} %get-tuple-element.35), channel_id=1, source_target_pairs={{0,4},{4,0},{8,12},{12,8},{1,5},{5,1},{9,13},{13,9},{2,6},{6,2},{1... | collective-permute-start | bytes 1376264 | tf_op jit(solution)/shard_map/ppermute | solution.py:361
  88.7 35.2 %copy-start.1 = (bf16[256,1792]{1,0:T(8,128)(2,1)S(1)}, bf16[256,1792]{1,0:T(8,128)(2,1)}, u32[]{:S(2)}) copy-start(bf16[256,1792]{1,0:T(8,128)(2,1)} %param.21) | copy-start | bytes 2752516
  90.6 7.7 %collective-permute-start.25 = (bf16[64,1792]{1,0:T(8,128)(2,1)S(1)}, bf16[64,1792]{1,0:T(8,128)(2,1)S(1)}, u32[]{:S(2)}, u32[]{:S(2)}) collective-permute-start(bf16[64,1792]{1,0:T(8,128)(2,1)S(1)} %get-tuple-element.33), channel_id=1, source_target_pairs={{0,8},{4,12},{8,0},{12,4},{1,9},{5,13},{9,1},{13,5},{2,10},{6,14},... | collective-permute-start | bytes 688136 | tf_op jit(solution)/shard_map/ppermute | solution.py:365
  92.1 10.0 %collective-permute-start.30 = (bf16[128,1792]{1,0:T(8,128)(2,1)S(1)}, bf16[128,1792]{1,0:T(8,128)(2,1)S(1)}, u32[]{:S(2)}, u32[]{:S(2)}) collective-permute-start(bf16[128,1792]{1,0:T(8,128)(2,1)S(1)} %get-tuple-element.39), channel_id=1, source_target_pairs={{0,4},{4,0},{8,12},{12,8},{1,5},{5,1},{9,13},{13,9},{2,6},{6,2},{1... | collective-permute-start | bytes 1376264 | tf_op jit(solution)/shard_map/ppermute | solution.py:361
  98.4 6.9 %collective-permute-start.28 = (bf16[64,1792]{1,0:T(8,128)(2,1)S(1)}, bf16[64,1792]{1,0:T(8,128)(2,1)S(1)}, u32[]{:S(2)}, u32[]{:S(2)}) collective-permute-start(bf16[64,1792]{1,0:T(8,128)(2,1)S(1)} %get-tuple-element.37), channel_id=1, source_target_pairs={{0,8},{4,12},{8,0},{12,4},{1,9},{5,13},{9,1},{13,5},{2,10},{6,14},... | collective-permute-start | bytes 688136 | tf_op jit(solution)/shard_map/ppermute | solution.py:365
  100.0 11.0 %collective-permute-start.33 = (bf16[128,1792]{1,0:T(8,128)(2,1)S(1)}, bf16[128,1792]{1,0:T(8,128)(2,1)S(1)}, u32[]{:S(2)}, u32[]{:S(2)}) collective-permute-start(bf16[128,1792]{1,0:T(8,128)(2,1)S(1)} %get-tuple-element.43), channel_id=1, source_target_pairs={{0,4},{4,0},{8,12},{12,8},{1,5},{5,1},{9,13},{13,9},{2,6},{6,2},{1... | collective-permute-start | bytes 1376264 | tf_op jit(solution)/shard_map/ppermute | solution.py:361
  100.0 8.4 %collective-permute-start.26 = (bf16[64,1792]{1,0:T(8,128)(2,1)S(1)}, bf16[64,1792]{1,0:T(8,128)(2,1)S(1)}, u32[]{:S(2)}, u32[]{:S(2)}) collective-permute-start(bf16[64,1792]{1,0:T(8,128)(2,1)S(1)} %add.64), channel_id=1, source_target_pairs={{0,1},{1,0},{2,3},{3,2},{4,5},{5,4},{6,7},{7,6},{8,9},{9,8},{10,11... | collective-permute-start | bytes 688136 | tf_op jit(solution)/shard_map/ppermute | solution.py:368
  105.4 6.1 %collective-permute-start.31 = (bf16[64,1792]{1,0:T(8,128)(2,1)S(1)}, bf16[64,1792]{1,0:T(8,128)(2,1)S(1)}, u32[]{:S(2)}, u32[]{:S(2)}) collective-permute-start(bf16[64,1792]{1,0:T(8,128)(2,1)S(1)} %get-tuple-element.41), channel_id=1, source_target_pairs={{0,8},{4,12},{8,0},{12,4},{1,9},{5,13},{9,1},{13,5},{2,10},{6,14},... | collective-permute-start | bytes 688136 | tf_op jit(solution)/shard_map/ppermute | solution.py:365
  108.5 13.4 %collective-permute-start.29 = (bf16[64,1792]{1,0:T(8,128)(2,1)S(1)}, bf16[64,1792]{1,0:T(8,128)(2,1)S(1)}, u32[]{:S(2)}, u32[]{:S(2)}) collective-permute-start(bf16[64,1792]{1,0:T(8,128)(2,1)S(1)} %add.66), channel_id=1, source_target_pairs={{0,2},{1,3},{2,0},{3,1},{4,6},{5,7},{6,4},{7,5},{8,10},{9,11},{10,... | collective-permute-start | bytes 688136 | tf_op jit(solution)/shard_map/ppermute | solution.py:368
  111.6 10.3 %collective-permute-start.34 = (bf16[64,1792]{1,0:T(8,128)(2,1)S(1)}, bf16[64,1792]{1,0:T(8,128)(2,1)S(1)}, u32[]{:S(2)}, u32[]{:S(2)}) collective-permute-start(bf16[64,1792]{1,0:T(8,128)(2,1)S(1)} %get-tuple-element.45), channel_id=1, source_target_pairs={{0,8},{4,12},{8,0},{12,4},{1,9},{5,13},{9,1},{13,5},{2,10},{6,14},... | collective-permute-start | bytes 688136 | tf_op jit(solution)/shard_map/ppermute | solution.py:365
  113.2 9.9 %collective-permute-start.32 = (bf16[64,1792]{1,0:T(8,128)(2,1)S(1)}, bf16[64,1792]{1,0:T(8,128)(2,1)S(1)}, u32[]{:S(2)}, u32[]{:S(2)}) collective-permute-start(bf16[64,1792]{1,0:T(8,128)(2,1)S(1)} %add.68), channel_id=1, source_target_pairs={{0,1},{1,0},{2,3},{3,2},{4,5},{5,4},{6,7},{7,6},{8,9},{9,8},{10,11... | collective-permute-start | bytes 688136 | tf_op jit(solution)/shard_map/ppermute | solution.py:368

commit v11 on v8

--- a/solution.py
+++ b/solution.py
@@ -47,14 +47,26 @@
     )(in_hbm(value), *after)
 
 
-def attention_kernel(step_rows, lengths, q_ref, qr_ref, k_ref, kr_ref, up_ref, *refs):
-    out_ref, latent, rope = refs[-3:]
+def attention_kernel(step_rows, pieces, ahead, lengths, q_ref, qr_ref, k_hbm, kr_hbm, up_ref, *refs):
+    out_ref, latent, rope, k_ref, kr_ref, sems = refs[-6:]
     step = pl.program_id(0)
+    steps = k_ref.shape[0] // step_rows
     heads, positions = q_ref.shape[1], k_ref.shape[1]
     rope_width = kr_ref.shape[1]
 
+    def copies(at):
+        whole = pl.ds(at * step_rows, step_rows)
+        made = [pltpu.make_async_copy(kr_hbm.at[whole], kr_ref.at[whole], sems.at[at, pieces])]
+        for i in range(pieces):
+            part = pl.ds(at * step_rows + i * (step_rows // pieces), step_rows // pieces)
+            made.append(pltpu.make_async_copy(k_hbm.at[part], k_ref.at[part], sems.at[at, i]))
+        return made
+
     @pl.when(step == 0)
     def _():
+        for at in range(min(ahead, steps)):
+            for copy in copies(at):
+                copy.start()
         all_rows = qr_ref.shape[0]
         width = heads * rope_width
         lane = lax.broadcasted_iota(jnp.int32, (heads, width), 1)
@@ -67,6 +79,13 @@
         fold = jnp.where(lane % rope_width == column, 1.0, 0.0).astype(jnp.bfloat16)
         rope[...] = jnp.dot(spread, fold, preferred_element_type=jnp.float32)
 
+    @pl.when(step + ahead < steps)
+    def _():
+        for copy in copies(step + ahead):
+            copy.start()
+
+    for copy in copies(step):
+        copy.wait()
     place = lax.broadcasted_iota(jnp.int32, (heads, positions), 1)
     lanes = latent.shape[2]
     lanes = latent.shape[2]
@@ -74,10 +93,10 @@
     for r in range(step_rows):
         first = pl.multiple_of((step * step_rows + r) * heads, heads)
         score = lax.dot_general(
-            q_ref[r], k_ref[r], (((1,), (1,)), ((), ())), preferred_element_type=jnp.float32
+            q_ref[r], k_ref[step * step_rows + r], (((1,), (1,)), ((), ())), preferred_element_type=jnp.float32
         )
         score += jnp.dot(
-            rope[pl.ds(first, heads), :].astype(jnp.bfloat16), kr_ref[r], preferred_element_type=jnp.float32
+            rope[pl.ds(first, heads), :].astype(jnp.bfloat16), kr_ref[step * step_rows + r], preferred_element_type=jnp.float32
         )
         scores.append(score)
     probabilities = []
@@ -89,7 +108,7 @@
         probabilities.append((weight / total).astype(jnp.bfloat16))
     for r in range(step_rows):
         first = pl.multiple_of((step * step_rows + r) * heads, heads)
-        mixed = jnp.dot(probabilities[r], k_ref[r], preferred_element_type=jnp.float32)
+        mixed = jnp.dot(probabilities[r], k_ref[step * step_rows + r], preferred_element_type=jnp.float32)
         for c in range(latent.shape[0]):
             latent[c, pl.ds(first, heads), :] = mixed[:, c * lanes : (c + 1) * lanes]
 
@@ -107,13 +126,12 @@
 
 def attend(query_latent, query_rope, cache_latent, cache_rope, cache_length, value_up, after):
     rows, heads, latent_width = query_latent.shape
-    positions = cache_latent.shape[1]
     rope_width = cache_rope.shape[1]
     value_width = value_up.shape[2]
-    step_rows = 16
+    step_rows, pieces, ahead = 8, 1, 3
     by_row = lambda i, lengths: (i, 0, 0)
     return pl.pallas_call(
-        functools.partial(attention_kernel, step_rows),
+        functools.partial(attention_kernel, step_rows, pieces, ahead),
         out_shape=jax.ShapeDtypeStruct((rows, heads * value_width), jnp.bfloat16),
         grid_spec=pltpu.PrefetchScalarGridSpec(
             num_scalar_prefetch=1,
@@ -121,8 +139,8 @@
             in_specs=[
                 pl.BlockSpec((step_rows, heads, latent_width), by_row),
                 pl.BlockSpec(query_rope.shape, lambda i, lengths: (0, 0)),
-                pl.BlockSpec((step_rows, positions, latent_width), by_row),
-                pl.BlockSpec((step_rows, rope_width, positions), by_row),
+                pl.BlockSpec(memory_space=pl.ANY),
+                pl.BlockSpec(memory_space=pl.ANY),
                 pl.BlockSpec(value_up.shape, lambda i, lengths: (0, 0, 0)),
             ]
             + [pl.BlockSpec(memory_space=pl.ANY)] * len(after),
@@ -130,12 +148,15 @@
             scratch_shapes=[
                 pltpu.VMEM((latent_width // 128, rows * heads, 128), jnp.float32),
                 pltpu.VMEM((rows * heads, rope_width), jnp.float32),
+                pltpu.VMEM(cache_latent.shape, jnp.bfloat16),
+                pltpu.VMEM(cache_rope.shape, jnp.bfloat16),
+                pltpu.SemaphoreType.DMA((rows // step_rows, pieces + 1)),
             ],
         ),
         cost_estimate=pl.CostEstimate(
             flops=64 * heads * cache_latent.size, bytes_accessed=2 * cache_latent.size, transcendentals=0
         ),
-        compiler_params=pltpu.CompilerParams(vmem_limit_bytes=20 * MIB),
+        compiler_params=pltpu.CompilerParams(vmem_limit_bytes=28 * MIB),
         name="attention",
     )(
         cache_length,
@@ -187,69 +208,79 @@
     )(places, *blocks, in_vmem(weight))
 
 
-def gate_kernel(row_blocks, column_blocks, model_width, places, *refs):
-    count = row_blocks * column_blocks
-    blocks, gains = refs[:count], refs[count : count + column_blocks]
-    gate, up = refs[count + column_blocks : count + column_blocks + 2]
-    active, x, gate_sum, up_sum = refs[-4:]
+def gate_kernel(row_blocks, cores, first, count, model_width, places, *refs):
+    blocks, gains = refs[: row_blocks * count], refs[row_blocks * count : (row_blocks + 1) * count]
+    refs = refs[(row_blocks + 1) * count :]
+    gate, up, refs = refs[0], refs[1], refs[2:]
+    if first:
+        before, (active, x) = refs[:3], refs[-2:]
+        gate_sum, up_sum, squares = before
+    else:
+        gate_sum, up_sum, squares, x = refs[-4:]
     height, width = blocks[0].shape
     hidden = gate.shape[2]
-    squares = [jnp.zeros((height, 1), jnp.float32) for _ in range(row_blocks)]
     tile = min(256, hidden)
-    for k in range(column_blocks):
+    sums = [[None] * (hidden // tile), [None] * (hidden // tile)]
+    totals = [squares[s * height : (s + 1) * height, :] if first else 0.0 for s in range(row_blocks)]
+    for k in range(count):
         for s in range(row_blocks):
-            wide = blocks[s * column_blocks + k][...].astype(jnp.float32)
-            squares[s] += jnp.sum(wide * wide, axis=-1, keepdims=True)
-            x[k, s * height : (s + 1) * height, :] = (wide * gains[k][...]).astype(jnp.bfloat16)
-        depth = pl.ds(pl.multiple_of(places[k] * width, 128), width)
-        for total, weight in ((gate_sum, gate), (up_sum, up)):
-            for j in range(hidden // tile):
-                cut = slice(j * tile, (j + 1) * tile)
-                product = jnp.dot(x[k], weight[0, depth, cut], preferred_element_type=jnp.float32)
-                if k == 0:
-                    total[:, cut] = product
-                else:
-                    total[:, cut] += product
-    for s in range(row_blocks):
-        rows = slice(s * height, (s + 1) * height)
-        scale = lax.rsqrt(squares[s] / model_width + norm_epsilon)
-        gate_part = gate_sum[rows, :] * scale
-        up_part = up_sum[rows, :] * scale
-        active[rows, :] = (gate_part / (1.0 + jnp.exp(-gate_part)) * up_part).astype(jnp.bfloat16)
-
-
-def activate(places, blocks, gains, gate_weight, up_weight, after):
-    row_blocks, column_blocks = len(blocks), len(blocks[0])
+            wide = blocks[s * count + k][...].astype(jnp.float32)
+            totals[s] += jnp.sum(wide * wide, axis=-1, keepdims=True)
+            x[s * height : (s + 1) * height, k * width : (k + 1) * width] = (wide * gains[k][...]).astype(jnp.bfloat16)
+    for w, (weight, start) in enumerate(((gate, gate_sum), (up, up_sum))):
+        for j in range(hidden // tile):
+            cut = slice(j * tile, (j + 1) * tile)
+            total = start[:, cut] if first else None
+            for k in range(count):
+                depth = pl.ds(pl.multiple_of(places[first + k] * width, 128), width)
+                product = jnp.dot(
+                    x[:, k * width : (k + 1) * width], weight[0, depth, cut], preferred_element_type=jnp.float32
+                )
+                total = product if total is None else total + product
+            sums[w][j] = total
+            if not first:
+                start[:, cut] = total
+    if not first:
+        for s in range(row_blocks):
+            squares[s * height : (s + 1) * height, :] = totals[s]
+        return
+    scale = jnp.concatenate([lax.rsqrt(t / model_width + norm_epsilon) for t in totals], axis=0)
+    for j in range(hidden // tile):
+        gate_part = sums[0][j] * scale
+        up_part = sums[1][j] * scale
+        active[:, j * tile : (j + 1) * tile] = (gate_part / (1.0 + jnp.exp(-gate_part)) * up_part).astype(jnp.bfloat16)
+
+
+def activate(places, blocks, gains, gate_weight, up_weight, cores, first, before):
+    row_blocks, count = len(blocks), len(blocks[0])
     height, width = blocks[0][0].shape
     rows = row_blocks * height
     model_width, hidden = gate_weight.shape[1:]
     whole = pl.BlockSpec(memory_space=pltpu.VMEM)
-    count = row_blocks * column_blocks
+    if first:
+        kinds = jax.ShapeDtypeStruct((rows, hidden), jnp.bfloat16)
+    else:
+        kinds = [jax.ShapeDtypeStruct((rows, n), jnp.float32) for n in (hidden, hidden, 1)]
     return pl.pallas_call(
-        functools.partial(gate_kernel, row_blocks, column_blocks, model_width),
-        out_shape=jax.ShapeDtypeStruct((rows, hidden), jnp.bfloat16),
-        in_specs=[pl.BlockSpec(memory_space=pltpu.SMEM)]
-        + [whole] * (count + column_blocks + 2)
-        + [pl.BlockSpec(memory_space=pl.ANY)] * len(after),
-        out_specs=whole,
-        scratch_shapes=[
-            pltpu.VMEM((column_blocks, rows, width), jnp.bfloat16),
-            pltpu.VMEM((rows, hidden), jnp.float32),
-            pltpu.VMEM((rows, hidden), jnp.float32),
-        ],
+        functools.partial(gate_kernel, row_blocks, cores, first, count, model_width),
+        out_shape=kinds,
+        in_specs=[pl.BlockSpec(memory_space=pltpu.SMEM)] + [whole] * ((row_blocks + 1) * count + 2 + len(before)),
+        out_specs=whole if first else [whole] * 3,
+        scratch_shapes=[pltpu.VMEM((rows, count * width), jnp.bfloat16)],
         cost_estimate=pl.CostEstimate(
-            flops=4 * rows * gate_weight.size, bytes_accessed=4 * gate_weight.size, transcendentals=rows * hidden
+            flops=4 * rows * hidden * count * width, bytes_accessed=4 * hidden * count * width, transcendentals=0
         ),
-        compiler_params=pltpu.CompilerParams(vmem_limit_bytes=2 * rows * (model_width + 4 * hidden) + 4 * MIB),
+        compiler_params=pltpu.CompilerParams(vmem_limit_bytes=2 * rows * (count * width + 8 * hidden) + 4 * MIB),
         name="activate",
-    )(places, *[b for row in blocks for b in row], *gains, in_vmem(gate_weight), in_vmem(up_weight), *after)
-
-
-def down_kernel(slots, column_blocks, cores, places, active, row_weight, down, *refs):
+    )(places, *[b for row in blocks for b in row], *gains, in_vmem(gate_weight), in_vmem(up_weight), *before)
+
+
+def down_kernel(slots, at, column_blocks, cores, places, active, row_weight, down, *refs):
     row_blocks = len(slots)
     outs = refs[-row_blocks * cores :]
     width = down.shape[2] // column_blocks
-    height = active.shape[0] // row_blocks
+    height = outs[0].shape[0] * cores // column_blocks
+    mine = slice(at * row_blocks * height, (at + 1) * row_blocks * height)
     order = [b * cores + c for c in reversed(range(cores)) for b in range(column_blocks // cores)]
     tile = 256 if width % 256 == 0 else 128
     weights = []
@@ -262,21 +293,21 @@
         for j in range(width // tile):
             cut = slice(j * tile, (j + 1) * tile)
             product = jnp.dot(
-                active[...], down[0, :, pl.ds(start + j * tile, tile)], preferred_element_type=jnp.float32
+                active[mine, :], down[0, :, pl.ds(start + j * tile, tile)], preferred_element_type=jnp.float32
             )
             for s in range(row_blocks):
                 part = product[s * height : (s + 1) * height, :] * weights[s]
                 outs[s * cores + c][b * height : (b + 1) * height, cut] = part.astype(jnp.bfloat16)
 
 
-def project_down(places, active, row_weight, down_weight, slots, column_blocks, cores, after):
+def project_down(places, active, row_weight, down_weight, slots, at, height, column_blocks, cores, after):
     row_blocks = len(slots)
-    rows, hidden = active.shape
+    rows = row_blocks * height
     width = down_weight.shape[2] // column_blocks
     whole = pl.BlockSpec(memory_space=pltpu.VMEM)
-    out = jax.ShapeDtypeStruct((rows // row_blocks * (column_blocks // cores), width), jnp.bfloat16)
+    out = jax.ShapeDtypeStruct((height * (column_blocks // cores), width), jnp.bfloat16)
     outs = pl.pallas_call(
-        functools.partial(down_kernel, slots, column_blocks, cores),
+        functools.partial(down_kernel, slots, at, column_blocks, cores),
         out_shape=[out] * (row_blocks * cores),
         in_specs=[pl.BlockSpec(memory_space=pltpu.SMEM)]
         + [whole] * 3
@@ -391,28 +422,46 @@
     stream, stream_out = add([stream_terms, stream_terms], block_rows, gains + [gate_weight, up_weight, down_weight])
 
     rows_of = {0: stream}
+    crossed = [from_chip(stream, b) for b in range(1, chips)]
     for k in range(1, tp_count):
         low = k & -k
-        rows_of[k] = from_tp(rows_of[k ^ low], low)
-    blocks = [gather_ep(rows_of[k]) for k in range(tp_count)]
-
+        source = rows_of[k ^ low]
+        if k == tp_count - 1:
+            (source,) = add([[(source, 0)]], block_rows, crossed)
+        rows_of[k] = from_tp(source, low)
     slots = list(reversed(range(tp_count)))
-    active = activate(places, [blocks[k] for k in slots], gains, gate_weight, up_weight, [])
-    outs = project_down(places, active, row_weight, down_weight, slots, ep_count, cores, [])
-    swapped = [from_core(out[1]) for out in outs]
+    near = {k: [rows_of[k], from_core(rows_of[k])] for k in slots}
+    sums = activate(places, [near[k] for k in slots], gains[:cores], gate_weight, up_weight, cores, 0, [])
+    far = {}
+    for k in [0] + slots[:-1]:
+        far[k] = []
+        for b in range(1, chips):
+            value = from_chip(rows_of[k], b) if k else crossed[b - 1]
+            (later,) = add([[(value, 0)]], block_rows, sums[-1:]) if k == 0 else (value,)
+            far[k] += [value, from_core(later)]
+    active = activate(places, [far[k] for k in slots], gains[cores:], gate_weight, up_weight, cores, cores, sums)
+
+    def send_back(k, after):
+        total = list(add([terms[k]], block_rows, after))
+        low = k & -k
+        terms[k ^ low].append((from_tp(total[0], low), 0))
+        return total
+
     terms = [[] for _ in range(tp_count)]
     arrivals = []
+    outs = project_down(places, active, row_weight, down_weight, slots, 0, block_rows, ep_count, cores, [])
+    swapped = [from_core(out[1]) for out in outs]
     for at, k in enumerate(slots):
-        before = arrivals[0] if len(arrivals) == 1 else arrivals[-2] if arrivals else []
+        before = arrivals[-2] + sent if len(arrivals) > 1 else []
         pair = [[(outs[at][0], c * block_rows), (swapped[at], c * block_rows)] for c in range(chips)]
-        sums = add(pair, block_rows, before)
-        across = [from_chip(sums[c], chips - c) for c in range(1, chips)]
+        added = add(pair, block_rows, before)
+        across = [from_chip(added[c], chips - c) for c in range(1, chips)]
         arrivals.append(across)
-        terms[k] += [(value, 0) for value in [sums[0]] + across]
-        if k:
-            (total,) = add([terms[k]], block_rows)
-            low = k & -k
-            terms[k ^ low].append((from_tp(total, low), 0))
+        terms[k] += [(value, 0) for value in [added[0]] + across]
+        if at == 0:
+            sent = send_back(k, [])
+    for k in slots[1:-1]:
+        sent = send_back(k, sent)
     (mixed,) = add([terms[0]], block_rows)
     return (stream_out, mixed)
 

time: 122 us -> 122 us (level)
  waiting for transfers between devices: 53.8 us -> 56.1 us
  starting transfers between devices: 29.3 us -> 27.1 us
    ppermute x10, waiting for transfers between devices: 25.6 us -> 28.9 us  [from_chip(): lax.ppermute(value, 'ep', [(i, (i + step) % ep_count) for i in range(ep_c...]
    ppermute x10, starting transfers between devices: 15.1 us -> 12.1 us  [from_chip(): lax.ppermute(value, 'ep', [(i, (i + step) % ep_count) for i in range(ep_c...]
    pallas_call x3 -> x4, Pallas kernels: 20.7 us -> 20.6 us  [the longest x1 12.4 us: attend(): pl.pallas_call(functools.partial(attention_kernel, step_rows, pieces, ahe...]
  transfers between devices with their start and end apart: 35 -> 35, of which waited for: 16 -> 19; matrix products, arithmetic and copies ran while one was open for 0% -> 0% of each run, Pallas kernels for 10% -> 12%
where the time goes in v11:
time: 122 us
  waiting for transfers between devices  56.1 us (46%)
  Pallas kernels  36.3 us (30%)
  starting transfers between devices  27.1 us (22%)
    ppermute x10, waiting for transfers between devices, from_chip(): lax.ppermute(value, 'ep', [(i, (i + step) % ep_count) for i in range(ep_c...  28.9 us
    ppermute x9, waiting for transfers between devices, from_tp(): return lax.ppermute(value, 'tp', [(i, i ^ bits) for i in range(tp_count)])  24.9 us
    ppermute x9, starting transfers between devices, from_tp(): return lax.ppermute(value, 'tp', [(i, i ^ bits) for i in range(tp_count)])  13.3 us
    pallas_call x1, Pallas kernels, attend(): pl.pallas_call(functools.partial(attention_kernel, step_rows, pieces, ahe...  12.4 us
    ppermute x10, starting transfers between devices, from_chip(): lax.ppermute(value, 'ep', [(i, (i + step) % ep_count) for i in range(ep_c...  12.1 us
    pallas_call x4, Pallas kernels, fetch(): pl.pallas_call(functools.partial(fetch_kernel, parts), out_shape=pltpu.VM...  11.6 us
    pallas_call x2, Pallas kernels, activate(): pl.pallas_call(functools.partial(gate_kernel, row_blocks, cores, first, c...  5.47 us
    pallas_call x1, Pallas kernels, project_down(): pl.pallas_call(functools.partial(down_kernel, slots, at, column_blocks, c...  2.69 us
  transfers between devices with their start and end apart: 35, of which 19 were waited for; matrix products, arithmetic and copies ran while one was open for 0% of the time, Pallas kernels for 12%

profile of v11, /device:TPU:0, one launch (start us, length us, event | category | flops | bytes accessed | tf_op | source)
XLA Modules:
  0.0 121.5 jit_solution(6325312865479340144)
XLA Ops:
  0.8 0.7 copy-done.2
  1.5 12.4 %attention.1.refs_1_.refs_0_ = bf16[64,1024]{1,0:T(8,128)(2,1)S(1)} custom-call(s32[64]{0:T(128)S(1)} %copy-done.2, bf16[64,8,512]{2,1,0:T(8,128)(2,1)} %q_ref.1, bf16[64,512]{1,0:T(8,128)(2,1)} %qr_ref.1, bf16[64,256,512]{2,1,0:T(8,128)(2,1)} %k_hbm.1, bf16[64,64,256]{2,1,0:T(8,128)(2,1)} %kr_hbm.1, bf16[8,512,128]{2,1,0:T(8,128)(2,1)} %up_ref.1, ...), custom_call_target="tpu_custom_call" | custom-call | flops 4294967296 | bytes 16777216 | tf_op jit(solution)/shard_map/attention/pallas_call | solution.py:133
  14.0 3.0 %collective-permute-start.1 = (bf16[64,1024]{1,0:T(8,128)(2,1)S(1)}, bf16[64,1024]{1,0:T(8,128)(2,1)S(1)}, u32[]{:S(2)}, u32[]{:S(2)}) collective-permute-start(bf16[64,1024]{1,0:T(8,128)(2,1)S(1)} %attention.1.refs_1_.refs_0_), channel_id=1, source_target_pairs={{0,8},{4,12},{8,0},{12,4},{1,9},{5,13},{9,1},{13,5},{2,10},{6,14},... | collective-permute-start | bytes 393224 | tf_op jit(solution)/shard_map/ppermute | solution.py:382
  17.2 3.3 %collective-permute-done.1.refs_2_ = bf16[64,1024]{1,0:T(8,128)(2,1)S(1)} collective-permute-done((bf16[64,1024]{1,0:T(8,128)(2,1)S(1)}, bf16[64,1024]{1,0:T(8,128)(2,1)S(1)}, u32[]{:S(2)}, u32[]{:S(2)}) %collective-permute-start.1) | collective-permute-done | bytes 131104 | tf_op jit(solution)/shard_map/ppermute | solution.py:382
  20.5 2.0 %fetch.4.refs_4_ = bf16[1024,1792]{1,0:T(8,128)(2,1)S(1)} custom-call(bf16[1024,1792]{1,0:T(8,128)(2,1)} %refs_0_.4, bf16[64,1024]{1,0:T(8,128)(2,1)S(1)} %attention.1.refs_1_.refs_0_, f32[256,1]{1,0:T(8,128)S(1)} %copy.16.refs_2_.row_weight, bf16[64,1792]{1,0:T(8,128)(2,1)S(1)} %constant_dynamic-slice_fusion.refs_3_.refs_7_, ...), custom_call_target="tpu_custom_call" | custom-call | bytes 7340032 | tf_op jit(solution)/shard_map/fetch/pallas_call | solution.py:38
  22.6 1.8 %projection.1 = (bf16[64,1792]{1,0:T(8,128)(2,1)S(1)}, bf16[64,1792]{1,0:T(8,128)(2,1)S(1)}, bf16[64,1792]{1,0:T(8,128)(2,1)S(1)}, bf16[64,1792]{1,0:T(8,128)(2,1)S(1)}) custom-call(s32[8]{0:T(128)S(1)} %stack.35.refs_0_.places, bf16[64,1024]{1,0:T(8,128)(2,1)S(1)} %attention.1.refs_1_.refs_0_, bf16[64,1024]{1,0:T(8,128)(2,1)S(1)} %collective-permute-done.refs_1_, ...), custom_call_target="tpu_custom_call" | custom-call | flops 939524096 | bytes 4194304 | tf_op jit(solution)/shard_map/projection/pallas_call | solution.py:196
  24.3 1.9 %collective-permute-start.3 = (bf16[64,1792]{1,0:T(8,128)(2,1)S(1)}, bf16[64,1792]{1,0:T(8,128)(2,1)S(1)}, u32[]{:S(2)}, u32[]{:S(2)}) collective-permute-start(bf16[64,1792]{1,0:T(8,128)(2,1)S(1)} %get-tuple-element.29), channel_id=1, source_target_pairs={{0,1},{1,0},{2,3},{3,2},{4,5},{5,4},{6,7},{7,6},{8,9},{9,8},{10,11... | collective-permute-start | bytes 688136 | tf_op jit(solution)/shard_map/ppermute | solution.py:385
  26.2 3.2 %fetch.5.refs_1_.refs_12_.refs_10_ = bf16[1,7168,512]{2,1,0:T(8,128)(2,1)S(1)} custom-call(bf16[1,7168,512]{2,1,0:T(8,128)(2,1)} %refs_0_.5, bf16[64,1792]{1,0:T(8,128)(2,1)S(1)} %get-tuple-element.27.refs_1_.refs_0_.refs_4_), custom_call_target="tpu_custom_call" | custom-call | bytes 14680064 | tf_op jit(solution)/shard_map/fetch/pallas_call | solution.py:38
  29.7 2.9 %collective-permute-done.3.refs_1_ = bf16[64,1792]{1,0:T(8,128)(2,1)S(1)} collective-permute-done((bf16[64,1792]{1,0:T(8,128)(2,1)S(1)}, bf16[64,1792]{1,0:T(8,128)(2,1)S(1)}, u32[]{:S(2)}, u32[]{:S(2)}) %collective-permute-start.3) | collective-permute-done | bytes 229408 | tf_op jit(solution)/shard_map/ppermute | solution.py:385
  32.7 3.0 %collective-permute-start.4 = (bf16[64,1792]{1,0:T(8,128)(2,1)S(1)}, bf16[64,1792]{1,0:T(8,128)(2,1)S(1)}, u32[]{:S(2)}, u32[]{:S(2)}) collective-permute-start(bf16[64,1792]{1,0:T(8,128)(2,1)S(1)} %add.62), channel_id=1, source_target_pairs={{0,2},{1,3},{2,0},{3,1},{4,6},{5,7},{6,4},{7,5},{8,10},{9,11},{10,... | collective-permute-start | bytes 688136 | tf_op jit(solution)/shard_map/ppermute | solution.py:385
  35.6 1.5 %collective-permute-start.7 = (f32[1,1792]{1,0:T(1,128)S(1)}, f32[1,1792]{1,0:T(1,128)S(1)}, u32[]{:S(2)}, u32[]{:S(2)}) collective-permute-start(f32[1,1792]{1,0:T(1,128)S(1)} %reshape.7.refs_4_.refs_8_), channel_id=1, source_target_pairs={{0,8},{4,12},{8,0},{12,4},{1,9},{5,13},{9,1},{13,5},{2,10},{6,14},... | collective-permute-start | bytes 21512 | tf_op jit(solution)/shard_map/ppermute | solution.py:382
  37.1 2.1 %collective-permute-done.7.refs_10_.refs_8_ = f32[1,1792]{1,0:T(1,128)S(1)} collective-permute-done((f32[1,1792]{1,0:T(1,128)S(1)}, f32[1,1792]{1,0:T(1,128)S(1)}, u32[]{:S(2)}, u32[]{:S(2)}) %collective-permute-start.7) | collective-permute-done | bytes 7200 | tf_op jit(solution)/shard_map/ppermute | solution.py:382
  39.3 3.2 %fetch.6.refs_13_.refs_11_ = bf16[1,7168,512]{2,1,0:T(8,128)(2,1)S(1)} custom-call(bf16[1,7168,512]{2,1,0:T(8,128)(2,1)} %refs_0_.6, bf16[64,1792]{1,0:T(8,128)(2,1)S(1)} %add.63.refs_1_), custom_call_target="tpu_custom_call" | custom-call | bytes 14680064 | tf_op jit(solution)/shard_map/fetch/pallas_call | solution.py:38
  42.5 3.2 %fetch.7.refs_14_.down = bf16[1,512,7168]{2,1,0:T(8,128)(2,1)S(1)} custom-call(bf16[1,512,7168]{2,1,0:T(8,128)(2,1)} %refs_0_.7, bf16[64,1792]{1,0:T(8,128)(2,1)S(1)} %add.63.refs_1_), custom_call_target="tpu_custom_call" | custom-call | bytes 14680064 | tf_op jit(solution)/shard_map/fetch/pallas_call | solution.py:38
  45.8 0.8 add.64
  46.7 1.5 %collective-permute-start.10 = (bf16[64,1792]{1,0:T(8,128)(2,1)S(1)}, bf16[64,1792]{1,0:T(8,128)(2,1)S(1)}, u32[]{:S(2)}, u32[]{:S(2)}) collective-permute-start(bf16[64,1792]{1,0:T(8,128)(2,1)S(1)} %get-tuple-element.32.refs_6_), channel_id=1, source_target_pairs={{0,8},{4,12},{8,0},{12,4},{1,9},{5,13},{9,1},{13,5},{2,10},{6,14},... | collective-permute-start | bytes 688136 | tf_op jit(solution)/shard_map/ppermute | solution.py:382
  48.4 3.9 %collective-permute-start.16 = (bf16[64,1792]{1,0:T(8,128)(2,1)S(1)}, bf16[64,1792]{1,0:T(8,128)(2,1)S(1)}, u32[]{:S(2)}, u32[]{:S(2)}) collective-permute-start(bf16[64,1792]{1,0:T(8,128)(2,1)S(1)} %get-tuple-element.32.refs_6_), channel_id=1, source_target_pairs={{0,1},{1,0},{2,3},{3,2},{4,5},{5,4},{6,7},{7,6},{8,9},{9,8},{10,11... | collective-permute-start | bytes 688136 | tf_op jit(solution)/shard_map/ppermute | solution.py:385
  52.4 2.2 %collective-permute-done.10.refs_1_.refs_0_.refs_6_ = bf16[64,1792]{1,0:T(8,128)(2,1)S(1)} collective-permute-done((bf16[64,1792]{1,0:T(8,128)(2,1)S(1)}, bf16[64,1792]{1,0:T(8,128)(2,1)S(1)}, u32[]{:S(2)}, u32[]{:S(2)}) %collective-permute-start.10) | collective-permute-done | bytes 229408 | tf_op jit(solution)/shard_map/ppermute | solution.py:382
  54.6 7.1 %collective-permute-done.9.refs_0_.refs_2_ = bf16[64,1792]{1,0:T(8,128)(2,1)S(1)} collective-permute-done((bf16[64,1792]{1,0:T(8,128)(2,1)S(1)}, bf16[64,1792]{1,0:T(8,128)(2,1)S(1)}, u32[]{:S(2)}, u32[]{:S(2)}) %collective-permute-start.9) | collective-permute-done | bytes 229408 | tf_op jit(solution)/shard_map/ppermute | solution.py:385
  61.8 0.6 collective-permute-start.14
  62.4 1.5 %collective-permute-start.17 = (bf16[64,1792]{1,0:T(8,128)(2,1)S(1)}, bf16[64,1792]{1,0:T(8,128)(2,1)S(1)}, u32[]{:S(2)}, u32[]{:S(2)}) collective-permute-start(bf16[64,1792]{1,0:T(8,128)(2,1)S(1)} %collective-permute-done.16.refs_4_), channel_id=1, source_target_pairs={{0,8},{4,12},{8,0},{12,4},{1,9},{5,13},{9,1},{13,5},{2,10},{6,14},... | collective-permute-start | bytes 688136 | tf_op jit(solution)/shard_map/ppermute | solution.py:382
  63.9 4.5 %collective-permute-done.11.refs_0_ = bf16[64,1792]{1,0:T(8,128)(2,1)S(1)} collective-permute-done((bf16[64,1792]{1,0:T(8,128)(2,1)S(1)}, bf16[64,1792]{1,0:T(8,128)(2,1)S(1)}, u32[]{:S(2)}, u32[]{:S(2)}) %collective-permute-start.11) | collective-permute-done | bytes 229408 | tf_op jit(solution)/shard_map/ppermute | solution.py:385
  68.5 0.6 collective-permute-start.12
  69.0 1.3 %collective-permute-done.14.refs_2_ = bf16[64,1792]{1,0:T(8,128)(2,1)S(1)} collective-permute-done((bf16[64,1792]{1,0:T(8,128)(2,1)S(1)}, bf16[64,1792]{1,0:T(8,128)(2,1)S(1)}, u32[]{:S(2)}, u32[]{:S(2)}) %collective-permute-start.14) | collective-permute-done | bytes 229408 | tf_op jit(solution)/shard_map/ppermute | solution.py:382
  70.3 4.9 %collective-permute-done.17.refs_4_ = bf16[64,1792]{1,0:T(8,128)(2,1)S(1)} collective-permute-done((bf16[64,1792]{1,0:T(8,128)(2,1)S(1)}, bf16[64,1792]{1,0:T(8,128)(2,1)S(1)}, u32[]{:S(2)}, u32[]{:S(2)}) %collective-permute-start.17) | collective-permute-done | bytes 229408 | tf_op jit(solution)/shard_map/ppermute | solution.py:382
  75.2 2.7 %activate.2 = (f32[256,512]{1,0:T(8,128)S(1)}, f32[256,512]{1,0:T(8,128)S(1)}, f32[256,1]{1,0:T(8,128)S(1)}) custom-call(s32[8]{0:T(128)S(1)} %stack.35.refs_0_.places, bf16[64,1792]{1,0:T(8,128)(2,1)S(1)} %collective-permute-done.11.refs_0_, bf16[64,1792]{1,0:T(8,128)(2,1)S(1)} %collective-permute-done.19.refs_1_, ...), custom_call_target="tpu_custom_call" | custom-call | flops 1879048192 | bytes 7340032 | tf_op jit(solution)/shard_map/activate/pallas_call | solution.py:264
  77.9 0.6 collective-permute-start.23
  78.5 1.2 collective-permute-done.12.refs_0_
  79.7 1.5 %collective-permute-done.13.refs_1_ = bf16[64,1792]{1,0:T(8,128)(2,1)S(1)} collective-permute-done((bf16[64,1792]{1,0:T(8,128)(2,1)S(1)}, bf16[64,1792]{1,0:T(8,128)(2,1)S(1)}, u32[]{:S(2)}, u32[]{:S(2)}) %collective-permute-start.13) | collective-permute-done | bytes 229408 | tf_op jit(solution)/shard_map/ppermute | solution.py:378
  81.2 2.8 %activate.3.active = bf16[256,512]{1,0:T(8,128)(2,1)S(1)} custom-call(s32[8]{0:T(128)S(1)} %stack.35.refs_0_.places, bf16[64,1792]{1,0:T(8,128)(2,1)S(1)} %collective-permute-done.12.refs_0_, bf16[64,1792]{1,0:T(8,128)(2,1)S(1)} %collective-permute-done.13.refs_1_, bf16[64,1792]{1,0:T(8,128)(2,1)S(1)} %collective-permute-done.14.refs_2_, ...), custom_call_target="tpu_custom_call" | custom-call | flops 1879048192 | bytes 7340032 | tf_op jit(solution)/shard_map/activate/pallas_call | solution.py:264
  84.0 2.7 %down.1 = (bf16[128,1792]{1,0:T(8,128)(2,1)S(1)}, bf16[128,1792]{1,0:T(8,128)(2,1)S(1)}, bf16[128,1792]{1,0:T(8,128)(2,1)S(1)}, bf16[128,1792]{1,0:T(8,128)(2,1)...) custom-call(s32[8]{0:T(128)S(1)} %stack.35.refs_0_.places, ...), custom_call_target="tpu_custom_call" | custom-call | flops 1879048192 | bytes 7340032 | tf_op jit(solution)/shard_map/down/pallas_call | solution.py:309
  86.9 0.4 collective-permute-start.25
  87.8 0.8 collective-permute-done.27.refs_1_.refs_3_
  88.7 0.6 collective-permute-start.28
  89.4 1.5 %collective-permute-start.26 = (bf16[64,1792]{1,0:T(8,128)(2,1)S(1)}, bf16[64,1792]{1,0:T(8,128)(2,1)S(1)}, u32[]{:S(2)}, u32[]{:S(2)}) collective-permute-start(bf16[64,1792]{1,0:T(8,128)(2,1)S(1)} %get-tuple-element.40), channel_id=1, source_target_pairs={{0,8},{4,12},{8,0},{12,4},{1,9},{5,13},{9,1},{13,5},{2,10},{6,14},... | collective-permute-start | bytes 688136 | tf_op jit(solution)/shard_map/ppermute | solution.py:382
  90.9 6.2 %collective-permute-done.28.refs_1_.refs_4_ = bf16[64,1792]{1,0:T(8,128)(2,1)S(1)} collective-permute-done((bf16[64,1792]{1,0:T(8,128)(2,1)S(1)}, bf16[64,1792]{1,0:T(8,128)(2,1)S(1)}, u32[]{:S(2)}, u32[]{:S(2)}) %collective-permute-start.28) | collective-permute-done | bytes 229408 | tf_op jit(solution)/shard_map/ppermute | solution.py:382
  97.2 2.0 %collective-permute-start.30 = (bf16[64,1792]{1,0:T(8,128)(2,1)S(1)}, bf16[64,1792]{1,0:T(8,128)(2,1)S(1)}, u32[]{:S(2)}, u32[]{:S(2)}) collective-permute-start(bf16[64,1792]{1,0:T(8,128)(2,1)S(1)} %add.69.refs_5_.refs_3_), channel_id=1, source_target_pairs={{0,1},{1,0},{2,3},{3,2},{4,5},{5,4},{6,7},{7,6},{8,9},{9,8},{10,11... | collective-permute-start | bytes 688136 | tf_op jit(solution)/shard_map/ppermute | solution.py:385
  99.4 0.6 collective-permute-start.33
  100.0 2.1 %collective-permute-done.26.refs_4_.refs_2_ = bf16[64,1792]{1,0:T(8,128)(2,1)S(1)} collective-permute-done((bf16[64,1792]{1,0:T(8,128)(2,1)S(1)}, bf16[64,1792]{1,0:T(8,128)(2,1)S(1)}, u32[]{:S(2)}, u32[]{:S(2)}) %collective-permute-start.26) | collective-permute-done | bytes 229408 | tf_op jit(solution)/shard_map/ppermute | solution.py:382
  102.2 0.6 collective-permute-start.29
  102.8 0.7 collective-permute-done.30.refs_0_
  103.7 4.3 %collective-permute-done.33.refs_1_ = bf16[64,1792]{1,0:T(8,128)(2,1)S(1)} collective-permute-done((bf16[64,1792]{1,0:T(8,128)(2,1)S(1)}, bf16[64,1792]{1,0:T(8,128)(2,1)S(1)}, u32[]{:S(2)}, u32[]{:S(2)}) %collective-permute-start.33) | collective-permute-done | bytes 229408 | tf_op jit(solution)/shard_map/ppermute | solution.py:382
  108.0 1.1 collective-permute-start.34
  109.1 0.9 collective-permute-start.31
  110.0 1.2 collective-permute-done.29.refs_1_
  111.2 5.8 %collective-permute-done.34.refs_3_ = bf16[64,1792]{1,0:T(8,128)(2,1)S(1)} collective-permute-done((bf16[64,1792]{1,0:T(8,128)(2,1)S(1)}, bf16[64,1792]{1,0:T(8,128)(2,1)S(1)}, u32[]{:S(2)}, u32[]{:S(2)}) %collective-permute-start.34) | collective-permute-done | bytes 229408 | tf_op jit(solution)/shard_map/ppermute | solution.py:385
  116.9 3.8 %collective-permute-done.31.refs_2_ = bf16[64,1792]{1,0:T(8,128)(2,1)S(1)} collective-permute-done((bf16[64,1792]{1,0:T(8,128)(2,1)S(1)}, bf16[64,1792]{1,0:T(8,128)(2,1)S(1)}, u32[]{:S(2)}, u32[]{:S(2)}) %collective-permute-start.31) | collective-permute-done | bytes 229408 | tf_op jit(solution)/shard_map/ppermute | solution.py:385
  120.7 0.8 add.74
  (61 shorter events, 2.6 us)
Async XLA Ops:
  0.6 19.9 %copy-start = (bf16[256,1792]{1,0:T(8,128)(2,1)S(1)}, bf16[256,1792]{1,0:T(8,128)(2,1)}, u32[]{:S(2)}) copy-start(bf16[256,1792]{1,0:T(8,128)(2,1)} %param.21) | copy-start | bytes 2752516
  0.8 0.7 copy-start.2
  1.5 15.5 %copy-start.4 = (f32[256,2]{0,1:T(2,128)S(1)}, f32[256,2]{0,1:T(2,128)}, u32[]{:S(2)}) copy-start(f32[256,2]{0,1:T(2,128)} %param.24) | copy-start | bytes 6148
  1.5 15.5 %copy-start.5 = (s32[256,2]{0,1:T(2,128)S(1)}, s32[256,2]{0,1:T(2,128)}, u32[]{:S(2)}) copy-start(s32[256,2]{0,1:T(2,128)} %param.23) | copy-start | bytes 6148
  1.5 15.6 %copy-start.3 = (f32[1792]{0:T(1024)S(1)}, f32[1792]{0:T(1024)}, u32[]{:S(2)}) copy-start(f32[1792]{0:T(1024)} %param.22) | copy-start | bytes 21508
  14.0 6.5 %collective-permute-start.1 = (bf16[64,1024]{1,0:T(8,128)(2,1)S(1)}, bf16[64,1024]{1,0:T(8,128)(2,1)S(1)}, u32[]{:S(2)}, u32[]{:S(2)}) collective-permute-start(bf16[64,1024]{1,0:T(8,128)(2,1)S(1)} %attention.1.refs_1_.refs_0_), channel_id=1, source_target_pairs={{0,8},{4,12},{8,0},{12,4},{1,9},{5,13},{9,1},{13,5},{2,10},{6,14},... | collective-permute-start | bytes 393224 | tf_op jit(solution)/shard_map/ppermute | solution.py:382
  17.0 5.6 %collective-permute-start = (bf16[64,1024]{1,0:T(8,128)(2,1)S(1)}, bf16[64,1024]{1,0:T(8,128)(2,1)S(1)}, u32[]{:S(2)}, u32[]{:S(2)}) collective-permute-start(bf16[64,1024]{1,0:T(8,128)(2,1)S(1)} %attention.1.refs_1_.refs_0_), channel_id=1, source_target_pairs={{0,4},{4,0},{8,12},{12,8},{1,5},{5,1},{9,13},{13,9},{2,6},{6,2},{1... | collective-permute-start | bytes 393224 | tf_op jit(solution)/shard_map/ppermute | solution.py:378
  20.5 2.1 %collective-permute-start.2 = (bf16[64,1024]{1,0:T(8,128)(2,1)S(1)}, bf16[64,1024]{1,0:T(8,128)(2,1)S(1)}, u32[]{:S(2)}, u32[]{:S(2)}) collective-permute-start(bf16[64,1024]{1,0:T(8,128)(2,1)S(1)} %collective-permute-done.1.refs_2_), channel_id=1, source_target_pairs={{0,4},{4,0},{8,12},{12,8},{1,5},{5,1},{9,13},{13,9},{2,6},{6,2},{1... | collective-permute-start | bytes 393224 | tf_op jit(solution)/shard_map/ppermute | solution.py:378
  24.3 8.3 %collective-permute-start.3 = (bf16[64,1792]{1,0:T(8,128)(2,1)S(1)}, bf16[64,1792]{1,0:T(8,128)(2,1)S(1)}, u32[]{:S(2)}, u32[]{:S(2)}) collective-permute-start(bf16[64,1792]{1,0:T(8,128)(2,1)S(1)} %get-tuple-element.29), channel_id=1, source_target_pairs={{0,1},{1,0},{2,3},{3,2},{4,5},{5,4},{6,7},{7,6},{8,9},{9,8},{10,11... | collective-permute-start | bytes 688136 | tf_op jit(solution)/shard_map/ppermute | solution.py:385
  29.4 16.3 %collective-permute-start.5 = (bf16[64,1792]{1,0:T(8,128)(2,1)S(1)}, bf16[64,1792]{1,0:T(8,128)(2,1)S(1)}, u32[]{:S(2)}, u32[]{:S(2)}) collective-permute-start(bf16[64,1792]{1,0:T(8,128)(2,1)S(1)} %add.63.refs_1_), channel_id=1, source_target_pairs={{0,1},{1,0},{2,3},{3,2},{4,5},{5,4},{6,7},{7,6},{8,9},{9,8},{10,11... | collective-permute-start | bytes 688136 | tf_op jit(solution)/shard_map/ppermute | solution.py:385
  32.7 13.2 %collective-permute-start.4 = (bf16[64,1792]{1,0:T(8,128)(2,1)S(1)}, bf16[64,1792]{1,0:T(8,128)(2,1)S(1)}, u32[]{:S(2)}, u32[]{:S(2)}) collective-permute-start(bf16[64,1792]{1,0:T(8,128)(2,1)S(1)} %add.62), channel_id=1, source_target_pairs={{0,2},{1,3},{2,0},{3,1},{4,6},{5,7},{6,4},{7,5},{8,10},{9,11},{10,... | collective-permute-start | bytes 688136 | tf_op jit(solution)/shard_map/ppermute | solution.py:385
  35.6 3.6 %collective-permute-start.7 = (f32[1,1792]{1,0:T(1,128)S(1)}, f32[1,1792]{1,0:T(1,128)S(1)}, u32[]{:S(2)}, u32[]{:S(2)}) collective-permute-start(f32[1,1792]{1,0:T(1,128)S(1)} %reshape.7.refs_4_.refs_8_), channel_id=1, source_target_pairs={{0,8},{4,12},{8,0},{12,4},{1,9},{5,13},{9,1},{13,5},{2,10},{6,14},... | collective-permute-start | bytes 21512 | tf_op jit(solution)/shard_map/ppermute | solution.py:382
  37.1 8.5 %collective-permute-start.6 = (f32[1,1792]{1,0:T(1,128)S(1)}, f32[1,1792]{1,0:T(1,128)S(1)}, u32[]{:S(2)}, u32[]{:S(2)}) collective-permute-start(f32[1,1792]{1,0:T(1,128)S(1)} %reshape.7.refs_4_.refs_8_), channel_id=1, source_target_pairs={{0,4},{4,0},{8,12},{12,8},{1,5},{5,1},{9,13},{13,9},{2,6},{6,2},{1... | collective-permute-start | bytes 21512 | tf_op jit(solution)/shard_map/ppermute | solution.py:378
  39.3 6.4 %collective-permute-start.8 = (f32[1,1792]{1,0:T(1,128)S(1)}, f32[1,1792]{1,0:T(1,128)S(1)}, u32[]{:S(2)}, u32[]{:S(2)}) collective-permute-start(f32[1,1792]{1,0:T(1,128)S(1)} %collective-permute-done.7.refs_10_.refs_8_), channel_id=1, source_target_pairs={{0,4},{4,0},{8,12},{12,8},{1,5},{5,1},{9,13},{13,9},{2,6},{6,2},{1... | collective-permute-start | bytes 21512 | tf_op jit(solution)/shard_map/ppermute | solution.py:378
  46.7 7.9 %collective-permute-start.10 = (bf16[64,1792]{1,0:T(8,128)(2,1)S(1)}, bf16[64,1792]{1,0:T(8,128)(2,1)S(1)}, u32[]{:S(2)}, u32[]{:S(2)}) collective-permute-start(bf16[64,1792]{1,0:T(8,128)(2,1)S(1)} %get-tuple-element.32.refs_6_), channel_id=1, source_target_pairs={{0,8},{4,12},{8,0},{12,4},{1,9},{5,13},{9,1},{13,5},{2,10},{6,14},... | collective-permute-start | bytes 688136 | tf_op jit(solution)/shard_map/ppermute | solution.py:382
  48.2 13.4 %collective-permute-start.9 = (bf16[64,1792]{1,0:T(8,128)(2,1)S(1)}, bf16[64,1792]{1,0:T(8,128)(2,1)S(1)}, u32[]{:S(2)}, u32[]{:S(2)}) collective-permute-start(bf16[64,1792]{1,0:T(8,128)(2,1)S(1)} %get-tuple-element.32.refs_6_), channel_id=1, source_target_pairs={{0,2},{1,3},{2,0},{3,1},{4,6},{5,7},{6,4},{7,5},{8,10},{9,11},{10,... | collective-permute-start | bytes 688136 | tf_op jit(solution)/shard_map/ppermute | solution.py:385
  48.4 14.0 %collective-permute-start.16 = (bf16[64,1792]{1,0:T(8,128)(2,1)S(1)}, bf16[64,1792]{1,0:T(8,128)(2,1)S(1)}, u32[]{:S(2)}, u32[]{:S(2)}) collective-permute-start(bf16[64,1792]{1,0:T(8,128)(2,1)S(1)} %get-tuple-element.32.refs_6_), channel_id=1, source_target_pairs={{0,1},{1,0},{2,3},{3,2},{4,5},{5,4},{6,7},{7,6},{8,9},{9,8},{10,11... | collective-permute-start | bytes 688136 | tf_op jit(solution)/shard_map/ppermute | solution.py:385
  52.4 11.6 %collective-permute-start.22 = (bf16[64,1792]{1,0:T(8,128)(2,1)S(1)}, bf16[64,1792]{1,0:T(8,128)(2,1)S(1)}, u32[]{:S(2)}, u32[]{:S(2)}) collective-permute-start(bf16[64,1792]{1,0:T(8,128)(2,1)S(1)} %get-tuple-element.32.refs_6_), channel_id=1, source_target_pairs={{0,4},{4,0},{8,12},{12,8},{1,5},{5,1},{9,13},{13,9},{2,6},{6,2},{1... | collective-permute-start | bytes 688136 | tf_op jit(solution)/shard_map/ppermute | solution.py:378
  61.7 6.8 %collective-permute-start.11 = (bf16[64,1792]{1,0:T(8,128)(2,1)S(1)}, bf16[64,1792]{1,0:T(8,128)(2,1)S(1)}, u32[]{:S(2)}, u32[]{:S(2)}) collective-permute-start(bf16[64,1792]{1,0:T(8,128)(2,1)S(1)} %add.65), channel_id=1, source_target_pairs={{0,1},{1,0},{2,3},{3,2},{4,5},{5,4},{6,7},{7,6},{8,9},{9,8},{10,11... | collective-permute-start | bytes 688136 | tf_op jit(solution)/shard_map/ppermute | solution.py:385
  61.8 6.7 %collective-permute-start.20 = (bf16[64,1792]{1,0:T(8,128)(2,1)S(1)}, bf16[64,1792]{1,0:T(8,128)(2,1)S(1)}, u32[]{:S(2)}, u32[]{:S(2)}) collective-permute-start(bf16[64,1792]{1,0:T(8,128)(2,1)S(1)} %collective-permute-done.9.refs_0_.refs_2_), channel_id=1, source_target_pairs={{0,4},{4,0},{8,12},{12,8},{1,5},{5,1},{9,13},{13,9},{2,6},{6,2},{1... | collective-permute-start | bytes 688136 | tf_op jit(solution)/shard_map/ppermute | solution.py:378
  61.8 8.5 %collective-permute-start.14 = (bf16[64,1792]{1,0:T(8,128)(2,1)S(1)}, bf16[64,1792]{1,0:T(8,128)(2,1)S(1)}, u32[]{:S(2)}, u32[]{:S(2)}) collective-permute-start(bf16[64,1792]{1,0:T(8,128)(2,1)S(1)} %collective-permute-done.9.refs_0_.refs_2_), channel_id=1, source_target_pairs={{0,8},{4,12},{8,0},{12,4},{1,9},{5,13},{9,1},{13,5},{2,10},{6,14},... | collective-permute-start | bytes 688136 | tf_op jit(solution)/shard_map/ppermute | solution.py:382
  62.4 12.8 %collective-permute-start.17 = (bf16[64,1792]{1,0:T(8,128)(2,1)S(1)}, bf16[64,1792]{1,0:T(8,128)(2,1)S(1)}, u32[]{:S(2)}, u32[]{:S(2)}) collective-permute-start(bf16[64,1792]{1,0:T(8,128)(2,1)S(1)} %collective-permute-done.16.refs_4_), channel_id=1, source_target_pairs={{0,8},{4,12},{8,0},{12,4},{1,9},{5,13},{9,1},{13,5},{2,10},{6,14},... | collective-permute-start | bytes 688136 | tf_op jit(solution)/shard_map/ppermute | solution.py:382
  63.9 11.3 %collective-permute-start.21 = (bf16[64,1792]{1,0:T(8,128)(2,1)S(1)}, bf16[64,1792]{1,0:T(8,128)(2,1)S(1)}, u32[]{:S(2)}, u32[]{:S(2)}) collective-permute-start(bf16[64,1792]{1,0:T(8,128)(2,1)S(1)} %collective-permute-done.16.refs_4_), channel_id=1, source_target_pairs={{0,4},{4,0},{8,12},{12,8},{1,5},{5,1},{9,13},{13,9},{2,6},{6,2},{1... | collective-permute-start | bytes 688136 | tf_op jit(solution)/shard_map/ppermute | solution.py:378
  68.5 6.8 %collective-permute-start.19 = (bf16[64,1792]{1,0:T(8,128)(2,1)S(1)}, bf16[64,1792]{1,0:T(8,128)(2,1)S(1)}, u32[]{:S(2)}, u32[]{:S(2)}) collective-permute-start(bf16[64,1792]{1,0:T(8,128)(2,1)S(1)} %collective-permute-done.11.refs_0_), channel_id=1, source_target_pairs={{0,4},{4,0},{8,12},{12,8},{1,5},{5,1},{9,13},{13,9},{2,6},{6,2},{1... | collective-permute-start | bytes 688136 | tf_op jit(solution)/shard_map/ppermute | solution.py:378
  68.5 11.2 %collective-permute-start.12 = (bf16[64,1792]{1,0:T(8,128)(2,1)S(1)}, bf16[64,1792]{1,0:T(8,128)(2,1)S(1)}, u32[]{:S(2)}, u32[]{:S(2)}) collective-permute-start(bf16[64,1792]{1,0:T(8,128)(2,1)S(1)} %collective-permute-done.11.refs_0_), channel_id=1, source_target_pairs={{0,8},{4,12},{8,0},{12,4},{1,9},{5,13},{9,1},{13,5},{2,10},{6,14},... | collective-permute-start | bytes 688136 | tf_op jit(solution)/shard_map/ppermute | solution.py:382
  70.3 9.4 %collective-permute-start.15 = (bf16[64,1792]{1,0:T(8,128)(2,1)S(1)}, bf16[64,1792]{1,0:T(8,128)(2,1)S(1)}, u32[]{:S(2)}, u32[]{:S(2)}) collective-permute-start(bf16[64,1792]{1,0:T(8,128)(2,1)S(1)} %collective-permute-done.14.refs_2_), channel_id=1, source_target_pairs={{0,4},{4,0},{8,12},{12,8},{1,5},{5,1},{9,13},{13,9},{2,6},{6,2},{1... | collective-permute-start | bytes 688136 | tf_op jit(solution)/shard_map/ppermute | solution.py:378
  75.2 4.5 %collective-permute-start.18 = (bf16[64,1792]{1,0:T(8,128)(2,1)S(1)}, bf16[64,1792]{1,0:T(8,128)(2,1)S(1)}, u32[]{:S(2)}, u32[]{:S(2)}) collective-permute-start(bf16[64,1792]{1,0:T(8,128)(2,1)S(1)} %collective-permute-done.17.refs_4_), channel_id=1, source_target_pairs={{0,4},{4,0},{8,12},{12,8},{1,5},{5,1},{9,13},{13,9},{2,6},{6,2},{1... | collective-permute-start | bytes 688136 | tf_op jit(solution)/shard_map/ppermute | solution.py:378
  77.9 1.8 %collective-permute-start.23 = (bf16[64,1792]{1,0:T(8,128)(2,1)S(1)}, bf16[64,1792]{1,0:T(8,128)(2,1)S(1)}, u32[]{:S(2)}, u32[]{:S(2)}) collective-permute-start(bf16[64,1792]{1,0:T(8,128)(2,1)S(1)} %add.66), channel_id=1, source_target_pairs={{0,4},{4,0},{8,12},{12,8},{1,5},{5,1},{9,13},{13,9},{2,6},{6,2},{1... | collective-permute-start | bytes 688136 | tf_op jit(solution)/shard_map/ppermute | solution.py:378
  79.7 1.5 %collective-permute-start.13 = (bf16[64,1792]{1,0:T(8,128)(2,1)S(1)}, bf16[64,1792]{1,0:T(8,128)(2,1)S(1)}, u32[]{:S(2)}, u32[]{:S(2)}) collective-permute-start(bf16[64,1792]{1,0:T(8,128)(2,1)S(1)} %collective-permute-done.12.refs_0_), channel_id=1, source_target_pairs={{0,4},{4,0},{8,12},{12,8},{1,5},{5,1},{9,13},{13,9},{2,6},{6,2},{1... | collective-permute-start | bytes 688136 | tf_op jit(solution)/shard_map/ppermute | solution.py:378
  84.0 37.5 %copy-start.1 = (bf16[256,1792]{1,0:T(8,128)(2,1)S(1)}, bf16[256,1792]{1,0:T(8,128)(2,1)}, u32[]{:S(2)}) copy-start(bf16[256,1792]{1,0:T(8,128)(2,1)} %param.21) | copy-start | bytes 2752516
  86.7 1.9 %collective-permute-start.27 = (bf16[128,1792]{1,0:T(8,128)(2,1)S(1)}, bf16[128,1792]{1,0:T(8,128)(2,1)S(1)}, u32[]{:S(2)}, u32[]{:S(2)}) collective-permute-start(bf16[128,1792]{1,0:T(8,128)(2,1)S(1)} %get-tuple-element.42), channel_id=1, source_target_pairs={{0,4},{4,0},{8,12},{12,8},{1,5},{5,1},{9,13},{13,9},{2,6},{6,2},{1... | collective-permute-start | bytes 1376264 | tf_op jit(solution)/shard_map/ppermute | solution.py:378
  86.9 2.4 %collective-permute-start.25 = (bf16[128,1792]{1,0:T(8,128)(2,1)S(1)}, bf16[128,1792]{1,0:T(8,128)(2,1)S(1)}, u32[]{:S(2)}, u32[]{:S(2)}) collective-permute-start(bf16[128,1792]{1,0:T(8,128)(2,1)S(1)} %get-tuple-element.39), channel_id=1, source_target_pairs={{0,4},{4,0},{8,12},{12,8},{1,5},{5,1},{9,13},{13,9},{2,6},{6,2},{1... | collective-permute-start | bytes 1376264 | tf_op jit(solution)/shard_map/ppermute | solution.py:378
  87.3 12.0 %collective-permute-start.32 = (bf16[128,1792]{1,0:T(8,128)(2,1)S(1)}, bf16[128,1792]{1,0:T(8,128)(2,1)S(1)}, u32[]{:S(2)}, u32[]{:S(2)}) collective-permute-start(bf16[128,1792]{1,0:T(8,128)(2,1)S(1)} %get-tuple-element.49), channel_id=1, source_target_pairs={{0,4},{4,0},{8,12},{12,8},{1,5},{5,1},{9,13},{13,9},{2,6},{6,2},{1... | collective-permute-start | bytes 1376264 | tf_op jit(solution)/shard_map/ppermute | solution.py:378
  87.4 12.5 %collective-permute-start.24 = (bf16[128,1792]{1,0:T(8,128)(2,1)S(1)}, bf16[128,1792]{1,0:T(8,128)(2,1)S(1)}, u32[]{:S(2)}, u32[]{:S(2)}) collective-permute-start(bf16[128,1792]{1,0:T(8,128)(2,1)S(1)} %get-tuple-element.37), channel_id=1, source_target_pairs={{0,4},{4,0},{8,12},{12,8},{1,5},{5,1},{9,13},{13,9},{2,6},{6,2},{1... | collective-permute-start | bytes 1376264 | tf_op jit(solution)/shard_map/ppermute | solution.py:378
  88.7 8.5 %collective-permute-start.28 = (bf16[64,1792]{1,0:T(8,128)(2,1)S(1)}, bf16[64,1792]{1,0:T(8,128)(2,1)S(1)}, u32[]{:S(2)}, u32[]{:S(2)}) collective-permute-start(bf16[64,1792]{1,0:T(8,128)(2,1)S(1)} %get-tuple-element.44), channel_id=1, source_target_pairs={{0,8},{4,12},{8,0},{12,4},{1,9},{5,13},{9,1},{13,5},{2,10},{6,14},... | collective-permute-start | bytes 688136 | tf_op jit(solution)/shard_map/ppermute | solution.py:382
  89.4 12.7 %collective-permute-start.26 = (bf16[64,1792]{1,0:T(8,128)(2,1)S(1)}, bf16[64,1792]{1,0:T(8,128)(2,1)S(1)}, u32[]{:S(2)}, u32[]{:S(2)}) collective-permute-start(bf16[64,1792]{1,0:T(8,128)(2,1)S(1)} %get-tuple-element.40), channel_id=1, source_target_pairs={{0,8},{4,12},{8,0},{12,4},{1,9},{5,13},{9,1},{13,5},{2,10},{6,14},... | collective-permute-start | bytes 688136 | tf_op jit(solution)/shard_map/ppermute | solution.py:382
  97.2 6.3 %collective-permute-start.30 = (bf16[64,1792]{1,0:T(8,128)(2,1)S(1)}, bf16[64,1792]{1,0:T(8,128)(2,1)S(1)}, u32[]{:S(2)}, u32[]{:S(2)}) collective-permute-start(bf16[64,1792]{1,0:T(8,128)(2,1)S(1)} %add.69.refs_5_.refs_3_), channel_id=1, source_target_pairs={{0,1},{1,0},{2,3},{3,2},{4,5},{5,4},{6,7},{7,6},{8,9},{9,8},{10,11... | collective-permute-start | bytes 688136 | tf_op jit(solution)/shard_map/ppermute | solution.py:385
  99.4 8.6 %collective-permute-start.33 = (bf16[64,1792]{1,0:T(8,128)(2,1)S(1)}, bf16[64,1792]{1,0:T(8,128)(2,1)S(1)}, u32[]{:S(2)}, u32[]{:S(2)}) collective-permute-start(bf16[64,1792]{1,0:T(8,128)(2,1)S(1)} %get-tuple-element.51), channel_id=1, source_target_pairs={{0,8},{4,12},{8,0},{12,4},{1,9},{5,13},{9,1},{13,5},{2,10},{6,14},... | collective-permute-start | bytes 688136 | tf_op jit(solution)/shard_map/ppermute | solution.py:382
  102.2 8.9 %collective-permute-start.29 = (bf16[64,1792]{1,0:T(8,128)(2,1)S(1)}, bf16[64,1792]{1,0:T(8,128)(2,1)S(1)}, u32[]{:S(2)}, u32[]{:S(2)}) collective-permute-start(bf16[64,1792]{1,0:T(8,128)(2,1)S(1)} %get-tuple-element.46), channel_id=1, source_target_pairs={{0,8},{4,12},{8,0},{12,4},{1,9},{5,13},{9,1},{13,5},{2,10},{6,14},... | collective-permute-start | bytes 688136 | tf_op jit(solution)/shard_map/ppermute | solution.py:382
  108.0 8.9 %collective-permute-start.34 = (bf16[64,1792]{1,0:T(8,128)(2,1)S(1)}, bf16[64,1792]{1,0:T(8,128)(2,1)S(1)}, u32[]{:S(2)}, u32[]{:S(2)}) collective-permute-start(bf16[64,1792]{1,0:T(8,128)(2,1)S(1)} %add.73), channel_id=1, source_target_pairs={{0,1},{1,0},{2,3},{3,2},{4,5},{5,4},{6,7},{7,6},{8,9},{9,8},{10,11... | collective-permute-start | bytes 688136 | tf_op jit(solution)/shard_map/ppermute | solution.py:385
  109.1 11.6 %collective-permute-start.31 = (bf16[64,1792]{1,0:T(8,128)(2,1)S(1)}, bf16[64,1792]{1,0:T(8,128)(2,1)S(1)}, u32[]{:S(2)}, u32[]{:S(2)}) collective-permute-start(bf16[64,1792]{1,0:T(8,128)(2,1)S(1)} %add.71.refs_2_), channel_id=1, source_target_pairs={{0,2},{1,3},{2,0},{3,1},{4,6},{5,7},{6,4},{7,5},{8,10},{9,11},{10,... | collective-permute-start | bytes 688136 | tf_op jit(solution)/shard_map/ppermute | solution.py:385

commit v12 on v11

--- a/solution.py
+++ b/solution.py
@@ -47,8 +47,8 @@
     )(in_hbm(value), *after)
 
 
-def attention_kernel(step_rows, pieces, ahead, lengths, q_ref, qr_ref, k_hbm, kr_hbm, up_ref, *refs):
-    out_ref, latent, rope, k_ref, kr_ref, sems = refs[-6:]
+def attention_kernel(step_rows, pieces, ahead, lengths, q_ref, qr_ref, k_hbm, kr_hbm, up_hbm, *refs):
+    out_ref, latent, rope, k_ref, kr_ref, up_ref, sems, up_sem = refs[-8:]
     step = pl.program_id(0)
     steps = k_ref.shape[0] // step_rows
     heads, positions = q_ref.shape[1], k_ref.shape[1]
@@ -67,6 +67,7 @@
         for at in range(min(ahead, steps)):
             for copy in copies(at):
                 copy.start()
+        pltpu.make_async_copy(up_hbm, up_ref, up_sem).start()
         all_rows = qr_ref.shape[0]
         width = heads * rope_width
         lane = lax.broadcasted_iota(jnp.int32, (heads, width), 1)
@@ -114,6 +115,7 @@
 
     @pl.when(step == pl.num_programs(0) - 1)
     def _():
+        pltpu.make_async_copy(up_hbm, up_ref, up_sem).wait()
         rows = out_ref.shape[0]
         width = up_ref.shape[2]
         for h in range(heads):
@@ -141,7 +143,7 @@
                 pl.BlockSpec(query_rope.shape, lambda i, lengths: (0, 0)),
                 pl.BlockSpec(memory_space=pl.ANY),
                 pl.BlockSpec(memory_space=pl.ANY),
-                pl.BlockSpec(value_up.shape, lambda i, lengths: (0, 0, 0)),
+                pl.BlockSpec(memory_space=pl.ANY),
             ]
             + [pl.BlockSpec(memory_space=pl.ANY)] * len(after),
             out_specs=pl.BlockSpec((rows, heads * value_width), lambda i, lengths: (0, 0)),
@@ -150,7 +152,9 @@
                 pltpu.VMEM((rows * heads, rope_width), jnp.float32),
                 pltpu.VMEM(cache_latent.shape, jnp.bfloat16),
                 pltpu.VMEM(cache_rope.shape, jnp.bfloat16),
+                pltpu.VMEM(value_up.shape, jnp.bfloat16),
                 pltpu.SemaphoreType.DMA((rows // step_rows, pieces + 1)),
+                pltpu.SemaphoreType.DMA,
             ],
         ),
         cost_estimate=pl.CostEstimate(
@@ -270,7 +274,7 @@
         cost_estimate=pl.CostEstimate(
             flops=4 * rows * hidden * count * width, bytes_accessed=4 * hidden * count * width, transcendentals=0
         ),
-        compiler_params=pltpu.CompilerParams(vmem_limit_bytes=2 * rows * (count * width + 8 * hidden) + 4 * MIB),
+        compiler_params=pltpu.CompilerParams(vmem_limit_bytes=2 * rows * (count * width + 8 * hidden) + 12 * MIB),
         name="activate",
     )(places, *[b for row in blocks for b in row], *gains, in_vmem(gate_weight), in_vmem(up_weight), *before)
 
@@ -332,16 +336,16 @@
             value = refs[at][first : first + out.shape[0], :].astype(jnp.float32)
             total = value if total is None else total + value
             at += 1
-        out[...] = total.astype(jnp.bfloat16)
-
-
-def add(groups, height, after=()):
+        out[...] = total.astype(out.dtype)
+
+
+def add(groups, height, after=(), kind=jnp.bfloat16):
     values = [value for group in groups for value, _ in group]
     width = values[0].shape[1]
     whole = pl.BlockSpec(memory_space=pltpu.VMEM)
     return pl.pallas_call(
         functools.partial(add_kernel, [[first for _, first in group] for group in groups]),
-        out_shape=[jax.ShapeDtypeStruct((height, width), jnp.bfloat16)] * len(groups),
+        out_shape=[jax.ShapeDtypeStruct((height, width), kind)] * len(groups),
         in_specs=[whole] * len(values) + [pl.BlockSpec(memory_space=pl.ANY)] * len(after),
         out_specs=[whole] * len(groups),
         compiler_params=pltpu.CompilerParams(vmem_limit_bytes=8 * MIB),
@@ -448,21 +452,22 @@
         return total
 
     terms = [[] for _ in range(tp_count)]
-    arrivals = []
+    arrivals, sent = [], []
     outs = project_down(places, active, row_weight, down_weight, slots, 0, block_rows, ep_count, cores, [])
     swapped = [from_core(out[1]) for out in outs]
     for at, k in enumerate(slots):
-        before = arrivals[-2] + sent if len(arrivals) > 1 else []
+        before = arrivals[-2] + sent[0] if len(arrivals) > 1 else []
         pair = [[(outs[at][0], c * block_rows), (swapped[at], c * block_rows)] for c in range(chips)]
         added = add(pair, block_rows, before)
         across = [from_chip(added[c], chips - c) for c in range(1, chips)]
         arrivals.append(across)
         terms[k] += [(value, 0) for value in [added[0]] + across]
         if at == 0:
-            sent = send_back(k, [])
+            sent = [send_back(k, [])]
     for k in slots[1:-1]:
-        sent = send_back(k, sent)
-    (mixed,) = add([terms[0]], block_rows)
+        send_back(k, [])
+    (most,) = add([terms[0][:-1]], block_rows, (), jnp.float32)
+    (mixed,) = add([[(most, 0), terms[0][-1]]], block_rows)
     return (stream_out, mixed)
 
 

time: 122 us -> 118 us (0.967)
  waiting for transfers between devices: 56.1 us -> 51.4 us
    ppermute x9, waiting for transfers between devices: 24.9 us -> 21.1 us  [from_tp(): return lax.ppermute(value, 'tp', [(i, i ^ bits) for i in range(tp_count)])]
  transfers between devices with their start and end apart: 35 -> 35, of which waited for: 19 -> 19; matrix products, arithmetic and copies ran while one was open for 0% -> 0% of each run, Pallas kernels for 12% -> 13%
where the time goes in v12:
time: 118 us
  waiting for transfers between devices  51.4 us (44%)
  Pallas kernels  36.3 us (31%)
  starting transfers between devices  28 us (24%)
    ppermute x10, waiting for transfers between devices, from_chip(): lax.ppermute(value, 'ep', [(i, (i + step) % ep_count) for i in range(ep_c...  28 us
    ppermute x9, waiting for transfers between devices, from_tp(): return lax.ppermute(value, 'tp', [(i, i ^ bits) for i in range(tp_count)])  21.1 us
    ppermute x9, starting transfers between devices, from_tp(): return lax.ppermute(value, 'tp', [(i, i ^ bits) for i in range(tp_count)])  14 us
    pallas_call x1, Pallas kernels, attend(): pl.pallas_call(functools.partial(attention_kernel, step_rows, pieces, ahe...  12.3 us
    ppermute x10, starting transfers between devices, from_chip(): lax.ppermute(value, 'ep', [(i, (i + step) % ep_count) for i in range(ep_c...  12.2 us
    pallas_call x4, Pallas kernels, fetch(): pl.pallas_call(functools.partial(fetch_kernel, parts), out_shape=pltpu.VM...  11.6 us
    pallas_call x2, Pallas kernels, activate(): pl.pallas_call(functools.partial(gate_kernel, row_blocks, cores, first, c...  5.55 us
    pallas_call x1, Pallas kernels, project_down(): pl.pallas_call(functools.partial(down_kernel, slots, at, column_blocks, c...  2.7 us
  transfers between devices with their start and end apart: 35, of which 19 were waited for; matrix products, arithmetic and copies ran while one was open for 0% of the time, Pallas kernels for 13%

profile of v12, /device:TPU:0, one launch (start us, length us, event | category | flops | bytes accessed | tf_op | source)
XLA Modules:
  0.0 117.7 jit_solution(6939223915659810880)
XLA Ops:
  0.8 0.7 copy-done.2
  1.5 12.3 %attention.1.refs_1_.refs_0_ = bf16[64,1024]{1,0:T(8,128)(2,1)S(1)} custom-call(s32[64]{0:T(128)S(1)} %copy-done.2, bf16[64,8,512]{2,1,0:T(8,128)(2,1)} %q_ref.1, bf16[64,512]{1,0:T(8,128)(2,1)} %qr_ref.1, bf16[64,256,512]{2,1,0:T(8,128)(2,1)} %k_hbm.1, bf16[64,64,256]{2,1,0:T(8,128)(2,1)} %kr_hbm.1, bf16[8,512,128]{2,1,0:T(8,128)(2,1)} %up_hbm.1, ...), custom_call_target="tpu_custom_call" | custom-call | flops 4294967296 | bytes 16777216 | tf_op jit(solution)/shard_map/attention/pallas_call | solution.py:135
  13.9 3.0 %collective-permute-start.1 = (bf16[64,1024]{1,0:T(8,128)(2,1)S(1)}, bf16[64,1024]{1,0:T(8,128)(2,1)S(1)}, u32[]{:S(2)}, u32[]{:S(2)}) collective-permute-start(bf16[64,1024]{1,0:T(8,128)(2,1)S(1)} %attention.1.refs_1_.refs_0_), channel_id=1, source_target_pairs={{0,8},{4,12},{8,0},{12,4},{1,9},{5,13},{9,1},{13,5},{2,10},{6,14},... | collective-permute-start | bytes 393224 | tf_op jit(solution)/shard_map/ppermute | solution.py:386
  17.1 3.3 %collective-permute-done.1.refs_2_ = bf16[64,1024]{1,0:T(8,128)(2,1)S(1)} collective-permute-done((bf16[64,1024]{1,0:T(8,128)(2,1)S(1)}, bf16[64,1024]{1,0:T(8,128)(2,1)S(1)}, u32[]{:S(2)}, u32[]{:S(2)}) %collective-permute-start.1) | collective-permute-done | bytes 131104 | tf_op jit(solution)/shard_map/ppermute | solution.py:386
  20.4 2.0 %fetch.4.refs_4_ = bf16[1024,1792]{1,0:T(8,128)(2,1)S(1)} custom-call(bf16[1024,1792]{1,0:T(8,128)(2,1)} %refs_0_.4, bf16[64,1024]{1,0:T(8,128)(2,1)S(1)} %attention.1.refs_1_.refs_0_, f32[256,1]{1,0:T(8,128)S(1)} %copy.16.refs_2_.row_weight, bf16[64,1792]{1,0:T(8,128)(2,1)S(1)} %constant_dynamic-slice_fusion.refs_3_.refs_7_, ...), custom_call_target="tpu_custom_call" | custom-call | bytes 7340032 | tf_op jit(solution)/shard_map/fetch/pallas_call | solution.py:38
  22.5 1.8 %projection.1 = (bf16[64,1792]{1,0:T(8,128)(2,1)S(1)}, bf16[64,1792]{1,0:T(8,128)(2,1)S(1)}, bf16[64,1792]{1,0:T(8,128)(2,1)S(1)}, bf16[64,1792]{1,0:T(8,128)(2,1)S(1)}) custom-call(s32[8]{0:T(128)S(1)} %stack.35.refs_0_.places, bf16[64,1024]{1,0:T(8,128)(2,1)S(1)} %attention.1.refs_1_.refs_0_, bf16[64,1024]{1,0:T(8,128)(2,1)S(1)} %collective-permute-done.refs_1_, ...), custom_call_target="tpu_custom_call" | custom-call | flops 939524096 | bytes 4194304 | tf_op jit(solution)/shard_map/projection/pallas_call | solution.py:200
  24.2 1.9 %collective-permute-start.3 = (bf16[64,1792]{1,0:T(8,128)(2,1)S(1)}, bf16[64,1792]{1,0:T(8,128)(2,1)S(1)}, u32[]{:S(2)}, u32[]{:S(2)}) collective-permute-start(bf16[64,1792]{1,0:T(8,128)(2,1)S(1)} %get-tuple-element.29), channel_id=1, source_target_pairs={{0,1},{1,0},{2,3},{3,2},{4,5},{5,4},{6,7},{7,6},{8,9},{9,8},{10,11... | collective-permute-start | bytes 688136 | tf_op jit(solution)/shard_map/ppermute | solution.py:389
  26.1 3.2 %fetch.5.refs_1_.refs_12_.refs_10_ = bf16[1,7168,512]{2,1,0:T(8,128)(2,1)S(1)} custom-call(bf16[1,7168,512]{2,1,0:T(8,128)(2,1)} %refs_0_.5, bf16[64,1792]{1,0:T(8,128)(2,1)S(1)} %get-tuple-element.27.refs_1_.refs_0_.refs_4_), custom_call_target="tpu_custom_call" | custom-call | bytes 14680064 | tf_op jit(solution)/shard_map/fetch/pallas_call | solution.py:38
  29.6 2.9 %collective-permute-done.3.refs_1_ = bf16[64,1792]{1,0:T(8,128)(2,1)S(1)} collective-permute-done((bf16[64,1792]{1,0:T(8,128)(2,1)S(1)}, bf16[64,1792]{1,0:T(8,128)(2,1)S(1)}, u32[]{:S(2)}, u32[]{:S(2)}) %collective-permute-start.3) | collective-permute-done | bytes 229408 | tf_op jit(solution)/shard_map/ppermute | solution.py:389
  32.6 3.0 %collective-permute-start.4 = (bf16[64,1792]{1,0:T(8,128)(2,1)S(1)}, bf16[64,1792]{1,0:T(8,128)(2,1)S(1)}, u32[]{:S(2)}, u32[]{:S(2)}) collective-permute-start(bf16[64,1792]{1,0:T(8,128)(2,1)S(1)} %add.63), channel_id=1, source_target_pairs={{0,2},{1,3},{2,0},{3,1},{4,6},{5,7},{6,4},{7,5},{8,10},{9,11},{10,... | collective-permute-start | bytes 688136 | tf_op jit(solution)/shard_map/ppermute | solution.py:389
  35.5 1.5 %collective-permute-start.7 = (f32[1,1792]{1,0:T(1,128)S(1)}, f32[1,1792]{1,0:T(1,128)S(1)}, u32[]{:S(2)}, u32[]{:S(2)}) collective-permute-start(f32[1,1792]{1,0:T(1,128)S(1)} %reshape.7.refs_4_.refs_8_), channel_id=1, source_target_pairs={{0,8},{4,12},{8,0},{12,4},{1,9},{5,13},{9,1},{13,5},{2,10},{6,14},... | collective-permute-start | bytes 21512 | tf_op jit(solution)/shard_map/ppermute | solution.py:386
  37.0 2.1 %collective-permute-done.7.refs_10_.refs_8_ = f32[1,1792]{1,0:T(1,128)S(1)} collective-permute-done((f32[1,1792]{1,0:T(1,128)S(1)}, f32[1,1792]{1,0:T(1,128)S(1)}, u32[]{:S(2)}, u32[]{:S(2)}) %collective-permute-start.7) | collective-permute-done | bytes 7200 | tf_op jit(solution)/shard_map/ppermute | solution.py:386
  39.2 3.2 %fetch.6.refs_13_.refs_11_ = bf16[1,7168,512]{2,1,0:T(8,128)(2,1)S(1)} custom-call(bf16[1,7168,512]{2,1,0:T(8,128)(2,1)} %refs_0_.6, bf16[64,1792]{1,0:T(8,128)(2,1)S(1)} %add.64.refs_1_), custom_call_target="tpu_custom_call" | custom-call | bytes 14680064 | tf_op jit(solution)/shard_map/fetch/pallas_call | solution.py:38
  42.4 3.2 %fetch.7.refs_14_.down = bf16[1,512,7168]{2,1,0:T(8,128)(2,1)S(1)} custom-call(bf16[1,512,7168]{2,1,0:T(8,128)(2,1)} %refs_0_.7, bf16[64,1792]{1,0:T(8,128)(2,1)S(1)} %add.64.refs_1_), custom_call_target="tpu_custom_call" | custom-call | bytes 14680064 | tf_op jit(solution)/shard_map/fetch/pallas_call | solution.py:38
  45.7 0.8 add.65
  46.6 1.5 %collective-permute-start.10 = (bf16[64,1792]{1,0:T(8,128)(2,1)S(1)}, bf16[64,1792]{1,0:T(8,128)(2,1)S(1)}, u32[]{:S(2)}, u32[]{:S(2)}) collective-permute-start(bf16[64,1792]{1,0:T(8,128)(2,1)S(1)} %get-tuple-element.32.refs_6_), channel_id=1, source_target_pairs={{0,8},{4,12},{8,0},{12,4},{1,9},{5,13},{9,1},{13,5},{2,10},{6,14},... | collective-permute-start | bytes 688136 | tf_op jit(solution)/shard_map/ppermute | solution.py:386
  48.3 4.0 %collective-permute-start.16 = (bf16[64,1792]{1,0:T(8,128)(2,1)S(1)}, bf16[64,1792]{1,0:T(8,128)(2,1)S(1)}, u32[]{:S(2)}, u32[]{:S(2)}) collective-permute-start(bf16[64,1792]{1,0:T(8,128)(2,1)S(1)} %get-tuple-element.32.refs_6_), channel_id=1, source_target_pairs={{0,1},{1,0},{2,3},{3,2},{4,5},{5,4},{6,7},{7,6},{8,9},{9,8},{10,11... | collective-permute-start | bytes 688136 | tf_op jit(solution)/shard_map/ppermute | solution.py:389
  52.3 2.2 %collective-permute-done.10.refs_1_.refs_0_.refs_6_ = bf16[64,1792]{1,0:T(8,128)(2,1)S(1)} collective-permute-done((bf16[64,1792]{1,0:T(8,128)(2,1)S(1)}, bf16[64,1792]{1,0:T(8,128)(2,1)S(1)}, u32[]{:S(2)}, u32[]{:S(2)}) %collective-permute-start.10) | collective-permute-done | bytes 229408 | tf_op jit(solution)/shard_map/ppermute | solution.py:386
  54.5 7.0 %collective-permute-done.9.refs_0_.refs_2_ = bf16[64,1792]{1,0:T(8,128)(2,1)S(1)} collective-permute-done((bf16[64,1792]{1,0:T(8,128)(2,1)S(1)}, bf16[64,1792]{1,0:T(8,128)(2,1)S(1)}, u32[]{:S(2)}, u32[]{:S(2)}) %collective-permute-start.9) | collective-permute-done | bytes 229408 | tf_op jit(solution)/shard_map/ppermute | solution.py:389
  61.7 0.6 collective-permute-start.14
  62.4 1.5 %collective-permute-start.17 = (bf16[64,1792]{1,0:T(8,128)(2,1)S(1)}, bf16[64,1792]{1,0:T(8,128)(2,1)S(1)}, u32[]{:S(2)}, u32[]{:S(2)}) collective-permute-start(bf16[64,1792]{1,0:T(8,128)(2,1)S(1)} %collective-permute-done.16.refs_4_), channel_id=1, source_target_pairs={{0,8},{4,12},{8,0},{12,4},{1,9},{5,13},{9,1},{13,5},{2,10},{6,14},... | collective-permute-start | bytes 688136 | tf_op jit(solution)/shard_map/ppermute | solution.py:386
  63.8 4.5 %collective-permute-done.11.refs_0_ = bf16[64,1792]{1,0:T(8,128)(2,1)S(1)} collective-permute-done((bf16[64,1792]{1,0:T(8,128)(2,1)S(1)}, bf16[64,1792]{1,0:T(8,128)(2,1)S(1)}, u32[]{:S(2)}, u32[]{:S(2)}) %collective-permute-start.11) | collective-permute-done | bytes 229408 | tf_op jit(solution)/shard_map/ppermute | solution.py:389
  68.4 0.7 collective-permute-start.12
  69.0 1.2 collective-permute-done.14.refs_2_
  70.2 4.9 %collective-permute-done.17.refs_4_ = bf16[64,1792]{1,0:T(8,128)(2,1)S(1)} collective-permute-done((bf16[64,1792]{1,0:T(8,128)(2,1)S(1)}, bf16[64,1792]{1,0:T(8,128)(2,1)S(1)}, u32[]{:S(2)}, u32[]{:S(2)}) %collective-permute-start.17) | collective-permute-done | bytes 229408 | tf_op jit(solution)/shard_map/ppermute | solution.py:386
  75.1 2.7 %activate.2 = (f32[256,512]{1,0:T(8,128)S(1)}, f32[256,512]{1,0:T(8,128)S(1)}, f32[256,1]{1,0:T(8,128)S(1)}) custom-call(s32[8]{0:T(128)S(1)} %stack.35.refs_0_.places, bf16[64,1792]{1,0:T(8,128)(2,1)S(1)} %collective-permute-done.11.refs_0_, bf16[64,1792]{1,0:T(8,128)(2,1)S(1)} %collective-permute-done.19.refs_1_, ...), custom_call_target="tpu_custom_call" | custom-call | flops 1879048192 | bytes 7340032 | tf_op jit(solution)/shard_map/activate/pallas_call | solution.py:268
  77.8 0.6 collective-permute-start.23
  78.4 1.2 collective-permute-done.12.refs_0_
  79.6 1.5 %collective-permute-done.13.refs_1_ = bf16[64,1792]{1,0:T(8,128)(2,1)S(1)} collective-permute-done((bf16[64,1792]{1,0:T(8,128)(2,1)S(1)}, bf16[64,1792]{1,0:T(8,128)(2,1)S(1)}, u32[]{:S(2)}, u32[]{:S(2)}) %collective-permute-start.13) | collective-permute-done | bytes 229408 | tf_op jit(solution)/shard_map/ppermute | solution.py:382
  81.1 2.9 %activate.3.active = bf16[256,512]{1,0:T(8,128)(2,1)S(1)} custom-call(s32[8]{0:T(128)S(1)} %stack.35.refs_0_.places, bf16[64,1792]{1,0:T(8,128)(2,1)S(1)} %collective-permute-done.12.refs_0_, bf16[64,1792]{1,0:T(8,128)(2,1)S(1)} %collective-permute-done.13.refs_1_, bf16[64,1792]{1,0:T(8,128)(2,1)S(1)} %collective-permute-done.14.refs_2_, ...), custom_call_target="tpu_custom_call" | custom-call | flops 1879048192 | bytes 7340032 | tf_op jit(solution)/shard_map/activate/pallas_call | solution.py:268
  83.9 2.7 %down.1 = (bf16[128,1792]{1,0:T(8,128)(2,1)S(1)}, bf16[128,1792]{1,0:T(8,128)(2,1)S(1)}, bf16[128,1792]{1,0:T(8,128)(2,1)S(1)}, bf16[128,1792]{1,0:T(8,128)(2,1)...) custom-call(s32[8]{0:T(128)S(1)} %stack.35.refs_0_.places, ...), custom_call_target="tpu_custom_call" | custom-call | flops 1879048192 | bytes 7340032 | tf_op jit(solution)/shard_map/down/pallas_call | solution.py:313
  86.8 0.4 collective-permute-start.25
  87.7 0.8 collective-permute-done.27.refs_1_.refs_3_
  88.6 0.6 collective-permute-start.28
  89.4 1.5 %collective-permute-start.26 = (bf16[64,1792]{1,0:T(8,128)(2,1)S(1)}, bf16[64,1792]{1,0:T(8,128)(2,1)S(1)}, u32[]{:S(2)}, u32[]{:S(2)}) collective-permute-start(bf16[64,1792]{1,0:T(8,128)(2,1)S(1)} %get-tuple-element.40), channel_id=1, source_target_pairs={{0,8},{4,12},{8,0},{12,4},{1,9},{5,13},{9,1},{13,5},{2,10},{6,14},... | collective-permute-start | bytes 688136 | tf_op jit(solution)/shard_map/ppermute | solution.py:386
  90.9 6.2 %collective-permute-done.28.refs_1_.refs_4_ = bf16[64,1792]{1,0:T(8,128)(2,1)S(1)} collective-permute-done((bf16[64,1792]{1,0:T(8,128)(2,1)S(1)}, bf16[64,1792]{1,0:T(8,128)(2,1)S(1)}, u32[]{:S(2)}, u32[]{:S(2)}) %collective-permute-start.28) | collective-permute-done | bytes 229408 | tf_op jit(solution)/shard_map/ppermute | solution.py:386
  97.2 2.0 %collective-permute-start.30 = (bf16[64,1792]{1,0:T(8,128)(2,1)S(1)}, bf16[64,1792]{1,0:T(8,128)(2,1)S(1)}, u32[]{:S(2)}, u32[]{:S(2)}) collective-permute-start(bf16[64,1792]{1,0:T(8,128)(2,1)S(1)} %add.70.refs_5_), channel_id=1, source_target_pairs={{0,1},{1,0},{2,3},{3,2},{4,5},{5,4},{6,7},{7,6},{8,9},{9,8},{10,11... | collective-permute-start | bytes 688136 | tf_op jit(solution)/shard_map/ppermute | solution.py:389
  99.3 0.6 collective-permute-start.33
  100.0 2.1 %collective-permute-done.26.refs_4_.refs_2_ = bf16[64,1792]{1,0:T(8,128)(2,1)S(1)} collective-permute-done((bf16[64,1792]{1,0:T(8,128)(2,1)S(1)}, bf16[64,1792]{1,0:T(8,128)(2,1)S(1)}, u32[]{:S(2)}, u32[]{:S(2)}) %collective-permute-start.26) | collective-permute-done | bytes 229408 | tf_op jit(solution)/shard_map/ppermute | solution.py:386
  102.2 0.6 collective-permute-start.29
  102.8 0.7 collective-permute-done.30.refs_0_
  103.6 1.6 %collective-permute-start.31 = (bf16[64,1792]{1,0:T(8,128)(2,1)S(1)}, bf16[64,1792]{1,0:T(8,128)(2,1)S(1)}, u32[]{:S(2)}, u32[]{:S(2)}) collective-permute-start(bf16[64,1792]{1,0:T(8,128)(2,1)S(1)} %add.72), channel_id=1, source_target_pairs={{0,2},{1,3},{2,0},{3,1},{4,6},{5,7},{6,4},{7,5},{8,10},{9,11},{10,... | collective-permute-start | bytes 688136 | tf_op jit(solution)/shard_map/ppermute | solution.py:389
  105.2 2.7 %collective-permute-done.33.refs_1_ = bf16[64,1792]{1,0:T(8,128)(2,1)S(1)} collective-permute-done((bf16[64,1792]{1,0:T(8,128)(2,1)S(1)}, bf16[64,1792]{1,0:T(8,128)(2,1)S(1)}, u32[]{:S(2)}, u32[]{:S(2)}) %collective-permute-start.33) | collective-permute-done | bytes 229408 | tf_op jit(solution)/shard_map/ppermute | solution.py:386
  108.0 1.1 collective-permute-start.34
  109.0 2.1 %collective-permute-done.29.refs_1_ = bf16[64,1792]{1,0:T(8,128)(2,1)S(1)} collective-permute-done((bf16[64,1792]{1,0:T(8,128)(2,1)S(1)}, bf16[64,1792]{1,0:T(8,128)(2,1)S(1)}, u32[]{:S(2)}, u32[]{:S(2)}) %collective-permute-start.29) | collective-permute-done | bytes 229408 | tf_op jit(solution)/shard_map/ppermute | solution.py:386
  111.1 3.7 %collective-permute-done.31.refs_2_ = bf16[64,1792]{1,0:T(8,128)(2,1)S(1)} collective-permute-done((bf16[64,1792]{1,0:T(8,128)(2,1)S(1)}, bf16[64,1792]{1,0:T(8,128)(2,1)S(1)}, u32[]{:S(2)}, u32[]{:S(2)}) %collective-permute-start.31) | collective-permute-done | bytes 229408 | tf_op jit(solution)/shard_map/ppermute | solution.py:389
  114.9 2.1 %collective-permute-done.34.refs_1_ = bf16[64,1792]{1,0:T(8,128)(2,1)S(1)} collective-permute-done((bf16[64,1792]{1,0:T(8,128)(2,1)S(1)}, bf16[64,1792]{1,0:T(8,128)(2,1)S(1)}, u32[]{:S(2)}, u32[]{:S(2)}) %collective-permute-start.34) | collective-permute-done | bytes 229408 | tf_op jit(solution)/shard_map/ppermute | solution.py:389
  117.0 0.7 add.76
  (62 shorter events, 2.6 us)
Async XLA Ops:
  0.6 19.7 %copy-start = (bf16[256,1792]{1,0:T(8,128)(2,1)S(1)}, bf16[256,1792]{1,0:T(8,128)(2,1)}, u32[]{:S(2)}) copy-start(bf16[256,1792]{1,0:T(8,128)(2,1)} %param.21) | copy-start | bytes 2752516
  0.8 0.7 copy-start.2
  1.5 15.3 %copy-start.4 = (f32[256,2]{0,1:T(2,128)S(1)}, f32[256,2]{0,1:T(2,128)}, u32[]{:S(2)}) copy-start(f32[256,2]{0,1:T(2,128)} %param.24) | copy-start | bytes 6148
  1.5 15.3 %copy-start.5 = (s32[256,2]{0,1:T(2,128)S(1)}, s32[256,2]{0,1:T(2,128)}, u32[]{:S(2)}) copy-start(s32[256,2]{0,1:T(2,128)} %param.23) | copy-start | bytes 6148
  1.5 15.5 %copy-start.3 = (f32[1792]{0:T(1024)S(1)}, f32[1792]{0:T(1024)}, u32[]{:S(2)}) copy-start(f32[1792]{0:T(1024)} %param.22) | copy-start | bytes 21508
  13.9 6.5 %collective-permute-start.1 = (bf16[64,1024]{1,0:T(8,128)(2,1)S(1)}, bf16[64,1024]{1,0:T(8,128)(2,1)S(1)}, u32[]{:S(2)}, u32[]{:S(2)}) collective-permute-start(bf16[64,1024]{1,0:T(8,128)(2,1)S(1)} %attention.1.refs_1_.refs_0_), channel_id=1, source_target_pairs={{0,8},{4,12},{8,0},{12,4},{1,9},{5,13},{9,1},{13,5},{2,10},{6,14},... | collective-permute-start | bytes 393224 | tf_op jit(solution)/shard_map/ppermute | solution.py:386
  16.9 5.6 %collective-permute-start = (bf16[64,1024]{1,0:T(8,128)(2,1)S(1)}, bf16[64,1024]{1,0:T(8,128)(2,1)S(1)}, u32[]{:S(2)}, u32[]{:S(2)}) collective-permute-start(bf16[64,1024]{1,0:T(8,128)(2,1)S(1)} %attention.1.refs_1_.refs_0_), channel_id=1, source_target_pairs={{0,4},{4,0},{8,12},{12,8},{1,5},{5,1},{9,13},{13,9},{2,6},{6,2},{1... | collective-permute-start | bytes 393224 | tf_op jit(solution)/shard_map/ppermute | solution.py:382
  20.4 2.1 %collective-permute-start.2 = (bf16[64,1024]{1,0:T(8,128)(2,1)S(1)}, bf16[64,1024]{1,0:T(8,128)(2,1)S(1)}, u32[]{:S(2)}, u32[]{:S(2)}) collective-permute-start(bf16[64,1024]{1,0:T(8,128)(2,1)S(1)} %collective-permute-done.1.refs_2_), channel_id=1, source_target_pairs={{0,4},{4,0},{8,12},{12,8},{1,5},{5,1},{9,13},{13,9},{2,6},{6,2},{1... | collective-permute-start | bytes 393224 | tf_op jit(solution)/shard_map/ppermute | solution.py:382
  24.2 8.3 %collective-permute-start.3 = (bf16[64,1792]{1,0:T(8,128)(2,1)S(1)}, bf16[64,1792]{1,0:T(8,128)(2,1)S(1)}, u32[]{:S(2)}, u32[]{:S(2)}) collective-permute-start(bf16[64,1792]{1,0:T(8,128)(2,1)S(1)} %get-tuple-element.29), channel_id=1, source_target_pairs={{0,1},{1,0},{2,3},{3,2},{4,5},{5,4},{6,7},{7,6},{8,9},{9,8},{10,11... | collective-permute-start | bytes 688136 | tf_op jit(solution)/shard_map/ppermute | solution.py:389
  29.3 16.2 %collective-permute-start.5 = (bf16[64,1792]{1,0:T(8,128)(2,1)S(1)}, bf16[64,1792]{1,0:T(8,128)(2,1)S(1)}, u32[]{:S(2)}, u32[]{:S(2)}) collective-permute-start(bf16[64,1792]{1,0:T(8,128)(2,1)S(1)} %add.64.refs_1_), channel_id=1, source_target_pairs={{0,1},{1,0},{2,3},{3,2},{4,5},{5,4},{6,7},{7,6},{8,9},{9,8},{10,11... | collective-permute-start | bytes 688136 | tf_op jit(solution)/shard_map/ppermute | solution.py:389
  32.6 13.2 %collective-permute-start.4 = (bf16[64,1792]{1,0:T(8,128)(2,1)S(1)}, bf16[64,1792]{1,0:T(8,128)(2,1)S(1)}, u32[]{:S(2)}, u32[]{:S(2)}) collective-permute-start(bf16[64,1792]{1,0:T(8,128)(2,1)S(1)} %add.63), channel_id=1, source_target_pairs={{0,2},{1,3},{2,0},{3,1},{4,6},{5,7},{6,4},{7,5},{8,10},{9,11},{10,... | collective-permute-start | bytes 688136 | tf_op jit(solution)/shard_map/ppermute | solution.py:389
  35.5 3.6 %collective-permute-start.7 = (f32[1,1792]{1,0:T(1,128)S(1)}, f32[1,1792]{1,0:T(1,128)S(1)}, u32[]{:S(2)}, u32[]{:S(2)}) collective-permute-start(f32[1,1792]{1,0:T(1,128)S(1)} %reshape.7.refs_4_.refs_8_), channel_id=1, source_target_pairs={{0,8},{4,12},{8,0},{12,4},{1,9},{5,13},{9,1},{13,5},{2,10},{6,14},... | collective-permute-start | bytes 21512 | tf_op jit(solution)/shard_map/ppermute | solution.py:386
  37.0 8.5 %collective-permute-start.6 = (f32[1,1792]{1,0:T(1,128)S(1)}, f32[1,1792]{1,0:T(1,128)S(1)}, u32[]{:S(2)}, u32[]{:S(2)}) collective-permute-start(f32[1,1792]{1,0:T(1,128)S(1)} %reshape.7.refs_4_.refs_8_), channel_id=1, source_target_pairs={{0,4},{4,0},{8,12},{12,8},{1,5},{5,1},{9,13},{13,9},{2,6},{6,2},{1... | collective-permute-start | bytes 21512 | tf_op jit(solution)/shard_map/ppermute | solution.py:382
  39.2 6.4 %collective-permute-start.8 = (f32[1,1792]{1,0:T(1,128)S(1)}, f32[1,1792]{1,0:T(1,128)S(1)}, u32[]{:S(2)}, u32[]{:S(2)}) collective-permute-start(f32[1,1792]{1,0:T(1,128)S(1)} %collective-permute-done.7.refs_10_.refs_8_), channel_id=1, source_target_pairs={{0,4},{4,0},{8,12},{12,8},{1,5},{5,1},{9,13},{13,9},{2,6},{6,2},{1... | collective-permute-start | bytes 21512 | tf_op jit(solution)/shard_map/ppermute | solution.py:382
  46.6 7.9 %collective-permute-start.10 = (bf16[64,1792]{1,0:T(8,128)(2,1)S(1)}, bf16[64,1792]{1,0:T(8,128)(2,1)S(1)}, u32[]{:S(2)}, u32[]{:S(2)}) collective-permute-start(bf16[64,1792]{1,0:T(8,128)(2,1)S(1)} %get-tuple-element.32.refs_6_), channel_id=1, source_target_pairs={{0,8},{4,12},{8,0},{12,4},{1,9},{5,13},{9,1},{13,5},{2,10},{6,14},... | collective-permute-start | bytes 688136 | tf_op jit(solution)/shard_map/ppermute | solution.py:386
  48.1 13.4 %collective-permute-start.9 = (bf16[64,1792]{1,0:T(8,128)(2,1)S(1)}, bf16[64,1792]{1,0:T(8,128)(2,1)S(1)}, u32[]{:S(2)}, u32[]{:S(2)}) collective-permute-start(bf16[64,1792]{1,0:T(8,128)(2,1)S(1)} %get-tuple-element.32.refs_6_), channel_id=1, source_target_pairs={{0,2},{1,3},{2,0},{3,1},{4,6},{5,7},{6,4},{7,5},{8,10},{9,11},{10,... | collective-permute-start | bytes 688136 | tf_op jit(solution)/shard_map/ppermute | solution.py:389
  48.3 14.1 %collective-permute-start.16 = (bf16[64,1792]{1,0:T(8,128)(2,1)S(1)}, bf16[64,1792]{1,0:T(8,128)(2,1)S(1)}, u32[]{:S(2)}, u32[]{:S(2)}) collective-permute-start(bf16[64,1792]{1,0:T(8,128)(2,1)S(1)} %get-tuple-element.32.refs_6_), channel_id=1, source_target_pairs={{0,1},{1,0},{2,3},{3,2},{4,5},{5,4},{6,7},{7,6},{8,9},{9,8},{10,11... | collective-permute-start | bytes 688136 | tf_op jit(solution)/shard_map/ppermute | solution.py:389
  52.3 11.6 %collective-permute-start.22 = (bf16[64,1792]{1,0:T(8,128)(2,1)S(1)}, bf16[64,1792]{1,0:T(8,128)(2,1)S(1)}, u32[]{:S(2)}, u32[]{:S(2)}) collective-permute-start(bf16[64,1792]{1,0:T(8,128)(2,1)S(1)} %get-tuple-element.32.refs_6_), channel_id=1, source_target_pairs={{0,4},{4,0},{8,12},{12,8},{1,5},{5,1},{9,13},{13,9},{2,6},{6,2},{1... | collective-permute-start | bytes 688136 | tf_op jit(solution)/shard_map/ppermute | solution.py:382
  61.6 6.8 %collective-permute-start.11 = (bf16[64,1792]{1,0:T(8,128)(2,1)S(1)}, bf16[64,1792]{1,0:T(8,128)(2,1)S(1)}, u32[]{:S(2)}, u32[]{:S(2)}) collective-permute-start(bf16[64,1792]{1,0:T(8,128)(2,1)S(1)} %add.66), channel_id=1, source_target_pairs={{0,1},{1,0},{2,3},{3,2},{4,5},{5,4},{6,7},{7,6},{8,9},{9,8},{10,11... | collective-permute-start | bytes 688136 | tf_op jit(solution)/shard_map/ppermute | solution.py:389
  61.6 6.7 %collective-permute-start.20 = (bf16[64,1792]{1,0:T(8,128)(2,1)S(1)}, bf16[64,1792]{1,0:T(8,128)(2,1)S(1)}, u32[]{:S(2)}, u32[]{:S(2)}) collective-permute-start(bf16[64,1792]{1,0:T(8,128)(2,1)S(1)} %collective-permute-done.9.refs_0_.refs_2_), channel_id=1, source_target_pairs={{0,4},{4,0},{8,12},{12,8},{1,5},{5,1},{9,13},{13,9},{2,6},{6,2},{1... | collective-permute-start | bytes 688136 | tf_op jit(solution)/shard_map/ppermute | solution.py:382
  61.7 8.5 %collective-permute-start.14 = (bf16[64,1792]{1,0:T(8,128)(2,1)S(1)}, bf16[64,1792]{1,0:T(8,128)(2,1)S(1)}, u32[]{:S(2)}, u32[]{:S(2)}) collective-permute-start(bf16[64,1792]{1,0:T(8,128)(2,1)S(1)} %collective-permute-done.9.refs_0_.refs_2_), channel_id=1, source_target_pairs={{0,8},{4,12},{8,0},{12,4},{1,9},{5,13},{9,1},{13,5},{2,10},{6,14},... | collective-permute-start | bytes 688136 | tf_op jit(solution)/shard_map/ppermute | solution.py:386
  62.4 12.8 %collective-permute-start.17 = (bf16[64,1792]{1,0:T(8,128)(2,1)S(1)}, bf16[64,1792]{1,0:T(8,128)(2,1)S(1)}, u32[]{:S(2)}, u32[]{:S(2)}) collective-permute-start(bf16[64,1792]{1,0:T(8,128)(2,1)S(1)} %collective-permute-done.16.refs_4_), channel_id=1, source_target_pairs={{0,8},{4,12},{8,0},{12,4},{1,9},{5,13},{9,1},{13,5},{2,10},{6,14},... | collective-permute-start | bytes 688136 | tf_op jit(solution)/shard_map/ppermute | solution.py:386
  63.8 11.3 %collective-permute-start.21 = (bf16[64,1792]{1,0:T(8,128)(2,1)S(1)}, bf16[64,1792]{1,0:T(8,128)(2,1)S(1)}, u32[]{:S(2)}, u32[]{:S(2)}) collective-permute-start(bf16[64,1792]{1,0:T(8,128)(2,1)S(1)} %collective-permute-done.16.refs_4_), channel_id=1, source_target_pairs={{0,4},{4,0},{8,12},{12,8},{1,5},{5,1},{9,13},{13,9},{2,6},{6,2},{1... | collective-permute-start | bytes 688136 | tf_op jit(solution)/shard_map/ppermute | solution.py:382
  68.4 6.8 %collective-permute-start.19 = (bf16[64,1792]{1,0:T(8,128)(2,1)S(1)}, bf16[64,1792]{1,0:T(8,128)(2,1)S(1)}, u32[]{:S(2)}, u32[]{:S(2)}) collective-permute-start(bf16[64,1792]{1,0:T(8,128)(2,1)S(1)} %collective-permute-done.11.refs_0_), channel_id=1, source_target_pairs={{0,4},{4,0},{8,12},{12,8},{1,5},{5,1},{9,13},{13,9},{2,6},{6,2},{1... | collective-permute-start | bytes 688136 | tf_op jit(solution)/shard_map/ppermute | solution.py:382
  68.4 11.2 %collective-permute-start.12 = (bf16[64,1792]{1,0:T(8,128)(2,1)S(1)}, bf16[64,1792]{1,0:T(8,128)(2,1)S(1)}, u32[]{:S(2)}, u32[]{:S(2)}) collective-permute-start(bf16[64,1792]{1,0:T(8,128)(2,1)S(1)} %collective-permute-done.11.refs_0_), channel_id=1, source_target_pairs={{0,8},{4,12},{8,0},{12,4},{1,9},{5,13},{9,1},{13,5},{2,10},{6,14},... | collective-permute-start | bytes 688136 | tf_op jit(solution)/shard_map/ppermute | solution.py:386
  70.2 9.4 %collective-permute-start.15 = (bf16[64,1792]{1,0:T(8,128)(2,1)S(1)}, bf16[64,1792]{1,0:T(8,128)(2,1)S(1)}, u32[]{:S(2)}, u32[]{:S(2)}) collective-permute-start(bf16[64,1792]{1,0:T(8,128)(2,1)S(1)} %collective-permute-done.14.refs_2_), channel_id=1, source_target_pairs={{0,4},{4,0},{8,12},{12,8},{1,5},{5,1},{9,13},{13,9},{2,6},{6,2},{1... | collective-permute-start | bytes 688136 | tf_op jit(solution)/shard_map/ppermute | solution.py:382
  75.1 4.5 %collective-permute-start.18 = (bf16[64,1792]{1,0:T(8,128)(2,1)S(1)}, bf16[64,1792]{1,0:T(8,128)(2,1)S(1)}, u32[]{:S(2)}, u32[]{:S(2)}) collective-permute-start(bf16[64,1792]{1,0:T(8,128)(2,1)S(1)} %collective-permute-done.17.refs_4_), channel_id=1, source_target_pairs={{0,4},{4,0},{8,12},{12,8},{1,5},{5,1},{9,13},{13,9},{2,6},{6,2},{1... | collective-permute-start | bytes 688136 | tf_op jit(solution)/shard_map/ppermute | solution.py:382
  77.8 1.7 %collective-permute-start.23 = (bf16[64,1792]{1,0:T(8,128)(2,1)S(1)}, bf16[64,1792]{1,0:T(8,128)(2,1)S(1)}, u32[]{:S(2)}, u32[]{:S(2)}) collective-permute-start(bf16[64,1792]{1,0:T(8,128)(2,1)S(1)} %add.67), channel_id=1, source_target_pairs={{0,4},{4,0},{8,12},{12,8},{1,5},{5,1},{9,13},{13,9},{2,6},{6,2},{1... | collective-permute-start | bytes 688136 | tf_op jit(solution)/shard_map/ppermute | solution.py:382
  79.6 1.5 %collective-permute-start.13 = (bf16[64,1792]{1,0:T(8,128)(2,1)S(1)}, bf16[64,1792]{1,0:T(8,128)(2,1)S(1)}, u32[]{:S(2)}, u32[]{:S(2)}) collective-permute-start(bf16[64,1792]{1,0:T(8,128)(2,1)S(1)} %collective-permute-done.12.refs_0_), channel_id=1, source_target_pairs={{0,4},{4,0},{8,12},{12,8},{1,5},{5,1},{9,13},{13,9},{2,6},{6,2},{1... | collective-permute-start | bytes 688136 | tf_op jit(solution)/shard_map/ppermute | solution.py:382
  83.9 33.8 %copy-start.1 = (bf16[256,1792]{1,0:T(8,128)(2,1)S(1)}, bf16[256,1792]{1,0:T(8,128)(2,1)}, u32[]{:S(2)}) copy-start(bf16[256,1792]{1,0:T(8,128)(2,1)} %param.21) | copy-start | bytes 2752516
  86.6 1.9 %collective-permute-start.27 = (bf16[128,1792]{1,0:T(8,128)(2,1)S(1)}, bf16[128,1792]{1,0:T(8,128)(2,1)S(1)}, u32[]{:S(2)}, u32[]{:S(2)}) collective-permute-start(bf16[128,1792]{1,0:T(8,128)(2,1)S(1)} %get-tuple-element.42), channel_id=1, source_target_pairs={{0,4},{4,0},{8,12},{12,8},{1,5},{5,1},{9,13},{13,9},{2,6},{6,2},{1... | collective-permute-start | bytes 1376264 | tf_op jit(solution)/shard_map/ppermute | solution.py:382
  86.8 2.4 %collective-permute-start.25 = (bf16[128,1792]{1,0:T(8,128)(2,1)S(1)}, bf16[128,1792]{1,0:T(8,128)(2,1)S(1)}, u32[]{:S(2)}, u32[]{:S(2)}) collective-permute-start(bf16[128,1792]{1,0:T(8,128)(2,1)S(1)} %get-tuple-element.39), channel_id=1, source_target_pairs={{0,4},{4,0},{8,12},{12,8},{1,5},{5,1},{9,13},{13,9},{2,6},{6,2},{1... | collective-permute-start | bytes 1376264 | tf_op jit(solution)/shard_map/ppermute | solution.py:382
  87.2 12.0 %collective-permute-start.32 = (bf16[128,1792]{1,0:T(8,128)(2,1)S(1)}, bf16[128,1792]{1,0:T(8,128)(2,1)S(1)}, u32[]{:S(2)}, u32[]{:S(2)}) collective-permute-start(bf16[128,1792]{1,0:T(8,128)(2,1)S(1)} %get-tuple-element.49), channel_id=1, source_target_pairs={{0,4},{4,0},{8,12},{12,8},{1,5},{5,1},{9,13},{13,9},{2,6},{6,2},{1... | collective-permute-start | bytes 1376264 | tf_op jit(solution)/shard_map/ppermute | solution.py:382
  87.4 12.6 %collective-permute-start.24 = (bf16[128,1792]{1,0:T(8,128)(2,1)S(1)}, bf16[128,1792]{1,0:T(8,128)(2,1)S(1)}, u32[]{:S(2)}, u32[]{:S(2)}) collective-permute-start(bf16[128,1792]{1,0:T(8,128)(2,1)S(1)} %get-tuple-element.37), channel_id=1, source_target_pairs={{0,4},{4,0},{8,12},{12,8},{1,5},{5,1},{9,13},{13,9},{2,6},{6,2},{1... | collective-permute-start | bytes 1376264 | tf_op jit(solution)/shard_map/ppermute | solution.py:382
  88.6 8.5 %collective-permute-start.28 = (bf16[64,1792]{1,0:T(8,128)(2,1)S(1)}, bf16[64,1792]{1,0:T(8,128)(2,1)S(1)}, u32[]{:S(2)}, u32[]{:S(2)}) collective-permute-start(bf16[64,1792]{1,0:T(8,128)(2,1)S(1)} %get-tuple-element.44), channel_id=1, source_target_pairs={{0,8},{4,12},{8,0},{12,4},{1,9},{5,13},{9,1},{13,5},{2,10},{6,14},... | collective-permute-start | bytes 688136 | tf_op jit(solution)/shard_map/ppermute | solution.py:386
  89.4 12.7 %collective-permute-start.26 = (bf16[64,1792]{1,0:T(8,128)(2,1)S(1)}, bf16[64,1792]{1,0:T(8,128)(2,1)S(1)}, u32[]{:S(2)}, u32[]{:S(2)}) collective-permute-start(bf16[64,1792]{1,0:T(8,128)(2,1)S(1)} %get-tuple-element.40), channel_id=1, source_target_pairs={{0,8},{4,12},{8,0},{12,4},{1,9},{5,13},{9,1},{13,5},{2,10},{6,14},... | collective-permute-start | bytes 688136 | tf_op jit(solution)/shard_map/ppermute | solution.py:386
  97.2 6.3 %collective-permute-start.30 = (bf16[64,1792]{1,0:T(8,128)(2,1)S(1)}, bf16[64,1792]{1,0:T(8,128)(2,1)S(1)}, u32[]{:S(2)}, u32[]{:S(2)}) collective-permute-start(bf16[64,1792]{1,0:T(8,128)(2,1)S(1)} %add.70.refs_5_), channel_id=1, source_target_pairs={{0,1},{1,0},{2,3},{3,2},{4,5},{5,4},{6,7},{7,6},{8,9},{9,8},{10,11... | collective-permute-start | bytes 688136 | tf_op jit(solution)/shard_map/ppermute | solution.py:389
  99.3 8.6 %collective-permute-start.33 = (bf16[64,1792]{1,0:T(8,128)(2,1)S(1)}, bf16[64,1792]{1,0:T(8,128)(2,1)S(1)}, u32[]{:S(2)}, u32[]{:S(2)}) collective-permute-start(bf16[64,1792]{1,0:T(8,128)(2,1)S(1)} %get-tuple-element.51), channel_id=1, source_target_pairs={{0,8},{4,12},{8,0},{12,4},{1,9},{5,13},{9,1},{13,5},{2,10},{6,14},... | collective-permute-start | bytes 688136 | tf_op jit(solution)/shard_map/ppermute | solution.py:386
  102.2 8.9 %collective-permute-start.29 = (bf16[64,1792]{1,0:T(8,128)(2,1)S(1)}, bf16[64,1792]{1,0:T(8,128)(2,1)S(1)}, u32[]{:S(2)}, u32[]{:S(2)}) collective-permute-start(bf16[64,1792]{1,0:T(8,128)(2,1)S(1)} %get-tuple-element.46), channel_id=1, source_target_pairs={{0,8},{4,12},{8,0},{12,4},{1,9},{5,13},{9,1},{13,5},{2,10},{6,14},... | collective-permute-start | bytes 688136 | tf_op jit(solution)/shard_map/ppermute | solution.py:386
  103.6 11.2 %collective-permute-start.31 = (bf16[64,1792]{1,0:T(8,128)(2,1)S(1)}, bf16[64,1792]{1,0:T(8,128)(2,1)S(1)}, u32[]{:S(2)}, u32[]{:S(2)}) collective-permute-start(bf16[64,1792]{1,0:T(8,128)(2,1)S(1)} %add.72), channel_id=1, source_target_pairs={{0,2},{1,3},{2,0},{3,1},{4,6},{5,7},{6,4},{7,5},{8,10},{9,11},{10,... | collective-permute-start | bytes 688136 | tf_op jit(solution)/shard_map/ppermute | solution.py:389
  108.0 9.0 %collective-permute-start.34 = (bf16[64,1792]{1,0:T(8,128)(2,1)S(1)}, bf16[64,1792]{1,0:T(8,128)(2,1)S(1)}, u32[]{:S(2)}, u32[]{:S(2)}) collective-permute-start(bf16[64,1792]{1,0:T(8,128)(2,1)S(1)} %add.75), channel_id=1, source_target_pairs={{0,1},{1,0},{2,3},{3,2},{4,5},{5,4},{6,7},{7,6},{8,9},{9,8},{10,11... | collective-permute-start | bytes 688136 | tf_op jit(solution)/shard_map/ppermute | solution.py:389

commit v13 on v12

--- a/solution.py
+++ b/solution.py
@@ -440,7 +440,12 @@
     for k in [0] + slots[:-1]:
         far[k] = []
         for b in range(1, chips):
-            value = from_chip(rows_of[k], b) if k else crossed[b - 1]
+            if k == 0:
+                value = crossed[b - 1]
+            elif k == 1:
+                value = from_tp(crossed[b - 1], 1)
+            else:
+                value = from_chip(rows_of[k], b)
             (later,) = add([[(value, 0)]], block_rows, sums[-1:]) if k == 0 else (value,)
             far[k] += [value, from_core(later)]
     active = activate(places, [far[k] for k in slots], gains[cores:], gate_weight, up_weight, cores, cores, sums)
@@ -455,19 +460,33 @@
     arrivals, sent = [], []
     outs = project_down(places, active, row_weight, down_weight, slots, 0, block_rows, ep_count, cores, [])
     swapped = [from_core(out[1]) for out in outs]
-    for at, k in enumerate(slots):
-        before = arrivals[-2] + sent[0] if len(arrivals) > 1 else []
-        pair = [[(outs[at][0], c * block_rows), (swapped[at], c * block_rows)] for c in range(chips)]
-        added = add(pair, block_rows, before)
+    def core_sums(k, after):
+        at = slots.index(k)
+        rows = [[(outs[at][0], c * block_rows), (swapped[at], c * block_rows)] for c in range(chips)]
+        return rows, after
+
+    def cross(k, extra, after):
+        rows, after = core_sums(k, after)
+        added = add([row + more for row, more in zip(rows, extra)], block_rows, after)
         across = [from_chip(added[c], chips - c) for c in range(1, chips)]
         arrivals.append(across)
         terms[k] += [(value, 0) for value in [added[0]] + across]
-        if at == 0:
-            sent = [send_back(k, [])]
-    for k in slots[1:-1]:
+
+    none = [[] for _ in range(chips)]
+    for k in slots[:-2]:
+        cross(k, none, arrivals[-2] if len(arrivals) > 1 else [])
+    rows, _ = core_sums(1, [])
+    added = add(rows, block_rows)
+    joined = [[]] + [[(from_tp(added[c], 1), 0)] for c in range(1, chips)]
+    early = [value for more in joined for value, _ in more]
+    sent = send_back(slots[0], early)
+    cross(0, joined, sent)
+    for k in slots[1:-2]:
         send_back(k, [])
-    (most,) = add([terms[0][:-1]], block_rows, (), jnp.float32)
-    (mixed,) = add([[(most, 0), terms[0][-1]]], block_rows)
+    terms[1].insert(0, (added[0], 0))
+    (kept,) = add([terms[1]], block_rows) if len(terms[1]) > 1 else (added[0],)
+    (most,) = add([terms[0]], block_rows, (), jnp.float32)
+    (mixed,) = add([[(most, 0), (from_tp(kept, 1), 0)]], block_rows)
     return (stream_out, mixed)
 
 

time: 118 us -> 115 us (0.975)
  starting transfers between devices: 28 us -> 25.8 us
    ppermute x10 -> x8, waiting for transfers between devices: 28 us -> 18.8 us  [from_chip(): lax.ppermute(value, 'ep', [(i, (i + step) % ep_count) for i in range(ep_c...]
    ppermute x9 -> x11, waiting for transfers between devices: 21.1 us -> 29.4 us  [from_tp(): return lax.ppermute(value, 'tp', [(i, i ^ bits) for i in range(tp_count)])]
    ppermute x10 -> x8, starting transfers between devices: 12.2 us -> 10.4 us  [from_chip(): lax.ppermute(value, 'ep', [(i, (i + step) % ep_count) for i in range(ep_c...]
    ppermute x9 -> x11, starting transfers between devices: 14 us -> 13.4 us  [from_tp(): return lax.ppermute(value, 'tp', [(i, i ^ bits) for i in range(tp_count)])]
    pallas_call x14 -> x13, Pallas kernels: 2.38 us -> 2.35 us  [add(): pl.pallas_call(functools.partial(add_kernel, [[first for _, first in grou...]
  transfers between devices with their start and end apart: 35 -> 35, of which waited for: 19 -> 17; matrix products, arithmetic and copies ran while one was open for 0% -> 0% of each run, Pallas kernels for 13% -> 13%
where the time goes in v13:
time: 115 us
  waiting for transfers between devices  50.8 us (44%)
  Pallas kernels  36.3 us (32%)
  starting transfers between devices  25.8 us (22%)
    ppermute x11, waiting for transfers between devices, from_tp(): return lax.ppermute(value, 'tp', [(i, i ^ bits) for i in range(tp_count)])  29.4 us
    ppermute x8, waiting for transfers between devices, from_chip(): lax.ppermute(value, 'ep', [(i, (i + step) % ep_count) for i in range(ep_c...  18.8 us
    ppermute x11, starting transfers between devices, from_tp(): return lax.ppermute(value, 'tp', [(i, i ^ bits) for i in range(tp_count)])  13.4 us
    pallas_call x1, Pallas kernels, attend(): pl.pallas_call(functools.partial(attention_kernel, step_rows, pieces, ahe...  12.3 us
    pallas_call x4, Pallas kernels, fetch(): pl.pallas_call(functools.partial(fetch_kernel, parts), out_shape=pltpu.VM...  11.6 us
    ppermute x8, starting transfers between devices, from_chip(): lax.ppermute(value, 'ep', [(i, (i + step) % ep_count) for i in range(ep_c...  10.4 us
    pallas_call x2, Pallas kernels, activate(): pl.pallas_call(functools.partial(gate_kernel, row_blocks, cores, first, c...  5.54 us
    pallas_call x1, Pallas kernels, project_down(): pl.pallas_call(functools.partial(down_kernel, slots, at, column_blocks, c...  2.7 us
  transfers between devices with their start and end apart: 35, of which 17 were waited for; matrix products, arithmetic and copies ran while one was open for 0% of the time, Pallas kernels for 13%

profile of v13, /device:TPU:0, one launch (start us, length us, event | category | flops | bytes accessed | tf_op | source)
XLA Modules:
  0.0 114.9 jit_solution(1196901973869962378)
XLA Ops:
  0.8 0.7 copy-done.2
  1.5 12.3 %attention.1.refs_1_.refs_0_ = bf16[64,1024]{1,0:T(8,128)(2,1)S(1)} custom-call(s32[64]{0:T(128)S(1)} %copy-done.2, bf16[64,8,512]{2,1,0:T(8,128)(2,1)} %q_ref.1, bf16[64,512]{1,0:T(8,128)(2,1)} %qr_ref.1, bf16[64,256,512]{2,1,0:T(8,128)(2,1)} %k_hbm.1, bf16[64,64,256]{2,1,0:T(8,128)(2,1)} %kr_hbm.1, bf16[8,512,128]{2,1,0:T(8,128)(2,1)} %up_hbm.1, ...), custom_call_target="tpu_custom_call" | custom-call | flops 4294967296 | bytes 16777216 | tf_op jit(solution)/shard_map/attention/pallas_call | solution.py:135
  13.9 3.0 %collective-permute-start.1 = (bf16[64,1024]{1,0:T(8,128)(2,1)S(1)}, bf16[64,1024]{1,0:T(8,128)(2,1)S(1)}, u32[]{:S(2)}, u32[]{:S(2)}) collective-permute-start(bf16[64,1024]{1,0:T(8,128)(2,1)S(1)} %attention.1.refs_1_.refs_0_), channel_id=1, source_target_pairs={{0,8},{4,12},{8,0},{12,4},{1,9},{5,13},{9,1},{13,5},{2,10},{6,14},... | collective-permute-start | bytes 393224 | tf_op jit(solution)/shard_map/ppermute | solution.py:386
  17.1 3.3 %collective-permute-done.1.refs_2_ = bf16[64,1024]{1,0:T(8,128)(2,1)S(1)} collective-permute-done((bf16[64,1024]{1,0:T(8,128)(2,1)S(1)}, bf16[64,1024]{1,0:T(8,128)(2,1)S(1)}, u32[]{:S(2)}, u32[]{:S(2)}) %collective-permute-start.1) | collective-permute-done | bytes 131104 | tf_op jit(solution)/shard_map/ppermute | solution.py:386
  20.4 2.0 %fetch.4.refs_4_ = bf16[1024,1792]{1,0:T(8,128)(2,1)S(1)} custom-call(bf16[1024,1792]{1,0:T(8,128)(2,1)} %refs_0_.4, bf16[64,1024]{1,0:T(8,128)(2,1)S(1)} %attention.1.refs_1_.refs_0_, f32[256,1]{1,0:T(8,128)S(1)} %copy.16.refs_2_.row_weight, bf16[64,1792]{1,0:T(8,128)(2,1)S(1)} %constant_dynamic-slice_fusion.refs_3_.refs_7_, ...), custom_call_target="tpu_custom_call" | custom-call | bytes 7340032 | tf_op jit(solution)/shard_map/fetch/pallas_call | solution.py:38
  22.5 1.8 %projection.1 = (bf16[64,1792]{1,0:T(8,128)(2,1)S(1)}, bf16[64,1792]{1,0:T(8,128)(2,1)S(1)}, bf16[64,1792]{1,0:T(8,128)(2,1)S(1)}, bf16[64,1792]{1,0:T(8,128)(2,1)S(1)}) custom-call(s32[8]{0:T(128)S(1)} %stack.35.refs_0_.places, bf16[64,1024]{1,0:T(8,128)(2,1)S(1)} %attention.1.refs_1_.refs_0_, bf16[64,1024]{1,0:T(8,128)(2,1)S(1)} %collective-permute-done.refs_1_, ...), custom_call_target="tpu_custom_call" | custom-call | flops 939524096 | bytes 4194304 | tf_op jit(solution)/shard_map/projection/pallas_call | solution.py:200
  24.2 1.9 %collective-permute-start.3 = (bf16[64,1792]{1,0:T(8,128)(2,1)S(1)}, bf16[64,1792]{1,0:T(8,128)(2,1)S(1)}, u32[]{:S(2)}, u32[]{:S(2)}) collective-permute-start(bf16[64,1792]{1,0:T(8,128)(2,1)S(1)} %get-tuple-element.29), channel_id=1, source_target_pairs={{0,1},{1,0},{2,3},{3,2},{4,5},{5,4},{6,7},{7,6},{8,9},{9,8},{10,11... | collective-permute-start | bytes 688136 | tf_op jit(solution)/shard_map/ppermute | solution.py:389
  26.1 3.2 %fetch.5.refs_1_.refs_12_.refs_10_ = bf16[1,7168,512]{2,1,0:T(8,128)(2,1)S(1)} custom-call(bf16[1,7168,512]{2,1,0:T(8,128)(2,1)} %refs_0_.5, bf16[64,1792]{1,0:T(8,128)(2,1)S(1)} %get-tuple-element.27.refs_1_.refs_0_.refs_4_), custom_call_target="tpu_custom_call" | custom-call | bytes 14680064 | tf_op jit(solution)/shard_map/fetch/pallas_call | solution.py:38
  29.3 0.3 collective-permute-start.5
  29.6 2.9 %collective-permute-done.3.refs_1_ = bf16[64,1792]{1,0:T(8,128)(2,1)S(1)} collective-permute-done((bf16[64,1792]{1,0:T(8,128)(2,1)S(1)}, bf16[64,1792]{1,0:T(8,128)(2,1)S(1)}, u32[]{:S(2)}, u32[]{:S(2)}) %collective-permute-start.3) | collective-permute-done | bytes 229408 | tf_op jit(solution)/shard_map/ppermute | solution.py:389
  32.6 3.0 %collective-permute-start.4 = (bf16[64,1792]{1,0:T(8,128)(2,1)S(1)}, bf16[64,1792]{1,0:T(8,128)(2,1)S(1)}, u32[]{:S(2)}, u32[]{:S(2)}) collective-permute-start(bf16[64,1792]{1,0:T(8,128)(2,1)S(1)} %add.62), channel_id=1, source_target_pairs={{0,2},{1,3},{2,0},{3,1},{4,6},{5,7},{6,4},{7,5},{8,10},{9,11},{10,... | collective-permute-start | bytes 688136 | tf_op jit(solution)/shard_map/ppermute | solution.py:389
  35.5 1.5 %collective-permute-start.7 = (f32[1,1792]{1,0:T(1,128)S(1)}, f32[1,1792]{1,0:T(1,128)S(1)}, u32[]{:S(2)}, u32[]{:S(2)}) collective-permute-start(f32[1,1792]{1,0:T(1,128)S(1)} %reshape.7.refs_4_.refs_8_), channel_id=1, source_target_pairs={{0,8},{4,12},{8,0},{12,4},{1,9},{5,13},{9,1},{13,5},{2,10},{6,14},... | collective-permute-start | bytes 21512 | tf_op jit(solution)/shard_map/ppermute | solution.py:386
  37.0 2.1 %collective-permute-done.7.refs_10_.refs_8_ = f32[1,1792]{1,0:T(1,128)S(1)} collective-permute-done((f32[1,1792]{1,0:T(1,128)S(1)}, f32[1,1792]{1,0:T(1,128)S(1)}, u32[]{:S(2)}, u32[]{:S(2)}) %collective-permute-start.7) | collective-permute-done | bytes 7200 | tf_op jit(solution)/shard_map/ppermute | solution.py:386
  39.2 3.2 %fetch.6.refs_13_.refs_11_ = bf16[1,7168,512]{2,1,0:T(8,128)(2,1)S(1)} custom-call(bf16[1,7168,512]{2,1,0:T(8,128)(2,1)} %refs_0_.6, bf16[64,1792]{1,0:T(8,128)(2,1)S(1)} %add.63.refs_1_), custom_call_target="tpu_custom_call" | custom-call | bytes 14680064 | tf_op jit(solution)/shard_map/fetch/pallas_call | solution.py:38
  42.4 3.2 %fetch.7.refs_14_.down = bf16[1,512,7168]{2,1,0:T(8,128)(2,1)S(1)} custom-call(bf16[1,512,7168]{2,1,0:T(8,128)(2,1)} %refs_0_.7, bf16[64,1792]{1,0:T(8,128)(2,1)S(1)} %add.63.refs_1_), custom_call_target="tpu_custom_call" | custom-call | bytes 14680064 | tf_op jit(solution)/shard_map/fetch/pallas_call | solution.py:38
  45.7 0.8 add.64
  46.6 1.5 %collective-permute-start.10 = (bf16[64,1792]{1,0:T(8,128)(2,1)S(1)}, bf16[64,1792]{1,0:T(8,128)(2,1)S(1)}, u32[]{:S(2)}, u32[]{:S(2)}) collective-permute-start(bf16[64,1792]{1,0:T(8,128)(2,1)S(1)} %get-tuple-element.32.refs_6_), channel_id=1, source_target_pairs={{0,8},{4,12},{8,0},{12,4},{1,9},{5,13},{9,1},{13,5},{2,10},{6,14},... | collective-permute-start | bytes 688136 | tf_op jit(solution)/shard_map/ppermute | solution.py:386
  48.3 4.0 %collective-permute-start.20 = (bf16[64,1792]{1,0:T(8,128)(2,1)S(1)}, bf16[64,1792]{1,0:T(8,128)(2,1)S(1)}, u32[]{:S(2)}, u32[]{:S(2)}) collective-permute-start(bf16[64,1792]{1,0:T(8,128)(2,1)S(1)} %get-tuple-element.32.refs_6_), channel_id=1, source_target_pairs={{0,1},{1,0},{2,3},{3,2},{4,5},{5,4},{6,7},{7,6},{8,9},{9,8},{10,11... | collective-permute-start | bytes 688136 | tf_op jit(solution)/shard_map/ppermute | solution.py:389
  52.3 2.2 %collective-permute-done.10.refs_1_.refs_0_.refs_6_ = bf16[64,1792]{1,0:T(8,128)(2,1)S(1)} collective-permute-done((bf16[64,1792]{1,0:T(8,128)(2,1)S(1)}, bf16[64,1792]{1,0:T(8,128)(2,1)S(1)}, u32[]{:S(2)}, u32[]{:S(2)}) %collective-permute-start.10) | collective-permute-done | bytes 229408 | tf_op jit(solution)/shard_map/ppermute | solution.py:386
  54.5 7.0 %collective-permute-done.9.refs_0_.refs_2_ = bf16[64,1792]{1,0:T(8,128)(2,1)S(1)} collective-permute-done((bf16[64,1792]{1,0:T(8,128)(2,1)S(1)}, bf16[64,1792]{1,0:T(8,128)(2,1)S(1)}, u32[]{:S(2)}, u32[]{:S(2)}) %collective-permute-start.9) | collective-permute-done | bytes 229408 | tf_op jit(solution)/shard_map/ppermute | solution.py:389
  61.7 0.6 collective-permute-start.14
  62.4 1.9 %collective-permute-start.16 = (bf16[64,1792]{1,0:T(8,128)(2,1)S(1)}, bf16[64,1792]{1,0:T(8,128)(2,1)S(1)}, u32[]{:S(2)}, u32[]{:S(2)}) collective-permute-start(bf16[64,1792]{1,0:T(8,128)(2,1)S(1)} %collective-permute-done.10.refs_1_.refs_0_.refs_6_), channel_id=1, source_target_pairs={{0,1},{1,0},{2,3},{3,2},{4,5},{5,4},{6,7},{7,6},{8,9},{9,8},{10,11... | collective-permute-start | bytes 688136 | tf_op jit(solution)/shard_map/ppermute | solution.py:389
  64.2 5.9 %collective-permute-done.11.refs_0_ = bf16[64,1792]{1,0:T(8,128)(2,1)S(1)} collective-permute-done((bf16[64,1792]{1,0:T(8,128)(2,1)S(1)}, bf16[64,1792]{1,0:T(8,128)(2,1)S(1)}, u32[]{:S(2)}, u32[]{:S(2)}) %collective-permute-start.11) | collective-permute-done | bytes 229408 | tf_op jit(solution)/shard_map/ppermute | solution.py:389
  70.2 0.6 collective-permute-start.12
  70.7 0.2 collective-permute-start.15
  71.0 2.3 %collective-permute-done.16.refs_4_ = bf16[64,1792]{1,0:T(8,128)(2,1)S(1)} collective-permute-done((bf16[64,1792]{1,0:T(8,128)(2,1)S(1)}, bf16[64,1792]{1,0:T(8,128)(2,1)S(1)}, u32[]{:S(2)}, u32[]{:S(2)}) %collective-permute-start.16) | collective-permute-done | bytes 229408 | tf_op jit(solution)/shard_map/ppermute | solution.py:389
  73.3 2.7 %activate.2 = (f32[256,512]{1,0:T(8,128)S(1)}, f32[256,512]{1,0:T(8,128)S(1)}, f32[256,1]{1,0:T(8,128)S(1)}) custom-call(s32[8]{0:T(128)S(1)} %stack.35.refs_0_.places, bf16[64,1792]{1,0:T(8,128)(2,1)S(1)} %collective-permute-done.11.refs_0_, bf16[64,1792]{1,0:T(8,128)(2,1)S(1)} %collective-permute-done.18.refs_1_, ...), custom_call_target="tpu_custom_call" | custom-call | flops 1879048192 | bytes 7340032 | tf_op jit(solution)/shard_map/activate/pallas_call | solution.py:268
  76.0 0.6 collective-permute-start.23
  76.6 1.6 %collective-permute-done.12.refs_0_ = bf16[64,1792]{1,0:T(8,128)(2,1)S(1)} collective-permute-done((bf16[64,1792]{1,0:T(8,128)(2,1)S(1)}, bf16[64,1792]{1,0:T(8,128)(2,1)S(1)}, u32[]{:S(2)}, u32[]{:S(2)}) %collective-permute-start.12) | collective-permute-done | bytes 229408 | tf_op jit(solution)/shard_map/ppermute | solution.py:386
  78.2 1.5 %collective-permute-done.13.refs_1_ = bf16[64,1792]{1,0:T(8,128)(2,1)S(1)} collective-permute-done((bf16[64,1792]{1,0:T(8,128)(2,1)S(1)}, bf16[64,1792]{1,0:T(8,128)(2,1)S(1)}, u32[]{:S(2)}, u32[]{:S(2)}) %collective-permute-start.13) | collective-permute-done | bytes 229408 | tf_op jit(solution)/shard_map/ppermute | solution.py:382
  79.7 2.8 %activate.3.active = bf16[256,512]{1,0:T(8,128)(2,1)S(1)} custom-call(s32[8]{0:T(128)S(1)} %stack.35.refs_0_.places, bf16[64,1792]{1,0:T(8,128)(2,1)S(1)} %collective-permute-done.12.refs_0_, bf16[64,1792]{1,0:T(8,128)(2,1)S(1)} %collective-permute-done.13.refs_1_, bf16[64,1792]{1,0:T(8,128)(2,1)S(1)} %collective-permute-done.14.refs_2_, ...), custom_call_target="tpu_custom_call" | custom-call | flops 1879048192 | bytes 7340032 | tf_op jit(solution)/shard_map/activate/pallas_call | solution.py:268
  82.6 2.7 %down.1 = (bf16[128,1792]{1,0:T(8,128)(2,1)S(1)}, bf16[128,1792]{1,0:T(8,128)(2,1)S(1)}, bf16[128,1792]{1,0:T(8,128)(2,1)S(1)}, bf16[128,1792]{1,0:T(8,128)(2,1)...) custom-call(s32[8]{0:T(128)S(1)} %stack.35.refs_0_.places, ...), custom_call_target="tpu_custom_call" | custom-call | flops 1879048192 | bytes 7340032 | tf_op jit(solution)/shard_map/down/pallas_call | solution.py:313
  85.5 0.4 collective-permute-start.25
  86.0 0.4 collective-permute-start.24
  86.3 0.8 collective-permute-done.27.refs_1_.refs_3_
  87.3 0.6 collective-permute-start.28
  88.1 0.4 collective-permute-done.30.refs_1_.refs_3_
  88.6 1.2 %collective-permute-start.31 = (bf16[64,1792]{1,0:T(8,128)(2,1)S(1)}, bf16[64,1792]{1,0:T(8,128)(2,1)S(1)}, u32[]{:S(2)}, u32[]{:S(2)}) collective-permute-start(bf16[64,1792]{1,0:T(8,128)(2,1)S(1)} %get-tuple-element.50), channel_id=1, source_target_pairs={{0,8},{4,12},{8,0},{12,4},{1,9},{5,13},{9,1},{13,5},{2,10},{6,14},... | collective-permute-start | bytes 688136 | tf_op jit(solution)/shard_map/ppermute | solution.py:386
  89.7 6.0 %collective-permute-done.28.refs_1_ = bf16[64,1792]{1,0:T(8,128)(2,1)S(1)} collective-permute-done((bf16[64,1792]{1,0:T(8,128)(2,1)S(1)}, bf16[64,1792]{1,0:T(8,128)(2,1)S(1)}, u32[]{:S(2)}, u32[]{:S(2)}) %collective-permute-start.28) | collective-permute-done | bytes 229408 | tf_op jit(solution)/shard_map/ppermute | solution.py:386
  95.8 0.2 collective-permute-start.32
  96.2 1.3 %collective-permute-start.29 = (bf16[64,1792]{1,0:T(8,128)(2,1)S(1)}, bf16[64,1792]{1,0:T(8,128)(2,1)S(1)}, u32[]{:S(2)}, u32[]{:S(2)}) collective-permute-start(bf16[64,1792]{1,0:T(8,128)(2,1)S(1)} %get-tuple-element.46), channel_id=1, source_target_pairs={{0,8},{4,12},{8,0},{12,4},{1,9},{5,13},{9,1},{13,5},{2,10},{6,14},... | collective-permute-start | bytes 688136 | tf_op jit(solution)/shard_map/ppermute | solution.py:386
  97.5 3.2 %collective-permute-done.31.refs_1_ = bf16[64,1792]{1,0:T(8,128)(2,1)S(1)} collective-permute-done((bf16[64,1792]{1,0:T(8,128)(2,1)S(1)}, bf16[64,1792]{1,0:T(8,128)(2,1)S(1)}, u32[]{:S(2)}, u32[]{:S(2)}) %collective-permute-start.31) | collective-permute-done | bytes 229408 | tf_op jit(solution)/shard_map/ppermute | solution.py:386
  100.7 1.8 %collective-permute-done.32.refs_2_ = bf16[64,1792]{1,0:T(8,128)(2,1)S(1)} collective-permute-done((bf16[64,1792]{1,0:T(8,128)(2,1)S(1)}, bf16[64,1792]{1,0:T(8,128)(2,1)S(1)}, u32[]{:S(2)}, u32[]{:S(2)}) %collective-permute-start.32) | collective-permute-done | bytes 229408 | tf_op jit(solution)/shard_map/ppermute | solution.py:389
  102.5 0.5 collective-permute-start.33
  103.1 1.4 %collective-permute-start.34 = (bf16[64,1792]{1,0:T(8,128)(2,1)S(1)}, bf16[64,1792]{1,0:T(8,128)(2,1)S(1)}, u32[]{:S(2)}, u32[]{:S(2)}) collective-permute-start(bf16[64,1792]{1,0:T(8,128)(2,1)S(1)} %get-tuple-element.51), channel_id=1, source_target_pairs={{0,1},{1,0},{2,3},{3,2},{4,5},{5,4},{6,7},{7,6},{8,9},{9,8},{10,11... | collective-permute-start | bytes 688136 | tf_op jit(solution)/shard_map/ppermute | solution.py:389
  104.5 0.3 collective-permute-done.29.refs_1_
  104.8 9.3 %collective-permute-done.33.refs_2_ = bf16[64,1792]{1,0:T(8,128)(2,1)S(1)} collective-permute-done((bf16[64,1792]{1,0:T(8,128)(2,1)S(1)}, bf16[64,1792]{1,0:T(8,128)(2,1)S(1)}, u32[]{:S(2)}, u32[]{:S(2)}) %collective-permute-start.33) | collective-permute-done | bytes 229408 | tf_op jit(solution)/shard_map/ppermute | solution.py:389
  114.1 0.7 add.74
  (61 shorter events, 2.0 us)
Async XLA Ops:
  0.6 19.7 %copy-start = (bf16[256,1792]{1,0:T(8,128)(2,1)S(1)}, bf16[256,1792]{1,0:T(8,128)(2,1)}, u32[]{:S(2)}) copy-start(bf16[256,1792]{1,0:T(8,128)(2,1)} %param.21) | copy-start | bytes 2752516
  0.8 0.7 copy-start.2
  1.5 15.3 %copy-start.4 = (f32[256,2]{0,1:T(2,128)S(1)}, f32[256,2]{0,1:T(2,128)}, u32[]{:S(2)}) copy-start(f32[256,2]{0,1:T(2,128)} %param.24) | copy-start | bytes 6148
  1.5 15.3 %copy-start.5 = (s32[256,2]{0,1:T(2,128)S(1)}, s32[256,2]{0,1:T(2,128)}, u32[]{:S(2)}) copy-start(s32[256,2]{0,1:T(2,128)} %param.23) | copy-start | bytes 6148
  1.5 15.5 %copy-start.3 = (f32[1792]{0:T(1024)S(1)}, f32[1792]{0:T(1024)}, u32[]{:S(2)}) copy-start(f32[1792]{0:T(1024)} %param.22) | copy-start | bytes 21508
  13.9 6.5 %collective-permute-start.1 = (bf16[64,1024]{1,0:T(8,128)(2,1)S(1)}, bf16[64,1024]{1,0:T(8,128)(2,1)S(1)}, u32[]{:S(2)}, u32[]{:S(2)}) collective-permute-start(bf16[64,1024]{1,0:T(8,128)(2,1)S(1)} %attention.1.refs_1_.refs_0_), channel_id=1, source_target_pairs={{0,8},{4,12},{8,0},{12,4},{1,9},{5,13},{9,1},{13,5},{2,10},{6,14},... | collective-permute-start | bytes 393224 | tf_op jit(solution)/shard_map/ppermute | solution.py:386
  16.9 5.6 %collective-permute-start = (bf16[64,1024]{1,0:T(8,128)(2,1)S(1)}, bf16[64,1024]{1,0:T(8,128)(2,1)S(1)}, u32[]{:S(2)}, u32[]{:S(2)}) collective-permute-start(bf16[64,1024]{1,0:T(8,128)(2,1)S(1)} %attention.1.refs_1_.refs_0_), channel_id=1, source_target_pairs={{0,4},{4,0},{8,12},{12,8},{1,5},{5,1},{9,13},{13,9},{2,6},{6,2},{1... | collective-permute-start | bytes 393224 | tf_op jit(solution)/shard_map/ppermute | solution.py:382
  20.4 2.1 %collective-permute-start.2 = (bf16[64,1024]{1,0:T(8,128)(2,1)S(1)}, bf16[64,1024]{1,0:T(8,128)(2,1)S(1)}, u32[]{:S(2)}, u32[]{:S(2)}) collective-permute-start(bf16[64,1024]{1,0:T(8,128)(2,1)S(1)} %collective-permute-done.1.refs_2_), channel_id=1, source_target_pairs={{0,4},{4,0},{8,12},{12,8},{1,5},{5,1},{9,13},{13,9},{2,6},{6,2},{1... | collective-permute-start | bytes 393224 | tf_op jit(solution)/shard_map/ppermute | solution.py:382
  24.2 8.3 %collective-permute-start.3 = (bf16[64,1792]{1,0:T(8,128)(2,1)S(1)}, bf16[64,1792]{1,0:T(8,128)(2,1)S(1)}, u32[]{:S(2)}, u32[]{:S(2)}) collective-permute-start(bf16[64,1792]{1,0:T(8,128)(2,1)S(1)} %get-tuple-element.29), channel_id=1, source_target_pairs={{0,1},{1,0},{2,3},{3,2},{4,5},{5,4},{6,7},{7,6},{8,9},{9,8},{10,11... | collective-permute-start | bytes 688136 | tf_op jit(solution)/shard_map/ppermute | solution.py:389
  29.3 16.2 %collective-permute-start.5 = (bf16[64,1792]{1,0:T(8,128)(2,1)S(1)}, bf16[64,1792]{1,0:T(8,128)(2,1)S(1)}, u32[]{:S(2)}, u32[]{:S(2)}) collective-permute-start(bf16[64,1792]{1,0:T(8,128)(2,1)S(1)} %add.63.refs_1_), channel_id=1, source_target_pairs={{0,1},{1,0},{2,3},{3,2},{4,5},{5,4},{6,7},{7,6},{8,9},{9,8},{10,11... | collective-permute-start | bytes 688136 | tf_op jit(solution)/shard_map/ppermute | solution.py:389
  32.6 13.2 %collective-permute-start.4 = (bf16[64,1792]{1,0:T(8,128)(2,1)S(1)}, bf16[64,1792]{1,0:T(8,128)(2,1)S(1)}, u32[]{:S(2)}, u32[]{:S(2)}) collective-permute-start(bf16[64,1792]{1,0:T(8,128)(2,1)S(1)} %add.62), channel_id=1, source_target_pairs={{0,2},{1,3},{2,0},{3,1},{4,6},{5,7},{6,4},{7,5},{8,10},{9,11},{10,... | collective-permute-start | bytes 688136 | tf_op jit(solution)/shard_map/ppermute | solution.py:389
  35.5 3.6 %collective-permute-start.7 = (f32[1,1792]{1,0:T(1,128)S(1)}, f32[1,1792]{1,0:T(1,128)S(1)}, u32[]{:S(2)}, u32[]{:S(2)}) collective-permute-start(f32[1,1792]{1,0:T(1,128)S(1)} %reshape.7.refs_4_.refs_8_), channel_id=1, source_target_pairs={{0,8},{4,12},{8,0},{12,4},{1,9},{5,13},{9,1},{13,5},{2,10},{6,14},... | collective-permute-start | bytes 21512 | tf_op jit(solution)/shard_map/ppermute | solution.py:386
  37.0 8.5 %collective-permute-start.6 = (f32[1,1792]{1,0:T(1,128)S(1)}, f32[1,1792]{1,0:T(1,128)S(1)}, u32[]{:S(2)}, u32[]{:S(2)}) collective-permute-start(f32[1,1792]{1,0:T(1,128)S(1)} %reshape.7.refs_4_.refs_8_), channel_id=1, source_target_pairs={{0,4},{4,0},{8,12},{12,8},{1,5},{5,1},{9,13},{13,9},{2,6},{6,2},{1... | collective-permute-start | bytes 21512 | tf_op jit(solution)/shard_map/ppermute | solution.py:382
  39.2 6.4 %collective-permute-start.8 = (f32[1,1792]{1,0:T(1,128)S(1)}, f32[1,1792]{1,0:T(1,128)S(1)}, u32[]{:S(2)}, u32[]{:S(2)}) collective-permute-start(f32[1,1792]{1,0:T(1,128)S(1)} %collective-permute-done.7.refs_10_.refs_8_), channel_id=1, source_target_pairs={{0,4},{4,0},{8,12},{12,8},{1,5},{5,1},{9,13},{13,9},{2,6},{6,2},{1... | collective-permute-start | bytes 21512 | tf_op jit(solution)/shard_map/ppermute | solution.py:382
  46.6 7.9 %collective-permute-start.10 = (bf16[64,1792]{1,0:T(8,128)(2,1)S(1)}, bf16[64,1792]{1,0:T(8,128)(2,1)S(1)}, u32[]{:S(2)}, u32[]{:S(2)}) collective-permute-start(bf16[64,1792]{1,0:T(8,128)(2,1)S(1)} %get-tuple-element.32.refs_6_), channel_id=1, source_target_pairs={{0,8},{4,12},{8,0},{12,4},{1,9},{5,13},{9,1},{13,5},{2,10},{6,14},... | collective-permute-start | bytes 688136 | tf_op jit(solution)/shard_map/ppermute | solution.py:386
  48.1 13.4 %collective-permute-start.9 = (bf16[64,1792]{1,0:T(8,128)(2,1)S(1)}, bf16[64,1792]{1,0:T(8,128)(2,1)S(1)}, u32[]{:S(2)}, u32[]{:S(2)}) collective-permute-start(bf16[64,1792]{1,0:T(8,128)(2,1)S(1)} %get-tuple-element.32.refs_6_), channel_id=1, source_target_pairs={{0,2},{1,3},{2,0},{3,1},{4,6},{5,7},{6,4},{7,5},{8,10},{9,11},{10,... | collective-permute-start | bytes 688136 | tf_op jit(solution)/shard_map/ppermute | solution.py:389
  48.3 14.1 %collective-permute-start.20 = (bf16[64,1792]{1,0:T(8,128)(2,1)S(1)}, bf16[64,1792]{1,0:T(8,128)(2,1)S(1)}, u32[]{:S(2)}, u32[]{:S(2)}) collective-permute-start(bf16[64,1792]{1,0:T(8,128)(2,1)S(1)} %get-tuple-element.32.refs_6_), channel_id=1, source_target_pairs={{0,1},{1,0},{2,3},{3,2},{4,5},{5,4},{6,7},{7,6},{8,9},{9,8},{10,11... | collective-permute-start | bytes 688136 | tf_op jit(solution)/shard_map/ppermute | solution.py:389
  52.3 12.0 %collective-permute-start.22 = (bf16[64,1792]{1,0:T(8,128)(2,1)S(1)}, bf16[64,1792]{1,0:T(8,128)(2,1)S(1)}, u32[]{:S(2)}, u32[]{:S(2)}) collective-permute-start(bf16[64,1792]{1,0:T(8,128)(2,1)S(1)} %get-tuple-element.32.refs_6_), channel_id=1, source_target_pairs={{0,4},{4,0},{8,12},{12,8},{1,5},{5,1},{9,13},{13,9},{2,6},{6,2},{1... | collective-permute-start | bytes 688136 | tf_op jit(solution)/shard_map/ppermute | solution.py:382
  61.6 8.6 %collective-permute-start.11 = (bf16[64,1792]{1,0:T(8,128)(2,1)S(1)}, bf16[64,1792]{1,0:T(8,128)(2,1)S(1)}, u32[]{:S(2)}, u32[]{:S(2)}) collective-permute-start(bf16[64,1792]{1,0:T(8,128)(2,1)S(1)} %add.65), channel_id=1, source_target_pairs={{0,1},{1,0},{2,3},{3,2},{4,5},{5,4},{6,7},{7,6},{8,9},{9,8},{10,11... | collective-permute-start | bytes 688136 | tf_op jit(solution)/shard_map/ppermute | solution.py:389
  61.6 8.5 %collective-permute-start.19 = (bf16[64,1792]{1,0:T(8,128)(2,1)S(1)}, bf16[64,1792]{1,0:T(8,128)(2,1)S(1)}, u32[]{:S(2)}, u32[]{:S(2)}) collective-permute-start(bf16[64,1792]{1,0:T(8,128)(2,1)S(1)} %collective-permute-done.9.refs_0_.refs_2_), channel_id=1, source_target_pairs={{0,4},{4,0},{8,12},{12,8},{1,5},{5,1},{9,13},{13,9},{2,6},{6,2},{1... | collective-permute-start | bytes 688136 | tf_op jit(solution)/shard_map/ppermute | solution.py:382
  61.7 9.0 %collective-permute-start.14 = (bf16[64,1792]{1,0:T(8,128)(2,1)S(1)}, bf16[64,1792]{1,0:T(8,128)(2,1)S(1)}, u32[]{:S(2)}, u32[]{:S(2)}) collective-permute-start(bf16[64,1792]{1,0:T(8,128)(2,1)S(1)} %collective-permute-done.9.refs_0_.refs_2_), channel_id=1, source_target_pairs={{0,8},{4,12},{8,0},{12,4},{1,9},{5,13},{9,1},{13,5},{2,10},{6,14},... | collective-permute-start | bytes 688136 | tf_op jit(solution)/shard_map/ppermute | solution.py:386
  62.4 10.9 %collective-permute-start.16 = (bf16[64,1792]{1,0:T(8,128)(2,1)S(1)}, bf16[64,1792]{1,0:T(8,128)(2,1)S(1)}, u32[]{:S(2)}, u32[]{:S(2)}) collective-permute-start(bf16[64,1792]{1,0:T(8,128)(2,1)S(1)} %collective-permute-done.10.refs_1_.refs_0_.refs_6_), channel_id=1, source_target_pairs={{0,1},{1,0},{2,3},{3,2},{4,5},{5,4},{6,7},{7,6},{8,9},{9,8},{10,11... | collective-permute-start | bytes 688136 | tf_op jit(solution)/shard_map/ppermute | solution.py:389
  64.2 9.1 %collective-permute-start.21 = (bf16[64,1792]{1,0:T(8,128)(2,1)S(1)}, bf16[64,1792]{1,0:T(8,128)(2,1)S(1)}, u32[]{:S(2)}, u32[]{:S(2)}) collective-permute-start(bf16[64,1792]{1,0:T(8,128)(2,1)S(1)} %collective-permute-done.20.refs_4_), channel_id=1, source_target_pairs={{0,4},{4,0},{8,12},{12,8},{1,5},{5,1},{9,13},{13,9},{2,6},{6,2},{1... | collective-permute-start | bytes 688136 | tf_op jit(solution)/shard_map/ppermute | solution.py:382
  70.2 3.1 %collective-permute-start.18 = (bf16[64,1792]{1,0:T(8,128)(2,1)S(1)}, bf16[64,1792]{1,0:T(8,128)(2,1)S(1)}, u32[]{:S(2)}, u32[]{:S(2)}) collective-permute-start(bf16[64,1792]{1,0:T(8,128)(2,1)S(1)} %collective-permute-done.11.refs_0_), channel_id=1, source_target_pairs={{0,4},{4,0},{8,12},{12,8},{1,5},{5,1},{9,13},{13,9},{2,6},{6,2},{1... | collective-permute-start | bytes 688136 | tf_op jit(solution)/shard_map/ppermute | solution.py:382
  70.2 8.0 %collective-permute-start.12 = (bf16[64,1792]{1,0:T(8,128)(2,1)S(1)}, bf16[64,1792]{1,0:T(8,128)(2,1)S(1)}, u32[]{:S(2)}, u32[]{:S(2)}) collective-permute-start(bf16[64,1792]{1,0:T(8,128)(2,1)S(1)} %collective-permute-done.11.refs_0_), channel_id=1, source_target_pairs={{0,8},{4,12},{8,0},{12,4},{1,9},{5,13},{9,1},{13,5},{2,10},{6,14},... | collective-permute-start | bytes 688136 | tf_op jit(solution)/shard_map/ppermute | solution.py:386
  70.7 7.5 %collective-permute-start.15 = (bf16[64,1792]{1,0:T(8,128)(2,1)S(1)}, bf16[64,1792]{1,0:T(8,128)(2,1)S(1)}, u32[]{:S(2)}, u32[]{:S(2)}) collective-permute-start(bf16[64,1792]{1,0:T(8,128)(2,1)S(1)} %collective-permute-done.14.refs_2_), channel_id=1, source_target_pairs={{0,4},{4,0},{8,12},{12,8},{1,5},{5,1},{9,13},{13,9},{2,6},{6,2},{1... | collective-permute-start | bytes 688136 | tf_op jit(solution)/shard_map/ppermute | solution.py:382
  73.3 4.9 %collective-permute-start.17 = (bf16[64,1792]{1,0:T(8,128)(2,1)S(1)}, bf16[64,1792]{1,0:T(8,128)(2,1)S(1)}, u32[]{:S(2)}, u32[]{:S(2)}) collective-permute-start(bf16[64,1792]{1,0:T(8,128)(2,1)S(1)} %collective-permute-done.16.refs_4_), channel_id=1, source_target_pairs={{0,4},{4,0},{8,12},{12,8},{1,5},{5,1},{9,13},{13,9},{2,6},{6,2},{1... | collective-permute-start | bytes 688136 | tf_op jit(solution)/shard_map/ppermute | solution.py:382
  76.0 2.2 %collective-permute-start.23 = (bf16[64,1792]{1,0:T(8,128)(2,1)S(1)}, bf16[64,1792]{1,0:T(8,128)(2,1)S(1)}, u32[]{:S(2)}, u32[]{:S(2)}) collective-permute-start(bf16[64,1792]{1,0:T(8,128)(2,1)S(1)} %add.66), channel_id=1, source_target_pairs={{0,4},{4,0},{8,12},{12,8},{1,5},{5,1},{9,13},{13,9},{2,6},{6,2},{1... | collective-permute-start | bytes 688136 | tf_op jit(solution)/shard_map/ppermute | solution.py:382
  78.2 1.5 %collective-permute-start.13 = (bf16[64,1792]{1,0:T(8,128)(2,1)S(1)}, bf16[64,1792]{1,0:T(8,128)(2,1)S(1)}, u32[]{:S(2)}, u32[]{:S(2)}) collective-permute-start(bf16[64,1792]{1,0:T(8,128)(2,1)S(1)} %collective-permute-done.12.refs_0_), channel_id=1, source_target_pairs={{0,4},{4,0},{8,12},{12,8},{1,5},{5,1},{9,13},{13,9},{2,6},{6,2},{1... | collective-permute-start | bytes 688136 | tf_op jit(solution)/shard_map/ppermute | solution.py:382
  82.5 32.3 %copy-start.1 = (bf16[256,1792]{1,0:T(8,128)(2,1)S(1)}, bf16[256,1792]{1,0:T(8,128)(2,1)}, u32[]{:S(2)}) copy-start(bf16[256,1792]{1,0:T(8,128)(2,1)} %param.21) | copy-start | bytes 2752516
  85.3 1.9 %collective-permute-start.27 = (bf16[128,1792]{1,0:T(8,128)(2,1)S(1)}, bf16[128,1792]{1,0:T(8,128)(2,1)S(1)}, u32[]{:S(2)}, u32[]{:S(2)}) collective-permute-start(bf16[128,1792]{1,0:T(8,128)(2,1)S(1)} %get-tuple-element.42), channel_id=1, source_target_pairs={{0,4},{4,0},{8,12},{12,8},{1,5},{5,1},{9,13},{13,9},{2,6},{6,2},{1... | collective-permute-start | bytes 1376264 | tf_op jit(solution)/shard_map/ppermute | solution.py:382
  85.5 2.4 %collective-permute-start.25 = (bf16[128,1792]{1,0:T(8,128)(2,1)S(1)}, bf16[128,1792]{1,0:T(8,128)(2,1)S(1)}, u32[]{:S(2)}, u32[]{:S(2)}) collective-permute-start(bf16[128,1792]{1,0:T(8,128)(2,1)S(1)} %get-tuple-element.39), channel_id=1, source_target_pairs={{0,4},{4,0},{8,12},{12,8},{1,5},{5,1},{9,13},{13,9},{2,6},{6,2},{1... | collective-permute-start | bytes 1376264 | tf_op jit(solution)/shard_map/ppermute | solution.py:382
  85.8 2.6 %collective-permute-start.30 = (bf16[128,1792]{1,0:T(8,128)(2,1)S(1)}, bf16[128,1792]{1,0:T(8,128)(2,1)S(1)}, u32[]{:S(2)}, u32[]{:S(2)}) collective-permute-start(bf16[128,1792]{1,0:T(8,128)(2,1)S(1)} %get-tuple-element.48), channel_id=1, source_target_pairs={{0,4},{4,0},{8,12},{12,8},{1,5},{5,1},{9,13},{13,9},{2,6},{6,2},{1... | collective-permute-start | bytes 1376264 | tf_op jit(solution)/shard_map/ppermute | solution.py:382
  86.0 10.1 %collective-permute-start.24 = (bf16[128,1792]{1,0:T(8,128)(2,1)S(1)}, bf16[128,1792]{1,0:T(8,128)(2,1)S(1)}, u32[]{:S(2)}, u32[]{:S(2)}) collective-permute-start(bf16[128,1792]{1,0:T(8,128)(2,1)S(1)} %get-tuple-element.37), channel_id=1, source_target_pairs={{0,4},{4,0},{8,12},{12,8},{1,5},{5,1},{9,13},{13,9},{2,6},{6,2},{1... | collective-permute-start | bytes 1376264 | tf_op jit(solution)/shard_map/ppermute | solution.py:382
  87.3 8.5 %collective-permute-start.28 = (bf16[64,1792]{1,0:T(8,128)(2,1)S(1)}, bf16[64,1792]{1,0:T(8,128)(2,1)S(1)}, u32[]{:S(2)}, u32[]{:S(2)}) collective-permute-start(bf16[64,1792]{1,0:T(8,128)(2,1)S(1)} %get-tuple-element.44), channel_id=1, source_target_pairs={{0,8},{4,12},{8,0},{12,4},{1,9},{5,13},{9,1},{13,5},{2,10},{6,14},... | collective-permute-start | bytes 688136 | tf_op jit(solution)/shard_map/ppermute | solution.py:386
  88.0 7.8 %collective-permute-start.26 = (bf16[64,1792]{1,0:T(8,128)(2,1)S(1)}, bf16[64,1792]{1,0:T(8,128)(2,1)S(1)}, u32[]{:S(2)}, u32[]{:S(2)}) collective-permute-start(bf16[64,1792]{1,0:T(8,128)(2,1)S(1)} %get-tuple-element.40), channel_id=1, source_target_pairs={{0,1},{1,0},{2,3},{3,2},{4,5},{5,4},{6,7},{7,6},{8,9},{9,8},{10,11... | collective-permute-start | bytes 688136 | tf_op jit(solution)/shard_map/ppermute | solution.py:389
  88.6 12.1 %collective-permute-start.31 = (bf16[64,1792]{1,0:T(8,128)(2,1)S(1)}, bf16[64,1792]{1,0:T(8,128)(2,1)S(1)}, u32[]{:S(2)}, u32[]{:S(2)}) collective-permute-start(bf16[64,1792]{1,0:T(8,128)(2,1)S(1)} %get-tuple-element.50), channel_id=1, source_target_pairs={{0,8},{4,12},{8,0},{12,4},{1,9},{5,13},{9,1},{13,5},{2,10},{6,14},... | collective-permute-start | bytes 688136 | tf_op jit(solution)/shard_map/ppermute | solution.py:386
  95.8 6.6 %collective-permute-start.32 = (bf16[64,1792]{1,0:T(8,128)(2,1)S(1)}, bf16[64,1792]{1,0:T(8,128)(2,1)S(1)}, u32[]{:S(2)}, u32[]{:S(2)}) collective-permute-start(bf16[64,1792]{1,0:T(8,128)(2,1)S(1)} %add.69.refs_5_), channel_id=1, source_target_pairs={{0,1},{1,0},{2,3},{3,2},{4,5},{5,4},{6,7},{7,6},{8,9},{9,8},{10,11... | collective-permute-start | bytes 688136 | tf_op jit(solution)/shard_map/ppermute | solution.py:389
  96.2 8.6 %collective-permute-start.29 = (bf16[64,1792]{1,0:T(8,128)(2,1)S(1)}, bf16[64,1792]{1,0:T(8,128)(2,1)S(1)}, u32[]{:S(2)}, u32[]{:S(2)}) collective-permute-start(bf16[64,1792]{1,0:T(8,128)(2,1)S(1)} %get-tuple-element.46), channel_id=1, source_target_pairs={{0,8},{4,12},{8,0},{12,4},{1,9},{5,13},{9,1},{13,5},{2,10},{6,14},... | collective-permute-start | bytes 688136 | tf_op jit(solution)/shard_map/ppermute | solution.py:386
  102.5 11.5 %collective-permute-start.33 = (bf16[64,1792]{1,0:T(8,128)(2,1)S(1)}, bf16[64,1792]{1,0:T(8,128)(2,1)S(1)}, u32[]{:S(2)}, u32[]{:S(2)}) collective-permute-start(bf16[64,1792]{1,0:T(8,128)(2,1)S(1)} %add.72), channel_id=1, source_target_pairs={{0,2},{1,3},{2,0},{3,1},{4,6},{5,7},{6,4},{7,5},{8,10},{9,11},{10,... | collective-permute-start | bytes 688136 | tf_op jit(solution)/shard_map/ppermute | solution.py:389
  103.1 11.1 %collective-permute-start.34 = (bf16[64,1792]{1,0:T(8,128)(2,1)S(1)}, bf16[64,1792]{1,0:T(8,128)(2,1)S(1)}, u32[]{:S(2)}, u32[]{:S(2)}) collective-permute-start(bf16[64,1792]{1,0:T(8,128)(2,1)S(1)} %get-tuple-element.51), channel_id=1, source_target_pairs={{0,1},{1,0},{2,3},{3,2},{4,5},{5,4},{6,7},{7,6},{8,9},{9,8},{10,11... | collective-permute-start | bytes 688136 | tf_op jit(solution)/shard_map/ppermute | solution.py:389

commit v14 on v13

--- a/solution.py
+++ b/solution.py
@@ -388,8 +388,10 @@
     def from_tp(value, bits):
         return lax.ppermute(value, "tp", [(i, i ^ bits) for i in range(tp_count)])
 
-    def gather_ep(value):
+    def gather_ep(value, after=()):
         same = [value] + [from_chip(value, b) for b in range(1, chips)]
+        if after:
+            same[1:] = [add([[(v, 0)]], v.shape[0], after)[0] for v in same[1:]]
         other = [from_core(v) for v in same]
         return [v for pair in zip(same, other) for v in pair]
 
@@ -409,7 +411,7 @@
 
     head_out = attend(query_latent, query_rope, cache_latent, cache_rope, cache_length, value_up, [places])
     output_weight = fetch(output_weight, [head_out, row_weight, own_residual, gain])
-    partial = project(places, gather_ep(head_out), output_weight, tp_count)
+    partial = project(places, gather_ep(head_out, [output_weight]), output_weight, tp_count)
 
     gate_weight = fetch(gate_weight, [partial[0]])
     terms = [[(value, 0)] for value in partial]
@@ -443,10 +445,11 @@
             if k == 0:
                 value = crossed[b - 1]
             elif k == 1:
-                value = from_tp(crossed[b - 1], 1)
+                (source,) = add([[(crossed[b - 1], 0)]], block_rows, [rows_of[tp_count - 1]])
+                value = from_tp(source, 1)
             else:
                 value = from_chip(rows_of[k], b)
-            (later,) = add([[(value, 0)]], block_rows, sums[-1:]) if k == 0 else (value,)
+            (later,) = add([[(value, 0)]], block_rows, sums[-1:]) if k == tp_count - 1 else (value,)
             far[k] += [value, from_core(later)]
     active = activate(places, [far[k] for k in slots], gains[cores:], gate_weight, up_weight, cores, cores, sums)
 

time: 115 us -> 113 us (0.983)
  waiting for transfers between devices: 50.8 us -> 46.7 us
  starting transfers between devices: 25.8 us -> 27.9 us
    ppermute x8, waiting for transfers between devices: 18.8 us -> 11.4 us  [from_chip(): lax.ppermute(value, 'ep', [(i, (i + step) % ep_count) for i in range(ep_c...]
    ppermute x11, waiting for transfers between devices: 29.4 us -> 31.6 us  [from_tp(): return lax.ppermute(value, 'tp', [(i, i ^ bits) for i in range(tp_count)])]
    ppermute x8, starting transfers between devices: 10.4 us -> 11.6 us  [from_chip(): lax.ppermute(value, 'ep', [(i, (i + step) % ep_count) for i in range(ep_c...]
    pallas_call x13 -> x15, Pallas kernels: 2.35 us -> 2.38 us  [add(): pl.pallas_call(functools.partial(add_kernel, [[first for _, first in grou...]
  transfers between devices with their start and end apart: 35 -> 35, of which waited for: 17 -> 18; matrix products, arithmetic and copies ran while one was open for 0% -> 0% of each run, Pallas kernels for 13% -> 13%
where the time goes in v14:
time: 113 us
  waiting for transfers between devices  46.7 us (41%)
  Pallas kernels  36.3 us (32%)
  starting transfers between devices  27.9 us (25%)
    ppermute x11, waiting for transfers between devices, from_tp(): return lax.ppermute(value, 'tp', [(i, i ^ bits) for i in range(tp_count)])  31.6 us
    ppermute x11, starting transfers between devices, from_tp(): return lax.ppermute(value, 'tp', [(i, i ^ bits) for i in range(tp_count)])  13.4 us
    pallas_call x1, Pallas kernels, attend(): pl.pallas_call(functools.partial(attention_kernel, step_rows, pieces, ahe...  12.3 us
    ppermute x8, starting transfers between devices, from_chip(): lax.ppermute(value, 'ep', [(i, (i + step) % ep_count) for i in range(ep_c...  11.6 us
    pallas_call x4, Pallas kernels, fetch(): pl.pallas_call(functools.partial(fetch_kernel, parts), out_shape=pltpu.VM...  11.6 us
    ppermute x8, waiting for transfers between devices, from_chip(): lax.ppermute(value, 'ep', [(i, (i + step) % ep_count) for i in range(ep_c...  11.4 us
    pallas_call x2, Pallas kernels, activate(): pl.pallas_call(functools.partial(gate_kernel, row_blocks, cores, first, c...  5.52 us
    ppermute x16, waiting for transfers between devices, from_core(): return lax.ppermute(value, 'ep', [(i, i ^ 1) for i in range(ep_count)])  3.81 us
  transfers between devices with their start and end apart: 35, of which 18 were waited for; matrix products, arithmetic and copies ran while one was open for 0% of the time, Pallas kernels for 13%

profile of v14, /device:TPU:0, one launch (start us, length us, event | category | flops | bytes accessed | tf_op | source)
XLA Modules:
  0.0 113.0 jit_solution(14369867483928810762)
XLA Ops:
  0.8 0.7 copy-done.2
  1.5 12.3 %attention.1.refs_1_.refs_0_ = bf16[64,1024]{1,0:T(8,128)(2,1)S(1)} custom-call(s32[64]{0:T(128)S(1)} %copy-done.2, bf16[64,8,512]{2,1,0:T(8,128)(2,1)} %q_ref.1, bf16[64,512]{1,0:T(8,128)(2,1)} %qr_ref.1, bf16[64,256,512]{2,1,0:T(8,128)(2,1)} %k_hbm.1, bf16[64,64,256]{2,1,0:T(8,128)(2,1)} %kr_hbm.1, bf16[8,512,128]{2,1,0:T(8,128)(2,1)} %up_hbm.1, ...), custom_call_target="tpu_custom_call" | custom-call | flops 4294967296 | bytes 16777216 | tf_op jit(solution)/shard_map/attention/pallas_call | solution.py:135
  13.9 0.5 collective-permute-start
  14.4 2.6 %collective-permute-start.1 = (bf16[64,1024]{1,0:T(8,128)(2,1)S(1)}, bf16[64,1024]{1,0:T(8,128)(2,1)S(1)}, u32[]{:S(2)}, u32[]{:S(2)}) collective-permute-start(bf16[64,1024]{1,0:T(8,128)(2,1)S(1)} %attention.1.refs_1_.refs_0_), channel_id=1, source_target_pairs={{0,8},{4,12},{8,0},{12,4},{1,9},{5,13},{9,1},{13,5},{2,10},{6,14},... | collective-permute-start | bytes 393224 | tf_op jit(solution)/shard_map/ppermute | solution.py:386
  17.2 2.0 %fetch.4.refs_1_.refs_4_ = bf16[1024,1792]{1,0:T(8,128)(2,1)S(1)} custom-call(bf16[1024,1792]{1,0:T(8,128)(2,1)} %refs_0_.4, bf16[64,1024]{1,0:T(8,128)(2,1)S(1)} %attention.1.refs_1_.refs_0_, f32[256,1]{1,0:T(8,128)S(1)} %copy.16.refs_2_.row_weight, bf16[64,1792]{1,0:T(8,128)(2,1)S(1)} %constant_dynamic-slice_fusion.refs_3_.refs_7_, ...), custom_call_target="tpu_custom_call" | custom-call | bytes 7340032 | tf_op jit(solution)/shard_map/fetch/pallas_call | solution.py:38
  19.2 1.8 %collective-permute-done.1.refs_0_ = bf16[64,1024]{1,0:T(8,128)(2,1)S(1)} collective-permute-done((bf16[64,1024]{1,0:T(8,128)(2,1)S(1)}, bf16[64,1024]{1,0:T(8,128)(2,1)S(1)}, u32[]{:S(2)}, u32[]{:S(2)}) %collective-permute-start.1) | collective-permute-done | bytes 131104 | tf_op jit(solution)/shard_map/ppermute | solution.py:386
  21.1 1.3 %collective-permute-done.2.refs_3_ = bf16[64,1024]{1,0:T(8,128)(2,1)S(1)} collective-permute-done((bf16[64,1024]{1,0:T(8,128)(2,1)S(1)}, bf16[64,1024]{1,0:T(8,128)(2,1)S(1)}, u32[]{:S(2)}, u32[]{:S(2)}) %collective-permute-start.2) | collective-permute-done | bytes 131104 | tf_op jit(solution)/shard_map/ppermute | solution.py:382
  22.5 1.8 %projection.1 = (bf16[64,1792]{1,0:T(8,128)(2,1)S(1)}, bf16[64,1792]{1,0:T(8,128)(2,1)S(1)}, bf16[64,1792]{1,0:T(8,128)(2,1)S(1)}, bf16[64,1792]{1,0:T(8,128)(2,1)S(1)}) custom-call(s32[8]{0:T(128)S(1)} %stack.35.refs_0_.places, bf16[64,1024]{1,0:T(8,128)(2,1)S(1)} %attention.1.refs_1_.refs_0_, bf16[64,1024]{1,0:T(8,128)(2,1)S(1)} %collective-permute-done.refs_1_, ...), custom_call_target="tpu_custom_call" | custom-call | flops 939524096 | bytes 4194304 | tf_op jit(solution)/shard_map/projection/pallas_call | solution.py:200
  24.2 1.9 %collective-permute-start.3 = (bf16[64,1792]{1,0:T(8,128)(2,1)S(1)}, bf16[64,1792]{1,0:T(8,128)(2,1)S(1)}, u32[]{:S(2)}, u32[]{:S(2)}) collective-permute-start(bf16[64,1792]{1,0:T(8,128)(2,1)S(1)} %get-tuple-element.29), channel_id=1, source_target_pairs={{0,1},{1,0},{2,3},{3,2},{4,5},{5,4},{6,7},{7,6},{8,9},{9,8},{10,11... | collective-permute-start | bytes 688136 | tf_op jit(solution)/shard_map/ppermute | solution.py:389
  26.1 3.2 %fetch.5.refs_1_.refs_12_.refs_10_ = bf16[1,7168,512]{2,1,0:T(8,128)(2,1)S(1)} custom-call(bf16[1,7168,512]{2,1,0:T(8,128)(2,1)} %refs_0_.5, bf16[64,1792]{1,0:T(8,128)(2,1)S(1)} %get-tuple-element.27.refs_1_.refs_0_.refs_4_), custom_call_target="tpu_custom_call" | custom-call | bytes 14680064 | tf_op jit(solution)/shard_map/fetch/pallas_call | solution.py:38
  29.6 2.6 %collective-permute-done.3.refs_1_ = bf16[64,1792]{1,0:T(8,128)(2,1)S(1)} collective-permute-done((bf16[64,1792]{1,0:T(8,128)(2,1)S(1)}, bf16[64,1792]{1,0:T(8,128)(2,1)S(1)}, u32[]{:S(2)}, u32[]{:S(2)}) %collective-permute-start.3) | collective-permute-done | bytes 229408 | tf_op jit(solution)/shard_map/ppermute | solution.py:389
  32.2 3.0 %collective-permute-start.4 = (bf16[64,1792]{1,0:T(8,128)(2,1)S(1)}, bf16[64,1792]{1,0:T(8,128)(2,1)S(1)}, u32[]{:S(2)}, u32[]{:S(2)}) collective-permute-start(bf16[64,1792]{1,0:T(8,128)(2,1)S(1)} %add.65), channel_id=1, source_target_pairs={{0,2},{1,3},{2,0},{3,1},{4,6},{5,7},{6,4},{7,5},{8,10},{9,11},{10,... | collective-permute-start | bytes 688136 | tf_op jit(solution)/shard_map/ppermute | solution.py:389
  35.2 1.5 %collective-permute-start.7 = (f32[1,1792]{1,0:T(1,128)S(1)}, f32[1,1792]{1,0:T(1,128)S(1)}, u32[]{:S(2)}, u32[]{:S(2)}) collective-permute-start(f32[1,1792]{1,0:T(1,128)S(1)} %reshape.7.refs_4_.refs_8_), channel_id=1, source_target_pairs={{0,8},{4,12},{8,0},{12,4},{1,9},{5,13},{9,1},{13,5},{2,10},{6,14},... | collective-permute-start | bytes 21512 | tf_op jit(solution)/shard_map/ppermute | solution.py:386
  36.7 2.2 %collective-permute-done.7.refs_10_.refs_8_ = f32[1,1792]{1,0:T(1,128)S(1)} collective-permute-done((f32[1,1792]{1,0:T(1,128)S(1)}, f32[1,1792]{1,0:T(1,128)S(1)}, u32[]{:S(2)}, u32[]{:S(2)}) %collective-permute-start.7) | collective-permute-done | bytes 7200 | tf_op jit(solution)/shard_map/ppermute | solution.py:386
  38.8 3.2 %fetch.6.refs_13_.refs_11_ = bf16[1,7168,512]{2,1,0:T(8,128)(2,1)S(1)} custom-call(bf16[1,7168,512]{2,1,0:T(8,128)(2,1)} %refs_0_.6, bf16[64,1792]{1,0:T(8,128)(2,1)S(1)} %add.66.refs_1_), custom_call_target="tpu_custom_call" | custom-call | bytes 14680064 | tf_op jit(solution)/shard_map/fetch/pallas_call | solution.py:38
  42.0 3.2 %fetch.7.refs_14_.down = bf16[1,512,7168]{2,1,0:T(8,128)(2,1)S(1)} custom-call(bf16[1,512,7168]{2,1,0:T(8,128)(2,1)} %refs_0_.7, bf16[64,1792]{1,0:T(8,128)(2,1)S(1)} %add.66.refs_1_), custom_call_target="tpu_custom_call" | custom-call | bytes 14680064 | tf_op jit(solution)/shard_map/fetch/pallas_call | solution.py:38
  45.3 0.8 add.67
  46.2 1.7 %collective-permute-start.10 = (bf16[64,1792]{1,0:T(8,128)(2,1)S(1)}, bf16[64,1792]{1,0:T(8,128)(2,1)S(1)}, u32[]{:S(2)}, u32[]{:S(2)}) collective-permute-start(bf16[64,1792]{1,0:T(8,128)(2,1)S(1)} %get-tuple-element.32.refs_6_), channel_id=1, source_target_pairs={{0,8},{4,12},{8,0},{12,4},{1,9},{5,13},{9,1},{13,5},{2,10},{6,14},... | collective-permute-start | bytes 688136 | tf_op jit(solution)/shard_map/ppermute | solution.py:386
  47.9 3.6 %collective-permute-start.15 = (bf16[64,1792]{1,0:T(8,128)(2,1)S(1)}, bf16[64,1792]{1,0:T(8,128)(2,1)S(1)}, u32[]{:S(2)}, u32[]{:S(2)}) collective-permute-start(bf16[64,1792]{1,0:T(8,128)(2,1)S(1)} %get-tuple-element.32.refs_6_), channel_id=1, source_target_pairs={{0,1},{1,0},{2,3},{3,2},{4,5},{5,4},{6,7},{7,6},{8,9},{9,8},{10,11... | collective-permute-start | bytes 688136 | tf_op jit(solution)/shard_map/ppermute | solution.py:389
  51.5 8.5 %collective-permute-done.9.refs_0_.refs_2_ = bf16[64,1792]{1,0:T(8,128)(2,1)S(1)} collective-permute-done((bf16[64,1792]{1,0:T(8,128)(2,1)S(1)}, bf16[64,1792]{1,0:T(8,128)(2,1)S(1)}, u32[]{:S(2)}, u32[]{:S(2)}) %collective-permute-start.9) | collective-permute-done | bytes 229408 | tf_op jit(solution)/shard_map/ppermute | solution.py:389
  60.1 0.5 collective-permute-start.14
  60.7 1.5 %collective-permute-start.19 = (bf16[64,1792]{1,0:T(8,128)(2,1)S(1)}, bf16[64,1792]{1,0:T(8,128)(2,1)S(1)}, u32[]{:S(2)}, u32[]{:S(2)}) collective-permute-start(bf16[64,1792]{1,0:T(8,128)(2,1)S(1)} %collective-permute-done.9.refs_0_.refs_2_), channel_id=1, source_target_pairs={{0,8},{4,12},{8,0},{12,4},{1,9},{5,13},{9,1},{13,5},{2,10},{6,14},... | collective-permute-start | bytes 688136 | tf_op jit(solution)/shard_map/ppermute | solution.py:386
  62.2 5.0 %collective-permute-done.11.refs_0_.refs_1_ = bf16[64,1792]{1,0:T(8,128)(2,1)S(1)} collective-permute-done((bf16[64,1792]{1,0:T(8,128)(2,1)S(1)}, bf16[64,1792]{1,0:T(8,128)(2,1)S(1)}, u32[]{:S(2)}, u32[]{:S(2)}) %collective-permute-start.11) | collective-permute-done | bytes 229408 | tf_op jit(solution)/shard_map/ppermute | solution.py:389
  67.3 1.5 %collective-permute-start.12 = (bf16[64,1792]{1,0:T(8,128)(2,1)S(1)}, bf16[64,1792]{1,0:T(8,128)(2,1)S(1)}, u32[]{:S(2)}, u32[]{:S(2)}) collective-permute-start(bf16[64,1792]{1,0:T(8,128)(2,1)S(1)} %collective-permute-done.11.refs_0_.refs_1_), channel_id=1, source_target_pairs={{0,8},{4,12},{8,0},{12,4},{1,9},{5,13},{9,1},{13,5},{2,10},{6,14},... | collective-permute-start | bytes 688136 | tf_op jit(solution)/shard_map/ppermute | solution.py:386
  69.2 0.5 collective-permute-start.20
  69.7 2.7 %activate.2 = (f32[256,512]{1,0:T(8,128)S(1)}, f32[256,512]{1,0:T(8,128)S(1)}, f32[256,1]{1,0:T(8,128)S(1)}) custom-call(s32[8]{0:T(128)S(1)} %stack.35.refs_0_.places, bf16[64,1792]{1,0:T(8,128)(2,1)S(1)} %collective-permute-done.11.refs_0_.refs_1_, bf16[64,1792]{1,0:T(8,128)(2,1)S(1)} %collective-permute-done.13.refs_1_, ...), custom_call_target="tpu_custom_call" | custom-call | flops 1879048192 | bytes 7340032 | tf_op jit(solution)/shard_map/activate/pallas_call | solution.py:268
  72.4 2.9 %collective-permute-done.12.refs_0_ = bf16[64,1792]{1,0:T(8,128)(2,1)S(1)} collective-permute-done((bf16[64,1792]{1,0:T(8,128)(2,1)S(1)}, bf16[64,1792]{1,0:T(8,128)(2,1)S(1)}, u32[]{:S(2)}, u32[]{:S(2)}) %collective-permute-start.12) | collective-permute-done | bytes 229408 | tf_op jit(solution)/shard_map/ppermute | solution.py:386
  75.4 1.2 %collective-permute-done.21.refs_4_ = bf16[64,1792]{1,0:T(8,128)(2,1)S(1)} collective-permute-done((bf16[64,1792]{1,0:T(8,128)(2,1)S(1)}, bf16[64,1792]{1,0:T(8,128)(2,1)S(1)}, u32[]{:S(2)}, u32[]{:S(2)}) %collective-permute-start.21) | collective-permute-done | bytes 229408 | tf_op jit(solution)/shard_map/ppermute | solution.py:389
  76.9 1.3 %collective-permute-done.22.refs_5_ = bf16[64,1792]{1,0:T(8,128)(2,1)S(1)} collective-permute-done((bf16[64,1792]{1,0:T(8,128)(2,1)S(1)}, bf16[64,1792]{1,0:T(8,128)(2,1)S(1)}, u32[]{:S(2)}, u32[]{:S(2)}) %collective-permute-start.22) | collective-permute-done | bytes 229408 | tf_op jit(solution)/shard_map/ppermute | solution.py:382
  78.1 2.8 %activate.3.active = bf16[256,512]{1,0:T(8,128)(2,1)S(1)} custom-call(s32[8]{0:T(128)S(1)} %stack.35.refs_0_.places, bf16[64,1792]{1,0:T(8,128)(2,1)S(1)} %collective-permute-done.12.refs_0_, bf16[64,1792]{1,0:T(8,128)(2,1)S(1)} %collective-permute-done.18.refs_1_, bf16[64,1792]{1,0:T(8,128)(2,1)S(1)} %collective-permute-done.19.refs_2_, ...), custom_call_target="tpu_custom_call" | custom-call | flops 1879048192 | bytes 7340032 | tf_op jit(solution)/shard_map/activate/pallas_call | solution.py:268
  81.0 2.7 %down.1 = (bf16[128,1792]{1,0:T(8,128)(2,1)S(1)}, bf16[128,1792]{1,0:T(8,128)(2,1)S(1)}, bf16[128,1792]{1,0:T(8,128)(2,1)S(1)}, bf16[128,1792]{1,0:T(8,128)(2,1)...) custom-call(s32[8]{0:T(128)S(1)} %stack.35.refs_0_.places, ...), custom_call_target="tpu_custom_call" | custom-call | flops 1879048192 | bytes 7340032 | tf_op jit(solution)/shard_map/down/pallas_call | solution.py:313
  83.9 0.4 collective-permute-start.27
  84.4 0.4 collective-permute-start.24
  84.8 0.8 collective-permute-done.25.refs_1_.refs_3_
  85.7 0.4 collective-permute-start.26
  86.4 0.7 collective-permute-start.28
  87.1 1.5 %collective-permute-start.31 = (bf16[64,1792]{1,0:T(8,128)(2,1)S(1)}, bf16[64,1792]{1,0:T(8,128)(2,1)S(1)}, u32[]{:S(2)}, u32[]{:S(2)}) collective-permute-start(bf16[64,1792]{1,0:T(8,128)(2,1)S(1)} %get-tuple-element.50), channel_id=1, source_target_pairs={{0,8},{4,12},{8,0},{12,4},{1,9},{5,13},{9,1},{13,5},{2,10},{6,14},... | collective-permute-start | bytes 688136 | tf_op jit(solution)/shard_map/ppermute | solution.py:386
  88.6 4.8 %collective-permute-done.26.refs_2_.refs_4_ = bf16[64,1792]{1,0:T(8,128)(2,1)S(1)} collective-permute-done((bf16[64,1792]{1,0:T(8,128)(2,1)S(1)}, bf16[64,1792]{1,0:T(8,128)(2,1)S(1)}, u32[]{:S(2)}, u32[]{:S(2)}) %collective-permute-start.26) | collective-permute-done | bytes 229408 | tf_op jit(solution)/shard_map/ppermute | solution.py:389
  93.4 1.5 %collective-permute-done.28.refs_1_ = bf16[64,1792]{1,0:T(8,128)(2,1)S(1)} collective-permute-done((bf16[64,1792]{1,0:T(8,128)(2,1)S(1)}, bf16[64,1792]{1,0:T(8,128)(2,1)S(1)}, u32[]{:S(2)}, u32[]{:S(2)}) %collective-permute-start.28) | collective-permute-done | bytes 229408 | tf_op jit(solution)/shard_map/ppermute | solution.py:386
  94.9 1.7 %collective-permute-start.32 = (bf16[64,1792]{1,0:T(8,128)(2,1)S(1)}, bf16[64,1792]{1,0:T(8,128)(2,1)S(1)}, u32[]{:S(2)}, u32[]{:S(2)}) collective-permute-start(bf16[64,1792]{1,0:T(8,128)(2,1)S(1)} %add.73.refs_5_), channel_id=1, source_target_pairs={{0,1},{1,0},{2,3},{3,2},{4,5},{5,4},{6,7},{7,6},{8,9},{9,8},{10,11... | collective-permute-start | bytes 688136 | tf_op jit(solution)/shard_map/ppermute | solution.py:389
  96.7 0.7 collective-permute-start.29
  97.4 2.4 %collective-permute-done.31.refs_1_ = bf16[64,1792]{1,0:T(8,128)(2,1)S(1)} collective-permute-done((bf16[64,1792]{1,0:T(8,128)(2,1)S(1)}, bf16[64,1792]{1,0:T(8,128)(2,1)S(1)}, u32[]{:S(2)}, u32[]{:S(2)}) %collective-permute-start.31) | collective-permute-done | bytes 229408 | tf_op jit(solution)/shard_map/ppermute | solution.py:386
  99.8 1.2 %collective-permute-done.32.refs_2_ = bf16[64,1792]{1,0:T(8,128)(2,1)S(1)} collective-permute-done((bf16[64,1792]{1,0:T(8,128)(2,1)S(1)}, bf16[64,1792]{1,0:T(8,128)(2,1)S(1)}, u32[]{:S(2)}, u32[]{:S(2)}) %collective-permute-start.32) | collective-permute-done | bytes 229408 | tf_op jit(solution)/shard_map/ppermute | solution.py:389
  101.1 1.7 %collective-permute-start.33 = (bf16[64,1792]{1,0:T(8,128)(2,1)S(1)}, bf16[64,1792]{1,0:T(8,128)(2,1)S(1)}, u32[]{:S(2)}, u32[]{:S(2)}) collective-permute-start(bf16[64,1792]{1,0:T(8,128)(2,1)S(1)} %add.76), channel_id=1, source_target_pairs={{0,2},{1,3},{2,0},{3,1},{4,6},{5,7},{6,4},{7,5},{8,10},{9,11},{10,... | collective-permute-start | bytes 688136 | tf_op jit(solution)/shard_map/ppermute | solution.py:389
  102.8 0.4 collective-permute-start.34
  103.3 0.6 collective-permute-done.29.refs_1_
  103.9 8.2 %collective-permute-done.33.refs_2_ = bf16[64,1792]{1,0:T(8,128)(2,1)S(1)} collective-permute-done((bf16[64,1792]{1,0:T(8,128)(2,1)S(1)}, bf16[64,1792]{1,0:T(8,128)(2,1)S(1)}, u32[]{:S(2)}, u32[]{:S(2)}) %collective-permute-start.33) | collective-permute-done | bytes 229408 | tf_op jit(solution)/shard_map/ppermute | solution.py:389
  112.2 0.7 add.78
  (63 shorter events, 3.0 us)
Async XLA Ops:
  0.6 16.5 %copy-start = (bf16[256,1792]{1,0:T(8,128)(2,1)S(1)}, bf16[256,1792]{1,0:T(8,128)(2,1)}, u32[]{:S(2)}) copy-start(bf16[256,1792]{1,0:T(8,128)(2,1)} %param.21) | copy-start | bytes 2752516
  0.8 0.7 copy-start.2
  1.5 15.4 %copy-start.4 = (f32[256,2]{0,1:T(2,128)S(1)}, f32[256,2]{0,1:T(2,128)}, u32[]{:S(2)}) copy-start(f32[256,2]{0,1:T(2,128)} %param.24) | copy-start | bytes 6148
  1.5 15.4 %copy-start.5 = (s32[256,2]{0,1:T(2,128)S(1)}, s32[256,2]{0,1:T(2,128)}, u32[]{:S(2)}) copy-start(s32[256,2]{0,1:T(2,128)} %param.23) | copy-start | bytes 6148
  1.5 15.6 %copy-start.3 = (f32[1792]{0:T(1024)S(1)}, f32[1792]{0:T(1024)}, u32[]{:S(2)}) copy-start(f32[1792]{0:T(1024)} %param.22) | copy-start | bytes 21508
  13.9 7.3 %collective-permute-start = (bf16[64,1024]{1,0:T(8,128)(2,1)S(1)}, bf16[64,1024]{1,0:T(8,128)(2,1)S(1)}, u32[]{:S(2)}, u32[]{:S(2)}) collective-permute-start(bf16[64,1024]{1,0:T(8,128)(2,1)S(1)} %attention.1.refs_1_.refs_0_), channel_id=1, source_target_pairs={{0,4},{4,0},{8,12},{12,8},{1,5},{5,1},{9,13},{13,9},{2,6},{6,2},{1... | collective-permute-start | bytes 393224 | tf_op jit(solution)/shard_map/ppermute | solution.py:382
  14.4 6.7 %collective-permute-start.1 = (bf16[64,1024]{1,0:T(8,128)(2,1)S(1)}, bf16[64,1024]{1,0:T(8,128)(2,1)S(1)}, u32[]{:S(2)}, u32[]{:S(2)}) collective-permute-start(bf16[64,1024]{1,0:T(8,128)(2,1)S(1)} %attention.1.refs_1_.refs_0_), channel_id=1, source_target_pairs={{0,8},{4,12},{8,0},{12,4},{1,9},{5,13},{9,1},{13,5},{2,10},{6,14},... | collective-permute-start | bytes 393224 | tf_op jit(solution)/shard_map/ppermute | solution.py:386
  21.0 1.4 %collective-permute-start.2 = (bf16[64,1024]{1,0:T(8,128)(2,1)S(1)}, bf16[64,1024]{1,0:T(8,128)(2,1)S(1)}, u32[]{:S(2)}, u32[]{:S(2)}) collective-permute-start(bf16[64,1024]{1,0:T(8,128)(2,1)S(1)} %add.64.refs_2_), channel_id=1, source_target_pairs={{0,4},{4,0},{8,12},{12,8},{1,5},{5,1},{9,13},{13,9},{2,6},{6,2},{1... | collective-permute-start | bytes 393224 | tf_op jit(solution)/shard_map/ppermute | solution.py:382
  24.2 7.9 %collective-permute-start.3 = (bf16[64,1792]{1,0:T(8,128)(2,1)S(1)}, bf16[64,1792]{1,0:T(8,128)(2,1)S(1)}, u32[]{:S(2)}, u32[]{:S(2)}) collective-permute-start(bf16[64,1792]{1,0:T(8,128)(2,1)S(1)} %get-tuple-element.29), channel_id=1, source_target_pairs={{0,1},{1,0},{2,3},{3,2},{4,5},{5,4},{6,7},{7,6},{8,9},{9,8},{10,11... | collective-permute-start | bytes 688136 | tf_op jit(solution)/shard_map/ppermute | solution.py:389
  29.4 15.9 %collective-permute-start.5 = (bf16[64,1792]{1,0:T(8,128)(2,1)S(1)}, bf16[64,1792]{1,0:T(8,128)(2,1)S(1)}, u32[]{:S(2)}, u32[]{:S(2)}) collective-permute-start(bf16[64,1792]{1,0:T(8,128)(2,1)S(1)} %add.66.refs_1_), channel_id=1, source_target_pairs={{0,1},{1,0},{2,3},{3,2},{4,5},{5,4},{6,7},{7,6},{8,9},{9,8},{10,11... | collective-permute-start | bytes 688136 | tf_op jit(solution)/shard_map/ppermute | solution.py:389
  32.2 13.1 %collective-permute-start.4 = (bf16[64,1792]{1,0:T(8,128)(2,1)S(1)}, bf16[64,1792]{1,0:T(8,128)(2,1)S(1)}, u32[]{:S(2)}, u32[]{:S(2)}) collective-permute-start(bf16[64,1792]{1,0:T(8,128)(2,1)S(1)} %add.65), channel_id=1, source_target_pairs={{0,2},{1,3},{2,0},{3,1},{4,6},{5,7},{6,4},{7,5},{8,10},{9,11},{10,... | collective-permute-start | bytes 688136 | tf_op jit(solution)/shard_map/ppermute | solution.py:389
  35.2 3.6 %collective-permute-start.7 = (f32[1,1792]{1,0:T(1,128)S(1)}, f32[1,1792]{1,0:T(1,128)S(1)}, u32[]{:S(2)}, u32[]{:S(2)}) collective-permute-start(f32[1,1792]{1,0:T(1,128)S(1)} %reshape.7.refs_4_.refs_8_), channel_id=1, source_target_pairs={{0,8},{4,12},{8,0},{12,4},{1,9},{5,13},{9,1},{13,5},{2,10},{6,14},... | collective-permute-start | bytes 21512 | tf_op jit(solution)/shard_map/ppermute | solution.py:386
  36.7 8.6 %collective-permute-start.6 = (f32[1,1792]{1,0:T(1,128)S(1)}, f32[1,1792]{1,0:T(1,128)S(1)}, u32[]{:S(2)}, u32[]{:S(2)}) collective-permute-start(f32[1,1792]{1,0:T(1,128)S(1)} %reshape.7.refs_4_.refs_8_), channel_id=1, source_target_pairs={{0,4},{4,0},{8,12},{12,8},{1,5},{5,1},{9,13},{13,9},{2,6},{6,2},{1... | collective-permute-start | bytes 21512 | tf_op jit(solution)/shard_map/ppermute | solution.py:382
  38.8 6.4 %collective-permute-start.8 = (f32[1,1792]{1,0:T(1,128)S(1)}, f32[1,1792]{1,0:T(1,128)S(1)}, u32[]{:S(2)}, u32[]{:S(2)}) collective-permute-start(f32[1,1792]{1,0:T(1,128)S(1)} %collective-permute-done.7.refs_10_.refs_8_), channel_id=1, source_target_pairs={{0,4},{4,0},{8,12},{12,8},{1,5},{5,1},{9,13},{13,9},{2,6},{6,2},{1... | collective-permute-start | bytes 21512 | tf_op jit(solution)/shard_map/ppermute | solution.py:382
  46.1 13.8 %collective-permute-start.9 = (bf16[64,1792]{1,0:T(8,128)(2,1)S(1)}, bf16[64,1792]{1,0:T(8,128)(2,1)S(1)}, u32[]{:S(2)}, u32[]{:S(2)}) collective-permute-start(bf16[64,1792]{1,0:T(8,128)(2,1)S(1)} %get-tuple-element.32.refs_6_), channel_id=1, source_target_pairs={{0,2},{1,3},{2,0},{3,1},{4,6},{5,7},{6,4},{7,5},{8,10},{9,11},{10,... | collective-permute-start | bytes 688136 | tf_op jit(solution)/shard_map/ppermute | solution.py:389
  46.2 13.8 %collective-permute-start.10 = (bf16[64,1792]{1,0:T(8,128)(2,1)S(1)}, bf16[64,1792]{1,0:T(8,128)(2,1)S(1)}, u32[]{:S(2)}, u32[]{:S(2)}) collective-permute-start(bf16[64,1792]{1,0:T(8,128)(2,1)S(1)} %get-tuple-element.32.refs_6_), channel_id=1, source_target_pairs={{0,8},{4,12},{8,0},{12,4},{1,9},{5,13},{9,1},{13,5},{2,10},{6,14},... | collective-permute-start | bytes 688136 | tf_op jit(solution)/shard_map/ppermute | solution.py:386
  47.9 12.7 %collective-permute-start.15 = (bf16[64,1792]{1,0:T(8,128)(2,1)S(1)}, bf16[64,1792]{1,0:T(8,128)(2,1)S(1)}, u32[]{:S(2)}, u32[]{:S(2)}) collective-permute-start(bf16[64,1792]{1,0:T(8,128)(2,1)S(1)} %get-tuple-element.32.refs_6_), channel_id=1, source_target_pairs={{0,1},{1,0},{2,3},{3,2},{4,5},{5,4},{6,7},{7,6},{8,9},{9,8},{10,11... | collective-permute-start | bytes 688136 | tf_op jit(solution)/shard_map/ppermute | solution.py:389
  60.0 7.3 %collective-permute-start.11 = (bf16[64,1792]{1,0:T(8,128)(2,1)S(1)}, bf16[64,1792]{1,0:T(8,128)(2,1)S(1)}, u32[]{:S(2)}, u32[]{:S(2)}) collective-permute-start(bf16[64,1792]{1,0:T(8,128)(2,1)S(1)} %add.68), channel_id=1, source_target_pairs={{0,1},{1,0},{2,3},{3,2},{4,5},{5,4},{6,7},{7,6},{8,9},{9,8},{10,11... | collective-permute-start | bytes 688136 | tf_op jit(solution)/shard_map/ppermute | solution.py:389
  60.1 7.2 %collective-permute-start.17 = (bf16[64,1792]{1,0:T(8,128)(2,1)S(1)}, bf16[64,1792]{1,0:T(8,128)(2,1)S(1)}, u32[]{:S(2)}, u32[]{:S(2)}) collective-permute-start(bf16[64,1792]{1,0:T(8,128)(2,1)S(1)} %get-tuple-element.32.refs_6_), channel_id=1, source_target_pairs={{0,4},{4,0},{8,12},{12,8},{1,5},{5,1},{9,13},{13,9},{2,6},{6,2},{1... | collective-permute-start | bytes 688136 | tf_op jit(solution)/shard_map/ppermute | solution.py:382
  60.1 8.7 %collective-permute-start.14 = (bf16[64,1792]{1,0:T(8,128)(2,1)S(1)}, bf16[64,1792]{1,0:T(8,128)(2,1)S(1)}, u32[]{:S(2)}, u32[]{:S(2)}) collective-permute-start(bf16[64,1792]{1,0:T(8,128)(2,1)S(1)} %collective-permute-done.9.refs_0_.refs_2_), channel_id=1, source_target_pairs={{0,4},{4,0},{8,12},{12,8},{1,5},{5,1},{9,13},{13,9},{2,6},{6,2},{1... | collective-permute-start | bytes 688136 | tf_op jit(solution)/shard_map/ppermute | solution.py:382
  60.6 8.6 %collective-permute-start.16 = (bf16[64,1792]{1,0:T(8,128)(2,1)S(1)}, bf16[64,1792]{1,0:T(8,128)(2,1)S(1)}, u32[]{:S(2)}, u32[]{:S(2)}) collective-permute-start(bf16[64,1792]{1,0:T(8,128)(2,1)S(1)} %collective-permute-done.15.refs_4_), channel_id=1, source_target_pairs={{0,4},{4,0},{8,12},{12,8},{1,5},{5,1},{9,13},{13,9},{2,6},{6,2},{1... | collective-permute-start | bytes 688136 | tf_op jit(solution)/shard_map/ppermute | solution.py:382
  60.7 8.5 %collective-permute-start.19 = (bf16[64,1792]{1,0:T(8,128)(2,1)S(1)}, bf16[64,1792]{1,0:T(8,128)(2,1)S(1)}, u32[]{:S(2)}, u32[]{:S(2)}) collective-permute-start(bf16[64,1792]{1,0:T(8,128)(2,1)S(1)} %collective-permute-done.9.refs_0_.refs_2_), channel_id=1, source_target_pairs={{0,8},{4,12},{8,0},{12,4},{1,9},{5,13},{9,1},{13,5},{2,10},{6,14},... | collective-permute-start | bytes 688136 | tf_op jit(solution)/shard_map/ppermute | solution.py:386
  67.3 2.4 %collective-permute-start.13 = (bf16[64,1792]{1,0:T(8,128)(2,1)S(1)}, bf16[64,1792]{1,0:T(8,128)(2,1)S(1)}, u32[]{:S(2)}, u32[]{:S(2)}) collective-permute-start(bf16[64,1792]{1,0:T(8,128)(2,1)S(1)} %collective-permute-done.11.refs_0_.refs_1_), channel_id=1, source_target_pairs={{0,4},{4,0},{8,12},{12,8},{1,5},{5,1},{9,13},{13,9},{2,6},{6,2},{1... | collective-permute-start | bytes 688136 | tf_op jit(solution)/shard_map/ppermute | solution.py:382
  67.3 8.0 %collective-permute-start.12 = (bf16[64,1792]{1,0:T(8,128)(2,1)S(1)}, bf16[64,1792]{1,0:T(8,128)(2,1)S(1)}, u32[]{:S(2)}, u32[]{:S(2)}) collective-permute-start(bf16[64,1792]{1,0:T(8,128)(2,1)S(1)} %collective-permute-done.11.refs_0_.refs_1_), channel_id=1, source_target_pairs={{0,8},{4,12},{8,0},{12,4},{1,9},{5,13},{9,1},{13,5},{2,10},{6,14},... | collective-permute-start | bytes 688136 | tf_op jit(solution)/shard_map/ppermute | solution.py:386
  68.8 7.8 %collective-permute-start.21 = (bf16[64,1792]{1,0:T(8,128)(2,1)S(1)}, bf16[64,1792]{1,0:T(8,128)(2,1)S(1)}, u32[]{:S(2)}, u32[]{:S(2)}) collective-permute-start(bf16[64,1792]{1,0:T(8,128)(2,1)S(1)} %add.70), channel_id=1, source_target_pairs={{0,1},{1,0},{2,3},{3,2},{4,5},{5,4},{6,7},{7,6},{8,9},{9,8},{10,11... | collective-permute-start | bytes 688136 | tf_op jit(solution)/shard_map/ppermute | solution.py:389
  69.2 7.5 %collective-permute-start.23 = (bf16[64,1792]{1,0:T(8,128)(2,1)S(1)}, bf16[64,1792]{1,0:T(8,128)(2,1)S(1)}, u32[]{:S(2)}, u32[]{:S(2)}) collective-permute-start(bf16[64,1792]{1,0:T(8,128)(2,1)S(1)} %collective-permute-done.10.refs_1_.refs_0_.refs_6_), channel_id=1, source_target_pairs={{0,4},{4,0},{8,12},{12,8},{1,5},{5,1},{9,13},{13,9},{2,6},{6,2},{1... | collective-permute-start | bytes 688136 | tf_op jit(solution)/shard_map/ppermute | solution.py:382
  69.2 7.4 %collective-permute-start.20 = (bf16[64,1792]{1,0:T(8,128)(2,1)S(1)}, bf16[64,1792]{1,0:T(8,128)(2,1)S(1)}, u32[]{:S(2)}, u32[]{:S(2)}) collective-permute-start(bf16[64,1792]{1,0:T(8,128)(2,1)S(1)} %collective-permute-done.19.refs_2_), channel_id=1, source_target_pairs={{0,4},{4,0},{8,12},{12,8},{1,5},{5,1},{9,13},{13,9},{2,6},{6,2},{1... | collective-permute-start | bytes 688136 | tf_op jit(solution)/shard_map/ppermute | solution.py:382
  75.3 1.6 %collective-permute-start.18 = (bf16[64,1792]{1,0:T(8,128)(2,1)S(1)}, bf16[64,1792]{1,0:T(8,128)(2,1)S(1)}, u32[]{:S(2)}, u32[]{:S(2)}) collective-permute-start(bf16[64,1792]{1,0:T(8,128)(2,1)S(1)} %add.69), channel_id=1, source_target_pairs={{0,4},{4,0},{8,12},{12,8},{1,5},{5,1},{9,13},{13,9},{2,6},{6,2},{1... | collective-permute-start | bytes 688136 | tf_op jit(solution)/shard_map/ppermute | solution.py:382
  76.6 1.5 %collective-permute-start.22 = (bf16[64,1792]{1,0:T(8,128)(2,1)S(1)}, bf16[64,1792]{1,0:T(8,128)(2,1)S(1)}, u32[]{:S(2)}, u32[]{:S(2)}) collective-permute-start(bf16[64,1792]{1,0:T(8,128)(2,1)S(1)} %collective-permute-done.21.refs_4_), channel_id=1, source_target_pairs={{0,4},{4,0},{8,12},{12,8},{1,5},{5,1},{9,13},{13,9},{2,6},{6,2},{1... | collective-permute-start | bytes 688136 | tf_op jit(solution)/shard_map/ppermute | solution.py:382
  81.0 32.0 %copy-start.1 = (bf16[256,1792]{1,0:T(8,128)(2,1)S(1)}, bf16[256,1792]{1,0:T(8,128)(2,1)}, u32[]{:S(2)}) copy-start(bf16[256,1792]{1,0:T(8,128)(2,1)} %param.21) | copy-start | bytes 2752516
  83.7 1.9 %collective-permute-start.25 = (bf16[128,1792]{1,0:T(8,128)(2,1)S(1)}, bf16[128,1792]{1,0:T(8,128)(2,1)S(1)}, u32[]{:S(2)}, u32[]{:S(2)}) collective-permute-start(bf16[128,1792]{1,0:T(8,128)(2,1)S(1)} %get-tuple-element.39), channel_id=1, source_target_pairs={{0,4},{4,0},{8,12},{12,8},{1,5},{5,1},{9,13},{13,9},{2,6},{6,2},{1... | collective-permute-start | bytes 1376264 | tf_op jit(solution)/shard_map/ppermute | solution.py:382
  83.9 2.3 %collective-permute-start.27 = (bf16[128,1792]{1,0:T(8,128)(2,1)S(1)}, bf16[128,1792]{1,0:T(8,128)(2,1)S(1)}, u32[]{:S(2)}, u32[]{:S(2)}) collective-permute-start(bf16[128,1792]{1,0:T(8,128)(2,1)S(1)} %get-tuple-element.42), channel_id=1, source_target_pairs={{0,4},{4,0},{8,12},{12,8},{1,5},{5,1},{9,13},{13,9},{2,6},{6,2},{1... | collective-permute-start | bytes 1376264 | tf_op jit(solution)/shard_map/ppermute | solution.py:382
  84.3 2.7 %collective-permute-start.30 = (bf16[128,1792]{1,0:T(8,128)(2,1)S(1)}, bf16[128,1792]{1,0:T(8,128)(2,1)S(1)}, u32[]{:S(2)}, u32[]{:S(2)}) collective-permute-start(bf16[128,1792]{1,0:T(8,128)(2,1)S(1)} %get-tuple-element.48), channel_id=1, source_target_pairs={{0,4},{4,0},{8,12},{12,8},{1,5},{5,1},{9,13},{13,9},{2,6},{6,2},{1... | collective-permute-start | bytes 1376264 | tf_op jit(solution)/shard_map/ppermute | solution.py:382
  84.4 12.2 %collective-permute-start.24 = (bf16[128,1792]{1,0:T(8,128)(2,1)S(1)}, bf16[128,1792]{1,0:T(8,128)(2,1)S(1)}, u32[]{:S(2)}, u32[]{:S(2)}) collective-permute-start(bf16[128,1792]{1,0:T(8,128)(2,1)S(1)} %get-tuple-element.37), channel_id=1, source_target_pairs={{0,4},{4,0},{8,12},{12,8},{1,5},{5,1},{9,13},{13,9},{2,6},{6,2},{1... | collective-permute-start | bytes 1376264 | tf_op jit(solution)/shard_map/ppermute | solution.py:382
  85.7 7.7 %collective-permute-start.26 = (bf16[64,1792]{1,0:T(8,128)(2,1)S(1)}, bf16[64,1792]{1,0:T(8,128)(2,1)S(1)}, u32[]{:S(2)}, u32[]{:S(2)}) collective-permute-start(bf16[64,1792]{1,0:T(8,128)(2,1)S(1)} %get-tuple-element.40), channel_id=1, source_target_pairs={{0,1},{1,0},{2,3},{3,2},{4,5},{5,4},{6,7},{7,6},{8,9},{9,8},{10,11... | collective-permute-start | bytes 688136 | tf_op jit(solution)/shard_map/ppermute | solution.py:389
  86.4 8.5 %collective-permute-start.28 = (bf16[64,1792]{1,0:T(8,128)(2,1)S(1)}, bf16[64,1792]{1,0:T(8,128)(2,1)S(1)}, u32[]{:S(2)}, u32[]{:S(2)}) collective-permute-start(bf16[64,1792]{1,0:T(8,128)(2,1)S(1)} %get-tuple-element.44), channel_id=1, source_target_pairs={{0,8},{4,12},{8,0},{12,4},{1,9},{5,13},{9,1},{13,5},{2,10},{6,14},... | collective-permute-start | bytes 688136 | tf_op jit(solution)/shard_map/ppermute | solution.py:386
  87.1 12.6 %collective-permute-start.31 = (bf16[64,1792]{1,0:T(8,128)(2,1)S(1)}, bf16[64,1792]{1,0:T(8,128)(2,1)S(1)}, u32[]{:S(2)}, u32[]{:S(2)}) collective-permute-start(bf16[64,1792]{1,0:T(8,128)(2,1)S(1)} %get-tuple-element.50), channel_id=1, source_target_pairs={{0,8},{4,12},{8,0},{12,4},{1,9},{5,13},{9,1},{13,5},{2,10},{6,14},... | collective-permute-start | bytes 688136 | tf_op jit(solution)/shard_map/ppermute | solution.py:386
  94.9 6.1 %collective-permute-start.32 = (bf16[64,1792]{1,0:T(8,128)(2,1)S(1)}, bf16[64,1792]{1,0:T(8,128)(2,1)S(1)}, u32[]{:S(2)}, u32[]{:S(2)}) collective-permute-start(bf16[64,1792]{1,0:T(8,128)(2,1)S(1)} %add.73.refs_5_), channel_id=1, source_target_pairs={{0,1},{1,0},{2,3},{3,2},{4,5},{5,4},{6,7},{7,6},{8,9},{9,8},{10,11... | collective-permute-start | bytes 688136 | tf_op jit(solution)/shard_map/ppermute | solution.py:389
  96.7 7.2 %collective-permute-start.29 = (bf16[64,1792]{1,0:T(8,128)(2,1)S(1)}, bf16[64,1792]{1,0:T(8,128)(2,1)S(1)}, u32[]{:S(2)}, u32[]{:S(2)}) collective-permute-start(bf16[64,1792]{1,0:T(8,128)(2,1)S(1)} %get-tuple-element.46), channel_id=1, source_target_pairs={{0,8},{4,12},{8,0},{12,4},{1,9},{5,13},{9,1},{13,5},{2,10},{6,14},... | collective-permute-start | bytes 688136 | tf_op jit(solution)/shard_map/ppermute | solution.py:386
  101.1 11.0 %collective-permute-start.33 = (bf16[64,1792]{1,0:T(8,128)(2,1)S(1)}, bf16[64,1792]{1,0:T(8,128)(2,1)S(1)}, u32[]{:S(2)}, u32[]{:S(2)}) collective-permute-start(bf16[64,1792]{1,0:T(8,128)(2,1)S(1)} %add.76), channel_id=1, source_target_pairs={{0,2},{1,3},{2,0},{3,1},{4,6},{5,7},{6,4},{7,5},{8,10},{9,11},{10,... | collective-permute-start | bytes 688136 | tf_op jit(solution)/shard_map/ppermute | solution.py:389
  102.8 9.4 %collective-permute-start.34 = (bf16[64,1792]{1,0:T(8,128)(2,1)S(1)}, bf16[64,1792]{1,0:T(8,128)(2,1)S(1)}, u32[]{:S(2)}, u32[]{:S(2)}) collective-permute-start(bf16[64,1792]{1,0:T(8,128)(2,1)S(1)} %get-tuple-element.51), channel_id=1, source_target_pairs={{0,1},{1,0},{2,3},{3,2},{4,5},{5,4},{6,7},{7,6},{8,9},{9,8},{10,11... | collective-permute-start | bytes 688136 | tf_op jit(solution)/shard_map/ppermute | solution.py:389

commit v15 on v14

--- a/solution.py
+++ b/solution.py
@@ -212,7 +212,7 @@
     )(places, *blocks, in_vmem(weight))
 
 
-def gate_kernel(row_blocks, cores, first, count, model_width, places, *refs):
+def gate_kernel(row_blocks, first, count, offset, model_width, places, *refs):
     blocks, gains = refs[: row_blocks * count], refs[row_blocks * count : (row_blocks + 1) * count]
     refs = refs[(row_blocks + 1) * count :]
     gate, up, refs = refs[0], refs[1], refs[2:]
@@ -225,7 +225,10 @@
     hidden = gate.shape[2]
     tile = min(256, hidden)
     sums = [[None] * (hidden // tile), [None] * (hidden // tile)]
-    totals = [squares[s * height : (s + 1) * height, :] if first else 0.0 for s in range(row_blocks)]
+    mine = slice(offset, offset + row_blocks * height)
+    totals = [0.0] * row_blocks
+    if first:
+        totals = [squares[offset + s * height : offset + (s + 1) * height, :] for s in range(row_blocks)]
     for k in range(count):
         for s in range(row_blocks):
             wide = blocks[s * count + k][...].astype(jnp.float32)
@@ -234,7 +237,7 @@
     for w, (weight, start) in enumerate(((gate, gate_sum), (up, up_sum))):
         for j in range(hidden // tile):
             cut = slice(j * tile, (j + 1) * tile)
-            total = start[:, cut] if first else None
+            total = start[mine, cut] if first else None
             for k in range(count):
                 depth = pl.ds(pl.multiple_of(places[first + k] * width, 128), width)
                 product = jnp.dot(
@@ -255,7 +258,7 @@
         active[:, j * tile : (j + 1) * tile] = (gate_part / (1.0 + jnp.exp(-gate_part)) * up_part).astype(jnp.bfloat16)
 
 
-def activate(places, blocks, gains, gate_weight, up_weight, cores, first, before):
+def activate(places, blocks, gains, gate_weight, up_weight, first, offset, before, after):
     row_blocks, count = len(blocks), len(blocks[0])
     height, width = blocks[0][0].shape
     rows = row_blocks * height
@@ -266,9 +269,10 @@
     else:
         kinds = [jax.ShapeDtypeStruct((rows, n), jnp.float32) for n in (hidden, hidden, 1)]
     return pl.pallas_call(
-        functools.partial(gate_kernel, row_blocks, cores, first, count, model_width),
+        functools.partial(gate_kernel, row_blocks, first, count, offset, model_width),
         out_shape=kinds,
-        in_specs=[pl.BlockSpec(memory_space=pltpu.SMEM)] + [whole] * ((row_blocks + 1) * count + 2 + len(before)),
+        in_specs=[pl.BlockSpec(memory_space=pltpu.SMEM)] + [whole] * ((row_blocks + 1) * count + 2 + len(before))
+        + [pl.BlockSpec(memory_space=pl.ANY)] * len(after),
         out_specs=whole if first else [whole] * 3,
         scratch_shapes=[pltpu.VMEM((rows, count * width), jnp.bfloat16)],
         cost_estimate=pl.CostEstimate(
@@ -276,7 +280,7 @@
         ),
         compiler_params=pltpu.CompilerParams(vmem_limit_bytes=2 * rows * (count * width + 8 * hidden) + 12 * MIB),
         name="activate",
-    )(places, *[b for row in blocks for b in row], *gains, in_vmem(gate_weight), in_vmem(up_weight), *before)
+    )(places, *[b for row in blocks for b in row], *gains, in_vmem(gate_weight), in_vmem(up_weight), *before, *after)
 
 
 def down_kernel(slots, at, column_blocks, cores, places, active, row_weight, down, *refs):
@@ -437,21 +441,45 @@
         rows_of[k] = from_tp(source, low)
     slots = list(reversed(range(tp_count)))
     near = {k: [rows_of[k], from_core(rows_of[k])] for k in slots}
-    sums = activate(places, [near[k] for k in slots], gains[:cores], gate_weight, up_weight, cores, 0, [])
-    far = {}
-    for k in [0] + slots[:-1]:
+    half = tp_count // 2
+    early = [k for k in slots if k % half == 0] if tp_count == 4 else slots[half:]
+    late = [k for k in slots if k not in early]
+    ordered = late + early
+    sums = activate(places, [near[k] for k in ordered], gains[:cores], gate_weight, up_weight, 0, 0, [], [])
+
+    def run_expert(group, after):
+        active = activate(
+            places,
+            [far[k] for k in group],
+            gains[cores:],
+            gate_weight,
+            up_weight,
+            cores,
+            ordered.index(group[0]) * block_rows,
+            sums,
+            after,
+        )
+        got = project_down(places, active, row_weight, down_weight, group, 0, block_rows, ep_count, cores, [])
+        outs.update(zip(group, got))
+        return got[0][:1]
+
+    far, outs = {}, {}
+    last = tp_count - 1
+    for k in early + late[::-1]:
         far[k] = []
+        if k == last:
+            done = run_expert(early, [])
         for b in range(1, chips):
             if k == 0:
                 value = crossed[b - 1]
             elif k == 1:
-                (source,) = add([[(crossed[b - 1], 0)]], block_rows, [rows_of[tp_count - 1]])
+                (source,) = add([[(crossed[b - 1], 0)]], block_rows, near[last][1:])
                 value = from_tp(source, 1)
             else:
                 value = from_chip(rows_of[k], b)
-            (later,) = add([[(value, 0)]], block_rows, sums[-1:]) if k == tp_count - 1 else (value,)
+            (later,) = add([[(value, 0)]], block_rows, done) if k == last else (value,)
             far[k] += [value, from_core(later)]
-    active = activate(places, [far[k] for k in slots], gains[cores:], gate_weight, up_weight, cores, cores, sums)
+    run_expert(late, done)
 
     def send_back(k, after):
         total = list(add([terms[k]], block_rows, after))
@@ -461,11 +489,9 @@
 
     terms = [[] for _ in range(tp_count)]
     arrivals, sent = [], []
-    outs = project_down(places, active, row_weight, down_weight, slots, 0, block_rows, ep_count, cores, [])
-    swapped = [from_core(out[1]) for out in outs]
+    swapped = {k: from_core(outs[k][1]) for k in slots}
     def core_sums(k, after):
-        at = slots.index(k)
-        rows = [[(outs[at][0], c * block_rows), (swapped[at], c * block_rows)] for c in range(chips)]
+        rows = [[(outs[k][0], c * block_rows), (swapped[k], c * block_rows)] for c in range(chips)]
         return rows, after
 
     def cross(k, extra, after):

time: 113 us -> 117 us (1.035)
  waiting for transfers between devices: 46.7 us -> 50.1 us
  Pallas kernels: 36.3 us -> 38 us
    ppermute x11, waiting for transfers between devices: 31.6 us -> 36.2 us  [from_tp(): return lax.ppermute(value, 'tp', [(i, i ^ bits) for i in range(tp_count)])]
    ppermute x11, starting transfers between devices: 13.4 us -> 11.8 us  [from_tp(): return lax.ppermute(value, 'tp', [(i, i ^ bits) for i in range(tp_count)])]
    pallas_call x1 -> x2, Pallas kernels: 2.7 us -> 3.55 us  [project_down(): pl.pallas_call(functools.partial(down_kernel, slots, at, column_blocks, c...]
    pallas_call x2 -> x3, Pallas kernels: 5.52 us -> 6.35 us  [activate(): pl.pallas_call(functools.partial(gate_kernel, row_blocks, first, count, o...]
  transfers between devices with their start and end apart: 35 -> 35, of which waited for: 18 -> 17; matrix products, arithmetic and copies ran while one was open for 0% -> 0% of each run, Pallas kernels for 13% -> 16%
where the time goes in v15:
time: 117 us
  waiting for transfers between devices  50.1 us (43%)
  Pallas kernels  38 us (32%)
  starting transfers between devices  26.9 us (23%)
    ppermute x11, waiting for transfers between devices, from_tp(): return lax.ppermute(value, 'tp', [(i, i ^ bits) for i in range(tp_count)])  36.2 us
    pallas_call x1, Pallas kernels, attend(): pl.pallas_call(functools.partial(attention_kernel, step_rows, pieces, ahe...  12.3 us
    ppermute x11, starting transfers between devices, from_tp(): return lax.ppermute(value, 'tp', [(i, i ^ bits) for i in range(tp_count)])  11.8 us
    ppermute x8, starting transfers between devices, from_chip(): lax.ppermute(value, 'ep', [(i, (i + step) % ep_count) for i in range(ep_c...  11.8 us
    pallas_call x4, Pallas kernels, fetch(): pl.pallas_call(functools.partial(fetch_kernel, parts), out_shape=pltpu.VM...  11.6 us
    ppermute x8, waiting for transfers between devices, from_chip(): lax.ppermute(value, 'ep', [(i, (i + step) % ep_count) for i in range(ep_c...  10.2 us
    pallas_call x3, Pallas kernels, activate(): pl.pallas_call(functools.partial(gate_kernel, row_blocks, first, count, o...  6.35 us
    ppermute x16, waiting for transfers between devices, from_core(): return lax.ppermute(value, 'ep', [(i, i ^ 1) for i in range(ep_count)])  3.64 us
  transfers between devices with their start and end apart: 35, of which 17 were waited for; matrix products, arithmetic and copies ran while one was open for 0% of the time, Pallas kernels for 16%

profile of v15, /device:TPU:0, one launch (start us, length us, event | category | flops | bytes accessed | tf_op | source)
XLA Modules:
  0.0 117.0 jit_solution(692576005880746363)
XLA Ops:
  0.8 0.7 copy-done.2
  1.5 12.3 %attention.1.refs_1_.refs_0_ = bf16[64,1024]{1,0:T(8,128)(2,1)S(1)} custom-call(s32[64]{0:T(128)S(1)} %copy-done.2, bf16[64,8,512]{2,1,0:T(8,128)(2,1)} %q_ref.1, bf16[64,512]{1,0:T(8,128)(2,1)} %qr_ref.1, bf16[64,256,512]{2,1,0:T(8,128)(2,1)} %k_hbm.1, bf16[64,64,256]{2,1,0:T(8,128)(2,1)} %kr_hbm.1, bf16[8,512,128]{2,1,0:T(8,128)(2,1)} %up_hbm.1, ...), custom_call_target="tpu_custom_call" | custom-call | flops 4294967296 | bytes 16777216 | tf_op jit(solution)/shard_map/attention/pallas_call | solution.py:135
  13.9 0.5 collective-permute-start
  14.4 2.6 %collective-permute-start.1 = (bf16[64,1024]{1,0:T(8,128)(2,1)S(1)}, bf16[64,1024]{1,0:T(8,128)(2,1)S(1)}, u32[]{:S(2)}, u32[]{:S(2)}) collective-permute-start(bf16[64,1024]{1,0:T(8,128)(2,1)S(1)} %attention.1.refs_1_.refs_0_), channel_id=1, source_target_pairs={{0,8},{4,12},{8,0},{12,4},{1,9},{5,13},{9,1},{13,5},{2,10},{6,14},... | collective-permute-start | bytes 393224 | tf_op jit(solution)/shard_map/ppermute | solution.py:390
  17.2 2.0 %fetch.4.refs_1_.refs_4_ = bf16[1024,1792]{1,0:T(8,128)(2,1)S(1)} custom-call(bf16[1024,1792]{1,0:T(8,128)(2,1)} %refs_0_.4, bf16[64,1024]{1,0:T(8,128)(2,1)S(1)} %attention.1.refs_1_.refs_0_, f32[256,1]{1,0:T(8,128)S(1)} %copy.16.refs_2_.row_weight, bf16[64,1792]{1,0:T(8,128)(2,1)S(1)} %constant_dynamic-slice_fusion.refs_3_.refs_7_, ...), custom_call_target="tpu_custom_call" | custom-call | bytes 7340032 | tf_op jit(solution)/shard_map/fetch/pallas_call | solution.py:38
  19.2 1.8 %collective-permute-done.1.refs_0_ = bf16[64,1024]{1,0:T(8,128)(2,1)S(1)} collective-permute-done((bf16[64,1024]{1,0:T(8,128)(2,1)S(1)}, bf16[64,1024]{1,0:T(8,128)(2,1)S(1)}, u32[]{:S(2)}, u32[]{:S(2)}) %collective-permute-start.1) | collective-permute-done | bytes 131104 | tf_op jit(solution)/shard_map/ppermute | solution.py:390
  21.1 1.3 %collective-permute-done.2.refs_3_ = bf16[64,1024]{1,0:T(8,128)(2,1)S(1)} collective-permute-done((bf16[64,1024]{1,0:T(8,128)(2,1)S(1)}, bf16[64,1024]{1,0:T(8,128)(2,1)S(1)}, u32[]{:S(2)}, u32[]{:S(2)}) %collective-permute-start.2) | collective-permute-done | bytes 131104 | tf_op jit(solution)/shard_map/ppermute | solution.py:386
  22.5 1.8 %projection.1 = (bf16[64,1792]{1,0:T(8,128)(2,1)S(1)}, bf16[64,1792]{1,0:T(8,128)(2,1)S(1)}, bf16[64,1792]{1,0:T(8,128)(2,1)S(1)}, bf16[64,1792]{1,0:T(8,128)(2,1)S(1)}) custom-call(s32[8]{0:T(128)S(1)} %stack.35.refs_0_.places, bf16[64,1024]{1,0:T(8,128)(2,1)S(1)} %attention.1.refs_1_.refs_0_, bf16[64,1024]{1,0:T(8,128)(2,1)S(1)} %collective-permute-done.refs_1_, ...), custom_call_target="tpu_custom_call" | custom-call | flops 939524096 | bytes 4194304 | tf_op jit(solution)/shard_map/projection/pallas_call | solution.py:200
  24.2 1.9 %collective-permute-start.3 = (bf16[64,1792]{1,0:T(8,128)(2,1)S(1)}, bf16[64,1792]{1,0:T(8,128)(2,1)S(1)}, u32[]{:S(2)}, u32[]{:S(2)}) collective-permute-start(bf16[64,1792]{1,0:T(8,128)(2,1)S(1)} %get-tuple-element.29), channel_id=1, source_target_pairs={{0,1},{1,0},{2,3},{3,2},{4,5},{5,4},{6,7},{7,6},{8,9},{9,8},{10,11... | collective-permute-start | bytes 688136 | tf_op jit(solution)/shard_map/ppermute | solution.py:393
  26.1 3.2 %fetch.5.refs_1_.refs_12_.refs_10_.refs_6_ = bf16[1,7168,512]{2,1,0:T(8,128)(2,1)S(1)} custom-call(bf16[1,7168,512]{2,1,0:T(8,128)(2,1)} %refs_0_.5, bf16[64,1792]{1,0:T(8,128)(2,1)S(1)} %get-tuple-element.27.refs_1_.refs_0_.refs_4_), custom_call_target="tpu_custom_call" | custom-call | bytes 14680064 | tf_op jit(solution)/shard_map/fetch/pallas_call | solution.py:38
  29.6 2.6 %collective-permute-done.3.refs_1_ = bf16[64,1792]{1,0:T(8,128)(2,1)S(1)} collective-permute-done((bf16[64,1792]{1,0:T(8,128)(2,1)S(1)}, bf16[64,1792]{1,0:T(8,128)(2,1)S(1)}, u32[]{:S(2)}, u32[]{:S(2)}) %collective-permute-start.3) | collective-permute-done | bytes 229408 | tf_op jit(solution)/shard_map/ppermute | solution.py:393
  32.2 3.0 %collective-permute-start.4 = (bf16[64,1792]{1,0:T(8,128)(2,1)S(1)}, bf16[64,1792]{1,0:T(8,128)(2,1)S(1)}, u32[]{:S(2)}, u32[]{:S(2)}) collective-permute-start(bf16[64,1792]{1,0:T(8,128)(2,1)S(1)} %add.65), channel_id=1, source_target_pairs={{0,2},{1,3},{2,0},{3,1},{4,6},{5,7},{6,4},{7,5},{8,10},{9,11},{10,... | collective-permute-start | bytes 688136 | tf_op jit(solution)/shard_map/ppermute | solution.py:393
  35.2 1.5 %collective-permute-start.7 = (f32[1,1792]{1,0:T(1,128)S(1)}, f32[1,1792]{1,0:T(1,128)S(1)}, u32[]{:S(2)}, u32[]{:S(2)}) collective-permute-start(f32[1,1792]{1,0:T(1,128)S(1)} %reshape.7.refs_4_.refs_8_), channel_id=1, source_target_pairs={{0,8},{4,12},{8,0},{12,4},{1,9},{5,13},{9,1},{13,5},{2,10},{6,14},... | collective-permute-start | bytes 21512 | tf_op jit(solution)/shard_map/ppermute | solution.py:390
  36.7 2.2 %collective-permute-done.7.refs_10_.refs_4_ = f32[1,1792]{1,0:T(1,128)S(1)} collective-permute-done((f32[1,1792]{1,0:T(1,128)S(1)}, f32[1,1792]{1,0:T(1,128)S(1)}, u32[]{:S(2)}, u32[]{:S(2)}) %collective-permute-start.7) | collective-permute-done | bytes 7200 | tf_op jit(solution)/shard_map/ppermute | solution.py:390
  38.8 3.2 %fetch.6.refs_13_.refs_11_.refs_7_ = bf16[1,7168,512]{2,1,0:T(8,128)(2,1)S(1)} custom-call(bf16[1,7168,512]{2,1,0:T(8,128)(2,1)} %refs_0_.6, bf16[64,1792]{1,0:T(8,128)(2,1)S(1)} %add.66.refs_1_), custom_call_target="tpu_custom_call" | custom-call | bytes 14680064 | tf_op jit(solution)/shard_map/fetch/pallas_call | solution.py:38
  42.0 3.2 %fetch.7.refs_14_.down = bf16[1,512,7168]{2,1,0:T(8,128)(2,1)S(1)} custom-call(bf16[1,512,7168]{2,1,0:T(8,128)(2,1)} %refs_0_.7, bf16[64,1792]{1,0:T(8,128)(2,1)S(1)} %add.66.refs_1_), custom_call_target="tpu_custom_call" | custom-call | bytes 14680064 | tf_op jit(solution)/shard_map/fetch/pallas_call | solution.py:38
  45.3 0.8 add.67
  46.2 1.7 %collective-permute-start.12 = (bf16[64,1792]{1,0:T(8,128)(2,1)S(1)}, bf16[64,1792]{1,0:T(8,128)(2,1)S(1)}, u32[]{:S(2)}, u32[]{:S(2)}) collective-permute-start(bf16[64,1792]{1,0:T(8,128)(2,1)S(1)} %get-tuple-element.32.refs_6_), channel_id=1, source_target_pairs={{0,8},{4,12},{8,0},{12,4},{1,9},{5,13},{9,1},{13,5},{2,10},{6,14},... | collective-permute-start | bytes 688136 | tf_op jit(solution)/shard_map/ppermute | solution.py:390
  47.9 12.0 %collective-permute-done.9.refs_0_.refs_4_ = bf16[64,1792]{1,0:T(8,128)(2,1)S(1)} collective-permute-done((bf16[64,1792]{1,0:T(8,128)(2,1)S(1)}, bf16[64,1792]{1,0:T(8,128)(2,1)S(1)}, u32[]{:S(2)}, u32[]{:S(2)}) %collective-permute-start.9) | collective-permute-done | bytes 229408 | tf_op jit(solution)/shard_map/ppermute | solution.py:393
  60.1 2.0 %collective-permute-start.16 = (bf16[64,1792]{1,0:T(8,128)(2,1)S(1)}, bf16[64,1792]{1,0:T(8,128)(2,1)S(1)}, u32[]{:S(2)}, u32[]{:S(2)}) collective-permute-start(bf16[64,1792]{1,0:T(8,128)(2,1)S(1)} %get-tuple-element.32.refs_6_), channel_id=1, source_target_pairs={{0,1},{1,0},{2,3},{3,2},{4,5},{5,4},{6,7},{7,6},{8,9},{9,8},{10,11... | collective-permute-start | bytes 688136 | tf_op jit(solution)/shard_map/ppermute | solution.py:393
  62.1 1.5 %collective-permute-start.10 = (bf16[64,1792]{1,0:T(8,128)(2,1)S(1)}, bf16[64,1792]{1,0:T(8,128)(2,1)S(1)}, u32[]{:S(2)}, u32[]{:S(2)}) collective-permute-start(bf16[64,1792]{1,0:T(8,128)(2,1)S(1)} %collective-permute-done.9.refs_0_.refs_4_), channel_id=1, source_target_pairs={{0,8},{4,12},{8,0},{12,4},{1,9},{5,13},{9,1},{13,5},{2,10},{6,14},... | collective-permute-start | bytes 688136 | tf_op jit(solution)/shard_map/ppermute | solution.py:390
  63.6 5.0 %collective-permute-done.14.refs_0_ = bf16[64,1792]{1,0:T(8,128)(2,1)S(1)} collective-permute-done((bf16[64,1792]{1,0:T(8,128)(2,1)S(1)}, bf16[64,1792]{1,0:T(8,128)(2,1)S(1)}, u32[]{:S(2)}, u32[]{:S(2)}) %collective-permute-start.14) | collective-permute-done | bytes 229408 | tf_op jit(solution)/shard_map/ppermute | solution.py:393
  68.6 0.5 collective-permute-start.19
  69.1 3.1 %collective-permute-done.16.refs_2_ = bf16[64,1792]{1,0:T(8,128)(2,1)S(1)} collective-permute-done((bf16[64,1792]{1,0:T(8,128)(2,1)S(1)}, bf16[64,1792]{1,0:T(8,128)(2,1)S(1)}, u32[]{:S(2)}, u32[]{:S(2)}) %collective-permute-start.16) | collective-permute-done | bytes 229408 | tf_op jit(solution)/shard_map/ppermute | solution.py:393
  72.2 0.5 collective-permute-start.18
  73.3 1.5 %collective-permute-start.21 = (bf16[64,1792]{1,0:T(8,128)(2,1)S(1)}, bf16[64,1792]{1,0:T(8,128)(2,1)S(1)}, u32[]{:S(2)}, u32[]{:S(2)}) collective-permute-start(bf16[64,1792]{1,0:T(8,128)(2,1)S(1)} %collective-permute-done.14.refs_0_), channel_id=1, source_target_pairs={{0,8},{4,12},{8,0},{12,4},{1,9},{5,13},{9,1},{13,5},{2,10},{6,14},... | collective-permute-start | bytes 688136 | tf_op jit(solution)/shard_map/ppermute | solution.py:390
  75.1 2.7 %activate.3 = (f32[256,512]{1,0:T(8,128)S(1)}, f32[256,512]{1,0:T(8,128)S(1)}, f32[256,1]{1,0:T(8,128)S(1)}) custom-call(s32[8]{0:T(128)S(1)} %stack.35.refs_0_.places, bf16[64,1792]{1,0:T(8,128)(2,1)S(1)} %collective-permute-done.14.refs_0_, bf16[64,1792]{1,0:T(8,128)(2,1)S(1)} %collective-permute-done.15.refs_1_, ...), custom_call_target="tpu_custom_call" | custom-call | flops 1879048192 | bytes 7340032 | tf_op jit(solution)/shard_map/activate/pallas_call | solution.py:271
  77.8 1.8 %activate.4.active = bf16[128,512]{1,0:T(8,128)(2,1)S(1)} custom-call(s32[8]{0:T(128)S(1)} %stack.35.refs_0_.places, bf16[64,1792]{1,0:T(8,128)(2,1)S(1)} %collective-permute-done.10.refs_0_, bf16[64,1792]{1,0:T(8,128)(2,1)S(1)} %collective-permute-done.11.refs_1_, bf16[64,1792]{1,0:T(8,128)(2,1)S(1)} %collective-permute-done.12.refs_1_.refs_2_.refs_0_, ...), custom_call_target="tpu_custom_call" | custom-call | flops 939524096 | bytes 7340032 | tf_op jit(solution)/shard_map/activate/pallas_call | solution.py:271
  79.6 1.8 %down.2 = (bf16[128,1792]{1,0:T(8,128)(2,1)S(1)}, bf16[128,1792]{1,0:T(8,128)(2,1)S(1)}, bf16[128,1792]{1,0:T(8,128)(2,1)S(1)}, bf16[128,1792]{1,0:T(8,128)(2,1)S(1)}) custom-call(s32[8]{0:T(128)S(1)} %stack.35.refs_0_.places, bf16[128,512]{1,0:T(8,128)(2,1)S(1)} %activate.4.active, f32[256,1]{1,0:T(8,128)S(1)} %copy.16.refs_2_.row_weight, ...), custom_call_target="tpu_custom_call" | custom-call | flops 939524096 | bytes 7340032 | tf_op jit(solution)/shard_map/down/pallas_call | solution.py:317
  81.5 0.6 collective-permute-done.23.refs_2_
  82.1 0.9 collective-permute-done.22.refs_1_
  83.0 0.6 collective-permute-done.24.refs_3_
  83.6 1.8 %activate.5.active = bf16[128,512]{1,0:T(8,128)(2,1)S(1)} custom-call(s32[8]{0:T(128)S(1)} %stack.35.refs_0_.places, bf16[64,1792]{1,0:T(8,128)(2,1)S(1)} %collective-permute-done.21.refs_0_, bf16[64,1792]{1,0:T(8,128)(2,1)S(1)} %collective-permute-done.22.refs_1_, bf16[64,1792]{1,0:T(8,128)(2,1)S(1)} %collective-permute-done.23.refs_2_, ...), custom_call_target="tpu_custom_call" | custom-call | flops 939524096 | bytes 7340032 | tf_op jit(solution)/shard_map/activate/pallas_call | solution.py:271
  85.4 1.8 %down.3 = (bf16[128,1792]{1,0:T(8,128)(2,1)S(1)}, bf16[128,1792]{1,0:T(8,128)(2,1)S(1)}, bf16[128,1792]{1,0:T(8,128)(2,1)S(1)}, bf16[128,1792]{1,0:T(8,128)(2,1)S(1)}) custom-call(s32[8]{0:T(128)S(1)} %stack.35.refs_0_.places, bf16[128,512]{1,0:T(8,128)(2,1)S(1)} %activate.5.active, f32[256,1]{1,0:T(8,128)S(1)} %copy.16.refs_2_.row_weight, ...), custom_call_target="tpu_custom_call" | custom-call | flops 939524096 | bytes 7340032 | tf_op jit(solution)/shard_map/down/pallas_call | solution.py:317
  88.3 0.8 collective-permute-done.25.refs_1_.refs_3_
  89.2 1.6 %collective-permute-start.26 = (bf16[64,1792]{1,0:T(8,128)(2,1)S(1)}, bf16[64,1792]{1,0:T(8,128)(2,1)S(1)}, u32[]{:S(2)}, u32[]{:S(2)}) collective-permute-start(bf16[64,1792]{1,0:T(8,128)(2,1)S(1)} %get-tuple-element.41), channel_id=1, source_target_pairs={{0,1},{1,0},{2,3},{3,2},{4,5},{5,4},{6,7},{7,6},{8,9},{9,8},{10,11... | collective-permute-start | bytes 688136 | tf_op jit(solution)/shard_map/ppermute | solution.py:393
  90.9 0.6 collective-permute-start.28
  91.6 1.6 %collective-permute-start.31 = (bf16[64,1792]{1,0:T(8,128)(2,1)S(1)}, bf16[64,1792]{1,0:T(8,128)(2,1)S(1)}, u32[]{:S(2)}, u32[]{:S(2)}) collective-permute-start(bf16[64,1792]{1,0:T(8,128)(2,1)S(1)} %get-tuple-element.50), channel_id=1, source_target_pairs={{0,8},{4,12},{8,0},{12,4},{1,9},{5,13},{9,1},{13,5},{2,10},{6,14},... | collective-permute-start | bytes 688136 | tf_op jit(solution)/shard_map/ppermute | solution.py:390
  93.2 3.8 %collective-permute-done.26.refs_2_.refs_4_ = bf16[64,1792]{1,0:T(8,128)(2,1)S(1)} collective-permute-done((bf16[64,1792]{1,0:T(8,128)(2,1)S(1)}, bf16[64,1792]{1,0:T(8,128)(2,1)S(1)}, u32[]{:S(2)}, u32[]{:S(2)}) %collective-permute-start.26) | collective-permute-done | bytes 229408 | tf_op jit(solution)/shard_map/ppermute | solution.py:393
  97.0 2.5 %collective-permute-done.28.refs_1_ = bf16[64,1792]{1,0:T(8,128)(2,1)S(1)} collective-permute-done((bf16[64,1792]{1,0:T(8,128)(2,1)S(1)}, bf16[64,1792]{1,0:T(8,128)(2,1)S(1)}, u32[]{:S(2)}, u32[]{:S(2)}) %collective-permute-start.28) | collective-permute-done | bytes 229408 | tf_op jit(solution)/shard_map/ppermute | solution.py:390
  99.5 0.5 collective-permute-start.32
  100.2 0.8 collective-permute-start.29
  101.0 3.4 %collective-permute-done.31.refs_1_ = bf16[64,1792]{1,0:T(8,128)(2,1)S(1)} collective-permute-done((bf16[64,1792]{1,0:T(8,128)(2,1)S(1)}, bf16[64,1792]{1,0:T(8,128)(2,1)S(1)}, u32[]{:S(2)}, u32[]{:S(2)}) %collective-permute-start.31) | collective-permute-done | bytes 229408 | tf_op jit(solution)/shard_map/ppermute | solution.py:390
  104.4 1.2 %collective-permute-done.32.refs_2_ = bf16[64,1792]{1,0:T(8,128)(2,1)S(1)} collective-permute-done((bf16[64,1792]{1,0:T(8,128)(2,1)S(1)}, bf16[64,1792]{1,0:T(8,128)(2,1)S(1)}, u32[]{:S(2)}, u32[]{:S(2)}) %collective-permute-start.32) | collective-permute-done | bytes 229408 | tf_op jit(solution)/shard_map/ppermute | solution.py:393
  105.7 0.6 collective-permute-start.33
  106.3 1.5 %collective-permute-start.34 = (bf16[64,1792]{1,0:T(8,128)(2,1)S(1)}, bf16[64,1792]{1,0:T(8,128)(2,1)S(1)}, u32[]{:S(2)}, u32[]{:S(2)}) collective-permute-start(bf16[64,1792]{1,0:T(8,128)(2,1)S(1)} %get-tuple-element.51), channel_id=1, source_target_pairs={{0,1},{1,0},{2,3},{3,2},{4,5},{5,4},{6,7},{7,6},{8,9},{9,8},{10,11... | collective-permute-start | bytes 688136 | tf_op jit(solution)/shard_map/ppermute | solution.py:393
  108.2 7.9 %collective-permute-done.33.refs_2_ = bf16[64,1792]{1,0:T(8,128)(2,1)S(1)} collective-permute-done((bf16[64,1792]{1,0:T(8,128)(2,1)S(1)}, bf16[64,1792]{1,0:T(8,128)(2,1)S(1)}, u32[]{:S(2)}, u32[]{:S(2)}) %collective-permute-start.33) | collective-permute-done | bytes 229408 | tf_op jit(solution)/shard_map/ppermute | solution.py:393
  116.2 0.7 add.78
  (65 shorter events, 4.0 us)
Async XLA Ops:
  0.6 16.5 %copy-start = (bf16[256,1792]{1,0:T(8,128)(2,1)S(1)}, bf16[256,1792]{1,0:T(8,128)(2,1)}, u32[]{:S(2)}) copy-start(bf16[256,1792]{1,0:T(8,128)(2,1)} %param.21) | copy-start | bytes 2752516
  0.8 0.7 copy-start.2
  1.5 15.4 %copy-start.4 = (f32[256,2]{0,1:T(2,128)S(1)}, f32[256,2]{0,1:T(2,128)}, u32[]{:S(2)}) copy-start(f32[256,2]{0,1:T(2,128)} %param.24) | copy-start | bytes 6148
  1.5 15.4 %copy-start.5 = (s32[256,2]{0,1:T(2,128)S(1)}, s32[256,2]{0,1:T(2,128)}, u32[]{:S(2)}) copy-start(s32[256,2]{0,1:T(2,128)} %param.23) | copy-start | bytes 6148
  1.5 15.6 %copy-start.3 = (f32[1792]{0:T(1024)S(1)}, f32[1792]{0:T(1024)}, u32[]{:S(2)}) copy-start(f32[1792]{0:T(1024)} %param.22) | copy-start | bytes 21508
  13.9 7.3 %collective-permute-start = (bf16[64,1024]{1,0:T(8,128)(2,1)S(1)}, bf16[64,1024]{1,0:T(8,128)(2,1)S(1)}, u32[]{:S(2)}, u32[]{:S(2)}) collective-permute-start(bf16[64,1024]{1,0:T(8,128)(2,1)S(1)} %attention.1.refs_1_.refs_0_), channel_id=1, source_target_pairs={{0,4},{4,0},{8,12},{12,8},{1,5},{5,1},{9,13},{13,9},{2,6},{6,2},{1... | collective-permute-start | bytes 393224 | tf_op jit(solution)/shard_map/ppermute | solution.py:386
  14.4 6.7 %collective-permute-start.1 = (bf16[64,1024]{1,0:T(8,128)(2,1)S(1)}, bf16[64,1024]{1,0:T(8,128)(2,1)S(1)}, u32[]{:S(2)}, u32[]{:S(2)}) collective-permute-start(bf16[64,1024]{1,0:T(8,128)(2,1)S(1)} %attention.1.refs_1_.refs_0_), channel_id=1, source_target_pairs={{0,8},{4,12},{8,0},{12,4},{1,9},{5,13},{9,1},{13,5},{2,10},{6,14},... | collective-permute-start | bytes 393224 | tf_op jit(solution)/shard_map/ppermute | solution.py:390
  21.0 1.4 %collective-permute-start.2 = (bf16[64,1024]{1,0:T(8,128)(2,1)S(1)}, bf16[64,1024]{1,0:T(8,128)(2,1)S(1)}, u32[]{:S(2)}, u32[]{:S(2)}) collective-permute-start(bf16[64,1024]{1,0:T(8,128)(2,1)S(1)} %add.64.refs_2_), channel_id=1, source_target_pairs={{0,4},{4,0},{8,12},{12,8},{1,5},{5,1},{9,13},{13,9},{2,6},{6,2},{1... | collective-permute-start | bytes 393224 | tf_op jit(solution)/shard_map/ppermute | solution.py:386
  24.2 7.9 %collective-permute-start.3 = (bf16[64,1792]{1,0:T(8,128)(2,1)S(1)}, bf16[64,1792]{1,0:T(8,128)(2,1)S(1)}, u32[]{:S(2)}, u32[]{:S(2)}) collective-permute-start(bf16[64,1792]{1,0:T(8,128)(2,1)S(1)} %get-tuple-element.29), channel_id=1, source_target_pairs={{0,1},{1,0},{2,3},{3,2},{4,5},{5,4},{6,7},{7,6},{8,9},{9,8},{10,11... | collective-permute-start | bytes 688136 | tf_op jit(solution)/shard_map/ppermute | solution.py:393
  29.4 15.9 %collective-permute-start.5 = (bf16[64,1792]{1,0:T(8,128)(2,1)S(1)}, bf16[64,1792]{1,0:T(8,128)(2,1)S(1)}, u32[]{:S(2)}, u32[]{:S(2)}) collective-permute-start(bf16[64,1792]{1,0:T(8,128)(2,1)S(1)} %add.66.refs_1_), channel_id=1, source_target_pairs={{0,1},{1,0},{2,3},{3,2},{4,5},{5,4},{6,7},{7,6},{8,9},{9,8},{10,11... | collective-permute-start | bytes 688136 | tf_op jit(solution)/shard_map/ppermute | solution.py:393
  32.2 13.1 %collective-permute-start.4 = (bf16[64,1792]{1,0:T(8,128)(2,1)S(1)}, bf16[64,1792]{1,0:T(8,128)(2,1)S(1)}, u32[]{:S(2)}, u32[]{:S(2)}) collective-permute-start(bf16[64,1792]{1,0:T(8,128)(2,1)S(1)} %add.65), channel_id=1, source_target_pairs={{0,2},{1,3},{2,0},{3,1},{4,6},{5,7},{6,4},{7,5},{8,10},{9,11},{10,... | collective-permute-start | bytes 688136 | tf_op jit(solution)/shard_map/ppermute | solution.py:393
  35.2 3.6 %collective-permute-start.7 = (f32[1,1792]{1,0:T(1,128)S(1)}, f32[1,1792]{1,0:T(1,128)S(1)}, u32[]{:S(2)}, u32[]{:S(2)}) collective-permute-start(f32[1,1792]{1,0:T(1,128)S(1)} %reshape.7.refs_4_.refs_8_), channel_id=1, source_target_pairs={{0,8},{4,12},{8,0},{12,4},{1,9},{5,13},{9,1},{13,5},{2,10},{6,14},... | collective-permute-start | bytes 21512 | tf_op jit(solution)/shard_map/ppermute | solution.py:390
  36.7 8.6 %collective-permute-start.6 = (f32[1,1792]{1,0:T(1,128)S(1)}, f32[1,1792]{1,0:T(1,128)S(1)}, u32[]{:S(2)}, u32[]{:S(2)}) collective-permute-start(f32[1,1792]{1,0:T(1,128)S(1)} %reshape.7.refs_4_.refs_8_), channel_id=1, source_target_pairs={{0,4},{4,0},{8,12},{12,8},{1,5},{5,1},{9,13},{13,9},{2,6},{6,2},{1... | collective-permute-start | bytes 21512 | tf_op jit(solution)/shard_map/ppermute | solution.py:386
  38.8 6.4 %collective-permute-start.8 = (f32[1,1792]{1,0:T(1,128)S(1)}, f32[1,1792]{1,0:T(1,128)S(1)}, u32[]{:S(2)}, u32[]{:S(2)}) collective-permute-start(f32[1,1792]{1,0:T(1,128)S(1)} %collective-permute-done.7.refs_10_.refs_4_), channel_id=1, source_target_pairs={{0,4},{4,0},{8,12},{12,8},{1,5},{5,1},{9,13},{13,9},{2,6},{6,2},{1... | collective-permute-start | bytes 21512 | tf_op jit(solution)/shard_map/ppermute | solution.py:386
  46.1 13.8 %collective-permute-start.9 = (bf16[64,1792]{1,0:T(8,128)(2,1)S(1)}, bf16[64,1792]{1,0:T(8,128)(2,1)S(1)}, u32[]{:S(2)}, u32[]{:S(2)}) collective-permute-start(bf16[64,1792]{1,0:T(8,128)(2,1)S(1)} %get-tuple-element.32.refs_6_), channel_id=1, source_target_pairs={{0,2},{1,3},{2,0},{3,1},{4,6},{5,7},{6,4},{7,5},{8,10},{9,11},{10,... | collective-permute-start | bytes 688136 | tf_op jit(solution)/shard_map/ppermute | solution.py:393
  46.2 13.8 %collective-permute-start.12 = (bf16[64,1792]{1,0:T(8,128)(2,1)S(1)}, bf16[64,1792]{1,0:T(8,128)(2,1)S(1)}, u32[]{:S(2)}, u32[]{:S(2)}) collective-permute-start(bf16[64,1792]{1,0:T(8,128)(2,1)S(1)} %get-tuple-element.32.refs_6_), channel_id=1, source_target_pairs={{0,8},{4,12},{8,0},{12,4},{1,9},{5,13},{9,1},{13,5},{2,10},{6,14},... | collective-permute-start | bytes 688136 | tf_op jit(solution)/shard_map/ppermute | solution.py:390
  60.0 8.6 %collective-permute-start.14 = (bf16[64,1792]{1,0:T(8,128)(2,1)S(1)}, bf16[64,1792]{1,0:T(8,128)(2,1)S(1)}, u32[]{:S(2)}, u32[]{:S(2)}) collective-permute-start(bf16[64,1792]{1,0:T(8,128)(2,1)S(1)} %add.68), channel_id=1, source_target_pairs={{0,1},{1,0},{2,3},{3,2},{4,5},{5,4},{6,7},{7,6},{8,9},{9,8},{10,11... | collective-permute-start | bytes 688136 | tf_op jit(solution)/shard_map/ppermute | solution.py:393
  60.1 12.1 %collective-permute-start.16 = (bf16[64,1792]{1,0:T(8,128)(2,1)S(1)}, bf16[64,1792]{1,0:T(8,128)(2,1)S(1)}, u32[]{:S(2)}, u32[]{:S(2)}) collective-permute-start(bf16[64,1792]{1,0:T(8,128)(2,1)S(1)} %get-tuple-element.32.refs_6_), channel_id=1, source_target_pairs={{0,1},{1,0},{2,3},{3,2},{4,5},{5,4},{6,7},{7,6},{8,9},{9,8},{10,11... | collective-permute-start | bytes 688136 | tf_op jit(solution)/shard_map/ppermute | solution.py:393
  62.1 10.6 %collective-permute-start.10 = (bf16[64,1792]{1,0:T(8,128)(2,1)S(1)}, bf16[64,1792]{1,0:T(8,128)(2,1)S(1)}, u32[]{:S(2)}, u32[]{:S(2)}) collective-permute-start(bf16[64,1792]{1,0:T(8,128)(2,1)S(1)} %collective-permute-done.9.refs_0_.refs_4_), channel_id=1, source_target_pairs={{0,8},{4,12},{8,0},{12,4},{1,9},{5,13},{9,1},{13,5},{2,10},{6,14},... | collective-permute-start | bytes 688136 | tf_op jit(solution)/shard_map/ppermute | solution.py:390
  68.6 4.2 %collective-permute-start.15 = (bf16[64,1792]{1,0:T(8,128)(2,1)S(1)}, bf16[64,1792]{1,0:T(8,128)(2,1)S(1)}, u32[]{:S(2)}, u32[]{:S(2)}) collective-permute-start(bf16[64,1792]{1,0:T(8,128)(2,1)S(1)} %collective-permute-done.14.refs_0_), channel_id=1, source_target_pairs={{0,4},{4,0},{8,12},{12,8},{1,5},{5,1},{9,13},{13,9},{2,6},{6,2},{1... | collective-permute-start | bytes 688136 | tf_op jit(solution)/shard_map/ppermute | solution.py:386
  68.6 4.7 %collective-permute-start.19 = (bf16[64,1792]{1,0:T(8,128)(2,1)S(1)}, bf16[64,1792]{1,0:T(8,128)(2,1)S(1)}, u32[]{:S(2)}, u32[]{:S(2)}) collective-permute-start(bf16[64,1792]{1,0:T(8,128)(2,1)S(1)} %get-tuple-element.32.refs_6_), channel_id=1, source_target_pairs={{0,4},{4,0},{8,12},{12,8},{1,5},{5,1},{9,13},{13,9},{2,6},{6,2},{1... | collective-permute-start | bytes 688136 | tf_op jit(solution)/shard_map/ppermute | solution.py:386
  72.2 2.6 %collective-permute-start.17 = (bf16[64,1792]{1,0:T(8,128)(2,1)S(1)}, bf16[64,1792]{1,0:T(8,128)(2,1)S(1)}, u32[]{:S(2)}, u32[]{:S(2)}) collective-permute-start(bf16[64,1792]{1,0:T(8,128)(2,1)S(1)} %collective-permute-done.16.refs_2_), channel_id=1, source_target_pairs={{0,4},{4,0},{8,12},{12,8},{1,5},{5,1},{9,13},{13,9},{2,6},{6,2},{1... | collective-permute-start | bytes 688136 | tf_op jit(solution)/shard_map/ppermute | solution.py:386
  72.2 2.9 %collective-permute-start.18 = (bf16[64,1792]{1,0:T(8,128)(2,1)S(1)}, bf16[64,1792]{1,0:T(8,128)(2,1)S(1)}, u32[]{:S(2)}, u32[]{:S(2)}) collective-permute-start(bf16[64,1792]{1,0:T(8,128)(2,1)S(1)} %collective-permute-done.9.refs_0_.refs_4_), channel_id=1, source_target_pairs={{0,4},{4,0},{8,12},{12,8},{1,5},{5,1},{9,13},{13,9},{2,6},{6,2},{1... | collective-permute-start | bytes 688136 | tf_op jit(solution)/shard_map/ppermute | solution.py:386
  72.7 5.1 %collective-permute-start.13 = (bf16[64,1792]{1,0:T(8,128)(2,1)S(1)}, bf16[64,1792]{1,0:T(8,128)(2,1)S(1)}, u32[]{:S(2)}, u32[]{:S(2)}) collective-permute-start(bf16[64,1792]{1,0:T(8,128)(2,1)S(1)} %collective-permute-done.12.refs_1_.refs_2_.refs_0_), channel_id=1, source_target_pairs={{0,4},{4,0},{8,12},{12,8},{1,5},{5,1},{9,13},{13,9},{2,6},{6,2},{1... | collective-permute-start | bytes 688136 | tf_op jit(solution)/shard_map/ppermute | solution.py:386
  72.7 5.1 %collective-permute-start.11 = (bf16[64,1792]{1,0:T(8,128)(2,1)S(1)}, bf16[64,1792]{1,0:T(8,128)(2,1)S(1)}, u32[]{:S(2)}, u32[]{:S(2)}) collective-permute-start(bf16[64,1792]{1,0:T(8,128)(2,1)S(1)} %collective-permute-done.10.refs_0_), channel_id=1, source_target_pairs={{0,4},{4,0},{8,12},{12,8},{1,5},{5,1},{9,13},{13,9},{2,6},{6,2},{1... | collective-permute-start | bytes 688136 | tf_op jit(solution)/shard_map/ppermute | solution.py:386
  73.3 8.2 %collective-permute-start.21 = (bf16[64,1792]{1,0:T(8,128)(2,1)S(1)}, bf16[64,1792]{1,0:T(8,128)(2,1)S(1)}, u32[]{:S(2)}, u32[]{:S(2)}) collective-permute-start(bf16[64,1792]{1,0:T(8,128)(2,1)S(1)} %collective-permute-done.14.refs_0_), channel_id=1, source_target_pairs={{0,8},{4,12},{8,0},{12,4},{1,9},{5,13},{9,1},{13,5},{2,10},{6,14},... | collective-permute-start | bytes 688136 | tf_op jit(solution)/shard_map/ppermute | solution.py:390
  74.8 7.3 %collective-permute-start.23 = (bf16[64,1792]{1,0:T(8,128)(2,1)S(1)}, bf16[64,1792]{1,0:T(8,128)(2,1)S(1)}, u32[]{:S(2)}, u32[]{:S(2)}) collective-permute-start(bf16[64,1792]{1,0:T(8,128)(2,1)S(1)} %add.70), channel_id=1, source_target_pairs={{0,1},{1,0},{2,3},{3,2},{4,5},{5,4},{6,7},{7,6},{8,9},{9,8},{10,11... | collective-permute-start | bytes 688136 | tf_op jit(solution)/shard_map/ppermute | solution.py:393
  81.5 1.6 %collective-permute-start.22 = (bf16[64,1792]{1,0:T(8,128)(2,1)S(1)}, bf16[64,1792]{1,0:T(8,128)(2,1)S(1)}, u32[]{:S(2)}, u32[]{:S(2)}) collective-permute-start(bf16[64,1792]{1,0:T(8,128)(2,1)S(1)} %add.69), channel_id=1, source_target_pairs={{0,4},{4,0},{8,12},{12,8},{1,5},{5,1},{9,13},{13,9},{2,6},{6,2},{1... | collective-permute-start | bytes 688136 | tf_op jit(solution)/shard_map/ppermute | solution.py:386
  82.1 1.5 %collective-permute-start.24 = (bf16[64,1792]{1,0:T(8,128)(2,1)S(1)}, bf16[64,1792]{1,0:T(8,128)(2,1)S(1)}, u32[]{:S(2)}, u32[]{:S(2)}) collective-permute-start(bf16[64,1792]{1,0:T(8,128)(2,1)S(1)} %collective-permute-done.23.refs_2_), channel_id=1, source_target_pairs={{0,4},{4,0},{8,12},{12,8},{1,5},{5,1},{9,13},{13,9},{2,6},{6,2},{1... | collective-permute-start | bytes 688136 | tf_op jit(solution)/shard_map/ppermute | solution.py:386
  85.4 31.5 %copy-start.1 = (bf16[256,1792]{1,0:T(8,128)(2,1)S(1)}, bf16[256,1792]{1,0:T(8,128)(2,1)}, u32[]{:S(2)}) copy-start(bf16[256,1792]{1,0:T(8,128)(2,1)} %param.21) | copy-start | bytes 2752516
  87.2 1.9 %collective-permute-start.25 = (bf16[128,1792]{1,0:T(8,128)(2,1)S(1)}, bf16[128,1792]{1,0:T(8,128)(2,1)S(1)}, u32[]{:S(2)}, u32[]{:S(2)}) collective-permute-start(bf16[128,1792]{1,0:T(8,128)(2,1)S(1)} %get-tuple-element.40), channel_id=1, source_target_pairs={{0,4},{4,0},{8,12},{12,8},{1,5},{5,1},{9,13},{13,9},{2,6},{6,2},{1... | collective-permute-start | bytes 1376264 | tf_op jit(solution)/shard_map/ppermute | solution.py:386
  87.5 3.3 %collective-permute-start.27 = (bf16[128,1792]{1,0:T(8,128)(2,1)S(1)}, bf16[128,1792]{1,0:T(8,128)(2,1)S(1)}, u32[]{:S(2)}, u32[]{:S(2)}) collective-permute-start(bf16[128,1792]{1,0:T(8,128)(2,1)S(1)} %get-tuple-element.43), channel_id=1, source_target_pairs={{0,4},{4,0},{8,12},{12,8},{1,5},{5,1},{9,13},{13,9},{2,6},{6,2},{1... | collective-permute-start | bytes 1376264 | tf_op jit(solution)/shard_map/ppermute | solution.py:386
  87.8 3.7 %collective-permute-start.30 = (bf16[128,1792]{1,0:T(8,128)(2,1)S(1)}, bf16[128,1792]{1,0:T(8,128)(2,1)S(1)}, u32[]{:S(2)}, u32[]{:S(2)}) collective-permute-start(bf16[128,1792]{1,0:T(8,128)(2,1)S(1)} %get-tuple-element.48), channel_id=1, source_target_pairs={{0,4},{4,0},{8,12},{12,8},{1,5},{5,1},{9,13},{13,9},{2,6},{6,2},{1... | collective-permute-start | bytes 1376264 | tf_op jit(solution)/shard_map/ppermute | solution.py:386
  88.0 12.1 %collective-permute-start.20 = (bf16[128,1792]{1,0:T(8,128)(2,1)S(1)}, bf16[128,1792]{1,0:T(8,128)(2,1)S(1)}, u32[]{:S(2)}, u32[]{:S(2)}) collective-permute-start(bf16[128,1792]{1,0:T(8,128)(2,1)S(1)} %get-tuple-element.37), channel_id=1, source_target_pairs={{0,4},{4,0},{8,12},{12,8},{1,5},{5,1},{9,13},{13,9},{2,6},{6,2},{1... | collective-permute-start | bytes 1376264 | tf_op jit(solution)/shard_map/ppermute | solution.py:386
  89.2 7.7 %collective-permute-start.26 = (bf16[64,1792]{1,0:T(8,128)(2,1)S(1)}, bf16[64,1792]{1,0:T(8,128)(2,1)S(1)}, u32[]{:S(2)}, u32[]{:S(2)}) collective-permute-start(bf16[64,1792]{1,0:T(8,128)(2,1)S(1)} %get-tuple-element.41), channel_id=1, source_target_pairs={{0,1},{1,0},{2,3},{3,2},{4,5},{5,4},{6,7},{7,6},{8,9},{9,8},{10,11... | collective-permute-start | bytes 688136 | tf_op jit(solution)/shard_map/ppermute | solution.py:393
  90.9 8.6 %collective-permute-start.28 = (bf16[64,1792]{1,0:T(8,128)(2,1)S(1)}, bf16[64,1792]{1,0:T(8,128)(2,1)S(1)}, u32[]{:S(2)}, u32[]{:S(2)}) collective-permute-start(bf16[64,1792]{1,0:T(8,128)(2,1)S(1)} %get-tuple-element.45), channel_id=1, source_target_pairs={{0,8},{4,12},{8,0},{12,4},{1,9},{5,13},{9,1},{13,5},{2,10},{6,14},... | collective-permute-start | bytes 688136 | tf_op jit(solution)/shard_map/ppermute | solution.py:390
  91.6 12.8 %collective-permute-start.31 = (bf16[64,1792]{1,0:T(8,128)(2,1)S(1)}, bf16[64,1792]{1,0:T(8,128)(2,1)S(1)}, u32[]{:S(2)}, u32[]{:S(2)}) collective-permute-start(bf16[64,1792]{1,0:T(8,128)(2,1)S(1)} %get-tuple-element.50), channel_id=1, source_target_pairs={{0,8},{4,12},{8,0},{12,4},{1,9},{5,13},{9,1},{13,5},{2,10},{6,14},... | collective-permute-start | bytes 688136 | tf_op jit(solution)/shard_map/ppermute | solution.py:390
  99.5 6.1 %collective-permute-start.32 = (bf16[64,1792]{1,0:T(8,128)(2,1)S(1)}, bf16[64,1792]{1,0:T(8,128)(2,1)S(1)}, u32[]{:S(2)}, u32[]{:S(2)}) collective-permute-start(bf16[64,1792]{1,0:T(8,128)(2,1)S(1)} %add.73.refs_5_), channel_id=1, source_target_pairs={{0,1},{1,0},{2,3},{3,2},{4,5},{5,4},{6,7},{7,6},{8,9},{9,8},{10,11... | collective-permute-start | bytes 688136 | tf_op jit(solution)/shard_map/ppermute | solution.py:393
  100.2 8.0 %collective-permute-start.29 = (bf16[64,1792]{1,0:T(8,128)(2,1)S(1)}, bf16[64,1792]{1,0:T(8,128)(2,1)S(1)}, u32[]{:S(2)}, u32[]{:S(2)}) collective-permute-start(bf16[64,1792]{1,0:T(8,128)(2,1)S(1)} %get-tuple-element.47), channel_id=1, source_target_pairs={{0,8},{4,12},{8,0},{12,4},{1,9},{5,13},{9,1},{13,5},{2,10},{6,14},... | collective-permute-start | bytes 688136 | tf_op jit(solution)/shard_map/ppermute | solution.py:390
  105.7 10.4 %collective-permute-start.33 = (bf16[64,1792]{1,0:T(8,128)(2,1)S(1)}, bf16[64,1792]{1,0:T(8,128)(2,1)S(1)}, u32[]{:S(2)}, u32[]{:S(2)}) collective-permute-start(bf16[64,1792]{1,0:T(8,128)(2,1)S(1)} %add.76), channel_id=1, source_target_pairs={{0,2},{1,3},{2,0},{3,1},{4,6},{5,7},{6,4},{7,5},{8,10},{9,11},{10,... | collective-permute-start | bytes 688136 | tf_op jit(solution)/shard_map/ppermute | solution.py:393
  106.3 9.9 %collective-permute-start.34 = (bf16[64,1792]{1,0:T(8,128)(2,1)S(1)}, bf16[64,1792]{1,0:T(8,128)(2,1)S(1)}, u32[]{:S(2)}, u32[]{:S(2)}) collective-permute-start(bf16[64,1792]{1,0:T(8,128)(2,1)S(1)} %get-tuple-element.51), channel_id=1, source_target_pairs={{0,1},{1,0},{2,3},{3,2},{4,5},{5,4},{6,7},{7,6},{8,9},{9,8},{10,11... | collective-permute-start | bytes 688136 | tf_op jit(solution)/shard_map/ppermute | solution.py:393

commit v16 on v14

--- a/solution.py
+++ b/solution.py
@@ -163,7 +163,7 @@
         compiler_params=pltpu.CompilerParams(vmem_limit_bytes=28 * MIB),
         name="attention",
     )(
-        cache_length,
+        in_hbm(cache_length),
         in_hbm(query_latent),
         in_hbm(query_rope),
         in_hbm(cache_latent),
@@ -255,7 +255,7 @@
         active[:, j * tile : (j + 1) * tile] = (gate_part / (1.0 + jnp.exp(-gate_part)) * up_part).astype(jnp.bfloat16)
 
 
-def activate(places, blocks, gains, gate_weight, up_weight, cores, first, before):
+def activate(places, blocks, gains, gate_weight, up_weight, cores, first, before, after):
     row_blocks, count = len(blocks), len(blocks[0])
     height, width = blocks[0][0].shape
     rows = row_blocks * height
@@ -268,7 +268,8 @@
     return pl.pallas_call(
         functools.partial(gate_kernel, row_blocks, cores, first, count, model_width),
         out_shape=kinds,
-        in_specs=[pl.BlockSpec(memory_space=pltpu.SMEM)] + [whole] * ((row_blocks + 1) * count + 2 + len(before)),
+        in_specs=[pl.BlockSpec(memory_space=pltpu.SMEM)] + [whole] * ((row_blocks + 1) * count + 2 + len(before))
+        + [pl.BlockSpec(memory_space=pl.ANY)] * len(after),
         out_specs=whole if first else [whole] * 3,
         scratch_shapes=[pltpu.VMEM((rows, count * width), jnp.bfloat16)],
         cost_estimate=pl.CostEstimate(
@@ -276,7 +277,7 @@
         ),
         compiler_params=pltpu.CompilerParams(vmem_limit_bytes=2 * rows * (count * width + 8 * hidden) + 12 * MIB),
         name="activate",
-    )(places, *[b for row in blocks for b in row], *gains, in_vmem(gate_weight), in_vmem(up_weight), *before)
+    )(places, *[b for row in blocks for b in row], *gains, in_vmem(gate_weight), in_vmem(up_weight), *before, *after)
 
 
 def down_kernel(slots, at, column_blocks, cores, places, active, row_weight, down, *refs):
@@ -423,9 +424,9 @@
         arrived = from_tp(total, low)
         terms[k ^ low].append((arrived, 0))
     up_weight = fetch(up_weight, [total])
-    down_weight = fetch(down_weight, [total])
     stream_terms = terms[0] + [(own_residual, 0)]
-    stream, stream_out = add([stream_terms, stream_terms], block_rows, gains + [gate_weight, up_weight, down_weight])
+    stream, stream_out = add([stream_terms, stream_terms], block_rows, gains + [gate_weight, up_weight])
+    down_weight = fetch(down_weight, [stream])
 
     rows_of = {0: stream}
     crossed = [from_chip(stream, b) for b in range(1, chips)]
@@ -437,7 +438,7 @@
         rows_of[k] = from_tp(source, low)
     slots = list(reversed(range(tp_count)))
     near = {k: [rows_of[k], from_core(rows_of[k])] for k in slots}
-    sums = activate(places, [near[k] for k in slots], gains[:cores], gate_weight, up_weight, cores, 0, [])
+    sums = activate(places, [near[k] for k in slots], gains[:cores], gate_weight, up_weight, cores, 0, [], [down_weight])
     far = {}
     for k in [0] + slots[:-1]:
         far[k] = []
@@ -451,7 +452,7 @@
                 value = from_chip(rows_of[k], b)
             (later,) = add([[(value, 0)]], block_rows, sums[-1:]) if k == tp_count - 1 else (value,)
             far[k] += [value, from_core(later)]
-    active = activate(places, [far[k] for k in slots], gains[cores:], gate_weight, up_weight, cores, cores, sums)
+    active = activate(places, [far[k] for k in slots], gains[cores:], gate_weight, up_weight, cores, cores, sums, [])
 
     def send_back(k, after):
         total = list(add([terms[k]], block_rows, after))

time: 113 us -> 109 us (0.965)
  waiting for transfers between devices: 46.7 us -> 42.8 us
    ppermute x11, starting transfers between devices: 13.4 us -> 15.5 us  [from_tp(): return lax.ppermute(value, 'tp', [(i, i ^ bits) for i in range(tp_count)])]
    ppermute x11, waiting for transfers between devices: 31.6 us -> 29.5 us  [from_tp(): return lax.ppermute(value, 'tp', [(i, i ^ bits) for i in range(tp_count)])]
    ppermute x8, starting transfers between devices: 11.6 us -> 9.64 us  [from_chip(): lax.ppermute(value, 'ep', [(i, (i + step) % ep_count) for i in range(ep_c...]
    ppermute x8, waiting for transfers between devices: 11.4 us -> 9.82 us  [from_chip(): lax.ppermute(value, 'ep', [(i, (i + step) % ep_count) for i in range(ep_c...]
  transfers between devices with their start and end apart: 35 -> 35, of which waited for: 18 -> 19; matrix products, arithmetic and copies ran while one was open for 0% -> 0% of each run, Pallas kernels for 13% -> 14%
where the time goes in v16:
time: 109 us
  waiting for transfers between devices  42.8 us (39%)
  Pallas kernels  36.5 us (33%)
  starting transfers between devices  28.4 us (26%)
    ppermute x11, waiting for transfers between devices, from_tp(): return lax.ppermute(value, 'tp', [(i, i ^ bits) for i in range(tp_count)])  29.5 us
    ppermute x11, starting transfers between devices, from_tp(): return lax.ppermute(value, 'tp', [(i, i ^ bits) for i in range(tp_count)])  15.5 us
    pallas_call x1, Pallas kernels, attend(): pl.pallas_call(functools.partial(attention_kernel, step_rows, pieces, ahe...  12.6 us
    pallas_call x4, Pallas kernels, fetch(): pl.pallas_call(functools.partial(fetch_kernel, parts), out_shape=pltpu.VM...  11.6 us
    ppermute x8, waiting for transfers between devices, from_chip(): lax.ppermute(value, 'ep', [(i, (i + step) % ep_count) for i in range(ep_c...  9.82 us
    ppermute x8, starting transfers between devices, from_chip(): lax.ppermute(value, 'ep', [(i, (i + step) % ep_count) for i in range(ep_c...  9.64 us
    pallas_call x2, Pallas kernels, activate(): pl.pallas_call(functools.partial(gate_kernel, row_blocks, cores, first, c...  5.52 us
    ppermute x16, waiting for transfers between devices, from_core(): return lax.ppermute(value, 'ep', [(i, i ^ 1) for i in range(ep_count)])  3.45 us
  transfers between devices with their start and end apart: 35, of which 19 were waited for; matrix products, arithmetic and copies ran while one was open for 0% of the time, Pallas kernels for 14%

profile of v16, /device:TPU:0, one launch (start us, length us, event | category | flops | bytes accessed | tf_op | source)
XLA Modules:
  0.0 109.1 jit_solution(5860939979903281915)
XLA Ops:
  0.8 12.6 %attention.1.refs_1_.refs_0_ = bf16[64,1024]{1,0:T(8,128)(2,1)S(1)} custom-call(s32[64]{0:T(128)} %lengths.1, bf16[64,8,512]{2,1,0:T(8,128)(2,1)} %q_ref.1, bf16[64,512]{1,0:T(8,128)(2,1)} %qr_ref.1, bf16[64,256,512]{2,1,0:T(8,128)(2,1)} %k_hbm.1, bf16[64,64,256]{2,1,0:T(8,128)(2,1)} %kr_hbm.1, bf16[8,512,128]{2,1,0:T(8,128)(2,1)} %up_hbm.1, ...), custom_call_target="tpu_custom_call" | custom-call | flops 4294967296 | bytes 16777216 | tf_op jit(solution)/shard_map/attention/pallas_call | solution.py:135
  13.4 0.5 collective-permute-start
  13.9 2.6 %collective-permute-start.1 = (bf16[64,1024]{1,0:T(8,128)(2,1)S(1)}, bf16[64,1024]{1,0:T(8,128)(2,1)S(1)}, u32[]{:S(2)}, u32[]{:S(2)}) collective-permute-start(bf16[64,1024]{1,0:T(8,128)(2,1)S(1)} %attention.1.refs_1_.refs_0_), channel_id=1, source_target_pairs={{0,8},{4,12},{8,0},{12,4},{1,9},{5,13},{9,1},{13,5},{2,10},{6,14},... | collective-permute-start | bytes 393224 | tf_op jit(solution)/shard_map/ppermute | solution.py:387
  16.7 2.0 %fetch.4.refs_1_.refs_4_ = bf16[1024,1792]{1,0:T(8,128)(2,1)S(1)} custom-call(bf16[1024,1792]{1,0:T(8,128)(2,1)} %refs_0_.4, bf16[64,1024]{1,0:T(8,128)(2,1)S(1)} %attention.1.refs_1_.refs_0_, f32[256,1]{1,0:T(8,128)S(1)} %copy.16.refs_2_.row_weight, bf16[64,1792]{1,0:T(8,128)(2,1)S(1)} %constant_dynamic-slice_fusion.refs_3_.refs_7_, ...), custom_call_target="tpu_custom_call" | custom-call | bytes 7340032 | tf_op jit(solution)/shard_map/fetch/pallas_call | solution.py:38
  18.8 1.8 %collective-permute-done.1.refs_0_ = bf16[64,1024]{1,0:T(8,128)(2,1)S(1)} collective-permute-done((bf16[64,1024]{1,0:T(8,128)(2,1)S(1)}, bf16[64,1024]{1,0:T(8,128)(2,1)S(1)}, u32[]{:S(2)}, u32[]{:S(2)}) %collective-permute-start.1) | collective-permute-done | bytes 131104 | tf_op jit(solution)/shard_map/ppermute | solution.py:387
  20.7 1.3 %collective-permute-done.2.refs_3_ = bf16[64,1024]{1,0:T(8,128)(2,1)S(1)} collective-permute-done((bf16[64,1024]{1,0:T(8,128)(2,1)S(1)}, bf16[64,1024]{1,0:T(8,128)(2,1)S(1)}, u32[]{:S(2)}, u32[]{:S(2)}) %collective-permute-start.2) | collective-permute-done | bytes 131104 | tf_op jit(solution)/shard_map/ppermute | solution.py:383
  22.0 1.8 %projection.1 = (bf16[64,1792]{1,0:T(8,128)(2,1)S(1)}, bf16[64,1792]{1,0:T(8,128)(2,1)S(1)}, bf16[64,1792]{1,0:T(8,128)(2,1)S(1)}, bf16[64,1792]{1,0:T(8,128)(2,1)S(1)}) custom-call(s32[8]{0:T(128)S(1)} %stack.35.refs_0_.places, bf16[64,1024]{1,0:T(8,128)(2,1)S(1)} %attention.1.refs_1_.refs_0_, bf16[64,1024]{1,0:T(8,128)(2,1)S(1)} %collective-permute-done.refs_1_, ...), custom_call_target="tpu_custom_call" | custom-call | flops 939524096 | bytes 4194304 | tf_op jit(solution)/shard_map/projection/pallas_call | solution.py:200
  23.8 1.9 %collective-permute-start.3 = (bf16[64,1792]{1,0:T(8,128)(2,1)S(1)}, bf16[64,1792]{1,0:T(8,128)(2,1)S(1)}, u32[]{:S(2)}, u32[]{:S(2)}) collective-permute-start(bf16[64,1792]{1,0:T(8,128)(2,1)S(1)} %get-tuple-element.29), channel_id=1, source_target_pairs={{0,1},{1,0},{2,3},{3,2},{4,5},{5,4},{6,7},{7,6},{8,9},{9,8},{10,11... | collective-permute-start | bytes 688136 | tf_op jit(solution)/shard_map/ppermute | solution.py:390
  25.7 3.2 %fetch.5.refs_1_.refs_12_.refs_10_ = bf16[1,7168,512]{2,1,0:T(8,128)(2,1)S(1)} custom-call(bf16[1,7168,512]{2,1,0:T(8,128)(2,1)} %refs_0_.5, bf16[64,1792]{1,0:T(8,128)(2,1)S(1)} %get-tuple-element.27.refs_1_.refs_0_.refs_4_), custom_call_target="tpu_custom_call" | custom-call | bytes 14680064 | tf_op jit(solution)/shard_map/fetch/pallas_call | solution.py:38
  29.1 2.5 %collective-permute-done.3.refs_1_ = bf16[64,1792]{1,0:T(8,128)(2,1)S(1)} collective-permute-done((bf16[64,1792]{1,0:T(8,128)(2,1)S(1)}, bf16[64,1792]{1,0:T(8,128)(2,1)S(1)}, u32[]{:S(2)}, u32[]{:S(2)}) %collective-permute-start.3) | collective-permute-done | bytes 229408 | tf_op jit(solution)/shard_map/ppermute | solution.py:390
  31.7 3.0 %collective-permute-start.4 = (bf16[64,1792]{1,0:T(8,128)(2,1)S(1)}, bf16[64,1792]{1,0:T(8,128)(2,1)S(1)}, u32[]{:S(2)}, u32[]{:S(2)}) collective-permute-start(bf16[64,1792]{1,0:T(8,128)(2,1)S(1)} %add.65), channel_id=1, source_target_pairs={{0,2},{1,3},{2,0},{3,1},{4,6},{5,7},{6,4},{7,5},{8,10},{9,11},{10,... | collective-permute-start | bytes 688136 | tf_op jit(solution)/shard_map/ppermute | solution.py:390
  34.7 1.5 %collective-permute-start.7 = (f32[1,1792]{1,0:T(1,128)S(1)}, f32[1,1792]{1,0:T(1,128)S(1)}, u32[]{:S(2)}, u32[]{:S(2)}) collective-permute-start(f32[1,1792]{1,0:T(1,128)S(1)} %reshape.7.refs_4_.refs_8_), channel_id=1, source_target_pairs={{0,8},{4,12},{8,0},{12,4},{1,9},{5,13},{9,1},{13,5},{2,10},{6,14},... | collective-permute-start | bytes 21512 | tf_op jit(solution)/shard_map/ppermute | solution.py:387
  36.2 2.1 %collective-permute-done.7.refs_10_.refs_8_ = f32[1,1792]{1,0:T(1,128)S(1)} collective-permute-done((f32[1,1792]{1,0:T(1,128)S(1)}, f32[1,1792]{1,0:T(1,128)S(1)}, u32[]{:S(2)}, u32[]{:S(2)}) %collective-permute-start.7) | collective-permute-done | bytes 7200 | tf_op jit(solution)/shard_map/ppermute | solution.py:387
  38.4 3.2 %fetch.6.refs_13_.refs_11_ = bf16[1,7168,512]{2,1,0:T(8,128)(2,1)S(1)} custom-call(bf16[1,7168,512]{2,1,0:T(8,128)(2,1)} %refs_0_.6, bf16[64,1792]{1,0:T(8,128)(2,1)S(1)} %add.66.refs_1_), custom_call_target="tpu_custom_call" | custom-call | bytes 14680064 | tf_op jit(solution)/shard_map/fetch/pallas_call | solution.py:38
  41.6 2.9 %collective-permute-done.4.refs_1_.refs_5_ = bf16[64,1792]{1,0:T(8,128)(2,1)S(1)} collective-permute-done((bf16[64,1792]{1,0:T(8,128)(2,1)S(1)}, bf16[64,1792]{1,0:T(8,128)(2,1)S(1)}, u32[]{:S(2)}, u32[]{:S(2)}) %collective-permute-start.4) | collective-permute-done | bytes 229408 | tf_op jit(solution)/shard_map/ppermute | solution.py:390
  44.5 0.8 add.67
  45.4 1.5 %collective-permute-start.10 = (bf16[64,1792]{1,0:T(8,128)(2,1)S(1)}, bf16[64,1792]{1,0:T(8,128)(2,1)S(1)}, u32[]{:S(2)}, u32[]{:S(2)}) collective-permute-start(bf16[64,1792]{1,0:T(8,128)(2,1)S(1)} %get-tuple-element.32.refs_1_.refs_6_), channel_id=1, source_target_pairs={{0,8},{4,12},{8,0},{12,4},{1,9},{5,13},{9,1},{13,5},{2,10},{6,14},... | collective-permute-start | bytes 688136 | tf_op jit(solution)/shard_map/ppermute | solution.py:387
  46.9 4.1 %collective-permute-start.15 = (bf16[64,1792]{1,0:T(8,128)(2,1)S(1)}, bf16[64,1792]{1,0:T(8,128)(2,1)S(1)}, u32[]{:S(2)}, u32[]{:S(2)}) collective-permute-start(bf16[64,1792]{1,0:T(8,128)(2,1)S(1)} %get-tuple-element.32.refs_1_.refs_6_), channel_id=1, source_target_pairs={{0,1},{1,0},{2,3},{3,2},{4,5},{5,4},{6,7},{7,6},{8,9},{9,8},{10,11... | collective-permute-start | bytes 688136 | tf_op jit(solution)/shard_map/ppermute | solution.py:390
  51.0 5.3 %collective-permute-done.9.refs_0_.refs_2_ = bf16[64,1792]{1,0:T(8,128)(2,1)S(1)} collective-permute-done((bf16[64,1792]{1,0:T(8,128)(2,1)S(1)}, bf16[64,1792]{1,0:T(8,128)(2,1)S(1)}, u32[]{:S(2)}, u32[]{:S(2)}) %collective-permute-start.9) | collective-permute-done | bytes 229408 | tf_op jit(solution)/shard_map/ppermute | solution.py:390
  56.6 0.5 collective-permute-start.14
  57.1 1.6 %collective-permute-done.15.refs_4_ = bf16[64,1792]{1,0:T(8,128)(2,1)S(1)} collective-permute-done((bf16[64,1792]{1,0:T(8,128)(2,1)S(1)}, bf16[64,1792]{1,0:T(8,128)(2,1)S(1)}, u32[]{:S(2)}, u32[]{:S(2)}) %collective-permute-start.15) | collective-permute-done | bytes 229408 | tf_op jit(solution)/shard_map/ppermute | solution.py:390
  58.7 3.9 %collective-permute-done.11.refs_0_.refs_1_ = bf16[64,1792]{1,0:T(8,128)(2,1)S(1)} collective-permute-done((bf16[64,1792]{1,0:T(8,128)(2,1)S(1)}, bf16[64,1792]{1,0:T(8,128)(2,1)S(1)}, u32[]{:S(2)}, u32[]{:S(2)}) %collective-permute-start.11) | collective-permute-done | bytes 229408 | tf_op jit(solution)/shard_map/ppermute | solution.py:390
  62.6 1.4 %collective-permute-start.12 = (bf16[64,1792]{1,0:T(8,128)(2,1)S(1)}, bf16[64,1792]{1,0:T(8,128)(2,1)S(1)}, u32[]{:S(2)}, u32[]{:S(2)}) collective-permute-start(bf16[64,1792]{1,0:T(8,128)(2,1)S(1)} %collective-permute-done.11.refs_0_.refs_1_), channel_id=1, source_target_pairs={{0,8},{4,12},{8,0},{12,4},{1,9},{5,13},{9,1},{13,5},{2,10},{6,14},... | collective-permute-start | bytes 688136 | tf_op jit(solution)/shard_map/ppermute | solution.py:387
  64.4 3.2 %fetch.7.refs_12_.down = bf16[1,512,7168]{2,1,0:T(8,128)(2,1)S(1)} custom-call(bf16[1,512,7168]{2,1,0:T(8,128)(2,1)} %refs_0_.7, bf16[64,1792]{1,0:T(8,128)(2,1)S(1)} %get-tuple-element.32.refs_1_.refs_6_), custom_call_target="tpu_custom_call" | custom-call | bytes 14680064 | tf_op jit(solution)/shard_map/fetch/pallas_call | solution.py:38
  67.7 0.5 collective-permute-start.20
  68.1 2.7 %activate.2 = (f32[256,512]{1,0:T(8,128)S(1)}, f32[256,512]{1,0:T(8,128)S(1)}, f32[256,1]{1,0:T(8,128)S(1)}) custom-call(s32[8]{0:T(128)S(1)} %stack.35.refs_0_.places, bf16[64,1792]{1,0:T(8,128)(2,1)S(1)} %collective-permute-done.11.refs_0_.refs_1_, bf16[64,1792]{1,0:T(8,128)(2,1)S(1)} %collective-permute-done.13.refs_1_, ...), custom_call_target="tpu_custom_call" | custom-call | flops 1879048192 | bytes 7340032 | tf_op jit(solution)/shard_map/activate/pallas_call | solution.py:268
  70.8 0.8 collective-permute-done.12.refs_0_
  71.8 0.4 collective-permute-start.22
  72.2 1.0 collective-permute-done.18.refs_1_
  73.5 2.8 %activate.3.active = bf16[256,512]{1,0:T(8,128)(2,1)S(1)} custom-call(s32[8]{0:T(128)S(1)} %stack.35.refs_0_.places, bf16[64,1792]{1,0:T(8,128)(2,1)S(1)} %collective-permute-done.12.refs_0_, bf16[64,1792]{1,0:T(8,128)(2,1)S(1)} %collective-permute-done.18.refs_1_, bf16[64,1792]{1,0:T(8,128)(2,1)S(1)} %collective-permute-done.19.refs_2_, ...), custom_call_target="tpu_custom_call" | custom-call | flops 1879048192 | bytes 7340032 | tf_op jit(solution)/shard_map/activate/pallas_call | solution.py:268
  76.4 2.7 %down.1 = (bf16[128,1792]{1,0:T(8,128)(2,1)S(1)}, bf16[128,1792]{1,0:T(8,128)(2,1)S(1)}, bf16[128,1792]{1,0:T(8,128)(2,1)S(1)}, bf16[128,1792]{1,0:T(8,128)(2,1)...) custom-call(s32[8]{0:T(128)S(1)} %stack.35.refs_0_.places, ...), custom_call_target="tpu_custom_call" | custom-call | flops 1879048192 | bytes 7340032 | tf_op jit(solution)/shard_map/down/pallas_call | solution.py:314
  79.3 0.3 collective-permute-start.27
  79.8 0.3 collective-permute-start.24
  80.2 0.8 collective-permute-done.25.refs_1_.refs_3_
  81.1 1.1 collective-permute-start.26
  82.2 0.9 collective-permute-start.28
  83.3 1.2 %collective-permute-start.31 = (bf16[64,1792]{1,0:T(8,128)(2,1)S(1)}, bf16[64,1792]{1,0:T(8,128)(2,1)S(1)}, u32[]{:S(2)}, u32[]{:S(2)}) collective-permute-start(bf16[64,1792]{1,0:T(8,128)(2,1)S(1)} %get-tuple-element.50), channel_id=1, source_target_pairs={{0,8},{4,12},{8,0},{12,4},{1,9},{5,13},{9,1},{13,5},{2,10},{6,14},... | collective-permute-start | bytes 688136 | tf_op jit(solution)/shard_map/ppermute | solution.py:387
  84.5 4.3 %collective-permute-done.26.refs_2_.refs_4_ = bf16[64,1792]{1,0:T(8,128)(2,1)S(1)} collective-permute-done((bf16[64,1792]{1,0:T(8,128)(2,1)S(1)}, bf16[64,1792]{1,0:T(8,128)(2,1)S(1)}, u32[]{:S(2)}, u32[]{:S(2)}) %collective-permute-start.26) | collective-permute-done | bytes 229408 | tf_op jit(solution)/shard_map/ppermute | solution.py:390
  88.8 2.0 %collective-permute-done.28.refs_1_ = bf16[64,1792]{1,0:T(8,128)(2,1)S(1)} collective-permute-done((bf16[64,1792]{1,0:T(8,128)(2,1)S(1)}, bf16[64,1792]{1,0:T(8,128)(2,1)S(1)}, u32[]{:S(2)}, u32[]{:S(2)}) %collective-permute-start.28) | collective-permute-done | bytes 229408 | tf_op jit(solution)/shard_map/ppermute | solution.py:387
  90.9 1.1 %collective-permute-start.32 = (bf16[64,1792]{1,0:T(8,128)(2,1)S(1)}, bf16[64,1792]{1,0:T(8,128)(2,1)S(1)}, u32[]{:S(2)}, u32[]{:S(2)}) collective-permute-start(bf16[64,1792]{1,0:T(8,128)(2,1)S(1)} %add.73.refs_5_), channel_id=1, source_target_pairs={{0,1},{1,0},{2,3},{3,2},{4,5},{5,4},{6,7},{7,6},{8,9},{9,8},{10,11... | collective-permute-start | bytes 688136 | tf_op jit(solution)/shard_map/ppermute | solution.py:390
  92.1 0.5 collective-permute-start.29
  92.6 3.1 %collective-permute-done.31.refs_1_ = bf16[64,1792]{1,0:T(8,128)(2,1)S(1)} collective-permute-done((bf16[64,1792]{1,0:T(8,128)(2,1)S(1)}, bf16[64,1792]{1,0:T(8,128)(2,1)S(1)}, u32[]{:S(2)}, u32[]{:S(2)}) %collective-permute-start.31) | collective-permute-done | bytes 229408 | tf_op jit(solution)/shard_map/ppermute | solution.py:387
  95.7 1.2 %collective-permute-done.32.refs_2_ = bf16[64,1792]{1,0:T(8,128)(2,1)S(1)} collective-permute-done((bf16[64,1792]{1,0:T(8,128)(2,1)S(1)}, bf16[64,1792]{1,0:T(8,128)(2,1)S(1)}, u32[]{:S(2)}, u32[]{:S(2)}) %collective-permute-start.32) | collective-permute-done | bytes 229408 | tf_op jit(solution)/shard_map/ppermute | solution.py:390
  97.0 3.1 %collective-permute-start.33 = (bf16[64,1792]{1,0:T(8,128)(2,1)S(1)}, bf16[64,1792]{1,0:T(8,128)(2,1)S(1)}, u32[]{:S(2)}, u32[]{:S(2)}) collective-permute-start(bf16[64,1792]{1,0:T(8,128)(2,1)S(1)} %add.76), channel_id=1, source_target_pairs={{0,2},{1,3},{2,0},{3,1},{4,6},{5,7},{6,4},{7,5},{8,10},{9,11},{10,... | collective-permute-start | bytes 688136 | tf_op jit(solution)/shard_map/ppermute | solution.py:390
  100.2 0.5 collective-permute-start.34
  100.7 6.9 %collective-permute-done.33.refs_2_ = bf16[64,1792]{1,0:T(8,128)(2,1)S(1)} collective-permute-done((bf16[64,1792]{1,0:T(8,128)(2,1)S(1)}, bf16[64,1792]{1,0:T(8,128)(2,1)S(1)}, u32[]{:S(2)}, u32[]{:S(2)}) %collective-permute-start.33) | collective-permute-done | bytes 229408 | tf_op jit(solution)/shard_map/ppermute | solution.py:390
  107.7 0.6 collective-permute-done.34.refs_1_
  108.3 0.7 add.78
  (61 shorter events, 3.0 us)
Async XLA Ops:
  0.6 16.0 %copy-start = (bf16[256,1792]{1,0:T(8,128)(2,1)S(1)}, bf16[256,1792]{1,0:T(8,128)(2,1)}, u32[]{:S(2)}) copy-start(bf16[256,1792]{1,0:T(8,128)(2,1)} %param.21) | copy-start | bytes 2752516
  0.8 15.7 %copy-start.3 = (f32[256,2]{0,1:T(2,128)S(1)}, f32[256,2]{0,1:T(2,128)}, u32[]{:S(2)}) copy-start(f32[256,2]{0,1:T(2,128)} %param.24) | copy-start | bytes 6148
  0.8 15.7 %copy-start.4 = (s32[256,2]{0,1:T(2,128)S(1)}, s32[256,2]{0,1:T(2,128)}, u32[]{:S(2)}) copy-start(s32[256,2]{0,1:T(2,128)} %param.23) | copy-start | bytes 6148
  0.8 15.9 %copy-start.2 = (f32[1792]{0:T(1024)S(1)}, f32[1792]{0:T(1024)}, u32[]{:S(2)}) copy-start(f32[1792]{0:T(1024)} %param.22) | copy-start | bytes 21508
  13.4 7.3 %collective-permute-start = (bf16[64,1024]{1,0:T(8,128)(2,1)S(1)}, bf16[64,1024]{1,0:T(8,128)(2,1)S(1)}, u32[]{:S(2)}, u32[]{:S(2)}) collective-permute-start(bf16[64,1024]{1,0:T(8,128)(2,1)S(1)} %attention.1.refs_1_.refs_0_), channel_id=1, source_target_pairs={{0,4},{4,0},{8,12},{12,8},{1,5},{5,1},{9,13},{13,9},{2,6},{6,2},{1... | collective-permute-start | bytes 393224 | tf_op jit(solution)/shard_map/ppermute | solution.py:383
  13.9 6.7 %collective-permute-start.1 = (bf16[64,1024]{1,0:T(8,128)(2,1)S(1)}, bf16[64,1024]{1,0:T(8,128)(2,1)S(1)}, u32[]{:S(2)}, u32[]{:S(2)}) collective-permute-start(bf16[64,1024]{1,0:T(8,128)(2,1)S(1)} %attention.1.refs_1_.refs_0_), channel_id=1, source_target_pairs={{0,8},{4,12},{8,0},{12,4},{1,9},{5,13},{9,1},{13,5},{2,10},{6,14},... | collective-permute-start | bytes 393224 | tf_op jit(solution)/shard_map/ppermute | solution.py:387
  20.6 1.4 %collective-permute-start.2 = (bf16[64,1024]{1,0:T(8,128)(2,1)S(1)}, bf16[64,1024]{1,0:T(8,128)(2,1)S(1)}, u32[]{:S(2)}, u32[]{:S(2)}) collective-permute-start(bf16[64,1024]{1,0:T(8,128)(2,1)S(1)} %add.64.refs_2_), channel_id=1, source_target_pairs={{0,4},{4,0},{8,12},{12,8},{1,5},{5,1},{9,13},{13,9},{2,6},{6,2},{1... | collective-permute-start | bytes 393224 | tf_op jit(solution)/shard_map/ppermute | solution.py:383
  23.8 7.9 %collective-permute-start.3 = (bf16[64,1792]{1,0:T(8,128)(2,1)S(1)}, bf16[64,1792]{1,0:T(8,128)(2,1)S(1)}, u32[]{:S(2)}, u32[]{:S(2)}) collective-permute-start(bf16[64,1792]{1,0:T(8,128)(2,1)S(1)} %get-tuple-element.29), channel_id=1, source_target_pairs={{0,1},{1,0},{2,3},{3,2},{4,5},{5,4},{6,7},{7,6},{8,9},{9,8},{10,11... | collective-permute-start | bytes 688136 | tf_op jit(solution)/shard_map/ppermute | solution.py:390
  28.9 12.7 %collective-permute-start.5 = (bf16[64,1792]{1,0:T(8,128)(2,1)S(1)}, bf16[64,1792]{1,0:T(8,128)(2,1)S(1)}, u32[]{:S(2)}, u32[]{:S(2)}) collective-permute-start(bf16[64,1792]{1,0:T(8,128)(2,1)S(1)} %add.66.refs_1_), channel_id=1, source_target_pairs={{0,1},{1,0},{2,3},{3,2},{4,5},{5,4},{6,7},{7,6},{8,9},{9,8},{10,11... | collective-permute-start | bytes 688136 | tf_op jit(solution)/shard_map/ppermute | solution.py:390
  31.7 12.8 %collective-permute-start.4 = (bf16[64,1792]{1,0:T(8,128)(2,1)S(1)}, bf16[64,1792]{1,0:T(8,128)(2,1)S(1)}, u32[]{:S(2)}, u32[]{:S(2)}) collective-permute-start(bf16[64,1792]{1,0:T(8,128)(2,1)S(1)} %add.65), channel_id=1, source_target_pairs={{0,2},{1,3},{2,0},{3,1},{4,6},{5,7},{6,4},{7,5},{8,10},{9,11},{10,... | collective-permute-start | bytes 688136 | tf_op jit(solution)/shard_map/ppermute | solution.py:390
  34.7 3.6 %collective-permute-start.7 = (f32[1,1792]{1,0:T(1,128)S(1)}, f32[1,1792]{1,0:T(1,128)S(1)}, u32[]{:S(2)}, u32[]{:S(2)}) collective-permute-start(f32[1,1792]{1,0:T(1,128)S(1)} %reshape.7.refs_4_.refs_8_), channel_id=1, source_target_pairs={{0,8},{4,12},{8,0},{12,4},{1,9},{5,13},{9,1},{13,5},{2,10},{6,14},... | collective-permute-start | bytes 21512 | tf_op jit(solution)/shard_map/ppermute | solution.py:387
  36.2 5.3 %collective-permute-start.6 = (f32[1,1792]{1,0:T(1,128)S(1)}, f32[1,1792]{1,0:T(1,128)S(1)}, u32[]{:S(2)}, u32[]{:S(2)}) collective-permute-start(f32[1,1792]{1,0:T(1,128)S(1)} %reshape.7.refs_4_.refs_8_), channel_id=1, source_target_pairs={{0,4},{4,0},{8,12},{12,8},{1,5},{5,1},{9,13},{13,9},{2,6},{6,2},{1... | collective-permute-start | bytes 21512 | tf_op jit(solution)/shard_map/ppermute | solution.py:383
  38.4 3.2 %collective-permute-start.8 = (f32[1,1792]{1,0:T(1,128)S(1)}, f32[1,1792]{1,0:T(1,128)S(1)}, u32[]{:S(2)}, u32[]{:S(2)}) collective-permute-start(f32[1,1792]{1,0:T(1,128)S(1)} %collective-permute-done.7.refs_10_.refs_8_), channel_id=1, source_target_pairs={{0,4},{4,0},{8,12},{12,8},{1,5},{5,1},{9,13},{13,9},{2,6},{6,2},{1... | collective-permute-start | bytes 21512 | tf_op jit(solution)/shard_map/ppermute | solution.py:383
  45.4 11.0 %collective-permute-start.9 = (bf16[64,1792]{1,0:T(8,128)(2,1)S(1)}, bf16[64,1792]{1,0:T(8,128)(2,1)S(1)}, u32[]{:S(2)}, u32[]{:S(2)}) collective-permute-start(bf16[64,1792]{1,0:T(8,128)(2,1)S(1)} %get-tuple-element.32.refs_1_.refs_6_), channel_id=1, source_target_pairs={{0,2},{1,3},{2,0},{3,1},{4,6},{5,7},{6,4},{7,5},{8,10},{9,11},{10,... | collective-permute-start | bytes 688136 | tf_op jit(solution)/shard_map/ppermute | solution.py:390
  45.4 11.0 %collective-permute-start.10 = (bf16[64,1792]{1,0:T(8,128)(2,1)S(1)}, bf16[64,1792]{1,0:T(8,128)(2,1)S(1)}, u32[]{:S(2)}, u32[]{:S(2)}) collective-permute-start(bf16[64,1792]{1,0:T(8,128)(2,1)S(1)} %get-tuple-element.32.refs_1_.refs_6_), channel_id=1, source_target_pairs={{0,8},{4,12},{8,0},{12,4},{1,9},{5,13},{9,1},{13,5},{2,10},{6,14},... | collective-permute-start | bytes 688136 | tf_op jit(solution)/shard_map/ppermute | solution.py:387
  46.9 11.8 %collective-permute-start.15 = (bf16[64,1792]{1,0:T(8,128)(2,1)S(1)}, bf16[64,1792]{1,0:T(8,128)(2,1)S(1)}, u32[]{:S(2)}, u32[]{:S(2)}) collective-permute-start(bf16[64,1792]{1,0:T(8,128)(2,1)S(1)} %get-tuple-element.32.refs_1_.refs_6_), channel_id=1, source_target_pairs={{0,1},{1,0},{2,3},{3,2},{4,5},{5,4},{6,7},{7,6},{8,9},{9,8},{10,11... | collective-permute-start | bytes 688136 | tf_op jit(solution)/shard_map/ppermute | solution.py:390
  56.4 6.2 %collective-permute-start.11 = (bf16[64,1792]{1,0:T(8,128)(2,1)S(1)}, bf16[64,1792]{1,0:T(8,128)(2,1)S(1)}, u32[]{:S(2)}, u32[]{:S(2)}) collective-permute-start(bf16[64,1792]{1,0:T(8,128)(2,1)S(1)} %add.68), channel_id=1, source_target_pairs={{0,1},{1,0},{2,3},{3,2},{4,5},{5,4},{6,7},{7,6},{8,9},{9,8},{10,11... | collective-permute-start | bytes 688136 | tf_op jit(solution)/shard_map/ppermute | solution.py:390
  56.5 6.1 %collective-permute-start.17 = (bf16[64,1792]{1,0:T(8,128)(2,1)S(1)}, bf16[64,1792]{1,0:T(8,128)(2,1)S(1)}, u32[]{:S(2)}, u32[]{:S(2)}) collective-permute-start(bf16[64,1792]{1,0:T(8,128)(2,1)S(1)} %get-tuple-element.32.refs_1_.refs_6_), channel_id=1, source_target_pairs={{0,4},{4,0},{8,12},{12,8},{1,5},{5,1},{9,13},{13,9},{2,6},{6,2},{1... | collective-permute-start | bytes 688136 | tf_op jit(solution)/shard_map/ppermute | solution.py:383
  56.6 7.5 %collective-permute-start.14 = (bf16[64,1792]{1,0:T(8,128)(2,1)S(1)}, bf16[64,1792]{1,0:T(8,128)(2,1)S(1)}, u32[]{:S(2)}, u32[]{:S(2)}) collective-permute-start(bf16[64,1792]{1,0:T(8,128)(2,1)S(1)} %collective-permute-done.9.refs_0_.refs_2_), channel_id=1, source_target_pairs={{0,4},{4,0},{8,12},{12,8},{1,5},{5,1},{9,13},{13,9},{2,6},{6,2},{1... | collective-permute-start | bytes 688136 | tf_op jit(solution)/shard_map/ppermute | solution.py:383
  58.7 8.9 %collective-permute-start.16 = (bf16[64,1792]{1,0:T(8,128)(2,1)S(1)}, bf16[64,1792]{1,0:T(8,128)(2,1)S(1)}, u32[]{:S(2)}, u32[]{:S(2)}) collective-permute-start(bf16[64,1792]{1,0:T(8,128)(2,1)S(1)} %collective-permute-done.15.refs_4_), channel_id=1, source_target_pairs={{0,4},{4,0},{8,12},{12,8},{1,5},{5,1},{9,13},{13,9},{2,6},{6,2},{1... | collective-permute-start | bytes 688136 | tf_op jit(solution)/shard_map/ppermute | solution.py:383
  58.7 9.0 %collective-permute-start.19 = (bf16[64,1792]{1,0:T(8,128)(2,1)S(1)}, bf16[64,1792]{1,0:T(8,128)(2,1)S(1)}, u32[]{:S(2)}, u32[]{:S(2)}) collective-permute-start(bf16[64,1792]{1,0:T(8,128)(2,1)S(1)} %collective-permute-done.9.refs_0_.refs_2_), channel_id=1, source_target_pairs={{0,8},{4,12},{8,0},{12,4},{1,9},{5,13},{9,1},{13,5},{2,10},{6,14},... | collective-permute-start | bytes 688136 | tf_op jit(solution)/shard_map/ppermute | solution.py:387
  62.6 5.5 %collective-permute-start.13 = (bf16[64,1792]{1,0:T(8,128)(2,1)S(1)}, bf16[64,1792]{1,0:T(8,128)(2,1)S(1)}, u32[]{:S(2)}, u32[]{:S(2)}) collective-permute-start(bf16[64,1792]{1,0:T(8,128)(2,1)S(1)} %collective-permute-done.11.refs_0_.refs_1_), channel_id=1, source_target_pairs={{0,4},{4,0},{8,12},{12,8},{1,5},{5,1},{9,13},{13,9},{2,6},{6,2},{1... | collective-permute-start | bytes 688136 | tf_op jit(solution)/shard_map/ppermute | solution.py:383
  62.6 9.0 %collective-permute-start.12 = (bf16[64,1792]{1,0:T(8,128)(2,1)S(1)}, bf16[64,1792]{1,0:T(8,128)(2,1)S(1)}, u32[]{:S(2)}, u32[]{:S(2)}) collective-permute-start(bf16[64,1792]{1,0:T(8,128)(2,1)S(1)} %collective-permute-done.11.refs_0_.refs_1_), channel_id=1, source_target_pairs={{0,8},{4,12},{8,0},{12,4},{1,9},{5,13},{9,1},{13,5},{2,10},{6,14},... | collective-permute-start | bytes 688136 | tf_op jit(solution)/shard_map/ppermute | solution.py:387
  64.0 7.8 %collective-permute-start.21 = (bf16[64,1792]{1,0:T(8,128)(2,1)S(1)}, bf16[64,1792]{1,0:T(8,128)(2,1)S(1)}, u32[]{:S(2)}, u32[]{:S(2)}) collective-permute-start(bf16[64,1792]{1,0:T(8,128)(2,1)S(1)} %add.70), channel_id=1, source_target_pairs={{0,1},{1,0},{2,3},{3,2},{4,5},{5,4},{6,7},{7,6},{8,9},{9,8},{10,11... | collective-permute-start | bytes 688136 | tf_op jit(solution)/shard_map/ppermute | solution.py:390
  67.6 4.7 %collective-permute-start.23 = (bf16[64,1792]{1,0:T(8,128)(2,1)S(1)}, bf16[64,1792]{1,0:T(8,128)(2,1)S(1)}, u32[]{:S(2)}, u32[]{:S(2)}) collective-permute-start(bf16[64,1792]{1,0:T(8,128)(2,1)S(1)} %collective-permute-done.10.refs_1_.refs_0_.refs_6_), channel_id=1, source_target_pairs={{0,4},{4,0},{8,12},{12,8},{1,5},{5,1},{9,13},{13,9},{2,6},{6,2},{1... | collective-permute-start | bytes 688136 | tf_op jit(solution)/shard_map/ppermute | solution.py:383
  67.7 4.6 %collective-permute-start.20 = (bf16[64,1792]{1,0:T(8,128)(2,1)S(1)}, bf16[64,1792]{1,0:T(8,128)(2,1)S(1)}, u32[]{:S(2)}, u32[]{:S(2)}) collective-permute-start(bf16[64,1792]{1,0:T(8,128)(2,1)S(1)} %collective-permute-done.19.refs_2_), channel_id=1, source_target_pairs={{0,4},{4,0},{8,12},{12,8},{1,5},{5,1},{9,13},{13,9},{2,6},{6,2},{1... | collective-permute-start | bytes 688136 | tf_op jit(solution)/shard_map/ppermute | solution.py:383
  71.6 1.6 %collective-permute-start.18 = (bf16[64,1792]{1,0:T(8,128)(2,1)S(1)}, bf16[64,1792]{1,0:T(8,128)(2,1)S(1)}, u32[]{:S(2)}, u32[]{:S(2)}) collective-permute-start(bf16[64,1792]{1,0:T(8,128)(2,1)S(1)} %add.69), channel_id=1, source_target_pairs={{0,4},{4,0},{8,12},{12,8},{1,5},{5,1},{9,13},{13,9},{2,6},{6,2},{1... | collective-permute-start | bytes 688136 | tf_op jit(solution)/shard_map/ppermute | solution.py:383
  71.8 1.7 %collective-permute-start.22 = (bf16[64,1792]{1,0:T(8,128)(2,1)S(1)}, bf16[64,1792]{1,0:T(8,128)(2,1)S(1)}, u32[]{:S(2)}, u32[]{:S(2)}) collective-permute-start(bf16[64,1792]{1,0:T(8,128)(2,1)S(1)} %collective-permute-done.21.refs_4_), channel_id=1, source_target_pairs={{0,4},{4,0},{8,12},{12,8},{1,5},{5,1},{9,13},{13,9},{2,6},{6,2},{1... | collective-permute-start | bytes 688136 | tf_op jit(solution)/shard_map/ppermute | solution.py:383
  76.4 32.7 %copy-start.1 = (bf16[256,1792]{1,0:T(8,128)(2,1)S(1)}, bf16[256,1792]{1,0:T(8,128)(2,1)}, u32[]{:S(2)}) copy-start(bf16[256,1792]{1,0:T(8,128)(2,1)} %param.21) | copy-start | bytes 2752516
  79.1 1.9 %collective-permute-start.25 = (bf16[128,1792]{1,0:T(8,128)(2,1)S(1)}, bf16[128,1792]{1,0:T(8,128)(2,1)S(1)}, u32[]{:S(2)}, u32[]{:S(2)}) collective-permute-start(bf16[128,1792]{1,0:T(8,128)(2,1)S(1)} %get-tuple-element.39), channel_id=1, source_target_pairs={{0,4},{4,0},{8,12},{12,8},{1,5},{5,1},{9,13},{13,9},{2,6},{6,2},{1... | collective-permute-start | bytes 1376264 | tf_op jit(solution)/shard_map/ppermute | solution.py:383
  79.3 2.8 %collective-permute-start.27 = (bf16[128,1792]{1,0:T(8,128)(2,1)S(1)}, bf16[128,1792]{1,0:T(8,128)(2,1)S(1)}, u32[]{:S(2)}, u32[]{:S(2)}) collective-permute-start(bf16[128,1792]{1,0:T(8,128)(2,1)S(1)} %get-tuple-element.42), channel_id=1, source_target_pairs={{0,4},{4,0},{8,12},{12,8},{1,5},{5,1},{9,13},{13,9},{2,6},{6,2},{1... | collective-permute-start | bytes 1376264 | tf_op jit(solution)/shard_map/ppermute | solution.py:383
  79.7 3.5 %collective-permute-start.30 = (bf16[128,1792]{1,0:T(8,128)(2,1)S(1)}, bf16[128,1792]{1,0:T(8,128)(2,1)S(1)}, u32[]{:S(2)}, u32[]{:S(2)}) collective-permute-start(bf16[128,1792]{1,0:T(8,128)(2,1)S(1)} %get-tuple-element.48), channel_id=1, source_target_pairs={{0,4},{4,0},{8,12},{12,8},{1,5},{5,1},{9,13},{13,9},{2,6},{6,2},{1... | collective-permute-start | bytes 1376264 | tf_op jit(solution)/shard_map/ppermute | solution.py:383
  79.8 12.1 %collective-permute-start.24 = (bf16[128,1792]{1,0:T(8,128)(2,1)S(1)}, bf16[128,1792]{1,0:T(8,128)(2,1)S(1)}, u32[]{:S(2)}, u32[]{:S(2)}) collective-permute-start(bf16[128,1792]{1,0:T(8,128)(2,1)S(1)} %get-tuple-element.37), channel_id=1, source_target_pairs={{0,4},{4,0},{8,12},{12,8},{1,5},{5,1},{9,13},{13,9},{2,6},{6,2},{1... | collective-permute-start | bytes 1376264 | tf_op jit(solution)/shard_map/ppermute | solution.py:383
  81.1 7.8 %collective-permute-start.26 = (bf16[64,1792]{1,0:T(8,128)(2,1)S(1)}, bf16[64,1792]{1,0:T(8,128)(2,1)S(1)}, u32[]{:S(2)}, u32[]{:S(2)}) collective-permute-start(bf16[64,1792]{1,0:T(8,128)(2,1)S(1)} %get-tuple-element.40), channel_id=1, source_target_pairs={{0,1},{1,0},{2,3},{3,2},{4,5},{5,4},{6,7},{7,6},{8,9},{9,8},{10,11... | collective-permute-start | bytes 688136 | tf_op jit(solution)/shard_map/ppermute | solution.py:390
  82.2 8.5 %collective-permute-start.28 = (bf16[64,1792]{1,0:T(8,128)(2,1)S(1)}, bf16[64,1792]{1,0:T(8,128)(2,1)S(1)}, u32[]{:S(2)}, u32[]{:S(2)}) collective-permute-start(bf16[64,1792]{1,0:T(8,128)(2,1)S(1)} %get-tuple-element.44), channel_id=1, source_target_pairs={{0,8},{4,12},{8,0},{12,4},{1,9},{5,13},{9,1},{13,5},{2,10},{6,14},... | collective-permute-start | bytes 688136 | tf_op jit(solution)/shard_map/ppermute | solution.py:387
  83.3 12.4 %collective-permute-start.31 = (bf16[64,1792]{1,0:T(8,128)(2,1)S(1)}, bf16[64,1792]{1,0:T(8,128)(2,1)S(1)}, u32[]{:S(2)}, u32[]{:S(2)}) collective-permute-start(bf16[64,1792]{1,0:T(8,128)(2,1)S(1)} %get-tuple-element.50), channel_id=1, source_target_pairs={{0,8},{4,12},{8,0},{12,4},{1,9},{5,13},{9,1},{13,5},{2,10},{6,14},... | collective-permute-start | bytes 688136 | tf_op jit(solution)/shard_map/ppermute | solution.py:387
  90.9 6.1 %collective-permute-start.32 = (bf16[64,1792]{1,0:T(8,128)(2,1)S(1)}, bf16[64,1792]{1,0:T(8,128)(2,1)S(1)}, u32[]{:S(2)}, u32[]{:S(2)}) collective-permute-start(bf16[64,1792]{1,0:T(8,128)(2,1)S(1)} %add.73.refs_5_), channel_id=1, source_target_pairs={{0,1},{1,0},{2,3},{3,2},{4,5},{5,4},{6,7},{7,6},{8,9},{9,8},{10,11... | collective-permute-start | bytes 688136 | tf_op jit(solution)/shard_map/ppermute | solution.py:390
  92.1 8.6 %collective-permute-start.29 = (bf16[64,1792]{1,0:T(8,128)(2,1)S(1)}, bf16[64,1792]{1,0:T(8,128)(2,1)S(1)}, u32[]{:S(2)}, u32[]{:S(2)}) collective-permute-start(bf16[64,1792]{1,0:T(8,128)(2,1)S(1)} %get-tuple-element.46), channel_id=1, source_target_pairs={{0,8},{4,12},{8,0},{12,4},{1,9},{5,13},{9,1},{13,5},{2,10},{6,14},... | collective-permute-start | bytes 688136 | tf_op jit(solution)/shard_map/ppermute | solution.py:387
  97.0 10.6 %collective-permute-start.33 = (bf16[64,1792]{1,0:T(8,128)(2,1)S(1)}, bf16[64,1792]{1,0:T(8,128)(2,1)S(1)}, u32[]{:S(2)}, u32[]{:S(2)}) collective-permute-start(bf16[64,1792]{1,0:T(8,128)(2,1)S(1)} %add.76), channel_id=1, source_target_pairs={{0,2},{1,3},{2,0},{3,1},{4,6},{5,7},{6,4},{7,5},{8,10},{9,11},{10,... | collective-permute-start | bytes 688136 | tf_op jit(solution)/shard_map/ppermute | solution.py:390
  100.2 8.2 %collective-permute-start.34 = (bf16[64,1792]{1,0:T(8,128)(2,1)S(1)}, bf16[64,1792]{1,0:T(8,128)(2,1)S(1)}, u32[]{:S(2)}, u32[]{:S(2)}) collective-permute-start(bf16[64,1792]{1,0:T(8,128)(2,1)S(1)} %get-tuple-element.51), channel_id=1, source_target_pairs={{0,1},{1,0},{2,3},{3,2},{4,5},{5,4},{6,7},{7,6},{8,9},{9,8},{10,11... | collective-permute-start | bytes 688136 | tf_op jit(solution)/shard_map/ppermute | solution.py:390

commit v17 on v16

--- a/solution.py
+++ b/solution.py
@@ -423,9 +423,9 @@
         low = k & -k
         arrived = from_tp(total, low)
         terms[k ^ low].append((arrived, 0))
-    up_weight = fetch(up_weight, [total])
     stream_terms = terms[0] + [(own_residual, 0)]
-    stream, stream_out = add([stream_terms, stream_terms], block_rows, gains + [gate_weight, up_weight])
+    stream, stream_out = add([stream_terms, stream_terms], block_rows, gains + [gate_weight])
+    up_weight = fetch(up_weight, [stream])
     down_weight = fetch(down_weight, [stream])
 
     rows_of = {0: stream}
@@ -434,7 +434,7 @@
         low = k & -k
         source = rows_of[k ^ low]
         if k == tp_count - 1:
-            (source,) = add([[(source, 0)]], block_rows, crossed)
+            (source,) = add([[(source, 0)]], block_rows, crossed + [up_weight])
         rows_of[k] = from_tp(source, low)
     slots = list(reversed(range(tp_count)))
     near = {k: [rows_of[k], from_core(rows_of[k])] for k in slots}

time: 109 us -> 109 us (level)
  waiting for transfers between devices: 42.8 us -> 39.7 us
  starting transfers between devices: 28.4 us -> 31.4 us
    ppermute x11, waiting for transfers between devices: 29.5 us -> 26.5 us  [from_tp(): return lax.ppermute(value, 'tp', [(i, i ^ bits) for i in range(tp_count)])]
    ppermute x11, starting transfers between devices: 15.5 us -> 17.3 us  [from_tp(): return lax.ppermute(value, 'tp', [(i, i ^ bits) for i in range(tp_count)])]
    ppermute x8, waiting for transfers between devices: 9.82 us -> 8.55 us  [from_chip(): lax.ppermute(value, 'ep', [(i, (i + step) % ep_count) for i in range(ep_c...]
    ppermute x8, starting transfers between devices: 9.64 us -> 10.9 us  [from_chip(): lax.ppermute(value, 'ep', [(i, (i + step) % ep_count) for i in range(ep_c...]
    ppermute x16, waiting for transfers between devices: 3.45 us -> 4.61 us  [from_core(): return lax.ppermute(value, 'ep', [(i, i ^ 1) for i in range(ep_count)])]
  transfers between devices with their start and end apart: 35 -> 35, of which waited for: 19 -> 20; matrix products, arithmetic and copies ran while one was open for 0% -> 0% of each run, Pallas kernels for 14% -> 14%
where the time goes in v17:
time: 109 us
  waiting for transfers between devices  39.7 us (36%)
  Pallas kernels  36.5 us (33%)
  starting transfers between devices  31.4 us (29%)
    ppermute x11, waiting for transfers between devices, from_tp(): return lax.ppermute(value, 'tp', [(i, i ^ bits) for i in range(tp_count)])  26.5 us
    ppermute x11, starting transfers between devices, from_tp(): return lax.ppermute(value, 'tp', [(i, i ^ bits) for i in range(tp_count)])  17.3 us
    pallas_call x1, Pallas kernels, attend(): pl.pallas_call(functools.partial(attention_kernel, step_rows, pieces, ahe...  12.6 us
    pallas_call x4, Pallas kernels, fetch(): pl.pallas_call(functools.partial(fetch_kernel, parts), out_shape=pltpu.VM...  11.6 us
    ppermute x8, starting transfers between devices, from_chip(): lax.ppermute(value, 'ep', [(i, (i + step) % ep_count) for i in range(ep_c...  10.9 us
    ppermute x8, waiting for transfers between devices, from_chip(): lax.ppermute(value, 'ep', [(i, (i + step) % ep_count) for i in range(ep_c...  8.55 us
    pallas_call x2, Pallas kernels, activate(): pl.pallas_call(functools.partial(gate_kernel, row_blocks, cores, first, c...  5.52 us
    ppermute x16, waiting for transfers between devices, from_core(): return lax.ppermute(value, 'ep', [(i, i ^ 1) for i in range(ep_count)])  4.61 us
  transfers between devices with their start and end apart: 35, of which 20 were waited for; matrix products, arithmetic and copies ran while one was open for 0% of the time, Pallas kernels for 14%

profile of v17, /device:TPU:0, one launch (start us, length us, event | category | flops | bytes accessed | tf_op | source)
XLA Modules:
  0.0 109.0 jit_solution(12066085628569308381)
XLA Ops:
  0.8 12.6 %attention.1.refs_1_.refs_0_ = bf16[64,1024]{1,0:T(8,128)(2,1)S(1)} custom-call(s32[64]{0:T(128)} %lengths.1, bf16[64,8,512]{2,1,0:T(8,128)(2,1)} %q_ref.1, bf16[64,512]{1,0:T(8,128)(2,1)} %qr_ref.1, bf16[64,256,512]{2,1,0:T(8,128)(2,1)} %k_hbm.1, bf16[64,64,256]{2,1,0:T(8,128)(2,1)} %kr_hbm.1, bf16[8,512,128]{2,1,0:T(8,128)(2,1)} %up_hbm.1, ...), custom_call_target="tpu_custom_call" | custom-call | flops 4294967296 | bytes 16777216 | tf_op jit(solution)/shard_map/attention/pallas_call | solution.py:135
  13.4 0.5 collective-permute-start
  13.9 2.6 %collective-permute-start.1 = (bf16[64,1024]{1,0:T(8,128)(2,1)S(1)}, bf16[64,1024]{1,0:T(8,128)(2,1)S(1)}, u32[]{:S(2)}, u32[]{:S(2)}) collective-permute-start(bf16[64,1024]{1,0:T(8,128)(2,1)S(1)} %attention.1.refs_1_.refs_0_), channel_id=1, source_target_pairs={{0,8},{4,12},{8,0},{12,4},{1,9},{5,13},{9,1},{13,5},{2,10},{6,14},... | collective-permute-start | bytes 393224 | tf_op jit(solution)/shard_map/ppermute | solution.py:387
  16.7 2.0 %fetch.4.refs_1_.refs_4_ = bf16[1024,1792]{1,0:T(8,128)(2,1)S(1)} custom-call(bf16[1024,1792]{1,0:T(8,128)(2,1)} %refs_0_.4, bf16[64,1024]{1,0:T(8,128)(2,1)S(1)} %attention.1.refs_1_.refs_0_, f32[256,1]{1,0:T(8,128)S(1)} %copy.16.refs_2_.row_weight, bf16[64,1792]{1,0:T(8,128)(2,1)S(1)} %constant_dynamic-slice_fusion.refs_3_.refs_7_, ...), custom_call_target="tpu_custom_call" | custom-call | bytes 7340032 | tf_op jit(solution)/shard_map/fetch/pallas_call | solution.py:38
  18.8 1.8 %collective-permute-done.1.refs_0_ = bf16[64,1024]{1,0:T(8,128)(2,1)S(1)} collective-permute-done((bf16[64,1024]{1,0:T(8,128)(2,1)S(1)}, bf16[64,1024]{1,0:T(8,128)(2,1)S(1)}, u32[]{:S(2)}, u32[]{:S(2)}) %collective-permute-start.1) | collective-permute-done | bytes 131104 | tf_op jit(solution)/shard_map/ppermute | solution.py:387
  20.7 1.3 %collective-permute-done.2.refs_3_ = bf16[64,1024]{1,0:T(8,128)(2,1)S(1)} collective-permute-done((bf16[64,1024]{1,0:T(8,128)(2,1)S(1)}, bf16[64,1024]{1,0:T(8,128)(2,1)S(1)}, u32[]{:S(2)}, u32[]{:S(2)}) %collective-permute-start.2) | collective-permute-done | bytes 131104 | tf_op jit(solution)/shard_map/ppermute | solution.py:383
  22.0 1.8 %projection.1 = (bf16[64,1792]{1,0:T(8,128)(2,1)S(1)}, bf16[64,1792]{1,0:T(8,128)(2,1)S(1)}, bf16[64,1792]{1,0:T(8,128)(2,1)S(1)}, bf16[64,1792]{1,0:T(8,128)(2,1)S(1)}) custom-call(s32[8]{0:T(128)S(1)} %stack.35.refs_0_.places, bf16[64,1024]{1,0:T(8,128)(2,1)S(1)} %attention.1.refs_1_.refs_0_, bf16[64,1024]{1,0:T(8,128)(2,1)S(1)} %collective-permute-done.refs_1_, ...), custom_call_target="tpu_custom_call" | custom-call | flops 939524096 | bytes 4194304 | tf_op jit(solution)/shard_map/projection/pallas_call | solution.py:200
  23.8 1.9 %collective-permute-start.3 = (bf16[64,1792]{1,0:T(8,128)(2,1)S(1)}, bf16[64,1792]{1,0:T(8,128)(2,1)S(1)}, u32[]{:S(2)}, u32[]{:S(2)}) collective-permute-start(bf16[64,1792]{1,0:T(8,128)(2,1)S(1)} %get-tuple-element.29), channel_id=1, source_target_pairs={{0,1},{1,0},{2,3},{3,2},{4,5},{5,4},{6,7},{7,6},{8,9},{9,8},{10,11... | collective-permute-start | bytes 688136 | tf_op jit(solution)/shard_map/ppermute | solution.py:390
  25.7 3.2 %fetch.5.refs_1_.refs_12_.refs_10_ = bf16[1,7168,512]{2,1,0:T(8,128)(2,1)S(1)} custom-call(bf16[1,7168,512]{2,1,0:T(8,128)(2,1)} %refs_0_.5, bf16[64,1792]{1,0:T(8,128)(2,1)S(1)} %get-tuple-element.27.refs_1_.refs_0_.refs_4_), custom_call_target="tpu_custom_call" | custom-call | bytes 14680064 | tf_op jit(solution)/shard_map/fetch/pallas_call | solution.py:38
  29.1 2.5 %collective-permute-done.3.refs_1_ = bf16[64,1792]{1,0:T(8,128)(2,1)S(1)} collective-permute-done((bf16[64,1792]{1,0:T(8,128)(2,1)S(1)}, bf16[64,1792]{1,0:T(8,128)(2,1)S(1)}, u32[]{:S(2)}, u32[]{:S(2)}) %collective-permute-start.3) | collective-permute-done | bytes 229408 | tf_op jit(solution)/shard_map/ppermute | solution.py:390
  31.7 3.0 %collective-permute-start.4 = (bf16[64,1792]{1,0:T(8,128)(2,1)S(1)}, bf16[64,1792]{1,0:T(8,128)(2,1)S(1)}, u32[]{:S(2)}, u32[]{:S(2)}) collective-permute-start(bf16[64,1792]{1,0:T(8,128)(2,1)S(1)} %add.65), channel_id=1, source_target_pairs={{0,2},{1,3},{2,0},{3,1},{4,6},{5,7},{6,4},{7,5},{8,10},{9,11},{10,... | collective-permute-start | bytes 688136 | tf_op jit(solution)/shard_map/ppermute | solution.py:390
  34.7 1.5 %collective-permute-start.7 = (f32[1,1792]{1,0:T(1,128)S(1)}, f32[1,1792]{1,0:T(1,128)S(1)}, u32[]{:S(2)}, u32[]{:S(2)}) collective-permute-start(f32[1,1792]{1,0:T(1,128)S(1)} %reshape.7.refs_4_.refs_8_), channel_id=1, source_target_pairs={{0,8},{4,12},{8,0},{12,4},{1,9},{5,13},{9,1},{13,5},{2,10},{6,14},... | collective-permute-start | bytes 21512 | tf_op jit(solution)/shard_map/ppermute | solution.py:387
  36.2 2.1 %collective-permute-done.7.refs_10_.refs_8_ = f32[1,1792]{1,0:T(1,128)S(1)} collective-permute-done((f32[1,1792]{1,0:T(1,128)S(1)}, f32[1,1792]{1,0:T(1,128)S(1)}, u32[]{:S(2)}, u32[]{:S(2)}) %collective-permute-start.7) | collective-permute-done | bytes 7200 | tf_op jit(solution)/shard_map/ppermute | solution.py:387
  38.4 1.2 %collective-permute-done.8.refs_11_.refs_9_ = f32[1,1792]{1,0:T(1,128)S(1)} collective-permute-done((f32[1,1792]{1,0:T(1,128)S(1)}, f32[1,1792]{1,0:T(1,128)S(1)}, u32[]{:S(2)}, u32[]{:S(2)}) %collective-permute-start.8) | collective-permute-done | bytes 7200 | tf_op jit(solution)/shard_map/ppermute | solution.py:383
  39.5 1.1 collective-permute-done.5.refs_2_.refs_6_
  40.6 3.9 %collective-permute-done.4.refs_1_.refs_5_ = bf16[64,1792]{1,0:T(8,128)(2,1)S(1)} collective-permute-done((bf16[64,1792]{1,0:T(8,128)(2,1)S(1)}, bf16[64,1792]{1,0:T(8,128)(2,1)S(1)}, u32[]{:S(2)}, u32[]{:S(2)}) %collective-permute-start.4) | collective-permute-done | bytes 229408 | tf_op jit(solution)/shard_map/ppermute | solution.py:390
  44.5 0.8 add.67
  45.4 1.5 %collective-permute-start.10 = (bf16[64,1792]{1,0:T(8,128)(2,1)S(1)}, bf16[64,1792]{1,0:T(8,128)(2,1)S(1)}, u32[]{:S(2)}, u32[]{:S(2)}) collective-permute-start(bf16[64,1792]{1,0:T(8,128)(2,1)S(1)} %get-tuple-element.32.refs_1_.refs_6_), channel_id=1, source_target_pairs={{0,8},{4,12},{8,0},{12,4},{1,9},{5,13},{9,1},{13,5},{2,10},{6,14},... | collective-permute-start | bytes 688136 | tf_op jit(solution)/shard_map/ppermute | solution.py:387
  46.9 4.1 %collective-permute-start.15 = (bf16[64,1792]{1,0:T(8,128)(2,1)S(1)}, bf16[64,1792]{1,0:T(8,128)(2,1)S(1)}, u32[]{:S(2)}, u32[]{:S(2)}) collective-permute-start(bf16[64,1792]{1,0:T(8,128)(2,1)S(1)} %get-tuple-element.32.refs_1_.refs_6_), channel_id=1, source_target_pairs={{0,1},{1,0},{2,3},{3,2},{4,5},{5,4},{6,7},{7,6},{8,9},{9,8},{10,11... | collective-permute-start | bytes 688136 | tf_op jit(solution)/shard_map/ppermute | solution.py:390
  51.0 3.2 %fetch.6.refs_2_.refs_11_ = bf16[1,7168,512]{2,1,0:T(8,128)(2,1)S(1)} custom-call(bf16[1,7168,512]{2,1,0:T(8,128)(2,1)} %refs_0_.6, bf16[64,1792]{1,0:T(8,128)(2,1)S(1)} %get-tuple-element.32.refs_1_.refs_6_), custom_call_target="tpu_custom_call" | custom-call | bytes 14680064 | tf_op jit(solution)/shard_map/fetch/pallas_call | solution.py:38
  54.2 1.4 %collective-permute-done.9.refs_0_.refs_2_ = bf16[64,1792]{1,0:T(8,128)(2,1)S(1)} collective-permute-done((bf16[64,1792]{1,0:T(8,128)(2,1)S(1)}, bf16[64,1792]{1,0:T(8,128)(2,1)S(1)}, u32[]{:S(2)}, u32[]{:S(2)}) %collective-permute-start.9) | collective-permute-done | bytes 229408 | tf_op jit(solution)/shard_map/ppermute | solution.py:390
  56.2 0.5 collective-permute-start.14
  56.7 0.8 collective-permute-done.15.refs_4_
  57.5 0.7 collective-permute-start.19
  58.2 3.8 %collective-permute-done.11.refs_0_.refs_1_ = bf16[64,1792]{1,0:T(8,128)(2,1)S(1)} collective-permute-done((bf16[64,1792]{1,0:T(8,128)(2,1)S(1)}, bf16[64,1792]{1,0:T(8,128)(2,1)S(1)}, u32[]{:S(2)}, u32[]{:S(2)}) %collective-permute-start.11) | collective-permute-done | bytes 229408 | tf_op jit(solution)/shard_map/ppermute | solution.py:390
  62.0 1.3 %collective-permute-start.12 = (bf16[64,1792]{1,0:T(8,128)(2,1)S(1)}, bf16[64,1792]{1,0:T(8,128)(2,1)S(1)}, u32[]{:S(2)}, u32[]{:S(2)}) collective-permute-start(bf16[64,1792]{1,0:T(8,128)(2,1)S(1)} %collective-permute-done.11.refs_0_.refs_1_), channel_id=1, source_target_pairs={{0,8},{4,12},{8,0},{12,4},{1,9},{5,13},{9,1},{13,5},{2,10},{6,14},... | collective-permute-start | bytes 688136 | tf_op jit(solution)/shard_map/ppermute | solution.py:387
  63.3 1.0 collective-permute-start.21
  64.4 3.2 %fetch.7.refs_12_.down = bf16[1,512,7168]{2,1,0:T(8,128)(2,1)S(1)} custom-call(bf16[1,512,7168]{2,1,0:T(8,128)(2,1)} %refs_0_.7, bf16[64,1792]{1,0:T(8,128)(2,1)S(1)} %get-tuple-element.32.refs_1_.refs_6_), custom_call_target="tpu_custom_call" | custom-call | bytes 14680064 | tf_op jit(solution)/shard_map/fetch/pallas_call | solution.py:38
  67.7 0.5 collective-permute-start.20
  68.2 2.7 %activate.2 = (f32[256,512]{1,0:T(8,128)S(1)}, f32[256,512]{1,0:T(8,128)S(1)}, f32[256,1]{1,0:T(8,128)S(1)}) custom-call(s32[8]{0:T(128)S(1)} %stack.35.refs_0_.places, bf16[64,1792]{1,0:T(8,128)(2,1)S(1)} %collective-permute-done.11.refs_0_.refs_1_, bf16[64,1792]{1,0:T(8,128)(2,1)S(1)} %collective-permute-done.13.refs_1_, ...), custom_call_target="tpu_custom_call" | custom-call | flops 1879048192 | bytes 7340032 | tf_op jit(solution)/shard_map/activate/pallas_call | solution.py:268
  71.5 1.0 collective-permute-done.18.refs_1_
  72.8 2.9 %activate.3.active = bf16[256,512]{1,0:T(8,128)(2,1)S(1)} custom-call(s32[8]{0:T(128)S(1)} %stack.35.refs_0_.places, bf16[64,1792]{1,0:T(8,128)(2,1)S(1)} %collective-permute-done.12.refs_0_, bf16[64,1792]{1,0:T(8,128)(2,1)S(1)} %collective-permute-done.18.refs_1_, bf16[64,1792]{1,0:T(8,128)(2,1)S(1)} %collective-permute-done.19.refs_2_, ...), custom_call_target="tpu_custom_call" | custom-call | flops 1879048192 | bytes 7340032 | tf_op jit(solution)/shard_map/activate/pallas_call | solution.py:268
  75.7 2.7 %down.1 = (bf16[128,1792]{1,0:T(8,128)(2,1)S(1)}, bf16[128,1792]{1,0:T(8,128)(2,1)S(1)}, bf16[128,1792]{1,0:T(8,128)(2,1)S(1)}, bf16[128,1792]{1,0:T(8,128)(2,1)...) custom-call(s32[8]{0:T(128)S(1)} %stack.35.refs_0_.places, ...), custom_call_target="tpu_custom_call" | custom-call | flops 1879048192 | bytes 7340032 | tf_op jit(solution)/shard_map/down/pallas_call | solution.py:314
  79.5 0.8 collective-permute-done.25.refs_1_.refs_3_
  80.4 1.1 %collective-permute-start.26 = (bf16[64,1792]{1,0:T(8,128)(2,1)S(1)}, bf16[64,1792]{1,0:T(8,128)(2,1)S(1)}, u32[]{:S(2)}, u32[]{:S(2)}) collective-permute-start(bf16[64,1792]{1,0:T(8,128)(2,1)S(1)} %get-tuple-element.40), channel_id=1, source_target_pairs={{0,1},{1,0},{2,3},{3,2},{4,5},{5,4},{6,7},{7,6},{8,9},{9,8},{10,11... | collective-permute-start | bytes 688136 | tf_op jit(solution)/shard_map/ppermute | solution.py:390
  81.6 0.9 collective-permute-start.28
  82.6 1.3 %collective-permute-start.31 = (bf16[64,1792]{1,0:T(8,128)(2,1)S(1)}, bf16[64,1792]{1,0:T(8,128)(2,1)S(1)}, u32[]{:S(2)}, u32[]{:S(2)}) collective-permute-start(bf16[64,1792]{1,0:T(8,128)(2,1)S(1)} %get-tuple-element.50), channel_id=1, source_target_pairs={{0,8},{4,12},{8,0},{12,4},{1,9},{5,13},{9,1},{13,5},{2,10},{6,14},... | collective-permute-start | bytes 688136 | tf_op jit(solution)/shard_map/ppermute | solution.py:387
  83.9 4.2 %collective-permute-done.26.refs_2_.refs_4_ = bf16[64,1792]{1,0:T(8,128)(2,1)S(1)} collective-permute-done((bf16[64,1792]{1,0:T(8,128)(2,1)S(1)}, bf16[64,1792]{1,0:T(8,128)(2,1)S(1)}, u32[]{:S(2)}, u32[]{:S(2)}) %collective-permute-start.26) | collective-permute-done | bytes 229408 | tf_op jit(solution)/shard_map/ppermute | solution.py:390
  88.1 2.0 %collective-permute-done.28.refs_1_ = bf16[64,1792]{1,0:T(8,128)(2,1)S(1)} collective-permute-done((bf16[64,1792]{1,0:T(8,128)(2,1)S(1)}, bf16[64,1792]{1,0:T(8,128)(2,1)S(1)}, u32[]{:S(2)}, u32[]{:S(2)}) %collective-permute-start.28) | collective-permute-done | bytes 229408 | tf_op jit(solution)/shard_map/ppermute | solution.py:387
  90.2 1.0 collective-permute-start.32
  91.4 1.1 collective-permute-start.29
  92.5 2.6 %collective-permute-done.31.refs_1_ = bf16[64,1792]{1,0:T(8,128)(2,1)S(1)} collective-permute-done((bf16[64,1792]{1,0:T(8,128)(2,1)S(1)}, bf16[64,1792]{1,0:T(8,128)(2,1)S(1)}, u32[]{:S(2)}, u32[]{:S(2)}) %collective-permute-start.31) | collective-permute-done | bytes 229408 | tf_op jit(solution)/shard_map/ppermute | solution.py:387
  95.1 1.2 %collective-permute-done.32.refs_2_ = bf16[64,1792]{1,0:T(8,128)(2,1)S(1)} collective-permute-done((bf16[64,1792]{1,0:T(8,128)(2,1)S(1)}, bf16[64,1792]{1,0:T(8,128)(2,1)S(1)}, u32[]{:S(2)}, u32[]{:S(2)}) %collective-permute-start.32) | collective-permute-done | bytes 229408 | tf_op jit(solution)/shard_map/ppermute | solution.py:390
  96.4 3.8 %collective-permute-start.33 = (bf16[64,1792]{1,0:T(8,128)(2,1)S(1)}, bf16[64,1792]{1,0:T(8,128)(2,1)S(1)}, u32[]{:S(2)}, u32[]{:S(2)}) collective-permute-start(bf16[64,1792]{1,0:T(8,128)(2,1)S(1)} %add.76), channel_id=1, source_target_pairs={{0,2},{1,3},{2,0},{3,1},{4,6},{5,7},{6,4},{7,5},{8,10},{9,11},{10,... | collective-permute-start | bytes 688136 | tf_op jit(solution)/shard_map/ppermute | solution.py:390
  100.2 0.6 collective-permute-start.34
  100.8 6.6 %collective-permute-done.33.refs_2_ = bf16[64,1792]{1,0:T(8,128)(2,1)S(1)} collective-permute-done((bf16[64,1792]{1,0:T(8,128)(2,1)S(1)}, bf16[64,1792]{1,0:T(8,128)(2,1)S(1)}, u32[]{:S(2)}, u32[]{:S(2)}) %collective-permute-start.33) | collective-permute-done | bytes 229408 | tf_op jit(solution)/shard_map/ppermute | solution.py:390
  107.5 0.8 collective-permute-done.34.refs_1_
  108.3 0.7 add.78
  (68 shorter events, 4.0 us)
Async XLA Ops:
  0.6 16.0 %copy-start = (bf16[256,1792]{1,0:T(8,128)(2,1)S(1)}, bf16[256,1792]{1,0:T(8,128)(2,1)}, u32[]{:S(2)}) copy-start(bf16[256,1792]{1,0:T(8,128)(2,1)} %param.21) | copy-start | bytes 2752516
  0.8 15.7 %copy-start.4 = (f32[256,2]{0,1:T(2,128)S(1)}, f32[256,2]{0,1:T(2,128)}, u32[]{:S(2)}) copy-start(f32[256,2]{0,1:T(2,128)} %param.24) | copy-start | bytes 6148
  0.8 15.7 %copy-start.5 = (s32[256,2]{0,1:T(2,128)S(1)}, s32[256,2]{0,1:T(2,128)}, u32[]{:S(2)}) copy-start(s32[256,2]{0,1:T(2,128)} %param.23) | copy-start | bytes 6148
  0.8 15.9 %copy-start.3 = (f32[1792]{0:T(1024)S(1)}, f32[1792]{0:T(1024)}, u32[]{:S(2)}) copy-start(f32[1792]{0:T(1024)} %param.22) | copy-start | bytes 21508
  13.4 7.3 %collective-permute-start = (bf16[64,1024]{1,0:T(8,128)(2,1)S(1)}, bf16[64,1024]{1,0:T(8,128)(2,1)S(1)}, u32[]{:S(2)}, u32[]{:S(2)}) collective-permute-start(bf16[64,1024]{1,0:T(8,128)(2,1)S(1)} %attention.1.refs_1_.refs_0_), channel_id=1, source_target_pairs={{0,4},{4,0},{8,12},{12,8},{1,5},{5,1},{9,13},{13,9},{2,6},{6,2},{1... | collective-permute-start | bytes 393224 | tf_op jit(solution)/shard_map/ppermute | solution.py:383
  13.9 6.7 %collective-permute-start.1 = (bf16[64,1024]{1,0:T(8,128)(2,1)S(1)}, bf16[64,1024]{1,0:T(8,128)(2,1)S(1)}, u32[]{:S(2)}, u32[]{:S(2)}) collective-permute-start(bf16[64,1024]{1,0:T(8,128)(2,1)S(1)} %attention.1.refs_1_.refs_0_), channel_id=1, source_target_pairs={{0,8},{4,12},{8,0},{12,4},{1,9},{5,13},{9,1},{13,5},{2,10},{6,14},... | collective-permute-start | bytes 393224 | tf_op jit(solution)/shard_map/ppermute | solution.py:387
  20.6 1.4 %collective-permute-start.2 = (bf16[64,1024]{1,0:T(8,128)(2,1)S(1)}, bf16[64,1024]{1,0:T(8,128)(2,1)S(1)}, u32[]{:S(2)}, u32[]{:S(2)}) collective-permute-start(bf16[64,1024]{1,0:T(8,128)(2,1)S(1)} %add.64.refs_2_), channel_id=1, source_target_pairs={{0,4},{4,0},{8,12},{12,8},{1,5},{5,1},{9,13},{13,9},{2,6},{6,2},{1... | collective-permute-start | bytes 393224 | tf_op jit(solution)/shard_map/ppermute | solution.py:383
  23.8 7.9 %collective-permute-start.3 = (bf16[64,1792]{1,0:T(8,128)(2,1)S(1)}, bf16[64,1792]{1,0:T(8,128)(2,1)S(1)}, u32[]{:S(2)}, u32[]{:S(2)}) collective-permute-start(bf16[64,1792]{1,0:T(8,128)(2,1)S(1)} %get-tuple-element.29), channel_id=1, source_target_pairs={{0,1},{1,0},{2,3},{3,2},{4,5},{5,4},{6,7},{7,6},{8,9},{9,8},{10,11... | collective-permute-start | bytes 688136 | tf_op jit(solution)/shard_map/ppermute | solution.py:390
  28.9 11.7 %collective-permute-start.5 = (bf16[64,1792]{1,0:T(8,128)(2,1)S(1)}, bf16[64,1792]{1,0:T(8,128)(2,1)S(1)}, u32[]{:S(2)}, u32[]{:S(2)}) collective-permute-start(bf16[64,1792]{1,0:T(8,128)(2,1)S(1)} %add.66), channel_id=1, source_target_pairs={{0,1},{1,0},{2,3},{3,2},{4,5},{5,4},{6,7},{7,6},{8,9},{9,8},{10,11... | collective-permute-start | bytes 688136 | tf_op jit(solution)/shard_map/ppermute | solution.py:390
  31.7 12.8 %collective-permute-start.4 = (bf16[64,1792]{1,0:T(8,128)(2,1)S(1)}, bf16[64,1792]{1,0:T(8,128)(2,1)S(1)}, u32[]{:S(2)}, u32[]{:S(2)}) collective-permute-start(bf16[64,1792]{1,0:T(8,128)(2,1)S(1)} %add.65), channel_id=1, source_target_pairs={{0,2},{1,3},{2,0},{3,1},{4,6},{5,7},{6,4},{7,5},{8,10},{9,11},{10,... | collective-permute-start | bytes 688136 | tf_op jit(solution)/shard_map/ppermute | solution.py:390
  34.7 3.6 %collective-permute-start.7 = (f32[1,1792]{1,0:T(1,128)S(1)}, f32[1,1792]{1,0:T(1,128)S(1)}, u32[]{:S(2)}, u32[]{:S(2)}) collective-permute-start(f32[1,1792]{1,0:T(1,128)S(1)} %reshape.7.refs_4_.refs_8_), channel_id=1, source_target_pairs={{0,8},{4,12},{8,0},{12,4},{1,9},{5,13},{9,1},{13,5},{2,10},{6,14},... | collective-permute-start | bytes 21512 | tf_op jit(solution)/shard_map/ppermute | solution.py:387
  36.2 2.1 %collective-permute-start.6 = (f32[1,1792]{1,0:T(1,128)S(1)}, f32[1,1792]{1,0:T(1,128)S(1)}, u32[]{:S(2)}, u32[]{:S(2)}) collective-permute-start(f32[1,1792]{1,0:T(1,128)S(1)} %reshape.7.refs_4_.refs_8_), channel_id=1, source_target_pairs={{0,4},{4,0},{8,12},{12,8},{1,5},{5,1},{9,13},{13,9},{2,6},{6,2},{1... | collective-permute-start | bytes 21512 | tf_op jit(solution)/shard_map/ppermute | solution.py:383
  38.4 1.2 %collective-permute-start.8 = (f32[1,1792]{1,0:T(1,128)S(1)}, f32[1,1792]{1,0:T(1,128)S(1)}, u32[]{:S(2)}, u32[]{:S(2)}) collective-permute-start(f32[1,1792]{1,0:T(1,128)S(1)} %collective-permute-done.7.refs_10_.refs_8_), channel_id=1, source_target_pairs={{0,4},{4,0},{8,12},{12,8},{1,5},{5,1},{9,13},{13,9},{2,6},{6,2},{1... | collective-permute-start | bytes 21512 | tf_op jit(solution)/shard_map/ppermute | solution.py:383
  45.4 10.3 %collective-permute-start.9 = (bf16[64,1792]{1,0:T(8,128)(2,1)S(1)}, bf16[64,1792]{1,0:T(8,128)(2,1)S(1)}, u32[]{:S(2)}, u32[]{:S(2)}) collective-permute-start(bf16[64,1792]{1,0:T(8,128)(2,1)S(1)} %get-tuple-element.32.refs_1_.refs_6_), channel_id=1, source_target_pairs={{0,2},{1,3},{2,0},{3,1},{4,6},{5,7},{6,4},{7,5},{8,10},{9,11},{10,... | collective-permute-start | bytes 688136 | tf_op jit(solution)/shard_map/ppermute | solution.py:390
  45.4 10.3 %collective-permute-start.10 = (bf16[64,1792]{1,0:T(8,128)(2,1)S(1)}, bf16[64,1792]{1,0:T(8,128)(2,1)S(1)}, u32[]{:S(2)}, u32[]{:S(2)}) collective-permute-start(bf16[64,1792]{1,0:T(8,128)(2,1)S(1)} %get-tuple-element.32.refs_1_.refs_6_), channel_id=1, source_target_pairs={{0,8},{4,12},{8,0},{12,4},{1,9},{5,13},{9,1},{13,5},{2,10},{6,14},... | collective-permute-start | bytes 688136 | tf_op jit(solution)/shard_map/ppermute | solution.py:387
  46.9 10.6 %collective-permute-start.15 = (bf16[64,1792]{1,0:T(8,128)(2,1)S(1)}, bf16[64,1792]{1,0:T(8,128)(2,1)S(1)}, u32[]{:S(2)}, u32[]{:S(2)}) collective-permute-start(bf16[64,1792]{1,0:T(8,128)(2,1)S(1)} %get-tuple-element.32.refs_1_.refs_6_), channel_id=1, source_target_pairs={{0,1},{1,0},{2,3},{3,2},{4,5},{5,4},{6,7},{7,6},{8,9},{9,8},{10,11... | collective-permute-start | bytes 688136 | tf_op jit(solution)/shard_map/ppermute | solution.py:390
  55.7 6.3 %collective-permute-start.11 = (bf16[64,1792]{1,0:T(8,128)(2,1)S(1)}, bf16[64,1792]{1,0:T(8,128)(2,1)S(1)}, u32[]{:S(2)}, u32[]{:S(2)}) collective-permute-start(bf16[64,1792]{1,0:T(8,128)(2,1)S(1)} %add.68), channel_id=1, source_target_pairs={{0,1},{1,0},{2,3},{3,2},{4,5},{5,4},{6,7},{7,6},{8,9},{9,8},{10,11... | collective-permute-start | bytes 688136 | tf_op jit(solution)/shard_map/ppermute | solution.py:390
  56.1 5.8 %collective-permute-start.17 = (bf16[64,1792]{1,0:T(8,128)(2,1)S(1)}, bf16[64,1792]{1,0:T(8,128)(2,1)S(1)}, u32[]{:S(2)}, u32[]{:S(2)}) collective-permute-start(bf16[64,1792]{1,0:T(8,128)(2,1)S(1)} %get-tuple-element.32.refs_1_.refs_6_), channel_id=1, source_target_pairs={{0,4},{4,0},{8,12},{12,8},{1,5},{5,1},{9,13},{13,9},{2,6},{6,2},{1... | collective-permute-start | bytes 688136 | tf_op jit(solution)/shard_map/ppermute | solution.py:383
  56.2 7.2 %collective-permute-start.14 = (bf16[64,1792]{1,0:T(8,128)(2,1)S(1)}, bf16[64,1792]{1,0:T(8,128)(2,1)S(1)}, u32[]{:S(2)}, u32[]{:S(2)}) collective-permute-start(bf16[64,1792]{1,0:T(8,128)(2,1)S(1)} %collective-permute-done.9.refs_0_.refs_2_), channel_id=1, source_target_pairs={{0,4},{4,0},{8,12},{12,8},{1,5},{5,1},{9,13},{13,9},{2,6},{6,2},{1... | collective-permute-start | bytes 688136 | tf_op jit(solution)/shard_map/ppermute | solution.py:383
  57.5 10.1 %collective-permute-start.16 = (bf16[64,1792]{1,0:T(8,128)(2,1)S(1)}, bf16[64,1792]{1,0:T(8,128)(2,1)S(1)}, u32[]{:S(2)}, u32[]{:S(2)}) collective-permute-start(bf16[64,1792]{1,0:T(8,128)(2,1)S(1)} %collective-permute-done.15.refs_4_), channel_id=1, source_target_pairs={{0,4},{4,0},{8,12},{12,8},{1,5},{5,1},{9,13},{13,9},{2,6},{6,2},{1... | collective-permute-start | bytes 688136 | tf_op jit(solution)/shard_map/ppermute | solution.py:383
  57.5 10.2 %collective-permute-start.19 = (bf16[64,1792]{1,0:T(8,128)(2,1)S(1)}, bf16[64,1792]{1,0:T(8,128)(2,1)S(1)}, u32[]{:S(2)}, u32[]{:S(2)}) collective-permute-start(bf16[64,1792]{1,0:T(8,128)(2,1)S(1)} %collective-permute-done.9.refs_0_.refs_2_), channel_id=1, source_target_pairs={{0,8},{4,12},{8,0},{12,4},{1,9},{5,13},{9,1},{13,5},{2,10},{6,14},... | collective-permute-start | bytes 688136 | tf_op jit(solution)/shard_map/ppermute | solution.py:387
  62.0 6.2 %collective-permute-start.13 = (bf16[64,1792]{1,0:T(8,128)(2,1)S(1)}, bf16[64,1792]{1,0:T(8,128)(2,1)S(1)}, u32[]{:S(2)}, u32[]{:S(2)}) collective-permute-start(bf16[64,1792]{1,0:T(8,128)(2,1)S(1)} %collective-permute-done.11.refs_0_.refs_1_), channel_id=1, source_target_pairs={{0,4},{4,0},{8,12},{12,8},{1,5},{5,1},{9,13},{13,9},{2,6},{6,2},{1... | collective-permute-start | bytes 688136 | tf_op jit(solution)/shard_map/ppermute | solution.py:383
  62.0 8.8 %collective-permute-start.12 = (bf16[64,1792]{1,0:T(8,128)(2,1)S(1)}, bf16[64,1792]{1,0:T(8,128)(2,1)S(1)}, u32[]{:S(2)}, u32[]{:S(2)}) collective-permute-start(bf16[64,1792]{1,0:T(8,128)(2,1)S(1)} %collective-permute-done.11.refs_0_.refs_1_), channel_id=1, source_target_pairs={{0,8},{4,12},{8,0},{12,4},{1,9},{5,13},{9,1},{13,5},{2,10},{6,14},... | collective-permute-start | bytes 688136 | tf_op jit(solution)/shard_map/ppermute | solution.py:387
  63.3 7.8 %collective-permute-start.21 = (bf16[64,1792]{1,0:T(8,128)(2,1)S(1)}, bf16[64,1792]{1,0:T(8,128)(2,1)S(1)}, u32[]{:S(2)}, u32[]{:S(2)}) collective-permute-start(bf16[64,1792]{1,0:T(8,128)(2,1)S(1)} %add.70), channel_id=1, source_target_pairs={{0,1},{1,0},{2,3},{3,2},{4,5},{5,4},{6,7},{7,6},{8,9},{9,8},{10,11... | collective-permute-start | bytes 688136 | tf_op jit(solution)/shard_map/ppermute | solution.py:390
  67.6 3.3 %copy-start.2 = (bf16[1,512,7168]{2,1,0:T(8,128)(2,1)}, bf16[1,512,7168]{2,1,0:T(8,128)(2,1)S(1)}, u32[]{:S(2)}) copy-start(bf16[1,512,7168]{2,1,0:T(8,128)(2,1)S(1)} %fetch.7.refs_12_.down) | copy-start | bytes 22020100
  67.6 3.9 %collective-permute-start.23 = (bf16[64,1792]{1,0:T(8,128)(2,1)S(1)}, bf16[64,1792]{1,0:T(8,128)(2,1)S(1)}, u32[]{:S(2)}, u32[]{:S(2)}) collective-permute-start(bf16[64,1792]{1,0:T(8,128)(2,1)S(1)} %collective-permute-done.10.refs_1_.refs_0_.refs_6_), channel_id=1, source_target_pairs={{0,4},{4,0},{8,12},{12,8},{1,5},{5,1},{9,13},{13,9},{2,6},{6,2},{1... | collective-permute-start | bytes 688136 | tf_op jit(solution)/shard_map/ppermute | solution.py:383
  67.7 3.8 %collective-permute-start.20 = (bf16[64,1792]{1,0:T(8,128)(2,1)S(1)}, bf16[64,1792]{1,0:T(8,128)(2,1)S(1)}, u32[]{:S(2)}, u32[]{:S(2)}) collective-permute-start(bf16[64,1792]{1,0:T(8,128)(2,1)S(1)} %collective-permute-done.19.refs_2_), channel_id=1, source_target_pairs={{0,4},{4,0},{8,12},{12,8},{1,5},{5,1},{9,13},{13,9},{2,6},{6,2},{1... | collective-permute-start | bytes 688136 | tf_op jit(solution)/shard_map/ppermute | solution.py:383
  70.8 4.8 %slice-start = ((s8[7340032]{0:T(1024)(128)(4,1)}), s8[4194304]{0:T(1024)(128)(4,1)S(1)}, s32[]{:S(2)}) async-start(s8[7340032]{0:T(1024)(128)(4,1)} %bitcast.9), calls=%async_computation | async-start | bytes 8388608
  70.9 1.6 %collective-permute-start.18 = (bf16[64,1792]{1,0:T(8,128)(2,1)S(1)}, bf16[64,1792]{1,0:T(8,128)(2,1)S(1)}, u32[]{:S(2)}, u32[]{:S(2)}) collective-permute-start(bf16[64,1792]{1,0:T(8,128)(2,1)S(1)} %add.69), channel_id=1, source_target_pairs={{0,4},{4,0},{8,12},{12,8},{1,5},{5,1},{9,13},{13,9},{2,6},{6,2},{1... | collective-permute-start | bytes 688136 | tf_op jit(solution)/shard_map/ppermute | solution.py:383
  71.1 1.6 %collective-permute-start.22 = (bf16[64,1792]{1,0:T(8,128)(2,1)S(1)}, bf16[64,1792]{1,0:T(8,128)(2,1)S(1)}, u32[]{:S(2)}, u32[]{:S(2)}) collective-permute-start(bf16[64,1792]{1,0:T(8,128)(2,1)S(1)} %collective-permute-done.21.refs_4_), channel_id=1, source_target_pairs={{0,4},{4,0},{8,12},{12,8},{1,5},{5,1},{9,13},{13,9},{2,6},{6,2},{1... | collective-permute-start | bytes 688136 | tf_op jit(solution)/shard_map/ppermute | solution.py:383
  72.8 2.9 %slice-start.1 = ((s8[7340032]{0:T(1024)(128)(4,1)}), s8[3145728]{0:T(1024)(128)(4,1)S(1)}, s32[]{:S(2)}) async-start(s8[7340032]{0:T(1024)(128)(4,1)} %bitcast.9), calls=%async_computation.1 | async-start | bytes 6291456
  75.7 33.3 %copy-start.1 = (bf16[256,1792]{1,0:T(8,128)(2,1)S(1)}, bf16[256,1792]{1,0:T(8,128)(2,1)}, u32[]{:S(2)}) copy-start(bf16[256,1792]{1,0:T(8,128)(2,1)} %param.21) | copy-start | bytes 2752516
  78.4 1.9 %collective-permute-start.25 = (bf16[128,1792]{1,0:T(8,128)(2,1)S(1)}, bf16[128,1792]{1,0:T(8,128)(2,1)S(1)}, u32[]{:S(2)}, u32[]{:S(2)}) collective-permute-start(bf16[128,1792]{1,0:T(8,128)(2,1)S(1)} %get-tuple-element.39), channel_id=1, source_target_pairs={{0,4},{4,0},{8,12},{12,8},{1,5},{5,1},{9,13},{13,9},{2,6},{6,2},{1... | collective-permute-start | bytes 1376264 | tf_op jit(solution)/shard_map/ppermute | solution.py:383
  78.6 2.9 %collective-permute-start.27 = (bf16[128,1792]{1,0:T(8,128)(2,1)S(1)}, bf16[128,1792]{1,0:T(8,128)(2,1)S(1)}, u32[]{:S(2)}, u32[]{:S(2)}) collective-permute-start(bf16[128,1792]{1,0:T(8,128)(2,1)S(1)} %get-tuple-element.42), channel_id=1, source_target_pairs={{0,4},{4,0},{8,12},{12,8},{1,5},{5,1},{9,13},{13,9},{2,6},{6,2},{1... | collective-permute-start | bytes 1376264 | tf_op jit(solution)/shard_map/ppermute | solution.py:383
  79.0 3.5 %collective-permute-start.30 = (bf16[128,1792]{1,0:T(8,128)(2,1)S(1)}, bf16[128,1792]{1,0:T(8,128)(2,1)S(1)}, u32[]{:S(2)}, u32[]{:S(2)}) collective-permute-start(bf16[128,1792]{1,0:T(8,128)(2,1)S(1)} %get-tuple-element.48), channel_id=1, source_target_pairs={{0,4},{4,0},{8,12},{12,8},{1,5},{5,1},{9,13},{13,9},{2,6},{6,2},{1... | collective-permute-start | bytes 1376264 | tf_op jit(solution)/shard_map/ppermute | solution.py:383
  79.1 12.1 %collective-permute-start.24 = (bf16[128,1792]{1,0:T(8,128)(2,1)S(1)}, bf16[128,1792]{1,0:T(8,128)(2,1)S(1)}, u32[]{:S(2)}, u32[]{:S(2)}) collective-permute-start(bf16[128,1792]{1,0:T(8,128)(2,1)S(1)} %get-tuple-element.37), channel_id=1, source_target_pairs={{0,4},{4,0},{8,12},{12,8},{1,5},{5,1},{9,13},{13,9},{2,6},{6,2},{1... | collective-permute-start | bytes 1376264 | tf_op jit(solution)/shard_map/ppermute | solution.py:383
  80.4 7.7 %collective-permute-start.26 = (bf16[64,1792]{1,0:T(8,128)(2,1)S(1)}, bf16[64,1792]{1,0:T(8,128)(2,1)S(1)}, u32[]{:S(2)}, u32[]{:S(2)}) collective-permute-start(bf16[64,1792]{1,0:T(8,128)(2,1)S(1)} %get-tuple-element.40), channel_id=1, source_target_pairs={{0,1},{1,0},{2,3},{3,2},{4,5},{5,4},{6,7},{7,6},{8,9},{9,8},{10,11... | collective-permute-start | bytes 688136 | tf_op jit(solution)/shard_map/ppermute | solution.py:390
  81.6 8.5 %collective-permute-start.28 = (bf16[64,1792]{1,0:T(8,128)(2,1)S(1)}, bf16[64,1792]{1,0:T(8,128)(2,1)S(1)}, u32[]{:S(2)}, u32[]{:S(2)}) collective-permute-start(bf16[64,1792]{1,0:T(8,128)(2,1)S(1)} %get-tuple-element.44), channel_id=1, source_target_pairs={{0,8},{4,12},{8,0},{12,4},{1,9},{5,13},{9,1},{13,5},{2,10},{6,14},... | collective-permute-start | bytes 688136 | tf_op jit(solution)/shard_map/ppermute | solution.py:387
  82.6 12.5 %collective-permute-start.31 = (bf16[64,1792]{1,0:T(8,128)(2,1)S(1)}, bf16[64,1792]{1,0:T(8,128)(2,1)S(1)}, u32[]{:S(2)}, u32[]{:S(2)}) collective-permute-start(bf16[64,1792]{1,0:T(8,128)(2,1)S(1)} %get-tuple-element.50), channel_id=1, source_target_pairs={{0,8},{4,12},{8,0},{12,4},{1,9},{5,13},{9,1},{13,5},{2,10},{6,14},... | collective-permute-start | bytes 688136 | tf_op jit(solution)/shard_map/ppermute | solution.py:387
  90.2 6.1 %collective-permute-start.32 = (bf16[64,1792]{1,0:T(8,128)(2,1)S(1)}, bf16[64,1792]{1,0:T(8,128)(2,1)S(1)}, u32[]{:S(2)}, u32[]{:S(2)}) collective-permute-start(bf16[64,1792]{1,0:T(8,128)(2,1)S(1)} %add.73.refs_5_), channel_id=1, source_target_pairs={{0,1},{1,0},{2,3},{3,2},{4,5},{5,4},{6,7},{7,6},{8,9},{9,8},{10,11... | collective-permute-start | bytes 688136 | tf_op jit(solution)/shard_map/ppermute | solution.py:390
  91.4 9.4 %collective-permute-start.29 = (bf16[64,1792]{1,0:T(8,128)(2,1)S(1)}, bf16[64,1792]{1,0:T(8,128)(2,1)S(1)}, u32[]{:S(2)}, u32[]{:S(2)}) collective-permute-start(bf16[64,1792]{1,0:T(8,128)(2,1)S(1)} %get-tuple-element.46), channel_id=1, source_target_pairs={{0,8},{4,12},{8,0},{12,4},{1,9},{5,13},{9,1},{13,5},{2,10},{6,14},... | collective-permute-start | bytes 688136 | tf_op jit(solution)/shard_map/ppermute | solution.py:387
  96.4 11.0 %collective-permute-start.33 = (bf16[64,1792]{1,0:T(8,128)(2,1)S(1)}, bf16[64,1792]{1,0:T(8,128)(2,1)S(1)}, u32[]{:S(2)}, u32[]{:S(2)}) collective-permute-start(bf16[64,1792]{1,0:T(8,128)(2,1)S(1)} %add.76), channel_id=1, source_target_pairs={{0,2},{1,3},{2,0},{3,1},{4,6},{5,7},{6,4},{7,5},{8,10},{9,11},{10,... | collective-permute-start | bytes 688136 | tf_op jit(solution)/shard_map/ppermute | solution.py:390
  100.2 8.0 %collective-permute-start.34 = (bf16[64,1792]{1,0:T(8,128)(2,1)S(1)}, bf16[64,1792]{1,0:T(8,128)(2,1)S(1)}, u32[]{:S(2)}, u32[]{:S(2)}) collective-permute-start(bf16[64,1792]{1,0:T(8,128)(2,1)S(1)} %get-tuple-element.51), channel_id=1, source_target_pairs={{0,1},{1,0},{2,3},{3,2},{4,5},{5,4},{6,7},{7,6},{8,9},{9,8},{10,11... | collective-permute-start | bytes 688136 | tf_op jit(solution)/shard_map/ppermute | solution.py:390

commit v18 on v17

--- a/solution.py
+++ b/solution.py
@@ -212,7 +212,7 @@
     )(places, *blocks, in_vmem(weight))
 
 
-def gate_kernel(row_blocks, cores, first, count, model_width, places, *refs):
+def gate_kernel(row_blocks, first, count, model_width, places, *refs):
     blocks, gains = refs[: row_blocks * count], refs[row_blocks * count : (row_blocks + 1) * count]
     refs = refs[(row_blocks + 1) * count :]
     gate, up, refs = refs[0], refs[1], refs[2:]
@@ -220,7 +220,14 @@
         before, (active, x) = refs[:3], refs[-2:]
         gate_sum, up_sum, squares = before
     else:
-        gate_sum, up_sum, squares, x = refs[-4:]
+        source, (gate_sum, up_sum, squares, target, x, sems) = refs[0], refs[-6:]
+        parts = sems.shape[0]
+        step = source.shape[1] // parts
+        copies = []
+        for i in range(parts):
+            cut = pl.ds(i * step, step)
+            copies.append(pltpu.make_async_copy(source.at[:, cut], target.at[:, cut], sems.at[i]))
+            copies[i].start()
     height, width = blocks[0].shape
     hidden = gate.shape[2]
     tile = min(256, hidden)
@@ -247,6 +254,8 @@
     if not first:
         for s in range(row_blocks):
             squares[s * height : (s + 1) * height, :] = totals[s]
+        for copy in copies:
+            copy.wait()
         return
     scale = jnp.concatenate([lax.rsqrt(t / model_width + norm_epsilon) for t in totals], axis=0)
     for j in range(hidden // tile):
@@ -255,29 +264,32 @@
         active[:, j * tile : (j + 1) * tile] = (gate_part / (1.0 + jnp.exp(-gate_part)) * up_part).astype(jnp.bfloat16)
 
 
-def activate(places, blocks, gains, gate_weight, up_weight, cores, first, before, after):
+def activate(places, blocks, gains, gate_weight, up_weight, first, before, following=None):
     row_blocks, count = len(blocks), len(blocks[0])
     height, width = blocks[0][0].shape
     rows = row_blocks * height
     model_width, hidden = gate_weight.shape[1:]
     whole = pl.BlockSpec(memory_space=pltpu.VMEM)
+    rest = [] if first else [in_hbm(following)]
     if first:
         kinds = jax.ShapeDtypeStruct((rows, hidden), jnp.bfloat16)
     else:
         kinds = [jax.ShapeDtypeStruct((rows, n), jnp.float32) for n in (hidden, hidden, 1)]
+        kinds.append(pltpu.VMEM(following.shape, following.dtype))
     return pl.pallas_call(
-        functools.partial(gate_kernel, row_blocks, cores, first, count, model_width),
+        functools.partial(gate_kernel, row_blocks, first, count, model_width),
         out_shape=kinds,
         in_specs=[pl.BlockSpec(memory_space=pltpu.SMEM)] + [whole] * ((row_blocks + 1) * count + 2 + len(before))
-        + [pl.BlockSpec(memory_space=pl.ANY)] * len(after),
-        out_specs=whole if first else [whole] * 3,
-        scratch_shapes=[pltpu.VMEM((rows, count * width), jnp.bfloat16)],
+        + [pl.BlockSpec(memory_space=pl.ANY)] * (0 if first else 1),
+        out_specs=whole if first else [whole] * 4,
+        scratch_shapes=[pltpu.VMEM((rows, count * width), jnp.bfloat16)]
+        + [pltpu.SemaphoreType.DMA((4,))] * (0 if first else 1),
         cost_estimate=pl.CostEstimate(
             flops=4 * rows * hidden * count * width, bytes_accessed=4 * hidden * count * width, transcendentals=0
         ),
         compiler_params=pltpu.CompilerParams(vmem_limit_bytes=2 * rows * (count * width + 8 * hidden) + 12 * MIB),
         name="activate",
-    )(places, *[b for row in blocks for b in row], *gains, in_vmem(gate_weight), in_vmem(up_weight), *before, *after)
+    )(places, *[b for row in blocks for b in row], *gains, in_vmem(gate_weight), in_vmem(up_weight), *before, *rest)
 
 
 def down_kernel(slots, at, column_blocks, cores, places, active, row_weight, down, *refs):
@@ -426,7 +438,6 @@
     stream_terms = terms[0] + [(own_residual, 0)]
     stream, stream_out = add([stream_terms, stream_terms], block_rows, gains + [gate_weight])
     up_weight = fetch(up_weight, [stream])
-    down_weight = fetch(down_weight, [stream])
 
     rows_of = {0: stream}
     crossed = [from_chip(stream, b) for b in range(1, chips)]
@@ -438,7 +449,9 @@
         rows_of[k] = from_tp(source, low)
     slots = list(reversed(range(tp_count)))
     near = {k: [rows_of[k], from_core(rows_of[k])] for k in slots}
-    sums = activate(places, [near[k] for k in slots], gains[:cores], gate_weight, up_weight, cores, 0, [], [down_weight])
+    *sums, down_weight = activate(
+        places, [near[k] for k in slots], gains[:cores], gate_weight, up_weight, 0, [], down_weight
+    )
     far = {}
     for k in [0] + slots[:-1]:
         far[k] = []
@@ -452,7 +465,7 @@
                 value = from_chip(rows_of[k], b)
             (later,) = add([[(value, 0)]], block_rows, sums[-1:]) if k == tp_count - 1 else (value,)
             far[k] += [value, from_core(later)]
-    active = activate(places, [far[k] for k in slots], gains[cores:], gate_weight, up_weight, cores, cores, sums, [])
+    active = activate(places, [far[k] for k in slots], gains[cores:], gate_weight, up_weight, cores, sums)
 
     def send_back(k, after):
         total = list(add([terms[k]], block_rows, after))

time: 109 us -> 112 us (1.028)
  local copies, waits for them, and re-layouts: 0.3 us -> 3.17 us
  waiting for transfers between devices: 39.7 us -> 42.3 us
  starting transfers between devices: 31.4 us -> 30 us
    pallas_call x4 -> x3, Pallas kernels: 11.6 us -> 8.42 us  [fetch(): pl.pallas_call(functools.partial(fetch_kernel, parts), out_shape=pltpu.VM...]
    unnamed x16, local copies, waits for them, and re-layouts: 0.04 us -> 2.92 us
    pallas_call x2, Pallas kernels: 5.52 us -> 8.01 us  [activate(): pl.pallas_call(functools.partial(gate_kernel, row_blocks, first, count, m...]
    ppermute x11, waiting for transfers between devices: 26.5 us -> 28.6 us  [from_tp(): return lax.ppermute(value, 'tp', [(i, i ^ bits) for i in range(tp_count)])]
  transfers between devices with their start and end apart: 35 -> 35, of which waited for: 20 -> 20; matrix products, arithmetic and copies ran while one was open for 0% -> 0% of each run, Pallas kernels for 14% -> 13%
where the time goes in v18:
time: 112 us
  waiting for transfers between devices  42.3 us (38%)
  Pallas kernels  35.8 us (32%)
  starting transfers between devices  30 us (27%)
  local copies, waits for them, and re-layouts  3.17 us (3%)
    ppermute x11, waiting for transfers between devices, from_tp(): return lax.ppermute(value, 'tp', [(i, i ^ bits) for i in range(tp_count)])  28.6 us
    ppermute x11, starting transfers between devices, from_tp(): return lax.ppermute(value, 'tp', [(i, i ^ bits) for i in range(tp_count)])  16.6 us
    pallas_call x1, Pallas kernels, attend(): pl.pallas_call(functools.partial(attention_kernel, step_rows, pieces, ahe...  12.6 us
    ppermute x8, starting transfers between devices, from_chip(): lax.ppermute(value, 'ep', [(i, (i + step) % ep_count) for i in range(ep_c...  10.6 us
    ppermute x8, waiting for transfers between devices, from_chip(): lax.ppermute(value, 'ep', [(i, (i + step) % ep_count) for i in range(ep_c...  8.94 us
    pallas_call x3, Pallas kernels, fetch(): pl.pallas_call(functools.partial(fetch_kernel, parts), out_shape=pltpu.VM...  8.42 us
    pallas_call x2, Pallas kernels, activate(): pl.pallas_call(functools.partial(gate_kernel, row_blocks, first, count, m...  8.01 us
    ppermute x16, waiting for transfers between devices, from_core(): return lax.ppermute(value, 'ep', [(i, i ^ 1) for i in range(ep_count)])  4.74 us
  transfers between devices with their start and end apart: 35, of which 20 were waited for; matrix products, arithmetic and copies ran while one was open for 0% of the time, Pallas kernels for 13%

profile of v18, /device:TPU:0, one launch (start us, length us, event | category | flops | bytes accessed | tf_op | source)
XLA Modules:
  0.0 112.3 jit_solution(13999887852992310757)
XLA Ops:
  0.8 12.6 %attention.1.refs_1_.refs_0_ = bf16[64,1024]{1,0:T(8,128)(2,1)S(1)} custom-call(s32[64]{0:T(128)} %lengths.1, bf16[64,8,512]{2,1,0:T(8,128)(2,1)} %q_ref.1, bf16[64,512]{1,0:T(8,128)(2,1)} %qr_ref.1, bf16[64,256,512]{2,1,0:T(8,128)(2,1)} %k_hbm.1, bf16[64,64,256]{2,1,0:T(8,128)(2,1)} %kr_hbm.1, bf16[8,512,128]{2,1,0:T(8,128)(2,1)} %up_hbm.1, ...), custom_call_target="tpu_custom_call" | custom-call | flops 4294967296 | bytes 16777216 | tf_op jit(solution)/shard_map/attention/pallas_call | solution.py:135
  13.4 0.5 collective-permute-start
  13.9 2.6 %collective-permute-start.1 = (bf16[64,1024]{1,0:T(8,128)(2,1)S(1)}, bf16[64,1024]{1,0:T(8,128)(2,1)S(1)}, u32[]{:S(2)}, u32[]{:S(2)}) collective-permute-start(bf16[64,1024]{1,0:T(8,128)(2,1)S(1)} %attention.1.refs_1_.refs_0_), channel_id=1, source_target_pairs={{0,8},{4,12},{8,0},{12,4},{1,9},{5,13},{9,1},{13,5},{2,10},{6,14},... | collective-permute-start | bytes 393224 | tf_op jit(solution)/shard_map/ppermute | solution.py:399
  16.7 2.0 %fetch.3.refs_1_.refs_4_ = bf16[1024,1792]{1,0:T(8,128)(2,1)S(1)} custom-call(bf16[1024,1792]{1,0:T(8,128)(2,1)} %refs_0_.3, bf16[64,1024]{1,0:T(8,128)(2,1)S(1)} %attention.1.refs_1_.refs_0_, f32[256,1]{1,0:T(8,128)S(1)} %copy.16.refs_2_.row_weight, bf16[64,1792]{1,0:T(8,128)(2,1)S(1)} %constant_dynamic-slice_fusion.refs_3_.refs_7_, ...), custom_call_target="tpu_custom_call" | custom-call | bytes 7340032 | tf_op jit(solution)/shard_map/fetch/pallas_call | solution.py:38
  18.8 1.8 %collective-permute-done.1.refs_0_ = bf16[64,1024]{1,0:T(8,128)(2,1)S(1)} collective-permute-done((bf16[64,1024]{1,0:T(8,128)(2,1)S(1)}, bf16[64,1024]{1,0:T(8,128)(2,1)S(1)}, u32[]{:S(2)}, u32[]{:S(2)}) %collective-permute-start.1) | collective-permute-done | bytes 131104 | tf_op jit(solution)/shard_map/ppermute | solution.py:399
  20.7 1.3 %collective-permute-done.2.refs_3_ = bf16[64,1024]{1,0:T(8,128)(2,1)S(1)} collective-permute-done((bf16[64,1024]{1,0:T(8,128)(2,1)S(1)}, bf16[64,1024]{1,0:T(8,128)(2,1)S(1)}, u32[]{:S(2)}, u32[]{:S(2)}) %collective-permute-start.2) | collective-permute-done | bytes 131104 | tf_op jit(solution)/shard_map/ppermute | solution.py:395
  22.0 1.8 %projection.1 = (bf16[64,1792]{1,0:T(8,128)(2,1)S(1)}, bf16[64,1792]{1,0:T(8,128)(2,1)S(1)}, bf16[64,1792]{1,0:T(8,128)(2,1)S(1)}, bf16[64,1792]{1,0:T(8,128)(2,1)S(1)}) custom-call(s32[8]{0:T(128)S(1)} %stack.35.refs_0_.places, bf16[64,1024]{1,0:T(8,128)(2,1)S(1)} %attention.1.refs_1_.refs_0_, bf16[64,1024]{1,0:T(8,128)(2,1)S(1)} %collective-permute-done.refs_1_, ...), custom_call_target="tpu_custom_call" | custom-call | flops 939524096 | bytes 4194304 | tf_op jit(solution)/shard_map/projection/pallas_call | solution.py:200
  23.8 1.9 %collective-permute-start.3 = (bf16[64,1792]{1,0:T(8,128)(2,1)S(1)}, bf16[64,1792]{1,0:T(8,128)(2,1)S(1)}, u32[]{:S(2)}, u32[]{:S(2)}) collective-permute-start(bf16[64,1792]{1,0:T(8,128)(2,1)S(1)} %get-tuple-element.30), channel_id=1, source_target_pairs={{0,1},{1,0},{2,3},{3,2},{4,5},{5,4},{6,7},{7,6},{8,9},{9,8},{10,11... | collective-permute-start | bytes 688136 | tf_op jit(solution)/shard_map/ppermute | solution.py:402
  25.7 3.2 %fetch.4.refs_1_.refs_12_.refs_10_ = bf16[1,7168,512]{2,1,0:T(8,128)(2,1)S(1)} custom-call(bf16[1,7168,512]{2,1,0:T(8,128)(2,1)} %refs_0_.4, bf16[64,1792]{1,0:T(8,128)(2,1)S(1)} %get-tuple-element.28.refs_1_.refs_0_.refs_4_), custom_call_target="tpu_custom_call" | custom-call | bytes 14680064 | tf_op jit(solution)/shard_map/fetch/pallas_call | solution.py:38
  29.1 2.5 %collective-permute-done.3.refs_1_ = bf16[64,1792]{1,0:T(8,128)(2,1)S(1)} collective-permute-done((bf16[64,1792]{1,0:T(8,128)(2,1)S(1)}, bf16[64,1792]{1,0:T(8,128)(2,1)S(1)}, u32[]{:S(2)}, u32[]{:S(2)}) %collective-permute-start.3) | collective-permute-done | bytes 229408 | tf_op jit(solution)/shard_map/ppermute | solution.py:402
  31.7 3.0 %collective-permute-start.4 = (bf16[64,1792]{1,0:T(8,128)(2,1)S(1)}, bf16[64,1792]{1,0:T(8,128)(2,1)S(1)}, u32[]{:S(2)}, u32[]{:S(2)}) collective-permute-start(bf16[64,1792]{1,0:T(8,128)(2,1)S(1)} %add.65), channel_id=1, source_target_pairs={{0,2},{1,3},{2,0},{3,1},{4,6},{5,7},{6,4},{7,5},{8,10},{9,11},{10,... | collective-permute-start | bytes 688136 | tf_op jit(solution)/shard_map/ppermute | solution.py:402
  34.7 1.5 %collective-permute-start.7 = (f32[1,1792]{1,0:T(1,128)S(1)}, f32[1,1792]{1,0:T(1,128)S(1)}, u32[]{:S(2)}, u32[]{:S(2)}) collective-permute-start(f32[1,1792]{1,0:T(1,128)S(1)} %reshape.7.refs_4_.refs_8_), channel_id=1, source_target_pairs={{0,8},{4,12},{8,0},{12,4},{1,9},{5,13},{9,1},{13,5},{2,10},{6,14},... | collective-permute-start | bytes 21512 | tf_op jit(solution)/shard_map/ppermute | solution.py:399
  36.2 2.1 %collective-permute-done.7.refs_10_.refs_8_ = f32[1,1792]{1,0:T(1,128)S(1)} collective-permute-done((f32[1,1792]{1,0:T(1,128)S(1)}, f32[1,1792]{1,0:T(1,128)S(1)}, u32[]{:S(2)}, u32[]{:S(2)}) %collective-permute-start.7) | collective-permute-done | bytes 7200 | tf_op jit(solution)/shard_map/ppermute | solution.py:399
  38.4 1.2 %collective-permute-done.8.refs_11_.refs_9_ = f32[1,1792]{1,0:T(1,128)S(1)} collective-permute-done((f32[1,1792]{1,0:T(1,128)S(1)}, f32[1,1792]{1,0:T(1,128)S(1)}, u32[]{:S(2)}, u32[]{:S(2)}) %collective-permute-start.8) | collective-permute-done | bytes 7200 | tf_op jit(solution)/shard_map/ppermute | solution.py:395
  39.5 1.1 collective-permute-done.5.refs_2_.refs_6_
  40.6 3.9 %collective-permute-done.4.refs_1_.refs_5_ = bf16[64,1792]{1,0:T(8,128)(2,1)S(1)} collective-permute-done((bf16[64,1792]{1,0:T(8,128)(2,1)S(1)}, bf16[64,1792]{1,0:T(8,128)(2,1)S(1)}, u32[]{:S(2)}, u32[]{:S(2)}) %collective-permute-start.4) | collective-permute-done | bytes 229408 | tf_op jit(solution)/shard_map/ppermute | solution.py:402
  44.5 0.8 add.67
  45.4 1.5 %collective-permute-start.10 = (bf16[64,1792]{1,0:T(8,128)(2,1)S(1)}, bf16[64,1792]{1,0:T(8,128)(2,1)S(1)}, u32[]{:S(2)}, u32[]{:S(2)}) collective-permute-start(bf16[64,1792]{1,0:T(8,128)(2,1)S(1)} %get-tuple-element.33.refs_1_.refs_6_), channel_id=1, source_target_pairs={{0,8},{4,12},{8,0},{12,4},{1,9},{5,13},{9,1},{13,5},{2,10},{6,14},... | collective-permute-start | bytes 688136 | tf_op jit(solution)/shard_map/ppermute | solution.py:399
  46.9 4.1 %collective-permute-start.15 = (bf16[64,1792]{1,0:T(8,128)(2,1)S(1)}, bf16[64,1792]{1,0:T(8,128)(2,1)S(1)}, u32[]{:S(2)}, u32[]{:S(2)}) collective-permute-start(bf16[64,1792]{1,0:T(8,128)(2,1)S(1)} %get-tuple-element.33.refs_1_.refs_6_), channel_id=1, source_target_pairs={{0,1},{1,0},{2,3},{3,2},{4,5},{5,4},{6,7},{7,6},{8,9},{9,8},{10,11... | collective-permute-start | bytes 688136 | tf_op jit(solution)/shard_map/ppermute | solution.py:402
  51.0 3.2 %fetch.5.refs_2_.refs_11_ = bf16[1,7168,512]{2,1,0:T(8,128)(2,1)S(1)} custom-call(bf16[1,7168,512]{2,1,0:T(8,128)(2,1)} %refs_0_.5, bf16[64,1792]{1,0:T(8,128)(2,1)S(1)} %get-tuple-element.33.refs_1_.refs_6_), custom_call_target="tpu_custom_call" | custom-call | bytes 14680064 | tf_op jit(solution)/shard_map/fetch/pallas_call | solution.py:38
  54.2 1.4 %collective-permute-done.9.refs_0_.refs_2_ = bf16[64,1792]{1,0:T(8,128)(2,1)S(1)} collective-permute-done((bf16[64,1792]{1,0:T(8,128)(2,1)S(1)}, bf16[64,1792]{1,0:T(8,128)(2,1)S(1)}, u32[]{:S(2)}, u32[]{:S(2)}) %collective-permute-start.9) | collective-permute-done | bytes 229408 | tf_op jit(solution)/shard_map/ppermute | solution.py:402
  55.7 0.5 collective-permute-start.11
  56.2 0.5 collective-permute-start.14
  56.7 0.8 collective-permute-done.15.refs_4_
  57.5 0.7 collective-permute-start.19
  58.2 3.8 %collective-permute-done.11.refs_0_.refs_1_ = bf16[64,1792]{1,0:T(8,128)(2,1)S(1)} collective-permute-done((bf16[64,1792]{1,0:T(8,128)(2,1)S(1)}, bf16[64,1792]{1,0:T(8,128)(2,1)S(1)}, u32[]{:S(2)}, u32[]{:S(2)}) %collective-permute-start.11) | collective-permute-done | bytes 229408 | tf_op jit(solution)/shard_map/ppermute | solution.py:402
  62.0 1.3 %collective-permute-start.12 = (bf16[64,1792]{1,0:T(8,128)(2,1)S(1)}, bf16[64,1792]{1,0:T(8,128)(2,1)S(1)}, u32[]{:S(2)}, u32[]{:S(2)}) collective-permute-start(bf16[64,1792]{1,0:T(8,128)(2,1)S(1)} %collective-permute-done.11.refs_0_.refs_1_), channel_id=1, source_target_pairs={{0,8},{4,12},{8,0},{12,4},{1,9},{5,13},{9,1},{13,5},{2,10},{6,14},... | collective-permute-start | bytes 688136 | tf_op jit(solution)/shard_map/ppermute | solution.py:399
  63.3 1.0 collective-permute-start.21
  64.4 1.5 %collective-permute-done.19.refs_2_ = bf16[64,1792]{1,0:T(8,128)(2,1)S(1)} collective-permute-done((bf16[64,1792]{1,0:T(8,128)(2,1)S(1)}, bf16[64,1792]{1,0:T(8,128)(2,1)S(1)}, u32[]{:S(2)}, u32[]{:S(2)}) %collective-permute-start.19) | collective-permute-done | bytes 229408 | tf_op jit(solution)/shard_map/ppermute | solution.py:399
  65.9 5.1 %activate.2 = (f32[256,512]{1,0:T(8,128)S(1)}, f32[256,512]{1,0:T(8,128)S(1)}, f32[256,1]{1,0:T(8,128)S(1)}, bf16[1,512,7168]{2,1,0:T(8,128)(2,1)S(1)}) custom-call(s32[8]{0:T(128)S(1)} %stack.35.refs_0_.places, bf16[64,1792]{1,0:T(8,128)(2,1)S(1)} %collective-permute-done.11.refs_0_.refs_1_, bf16[64,1792]{1,0:T(8,128)(2,1)S(1)} %collective-permute-done.13.refs_1_, ...), custom_call_target="tpu_custom_call" | custom-call | flops 1879048192 | bytes 7340032 | tf_op jit(solution)/shard_map/activate/pallas_call | solution.py:279
  71.0 2.9 %copy-done.2 = bf16[1,512,7168]{2,1,0:T(8,128)(2,1)} copy-done((bf16[1,512,7168]{2,1,0:T(8,128)(2,1)}, bf16[1,512,7168]{2,1,0:T(8,128)(2,1)S(1)}, u32[]{:S(2)}) %copy-start.2) | copy-done | bytes 7340056
  73.9 0.6 collective-permute-start.18
  74.6 1.0 collective-permute-done.18.refs_1_
  76.0 2.9 %activate.3.active = bf16[256,512]{1,0:T(8,128)(2,1)S(1)} custom-call(s32[8]{0:T(128)S(1)} %stack.35.refs_0_.places, bf16[64,1792]{1,0:T(8,128)(2,1)S(1)} %collective-permute-done.12.refs_0_, bf16[64,1792]{1,0:T(8,128)(2,1)S(1)} %collective-permute-done.18.refs_1_, bf16[64,1792]{1,0:T(8,128)(2,1)S(1)} %collective-permute-done.19.refs_2_, ...), custom_call_target="tpu_custom_call" | custom-call | flops 1879048192 | bytes 7340032 | tf_op jit(solution)/shard_map/activate/pallas_call | solution.py:279
  78.9 2.7 %down.1 = (bf16[128,1792]{1,0:T(8,128)(2,1)S(1)}, bf16[128,1792]{1,0:T(8,128)(2,1)S(1)}, bf16[128,1792]{1,0:T(8,128)(2,1)S(1)}, bf16[128,1792]{1,0:T(8,128)(2,1)...) custom-call(s32[8]{0:T(128)S(1)} %stack.35.refs_0_.places, ...), custom_call_target="tpu_custom_call" | custom-call | flops 1879048192 | bytes 7340032 | tf_op jit(solution)/shard_map/down/pallas_call | solution.py:326
  82.7 0.8 collective-permute-done.25.refs_1_.refs_3_
  83.6 0.5 collective-permute-start.26
  84.3 1.9 %collective-permute-start.28 = (bf16[64,1792]{1,0:T(8,128)(2,1)S(1)}, bf16[64,1792]{1,0:T(8,128)(2,1)S(1)}, u32[]{:S(2)}, u32[]{:S(2)}) collective-permute-start(bf16[64,1792]{1,0:T(8,128)(2,1)S(1)} %get-tuple-element.46), channel_id=1, source_target_pairs={{0,8},{4,12},{8,0},{12,4},{1,9},{5,13},{9,1},{13,5},{2,10},{6,14},... | collective-permute-start | bytes 688136 | tf_op jit(solution)/shard_map/ppermute | solution.py:399
  86.5 5.0 %collective-permute-done.26.refs_2_.refs_4_ = bf16[64,1792]{1,0:T(8,128)(2,1)S(1)} collective-permute-done((bf16[64,1792]{1,0:T(8,128)(2,1)S(1)}, bf16[64,1792]{1,0:T(8,128)(2,1)S(1)}, u32[]{:S(2)}, u32[]{:S(2)}) %collective-permute-start.26) | collective-permute-done | bytes 229408 | tf_op jit(solution)/shard_map/ppermute | solution.py:402
  91.5 1.3 %collective-permute-done.28.refs_1_ = bf16[64,1792]{1,0:T(8,128)(2,1)S(1)} collective-permute-done((bf16[64,1792]{1,0:T(8,128)(2,1)S(1)}, bf16[64,1792]{1,0:T(8,128)(2,1)S(1)}, u32[]{:S(2)}, u32[]{:S(2)}) %collective-permute-start.28) | collective-permute-done | bytes 229408 | tf_op jit(solution)/shard_map/ppermute | solution.py:399
  92.8 1.7 %collective-permute-start.32 = (bf16[64,1792]{1,0:T(8,128)(2,1)S(1)}, bf16[64,1792]{1,0:T(8,128)(2,1)S(1)}, u32[]{:S(2)}, u32[]{:S(2)}) collective-permute-start(bf16[64,1792]{1,0:T(8,128)(2,1)S(1)} %add.73.refs_5_), channel_id=1, source_target_pairs={{0,1},{1,0},{2,3},{3,2},{4,5},{5,4},{6,7},{7,6},{8,9},{9,8},{10,11... | collective-permute-start | bytes 688136 | tf_op jit(solution)/shard_map/ppermute | solution.py:402
  94.6 0.8 collective-permute-start.29
  95.4 2.2 %collective-permute-done.31.refs_1_ = bf16[64,1792]{1,0:T(8,128)(2,1)S(1)} collective-permute-done((bf16[64,1792]{1,0:T(8,128)(2,1)S(1)}, bf16[64,1792]{1,0:T(8,128)(2,1)S(1)}, u32[]{:S(2)}, u32[]{:S(2)}) %collective-permute-start.31) | collective-permute-done | bytes 229408 | tf_op jit(solution)/shard_map/ppermute | solution.py:399
  97.7 1.6 %collective-permute-done.32.refs_2_ = bf16[64,1792]{1,0:T(8,128)(2,1)S(1)} collective-permute-done((bf16[64,1792]{1,0:T(8,128)(2,1)S(1)}, bf16[64,1792]{1,0:T(8,128)(2,1)S(1)}, u32[]{:S(2)}, u32[]{:S(2)}) %collective-permute-start.32) | collective-permute-done | bytes 229408 | tf_op jit(solution)/shard_map/ppermute | solution.py:402
  99.4 3.3 %collective-permute-start.33 = (bf16[64,1792]{1,0:T(8,128)(2,1)S(1)}, bf16[64,1792]{1,0:T(8,128)(2,1)S(1)}, u32[]{:S(2)}, u32[]{:S(2)}) collective-permute-start(bf16[64,1792]{1,0:T(8,128)(2,1)S(1)} %add.76), channel_id=1, source_target_pairs={{0,2},{1,3},{2,0},{3,1},{4,6},{5,7},{6,4},{7,5},{8,10},{9,11},{10,... | collective-permute-start | bytes 688136 | tf_op jit(solution)/shard_map/ppermute | solution.py:402
  103.0 7.8 %collective-permute-done.33.refs_2_ = bf16[64,1792]{1,0:T(8,128)(2,1)S(1)} collective-permute-done((bf16[64,1792]{1,0:T(8,128)(2,1)S(1)}, bf16[64,1792]{1,0:T(8,128)(2,1)S(1)}, u32[]{:S(2)}, u32[]{:S(2)}) %collective-permute-start.33) | collective-permute-done | bytes 229408 | tf_op jit(solution)/shard_map/ppermute | solution.py:402
  110.9 0.6 collective-permute-done.34.refs_1_
  111.6 0.7 add.78
  (67 shorter events, 3.7 us)
Async XLA Ops:
  0.6 16.0 %copy-start = (bf16[256,1792]{1,0:T(8,128)(2,1)S(1)}, bf16[256,1792]{1,0:T(8,128)(2,1)}, u32[]{:S(2)}) copy-start(bf16[256,1792]{1,0:T(8,128)(2,1)} %param.21) | copy-start | bytes 2752516
  0.8 15.7 %copy-start.4 = (f32[256,2]{0,1:T(2,128)S(1)}, f32[256,2]{0,1:T(2,128)}, u32[]{:S(2)}) copy-start(f32[256,2]{0,1:T(2,128)} %param.24) | copy-start | bytes 6148
  0.8 15.7 %copy-start.5 = (s32[256,2]{0,1:T(2,128)S(1)}, s32[256,2]{0,1:T(2,128)}, u32[]{:S(2)}) copy-start(s32[256,2]{0,1:T(2,128)} %param.23) | copy-start | bytes 6148
  0.8 15.9 %copy-start.3 = (f32[1792]{0:T(1024)S(1)}, f32[1792]{0:T(1024)}, u32[]{:S(2)}) copy-start(f32[1792]{0:T(1024)} %param.22) | copy-start | bytes 21508
  13.4 7.3 %collective-permute-start = (bf16[64,1024]{1,0:T(8,128)(2,1)S(1)}, bf16[64,1024]{1,0:T(8,128)(2,1)S(1)}, u32[]{:S(2)}, u32[]{:S(2)}) collective-permute-start(bf16[64,1024]{1,0:T(8,128)(2,1)S(1)} %attention.1.refs_1_.refs_0_), channel_id=1, source_target_pairs={{0,4},{4,0},{8,12},{12,8},{1,5},{5,1},{9,13},{13,9},{2,6},{6,2},{1... | collective-permute-start | bytes 393224 | tf_op jit(solution)/shard_map/ppermute | solution.py:395
  13.9 6.7 %collective-permute-start.1 = (bf16[64,1024]{1,0:T(8,128)(2,1)S(1)}, bf16[64,1024]{1,0:T(8,128)(2,1)S(1)}, u32[]{:S(2)}, u32[]{:S(2)}) collective-permute-start(bf16[64,1024]{1,0:T(8,128)(2,1)S(1)} %attention.1.refs_1_.refs_0_), channel_id=1, source_target_pairs={{0,8},{4,12},{8,0},{12,4},{1,9},{5,13},{9,1},{13,5},{2,10},{6,14},... | collective-permute-start | bytes 393224 | tf_op jit(solution)/shard_map/ppermute | solution.py:399
  20.6 1.4 %collective-permute-start.2 = (bf16[64,1024]{1,0:T(8,128)(2,1)S(1)}, bf16[64,1024]{1,0:T(8,128)(2,1)S(1)}, u32[]{:S(2)}, u32[]{:S(2)}) collective-permute-start(bf16[64,1024]{1,0:T(8,128)(2,1)S(1)} %add.64.refs_2_), channel_id=1, source_target_pairs={{0,4},{4,0},{8,12},{12,8},{1,5},{5,1},{9,13},{13,9},{2,6},{6,2},{1... | collective-permute-start | bytes 393224 | tf_op jit(solution)/shard_map/ppermute | solution.py:395
  23.8 7.9 %collective-permute-start.3 = (bf16[64,1792]{1,0:T(8,128)(2,1)S(1)}, bf16[64,1792]{1,0:T(8,128)(2,1)S(1)}, u32[]{:S(2)}, u32[]{:S(2)}) collective-permute-start(bf16[64,1792]{1,0:T(8,128)(2,1)S(1)} %get-tuple-element.30), channel_id=1, source_target_pairs={{0,1},{1,0},{2,3},{3,2},{4,5},{5,4},{6,7},{7,6},{8,9},{9,8},{10,11... | collective-permute-start | bytes 688136 | tf_op jit(solution)/shard_map/ppermute | solution.py:402
  28.9 11.7 %collective-permute-start.5 = (bf16[64,1792]{1,0:T(8,128)(2,1)S(1)}, bf16[64,1792]{1,0:T(8,128)(2,1)S(1)}, u32[]{:S(2)}, u32[]{:S(2)}) collective-permute-start(bf16[64,1792]{1,0:T(8,128)(2,1)S(1)} %add.66), channel_id=1, source_target_pairs={{0,1},{1,0},{2,3},{3,2},{4,5},{5,4},{6,7},{7,6},{8,9},{9,8},{10,11... | collective-permute-start | bytes 688136 | tf_op jit(solution)/shard_map/ppermute | solution.py:402
  31.7 12.8 %collective-permute-start.4 = (bf16[64,1792]{1,0:T(8,128)(2,1)S(1)}, bf16[64,1792]{1,0:T(8,128)(2,1)S(1)}, u32[]{:S(2)}, u32[]{:S(2)}) collective-permute-start(bf16[64,1792]{1,0:T(8,128)(2,1)S(1)} %add.65), channel_id=1, source_target_pairs={{0,2},{1,3},{2,0},{3,1},{4,6},{5,7},{6,4},{7,5},{8,10},{9,11},{10,... | collective-permute-start | bytes 688136 | tf_op jit(solution)/shard_map/ppermute | solution.py:402
  34.7 3.6 %collective-permute-start.7 = (f32[1,1792]{1,0:T(1,128)S(1)}, f32[1,1792]{1,0:T(1,128)S(1)}, u32[]{:S(2)}, u32[]{:S(2)}) collective-permute-start(f32[1,1792]{1,0:T(1,128)S(1)} %reshape.7.refs_4_.refs_8_), channel_id=1, source_target_pairs={{0,8},{4,12},{8,0},{12,4},{1,9},{5,13},{9,1},{13,5},{2,10},{6,14},... | collective-permute-start | bytes 21512 | tf_op jit(solution)/shard_map/ppermute | solution.py:399
  36.2 2.1 %collective-permute-start.6 = (f32[1,1792]{1,0:T(1,128)S(1)}, f32[1,1792]{1,0:T(1,128)S(1)}, u32[]{:S(2)}, u32[]{:S(2)}) collective-permute-start(f32[1,1792]{1,0:T(1,128)S(1)} %reshape.7.refs_4_.refs_8_), channel_id=1, source_target_pairs={{0,4},{4,0},{8,12},{12,8},{1,5},{5,1},{9,13},{13,9},{2,6},{6,2},{1... | collective-permute-start | bytes 21512 | tf_op jit(solution)/shard_map/ppermute | solution.py:395
  38.4 1.2 %collective-permute-start.8 = (f32[1,1792]{1,0:T(1,128)S(1)}, f32[1,1792]{1,0:T(1,128)S(1)}, u32[]{:S(2)}, u32[]{:S(2)}) collective-permute-start(f32[1,1792]{1,0:T(1,128)S(1)} %collective-permute-done.7.refs_10_.refs_8_), channel_id=1, source_target_pairs={{0,4},{4,0},{8,12},{12,8},{1,5},{5,1},{9,13},{13,9},{2,6},{6,2},{1... | collective-permute-start | bytes 21512 | tf_op jit(solution)/shard_map/ppermute | solution.py:395
  45.4 10.3 %collective-permute-start.9 = (bf16[64,1792]{1,0:T(8,128)(2,1)S(1)}, bf16[64,1792]{1,0:T(8,128)(2,1)S(1)}, u32[]{:S(2)}, u32[]{:S(2)}) collective-permute-start(bf16[64,1792]{1,0:T(8,128)(2,1)S(1)} %get-tuple-element.33.refs_1_.refs_6_), channel_id=1, source_target_pairs={{0,2},{1,3},{2,0},{3,1},{4,6},{5,7},{6,4},{7,5},{8,10},{9,11},{10,... | collective-permute-start | bytes 688136 | tf_op jit(solution)/shard_map/ppermute | solution.py:402
  45.4 10.3 %collective-permute-start.10 = (bf16[64,1792]{1,0:T(8,128)(2,1)S(1)}, bf16[64,1792]{1,0:T(8,128)(2,1)S(1)}, u32[]{:S(2)}, u32[]{:S(2)}) collective-permute-start(bf16[64,1792]{1,0:T(8,128)(2,1)S(1)} %get-tuple-element.33.refs_1_.refs_6_), channel_id=1, source_target_pairs={{0,8},{4,12},{8,0},{12,4},{1,9},{5,13},{9,1},{13,5},{2,10},{6,14},... | collective-permute-start | bytes 688136 | tf_op jit(solution)/shard_map/ppermute | solution.py:399
  46.9 10.6 %collective-permute-start.15 = (bf16[64,1792]{1,0:T(8,128)(2,1)S(1)}, bf16[64,1792]{1,0:T(8,128)(2,1)S(1)}, u32[]{:S(2)}, u32[]{:S(2)}) collective-permute-start(bf16[64,1792]{1,0:T(8,128)(2,1)S(1)} %get-tuple-element.33.refs_1_.refs_6_), channel_id=1, source_target_pairs={{0,1},{1,0},{2,3},{3,2},{4,5},{5,4},{6,7},{7,6},{8,9},{9,8},{10,11... | collective-permute-start | bytes 688136 | tf_op jit(solution)/shard_map/ppermute | solution.py:402
  55.7 6.3 %collective-permute-start.11 = (bf16[64,1792]{1,0:T(8,128)(2,1)S(1)}, bf16[64,1792]{1,0:T(8,128)(2,1)S(1)}, u32[]{:S(2)}, u32[]{:S(2)}) collective-permute-start(bf16[64,1792]{1,0:T(8,128)(2,1)S(1)} %add.68), channel_id=1, source_target_pairs={{0,1},{1,0},{2,3},{3,2},{4,5},{5,4},{6,7},{7,6},{8,9},{9,8},{10,11... | collective-permute-start | bytes 688136 | tf_op jit(solution)/shard_map/ppermute | solution.py:402
  56.1 5.8 %collective-permute-start.17 = (bf16[64,1792]{1,0:T(8,128)(2,1)S(1)}, bf16[64,1792]{1,0:T(8,128)(2,1)S(1)}, u32[]{:S(2)}, u32[]{:S(2)}) collective-permute-start(bf16[64,1792]{1,0:T(8,128)(2,1)S(1)} %get-tuple-element.33.refs_1_.refs_6_), channel_id=1, source_target_pairs={{0,4},{4,0},{8,12},{12,8},{1,5},{5,1},{9,13},{13,9},{2,6},{6,2},{1... | collective-permute-start | bytes 688136 | tf_op jit(solution)/shard_map/ppermute | solution.py:395
  56.2 7.2 %collective-permute-start.14 = (bf16[64,1792]{1,0:T(8,128)(2,1)S(1)}, bf16[64,1792]{1,0:T(8,128)(2,1)S(1)}, u32[]{:S(2)}, u32[]{:S(2)}) collective-permute-start(bf16[64,1792]{1,0:T(8,128)(2,1)S(1)} %collective-permute-done.9.refs_0_.refs_2_), channel_id=1, source_target_pairs={{0,4},{4,0},{8,12},{12,8},{1,5},{5,1},{9,13},{13,9},{2,6},{6,2},{1... | collective-permute-start | bytes 688136 | tf_op jit(solution)/shard_map/ppermute | solution.py:395
  57.5 6.9 %collective-permute-start.16 = (bf16[64,1792]{1,0:T(8,128)(2,1)S(1)}, bf16[64,1792]{1,0:T(8,128)(2,1)S(1)}, u32[]{:S(2)}, u32[]{:S(2)}) collective-permute-start(bf16[64,1792]{1,0:T(8,128)(2,1)S(1)} %collective-permute-done.15.refs_4_), channel_id=1, source_target_pairs={{0,4},{4,0},{8,12},{12,8},{1,5},{5,1},{9,13},{13,9},{2,6},{6,2},{1... | collective-permute-start | bytes 688136 | tf_op jit(solution)/shard_map/ppermute | solution.py:395
  57.5 8.4 %collective-permute-start.19 = (bf16[64,1792]{1,0:T(8,128)(2,1)S(1)}, bf16[64,1792]{1,0:T(8,128)(2,1)S(1)}, u32[]{:S(2)}, u32[]{:S(2)}) collective-permute-start(bf16[64,1792]{1,0:T(8,128)(2,1)S(1)} %collective-permute-done.9.refs_0_.refs_2_), channel_id=1, source_target_pairs={{0,8},{4,12},{8,0},{12,4},{1,9},{5,13},{9,1},{13,5},{2,10},{6,14},... | collective-permute-start | bytes 688136 | tf_op jit(solution)/shard_map/ppermute | solution.py:399
  62.0 3.9 %collective-permute-start.13 = (bf16[64,1792]{1,0:T(8,128)(2,1)S(1)}, bf16[64,1792]{1,0:T(8,128)(2,1)S(1)}, u32[]{:S(2)}, u32[]{:S(2)}) collective-permute-start(bf16[64,1792]{1,0:T(8,128)(2,1)S(1)} %collective-permute-done.11.refs_0_.refs_1_), channel_id=1, source_target_pairs={{0,4},{4,0},{8,12},{12,8},{1,5},{5,1},{9,13},{13,9},{2,6},{6,2},{1... | collective-permute-start | bytes 688136 | tf_op jit(solution)/shard_map/ppermute | solution.py:395
  62.0 11.9 %collective-permute-start.12 = (bf16[64,1792]{1,0:T(8,128)(2,1)S(1)}, bf16[64,1792]{1,0:T(8,128)(2,1)S(1)}, u32[]{:S(2)}, u32[]{:S(2)}) collective-permute-start(bf16[64,1792]{1,0:T(8,128)(2,1)S(1)} %collective-permute-done.11.refs_0_.refs_1_), channel_id=1, source_target_pairs={{0,8},{4,12},{8,0},{12,4},{1,9},{5,13},{9,1},{13,5},{2,10},{6,14},... | collective-permute-start | bytes 688136 | tf_op jit(solution)/shard_map/ppermute | solution.py:399
  63.3 11.2 %collective-permute-start.21 = (bf16[64,1792]{1,0:T(8,128)(2,1)S(1)}, bf16[64,1792]{1,0:T(8,128)(2,1)S(1)}, u32[]{:S(2)}, u32[]{:S(2)}) collective-permute-start(bf16[64,1792]{1,0:T(8,128)(2,1)S(1)} %add.70), channel_id=1, source_target_pairs={{0,1},{1,0},{2,3},{3,2},{4,5},{5,4},{6,7},{7,6},{8,9},{9,8},{10,11... | collective-permute-start | bytes 688136 | tf_op jit(solution)/shard_map/ppermute | solution.py:402
  64.4 10.2 %collective-permute-start.23 = (bf16[64,1792]{1,0:T(8,128)(2,1)S(1)}, bf16[64,1792]{1,0:T(8,128)(2,1)S(1)}, u32[]{:S(2)}, u32[]{:S(2)}) collective-permute-start(bf16[64,1792]{1,0:T(8,128)(2,1)S(1)} %collective-permute-done.10.refs_1_.refs_0_.refs_6_), channel_id=1, source_target_pairs={{0,4},{4,0},{8,12},{12,8},{1,5},{5,1},{9,13},{13,9},{2,6},{6,2},{1... | collective-permute-start | bytes 688136 | tf_op jit(solution)/shard_map/ppermute | solution.py:395
  65.9 8.7 %collective-permute-start.20 = (bf16[64,1792]{1,0:T(8,128)(2,1)S(1)}, bf16[64,1792]{1,0:T(8,128)(2,1)S(1)}, u32[]{:S(2)}, u32[]{:S(2)}) collective-permute-start(bf16[64,1792]{1,0:T(8,128)(2,1)S(1)} %collective-permute-done.19.refs_2_), channel_id=1, source_target_pairs={{0,4},{4,0},{8,12},{12,8},{1,5},{5,1},{9,13},{13,9},{2,6},{6,2},{1... | collective-permute-start | bytes 688136 | tf_op jit(solution)/shard_map/ppermute | solution.py:395
  71.0 2.9 %copy-start.2 = (bf16[1,512,7168]{2,1,0:T(8,128)(2,1)}, bf16[1,512,7168]{2,1,0:T(8,128)(2,1)S(1)}, u32[]{:S(2)}) copy-start(bf16[1,512,7168]{2,1,0:T(8,128)(2,1)S(1)} %get-tuple-element.37.down) | copy-start | bytes 22020100
  73.9 4.9 %slice-start = ((s8[7340032]{0:T(1024)(128)(4,1)}), s8[4194304]{0:T(1024)(128)(4,1)S(1)}, s32[]{:S(2)}) async-start(s8[7340032]{0:T(1024)(128)(4,1)} %bitcast.9), calls=%async_computation | async-start | bytes 8388608
  73.9 1.7 %collective-permute-start.18 = (bf16[64,1792]{1,0:T(8,128)(2,1)S(1)}, bf16[64,1792]{1,0:T(8,128)(2,1)S(1)}, u32[]{:S(2)}, u32[]{:S(2)}) collective-permute-start(bf16[64,1792]{1,0:T(8,128)(2,1)S(1)} %add.69), channel_id=1, source_target_pairs={{0,4},{4,0},{8,12},{12,8},{1,5},{5,1},{9,13},{13,9},{2,6},{6,2},{1... | collective-permute-start | bytes 688136 | tf_op jit(solution)/shard_map/ppermute | solution.py:395
  74.5 1.5 %collective-permute-start.22 = (bf16[64,1792]{1,0:T(8,128)(2,1)S(1)}, bf16[64,1792]{1,0:T(8,128)(2,1)S(1)}, u32[]{:S(2)}, u32[]{:S(2)}) collective-permute-start(bf16[64,1792]{1,0:T(8,128)(2,1)S(1)} %collective-permute-done.21.refs_4_), channel_id=1, source_target_pairs={{0,4},{4,0},{8,12},{12,8},{1,5},{5,1},{9,13},{13,9},{2,6},{6,2},{1... | collective-permute-start | bytes 688136 | tf_op jit(solution)/shard_map/ppermute | solution.py:395
  76.0 2.9 %slice-start.1 = ((s8[7340032]{0:T(1024)(128)(4,1)}), s8[3145728]{0:T(1024)(128)(4,1)S(1)}, s32[]{:S(2)}) async-start(s8[7340032]{0:T(1024)(128)(4,1)} %bitcast.9), calls=%async_computation.1 | async-start | bytes 6291456
  78.9 33.4 %copy-start.1 = (bf16[256,1792]{1,0:T(8,128)(2,1)S(1)}, bf16[256,1792]{1,0:T(8,128)(2,1)}, u32[]{:S(2)}) copy-start(bf16[256,1792]{1,0:T(8,128)(2,1)} %param.21) | copy-start | bytes 2752516
  81.6 1.9 %collective-permute-start.25 = (bf16[128,1792]{1,0:T(8,128)(2,1)S(1)}, bf16[128,1792]{1,0:T(8,128)(2,1)S(1)}, u32[]{:S(2)}, u32[]{:S(2)}) collective-permute-start(bf16[128,1792]{1,0:T(8,128)(2,1)S(1)} %get-tuple-element.41), channel_id=1, source_target_pairs={{0,4},{4,0},{8,12},{12,8},{1,5},{5,1},{9,13},{13,9},{2,6},{6,2},{1... | collective-permute-start | bytes 1376264 | tf_op jit(solution)/shard_map/ppermute | solution.py:395
  82.0 2.2 %collective-permute-start.27 = (bf16[128,1792]{1,0:T(8,128)(2,1)S(1)}, bf16[128,1792]{1,0:T(8,128)(2,1)S(1)}, u32[]{:S(2)}, u32[]{:S(2)}) collective-permute-start(bf16[128,1792]{1,0:T(8,128)(2,1)S(1)} %get-tuple-element.44), channel_id=1, source_target_pairs={{0,4},{4,0},{8,12},{12,8},{1,5},{5,1},{9,13},{13,9},{2,6},{6,2},{1... | collective-permute-start | bytes 1376264 | tf_op jit(solution)/shard_map/ppermute | solution.py:395
  82.2 4.0 %collective-permute-start.30 = (bf16[128,1792]{1,0:T(8,128)(2,1)S(1)}, bf16[128,1792]{1,0:T(8,128)(2,1)S(1)}, u32[]{:S(2)}, u32[]{:S(2)}) collective-permute-start(bf16[128,1792]{1,0:T(8,128)(2,1)S(1)} %get-tuple-element.50), channel_id=1, source_target_pairs={{0,4},{4,0},{8,12},{12,8},{1,5},{5,1},{9,13},{13,9},{2,6},{6,2},{1... | collective-permute-start | bytes 1376264 | tf_op jit(solution)/shard_map/ppermute | solution.py:395
  82.5 12.0 %collective-permute-start.24 = (bf16[128,1792]{1,0:T(8,128)(2,1)S(1)}, bf16[128,1792]{1,0:T(8,128)(2,1)S(1)}, u32[]{:S(2)}, u32[]{:S(2)}) collective-permute-start(bf16[128,1792]{1,0:T(8,128)(2,1)S(1)} %get-tuple-element.39), channel_id=1, source_target_pairs={{0,4},{4,0},{8,12},{12,8},{1,5},{5,1},{9,13},{13,9},{2,6},{6,2},{1... | collective-permute-start | bytes 1376264 | tf_op jit(solution)/shard_map/ppermute | solution.py:395
  83.6 7.9 %collective-permute-start.26 = (bf16[64,1792]{1,0:T(8,128)(2,1)S(1)}, bf16[64,1792]{1,0:T(8,128)(2,1)S(1)}, u32[]{:S(2)}, u32[]{:S(2)}) collective-permute-start(bf16[64,1792]{1,0:T(8,128)(2,1)S(1)} %get-tuple-element.42), channel_id=1, source_target_pairs={{0,1},{1,0},{2,3},{3,2},{4,5},{5,4},{6,7},{7,6},{8,9},{9,8},{10,11... | collective-permute-start | bytes 688136 | tf_op jit(solution)/shard_map/ppermute | solution.py:402
  84.3 8.5 %collective-permute-start.28 = (bf16[64,1792]{1,0:T(8,128)(2,1)S(1)}, bf16[64,1792]{1,0:T(8,128)(2,1)S(1)}, u32[]{:S(2)}, u32[]{:S(2)}) collective-permute-start(bf16[64,1792]{1,0:T(8,128)(2,1)S(1)} %get-tuple-element.46), channel_id=1, source_target_pairs={{0,8},{4,12},{8,0},{12,4},{1,9},{5,13},{9,1},{13,5},{2,10},{6,14},... | collective-permute-start | bytes 688136 | tf_op jit(solution)/shard_map/ppermute | solution.py:399
  86.3 11.4 %collective-permute-start.31 = (bf16[64,1792]{1,0:T(8,128)(2,1)S(1)}, bf16[64,1792]{1,0:T(8,128)(2,1)S(1)}, u32[]{:S(2)}, u32[]{:S(2)}) collective-permute-start(bf16[64,1792]{1,0:T(8,128)(2,1)S(1)} %get-tuple-element.52), channel_id=1, source_target_pairs={{0,8},{4,12},{8,0},{12,4},{1,9},{5,13},{9,1},{13,5},{2,10},{6,14},... | collective-permute-start | bytes 688136 | tf_op jit(solution)/shard_map/ppermute | solution.py:399
  92.8 6.5 %collective-permute-start.32 = (bf16[64,1792]{1,0:T(8,128)(2,1)S(1)}, bf16[64,1792]{1,0:T(8,128)(2,1)S(1)}, u32[]{:S(2)}, u32[]{:S(2)}) collective-permute-start(bf16[64,1792]{1,0:T(8,128)(2,1)S(1)} %add.73.refs_5_), channel_id=1, source_target_pairs={{0,1},{1,0},{2,3},{3,2},{4,5},{5,4},{6,7},{7,6},{8,9},{9,8},{10,11... | collective-permute-start | bytes 688136 | tf_op jit(solution)/shard_map/ppermute | solution.py:402
  94.6 8.4 %collective-permute-start.29 = (bf16[64,1792]{1,0:T(8,128)(2,1)S(1)}, bf16[64,1792]{1,0:T(8,128)(2,1)S(1)}, u32[]{:S(2)}, u32[]{:S(2)}) collective-permute-start(bf16[64,1792]{1,0:T(8,128)(2,1)S(1)} %get-tuple-element.48), channel_id=1, source_target_pairs={{0,8},{4,12},{8,0},{12,4},{1,9},{5,13},{9,1},{13,5},{2,10},{6,14},... | collective-permute-start | bytes 688136 | tf_op jit(solution)/shard_map/ppermute | solution.py:399
  99.4 11.5 %collective-permute-start.33 = (bf16[64,1792]{1,0:T(8,128)(2,1)S(1)}, bf16[64,1792]{1,0:T(8,128)(2,1)S(1)}, u32[]{:S(2)}, u32[]{:S(2)}) collective-permute-start(bf16[64,1792]{1,0:T(8,128)(2,1)S(1)} %add.76), channel_id=1, source_target_pairs={{0,2},{1,3},{2,0},{3,1},{4,6},{5,7},{6,4},{7,5},{8,10},{9,11},{10,... | collective-permute-start | bytes 688136 | tf_op jit(solution)/shard_map/ppermute | solution.py:402
  102.7 8.9 %collective-permute-start.34 = (bf16[64,1792]{1,0:T(8,128)(2,1)S(1)}, bf16[64,1792]{1,0:T(8,128)(2,1)S(1)}, u32[]{:S(2)}, u32[]{:S(2)}) collective-permute-start(bf16[64,1792]{1,0:T(8,128)(2,1)S(1)} %get-tuple-element.53), channel_id=1, source_target_pairs={{0,1},{1,0},{2,3},{3,2},{4,5},{5,4},{6,7},{7,6},{8,9},{9,8},{10,11... | collective-permute-start | bytes 688136 | tf_op jit(solution)/shard_map/ppermute | solution.py:402

commit v19 on v16

--- a/solution.py
+++ b/solution.py
@@ -434,7 +434,7 @@
         low = k & -k
         source = rows_of[k ^ low]
         if k == tp_count - 1:
-            (source,) = add([[(source, 0)]], block_rows, crossed)
+            (source,) = add([[(source, 0)]], block_rows, crossed + [down_weight])
         rows_of[k] = from_tp(source, low)
     slots = list(reversed(range(tp_count)))
     near = {k: [rows_of[k], from_core(rows_of[k])] for k in slots}

time: 109 us -> 109 us (level)
    ppermute x8, waiting for transfers between devices: 9.82 us -> 12.4 us  [from_chip(): lax.ppermute(value, 'ep', [(i, (i + step) % ep_count) for i in range(ep_c...]
    ppermute x11, waiting for transfers between devices: 29.5 us -> 27.6 us  [from_tp(): return lax.ppermute(value, 'tp', [(i, i ^ bits) for i in range(tp_count)])]
  transfers between devices with their start and end apart: 35 -> 35, of which waited for: 19 -> 21; matrix products, arithmetic and copies ran while one was open for 0% -> 0% of each run, Pallas kernels for 14% -> 14%
where the time goes in v19:
time: 109 us
  waiting for transfers between devices  43.6 us (40%)
  Pallas kernels  36.5 us (33%)
  starting transfers between devices  27.7 us (25%)
    ppermute x11, waiting for transfers between devices, from_tp(): return lax.ppermute(value, 'tp', [(i, i ^ bits) for i in range(tp_count)])  27.6 us
    ppermute x11, starting transfers between devices, from_tp(): return lax.ppermute(value, 'tp', [(i, i ^ bits) for i in range(tp_count)])  15.3 us
    pallas_call x1, Pallas kernels, attend(): pl.pallas_call(functools.partial(attention_kernel, step_rows, pieces, ahe...  12.6 us
    ppermute x8, waiting for transfers between devices, from_chip(): lax.ppermute(value, 'ep', [(i, (i + step) % ep_count) for i in range(ep_c...  12.4 us
    pallas_call x4, Pallas kernels, fetch(): pl.pallas_call(functools.partial(fetch_kernel, parts), out_shape=pltpu.VM...  11.6 us
    ppermute x8, starting transfers between devices, from_chip(): lax.ppermute(value, 'ep', [(i, (i + step) % ep_count) for i in range(ep_c...  9.64 us
    pallas_call x2, Pallas kernels, activate(): pl.pallas_call(functools.partial(gate_kernel, row_blocks, cores, first, c...  5.52 us
    ppermute x16, waiting for transfers between devices, from_core(): return lax.ppermute(value, 'ep', [(i, i ^ 1) for i in range(ep_count)])  3.59 us
  transfers between devices with their start and end apart: 35, of which 21 were waited for; matrix products, arithmetic and copies ran while one was open for 0% of the time, Pallas kernels for 14%

profile of v19, /device:TPU:0, one launch (start us, length us, event | category | flops | bytes accessed | tf_op | source)
XLA Modules:
  0.0 109.2 jit_solution(11915337046662607347)
XLA Ops:
  0.8 12.6 %attention.1.refs_1_.refs_0_ = bf16[64,1024]{1,0:T(8,128)(2,1)S(1)} custom-call(s32[64]{0:T(128)} %lengths.1, bf16[64,8,512]{2,1,0:T(8,128)(2,1)} %q_ref.1, bf16[64,512]{1,0:T(8,128)(2,1)} %qr_ref.1, bf16[64,256,512]{2,1,0:T(8,128)(2,1)} %k_hbm.1, bf16[64,64,256]{2,1,0:T(8,128)(2,1)} %kr_hbm.1, bf16[8,512,128]{2,1,0:T(8,128)(2,1)} %up_hbm.1, ...), custom_call_target="tpu_custom_call" | custom-call | flops 4294967296 | bytes 16777216 | tf_op jit(solution)/shard_map/attention/pallas_call | solution.py:135
  13.4 0.5 collective-permute-start
  13.9 2.6 %collective-permute-start.1 = (bf16[64,1024]{1,0:T(8,128)(2,1)S(1)}, bf16[64,1024]{1,0:T(8,128)(2,1)S(1)}, u32[]{:S(2)}, u32[]{:S(2)}) collective-permute-start(bf16[64,1024]{1,0:T(8,128)(2,1)S(1)} %attention.1.refs_1_.refs_0_), channel_id=1, source_target_pairs={{0,8},{4,12},{8,0},{12,4},{1,9},{5,13},{9,1},{13,5},{2,10},{6,14},... | collective-permute-start | bytes 393224 | tf_op jit(solution)/shard_map/ppermute | solution.py:387
  16.7 2.0 %fetch.4.refs_1_.refs_4_ = bf16[1024,1792]{1,0:T(8,128)(2,1)S(1)} custom-call(bf16[1024,1792]{1,0:T(8,128)(2,1)} %refs_0_.4, bf16[64,1024]{1,0:T(8,128)(2,1)S(1)} %attention.1.refs_1_.refs_0_, f32[256,1]{1,0:T(8,128)S(1)} %copy.16.refs_2_.row_weight, bf16[64,1792]{1,0:T(8,128)(2,1)S(1)} %constant_dynamic-slice_fusion.refs_3_.refs_7_, ...), custom_call_target="tpu_custom_call" | custom-call | bytes 7340032 | tf_op jit(solution)/shard_map/fetch/pallas_call | solution.py:38
  18.8 1.8 %collective-permute-done.1.refs_0_ = bf16[64,1024]{1,0:T(8,128)(2,1)S(1)} collective-permute-done((bf16[64,1024]{1,0:T(8,128)(2,1)S(1)}, bf16[64,1024]{1,0:T(8,128)(2,1)S(1)}, u32[]{:S(2)}, u32[]{:S(2)}) %collective-permute-start.1) | collective-permute-done | bytes 131104 | tf_op jit(solution)/shard_map/ppermute | solution.py:387
  20.7 1.3 %collective-permute-done.2.refs_3_ = bf16[64,1024]{1,0:T(8,128)(2,1)S(1)} collective-permute-done((bf16[64,1024]{1,0:T(8,128)(2,1)S(1)}, bf16[64,1024]{1,0:T(8,128)(2,1)S(1)}, u32[]{:S(2)}, u32[]{:S(2)}) %collective-permute-start.2) | collective-permute-done | bytes 131104 | tf_op jit(solution)/shard_map/ppermute | solution.py:383
  22.0 1.8 %projection.1 = (bf16[64,1792]{1,0:T(8,128)(2,1)S(1)}, bf16[64,1792]{1,0:T(8,128)(2,1)S(1)}, bf16[64,1792]{1,0:T(8,128)(2,1)S(1)}, bf16[64,1792]{1,0:T(8,128)(2,1)S(1)}) custom-call(s32[8]{0:T(128)S(1)} %stack.35.refs_0_.places, bf16[64,1024]{1,0:T(8,128)(2,1)S(1)} %attention.1.refs_1_.refs_0_, bf16[64,1024]{1,0:T(8,128)(2,1)S(1)} %collective-permute-done.refs_1_, ...), custom_call_target="tpu_custom_call" | custom-call | flops 939524096 | bytes 4194304 | tf_op jit(solution)/shard_map/projection/pallas_call | solution.py:200
  23.8 1.9 %collective-permute-start.3 = (bf16[64,1792]{1,0:T(8,128)(2,1)S(1)}, bf16[64,1792]{1,0:T(8,128)(2,1)S(1)}, u32[]{:S(2)}, u32[]{:S(2)}) collective-permute-start(bf16[64,1792]{1,0:T(8,128)(2,1)S(1)} %get-tuple-element.29), channel_id=1, source_target_pairs={{0,1},{1,0},{2,3},{3,2},{4,5},{5,4},{6,7},{7,6},{8,9},{9,8},{10,11... | collective-permute-start | bytes 688136 | tf_op jit(solution)/shard_map/ppermute | solution.py:390
  25.7 3.2 %fetch.5.refs_1_.refs_12_.refs_10_ = bf16[1,7168,512]{2,1,0:T(8,128)(2,1)S(1)} custom-call(bf16[1,7168,512]{2,1,0:T(8,128)(2,1)} %refs_0_.5, bf16[64,1792]{1,0:T(8,128)(2,1)S(1)} %get-tuple-element.27.refs_1_.refs_0_.refs_4_), custom_call_target="tpu_custom_call" | custom-call | bytes 14680064 | tf_op jit(solution)/shard_map/fetch/pallas_call | solution.py:38
  29.1 2.5 %collective-permute-done.3.refs_1_ = bf16[64,1792]{1,0:T(8,128)(2,1)S(1)} collective-permute-done((bf16[64,1792]{1,0:T(8,128)(2,1)S(1)}, bf16[64,1792]{1,0:T(8,128)(2,1)S(1)}, u32[]{:S(2)}, u32[]{:S(2)}) %collective-permute-start.3) | collective-permute-done | bytes 229408 | tf_op jit(solution)/shard_map/ppermute | solution.py:390
  31.7 3.0 %collective-permute-start.4 = (bf16[64,1792]{1,0:T(8,128)(2,1)S(1)}, bf16[64,1792]{1,0:T(8,128)(2,1)S(1)}, u32[]{:S(2)}, u32[]{:S(2)}) collective-permute-start(bf16[64,1792]{1,0:T(8,128)(2,1)S(1)} %add.65), channel_id=1, source_target_pairs={{0,2},{1,3},{2,0},{3,1},{4,6},{5,7},{6,4},{7,5},{8,10},{9,11},{10,... | collective-permute-start | bytes 688136 | tf_op jit(solution)/shard_map/ppermute | solution.py:390
  34.7 1.5 %collective-permute-start.7 = (f32[1,1792]{1,0:T(1,128)S(1)}, f32[1,1792]{1,0:T(1,128)S(1)}, u32[]{:S(2)}, u32[]{:S(2)}) collective-permute-start(f32[1,1792]{1,0:T(1,128)S(1)} %reshape.7.refs_4_.refs_8_), channel_id=1, source_target_pairs={{0,8},{4,12},{8,0},{12,4},{1,9},{5,13},{9,1},{13,5},{2,10},{6,14},... | collective-permute-start | bytes 21512 | tf_op jit(solution)/shard_map/ppermute | solution.py:387
  36.2 2.1 %collective-permute-done.7.refs_10_.refs_8_ = f32[1,1792]{1,0:T(1,128)S(1)} collective-permute-done((f32[1,1792]{1,0:T(1,128)S(1)}, f32[1,1792]{1,0:T(1,128)S(1)}, u32[]{:S(2)}, u32[]{:S(2)}) %collective-permute-start.7) | collective-permute-done | bytes 7200 | tf_op jit(solution)/shard_map/ppermute | solution.py:387
  38.4 3.2 %fetch.6.refs_13_.refs_11_ = bf16[1,7168,512]{2,1,0:T(8,128)(2,1)S(1)} custom-call(bf16[1,7168,512]{2,1,0:T(8,128)(2,1)} %refs_0_.6, bf16[64,1792]{1,0:T(8,128)(2,1)S(1)} %add.66.refs_1_), custom_call_target="tpu_custom_call" | custom-call | bytes 14680064 | tf_op jit(solution)/shard_map/fetch/pallas_call | solution.py:38
  41.6 2.9 %collective-permute-done.4.refs_1_.refs_5_ = bf16[64,1792]{1,0:T(8,128)(2,1)S(1)} collective-permute-done((bf16[64,1792]{1,0:T(8,128)(2,1)S(1)}, bf16[64,1792]{1,0:T(8,128)(2,1)S(1)}, u32[]{:S(2)}, u32[]{:S(2)}) %collective-permute-start.4) | collective-permute-done | bytes 229408 | tf_op jit(solution)/shard_map/ppermute | solution.py:390
  44.5 0.8 add.67
  45.4 1.5 %collective-permute-start.10 = (bf16[64,1792]{1,0:T(8,128)(2,1)S(1)}, bf16[64,1792]{1,0:T(8,128)(2,1)S(1)}, u32[]{:S(2)}, u32[]{:S(2)}) collective-permute-start(bf16[64,1792]{1,0:T(8,128)(2,1)S(1)} %get-tuple-element.32.refs_1_.refs_6_), channel_id=1, source_target_pairs={{0,8},{4,12},{8,0},{12,4},{1,9},{5,13},{9,1},{13,5},{2,10},{6,14},... | collective-permute-start | bytes 688136 | tf_op jit(solution)/shard_map/ppermute | solution.py:387
  46.9 4.1 %collective-permute-start.15 = (bf16[64,1792]{1,0:T(8,128)(2,1)S(1)}, bf16[64,1792]{1,0:T(8,128)(2,1)S(1)}, u32[]{:S(2)}, u32[]{:S(2)}) collective-permute-start(bf16[64,1792]{1,0:T(8,128)(2,1)S(1)} %get-tuple-element.32.refs_1_.refs_6_), channel_id=1, source_target_pairs={{0,1},{1,0},{2,3},{3,2},{4,5},{5,4},{6,7},{7,6},{8,9},{9,8},{10,11... | collective-permute-start | bytes 688136 | tf_op jit(solution)/shard_map/ppermute | solution.py:390
  51.0 3.2 %fetch.7.refs_2_.refs_12_.down = bf16[1,512,7168]{2,1,0:T(8,128)(2,1)S(1)} custom-call(bf16[1,512,7168]{2,1,0:T(8,128)(2,1)} %refs_0_.7, bf16[64,1792]{1,0:T(8,128)(2,1)S(1)} %get-tuple-element.32.refs_1_.refs_6_), custom_call_target="tpu_custom_call" | custom-call | bytes 14680064 | tf_op jit(solution)/shard_map/fetch/pallas_call | solution.py:38
  54.2 2.2 %collective-permute-done.9.refs_0_.refs_2_ = bf16[64,1792]{1,0:T(8,128)(2,1)S(1)} collective-permute-done((bf16[64,1792]{1,0:T(8,128)(2,1)S(1)}, bf16[64,1792]{1,0:T(8,128)(2,1)S(1)}, u32[]{:S(2)}, u32[]{:S(2)}) %collective-permute-start.9) | collective-permute-done | bytes 229408 | tf_op jit(solution)/shard_map/ppermute | solution.py:390
  56.6 0.5 collective-permute-start.14
  57.1 1.6 %collective-permute-done.15.refs_4_ = bf16[64,1792]{1,0:T(8,128)(2,1)S(1)} collective-permute-done((bf16[64,1792]{1,0:T(8,128)(2,1)S(1)}, bf16[64,1792]{1,0:T(8,128)(2,1)S(1)}, u32[]{:S(2)}, u32[]{:S(2)}) %collective-permute-start.15) | collective-permute-done | bytes 229408 | tf_op jit(solution)/shard_map/ppermute | solution.py:390
  58.7 3.9 %collective-permute-done.11.refs_0_.refs_1_ = bf16[64,1792]{1,0:T(8,128)(2,1)S(1)} collective-permute-done((bf16[64,1792]{1,0:T(8,128)(2,1)S(1)}, bf16[64,1792]{1,0:T(8,128)(2,1)S(1)}, u32[]{:S(2)}, u32[]{:S(2)}) %collective-permute-start.11) | collective-permute-done | bytes 229408 | tf_op jit(solution)/shard_map/ppermute | solution.py:390
  62.6 1.4 %collective-permute-start.12 = (bf16[64,1792]{1,0:T(8,128)(2,1)S(1)}, bf16[64,1792]{1,0:T(8,128)(2,1)S(1)}, u32[]{:S(2)}, u32[]{:S(2)}) collective-permute-start(bf16[64,1792]{1,0:T(8,128)(2,1)S(1)} %collective-permute-done.11.refs_0_.refs_1_), channel_id=1, source_target_pairs={{0,8},{4,12},{8,0},{12,4},{1,9},{5,13},{9,1},{13,5},{2,10},{6,14},... | collective-permute-start | bytes 688136 | tf_op jit(solution)/shard_map/ppermute | solution.py:387
  64.4 2.7 %collective-permute-done.19.refs_2_ = bf16[64,1792]{1,0:T(8,128)(2,1)S(1)} collective-permute-done((bf16[64,1792]{1,0:T(8,128)(2,1)S(1)}, bf16[64,1792]{1,0:T(8,128)(2,1)S(1)}, u32[]{:S(2)}, u32[]{:S(2)}) %collective-permute-start.19) | collective-permute-done | bytes 229408 | tf_op jit(solution)/shard_map/ppermute | solution.py:387
  67.1 2.7 %activate.2 = (f32[256,512]{1,0:T(8,128)S(1)}, f32[256,512]{1,0:T(8,128)S(1)}, f32[256,1]{1,0:T(8,128)S(1)}) custom-call(s32[8]{0:T(128)S(1)} %stack.35.refs_0_.places, bf16[64,1792]{1,0:T(8,128)(2,1)S(1)} %collective-permute-done.11.refs_0_.refs_1_, bf16[64,1792]{1,0:T(8,128)(2,1)S(1)} %collective-permute-done.13.refs_1_, ...), custom_call_target="tpu_custom_call" | custom-call | flops 1879048192 | bytes 7340032 | tf_op jit(solution)/shard_map/activate/pallas_call | solution.py:268
  69.8 1.8 %collective-permute-done.12.refs_0_ = bf16[64,1792]{1,0:T(8,128)(2,1)S(1)} collective-permute-done((bf16[64,1792]{1,0:T(8,128)(2,1)S(1)}, bf16[64,1792]{1,0:T(8,128)(2,1)S(1)}, u32[]{:S(2)}, u32[]{:S(2)}) %collective-permute-start.12) | collective-permute-done | bytes 229408 | tf_op jit(solution)/shard_map/ppermute | solution.py:387
  71.8 0.4 collective-permute-start.22
  72.2 1.0 collective-permute-done.18.refs_1_
  73.2 0.3 collective-permute-done.22.refs_5_
  73.5 2.8 %activate.3.active = bf16[256,512]{1,0:T(8,128)(2,1)S(1)} custom-call(s32[8]{0:T(128)S(1)} %stack.35.refs_0_.places, bf16[64,1792]{1,0:T(8,128)(2,1)S(1)} %collective-permute-done.12.refs_0_, bf16[64,1792]{1,0:T(8,128)(2,1)S(1)} %collective-permute-done.18.refs_1_, bf16[64,1792]{1,0:T(8,128)(2,1)S(1)} %collective-permute-done.19.refs_2_, ...), custom_call_target="tpu_custom_call" | custom-call | flops 1879048192 | bytes 7340032 | tf_op jit(solution)/shard_map/activate/pallas_call | solution.py:268
  76.4 2.7 %down.1 = (bf16[128,1792]{1,0:T(8,128)(2,1)S(1)}, bf16[128,1792]{1,0:T(8,128)(2,1)S(1)}, bf16[128,1792]{1,0:T(8,128)(2,1)S(1)}, bf16[128,1792]{1,0:T(8,128)(2,1)...) custom-call(s32[8]{0:T(128)S(1)} %stack.35.refs_0_.places, ...), custom_call_target="tpu_custom_call" | custom-call | flops 1879048192 | bytes 7340032 | tf_op jit(solution)/shard_map/down/pallas_call | solution.py:314
  79.3 0.3 collective-permute-start.27
  79.8 0.3 collective-permute-start.24
  80.2 0.8 collective-permute-done.25.refs_1_.refs_3_
  81.1 0.4 collective-permute-start.26
  81.7 1.4 %collective-permute-start.28 = (bf16[64,1792]{1,0:T(8,128)(2,1)S(1)}, bf16[64,1792]{1,0:T(8,128)(2,1)S(1)}, u32[]{:S(2)}, u32[]{:S(2)}) collective-permute-start(bf16[64,1792]{1,0:T(8,128)(2,1)S(1)} %get-tuple-element.44), channel_id=1, source_target_pairs={{0,8},{4,12},{8,0},{12,4},{1,9},{5,13},{9,1},{13,5},{2,10},{6,14},... | collective-permute-start | bytes 688136 | tf_op jit(solution)/shard_map/ppermute | solution.py:387
  83.3 0.7 collective-permute-start.31
  84.0 4.8 %collective-permute-done.26.refs_2_.refs_4_ = bf16[64,1792]{1,0:T(8,128)(2,1)S(1)} collective-permute-done((bf16[64,1792]{1,0:T(8,128)(2,1)S(1)}, bf16[64,1792]{1,0:T(8,128)(2,1)S(1)}, u32[]{:S(2)}, u32[]{:S(2)}) %collective-permute-start.26) | collective-permute-done | bytes 229408 | tf_op jit(solution)/shard_map/ppermute | solution.py:390
  88.8 1.4 %collective-permute-done.28.refs_1_ = bf16[64,1792]{1,0:T(8,128)(2,1)S(1)} collective-permute-done((bf16[64,1792]{1,0:T(8,128)(2,1)S(1)}, bf16[64,1792]{1,0:T(8,128)(2,1)S(1)}, u32[]{:S(2)}, u32[]{:S(2)}) %collective-permute-start.28) | collective-permute-done | bytes 229408 | tf_op jit(solution)/shard_map/ppermute | solution.py:387
  90.3 1.7 %collective-permute-start.32 = (bf16[64,1792]{1,0:T(8,128)(2,1)S(1)}, bf16[64,1792]{1,0:T(8,128)(2,1)S(1)}, u32[]{:S(2)}, u32[]{:S(2)}) collective-permute-start(bf16[64,1792]{1,0:T(8,128)(2,1)S(1)} %add.73.refs_5_), channel_id=1, source_target_pairs={{0,1},{1,0},{2,3},{3,2},{4,5},{5,4},{6,7},{7,6},{8,9},{9,8},{10,11... | collective-permute-start | bytes 688136 | tf_op jit(solution)/shard_map/ppermute | solution.py:390
  92.1 0.5 collective-permute-start.29
  92.6 2.6 %collective-permute-done.31.refs_1_ = bf16[64,1792]{1,0:T(8,128)(2,1)S(1)} collective-permute-done((bf16[64,1792]{1,0:T(8,128)(2,1)S(1)}, bf16[64,1792]{1,0:T(8,128)(2,1)S(1)}, u32[]{:S(2)}, u32[]{:S(2)}) %collective-permute-start.31) | collective-permute-done | bytes 229408 | tf_op jit(solution)/shard_map/ppermute | solution.py:387
  95.2 1.3 %collective-permute-done.32.refs_2_ = bf16[64,1792]{1,0:T(8,128)(2,1)S(1)} collective-permute-done((bf16[64,1792]{1,0:T(8,128)(2,1)S(1)}, bf16[64,1792]{1,0:T(8,128)(2,1)S(1)}, u32[]{:S(2)}, u32[]{:S(2)}) %collective-permute-start.32) | collective-permute-done | bytes 229408 | tf_op jit(solution)/shard_map/ppermute | solution.py:390
  96.6 3.6 %collective-permute-start.33 = (bf16[64,1792]{1,0:T(8,128)(2,1)S(1)}, bf16[64,1792]{1,0:T(8,128)(2,1)S(1)}, u32[]{:S(2)}, u32[]{:S(2)}) collective-permute-start(bf16[64,1792]{1,0:T(8,128)(2,1)S(1)} %add.76), channel_id=1, source_target_pairs={{0,2},{1,3},{2,0},{3,1},{4,6},{5,7},{6,4},{7,5},{8,10},{9,11},{10,... | collective-permute-start | bytes 688136 | tf_op jit(solution)/shard_map/ppermute | solution.py:390
  100.2 7.5 %collective-permute-done.33.refs_2_ = bf16[64,1792]{1,0:T(8,128)(2,1)S(1)} collective-permute-done((bf16[64,1792]{1,0:T(8,128)(2,1)S(1)}, bf16[64,1792]{1,0:T(8,128)(2,1)S(1)}, u32[]{:S(2)}, u32[]{:S(2)}) %collective-permute-start.33) | collective-permute-done | bytes 229408 | tf_op jit(solution)/shard_map/ppermute | solution.py:390
  107.8 0.6 collective-permute-done.34.refs_1_
  108.4 0.7 add.78
  (61 shorter events, 2.8 us)
Async XLA Ops:
  0.6 16.0 %copy-start = (bf16[256,1792]{1,0:T(8,128)(2,1)S(1)}, bf16[256,1792]{1,0:T(8,128)(2,1)}, u32[]{:S(2)}) copy-start(bf16[256,1792]{1,0:T(8,128)(2,1)} %param.21) | copy-start | bytes 2752516
  0.8 15.7 %copy-start.3 = (f32[256,2]{0,1:T(2,128)S(1)}, f32[256,2]{0,1:T(2,128)}, u32[]{:S(2)}) copy-start(f32[256,2]{0,1:T(2,128)} %param.24) | copy-start | bytes 6148
  0.8 15.7 %copy-start.4 = (s32[256,2]{0,1:T(2,128)S(1)}, s32[256,2]{0,1:T(2,128)}, u32[]{:S(2)}) copy-start(s32[256,2]{0,1:T(2,128)} %param.23) | copy-start | bytes 6148
  0.8 15.9 %copy-start.2 = (f32[1792]{0:T(1024)S(1)}, f32[1792]{0:T(1024)}, u32[]{:S(2)}) copy-start(f32[1792]{0:T(1024)} %param.22) | copy-start | bytes 21508
  13.4 7.3 %collective-permute-start = (bf16[64,1024]{1,0:T(8,128)(2,1)S(1)}, bf16[64,1024]{1,0:T(8,128)(2,1)S(1)}, u32[]{:S(2)}, u32[]{:S(2)}) collective-permute-start(bf16[64,1024]{1,0:T(8,128)(2,1)S(1)} %attention.1.refs_1_.refs_0_), channel_id=1, source_target_pairs={{0,4},{4,0},{8,12},{12,8},{1,5},{5,1},{9,13},{13,9},{2,6},{6,2},{1... | collective-permute-start | bytes 393224 | tf_op jit(solution)/shard_map/ppermute | solution.py:383
  13.9 6.7 %collective-permute-start.1 = (bf16[64,1024]{1,0:T(8,128)(2,1)S(1)}, bf16[64,1024]{1,0:T(8,128)(2,1)S(1)}, u32[]{:S(2)}, u32[]{:S(2)}) collective-permute-start(bf16[64,1024]{1,0:T(8,128)(2,1)S(1)} %attention.1.refs_1_.refs_0_), channel_id=1, source_target_pairs={{0,8},{4,12},{8,0},{12,4},{1,9},{5,13},{9,1},{13,5},{2,10},{6,14},... | collective-permute-start | bytes 393224 | tf_op jit(solution)/shard_map/ppermute | solution.py:387
  20.6 1.4 %collective-permute-start.2 = (bf16[64,1024]{1,0:T(8,128)(2,1)S(1)}, bf16[64,1024]{1,0:T(8,128)(2,1)S(1)}, u32[]{:S(2)}, u32[]{:S(2)}) collective-permute-start(bf16[64,1024]{1,0:T(8,128)(2,1)S(1)} %add.64.refs_2_), channel_id=1, source_target_pairs={{0,4},{4,0},{8,12},{12,8},{1,5},{5,1},{9,13},{13,9},{2,6},{6,2},{1... | collective-permute-start | bytes 393224 | tf_op jit(solution)/shard_map/ppermute | solution.py:383
  23.8 7.9 %collective-permute-start.3 = (bf16[64,1792]{1,0:T(8,128)(2,1)S(1)}, bf16[64,1792]{1,0:T(8,128)(2,1)S(1)}, u32[]{:S(2)}, u32[]{:S(2)}) collective-permute-start(bf16[64,1792]{1,0:T(8,128)(2,1)S(1)} %get-tuple-element.29), channel_id=1, source_target_pairs={{0,1},{1,0},{2,3},{3,2},{4,5},{5,4},{6,7},{7,6},{8,9},{9,8},{10,11... | collective-permute-start | bytes 688136 | tf_op jit(solution)/shard_map/ppermute | solution.py:390
  28.9 12.7 %collective-permute-start.5 = (bf16[64,1792]{1,0:T(8,128)(2,1)S(1)}, bf16[64,1792]{1,0:T(8,128)(2,1)S(1)}, u32[]{:S(2)}, u32[]{:S(2)}) collective-permute-start(bf16[64,1792]{1,0:T(8,128)(2,1)S(1)} %add.66.refs_1_), channel_id=1, source_target_pairs={{0,1},{1,0},{2,3},{3,2},{4,5},{5,4},{6,7},{7,6},{8,9},{9,8},{10,11... | collective-permute-start | bytes 688136 | tf_op jit(solution)/shard_map/ppermute | solution.py:390
  31.7 12.8 %collective-permute-start.4 = (bf16[64,1792]{1,0:T(8,128)(2,1)S(1)}, bf16[64,1792]{1,0:T(8,128)(2,1)S(1)}, u32[]{:S(2)}, u32[]{:S(2)}) collective-permute-start(bf16[64,1792]{1,0:T(8,128)(2,1)S(1)} %add.65), channel_id=1, source_target_pairs={{0,2},{1,3},{2,0},{3,1},{4,6},{5,7},{6,4},{7,5},{8,10},{9,11},{10,... | collective-permute-start | bytes 688136 | tf_op jit(solution)/shard_map/ppermute | solution.py:390
  34.7 3.6 %collective-permute-start.7 = (f32[1,1792]{1,0:T(1,128)S(1)}, f32[1,1792]{1,0:T(1,128)S(1)}, u32[]{:S(2)}, u32[]{:S(2)}) collective-permute-start(f32[1,1792]{1,0:T(1,128)S(1)} %reshape.7.refs_4_.refs_8_), channel_id=1, source_target_pairs={{0,8},{4,12},{8,0},{12,4},{1,9},{5,13},{9,1},{13,5},{2,10},{6,14},... | collective-permute-start | bytes 21512 | tf_op jit(solution)/shard_map/ppermute | solution.py:387
  36.2 5.3 %collective-permute-start.6 = (f32[1,1792]{1,0:T(1,128)S(1)}, f32[1,1792]{1,0:T(1,128)S(1)}, u32[]{:S(2)}, u32[]{:S(2)}) collective-permute-start(f32[1,1792]{1,0:T(1,128)S(1)} %reshape.7.refs_4_.refs_8_), channel_id=1, source_target_pairs={{0,4},{4,0},{8,12},{12,8},{1,5},{5,1},{9,13},{13,9},{2,6},{6,2},{1... | collective-permute-start | bytes 21512 | tf_op jit(solution)/shard_map/ppermute | solution.py:383
  38.4 3.2 %collective-permute-start.8 = (f32[1,1792]{1,0:T(1,128)S(1)}, f32[1,1792]{1,0:T(1,128)S(1)}, u32[]{:S(2)}, u32[]{:S(2)}) collective-permute-start(f32[1,1792]{1,0:T(1,128)S(1)} %collective-permute-done.7.refs_10_.refs_8_), channel_id=1, source_target_pairs={{0,4},{4,0},{8,12},{12,8},{1,5},{5,1},{9,13},{13,9},{2,6},{6,2},{1... | collective-permute-start | bytes 21512 | tf_op jit(solution)/shard_map/ppermute | solution.py:383
  45.4 11.0 %collective-permute-start.9 = (bf16[64,1792]{1,0:T(8,128)(2,1)S(1)}, bf16[64,1792]{1,0:T(8,128)(2,1)S(1)}, u32[]{:S(2)}, u32[]{:S(2)}) collective-permute-start(bf16[64,1792]{1,0:T(8,128)(2,1)S(1)} %get-tuple-element.32.refs_1_.refs_6_), channel_id=1, source_target_pairs={{0,2},{1,3},{2,0},{3,1},{4,6},{5,7},{6,4},{7,5},{8,10},{9,11},{10,... | collective-permute-start | bytes 688136 | tf_op jit(solution)/shard_map/ppermute | solution.py:390
  45.4 11.0 %collective-permute-start.10 = (bf16[64,1792]{1,0:T(8,128)(2,1)S(1)}, bf16[64,1792]{1,0:T(8,128)(2,1)S(1)}, u32[]{:S(2)}, u32[]{:S(2)}) collective-permute-start(bf16[64,1792]{1,0:T(8,128)(2,1)S(1)} %get-tuple-element.32.refs_1_.refs_6_), channel_id=1, source_target_pairs={{0,8},{4,12},{8,0},{12,4},{1,9},{5,13},{9,1},{13,5},{2,10},{6,14},... | collective-permute-start | bytes 688136 | tf_op jit(solution)/shard_map/ppermute | solution.py:387
  46.9 11.8 %collective-permute-start.15 = (bf16[64,1792]{1,0:T(8,128)(2,1)S(1)}, bf16[64,1792]{1,0:T(8,128)(2,1)S(1)}, u32[]{:S(2)}, u32[]{:S(2)}) collective-permute-start(bf16[64,1792]{1,0:T(8,128)(2,1)S(1)} %get-tuple-element.32.refs_1_.refs_6_), channel_id=1, source_target_pairs={{0,1},{1,0},{2,3},{3,2},{4,5},{5,4},{6,7},{7,6},{8,9},{9,8},{10,11... | collective-permute-start | bytes 688136 | tf_op jit(solution)/shard_map/ppermute | solution.py:390
  56.4 6.2 %collective-permute-start.11 = (bf16[64,1792]{1,0:T(8,128)(2,1)S(1)}, bf16[64,1792]{1,0:T(8,128)(2,1)S(1)}, u32[]{:S(2)}, u32[]{:S(2)}) collective-permute-start(bf16[64,1792]{1,0:T(8,128)(2,1)S(1)} %add.68), channel_id=1, source_target_pairs={{0,1},{1,0},{2,3},{3,2},{4,5},{5,4},{6,7},{7,6},{8,9},{9,8},{10,11... | collective-permute-start | bytes 688136 | tf_op jit(solution)/shard_map/ppermute | solution.py:390
  56.5 6.1 %collective-permute-start.17 = (bf16[64,1792]{1,0:T(8,128)(2,1)S(1)}, bf16[64,1792]{1,0:T(8,128)(2,1)S(1)}, u32[]{:S(2)}, u32[]{:S(2)}) collective-permute-start(bf16[64,1792]{1,0:T(8,128)(2,1)S(1)} %get-tuple-element.32.refs_1_.refs_6_), channel_id=1, source_target_pairs={{0,4},{4,0},{8,12},{12,8},{1,5},{5,1},{9,13},{13,9},{2,6},{6,2},{1... | collective-permute-start | bytes 688136 | tf_op jit(solution)/shard_map/ppermute | solution.py:383
  56.6 7.5 %collective-permute-start.14 = (bf16[64,1792]{1,0:T(8,128)(2,1)S(1)}, bf16[64,1792]{1,0:T(8,128)(2,1)S(1)}, u32[]{:S(2)}, u32[]{:S(2)}) collective-permute-start(bf16[64,1792]{1,0:T(8,128)(2,1)S(1)} %collective-permute-done.9.refs_0_.refs_2_), channel_id=1, source_target_pairs={{0,4},{4,0},{8,12},{12,8},{1,5},{5,1},{9,13},{13,9},{2,6},{6,2},{1... | collective-permute-start | bytes 688136 | tf_op jit(solution)/shard_map/ppermute | solution.py:383
  58.7 5.7 %collective-permute-start.16 = (bf16[64,1792]{1,0:T(8,128)(2,1)S(1)}, bf16[64,1792]{1,0:T(8,128)(2,1)S(1)}, u32[]{:S(2)}, u32[]{:S(2)}) collective-permute-start(bf16[64,1792]{1,0:T(8,128)(2,1)S(1)} %collective-permute-done.15.refs_4_), channel_id=1, source_target_pairs={{0,4},{4,0},{8,12},{12,8},{1,5},{5,1},{9,13},{13,9},{2,6},{6,2},{1... | collective-permute-start | bytes 688136 | tf_op jit(solution)/shard_map/ppermute | solution.py:383
  58.7 8.4 %collective-permute-start.19 = (bf16[64,1792]{1,0:T(8,128)(2,1)S(1)}, bf16[64,1792]{1,0:T(8,128)(2,1)S(1)}, u32[]{:S(2)}, u32[]{:S(2)}) collective-permute-start(bf16[64,1792]{1,0:T(8,128)(2,1)S(1)} %collective-permute-done.9.refs_0_.refs_2_), channel_id=1, source_target_pairs={{0,8},{4,12},{8,0},{12,4},{1,9},{5,13},{9,1},{13,5},{2,10},{6,14},... | collective-permute-start | bytes 688136 | tf_op jit(solution)/shard_map/ppermute | solution.py:387
  62.6 4.5 %collective-permute-start.13 = (bf16[64,1792]{1,0:T(8,128)(2,1)S(1)}, bf16[64,1792]{1,0:T(8,128)(2,1)S(1)}, u32[]{:S(2)}, u32[]{:S(2)}) collective-permute-start(bf16[64,1792]{1,0:T(8,128)(2,1)S(1)} %collective-permute-done.11.refs_0_.refs_1_), channel_id=1, source_target_pairs={{0,4},{4,0},{8,12},{12,8},{1,5},{5,1},{9,13},{13,9},{2,6},{6,2},{1... | collective-permute-start | bytes 688136 | tf_op jit(solution)/shard_map/ppermute | solution.py:383
  62.6 9.0 %collective-permute-start.12 = (bf16[64,1792]{1,0:T(8,128)(2,1)S(1)}, bf16[64,1792]{1,0:T(8,128)(2,1)S(1)}, u32[]{:S(2)}, u32[]{:S(2)}) collective-permute-start(bf16[64,1792]{1,0:T(8,128)(2,1)S(1)} %collective-permute-done.11.refs_0_.refs_1_), channel_id=1, source_target_pairs={{0,8},{4,12},{8,0},{12,4},{1,9},{5,13},{9,1},{13,5},{2,10},{6,14},... | collective-permute-start | bytes 688136 | tf_op jit(solution)/shard_map/ppermute | solution.py:387
  64.0 7.8 %collective-permute-start.21 = (bf16[64,1792]{1,0:T(8,128)(2,1)S(1)}, bf16[64,1792]{1,0:T(8,128)(2,1)S(1)}, u32[]{:S(2)}, u32[]{:S(2)}) collective-permute-start(bf16[64,1792]{1,0:T(8,128)(2,1)S(1)} %add.70), channel_id=1, source_target_pairs={{0,1},{1,0},{2,3},{3,2},{4,5},{5,4},{6,7},{7,6},{8,9},{9,8},{10,11... | collective-permute-start | bytes 688136 | tf_op jit(solution)/shard_map/ppermute | solution.py:390
  64.4 7.9 %collective-permute-start.23 = (bf16[64,1792]{1,0:T(8,128)(2,1)S(1)}, bf16[64,1792]{1,0:T(8,128)(2,1)S(1)}, u32[]{:S(2)}, u32[]{:S(2)}) collective-permute-start(bf16[64,1792]{1,0:T(8,128)(2,1)S(1)} %collective-permute-done.10.refs_1_.refs_0_.refs_6_), channel_id=1, source_target_pairs={{0,4},{4,0},{8,12},{12,8},{1,5},{5,1},{9,13},{13,9},{2,6},{6,2},{1... | collective-permute-start | bytes 688136 | tf_op jit(solution)/shard_map/ppermute | solution.py:383
  67.1 5.1 %collective-permute-start.20 = (bf16[64,1792]{1,0:T(8,128)(2,1)S(1)}, bf16[64,1792]{1,0:T(8,128)(2,1)S(1)}, u32[]{:S(2)}, u32[]{:S(2)}) collective-permute-start(bf16[64,1792]{1,0:T(8,128)(2,1)S(1)} %collective-permute-done.19.refs_2_), channel_id=1, source_target_pairs={{0,4},{4,0},{8,12},{12,8},{1,5},{5,1},{9,13},{13,9},{2,6},{6,2},{1... | collective-permute-start | bytes 688136 | tf_op jit(solution)/shard_map/ppermute | solution.py:383
  71.6 1.6 %collective-permute-start.18 = (bf16[64,1792]{1,0:T(8,128)(2,1)S(1)}, bf16[64,1792]{1,0:T(8,128)(2,1)S(1)}, u32[]{:S(2)}, u32[]{:S(2)}) collective-permute-start(bf16[64,1792]{1,0:T(8,128)(2,1)S(1)} %add.69), channel_id=1, source_target_pairs={{0,4},{4,0},{8,12},{12,8},{1,5},{5,1},{9,13},{13,9},{2,6},{6,2},{1... | collective-permute-start | bytes 688136 | tf_op jit(solution)/shard_map/ppermute | solution.py:383
  71.8 1.7 %collective-permute-start.22 = (bf16[64,1792]{1,0:T(8,128)(2,1)S(1)}, bf16[64,1792]{1,0:T(8,128)(2,1)S(1)}, u32[]{:S(2)}, u32[]{:S(2)}) collective-permute-start(bf16[64,1792]{1,0:T(8,128)(2,1)S(1)} %collective-permute-done.21.refs_4_), channel_id=1, source_target_pairs={{0,4},{4,0},{8,12},{12,8},{1,5},{5,1},{9,13},{13,9},{2,6},{6,2},{1... | collective-permute-start | bytes 688136 | tf_op jit(solution)/shard_map/ppermute | solution.py:383
  76.4 32.8 %copy-start.1 = (bf16[256,1792]{1,0:T(8,128)(2,1)S(1)}, bf16[256,1792]{1,0:T(8,128)(2,1)}, u32[]{:S(2)}) copy-start(bf16[256,1792]{1,0:T(8,128)(2,1)} %param.21) | copy-start | bytes 2752516
  79.1 1.9 %collective-permute-start.25 = (bf16[128,1792]{1,0:T(8,128)(2,1)S(1)}, bf16[128,1792]{1,0:T(8,128)(2,1)S(1)}, u32[]{:S(2)}, u32[]{:S(2)}) collective-permute-start(bf16[128,1792]{1,0:T(8,128)(2,1)S(1)} %get-tuple-element.39), channel_id=1, source_target_pairs={{0,4},{4,0},{8,12},{12,8},{1,5},{5,1},{9,13},{13,9},{2,6},{6,2},{1... | collective-permute-start | bytes 1376264 | tf_op jit(solution)/shard_map/ppermute | solution.py:383
  79.3 2.3 %collective-permute-start.27 = (bf16[128,1792]{1,0:T(8,128)(2,1)S(1)}, bf16[128,1792]{1,0:T(8,128)(2,1)S(1)}, u32[]{:S(2)}, u32[]{:S(2)}) collective-permute-start(bf16[128,1792]{1,0:T(8,128)(2,1)S(1)} %get-tuple-element.42), channel_id=1, source_target_pairs={{0,4},{4,0},{8,12},{12,8},{1,5},{5,1},{9,13},{13,9},{2,6},{6,2},{1... | collective-permute-start | bytes 1376264 | tf_op jit(solution)/shard_map/ppermute | solution.py:383
  79.7 3.5 %collective-permute-start.30 = (bf16[128,1792]{1,0:T(8,128)(2,1)S(1)}, bf16[128,1792]{1,0:T(8,128)(2,1)S(1)}, u32[]{:S(2)}, u32[]{:S(2)}) collective-permute-start(bf16[128,1792]{1,0:T(8,128)(2,1)S(1)} %get-tuple-element.48), channel_id=1, source_target_pairs={{0,4},{4,0},{8,12},{12,8},{1,5},{5,1},{9,13},{13,9},{2,6},{6,2},{1... | collective-permute-start | bytes 1376264 | tf_op jit(solution)/shard_map/ppermute | solution.py:383
  79.8 12.1 %collective-permute-start.24 = (bf16[128,1792]{1,0:T(8,128)(2,1)S(1)}, bf16[128,1792]{1,0:T(8,128)(2,1)S(1)}, u32[]{:S(2)}, u32[]{:S(2)}) collective-permute-start(bf16[128,1792]{1,0:T(8,128)(2,1)S(1)} %get-tuple-element.37), channel_id=1, source_target_pairs={{0,4},{4,0},{8,12},{12,8},{1,5},{5,1},{9,13},{13,9},{2,6},{6,2},{1... | collective-permute-start | bytes 1376264 | tf_op jit(solution)/shard_map/ppermute | solution.py:383
  81.1 7.8 %collective-permute-start.26 = (bf16[64,1792]{1,0:T(8,128)(2,1)S(1)}, bf16[64,1792]{1,0:T(8,128)(2,1)S(1)}, u32[]{:S(2)}, u32[]{:S(2)}) collective-permute-start(bf16[64,1792]{1,0:T(8,128)(2,1)S(1)} %get-tuple-element.40), channel_id=1, source_target_pairs={{0,1},{1,0},{2,3},{3,2},{4,5},{5,4},{6,7},{7,6},{8,9},{9,8},{10,11... | collective-permute-start | bytes 688136 | tf_op jit(solution)/shard_map/ppermute | solution.py:390
  81.7 8.5 %collective-permute-start.28 = (bf16[64,1792]{1,0:T(8,128)(2,1)S(1)}, bf16[64,1792]{1,0:T(8,128)(2,1)S(1)}, u32[]{:S(2)}, u32[]{:S(2)}) collective-permute-start(bf16[64,1792]{1,0:T(8,128)(2,1)S(1)} %get-tuple-element.44), channel_id=1, source_target_pairs={{0,8},{4,12},{8,0},{12,4},{1,9},{5,13},{9,1},{13,5},{2,10},{6,14},... | collective-permute-start | bytes 688136 | tf_op jit(solution)/shard_map/ppermute | solution.py:387
  83.3 11.9 %collective-permute-start.31 = (bf16[64,1792]{1,0:T(8,128)(2,1)S(1)}, bf16[64,1792]{1,0:T(8,128)(2,1)S(1)}, u32[]{:S(2)}, u32[]{:S(2)}) collective-permute-start(bf16[64,1792]{1,0:T(8,128)(2,1)S(1)} %get-tuple-element.50), channel_id=1, source_target_pairs={{0,8},{4,12},{8,0},{12,4},{1,9},{5,13},{9,1},{13,5},{2,10},{6,14},... | collective-permute-start | bytes 688136 | tf_op jit(solution)/shard_map/ppermute | solution.py:387
  90.3 6.2 %collective-permute-start.32 = (bf16[64,1792]{1,0:T(8,128)(2,1)S(1)}, bf16[64,1792]{1,0:T(8,128)(2,1)S(1)}, u32[]{:S(2)}, u32[]{:S(2)}) collective-permute-start(bf16[64,1792]{1,0:T(8,128)(2,1)S(1)} %add.73.refs_5_), channel_id=1, source_target_pairs={{0,1},{1,0},{2,3},{3,2},{4,5},{5,4},{6,7},{7,6},{8,9},{9,8},{10,11... | collective-permute-start | bytes 688136 | tf_op jit(solution)/shard_map/ppermute | solution.py:390
  92.1 8.1 %collective-permute-start.29 = (bf16[64,1792]{1,0:T(8,128)(2,1)S(1)}, bf16[64,1792]{1,0:T(8,128)(2,1)S(1)}, u32[]{:S(2)}, u32[]{:S(2)}) collective-permute-start(bf16[64,1792]{1,0:T(8,128)(2,1)S(1)} %get-tuple-element.46), channel_id=1, source_target_pairs={{0,8},{4,12},{8,0},{12,4},{1,9},{5,13},{9,1},{13,5},{2,10},{6,14},... | collective-permute-start | bytes 688136 | tf_op jit(solution)/shard_map/ppermute | solution.py:387
  96.6 11.2 %collective-permute-start.33 = (bf16[64,1792]{1,0:T(8,128)(2,1)S(1)}, bf16[64,1792]{1,0:T(8,128)(2,1)S(1)}, u32[]{:S(2)}, u32[]{:S(2)}) collective-permute-start(bf16[64,1792]{1,0:T(8,128)(2,1)S(1)} %add.76), channel_id=1, source_target_pairs={{0,2},{1,3},{2,0},{3,1},{4,6},{5,7},{6,4},{7,5},{8,10},{9,11},{10,... | collective-permute-start | bytes 688136 | tf_op jit(solution)/shard_map/ppermute | solution.py:390
  100.2 8.3 %collective-permute-start.34 = (bf16[64,1792]{1,0:T(8,128)(2,1)S(1)}, bf16[64,1792]{1,0:T(8,128)(2,1)S(1)}, u32[]{:S(2)}, u32[]{:S(2)}) collective-permute-start(bf16[64,1792]{1,0:T(8,128)(2,1)S(1)} %get-tuple-element.51), channel_id=1, source_target_pairs={{0,1},{1,0},{2,3},{3,2},{4,5},{5,4},{6,7},{7,6},{8,9},{9,8},{10,11... | collective-permute-start | bytes 688136 | tf_op jit(solution)/shard_map/ppermute | solution.py:390

commit v20 on v17

--- a/solution.py
+++ b/solution.py
@@ -64,10 +64,8 @@
 
     @pl.when(step == 0)
     def _():
-        for at in range(min(ahead, steps)):
-            for copy in copies(at):
-                copy.start()
-        pltpu.make_async_copy(up_hbm, up_ref, up_sem).start()
+        for copy in copies(0):
+            copy.start()
         all_rows = qr_ref.shape[0]
         width = heads * rope_width
         lane = lax.broadcasted_iota(jnp.int32, (heads, width), 1)
@@ -80,13 +78,24 @@
         fold = jnp.where(lane % rope_width == column, 1.0, 0.0).astype(jnp.bfloat16)
         rope[...] = jnp.dot(spread, fold, preferred_element_type=jnp.float32)
 
+    @pl.when(step == 0)
+    def _():
+        for at in range(1, min(ahead, steps)):
+            for copy in copies(at):
+                copy.start()
+
+    for copy in copies(step):
+        copy.wait()
+
     @pl.when(step + ahead < steps)
     def _():
         for copy in copies(step + ahead):
             copy.start()
 
-    for copy in copies(step):
-        copy.wait()
+    @pl.when(step == steps // 2)
+    def _():
+        pltpu.make_async_copy(up_hbm, up_ref, up_sem).start()
+
     place = lax.broadcasted_iota(jnp.int32, (heads, positions), 1)
     lanes = latent.shape[2]
     lanes = latent.shape[2]
@@ -130,7 +139,7 @@
     rows, heads, latent_width = query_latent.shape
     rope_width = cache_rope.shape[1]
     value_width = value_up.shape[2]
-    step_rows, pieces, ahead = 8, 1, 3
+    step_rows, pieces, ahead = 8, 1, 2
     by_row = lambda i, lengths: (i, 0, 0)
     return pl.pallas_call(
         functools.partial(attention_kernel, step_rows, pieces, ahead),

time: 109 us -> 109 us (level)
  no operation moved by 1% of the time
where the time goes in v20:
time: 109 us
  waiting for transfers between devices  39.6 us (36%)
  Pallas kernels  36.4 us (33%)
  starting transfers between devices  31.5 us (29%)
    ppermute x11, waiting for transfers between devices, from_tp(): return lax.ppermute(value, 'tp', [(i, i ^ bits) for i in range(tp_count)])  26.5 us
    ppermute x11, starting transfers between devices, from_tp(): return lax.ppermute(value, 'tp', [(i, i ^ bits) for i in range(tp_count)])  17.4 us
    pallas_call x1, Pallas kernels, attend(): pl.pallas_call(functools.partial(attention_kernel, step_rows, pieces, ahe...  12.5 us
    pallas_call x4, Pallas kernels, fetch(): pl.pallas_call(functools.partial(fetch_kernel, parts), out_shape=pltpu.VM...  11.6 us
    ppermute x8, starting transfers between devices, from_chip(): lax.ppermute(value, 'ep', [(i, (i + step) % ep_count) for i in range(ep_c...  10.9 us
    ppermute x8, waiting for transfers between devices, from_chip(): lax.ppermute(value, 'ep', [(i, (i + step) % ep_count) for i in range(ep_c...  8.54 us
    pallas_call x2, Pallas kernels, activate(): pl.pallas_call(functools.partial(gate_kernel, row_blocks, cores, first, c...  5.54 us
    ppermute x16, waiting for transfers between devices, from_core(): return lax.ppermute(value, 'ep', [(i, i ^ 1) for i in range(ep_count)])  4.61 us
  transfers between devices with their start and end apart: 35, of which 20 were waited for; matrix products, arithmetic and copies ran while one was open for 0% of the time, Pallas kernels for 14%

profile of v20, /device:TPU:0, one launch (start us, length us, event | category | flops | bytes accessed | tf_op | source)
XLA Modules:
  0.0 108.8 jit_solution(9657414357616749658)
XLA Ops:
  0.8 12.5 %attention.1.refs_1_.refs_0_ = bf16[64,1024]{1,0:T(8,128)(2,1)S(1)} custom-call(s32[64]{0:T(128)} %lengths.1, bf16[64,8,512]{2,1,0:T(8,128)(2,1)} %q_ref.1, bf16[64,512]{1,0:T(8,128)(2,1)} %qr_ref.1, bf16[64,256,512]{2,1,0:T(8,128)(2,1)} %k_hbm.1, bf16[64,64,256]{2,1,0:T(8,128)(2,1)} %kr_hbm.1, bf16[8,512,128]{2,1,0:T(8,128)(2,1)} %up_hbm.1, ...), custom_call_target="tpu_custom_call" | custom-call | flops 4294967296 | bytes 16777216 | tf_op jit(solution)/shard_map/attention/pallas_call | solution.py:144
  13.3 0.5 collective-permute-start
  13.8 2.6 %collective-permute-start.1 = (bf16[64,1024]{1,0:T(8,128)(2,1)S(1)}, bf16[64,1024]{1,0:T(8,128)(2,1)S(1)}, u32[]{:S(2)}, u32[]{:S(2)}) collective-permute-start(bf16[64,1024]{1,0:T(8,128)(2,1)S(1)} %attention.1.refs_1_.refs_0_), channel_id=1, source_target_pairs={{0,8},{4,12},{8,0},{12,4},{1,9},{5,13},{9,1},{13,5},{2,10},{6,14},... | collective-permute-start | bytes 393224 | tf_op jit(solution)/shard_map/ppermute | solution.py:396
  16.6 2.0 %fetch.4.refs_1_.refs_4_ = bf16[1024,1792]{1,0:T(8,128)(2,1)S(1)} custom-call(bf16[1024,1792]{1,0:T(8,128)(2,1)} %refs_0_.4, bf16[64,1024]{1,0:T(8,128)(2,1)S(1)} %attention.1.refs_1_.refs_0_, f32[256,1]{1,0:T(8,128)S(1)} %copy.16.refs_2_.row_weight, bf16[64,1792]{1,0:T(8,128)(2,1)S(1)} %constant_dynamic-slice_fusion.refs_3_.refs_7_, ...), custom_call_target="tpu_custom_call" | custom-call | bytes 7340032 | tf_op jit(solution)/shard_map/fetch/pallas_call | solution.py:38
  18.7 1.8 %collective-permute-done.1.refs_0_ = bf16[64,1024]{1,0:T(8,128)(2,1)S(1)} collective-permute-done((bf16[64,1024]{1,0:T(8,128)(2,1)S(1)}, bf16[64,1024]{1,0:T(8,128)(2,1)S(1)}, u32[]{:S(2)}, u32[]{:S(2)}) %collective-permute-start.1) | collective-permute-done | bytes 131104 | tf_op jit(solution)/shard_map/ppermute | solution.py:396
  20.6 1.3 %collective-permute-done.2.refs_3_ = bf16[64,1024]{1,0:T(8,128)(2,1)S(1)} collective-permute-done((bf16[64,1024]{1,0:T(8,128)(2,1)S(1)}, bf16[64,1024]{1,0:T(8,128)(2,1)S(1)}, u32[]{:S(2)}, u32[]{:S(2)}) %collective-permute-start.2) | collective-permute-done | bytes 131104 | tf_op jit(solution)/shard_map/ppermute | solution.py:392
  21.9 1.8 %projection.1 = (bf16[64,1792]{1,0:T(8,128)(2,1)S(1)}, bf16[64,1792]{1,0:T(8,128)(2,1)S(1)}, bf16[64,1792]{1,0:T(8,128)(2,1)S(1)}, bf16[64,1792]{1,0:T(8,128)(2,1)S(1)}) custom-call(s32[8]{0:T(128)S(1)} %stack.35.refs_0_.places, bf16[64,1024]{1,0:T(8,128)(2,1)S(1)} %attention.1.refs_1_.refs_0_, bf16[64,1024]{1,0:T(8,128)(2,1)S(1)} %collective-permute-done.refs_1_, ...), custom_call_target="tpu_custom_call" | custom-call | flops 939524096 | bytes 4194304 | tf_op jit(solution)/shard_map/projection/pallas_call | solution.py:209
  23.6 1.9 %collective-permute-start.3 = (bf16[64,1792]{1,0:T(8,128)(2,1)S(1)}, bf16[64,1792]{1,0:T(8,128)(2,1)S(1)}, u32[]{:S(2)}, u32[]{:S(2)}) collective-permute-start(bf16[64,1792]{1,0:T(8,128)(2,1)S(1)} %get-tuple-element.29), channel_id=1, source_target_pairs={{0,1},{1,0},{2,3},{3,2},{4,5},{5,4},{6,7},{7,6},{8,9},{9,8},{10,11... | collective-permute-start | bytes 688136 | tf_op jit(solution)/shard_map/ppermute | solution.py:399
  25.5 3.2 %fetch.5.refs_1_.refs_12_.refs_10_ = bf16[1,7168,512]{2,1,0:T(8,128)(2,1)S(1)} custom-call(bf16[1,7168,512]{2,1,0:T(8,128)(2,1)} %refs_0_.5, bf16[64,1792]{1,0:T(8,128)(2,1)S(1)} %get-tuple-element.27.refs_1_.refs_0_.refs_4_), custom_call_target="tpu_custom_call" | custom-call | bytes 14680064 | tf_op jit(solution)/shard_map/fetch/pallas_call | solution.py:38
  29.0 2.5 %collective-permute-done.3.refs_1_ = bf16[64,1792]{1,0:T(8,128)(2,1)S(1)} collective-permute-done((bf16[64,1792]{1,0:T(8,128)(2,1)S(1)}, bf16[64,1792]{1,0:T(8,128)(2,1)S(1)}, u32[]{:S(2)}, u32[]{:S(2)}) %collective-permute-start.3) | collective-permute-done | bytes 229408 | tf_op jit(solution)/shard_map/ppermute | solution.py:399
  31.6 3.0 %collective-permute-start.4 = (bf16[64,1792]{1,0:T(8,128)(2,1)S(1)}, bf16[64,1792]{1,0:T(8,128)(2,1)S(1)}, u32[]{:S(2)}, u32[]{:S(2)}) collective-permute-start(bf16[64,1792]{1,0:T(8,128)(2,1)S(1)} %add.65), channel_id=1, source_target_pairs={{0,2},{1,3},{2,0},{3,1},{4,6},{5,7},{6,4},{7,5},{8,10},{9,11},{10,... | collective-permute-start | bytes 688136 | tf_op jit(solution)/shard_map/ppermute | solution.py:399
  34.6 1.5 %collective-permute-start.7 = (f32[1,1792]{1,0:T(1,128)S(1)}, f32[1,1792]{1,0:T(1,128)S(1)}, u32[]{:S(2)}, u32[]{:S(2)}) collective-permute-start(f32[1,1792]{1,0:T(1,128)S(1)} %reshape.7.refs_4_.refs_8_), channel_id=1, source_target_pairs={{0,8},{4,12},{8,0},{12,4},{1,9},{5,13},{9,1},{13,5},{2,10},{6,14},... | collective-permute-start | bytes 21512 | tf_op jit(solution)/shard_map/ppermute | solution.py:396
  36.1 2.1 %collective-permute-done.7.refs_10_.refs_8_ = f32[1,1792]{1,0:T(1,128)S(1)} collective-permute-done((f32[1,1792]{1,0:T(1,128)S(1)}, f32[1,1792]{1,0:T(1,128)S(1)}, u32[]{:S(2)}, u32[]{:S(2)}) %collective-permute-start.7) | collective-permute-done | bytes 7200 | tf_op jit(solution)/shard_map/ppermute | solution.py:396
  38.3 1.2 %collective-permute-done.8.refs_11_.refs_9_ = f32[1,1792]{1,0:T(1,128)S(1)} collective-permute-done((f32[1,1792]{1,0:T(1,128)S(1)}, f32[1,1792]{1,0:T(1,128)S(1)}, u32[]{:S(2)}, u32[]{:S(2)}) %collective-permute-start.8) | collective-permute-done | bytes 7200 | tf_op jit(solution)/shard_map/ppermute | solution.py:392
  39.4 1.1 collective-permute-done.5.refs_2_.refs_6_
  40.5 3.9 %collective-permute-done.4.refs_1_.refs_5_ = bf16[64,1792]{1,0:T(8,128)(2,1)S(1)} collective-permute-done((bf16[64,1792]{1,0:T(8,128)(2,1)S(1)}, bf16[64,1792]{1,0:T(8,128)(2,1)S(1)}, u32[]{:S(2)}, u32[]{:S(2)}) %collective-permute-start.4) | collective-permute-done | bytes 229408 | tf_op jit(solution)/shard_map/ppermute | solution.py:399
  44.4 0.8 add.67
  45.2 1.5 %collective-permute-start.10 = (bf16[64,1792]{1,0:T(8,128)(2,1)S(1)}, bf16[64,1792]{1,0:T(8,128)(2,1)S(1)}, u32[]{:S(2)}, u32[]{:S(2)}) collective-permute-start(bf16[64,1792]{1,0:T(8,128)(2,1)S(1)} %get-tuple-element.32.refs_1_.refs_6_), channel_id=1, source_target_pairs={{0,8},{4,12},{8,0},{12,4},{1,9},{5,13},{9,1},{13,5},{2,10},{6,14},... | collective-permute-start | bytes 688136 | tf_op jit(solution)/shard_map/ppermute | solution.py:396
  46.8 4.1 %collective-permute-start.15 = (bf16[64,1792]{1,0:T(8,128)(2,1)S(1)}, bf16[64,1792]{1,0:T(8,128)(2,1)S(1)}, u32[]{:S(2)}, u32[]{:S(2)}) collective-permute-start(bf16[64,1792]{1,0:T(8,128)(2,1)S(1)} %get-tuple-element.32.refs_1_.refs_6_), channel_id=1, source_target_pairs={{0,1},{1,0},{2,3},{3,2},{4,5},{5,4},{6,7},{7,6},{8,9},{9,8},{10,11... | collective-permute-start | bytes 688136 | tf_op jit(solution)/shard_map/ppermute | solution.py:399
  50.9 3.2 %fetch.6.refs_2_.refs_11_ = bf16[1,7168,512]{2,1,0:T(8,128)(2,1)S(1)} custom-call(bf16[1,7168,512]{2,1,0:T(8,128)(2,1)} %refs_0_.6, bf16[64,1792]{1,0:T(8,128)(2,1)S(1)} %get-tuple-element.32.refs_1_.refs_6_), custom_call_target="tpu_custom_call" | custom-call | bytes 14680064 | tf_op jit(solution)/shard_map/fetch/pallas_call | solution.py:38
  54.1 1.4 %collective-permute-done.9.refs_0_.refs_2_ = bf16[64,1792]{1,0:T(8,128)(2,1)S(1)} collective-permute-done((bf16[64,1792]{1,0:T(8,128)(2,1)S(1)}, bf16[64,1792]{1,0:T(8,128)(2,1)S(1)}, u32[]{:S(2)}, u32[]{:S(2)}) %collective-permute-start.9) | collective-permute-done | bytes 229408 | tf_op jit(solution)/shard_map/ppermute | solution.py:399
  56.0 0.5 collective-permute-start.14
  56.5 0.8 collective-permute-done.15.refs_4_
  57.3 0.7 collective-permute-start.19
  58.0 3.8 %collective-permute-done.11.refs_0_.refs_1_ = bf16[64,1792]{1,0:T(8,128)(2,1)S(1)} collective-permute-done((bf16[64,1792]{1,0:T(8,128)(2,1)S(1)}, bf16[64,1792]{1,0:T(8,128)(2,1)S(1)}, u32[]{:S(2)}, u32[]{:S(2)}) %collective-permute-start.11) | collective-permute-done | bytes 229408 | tf_op jit(solution)/shard_map/ppermute | solution.py:399
  61.9 1.3 %collective-permute-start.12 = (bf16[64,1792]{1,0:T(8,128)(2,1)S(1)}, bf16[64,1792]{1,0:T(8,128)(2,1)S(1)}, u32[]{:S(2)}, u32[]{:S(2)}) collective-permute-start(bf16[64,1792]{1,0:T(8,128)(2,1)S(1)} %collective-permute-done.11.refs_0_.refs_1_), channel_id=1, source_target_pairs={{0,8},{4,12},{8,0},{12,4},{1,9},{5,13},{9,1},{13,5},{2,10},{6,14},... | collective-permute-start | bytes 688136 | tf_op jit(solution)/shard_map/ppermute | solution.py:396
  63.2 1.0 collective-permute-start.21
  64.2 3.2 %fetch.7.refs_12_.down = bf16[1,512,7168]{2,1,0:T(8,128)(2,1)S(1)} custom-call(bf16[1,512,7168]{2,1,0:T(8,128)(2,1)} %refs_0_.7, bf16[64,1792]{1,0:T(8,128)(2,1)S(1)} %get-tuple-element.32.refs_1_.refs_6_), custom_call_target="tpu_custom_call" | custom-call | bytes 14680064 | tf_op jit(solution)/shard_map/fetch/pallas_call | solution.py:38
  67.5 0.5 collective-permute-start.20
  68.0 2.7 %activate.2 = (f32[256,512]{1,0:T(8,128)S(1)}, f32[256,512]{1,0:T(8,128)S(1)}, f32[256,1]{1,0:T(8,128)S(1)}) custom-call(s32[8]{0:T(128)S(1)} %stack.35.refs_0_.places, bf16[64,1792]{1,0:T(8,128)(2,1)S(1)} %collective-permute-done.11.refs_0_.refs_1_, bf16[64,1792]{1,0:T(8,128)(2,1)S(1)} %collective-permute-done.13.refs_1_, ...), custom_call_target="tpu_custom_call" | custom-call | flops 1879048192 | bytes 7340032 | tf_op jit(solution)/shard_map/activate/pallas_call | solution.py:277
  71.4 1.0 collective-permute-done.18.refs_1_
  72.7 2.9 %activate.3.active = bf16[256,512]{1,0:T(8,128)(2,1)S(1)} custom-call(s32[8]{0:T(128)S(1)} %stack.35.refs_0_.places, bf16[64,1792]{1,0:T(8,128)(2,1)S(1)} %collective-permute-done.12.refs_0_, bf16[64,1792]{1,0:T(8,128)(2,1)S(1)} %collective-permute-done.18.refs_1_, bf16[64,1792]{1,0:T(8,128)(2,1)S(1)} %collective-permute-done.19.refs_2_, ...), custom_call_target="tpu_custom_call" | custom-call | flops 1879048192 | bytes 7340032 | tf_op jit(solution)/shard_map/activate/pallas_call | solution.py:277
  75.6 2.7 %down.1 = (bf16[128,1792]{1,0:T(8,128)(2,1)S(1)}, bf16[128,1792]{1,0:T(8,128)(2,1)S(1)}, bf16[128,1792]{1,0:T(8,128)(2,1)S(1)}, bf16[128,1792]{1,0:T(8,128)(2,1)...) custom-call(s32[8]{0:T(128)S(1)} %stack.35.refs_0_.places, ...), custom_call_target="tpu_custom_call" | custom-call | flops 1879048192 | bytes 7340032 | tf_op jit(solution)/shard_map/down/pallas_call | solution.py:323
  79.3 0.8 collective-permute-done.25.refs_1_.refs_3_
  80.3 1.1 %collective-permute-start.26 = (bf16[64,1792]{1,0:T(8,128)(2,1)S(1)}, bf16[64,1792]{1,0:T(8,128)(2,1)S(1)}, u32[]{:S(2)}, u32[]{:S(2)}) collective-permute-start(bf16[64,1792]{1,0:T(8,128)(2,1)S(1)} %get-tuple-element.40), channel_id=1, source_target_pairs={{0,1},{1,0},{2,3},{3,2},{4,5},{5,4},{6,7},{7,6},{8,9},{9,8},{10,11... | collective-permute-start | bytes 688136 | tf_op jit(solution)/shard_map/ppermute | solution.py:399
  81.5 0.9 collective-permute-start.28
  82.5 1.3 %collective-permute-start.31 = (bf16[64,1792]{1,0:T(8,128)(2,1)S(1)}, bf16[64,1792]{1,0:T(8,128)(2,1)S(1)}, u32[]{:S(2)}, u32[]{:S(2)}) collective-permute-start(bf16[64,1792]{1,0:T(8,128)(2,1)S(1)} %get-tuple-element.50), channel_id=1, source_target_pairs={{0,8},{4,12},{8,0},{12,4},{1,9},{5,13},{9,1},{13,5},{2,10},{6,14},... | collective-permute-start | bytes 688136 | tf_op jit(solution)/shard_map/ppermute | solution.py:396
  83.7 4.3 %collective-permute-done.26.refs_2_.refs_4_ = bf16[64,1792]{1,0:T(8,128)(2,1)S(1)} collective-permute-done((bf16[64,1792]{1,0:T(8,128)(2,1)S(1)}, bf16[64,1792]{1,0:T(8,128)(2,1)S(1)}, u32[]{:S(2)}, u32[]{:S(2)}) %collective-permute-start.26) | collective-permute-done | bytes 229408 | tf_op jit(solution)/shard_map/ppermute | solution.py:399
  88.0 2.0 %collective-permute-done.28.refs_1_ = bf16[64,1792]{1,0:T(8,128)(2,1)S(1)} collective-permute-done((bf16[64,1792]{1,0:T(8,128)(2,1)S(1)}, bf16[64,1792]{1,0:T(8,128)(2,1)S(1)}, u32[]{:S(2)}, u32[]{:S(2)}) %collective-permute-start.28) | collective-permute-done | bytes 229408 | tf_op jit(solution)/shard_map/ppermute | solution.py:396
  90.1 1.0 collective-permute-start.32
  91.3 1.1 %collective-permute-start.29 = (bf16[64,1792]{1,0:T(8,128)(2,1)S(1)}, bf16[64,1792]{1,0:T(8,128)(2,1)S(1)}, u32[]{:S(2)}, u32[]{:S(2)}) collective-permute-start(bf16[64,1792]{1,0:T(8,128)(2,1)S(1)} %get-tuple-element.46), channel_id=1, source_target_pairs={{0,8},{4,12},{8,0},{12,4},{1,9},{5,13},{9,1},{13,5},{2,10},{6,14},... | collective-permute-start | bytes 688136 | tf_op jit(solution)/shard_map/ppermute | solution.py:396
  92.4 2.6 %collective-permute-done.31.refs_1_ = bf16[64,1792]{1,0:T(8,128)(2,1)S(1)} collective-permute-done((bf16[64,1792]{1,0:T(8,128)(2,1)S(1)}, bf16[64,1792]{1,0:T(8,128)(2,1)S(1)}, u32[]{:S(2)}, u32[]{:S(2)}) %collective-permute-start.31) | collective-permute-done | bytes 229408 | tf_op jit(solution)/shard_map/ppermute | solution.py:396
  94.9 1.2 %collective-permute-done.32.refs_2_ = bf16[64,1792]{1,0:T(8,128)(2,1)S(1)} collective-permute-done((bf16[64,1792]{1,0:T(8,128)(2,1)S(1)}, bf16[64,1792]{1,0:T(8,128)(2,1)S(1)}, u32[]{:S(2)}, u32[]{:S(2)}) %collective-permute-start.32) | collective-permute-done | bytes 229408 | tf_op jit(solution)/shard_map/ppermute | solution.py:399
  96.3 3.8 %collective-permute-start.33 = (bf16[64,1792]{1,0:T(8,128)(2,1)S(1)}, bf16[64,1792]{1,0:T(8,128)(2,1)S(1)}, u32[]{:S(2)}, u32[]{:S(2)}) collective-permute-start(bf16[64,1792]{1,0:T(8,128)(2,1)S(1)} %add.76), channel_id=1, source_target_pairs={{0,2},{1,3},{2,0},{3,1},{4,6},{5,7},{6,4},{7,5},{8,10},{9,11},{10,... | collective-permute-start | bytes 688136 | tf_op jit(solution)/shard_map/ppermute | solution.py:399
  100.1 0.6 collective-permute-start.34
  100.7 6.6 %collective-permute-done.33.refs_2_ = bf16[64,1792]{1,0:T(8,128)(2,1)S(1)} collective-permute-done((bf16[64,1792]{1,0:T(8,128)(2,1)S(1)}, bf16[64,1792]{1,0:T(8,128)(2,1)S(1)}, u32[]{:S(2)}, u32[]{:S(2)}) %collective-permute-start.33) | collective-permute-done | bytes 229408 | tf_op jit(solution)/shard_map/ppermute | solution.py:399
  107.4 0.8 collective-permute-done.34.refs_1_
  108.1 0.7 add.78
  (68 shorter events, 4.0 us)
Async XLA Ops:
  0.6 15.9 %copy-start = (bf16[256,1792]{1,0:T(8,128)(2,1)S(1)}, bf16[256,1792]{1,0:T(8,128)(2,1)}, u32[]{:S(2)}) copy-start(bf16[256,1792]{1,0:T(8,128)(2,1)} %param.21) | copy-start | bytes 2752516
  0.8 15.6 %copy-start.4 = (f32[256,2]{0,1:T(2,128)S(1)}, f32[256,2]{0,1:T(2,128)}, u32[]{:S(2)}) copy-start(f32[256,2]{0,1:T(2,128)} %param.24) | copy-start | bytes 6148
  0.8 15.6 %copy-start.5 = (s32[256,2]{0,1:T(2,128)S(1)}, s32[256,2]{0,1:T(2,128)}, u32[]{:S(2)}) copy-start(s32[256,2]{0,1:T(2,128)} %param.23) | copy-start | bytes 6148
  0.8 15.7 %copy-start.3 = (f32[1792]{0:T(1024)S(1)}, f32[1792]{0:T(1024)}, u32[]{:S(2)}) copy-start(f32[1792]{0:T(1024)} %param.22) | copy-start | bytes 21508
  13.3 7.3 %collective-permute-start = (bf16[64,1024]{1,0:T(8,128)(2,1)S(1)}, bf16[64,1024]{1,0:T(8,128)(2,1)S(1)}, u32[]{:S(2)}, u32[]{:S(2)}) collective-permute-start(bf16[64,1024]{1,0:T(8,128)(2,1)S(1)} %attention.1.refs_1_.refs_0_), channel_id=1, source_target_pairs={{0,4},{4,0},{8,12},{12,8},{1,5},{5,1},{9,13},{13,9},{2,6},{6,2},{1... | collective-permute-start | bytes 393224 | tf_op jit(solution)/shard_map/ppermute | solution.py:392
  13.8 6.7 %collective-permute-start.1 = (bf16[64,1024]{1,0:T(8,128)(2,1)S(1)}, bf16[64,1024]{1,0:T(8,128)(2,1)S(1)}, u32[]{:S(2)}, u32[]{:S(2)}) collective-permute-start(bf16[64,1024]{1,0:T(8,128)(2,1)S(1)} %attention.1.refs_1_.refs_0_), channel_id=1, source_target_pairs={{0,8},{4,12},{8,0},{12,4},{1,9},{5,13},{9,1},{13,5},{2,10},{6,14},... | collective-permute-start | bytes 393224 | tf_op jit(solution)/shard_map/ppermute | solution.py:396
  20.5 1.4 %collective-permute-start.2 = (bf16[64,1024]{1,0:T(8,128)(2,1)S(1)}, bf16[64,1024]{1,0:T(8,128)(2,1)S(1)}, u32[]{:S(2)}, u32[]{:S(2)}) collective-permute-start(bf16[64,1024]{1,0:T(8,128)(2,1)S(1)} %add.64.refs_2_), channel_id=1, source_target_pairs={{0,4},{4,0},{8,12},{12,8},{1,5},{5,1},{9,13},{13,9},{2,6},{6,2},{1... | collective-permute-start | bytes 393224 | tf_op jit(solution)/shard_map/ppermute | solution.py:392
  23.6 7.9 %collective-permute-start.3 = (bf16[64,1792]{1,0:T(8,128)(2,1)S(1)}, bf16[64,1792]{1,0:T(8,128)(2,1)S(1)}, u32[]{:S(2)}, u32[]{:S(2)}) collective-permute-start(bf16[64,1792]{1,0:T(8,128)(2,1)S(1)} %get-tuple-element.29), channel_id=1, source_target_pairs={{0,1},{1,0},{2,3},{3,2},{4,5},{5,4},{6,7},{7,6},{8,9},{9,8},{10,11... | collective-permute-start | bytes 688136 | tf_op jit(solution)/shard_map/ppermute | solution.py:399
  28.8 11.7 %collective-permute-start.5 = (bf16[64,1792]{1,0:T(8,128)(2,1)S(1)}, bf16[64,1792]{1,0:T(8,128)(2,1)S(1)}, u32[]{:S(2)}, u32[]{:S(2)}) collective-permute-start(bf16[64,1792]{1,0:T(8,128)(2,1)S(1)} %add.66), channel_id=1, source_target_pairs={{0,1},{1,0},{2,3},{3,2},{4,5},{5,4},{6,7},{7,6},{8,9},{9,8},{10,11... | collective-permute-start | bytes 688136 | tf_op jit(solution)/shard_map/ppermute | solution.py:399
  31.6 12.8 %collective-permute-start.4 = (bf16[64,1792]{1,0:T(8,128)(2,1)S(1)}, bf16[64,1792]{1,0:T(8,128)(2,1)S(1)}, u32[]{:S(2)}, u32[]{:S(2)}) collective-permute-start(bf16[64,1792]{1,0:T(8,128)(2,1)S(1)} %add.65), channel_id=1, source_target_pairs={{0,2},{1,3},{2,0},{3,1},{4,6},{5,7},{6,4},{7,5},{8,10},{9,11},{10,... | collective-permute-start | bytes 688136 | tf_op jit(solution)/shard_map/ppermute | solution.py:399
  34.6 3.6 %collective-permute-start.7 = (f32[1,1792]{1,0:T(1,128)S(1)}, f32[1,1792]{1,0:T(1,128)S(1)}, u32[]{:S(2)}, u32[]{:S(2)}) collective-permute-start(f32[1,1792]{1,0:T(1,128)S(1)} %reshape.7.refs_4_.refs_8_), channel_id=1, source_target_pairs={{0,8},{4,12},{8,0},{12,4},{1,9},{5,13},{9,1},{13,5},{2,10},{6,14},... | collective-permute-start | bytes 21512 | tf_op jit(solution)/shard_map/ppermute | solution.py:396
  36.1 2.2 %collective-permute-start.6 = (f32[1,1792]{1,0:T(1,128)S(1)}, f32[1,1792]{1,0:T(1,128)S(1)}, u32[]{:S(2)}, u32[]{:S(2)}) collective-permute-start(f32[1,1792]{1,0:T(1,128)S(1)} %reshape.7.refs_4_.refs_8_), channel_id=1, source_target_pairs={{0,4},{4,0},{8,12},{12,8},{1,5},{5,1},{9,13},{13,9},{2,6},{6,2},{1... | collective-permute-start | bytes 21512 | tf_op jit(solution)/shard_map/ppermute | solution.py:392
  38.2 1.2 %collective-permute-start.8 = (f32[1,1792]{1,0:T(1,128)S(1)}, f32[1,1792]{1,0:T(1,128)S(1)}, u32[]{:S(2)}, u32[]{:S(2)}) collective-permute-start(f32[1,1792]{1,0:T(1,128)S(1)} %collective-permute-done.7.refs_10_.refs_8_), channel_id=1, source_target_pairs={{0,4},{4,0},{8,12},{12,8},{1,5},{5,1},{9,13},{13,9},{2,6},{6,2},{1... | collective-permute-start | bytes 21512 | tf_op jit(solution)/shard_map/ppermute | solution.py:392
  45.2 10.3 %collective-permute-start.9 = (bf16[64,1792]{1,0:T(8,128)(2,1)S(1)}, bf16[64,1792]{1,0:T(8,128)(2,1)S(1)}, u32[]{:S(2)}, u32[]{:S(2)}) collective-permute-start(bf16[64,1792]{1,0:T(8,128)(2,1)S(1)} %get-tuple-element.32.refs_1_.refs_6_), channel_id=1, source_target_pairs={{0,2},{1,3},{2,0},{3,1},{4,6},{5,7},{6,4},{7,5},{8,10},{9,11},{10,... | collective-permute-start | bytes 688136 | tf_op jit(solution)/shard_map/ppermute | solution.py:399
  45.2 10.3 %collective-permute-start.10 = (bf16[64,1792]{1,0:T(8,128)(2,1)S(1)}, bf16[64,1792]{1,0:T(8,128)(2,1)S(1)}, u32[]{:S(2)}, u32[]{:S(2)}) collective-permute-start(bf16[64,1792]{1,0:T(8,128)(2,1)S(1)} %get-tuple-element.32.refs_1_.refs_6_), channel_id=1, source_target_pairs={{0,8},{4,12},{8,0},{12,4},{1,9},{5,13},{9,1},{13,5},{2,10},{6,14},... | collective-permute-start | bytes 688136 | tf_op jit(solution)/shard_map/ppermute | solution.py:396
  46.8 10.5 %collective-permute-start.15 = (bf16[64,1792]{1,0:T(8,128)(2,1)S(1)}, bf16[64,1792]{1,0:T(8,128)(2,1)S(1)}, u32[]{:S(2)}, u32[]{:S(2)}) collective-permute-start(bf16[64,1792]{1,0:T(8,128)(2,1)S(1)} %get-tuple-element.32.refs_1_.refs_6_), channel_id=1, source_target_pairs={{0,1},{1,0},{2,3},{3,2},{4,5},{5,4},{6,7},{7,6},{8,9},{9,8},{10,11... | collective-permute-start | bytes 688136 | tf_op jit(solution)/shard_map/ppermute | solution.py:399
  55.6 6.3 %collective-permute-start.11 = (bf16[64,1792]{1,0:T(8,128)(2,1)S(1)}, bf16[64,1792]{1,0:T(8,128)(2,1)S(1)}, u32[]{:S(2)}, u32[]{:S(2)}) collective-permute-start(bf16[64,1792]{1,0:T(8,128)(2,1)S(1)} %add.68), channel_id=1, source_target_pairs={{0,1},{1,0},{2,3},{3,2},{4,5},{5,4},{6,7},{7,6},{8,9},{9,8},{10,11... | collective-permute-start | bytes 688136 | tf_op jit(solution)/shard_map/ppermute | solution.py:399
  56.0 5.8 %collective-permute-start.17 = (bf16[64,1792]{1,0:T(8,128)(2,1)S(1)}, bf16[64,1792]{1,0:T(8,128)(2,1)S(1)}, u32[]{:S(2)}, u32[]{:S(2)}) collective-permute-start(bf16[64,1792]{1,0:T(8,128)(2,1)S(1)} %get-tuple-element.32.refs_1_.refs_6_), channel_id=1, source_target_pairs={{0,4},{4,0},{8,12},{12,8},{1,5},{5,1},{9,13},{13,9},{2,6},{6,2},{1... | collective-permute-start | bytes 688136 | tf_op jit(solution)/shard_map/ppermute | solution.py:392
  56.0 7.2 %collective-permute-start.14 = (bf16[64,1792]{1,0:T(8,128)(2,1)S(1)}, bf16[64,1792]{1,0:T(8,128)(2,1)S(1)}, u32[]{:S(2)}, u32[]{:S(2)}) collective-permute-start(bf16[64,1792]{1,0:T(8,128)(2,1)S(1)} %collective-permute-done.9.refs_0_.refs_2_), channel_id=1, source_target_pairs={{0,4},{4,0},{8,12},{12,8},{1,5},{5,1},{9,13},{13,9},{2,6},{6,2},{1... | collective-permute-start | bytes 688136 | tf_op jit(solution)/shard_map/ppermute | solution.py:392
  57.3 10.1 %collective-permute-start.16 = (bf16[64,1792]{1,0:T(8,128)(2,1)S(1)}, bf16[64,1792]{1,0:T(8,128)(2,1)S(1)}, u32[]{:S(2)}, u32[]{:S(2)}) collective-permute-start(bf16[64,1792]{1,0:T(8,128)(2,1)S(1)} %collective-permute-done.15.refs_4_), channel_id=1, source_target_pairs={{0,4},{4,0},{8,12},{12,8},{1,5},{5,1},{9,13},{13,9},{2,6},{6,2},{1... | collective-permute-start | bytes 688136 | tf_op jit(solution)/shard_map/ppermute | solution.py:392
  57.3 10.2 %collective-permute-start.19 = (bf16[64,1792]{1,0:T(8,128)(2,1)S(1)}, bf16[64,1792]{1,0:T(8,128)(2,1)S(1)}, u32[]{:S(2)}, u32[]{:S(2)}) collective-permute-start(bf16[64,1792]{1,0:T(8,128)(2,1)S(1)} %collective-permute-done.9.refs_0_.refs_2_), channel_id=1, source_target_pairs={{0,8},{4,12},{8,0},{12,4},{1,9},{5,13},{9,1},{13,5},{2,10},{6,14},... | collective-permute-start | bytes 688136 | tf_op jit(solution)/shard_map/ppermute | solution.py:396
  61.9 6.2 %collective-permute-start.13 = (bf16[64,1792]{1,0:T(8,128)(2,1)S(1)}, bf16[64,1792]{1,0:T(8,128)(2,1)S(1)}, u32[]{:S(2)}, u32[]{:S(2)}) collective-permute-start(bf16[64,1792]{1,0:T(8,128)(2,1)S(1)} %collective-permute-done.11.refs_0_.refs_1_), channel_id=1, source_target_pairs={{0,4},{4,0},{8,12},{12,8},{1,5},{5,1},{9,13},{13,9},{2,6},{6,2},{1... | collective-permute-start | bytes 688136 | tf_op jit(solution)/shard_map/ppermute | solution.py:392
  61.9 8.9 %collective-permute-start.12 = (bf16[64,1792]{1,0:T(8,128)(2,1)S(1)}, bf16[64,1792]{1,0:T(8,128)(2,1)S(1)}, u32[]{:S(2)}, u32[]{:S(2)}) collective-permute-start(bf16[64,1792]{1,0:T(8,128)(2,1)S(1)} %collective-permute-done.11.refs_0_.refs_1_), channel_id=1, source_target_pairs={{0,8},{4,12},{8,0},{12,4},{1,9},{5,13},{9,1},{13,5},{2,10},{6,14},... | collective-permute-start | bytes 688136 | tf_op jit(solution)/shard_map/ppermute | solution.py:396
  63.2 7.8 %collective-permute-start.21 = (bf16[64,1792]{1,0:T(8,128)(2,1)S(1)}, bf16[64,1792]{1,0:T(8,128)(2,1)S(1)}, u32[]{:S(2)}, u32[]{:S(2)}) collective-permute-start(bf16[64,1792]{1,0:T(8,128)(2,1)S(1)} %add.70), channel_id=1, source_target_pairs={{0,1},{1,0},{2,3},{3,2},{4,5},{5,4},{6,7},{7,6},{8,9},{9,8},{10,11... | collective-permute-start | bytes 688136 | tf_op jit(solution)/shard_map/ppermute | solution.py:399
  67.4 3.3 %copy-start.2 = (bf16[1,512,7168]{2,1,0:T(8,128)(2,1)}, bf16[1,512,7168]{2,1,0:T(8,128)(2,1)S(1)}, u32[]{:S(2)}) copy-start(bf16[1,512,7168]{2,1,0:T(8,128)(2,1)S(1)} %fetch.7.refs_12_.down) | copy-start | bytes 22020100
  67.4 3.9 %collective-permute-start.23 = (bf16[64,1792]{1,0:T(8,128)(2,1)S(1)}, bf16[64,1792]{1,0:T(8,128)(2,1)S(1)}, u32[]{:S(2)}, u32[]{:S(2)}) collective-permute-start(bf16[64,1792]{1,0:T(8,128)(2,1)S(1)} %collective-permute-done.10.refs_1_.refs_0_.refs_6_), channel_id=1, source_target_pairs={{0,4},{4,0},{8,12},{12,8},{1,5},{5,1},{9,13},{13,9},{2,6},{6,2},{1... | collective-permute-start | bytes 688136 | tf_op jit(solution)/shard_map/ppermute | solution.py:392
  67.5 3.8 %collective-permute-start.20 = (bf16[64,1792]{1,0:T(8,128)(2,1)S(1)}, bf16[64,1792]{1,0:T(8,128)(2,1)S(1)}, u32[]{:S(2)}, u32[]{:S(2)}) collective-permute-start(bf16[64,1792]{1,0:T(8,128)(2,1)S(1)} %collective-permute-done.19.refs_2_), channel_id=1, source_target_pairs={{0,4},{4,0},{8,12},{12,8},{1,5},{5,1},{9,13},{13,9},{2,6},{6,2},{1... | collective-permute-start | bytes 688136 | tf_op jit(solution)/shard_map/ppermute | solution.py:392
  70.7 4.8 %slice-start = ((s8[7340032]{0:T(1024)(128)(4,1)}), s8[4194304]{0:T(1024)(128)(4,1)S(1)}, s32[]{:S(2)}) async-start(s8[7340032]{0:T(1024)(128)(4,1)} %bitcast.9), calls=%async_computation | async-start | bytes 8388608
  70.8 1.6 %collective-permute-start.18 = (bf16[64,1792]{1,0:T(8,128)(2,1)S(1)}, bf16[64,1792]{1,0:T(8,128)(2,1)S(1)}, u32[]{:S(2)}, u32[]{:S(2)}) collective-permute-start(bf16[64,1792]{1,0:T(8,128)(2,1)S(1)} %add.69), channel_id=1, source_target_pairs={{0,4},{4,0},{8,12},{12,8},{1,5},{5,1},{9,13},{13,9},{2,6},{6,2},{1... | collective-permute-start | bytes 688136 | tf_op jit(solution)/shard_map/ppermute | solution.py:392
  71.0 1.7 %collective-permute-start.22 = (bf16[64,1792]{1,0:T(8,128)(2,1)S(1)}, bf16[64,1792]{1,0:T(8,128)(2,1)S(1)}, u32[]{:S(2)}, u32[]{:S(2)}) collective-permute-start(bf16[64,1792]{1,0:T(8,128)(2,1)S(1)} %collective-permute-done.21.refs_4_), channel_id=1, source_target_pairs={{0,4},{4,0},{8,12},{12,8},{1,5},{5,1},{9,13},{13,9},{2,6},{6,2},{1... | collective-permute-start | bytes 688136 | tf_op jit(solution)/shard_map/ppermute | solution.py:392
  72.7 2.9 %slice-start.1 = ((s8[7340032]{0:T(1024)(128)(4,1)}), s8[3145728]{0:T(1024)(128)(4,1)S(1)}, s32[]{:S(2)}) async-start(s8[7340032]{0:T(1024)(128)(4,1)} %bitcast.9), calls=%async_computation.1 | async-start | bytes 6291456
  75.5 33.3 %copy-start.1 = (bf16[256,1792]{1,0:T(8,128)(2,1)S(1)}, bf16[256,1792]{1,0:T(8,128)(2,1)}, u32[]{:S(2)}) copy-start(bf16[256,1792]{1,0:T(8,128)(2,1)} %param.21) | copy-start | bytes 2752516
  78.3 1.9 %collective-permute-start.25 = (bf16[128,1792]{1,0:T(8,128)(2,1)S(1)}, bf16[128,1792]{1,0:T(8,128)(2,1)S(1)}, u32[]{:S(2)}, u32[]{:S(2)}) collective-permute-start(bf16[128,1792]{1,0:T(8,128)(2,1)S(1)} %get-tuple-element.39), channel_id=1, source_target_pairs={{0,4},{4,0},{8,12},{12,8},{1,5},{5,1},{9,13},{13,9},{2,6},{6,2},{1... | collective-permute-start | bytes 1376264 | tf_op jit(solution)/shard_map/ppermute | solution.py:392
  78.5 2.9 %collective-permute-start.27 = (bf16[128,1792]{1,0:T(8,128)(2,1)S(1)}, bf16[128,1792]{1,0:T(8,128)(2,1)S(1)}, u32[]{:S(2)}, u32[]{:S(2)}) collective-permute-start(bf16[128,1792]{1,0:T(8,128)(2,1)S(1)} %get-tuple-element.42), channel_id=1, source_target_pairs={{0,4},{4,0},{8,12},{12,8},{1,5},{5,1},{9,13},{13,9},{2,6},{6,2},{1... | collective-permute-start | bytes 1376264 | tf_op jit(solution)/shard_map/ppermute | solution.py:392
  78.8 3.5 %collective-permute-start.30 = (bf16[128,1792]{1,0:T(8,128)(2,1)S(1)}, bf16[128,1792]{1,0:T(8,128)(2,1)S(1)}, u32[]{:S(2)}, u32[]{:S(2)}) collective-permute-start(bf16[128,1792]{1,0:T(8,128)(2,1)S(1)} %get-tuple-element.48), channel_id=1, source_target_pairs={{0,4},{4,0},{8,12},{12,8},{1,5},{5,1},{9,13},{13,9},{2,6},{6,2},{1... | collective-permute-start | bytes 1376264 | tf_op jit(solution)/shard_map/ppermute | solution.py:392
  79.0 12.1 %collective-permute-start.24 = (bf16[128,1792]{1,0:T(8,128)(2,1)S(1)}, bf16[128,1792]{1,0:T(8,128)(2,1)S(1)}, u32[]{:S(2)}, u32[]{:S(2)}) collective-permute-start(bf16[128,1792]{1,0:T(8,128)(2,1)S(1)} %get-tuple-element.37), channel_id=1, source_target_pairs={{0,4},{4,0},{8,12},{12,8},{1,5},{5,1},{9,13},{13,9},{2,6},{6,2},{1... | collective-permute-start | bytes 1376264 | tf_op jit(solution)/shard_map/ppermute | solution.py:392
  80.3 7.8 %collective-permute-start.26 = (bf16[64,1792]{1,0:T(8,128)(2,1)S(1)}, bf16[64,1792]{1,0:T(8,128)(2,1)S(1)}, u32[]{:S(2)}, u32[]{:S(2)}) collective-permute-start(bf16[64,1792]{1,0:T(8,128)(2,1)S(1)} %get-tuple-element.40), channel_id=1, source_target_pairs={{0,1},{1,0},{2,3},{3,2},{4,5},{5,4},{6,7},{7,6},{8,9},{9,8},{10,11... | collective-permute-start | bytes 688136 | tf_op jit(solution)/shard_map/ppermute | solution.py:399
  81.5 8.6 %collective-permute-start.28 = (bf16[64,1792]{1,0:T(8,128)(2,1)S(1)}, bf16[64,1792]{1,0:T(8,128)(2,1)S(1)}, u32[]{:S(2)}, u32[]{:S(2)}) collective-permute-start(bf16[64,1792]{1,0:T(8,128)(2,1)S(1)} %get-tuple-element.44), channel_id=1, source_target_pairs={{0,8},{4,12},{8,0},{12,4},{1,9},{5,13},{9,1},{13,5},{2,10},{6,14},... | collective-permute-start | bytes 688136 | tf_op jit(solution)/shard_map/ppermute | solution.py:396
  82.5 12.5 %collective-permute-start.31 = (bf16[64,1792]{1,0:T(8,128)(2,1)S(1)}, bf16[64,1792]{1,0:T(8,128)(2,1)S(1)}, u32[]{:S(2)}, u32[]{:S(2)}) collective-permute-start(bf16[64,1792]{1,0:T(8,128)(2,1)S(1)} %get-tuple-element.50), channel_id=1, source_target_pairs={{0,8},{4,12},{8,0},{12,4},{1,9},{5,13},{9,1},{13,5},{2,10},{6,14},... | collective-permute-start | bytes 688136 | tf_op jit(solution)/shard_map/ppermute | solution.py:396
  90.1 6.1 %collective-permute-start.32 = (bf16[64,1792]{1,0:T(8,128)(2,1)S(1)}, bf16[64,1792]{1,0:T(8,128)(2,1)S(1)}, u32[]{:S(2)}, u32[]{:S(2)}) collective-permute-start(bf16[64,1792]{1,0:T(8,128)(2,1)S(1)} %add.73.refs_5_), channel_id=1, source_target_pairs={{0,1},{1,0},{2,3},{3,2},{4,5},{5,4},{6,7},{7,6},{8,9},{9,8},{10,11... | collective-permute-start | bytes 688136 | tf_op jit(solution)/shard_map/ppermute | solution.py:399
  91.3 9.4 %collective-permute-start.29 = (bf16[64,1792]{1,0:T(8,128)(2,1)S(1)}, bf16[64,1792]{1,0:T(8,128)(2,1)S(1)}, u32[]{:S(2)}, u32[]{:S(2)}) collective-permute-start(bf16[64,1792]{1,0:T(8,128)(2,1)S(1)} %get-tuple-element.46), channel_id=1, source_target_pairs={{0,8},{4,12},{8,0},{12,4},{1,9},{5,13},{9,1},{13,5},{2,10},{6,14},... | collective-permute-start | bytes 688136 | tf_op jit(solution)/shard_map/ppermute | solution.py:396
  96.3 11.0 %collective-permute-start.33 = (bf16[64,1792]{1,0:T(8,128)(2,1)S(1)}, bf16[64,1792]{1,0:T(8,128)(2,1)S(1)}, u32[]{:S(2)}, u32[]{:S(2)}) collective-permute-start(bf16[64,1792]{1,0:T(8,128)(2,1)S(1)} %add.76), channel_id=1, source_target_pairs={{0,2},{1,3},{2,0},{3,1},{4,6},{5,7},{6,4},{7,5},{8,10},{9,11},{10,... | collective-permute-start | bytes 688136 | tf_op jit(solution)/shard_map/ppermute | solution.py:399
  100.1 8.0 %collective-permute-start.34 = (bf16[64,1792]{1,0:T(8,128)(2,1)S(1)}, bf16[64,1792]{1,0:T(8,128)(2,1)S(1)}, u32[]{:S(2)}, u32[]{:S(2)}) collective-permute-start(bf16[64,1792]{1,0:T(8,128)(2,1)S(1)} %get-tuple-element.51), channel_id=1, source_target_pairs={{0,1},{1,0},{2,3},{3,2},{4,5},{5,4},{6,7},{7,6},{8,9},{9,8},{10,11... | collective-permute-start | bytes 688136 | tf_op jit(solution)/shard_map/ppermute | solution.py:399
